TPU v7x, 32 devices: a whole 2x2x4 slice. The times are simulated.
32 devices in a mesh: parts: 2 (over y), mem: 4 (over z), tp: 2 (over x), rep: 2 (over core).
Axes of the slice: x: 2, y: 2, z: 4, core: 2. Of those that a mesh axis runs over, the one named last changes fastest.
Arguments:
- hidden: bfloat16 [4096, 4608], P(('parts', 'mem', 'rep'), 'tp'), parts along dimension 0, may hold values from -40 to 40
- row_ids: int32 [4096, 16], P(('parts', 'mem', 'rep'), 'tp'), parts along dimension 0, may hold values from 0 to 4095, as said below
- row_place: int32 [8192], P('parts'), parts along dimension 0, may hold values from 0 to 4095, as said below
- table_codes: bfloat16 [32, 4096, 80], P(('parts', 'tp'), 'mem'), parts along dimension 0, may hold values from -4 to 4
- table_scales: bfloat16 [32, 4096, 5], P(('parts', 'tp'), 'mem'), parts along dimension 0, may hold values from 0.25 to 4
- key_weight: bfloat16 [1280, 4608], P(None, ('tp', 'rep')), may hold values from -0.36336105 to 0.36336105
- value_weight: bfloat16 [1280, 4608], P(None, ('tp', 'rep')), may hold values from -0.36336105 to 0.36336105
- conv_weight: float32 [4, 4608], P(None, 'tp'), may hold values from -2.5 to 2.5
Outputs:
- output: bfloat16 [4096, 4608], P(('parts', 'mem', 'rep'), 'tp'), parts along dimension 0
There are 2 independent parts, one for each index of `parts`. A program takes and returns all parts, laid end to end along the dimension named above; an argument that names none is the same for every part. Nothing has to cross between parts.
Inputs may be any that keep to these rules, and one draw needn't show every extreme that they name: row_place is a permutation; row r of table g is stored at position row_place[r], on mem index row_place[r] // 1024. `row_ids`: within the 256 tokens of one index of mem+rep and the 8 heads of one index of tp, at most 1280 of the 2048 requested rows are stored on one index of mem; for each index of rep and of tp, some index of mem receives exactly 1280 from every such block.
All inputs are finite; a program needn't handle non-finite values.
Results may differ from a plain program's by a relative error of at most 0.0039.
Values may be sent and summed in bfloat16 or wider, within the bound.
No kernel may reach another device: no remote copies, remote signals or barrier semaphores. Data moves between devices by JAX's collectives and lax.ppermute only.
A program may use at most 128 MiB of HBM per device.

v0:
```python
import jax
import jax.numpy as jnp
from jax import lax
from jax.sharding import PartitionSpec as P

D = 4608
KERNEL = 4
DILATION = 3
SEQS = 4


EPSILON = 1e-06


def from_behind(x, axis, by):
    length = lax.axis_size(axis)
    pairs = [(i, i + by) for i in range(length) if 0 <= i + by < length]
    return lax.ppermute(x, axis, pairs)


def hadamard_block():
    entry_index = jnp.arange(16, dtype=jnp.int32)
    parity = jnp.zeros((16, 16), jnp.int32)
    for shift_bit in range(4):
        parity = parity + (entry_index[:, None] >> shift_bit & 1) * (
            entry_index[None, :] >> shift_bit & 1
        )
    return (1.0 - 2.0 * (parity % 2)).astype(jnp.float32) * 0.25


def decode_rows(codes, scales):
    lead_shape = codes.shape[:-1]
    row_width = codes.shape[-1]
    flat_codes = codes.astype(jnp.float32).reshape(-1, 16)
    flat_scales = scales.astype(jnp.float32).reshape(-1, 1)
    rotated = jnp.dot(
        flat_codes * flat_scales,
        hadamard_block(),
        precision=lax.Precision.HIGHEST,
        preferred_element_type=jnp.float32,
    )
    return rotated.reshape(lead_shape + (row_width,)).astype(jnp.bfloat16)


def add_columns(left_side, pieces):
    key_part = jnp.dot(left_side, pieces[0], preferred_element_type=jnp.float32)
    value_part = jnp.dot(left_side, pieces[1], preferred_element_type=jnp.float32)
    return (key_part, value_part)


def gate_from(power_states, power_keys, inner_sum):
    inverse_states = lax.rsqrt(power_states / D + EPSILON)
    inverse_keys = lax.rsqrt(power_keys / D + EPSILON)
    return jax.nn.sigmoid(inner_sum * inverse_states * inverse_keys / D**0.5)


def shards(
    hidden, row_ids, row_place, table_codes, table_scales, key_weight, value_weight, conv_weight
):
    mem_count = lax.axis_size("mem")
    tok_rows, head_count = row_ids.shape
    table_rows = table_codes.shape[1]
    row_width = table_codes.shape[2]
    block_count = row_width // 16
    requests = tok_rows * head_count
    capacity = 5 * requests // (2 * mem_count)
    stored = row_place[row_ids.reshape(requests)]
    owner_index = stored // table_rows
    within = stored % table_rows
    head_of = jnp.tile(jnp.arange(head_count, dtype=jnp.int32), tok_rows)
    wanted = head_of * table_rows + within
    owner_hot = (owner_index[:, None] == jnp.arange(mem_count, dtype=jnp.int32)[None, :]).astype(
        jnp.int32
    )
    before = jnp.cumsum(owner_hot, axis=0) - owner_hot
    rank_index = jnp.sum(before * owner_hot, axis=1)
    slot_index = owner_index * capacity + rank_index
    outgoing = (
        jnp.zeros((mem_count * capacity,), jnp.int32)
        .at[slot_index]
        .set(wanted)
        .reshape(mem_count, capacity)
    )
    flat_codes = table_codes.reshape(head_count * table_rows, row_width)
    flat_scales = table_scales.reshape(head_count * table_rows, block_count)
    asked = lax.all_to_all(outgoing, "mem", split_axis=0, concat_axis=0, tiled=True)
    found = (flat_codes[asked], flat_scales[asked])
    found_rows, found_scales = found
    back_rows, back_scales = (
        lax.all_to_all(
            found_rows.reshape(mem_count, capacity * row_width),
            "mem",
            split_axis=0,
            concat_axis=0,
            tiled=True,
        ),
        lax.all_to_all(
            found_scales.reshape(mem_count, capacity * block_count),
            "mem",
            split_axis=0,
            concat_axis=0,
            tiled=True,
        ),
    )
    got_rows = back_rows.reshape(mem_count * capacity, row_width)[slot_index]
    got_scales = back_scales.reshape(mem_count * capacity, block_count)[slot_index]
    memory = decode_rows(got_rows, got_scales).reshape(tok_rows, head_count * row_width)
    whole_memory = lax.all_gather(memory, "tp", axis=1, tiled=True)
    key_field, value_field = add_columns(
        whole_memory,
        (
            lax.all_gather(key_weight, "rep", axis=1, tiled=True),
            lax.all_gather(value_weight, "rep", axis=1, tiled=True),
        ),
    )
    states = hidden.astype(jnp.float32)
    power_states, power_keys, inner_sum, power_values = lax.psum(
        (
            jnp.sum(states * states, axis=1),
            jnp.sum(key_field * key_field, axis=1),
            jnp.sum(states * key_field, axis=1),
            jnp.sum(value_field * value_field, axis=1),
        ),
        "tp",
    )
    gate_open = gate_from(power_states, power_keys, inner_sum)
    gated_value = gate_open[:, None] * value_field
    power_gated = gate_open * gate_open * power_values
    normed = gated_value * lax.rsqrt(power_gated / D + EPSILON)[:, None]
    reach_rows = DILATION * (KERNEL - 1)
    rim_rows = from_behind(
        normed[tok_rows - reach_rows :].astype(jnp.bfloat16), ("mem", "rep"), 1
    ).astype(jnp.float32)
    extended = jnp.concatenate([rim_rows, normed], 0)
    seq_length = tok_rows * lax.axis_size(("mem", "rep")) // SEQS
    position = (
        lax.axis_index(("mem", "rep")) * tok_rows + jnp.arange(tok_rows, dtype=jnp.int32)
    ) % seq_length
    conv_sum = jnp.zeros_like(normed)
    for tap_index in range(KERNEL):
        lag_rows = DILATION * tap_index
        shifted = extended[reach_rows - lag_rows : reach_rows - lag_rows + tok_rows]
        conv_sum = conv_sum + conv_weight[tap_index][None, :] * jnp.where(
            (position >= lag_rows)[:, None], shifted, 0.0
        )
    return (states + jax.nn.silu(conv_sum) + gated_value).astype(jnp.bfloat16)


def solution(mesh):
    in_specs = (
        P(("parts", "mem", "rep"), "tp"),
        P(("parts", "mem", "rep"), "tp"),
        P("parts"),
        P(("parts", "tp"), "mem", None),
        P(("parts", "tp"), "mem", None),
        P(None, ("tp", "rep")),
        P(None, ("tp", "rep")),
        P(None, "tp"),
    )
    out_specs = P(("parts", "mem", "rep"), "tp")
    return jax.shard_map(shards, mesh=mesh, in_specs=in_specs, out_specs=out_specs, check_vma=False)
```

profile of v0, /device:TPU:0, one launch (start us, length us, event | category | flops | bytes accessed | tf_op | source)
XLA Modules:
  0.0 184.2 jit_solution(12774943811482583605)
XLA Ops:
  6.5 0.7 all-gather.5.cloned.1.call-update
  7.3 0.7 all-gather.3.cloned.1.call-update
  8.0 0.1 copy.16
  8.1 0.1 reshape.274
  8.3 11.8 %gather_fusion = s32[2048]{0:T(1024)S(1)} fusion(s32[4096]{0:T(1024)S(1)} %copy-done, s32[2048]{0:T(1024)S(1)} %broadcast_clamp_fusion.2), kind=kCustom, calls=%fused_computation | custom fusion | bytes 24576 | tf_op jit(solution)/shard_map/gather | solution.py:67
  20.1 1.2 reduce-window.6
  21.3 0.2 slice_reduce_fusion
  21.5 0.2 reduce-window.9
  22.0 8.6 %scatter_custom_fusion = s32[5120]{0:T(1024)} fusion(s32[2048]{0:T(1024)S(1)} %bitcast.53, s32[2048]{0:T(1024)S(1)} %get-tuple-element.18, s32[]{:T(128)} %constant.60.clone.1), kind=kCustom, calls=%fused_computation.66 | custom fusion | bytes 20484 | tf_op jit(solution)/shard_map/scatter | solution.py:81
  30.7 6.3 %all-to-all-start = ((s32[4,1,1280]{2,1,0:T(1,128)}), s32[4,1,1280]{2,1,0:T(1,128)S(1)}, u32[]{:S(2)}, u32[]{:S(2)}) async-start(s32[4,1,1280]{2,1,0:T(1,128)} %bitcast.7), calls=%async_computation | async-start | bytes 40960 | tf_op jit(solution)/shard_map/all_to_all | solution.py:86
  37.0 1.1 copy.18
  38.1 4.5 %all-to-all-done = s32[4,1,1280]{2,1,0:T(1,128)S(1)} async-done(((s32[4,1,1280]{2,1,0:T(1,128)}), s32[4,1,1280]{2,1,0:T(1,128)S(1)}, u32[]{:S(2)}, u32[]{:S(2)}) %all-to-all-start) | async-done | bytes 20512 | tf_op jit(solution)/shard_map/all_to_all | solution.py:86
  42.7 15.1 %gather_fusion.3 = bf16[5120,5]{1,0:T(8,128)(2,1)S(1)} fusion(bf16[8192,5]{1,0:T(8,128)(2,1)S(1)} %bitcast.49, s32[5120]{0:T(1024)S(1)} %broadcast_clamp_fusion), kind=kCustom, calls=%fused_computation.3 | custom fusion | bytes 122880 | tf_op jit(solution)/shard_map/gather | solution.py:87
  57.8 2.1 %all_to_all.28 = bf16[4,1,6400]{2,1,0:T(2,128)(2,1)S(1)} reshape(bf16[5120,5]{1,0:T(8,128)(2,1)S(1)} %gather_fusion.3) | data formatting | bytes 102400 | tf_op jit(solution)/shard_map/all_to_all | solution.py:97
  59.9 0.5 broadcast.464
  60.4 0.9 reduce.13
  61.3 0.6 reshape.344
  62.0 3.5 %all-to-all-start.2 = ((bf16[4,2,3200]{2,1,0:T(2,128)(2,1)}), bf16[4,2,3200]{2,1,0:T(2,128)(2,1)S(1)}, u32[]{:S(2)}, u32[]{:S(2)}) async-start(bf16[4,2,3200]{2,1,0:T(2,128)(2,1)} %reshape.344), calls=%async_computation.2 | async-start | bytes 102400 | tf_op jit(solution)/shard_map/all_to_all | solution.py:97
  65.4 2.9 %copy.15 = bf16[8,1024,80]{2,1,0:T(8,128)(2,1)S(1)} copy(bf16[8,1024,80]{1,2,0:T(8,128)(2,1)} %param.11) | data formatting | bytes 2621440 | tf_op args[3]
  68.3 15.1 %gather_fusion.1 = bf16[5120,80]{1,0:T(8,128)(2,1)S(1)} fusion(bf16[8192,80]{1,0:T(8,128)(2,1)S(1)} %bitcast.50, s32[5120]{0:T(1024)S(1)} %broadcast_clamp_fusion), kind=kCustom, calls=%fused_computation.1 | custom fusion | bytes 1658880 | tf_op jit(solution)/shard_map/gather | solution.py:87
  83.4 1.7 all_to_all.27
  85.1 6.0 %reduce.12 = bf16[4,102400]{1,0:T(4,128)(2,1)S(1)} reduce(bf16[4,1,102400]{2,1,0:T(2,128)(2,1)S(1)} %all_to_all.27, bf16[]{:T(256)} %broadcast.464), dimensions={1}, to_apply=%all_to_all.27.reduce_sub_computation | reduce | bytes 1638402 | tf_op jit(solution)/shard_map/all_to_all | solution.py:90
  91.1 1.7 reshape.342
  92.8 4.9 %all-to-all-start.1 = ((bf16[4,2,51200]{2,1,0:T(2,128)(2,1)}), bf16[4,2,51200]{2,1,0:T(2,128)(2,1)S(1)}, u32[]{:S(2)}, u32[]{:S(2)}) async-start(bf16[4,2,51200]{2,1,0:T(2,128)(2,1)} %reshape.342), calls=%async_computation.1 | async-start | bytes 1638400 | tf_op jit(solution)/shard_map/all_to_all | solution.py:90
  97.7 0.6 broadcast_compare_fusion
  98.3 0.7 slice_reduce_fusion.4
  99.1 0.3 reduce.3
  99.4 2.6 %reshape.278 = bf16[5120,5]{1,0:T(8,128)(2,1)S(1)} reshape(bf16[4,6400]{1,0:T(4,128)(2,1)S(1)} %reduce.3) | data formatting | bytes 102400 | tf_op jit(solution)/shard_map/reshape | solution.py:106
  102.0 6.2 %gather_fusion.4 = bf16[2048,5]{1,0:T(8,128)(2,1)S(1)} fusion(bf16[5120,5]{1,0:T(8,128)(2,1)S(1)} %reshape.278, s32[2048]{0:T(1024)S(1)} %broadcast_clamp_fusion.1), kind=kCustom, calls=%fused_computation.4 | custom fusion | bytes 49152 | tf_op jit(solution)/shard_map/gather | solution.py:106
  108.1 0.8 reshape.280
  108.9 7.9 %all-to-all-done.1 = bf16[4,2,51200]{2,1,0:T(2,128)(2,1)S(1)} async-done(((bf16[4,2,51200]{2,1,0:T(2,128)(2,1)}), bf16[4,2,51200]{2,1,0:T(2,128)(2,1)S(1)}, u32[]{:S(2)}, u32[]{:S(2)}) %all-to-all-start.1) | async-done | bytes 819232 | tf_op jit(solution)/shard_map/all_to_all | solution.py:90
  116.8 0.8 reshape.343
  117.6 5.3 %reduce.2 = bf16[4,102400]{1,0:T(4,128)(2,1)S(1)} reduce(bf16[4,1,102400]{2,1,0:T(2,128)(2,1)S(1)} %reshape.343, bf16[]{:T(256)} %constant.121), dimensions={1}, to_apply=%all_to_all.24.reduce_sub_computation | reduce | bytes 1638402 | tf_op jit(solution)/shard_map/all_to_all | solution.py:90
  122.9 1.6 reshape.276
  124.5 6.2 %gather_fusion.2 = bf16[2048,80]{1,0:T(8,128)(2,1)S(1)} fusion(bf16[5120,80]{1,0:T(8,128)(2,1)S(1)} %reshape.276, s32[2048]{0:T(1024)S(1)} %broadcast_clamp_fusion.1), kind=kCustom, calls=%fused_computation.2 | custom fusion | bytes 663552 | tf_op jit(solution)/shard_map/gather | solution.py:105
  130.7 3.7 %reshape.279 = f32[10240,16]{1,0:T(8,128)} reshape(bf16[2048,80]{1,0:T(8,128)(2,1)S(1)} %gather_fusion.2) | data formatting | bytes 983040 | tf_op jit(solution)/shard_map/convert_element_type | solution.py:34
  134.4 7.0 %convolution_convert_fusion = bf16[10240,16]{0,1:T(8,128)(2,1)S(1)} fusion(f32[10240,16]{1,0:T(8,128)} %reshape.279, f32[10240]{0:T(1024)S(1)} %reshape.280, s32[16]{0:T(128)S(1)} %get-tuple-element.22, s32[16]{0:T(128)S(1)} %get-tuple-element.23, s32[16]{0:T(128)S(1)} %get-tuple-element.24, s32[16]{0:T(128)S(1)} %get-tuple-element.25), kind=kOutput, calls=%fused_computation.6 | convolution fusion | flops 31790592 | bytes 1024256 | tf_op jit(solution)/shard_map/dot_general | solution.py:36
  141.4 1.2 copy.20
  142.6 1.7 convert_element_type.53
  144.4 9.4 %all_gather.9 = bf16[256,1280]{1,0:T(8,128)(2,1)} all-gather(bf16[256,640]{1,0:T(8,128)(2,1)S(1)} %convert_element_type.53), channel_id=1, replica_groups=mesh['parts'=2,'mem'=4,'tp'=2,'rep'=2] {'tp'}, dimensions={1}, use_global_device_ids=true | all-gather | bytes 983040 | tf_op jit(solution)/shard_map/all_gather | solution.py:108
  153.8 5.3 %multiply_reduce_fusion = (f32[256]{0:T(256)}, f32[256,2304]{1,0:T(8,128)S(1)}) fusion(bf16[256,1280]{1,0:T(8,128)(2,1)} %all_gather.9, bf16[1280,2304]{1,0:T(8,128)(2,1)} %all-gather.5.cloned.1.call-done), kind=kOutput, calls=%fused_computation.32 | convolution fusion | flops 1511128832 | bytes 8913920 | tf_op jit(solution)/shard_map/dot_general | solution.py:47
  159.1 5.3 %fusion.11 = (f32[256]{0:T(256)}, f32[256]{0:T(256)}, f32[256]{0:T(256)}) fusion(bf16[256,2304]{1,0:T(8,128)(2,1)S(1)} %copy-done.1, bf16[256,1280]{1,0:T(8,128)(2,1)} %all_gather.9, bf16[1280,2304]{1,0:T(8,128)(2,1)} %all-gather.3.cloned.1.call-done), kind=kOutput, calls=%fused_computation.25 | convolution fusion | flops 1514077440 | bytes 7736320 | tf_op jit(solution)/shard_map/dot_general | solution.py:46
  164.5 5.6 %all-reduce = (f32[256]{0:T(256)}, f32[256]{0:T(256)}, f32[256]{0:T(256)}, f32[256]{0:T(256)}) all-reduce(f32[256]{0:T(256)} %get-tuple-element.20, f32[256]{0:T(256)} %get-tuple-element.6, f32[256]{0:T(256)} %get-tuple-element.5, f32[256]{0:T(256)} %get-tuple-element.7), channel_id=1, replica_groups=mesh['parts'=2,'mem'=4,'tp'=2,'rep'=2] {'tp'}, use_global_device_ids=true, to_apply=%region_11.12 | all-reduce | flops 1024 | bytes 8192 | tf_op jit(solution)/shard_map/psum | solution.py:117
  170.1 0.7 add_rsqrt_fusion
  170.8 0.3 multiply_multiply_fusion
  171.2 1.3 collective-permute-start
  172.5 0.9 collective-permute-done
  173.4 3.9 %fusion.14 = bf16[256,2304]{1,0:T(8,128)(2,1)} fusion(bf16[256,2304]{1,0:T(8,128)(2,1)S(1)} %copy-done.1, f32[256,2304]{1,0:T(8,128)S(1)} %multiply_multiply_fusion, f32[9,2304]{1,0:T(8,128)S(1)} %convert_element_type.54, f32[256,2304]{1,0:T(8,128)S(1)} %get-tuple-element.21, f32[2304]{0:T(1024)S(1)} %copy-done.5, f32[2304]{0:T(1024)S(1)} %copy-done.6, ...), kind=kLoop, calls=%fused_computation.28 | loop fusion | flops 13565952 | bytes 7199744 | tf_op jit(solution)/shard_map/convert_element_type | solution.py:146
  (46 shorter events, 0.6 us)
Async XLA Ops:
  6.5 1.8 copy-start
  6.5 1.5 copy-start.8
  6.5 147.3 %all-gather.5.cloned.1.call-start = ((), (), s32[]{:S(2)}) async-start(), calls=%async_computation.4 | async-start | bytes 8847360 | tf_op jit(solution)/shard_map/all_gather | solution.py:113
  7.3 151.9 %all-gather.3.cloned.1.call-start = ((), (), s32[]{:S(2)}) async-start(), calls=%async_computation.3 | async-start | bytes 8847360 | tf_op jit(solution)/shard_map/all_gather | solution.py:112
  8.3 28.7 %copy-start.2 = (bf16[8,1024,5]{1,0,2:T(8,128)(2,1)S(1)}, bf16[8,1024,5]{1,0,2:T(8,128)(2,1)}, u32[]{:S(2)}) copy-start(bf16[8,1024,5]{1,0,2:T(8,128)(2,1)} %param.12) | copy-start | bytes 245764
  30.7 11.9 %all-to-all-start = ((s32[4,1,1280]{2,1,0:T(1,128)}), s32[4,1,1280]{2,1,0:T(1,128)S(1)}, u32[]{:S(2)}, u32[]{:S(2)}) async-start(s32[4,1,1280]{2,1,0:T(1,128)} %bitcast.7), calls=%async_computation | async-start | bytes 40960 | tf_op jit(solution)/shard_map/all_to_all | solution.py:86
  62.0 30.9 %all-to-all-start.2 = ((bf16[4,2,3200]{2,1,0:T(2,128)(2,1)}), bf16[4,2,3200]{2,1,0:T(2,128)(2,1)S(1)}, u32[]{:S(2)}, u32[]{:S(2)}) async-start(bf16[4,2,3200]{2,1,0:T(2,128)(2,1)} %reshape.344), calls=%async_computation.2 | async-start | bytes 102400 | tf_op jit(solution)/shard_map/all_to_all | solution.py:97
  85.1 13.2 %copy-start.7 = (f32[4,2304]{1,0:T(4,128)S(1)}, f32[4,2304]{1,0:T(4,128)}, u32[]{:S(2)}) copy-start(f32[4,2304]{1,0:T(4,128)} %param.15) | copy-start | bytes 110596
  92.8 24.0 %all-to-all-start.1 = ((bf16[4,2,51200]{2,1,0:T(2,128)(2,1)}), bf16[4,2,51200]{2,1,0:T(2,128)(2,1)S(1)}, u32[]{:S(2)}, u32[]{:S(2)}) async-start(bf16[4,2,51200]{2,1,0:T(2,128)(2,1)} %reshape.342), calls=%async_computation.1 | async-start | bytes 1638400 | tf_op jit(solution)/shard_map/all_to_all | solution.py:90
  153.8 5.3 %copy-start.1 = (bf16[256,2304]{1,0:T(8,128)(2,1)S(1)}, bf16[256,2304]{1,0:T(8,128)(2,1)}, u32[]{:S(2)}) copy-start(bf16[256,2304]{1,0:T(8,128)(2,1)} %param.8) | copy-start | bytes 3538948
  170.8 2.6 %copy-start.3 = (f32[2304]{0:T(1024)S(1)}, f32[2304]{0:T(1024)}, u32[]{:S(2)}) copy-start(f32[2304]{0:T(1024)} %get-tuple-element.8) | copy-start | bytes 27652
  170.8 2.6 %copy-start.4 = (f32[2304]{0:T(1024)S(1)}, f32[2304]{0:T(1024)}, u32[]{:S(2)}) copy-start(f32[2304]{0:T(1024)} %get-tuple-element.9) | copy-start | bytes 27652
  170.8 2.6 %copy-start.5 = (f32[2304]{0:T(1024)S(1)}, f32[2304]{0:T(1024)}, u32[]{:S(2)}) copy-start(f32[2304]{0:T(1024)} %get-tuple-element.10) | copy-start | bytes 27652
  170.8 2.6 %copy-start.6 = (f32[2304]{0:T(1024)S(1)}, f32[2304]{0:T(1024)}, u32[]{:S(2)}) copy-start(f32[2304]{0:T(1024)} %get-tuple-element.11) | copy-start | bytes 27652
  170.8 2.6 %copy-start.9 = (pred[256]{0:T(512)(128)(4,1)S(1)}, pred[256]{0:T(512)(128)(4,1)}, u32[]{:S(2)}) copy-start(pred[256]{0:T(512)(128)(4,1)} %get-tuple-element.26) | copy-start | bytes 772
  170.8 2.6 %copy-start.10 = (pred[256]{0:T(512)(128)(4,1)S(1)}, pred[256]{0:T(512)(128)(4,1)}, u32[]{:S(2)}) copy-start(pred[256]{0:T(512)(128)(4,1)} %get-tuple-element.27) | copy-start | bytes 772
  171.2 2.2 %collective-permute-start = (bf16[9,2304]{1,0:T(8,128)(2,1)S(1)}, bf16[9,2304]{1,0:T(8,128)(2,1)S(1)}, u32[]{:S(2)}, u32[]{:S(2)}) collective-permute-start(bf16[9,2304]{1,0:T(8,128)(2,1)S(1)} %slice.99), channel_id=1, source_target_pairs={{0,1},{1,4},{4,5},{5,8},{8,9},{9,12},{12,13},{2,3},{3,6},{6,7},{7,... | collective-permute-start | bytes 124424 | tf_op jit(solution)/shard_map/ppermute | solution.py:18
Sparse Core Ops, SparseCore 0:
  8.9 18.8 all-gather.4
  29.3 17.2 all-gather.2
where the time goes:
time: 185 us; the launch traced here: 184 us
  local copies, waits for them, and re-layouts  87.4 us (47%)
  other arithmetic  19.6 us (11%)
  matrix products  17.6 us (10%)
  starting transfers between devices  16 us (9%)
  blocking collectives  15.1 us (8%)
  waiting for transfers between devices  14.7 us (8%)
  between operations  13.8 us (7%)
    gather x2, local copies, waits for them, and re-layouts, shards(): found = (flat_codes[asked], flat_scales[asked])  30.2 us
    gather x1, local copies, waits for them, and re-layouts, shards(): stored = row_place[row_ids.reshape(requests)]  11.8 us
    all_to_all x2, other arithmetic, shards(): lax.all_to_all(found_rows.reshape(mem_count, capacity * row_width), 'mem'...  11.2 us
    all_gather x1, blocking collectives, shards(): whole_memory = lax.all_gather(memory, 'tp', axis=1, tiled=True)  9.45 us
    scatter x1, local copies, waits for them, and re-layouts, shards(): outgoing = jnp.zeros((mem_count * capacity,), jnp.int32).at[slot_index].s...  8.63 us
    all_to_all x1, waiting for transfers between devices, shards(): lax.all_to_all(found_rows.reshape(mem_count, capacity * row_width), 'mem'...  7.89 us
    unnamed x29, local copies, waits for them, and re-layouts  7.28 us
    dot_general x1, matrix products, decode_rows(): jnp.dot(flat_codes * flat_scales, hadamard_block(), precision=lax.Precisi...  6.95 us
  transfers between devices with their start and end apart: 6, of which 3 were waited for; matrix products, arithmetic and copies ran while one was open for 60% of the time, Pallas kernels for 0%

commit v1 on v0

v1 whole, which is shorter than its diff:
```python
import functools

import jax
import jax.numpy as jnp
from jax import lax
from jax.experimental import pallas as pl
from jax.experimental.pallas import tpu as pltpu
from jax.sharding import PartitionSpec as P

D = 4608
KERNEL = 4
DILATION = 3
SEQS = 4
EPSILON = 1e-06
RIM = 16
LANES = 128

F32 = jnp.float32
BF16 = jnp.bfloat16
I32 = jnp.int32


def iota(shape, axis):
    return lax.broadcasted_iota(I32, shape, axis)


def dot(a, b):
    return jnp.dot(a, b, preferred_element_type=F32)


def dot_nt(a, b, precision=None):
    return lax.dot_general(
        a, b, (((1,), (1,)), ((), ())), precision=precision, preferred_element_type=F32
    )


def unit(n, dtype):
    return (iota((n, n), 0) == iota((n, n), 1)).astype(F32).astype(dtype)


def to_bf16(x):
    return x.astype(F32).astype(BF16)


def flipped(ids):
    eye = unit(ids.shape[1], BF16)
    return (dot_nt(eye, to_bf16(ids >> 8)) * 256.0 + dot_nt(eye, to_bf16(ids & 255))).astype(I32)


def place_kernel(ids_ref, place_ref, out_ref):
    ids = ids_ref[...]
    place = place_ref[...]
    heads = ids.shape[1]
    rows = place.shape[0]
    eye = unit(LANES, BF16)
    table = jnp.concatenate(
        [dot_nt(eye, to_bf16(place >> 8)), dot_nt(eye, to_bf16(place & 255))], axis=0
    ).astype(BF16)
    turned = flipped(ids)
    for head in range(heads):
        row = turned[head : head + 1, :]
        hot = to_bf16(iota((rows, row.shape[1]), 0) == (row >> 7))
        both = dot(table, hot)
        value = both[:LANES] * 256.0 + both[LANES:]
        chosen = jnp.where(iota(value.shape, 0) == (row & 127), value, 0.0)
        out_ref[head : head + 1, :] = jnp.sum(chosen, axis=0, keepdims=True).astype(I32)


def decode_kernel(codes_ref, scales_ref, out_ref):
    width = codes_ref.shape[-1]
    blocks = scales_ref.shape[-1]
    wide = out_ref.shape[-1]
    offset = (pl.program_id(0) * width) % LANES
    spread = to_bf16((iota((blocks, width), 1) >> 4) == iota((blocks, width), 0))
    scaled = codes_ref[0].astype(F32) * dot(scales_ref[0], spread)
    upper = scaled.astype(BF16)
    lower = (scaled - upper.astype(F32)).astype(BF16)
    entry = iota((width, wide), 0)
    column = iota((width, wide), 1) - offset
    parity = entry & column & 15
    parity = parity ^ (parity >> 2)
    parity = (parity ^ (parity >> 1)) & 1
    same = (entry >> 4) == (column >> 4)
    rotation = jnp.where(same, 0.25 - 0.5 * parity.astype(F32), 0.0).astype(BF16)
    out_ref[0] = (dot(upper, rotation) + dot(lower, rotation)).astype(BF16)


def pick_kernel(width, base_ref, ids_ref, table_ref, out_ref, total):
    heads, tokens = ids_ref.shape[1:]
    rows = table_ref.shape[1]
    wide = table_ref.shape[2]
    local = flipped(ids_ref[0]) - base_ref[0]
    total[...] = jnp.zeros_like(total)
    for head in range(heads):
        hot = to_bf16(iota((tokens, rows), 1) == local[:, head : head + 1])
        start = head * width // LANES * LANES
        total[:, start : start + wide] += dot(hot, table_ref[head])
    out_ref[...] = total[:, : out_ref.shape[1]].astype(BF16)


def project_kernel(count, where_ref, *refs):
    halos = refs[:count]
    pieces = refs[count : 2 * count]
    hidden_halo, hidden = refs[2 * count : 2 * count + 2]
    weights = refs[2 * count + 2 : 2 * count + 6]
    value_ref, stats_ref = refs[2 * count + 6 : 2 * count + 8]
    held, memory, sems = refs[2 * count + 8 :]
    half = value_ref.shape[-1]
    depth = memory.shape[-1]
    rep = where_ref[0]
    tp = where_ref[1]
    copies = []
    for far in range(2):
        slot = rep if far == 0 else 1 - rep
        for which in range(2):
            copy = pltpu.make_async_copy(
                weights[2 * far + which], held.at[slot, which], sems.at[2 * far + which]
            )
            copy.start()
            copies.append(copy)
    for s in range(count):
        memory[s, :RIM] = halos[s][...]
        memory[s, RIM:] = pieces[s][...]
    for copy in copies:
        copy.wait()
    sums = [0.0] * 4
    for j in range(2):
        fields = []
        for which in range(2):
            field = None
            for s in range(count):
                at = pl.multiple_of(lax.rem(tp + count - s, count) * depth, depth)
                part = dot(memory[s], held[j, which, pl.ds(at, depth), :])
                field = part if field is None else field + part
            fields.append(field)
        keys, values = fields
        span = slice(j * half, (j + 1) * half)
        states = jnp.concatenate([hidden_halo[:, span], hidden[:, span]], axis=0).astype(F32)
        terms = (states * states, keys * keys, states * keys, values * values)
        sums = [a + jnp.sum(t, axis=1, keepdims=True) for a, t in zip(sums, terms)]
        value_ref[j] = values
    rows = memory.shape[1]
    lane = iota((rows, 8), 1)
    packed = jnp.zeros((rows, 8), F32)
    for k in range(4):
        packed = jnp.where(lane == k, sums[k], packed)
    stats_ref[...] = dot_nt(unit(8, F32), packed, lax.Precision.HIGHEST)


def finish_kernel(count, keep_ref, *refs):
    stats = refs[:count]
    value_ref, hidden_ref, taps_ref, out_ref, columns, normed = refs[count:]
    rows = normed.shape[0]
    tokens = out_ref.shape[0]

    @pl.when(pl.program_id(0) == 0)
    def _():
        total = stats[0][...]
        for other in stats[1:]:
            total = total + other[...]
        inverse_states = lax.rsqrt(total[0:1] / D + EPSILON)
        inverse_keys = lax.rsqrt(total[1:2] / D + EPSILON)
        gate = jax.nn.sigmoid(total[2:3] * inverse_states * inverse_keys / D**0.5)
        factor = gate * lax.rsqrt(gate * gate * total[3:4] / D + EPSILON)
        factor = jnp.where((iota(factor.shape, 1) < RIM) & (keep_ref[0] == 0), 0.0, factor)
        line = iota(total.shape, 0)
        both = jnp.where(line == 0, gate, jnp.where(line == 1, factor, 0.0))
        columns[...] = dot_nt(unit(rows, F32), both, lax.Precision.HIGHEST)

    values = value_ref[...]
    normed[...] = values * columns[:, 1:2]
    conv = None
    for tap in range(KERNEL):
        lag = DILATION * tap
        term = taps_ref[tap : tap + 1, :] * normed[RIM - lag : RIM - lag + tokens, :]
        conv = term if conv is None else conv + term
    gated = values[RIM:] * columns[RIM:, 0:1]
    out_ref[...] = (hidden_ref[...].astype(F32) + jax.nn.silu(conv) + gated).astype(BF16)


def whole(array):
    return pl.BlockSpec(array.shape, lambda *_: (0,) * array.ndim)


def shards(
    hidden, row_ids, row_place, table_codes, table_scales, key_weight, value_weight, conv_weight
):
    mems = lax.axis_size("mem")
    tps = lax.axis_size("tp")
    reps = lax.axis_size("rep")
    blocks = mems * reps
    tokens, heads = row_ids.shape
    rows, width = table_codes.shape[1:]
    depth = heads * width
    entries, half = key_weight.shape
    seq_length = tokens * blocks // SEQS
    assert reps == 2 and seq_length % tokens == 0 and row_place.shape[0] % LANES == 0
    block = lax.axis_index(("mem", "rep"))
    smem = pl.BlockSpec(memory_space=pltpu.SMEM)
    anywhere = pl.BlockSpec(memory_space=pl.ANY)

    def shift(x, axis, by, wrap):
        size = lax.axis_size(axis)
        pairs = [
            (i, (i + by) % size) for i in range(size) if wrap or 0 <= i + by < size
        ]
        return lax.ppermute(x, axis, pairs)

    stored = pl.pallas_call(
        place_kernel,
        out_shape=jax.ShapeDtypeStruct((heads, tokens), I32),
        name="place_rows",
    )(row_ids, row_place.reshape(-1, LANES))
    asked = lax.all_gather(stored, "mem", axis=0)

    other_key = shift(key_weight, "rep", 1, True)
    other_value = shift(value_weight, "rep", 1, True)
    hidden_halo = shift(hidden[tokens - RIM :], ("mem", "rep"), 1, False)

    wide = 2 * LANES
    decoded = pl.pallas_call(
        decode_kernel,
        grid=(heads,),
        in_specs=[
            pl.BlockSpec((1, rows, width), lambda h: (h, 0, 0)),
            pl.BlockSpec((1, rows, table_scales.shape[2]), lambda h: (h, 0, 0)),
        ],
        out_specs=pl.BlockSpec((1, rows, wide), lambda h: (h, 0, 0)),
        out_shape=jax.ShapeDtypeStruct((heads, rows, wide), BF16),
        name="decode_tables",
    )(table_codes, table_scales)

    base = (lax.axis_index("mem") * rows).astype(I32).reshape(1)
    total_width = ((heads - 1) * width // LANES) * LANES + wide
    total_width = max(total_width, depth)
    partial = pl.pallas_call(
        functools.partial(pick_kernel, width),
        grid=(mems,),
        in_specs=[
            smem,
            pl.BlockSpec((1, heads, tokens), lambda m: (m, 0, 0)),
            whole(decoded),
        ],
        out_specs=pl.BlockSpec((tokens, depth), lambda m: (m, 0)),
        out_shape=jax.ShapeDtypeStruct((mems * tokens, depth), BF16),
        scratch_shapes=[pltpu.VMEM((tokens, total_width), F32)],
        compiler_params=pltpu.CompilerParams(vmem_limit_bytes=40 << 20),
        name="pick_rows",
    )(base, asked, decoded)
    memory = lax.psum_scatter(partial, "mem", scatter_dimension=0, tiled=True)

    halo = shift(memory[tokens - RIM :], ("mem", "rep"), 1, False)
    pieces = [memory] + [shift(memory, "tp", s, True) for s in range(1, tps)]
    halos = [halo] + [shift(halo, "tp", s, True) for s in range(1, tps)]

    where = jnp.stack([lax.axis_index("rep"), lax.axis_index("tp")]).astype(I32)
    extended = tokens + RIM
    operands = (*halos, *pieces, hidden_halo, hidden)
    values, stats = pl.pallas_call(
        functools.partial(project_kernel, tps),
        in_specs=[smem] + [pl.BlockSpec(memory_space=pltpu.VMEM)] * len(operands) + [anywhere] * 4,
        out_shape=(
            jax.ShapeDtypeStruct((2, extended, half), F32),
            jax.ShapeDtypeStruct((8, extended), F32),
        ),
        scratch_shapes=[
            pltpu.VMEM((2, 2, entries, half), BF16),
            pltpu.VMEM((tps, extended, depth), BF16),
            pltpu.SemaphoreType.DMA((4,)),
        ],
        compiler_params=pltpu.CompilerParams(vmem_limit_bytes=56 << 20),
        name="project",
    )(where, *operands, key_weight, value_weight, other_key, other_value)

    all_stats = [stats] + [shift(stats, "tp", s, True) for s in range(1, tps)]
    keep = (block * tokens % seq_length != 0).astype(I32).reshape(1)
    aligned = half % LANES == 0
    if aligned:
        step = next(c for c in (384, 256, 128) if half % c == 0)
        split = lambda x: x
        spec = lambda r: pl.BlockSpec((r, step), lambda i: (0, i))
        out_shape = jax.ShapeDtypeStruct((tokens, 2 * half), BF16)
    else:
        step = half
        split = lambda x: jnp.stack([x[:, :half], x[:, half:]])
        spec = lambda r: pl.BlockSpec((None, r, step), lambda i: (i, 0, 0))
        out_shape = jax.ShapeDtypeStruct((2, tokens, half), BF16)
    per = half // step
    out = pl.pallas_call(
        functools.partial(finish_kernel, tps),
        grid=(2 * per,),
        in_specs=[smem]
        + [whole(stats)] * tps
        + [
            pl.BlockSpec((None, extended, step), lambda i: (i // per, 0, i % per)),
            spec(tokens),
            spec(KERNEL),
        ],
        out_specs=spec(tokens),
        out_shape=out_shape,
        scratch_shapes=[pltpu.VMEM((extended, 8), F32), pltpu.VMEM((extended, step), F32)],
        compiler_params=pltpu.CompilerParams(vmem_limit_bytes=40 << 20),
        name="finish",
    )(keep, *all_stats, values, split(hidden), split(conv_weight))
    return out if aligned else jnp.concatenate([out[0], out[1]], axis=1)


def solution(mesh):
    in_specs = (
        P(("parts", "mem", "rep"), "tp"),
        P(("parts", "mem", "rep"), "tp"),
        P("parts"),
        P(("parts", "tp"), "mem", None),
        P(("parts", "tp"), "mem", None),
        P(None, ("tp", "rep")),
        P(None, ("tp", "rep")),
        P(None, "tp"),
    )
    out_specs = P(("parts", "mem", "rep"), "tp")
    return jax.shard_map(shards, mesh=mesh, in_specs=in_specs, out_specs=out_specs, check_vma=False)
```

time: 185 us -> 123 us (0.66)
  local copies, waits for them, and re-layouts: 87.4 us -> 14 us
  Pallas kernels: 0 us -> 34.3 us
  waiting for transfers between devices: 14.7 us -> 37.5 us
  other arithmetic: 19.6 us -> 0.59 us
  matrix products: 17.6 us -> 0 us
  starting transfers between devices: 16 us -> 7.1 us
    gather x5 -> x0, local copies, waits for them, and re-layouts: 54.3 us -> none  [the longest x2 30.2 us: shards(): found = (flat_codes[asked], flat_scales[asked])]
    pallas_call x0 -> x5, Pallas kernels: none -> 34.3 us  [the longest x1 12.1 us: shards(): pl.pallas_call(functools.partial(project_kernel, tps), in_specs=[smem] +...]
    reduce_scatter x0 -> x1, waiting for transfers between devices: none -> 31.8 us  [shards(): memory = lax.psum_scatter(partial, 'mem', scatter_dimension=0, tiled=True)]
    dot_general x3 -> x0, matrix products: 17.6 us -> none  [the longest x1 6.95 us: decode_rows(): jnp.dot(flat_codes * flat_scales, hadamard_block(), precision=lax.Precisi...]
    all_to_all x3 -> x0, starting transfers between devices: 14.6 us -> none  [the longest x1 6.32 us: shards(): lax.all_to_all(outgoing, 'mem', split_axis=0, concat_axis=0, tiled=True)]
    all_to_all x4 -> x0, other arithmetic: 12.5 us -> none  [the longest x2 11.2 us: shards(): lax.all_to_all(found_rows.reshape(mem_count, capacity * row_width), 'mem'...]
    all_to_all x3 -> x0, waiting for transfers between devices: 12.4 us -> none  [the longest x1 7.89 us: shards(): lax.all_to_all(found_rows.reshape(mem_count, capacity * row_width), 'mem'...]
    scatter x1 -> x0, local copies, waits for them, and re-layouts: 8.63 us -> none  [shards(): outgoing = jnp.zeros((mem_count * capacity,), jnp.int32).at[slot_index].s...]
  transfers between devices with their start and end apart: 6 -> 8, of which waited for: 3 -> 3; matrix products, arithmetic and copies ran while one was open for 60% -> 2% of each run, Pallas kernels for 0% -> 0%
where the time goes in v1:
time: 123 us; the launch traced here: 122 us
  waiting for transfers between devices  37.5 us (30%)
  Pallas kernels  34.3 us (28%)
  blocking collectives  15 us (12%)
  local copies, waits for them, and re-layouts  14 us (11%)
  between operations  13.5 us (11%)
  starting transfers between devices  7.1 us (6%)
    reduce_scatter x1, waiting for transfers between devices, shards(): memory = lax.psum_scatter(partial, 'mem', scatter_dimension=0, tiled=True)  31.8 us
    all_gather x1, blocking collectives, shards(): asked = lax.all_gather(stored, 'mem', axis=0)  15 us
    unnamed x23, local copies, waits for them, and re-layouts  12.3 us
    pallas_call x1, Pallas kernels, shards(): pl.pallas_call(functools.partial(project_kernel, tps), in_specs=[smem] +...  12.1 us
    pallas_call x1, Pallas kernels, shards(): pl.pallas_call(decode_kernel, grid=(heads,), in_specs=[pl.BlockSpec((1, r...  9.08 us
    ppermute x7, starting transfers between devices, shift(): return lax.ppermute(x, axis, pairs)  7.1 us
    pallas_call x1, Pallas kernels, shards(): pl.pallas_call(functools.partial(pick_kernel, width), grid=(mems,), in_sp...  6.62 us
    ppermute x7, waiting for transfers between devices, shift(): return lax.ppermute(x, axis, pairs)  5.67 us
  transfers between devices with their start and end apart: 8, of which 3 were waited for; matrix products, arithmetic and copies ran while one was open for 2% of the time, Pallas kernels for 0%

profile of v1, /device:TPU:0, one launch (start us, length us, event | category | flops | bytes accessed | tf_op | source)
XLA Modules:
  0.0 121.9 jit_solution(14678483911792096750)
XLA Ops:
  6.5 0.0 reduce-scatter.2.cloned.1.call-start
  6.5 1.5 %copy.9.ids_ref = s32[256,8]{1,0:T(8,128)} copy(s32[256,8]{0,1:T(8,128)} %param.9) | data formatting | bytes 16384 | tf_op args[1]
  8.1 2.1 %place_rows.1 = s32[8,256]{1,0:T(8,128)} custom-call(s32[256,8]{1,0:T(8,128)} %copy.9.ids_ref, s32[32,128]{1,0:T(8,128)} %bitcast.7), custom_call_target="tpu_custom_call" | custom-call | tf_op jit(solution)/shard_map/place_rows/pallas_call | solution.py:209
  10.2 15.0 %all-gather = s32[32,256]{1,0:T(8,128)S(1)} all-gather(s32[8,256]{1,0:T(8,128)} %place_rows.1), channel_id=2, replica_groups=mesh['parts'=2,'mem'=4,'tp'=2,'rep'=2] {'mem'}, dimensions={0}, use_global_device_ids=true | all-gather | bytes 40960 | tf_op jit(solution)/shard_map/all_gather | solution.py:214
  25.2 3.6 %copy.10.codes_ref = bf16[8,1024,80]{2,1,0:T(8,128)(2,1)} copy(bf16[8,1024,80]{1,2,0:T(8,128)(2,1)} %param.11) | data formatting | bytes 2621440 | tf_op args[3]
  28.8 0.0 copy-done.6
  28.8 1.9 %copy.11.scales_ref = bf16[8,1024,5]{2,1,0:T(8,128)(2,1)} copy(bf16[8,1024,5]{1,0,2:T(8,128)(2,1)S(1)} %copy-done.6) | data formatting | bytes 163840 | tf_op args[4]
  30.7 9.1 %decode_tables.1.table_ref = bf16[8,1024,256]{2,1,0:T(8,128)(2,1)} custom-call(bf16[8,1024,80]{2,1,0:T(8,128)(2,1)} %copy.10.codes_ref, bf16[8,1024,5]{2,1,0:T(8,128)(2,1)} %copy.11.scales_ref), custom_call_target="tpu_custom_call" | custom-call | tf_op jit(solution)/shard_map/decode_tables/pallas_call | solution.py:221
  39.7 0.0 copy-start
  39.7 2.2 %copy-done = bf16[8,1024,256]{2,1,0:T(8,128)(2,1)S(1)} copy-done((bf16[8,1024,256]{2,1,0:T(8,128)(2,1)S(1)}, bf16[8,1024,256]{2,1,0:T(8,128)(2,1)}, u32[]{:S(2)}) %copy-start) | copy-done | bytes 4194328
  41.9 6.6 %pick_rows.1 = bf16[1024,640]{1,0:T(8,128)(2,1)} custom-call(s32[1]{0:T(128)} %bitcast.3.base_ref, s32[4,8,256]{2,1,0:T(8,128)S(1)} %bitcast.6, bf16[8,1024,256]{2,1,0:T(8,128)(2,1)S(1)} %copy-done), custom_call_target="tpu_custom_call" | custom-call | tf_op jit(solution)/shard_map/pick_rows/pallas_call | solution.py:236
  48.6 0.0 reduce-scatter.2.cloned.1.call-update
  48.6 0.1 collective-permute-start.4
  48.7 0.5 collective-permute-start.5
  49.2 31.8 %reduce-scatter.2.cloned.1.call-done.refs_2_ = bf16[256,640]{1,0:T(8,128)(2,1)} async-done(((bf16[1024,640]{1,0:T(8,128)(2,1)}), bf16[256,640]{1,0:T(8,128)(2,1)}) %reduce-scatter.2.cloned.1.call-update) | async-done | bytes 327696 | tf_op jit(solution)/shard_map/reduce_scatter | solution.py:250
  81.0 1.5 %collective-permute-start.2 = (bf16[256,640]{1,0:T(8,128)(2,1)}, bf16[256,640]{1,0:T(8,128)(2,1)S(1)}, u32[]{:S(2)}, u32[]{:S(2)}) collective-permute-start(bf16[256,640]{1,0:T(8,128)(2,1)} %reduce-scatter.2.cloned.1.call-done.refs_2_), channel_id=1, source_target_pairs={{0,2},{2,0},{1,3},{3,1},{4,6},{6,4},{5,7},{7,5},{8,10},{10,8},{9,1... | collective-permute-start | bytes 983048 | tf_op jit(solution)/shard_map/ppermute | solution.py:207
  82.4 0.8 slice.8
  83.2 1.3 %collective-permute-start = (bf16[16,640]{1,0:T(8,128)(2,1)S(1)}, bf16[16,640]{1,0:T(8,128)(2,1)S(1)}, u32[]{:S(2)}, u32[]{:S(2)}) collective-permute-start(bf16[16,640]{1,0:T(8,128)(2,1)S(1)} %slice.8), channel_id=1, source_target_pairs={{0,1},{1,4},{4,5},{5,8},{8,9},{9,12},{12,13},{2,3},{3,6},{6,7},{7,... | collective-permute-start | bytes 61448 | tf_op jit(solution)/shard_map/ppermute | solution.py:207
  84.5 0.9 slice.7
  85.4 2.2 %collective-permute-start.3 = (bf16[16,2304]{1,0:T(8,128)(2,1)S(1)}, bf16[16,2304]{1,0:T(8,128)(2,1)S(1)}, u32[]{:S(2)}, u32[]{:S(2)}) collective-permute-start(bf16[16,2304]{1,0:T(8,128)(2,1)S(1)} %slice.7), channel_id=1, source_target_pairs={{0,1},{1,4},{4,5},{5,8},{8,9},{9,12},{12,13},{2,3},{3,6},{6,7},{7,... | collective-permute-start | bytes 221192 | tf_op jit(solution)/shard_map/ppermute | solution.py:207
  87.6 0.0 collective-permute-done.refs_0_
  87.6 0.0 copy-start.8
  87.6 0.6 collective-permute-start.1
  88.2 0.6 pad_add_fusion.where_ref
  88.8 0.0 copy-start.1
  88.8 0.0 copy-start.3
  88.8 0.0 collective-permute-done.3.refs_4_
  88.8 0.0 copy-start.7
  88.8 2.6 %collective-permute-done.1.refs_1_ = bf16[16,640]{1,0:T(8,128)(2,1)S(1)} collective-permute-done((bf16[16,640]{1,0:T(8,128)(2,1)S(1)}, bf16[16,640]{1,0:T(8,128)(2,1)S(1)}, u32[]{:S(2)}, u32[]{:S(2)}) %collective-permute-start.1) | collective-permute-done | bytes 20512 | tf_op jit(solution)/shard_map/ppermute | solution.py:207
  91.5 0.0 copy-start.9
  91.5 0.0 collective-permute-done.2.refs_3_
  91.5 0.0 copy-start.5
  91.5 0.0 collective-permute-done.4.refs_8_
  91.5 0.0 collective-permute-done.5.refs_9_
  91.5 0.0 copy-done.8
  91.5 0.0 copy-done.7
  91.5 0.6 copy-done.9
  92.1 0.1 copy-done.5
  92.2 12.1 %project.1 = (f32[2,272,1152]{2,1,0:T(8,128)}, f32[8,272]{1,0:T(8,128)}) custom-call(s32[2]{0:T(128)} %pad_add_fusion.where_ref, bf16[16,640]{1,0:T(8,128)(2,1)} %copy-done.8, bf16[16,640]{1,0:T(8,128)(2,1)} %copy-done.9, bf16[256,640]{1,0:T(8,128)(2,1)} %reduce-scatter.2.cloned.1.call-done.refs_2_, bf16[256,640]{1,0:T(8,128)(2,1)} %copy-done.5, ...), custom_call_target="tpu_custom_call" | custom-call | tf_op jit(solution)/shard_map/project/pallas_call | solution.py:259
  104.3 1.0 collective-permute-start.6
  105.3 3.0 %collective-permute-done.6.refs_1_ = f32[8,272]{1,0:T(8,128)S(1)} collective-permute-done((f32[8,272]{1,0:T(8,128)}, f32[8,272]{1,0:T(8,128)S(1)}, u32[]{:S(2)}, u32[]{:S(2)}) %collective-permute-start.6) | collective-permute-done | bytes 8736 | tf_op jit(solution)/shard_map/ppermute | solution.py:207
  108.3 0.0 copy-done.1
  108.3 0.0 copy-done.3
  108.3 0.0 copy-start.2
  108.3 1.7 %copy-done.2 = f32[2,272,1152]{2,1,0:T(8,128)S(1)} copy-done((f32[2,272,1152]{2,1,0:T(8,128)S(1)}, f32[2,272,1152]{2,1,0:T(8,128)}, u32[]{:S(2)}) %copy-start.2) | copy-done | bytes 2506776
  110.0 0.0 copy-start.4
  110.0 0.7 copy-done.4
  110.7 4.3 %finish.1 = bf16[256,2304]{1,0:T(8,128)(2,1)} custom-call(s32[1]{0:T(128)} %bitcast.keep_ref, f32[8,272]{1,0:T(8,128)S(1)} %copy-done.4, f32[8,272]{1,0:T(8,128)S(1)} %collective-permute-done.6.refs_1_, f32[2,272,1152]{2,1,0:T(8,128)S(1)} %copy-done.2, bf16[256,2304]{1,0:T(8,128)(2,1)S(1)} %copy-done.1, f32[4,2304]{1,0:T(4,128)S(1)} %copy-done.3), custom_call_target="tpu_custom_call" | custom-call | tf_op jit(solution)/shard_map/finish/pallas_call | solution.py:289
  (1 shorter events, 0.0 us)
Async XLA Ops:
  6.5 22.3 %copy-start.6 = (bf16[8,1024,5]{1,0,2:T(8,128)(2,1)S(1)}, bf16[8,1024,5]{1,0,2:T(8,128)(2,1)}, u32[]{:S(2)}) copy-start(bf16[8,1024,5]{1,0,2:T(8,128)(2,1)} %param.12) | copy-start | bytes 245764
  6.5 74.4 %reduce-scatter.2.cloned.1.call-start = ((), (), s32[]{:S(2)}) async-start(), calls=%async_computation.1 | async-start | bytes 1638400 | tf_op jit(solution)/shard_map/reduce_scatter | solution.py:250
  39.7 2.2 %copy-start = (bf16[8,1024,256]{2,1,0:T(8,128)(2,1)S(1)}, bf16[8,1024,256]{2,1,0:T(8,128)(2,1)}, u32[]{:S(2)}) copy-start(bf16[8,1024,256]{2,1,0:T(8,128)(2,1)} %decode_tables.1.table_ref) | copy-start | bytes 12582916
  48.6 42.9 %collective-permute-start.4 = (bf16[1280,1152]{1,0:T(8,128)(2,1)}, bf16[1280,1152]{1,0:T(8,128)(2,1)}, u32[]{:S(2)}, u32[]{:S(2)}) collective-permute-start(bf16[1280,1152]{1,0:T(8,128)(2,1)} %refs_6_.1), channel_id=1, source_target_pairs={{0,1},{1,0},{2,3},{3,2},{4,5},{5,4},{6,7},{7,6},{8,9},{9,8},{10,11... | collective-permute-start | bytes 8847368 | tf_op jit(solution)/shard_map/ppermute | solution.py:207
  48.7 42.8 %collective-permute-start.5 = (bf16[1280,1152]{1,0:T(8,128)(2,1)}, bf16[1280,1152]{1,0:T(8,128)(2,1)}, u32[]{:S(2)}, u32[]{:S(2)}) collective-permute-start(bf16[1280,1152]{1,0:T(8,128)(2,1)} %refs_7_.1), channel_id=1, source_target_pairs={{0,1},{1,0},{2,3},{3,2},{4,5},{5,4},{6,7},{7,6},{8,9},{9,8},{10,11... | collective-permute-start | bytes 8847368 | tf_op jit(solution)/shard_map/ppermute | solution.py:207
  81.0 10.5 %collective-permute-start.2 = (bf16[256,640]{1,0:T(8,128)(2,1)}, bf16[256,640]{1,0:T(8,128)(2,1)S(1)}, u32[]{:S(2)}, u32[]{:S(2)}) collective-permute-start(bf16[256,640]{1,0:T(8,128)(2,1)} %reduce-scatter.2.cloned.1.call-done.refs_2_), channel_id=1, source_target_pairs={{0,2},{2,0},{1,3},{3,1},{4,6},{6,4},{5,7},{7,5},{8,10},{10,8},{9,1... | collective-permute-start | bytes 983048 | tf_op jit(solution)/shard_map/ppermute | solution.py:207
  83.2 4.4 %collective-permute-start = (bf16[16,640]{1,0:T(8,128)(2,1)S(1)}, bf16[16,640]{1,0:T(8,128)(2,1)S(1)}, u32[]{:S(2)}, u32[]{:S(2)}) collective-permute-start(bf16[16,640]{1,0:T(8,128)(2,1)S(1)} %slice.8), channel_id=1, source_target_pairs={{0,1},{1,4},{4,5},{5,8},{8,9},{9,12},{12,13},{2,3},{3,6},{6,7},{7,... | collective-permute-start | bytes 61448 | tf_op jit(solution)/shard_map/ppermute | solution.py:207
  85.4 3.5 %collective-permute-start.3 = (bf16[16,2304]{1,0:T(8,128)(2,1)S(1)}, bf16[16,2304]{1,0:T(8,128)(2,1)S(1)}, u32[]{:S(2)}, u32[]{:S(2)}) collective-permute-start(bf16[16,2304]{1,0:T(8,128)(2,1)S(1)} %slice.7), channel_id=1, source_target_pairs={{0,1},{1,4},{4,5},{5,8},{8,9},{9,12},{12,13},{2,3},{3,6},{6,7},{7,... | collective-permute-start | bytes 221192 | tf_op jit(solution)/shard_map/ppermute | solution.py:207
  87.6 3.9 %copy-start.8 = (bf16[16,640]{1,0:T(8,128)(2,1)}, bf16[16,640]{1,0:T(8,128)(2,1)S(1)}, u32[]{:S(2)}) copy-start(bf16[16,640]{1,0:T(8,128)(2,1)S(1)} %collective-permute-done.refs_0_) | copy-start | bytes 61444
  87.6 3.8 %collective-permute-start.1 = (bf16[16,640]{1,0:T(8,128)(2,1)S(1)}, bf16[16,640]{1,0:T(8,128)(2,1)S(1)}, u32[]{:S(2)}, u32[]{:S(2)}) collective-permute-start(bf16[16,640]{1,0:T(8,128)(2,1)S(1)} %collective-permute-done.refs_0_), channel_id=1, source_target_pairs={{0,2},{2,0},{1,3},{3,1},{4,6},{6,4},{5,7},{7,5},{8,10},{10,8},{9,1... | collective-permute-start | bytes 61448 | tf_op jit(solution)/shard_map/ppermute | solution.py:207
  88.8 19.5 %copy-start.1 = (bf16[256,2304]{1,0:T(8,128)(2,1)S(1)}, bf16[256,2304]{1,0:T(8,128)(2,1)}, u32[]{:S(2)}) copy-start(bf16[256,2304]{1,0:T(8,128)(2,1)} %refs_3_.1) | copy-start | bytes 3538948
  88.8 19.5 %copy-start.3 = (f32[4,2304]{1,0:T(4,128)S(1)}, f32[4,2304]{1,0:T(4,128)}, u32[]{:S(2)}) copy-start(f32[4,2304]{1,0:T(4,128)} %refs_4_.1) | copy-start | bytes 110596
  88.8 2.7 %copy-start.7 = (bf16[16,2304]{1,0:T(8,128)(2,1)}, bf16[16,2304]{1,0:T(8,128)(2,1)S(1)}, u32[]{:S(2)}) copy-start(bf16[16,2304]{1,0:T(8,128)(2,1)S(1)} %collective-permute-done.3.refs_4_) | copy-start | bytes 221188
  91.5 0.6 copy-start.9
  91.5 0.7 copy-start.5
  104.3 4.0 %collective-permute-start.6 = (f32[8,272]{1,0:T(8,128)}, f32[8,272]{1,0:T(8,128)S(1)}, u32[]{:S(2)}, u32[]{:S(2)}) collective-permute-start(f32[8,272]{1,0:T(8,128)} %get-tuple-element.7.refs_0_), channel_id=1, source_target_pairs={{0,2},{2,0},{1,3},{3,1},{4,6},{6,4},{5,7},{7,5},{8,10},{10,8},{9,1... | collective-permute-start | bytes 26120 | tf_op jit(solution)/shard_map/ppermute | solution.py:207
  108.3 1.7 %copy-start.2 = (f32[2,272,1152]{2,1,0:T(8,128)S(1)}, f32[2,272,1152]{2,1,0:T(8,128)}, u32[]{:S(2)}) copy-start(f32[2,272,1152]{2,1,0:T(8,128)} %get-tuple-element.8.refs_2_) | copy-start | bytes 7520260
  110.0 0.7 copy-start.4
Sparse Core Ops, SparseCore 0:
  48.7 32.2 reduce-scatter.1

commit v2 on v1

--- a/solution.py
+++ b/solution.py
@@ -42,24 +42,17 @@
     return x.astype(F32).astype(BF16)
 
 
-def flipped(ids):
-    eye = unit(ids.shape[1], BF16)
-    return (dot_nt(eye, to_bf16(ids >> 8)) * 256.0 + dot_nt(eye, to_bf16(ids & 255))).astype(I32)
-
-
 def place_kernel(ids_ref, place_ref, out_ref):
-    ids = ids_ref[...]
     place = place_ref[...]
-    heads = ids.shape[1]
     rows = place.shape[0]
+    heads, tokens = ids_ref.shape
     eye = unit(LANES, BF16)
     table = jnp.concatenate(
         [dot_nt(eye, to_bf16(place >> 8)), dot_nt(eye, to_bf16(place & 255))], axis=0
     ).astype(BF16)
-    turned = flipped(ids)
     for head in range(heads):
-        row = turned[head : head + 1, :]
-        hot = to_bf16(iota((rows, row.shape[1]), 0) == (row >> 7))
+        row = ids_ref[head : head + 1, :]
+        hot = to_bf16(iota((rows, tokens), 0) == (row >> 7))
         both = dot(table, hot)
         value = both[:LANES] * 256.0 + both[LANES:]
         chosen = jnp.where(iota(value.shape, 0) == (row & 127), value, 0.0)
@@ -67,35 +60,52 @@
 
 
 def decode_kernel(codes_ref, scales_ref, out_ref):
-    width = codes_ref.shape[-1]
-    blocks = scales_ref.shape[-1]
-    wide = out_ref.shape[-1]
-    offset = (pl.program_id(0) * width) % LANES
-    spread = to_bf16((iota((blocks, width), 1) >> 4) == iota((blocks, width), 0))
-    scaled = codes_ref[0].astype(F32) * dot(scales_ref[0], spread)
-    upper = scaled.astype(BF16)
-    lower = (scaled - upper.astype(F32)).astype(BF16)
-    entry = iota((width, wide), 0)
-    column = iota((width, wide), 1) - offset
+    heads, width, rows = codes_ref.shape
+    blocks = scales_ref.shape[0]
+    entry = iota((width, 2 * width), 0)
+    column = iota((width, 2 * width), 1)
+    column = jnp.where(column < width, column, column - width)
     parity = entry & column & 15
     parity = parity ^ (parity >> 2)
     parity = (parity ^ (parity >> 1)) & 1
     same = (entry >> 4) == (column >> 4)
     rotation = jnp.where(same, 0.25 - 0.5 * parity.astype(F32), 0.0).astype(BF16)
-    out_ref[0] = (dot(upper, rotation) + dot(lower, rotation)).astype(BF16)
-
-
-def pick_kernel(width, base_ref, ids_ref, table_ref, out_ref, total):
-    heads, tokens = ids_ref.shape[1:]
-    rows = table_ref.shape[1]
-    wide = table_ref.shape[2]
-    local = flipped(ids_ref[0]) - base_ref[0]
-    total[...] = jnp.zeros_like(total)
     for head in range(heads):
-        hot = to_bf16(iota((tokens, rows), 1) == local[:, head : head + 1])
-        start = head * width // LANES * LANES
-        total[:, start : start + wide] += dot(hot, table_ref[head])
-    out_ref[...] = total[:, : out_ref.shape[1]].astype(BF16)
+        factors = jnp.concatenate(
+            [
+                jnp.broadcast_to(scales_ref[b, head : head + 1, :].astype(F32), (16, rows))
+                for b in range(blocks)
+            ],
+            axis=0,
+        )
+        scaled = codes_ref[head].astype(F32) * factors
+        upper = scaled.astype(BF16)
+        lower = (scaled - upper.astype(F32)).astype(BF16)
+        out_ref[head] = dot(rotation, jnp.concatenate([upper, lower], axis=0)).astype(BF16)
+
+
+def pick_kernel(count, scalars_ref, *refs):
+    pieces = refs[:count]
+    table_ref, out_ref, stack = refs[count:]
+    heads, width, rows = table_ref.shape
+    tokens = out_ref.shape[0]
+    step = pl.program_id(0)
+    if count > 1:
+
+        @pl.when(step == 0)
+        def _():
+            for k in range(count):
+                stack[k] = pieces[k][...]
+
+        ids = stack[scalars_ref[1 + step]]
+    else:
+        ids = pieces[0][step]
+    local = ids - scalars_ref[0]
+    found = []
+    for head in range(heads):
+        hot = to_bf16(iota((rows, tokens), 0) == local[head : head + 1, :])
+        found.append(dot(table_ref[head], hot))
+    out_ref[...] = jnp.concatenate(found, axis=0).T.astype(BF16)
 
 
 def project_kernel(count, where_ref, *refs):
@@ -104,41 +114,33 @@
     hidden_halo, hidden = refs[2 * count : 2 * count + 2]
     weights = refs[2 * count + 2 : 2 * count + 6]
     value_ref, stats_ref = refs[2 * count + 6 : 2 * count + 8]
-    held, memory, sems = refs[2 * count + 8 :]
+    memory, states = refs[2 * count + 8 :]
     half = value_ref.shape[-1]
     depth = memory.shape[-1]
     rep = where_ref[0]
     tp = where_ref[1]
-    copies = []
-    for far in range(2):
-        slot = rep if far == 0 else 1 - rep
-        for which in range(2):
-            copy = pltpu.make_async_copy(
-                weights[2 * far + which], held.at[slot, which], sems.at[2 * far + which]
-            )
-            copy.start()
-            copies.append(copy)
     for s in range(count):
         memory[s, :RIM] = halos[s][...]
         memory[s, RIM:] = pieces[s][...]
-    for copy in copies:
-        copy.wait()
+    for slot in range(2):
+        states[slot, :RIM] = hidden_halo[:, slot * half : (slot + 1) * half]
+        states[slot, RIM:] = hidden[:, slot * half : (slot + 1) * half]
     sums = [0.0] * 4
-    for j in range(2):
+    for far in range(2):
+        slot = rep if far == 0 else 1 - rep
         fields = []
         for which in range(2):
             field = None
             for s in range(count):
                 at = pl.multiple_of(lax.rem(tp + count - s, count) * depth, depth)
-                part = dot(memory[s], held[j, which, pl.ds(at, depth), :])
+                part = dot(memory[s], weights[2 * far + which][pl.ds(at, depth), :])
                 field = part if field is None else field + part
             fields.append(field)
         keys, values = fields
-        span = slice(j * half, (j + 1) * half)
-        states = jnp.concatenate([hidden_halo[:, span], hidden[:, span]], axis=0).astype(F32)
-        terms = (states * states, keys * keys, states * keys, values * values)
+        here = states[slot].astype(F32)
+        terms = (here * here, keys * keys, here * keys, values * values)
         sums = [a + jnp.sum(t, axis=1, keepdims=True) for a, t in zip(sums, terms)]
-        value_ref[j] = values
+        value_ref[slot] = values
     rows = memory.shape[1]
     lane = iota((rows, 8), 1)
     packed = jnp.zeros((rows, 8), F32)
@@ -192,12 +194,11 @@
     tokens, heads = row_ids.shape
     rows, width = table_codes.shape[1:]
     depth = heads * width
-    entries, half = key_weight.shape
+    half = key_weight.shape[1]
     seq_length = tokens * blocks // SEQS
     assert reps == 2 and seq_length % tokens == 0 and row_place.shape[0] % LANES == 0
     block = lax.axis_index(("mem", "rep"))
     smem = pl.BlockSpec(memory_space=pltpu.SMEM)
-    anywhere = pl.BlockSpec(memory_space=pl.ANY)
 
     def shift(x, axis, by, wrap):
         size = lax.axis_size(axis)
@@ -210,43 +211,39 @@
         place_kernel,
         out_shape=jax.ShapeDtypeStruct((heads, tokens), I32),
         name="place_rows",
-    )(row_ids, row_place.reshape(-1, LANES))
-    asked = lax.all_gather(stored, "mem", axis=0)
-
+    )(row_ids.T, row_place.reshape(-1, LANES))
+    here = lax.axis_index("mem")
+    if mems <= 4:
+        asked = [stored] + [
+            lax.ppermute(stored, "mem", [(i, i ^ x) for i in range(mems)]) for x in range(1, mems)
+        ]
+        order = [here ^ m for m in range(mems)]
+    else:
+        asked = [lax.all_gather(stored, "mem", axis=0)]
+        order = list(range(mems))
+    hidden_halo = shift(hidden[tokens - RIM :], ("mem", "rep"), 1, False)
+    asked, hidden_halo = lax.optimization_barrier((asked, hidden_halo))
     other_key = shift(key_weight, "rep", 1, True)
     other_value = shift(value_weight, "rep", 1, True)
-    hidden_halo = shift(hidden[tokens - RIM :], ("mem", "rep"), 1, False)
-
-    wide = 2 * LANES
+
     decoded = pl.pallas_call(
         decode_kernel,
-        grid=(heads,),
-        in_specs=[
-            pl.BlockSpec((1, rows, width), lambda h: (h, 0, 0)),
-            pl.BlockSpec((1, rows, table_scales.shape[2]), lambda h: (h, 0, 0)),
-        ],
-        out_specs=pl.BlockSpec((1, rows, wide), lambda h: (h, 0, 0)),
-        out_shape=jax.ShapeDtypeStruct((heads, rows, wide), BF16),
+        out_shape=jax.ShapeDtypeStruct((heads, width, rows), BF16),
+        compiler_params=pltpu.CompilerParams(vmem_limit_bytes=16 << 20),
         name="decode_tables",
-    )(table_codes, table_scales)
-
-    base = (lax.axis_index("mem") * rows).astype(I32).reshape(1)
-    total_width = ((heads - 1) * width // LANES) * LANES + wide
-    total_width = max(total_width, depth)
+    )(table_codes.transpose(0, 2, 1), table_scales.transpose(2, 0, 1))
+
+    scalars = jnp.stack([here * rows] + order).astype(I32)
     partial = pl.pallas_call(
-        functools.partial(pick_kernel, width),
+        functools.partial(pick_kernel, len(asked)),
         grid=(mems,),
-        in_specs=[
-            smem,
-            pl.BlockSpec((1, heads, tokens), lambda m: (m, 0, 0)),
-            whole(decoded),
-        ],
+        in_specs=[smem] + [whole(a) for a in asked] + [whole(decoded)],
         out_specs=pl.BlockSpec((tokens, depth), lambda m: (m, 0)),
         out_shape=jax.ShapeDtypeStruct((mems * tokens, depth), BF16),
-        scratch_shapes=[pltpu.VMEM((tokens, total_width), F32)],
-        compiler_params=pltpu.CompilerParams(vmem_limit_bytes=40 << 20),
+        scratch_shapes=[pltpu.VMEM((len(asked), heads, tokens), I32)],
+        compiler_params=pltpu.CompilerParams(vmem_limit_bytes=16 << 20),
         name="pick_rows",
-    )(base, asked, decoded)
+    )(scalars, *asked, decoded)
     memory = lax.psum_scatter(partial, "mem", scatter_dimension=0, tiled=True)
 
     halo = shift(memory[tokens - RIM :], ("mem", "rep"), 1, False)
@@ -256,21 +253,22 @@
     where = jnp.stack([lax.axis_index("rep"), lax.axis_index("tp")]).astype(I32)
     extended = tokens + RIM
     operands = (*halos, *pieces, hidden_halo, hidden)
+    weights = (key_weight, value_weight, other_key, other_value)
+    weights = [pltpu.with_memory_space_constraint(w, pltpu.VMEM) for w in weights]
     values, stats = pl.pallas_call(
         functools.partial(project_kernel, tps),
-        in_specs=[smem] + [pl.BlockSpec(memory_space=pltpu.VMEM)] * len(operands) + [anywhere] * 4,
+        in_specs=[smem] + [pl.BlockSpec(memory_space=pltpu.VMEM)] * (len(operands) + 4),
         out_shape=(
             jax.ShapeDtypeStruct((2, extended, half), F32),
             jax.ShapeDtypeStruct((8, extended), F32),
         ),
         scratch_shapes=[
-            pltpu.VMEM((2, 2, entries, half), BF16),
             pltpu.VMEM((tps, extended, depth), BF16),
-            pltpu.SemaphoreType.DMA((4,)),
+            pltpu.VMEM((2, extended, half), BF16),
         ],
-        compiler_params=pltpu.CompilerParams(vmem_limit_bytes=56 << 20),
+        compiler_params=pltpu.CompilerParams(vmem_limit_bytes=24 << 20),
         name="project",
-    )(where, *operands, key_weight, value_weight, other_key, other_value)
+    )(where, *operands, *weights)
 
     all_stats = [stats] + [shift(stats, "tp", s, True) for s in range(1, tps)]
     keep = (block * tokens % seq_length != 0).astype(I32).reshape(1)
@@ -299,7 +297,7 @@
         out_specs=spec(tokens),
         out_shape=out_shape,
         scratch_shapes=[pltpu.VMEM((extended, 8), F32), pltpu.VMEM((extended, step), F32)],
-        compiler_params=pltpu.CompilerParams(vmem_limit_bytes=40 << 20),
+        compiler_params=pltpu.CompilerParams(vmem_limit_bytes=16 << 20),
         name="finish",
     )(keep, *all_stats, values, split(hidden), split(conv_weight))
     return out if aligned else jnp.concatenate([out[0], out[1]], axis=1)

time: 123 us -> 99.8 us (0.81)
  blocking collectives: 15 us -> 0 us
  Pallas kernels: 34.3 us -> 20.3 us
  starting transfers between devices: 7.1 us -> 13.4 us
  waiting for transfers between devices: 37.5 us -> 40.3 us
  local copies, waits for them, and re-layouts: 14 us -> 11.8 us
    all_gather x1 -> x0, blocking collectives: 15 us -> none  [shards(): asked = lax.all_gather(stored, 'mem', axis=0)]
    pallas_call x2, Pallas kernels: 15.7 us -> 6.1 us  [the longest x1 5.22 us: shards(): pl.pallas_call(functools.partial(pick_kernel, len(asked)), grid=(mems,),...]
    ppermute x0 -> x3, starting transfers between devices: none -> 5.17 us  [shards(): lax.ppermute(stored, 'mem', [(i, i ^ x) for i in range(mems)])]
    pallas_call x1, Pallas kernels: 12.1 us -> 7.91 us  [shards(): pl.pallas_call(functools.partial(project_kernel, tps), in_specs=[smem] +...]
    ppermute x7, waiting for transfers between devices: 5.67 us -> 8 us  [shift(): return lax.ppermute(x, axis, pairs)]
    unnamed x23 -> x20, local copies, waits for them, and re-layouts: 12.3 us -> 10.1 us
  transfers between devices with their start and end apart: 8 -> 11, of which waited for: 3 -> 4; matrix products, arithmetic and copies ran while one was open for 2% -> 1% of each run, Pallas kernels for 0% -> 8%
where the time goes in v2:
time: 99.8 us; the launch traced here: 99.3 us
  waiting for transfers between devices  40.3 us (40%)
  Pallas kernels  20.3 us (20%)
  between operations  13.5 us (14%)
  starting transfers between devices  13.4 us (13%)
  local copies, waits for them, and re-layouts  11.8 us (12%)
    reduce_scatter x1, waiting for transfers between devices, shards(): memory = lax.psum_scatter(partial, 'mem', scatter_dimension=0, tiled=True)  32.3 us
    unnamed x20, local copies, waits for them, and re-layouts  10.1 us
    ppermute x7, starting transfers between devices, shift(): return lax.ppermute(x, axis, pairs)  8.21 us
    ppermute x7, waiting for transfers between devices, shift(): return lax.ppermute(x, axis, pairs)  8 us
    pallas_call x1, Pallas kernels, shards(): pl.pallas_call(functools.partial(project_kernel, tps), in_specs=[smem] +...  7.91 us
    pallas_call x1, Pallas kernels, shards(): pl.pallas_call(functools.partial(pick_kernel, len(asked)), grid=(mems,),...  5.22 us
    ppermute x3, starting transfers between devices, shards(): lax.ppermute(stored, 'mem', [(i, i ^ x) for i in range(mems)])  5.17 us
    pallas_call x1, Pallas kernels, shards(): pl.pallas_call(functools.partial(finish_kernel, tps), grid=(2 * per,), in...  4.33 us
  transfers between devices with their start and end apart: 11, of which 4 were waited for; matrix products, arithmetic and copies ran while one was open for 1% of the time, Pallas kernels for 8%

profile of v2, /device:TPU:0, one launch (start us, length us, event | category | flops | bytes accessed | tf_op | source)
XLA Modules:
  0.0 99.3 jit_solution(17161570768665991102)
XLA Ops:
  6.5 0.0 reduce-scatter.2.cloned.1.call-start
  6.5 0.9 slice.6
  7.4 2.3 %collective-permute-start.3 = (bf16[16,2304]{1,0:T(8,128)(2,1)S(1)}, bf16[16,2304]{1,0:T(8,128)(2,1)S(1)}, u32[]{:S(2)}, u32[]{:S(2)}) collective-permute-start(bf16[16,2304]{1,0:T(8,128)(2,1)S(1)} %slice.6), channel_id=1, source_target_pairs={{0,1},{1,4},{4,5},{5,8},{8,9},{9,12},{12,13},{2,3},{3,6},{6,7},{7,... | collective-permute-start | bytes 221192 | tf_op jit(solution)/shard_map/ppermute | solution.py:208
  9.8 1.9 %place_rows.1.refs_0_ = s32[8,256]{1,0:T(8,128)} custom-call(s32[8,256]{1,0:T(8,128)} %bitcast.15, s32[32,128]{1,0:T(8,128)} %bitcast.14), custom_call_target="tpu_custom_call" | custom-call | tf_op jit(solution)/shard_map/place_rows/pallas_call | solution.py:210
  11.7 0.0 copy-start.9
  11.7 4.6 %collective-permute-start.2 = (s32[8,256]{1,0:T(8,128)}, s32[8,256]{1,0:T(8,128)S(1)}, u32[]{:S(2)}, u32[]{:S(2)}) collective-permute-start(s32[8,256]{1,0:T(8,128)} %place_rows.1.refs_0_), channel_id=1, source_target_pairs={{0,12},{4,8},{8,4},{12,0},{1,13},{5,9},{9,5},{13,1},{2,14},{6,10},... | collective-permute-start | bytes 24584 | tf_op jit(solution)/shard_map/ppermute | solution.py:218
  16.3 0.0 collective-permute-start.1
  16.3 0.6 collective-permute-start
  16.9 1.1 %collective-permute-start.7 = (bf16[1280,1152]{1,0:T(8,128)(2,1)}, bf16[1280,1152]{1,0:T(8,128)(2,1)}, u32[]{:S(2)}, u32[]{:S(2)}) collective-permute-start(bf16[1280,1152]{1,0:T(8,128)(2,1)} %refs_6_.1), channel_id=1, source_target_pairs={{0,1},{1,0},{2,3},{3,2},{4,5},{5,4},{6,7},{7,6},{8,9},{9,8},{10,11... | collective-permute-start | bytes 8847368 | tf_op jit(solution)/shard_map/ppermute | solution.py:208
  17.9 0.0 copy-start.5
  17.9 1.3 %copy-done.5 = bf16[8,1024,80]{1,2,0:T(8,128)(2,1)S(1)} copy-done((bf16[8,1024,80]{1,2,0:T(8,128)(2,1)S(1)}, bf16[8,1024,80]{1,2,0:T(8,128)(2,1)}, u32[]{:S(2)}) %copy-start.5) | copy-done | bytes 1310744
  19.3 0.0 copy-start.7
  19.3 0.9 copy-done.7
  20.1 0.9 decode_tables.1.refs_4_
  21.0 0.0 copy-start
  21.0 0.1 stack.35.scalars_ref
  21.1 0.0 collective-permute-done.2.refs_3_
  21.1 0.0 collective-permute-start.8
  21.1 0.0 collective-permute-done.1.refs_2_
  21.2 0.0 collective-permute-done.refs_1_
  21.2 0.0 collective-permute-done.3.refs_4_
  21.2 0.0 copy-done.9
  21.2 5.2 %pick_rows.1 = bf16[1024,640]{1,0:T(8,128)(2,1)} custom-call(s32[5]{0:T(128)S(1)} %stack.35.scalars_ref, s32[8,256]{1,0:T(8,128)S(1)} %copy-done.9, s32[8,256]{1,0:T(8,128)S(1)} %collective-permute-done.refs_1_, s32[8,256]{1,0:T(8,128)S(1)} %collective-permute-done.1.refs_2_, s32[8,256]{1,0:T(8,128)S(1)} %collective-permute-done.2.refs_3_, ...), custom_call_target="tpu_custom_call" | custom-call | tf_op jit(solution)/shard_map/pick_rows/pallas_call | solution.py:237
  26.4 0.0 reduce-scatter.2.cloned.1.call-update
  26.4 32.3 %reduce-scatter.2.cloned.1.call-done.refs_2_ = bf16[256,640]{1,0:T(8,128)(2,1)} async-done(((bf16[1024,640]{1,0:T(8,128)(2,1)}), bf16[256,640]{1,0:T(8,128)(2,1)}) %reduce-scatter.2.cloned.1.call-update) | async-done | bytes 327696 | tf_op jit(solution)/shard_map/reduce_scatter | solution.py:247
  58.7 1.5 %collective-permute-start.6 = (bf16[256,640]{1,0:T(8,128)(2,1)}, bf16[256,640]{1,0:T(8,128)(2,1)S(1)}, u32[]{:S(2)}, u32[]{:S(2)}) collective-permute-start(bf16[256,640]{1,0:T(8,128)(2,1)} %reduce-scatter.2.cloned.1.call-done.refs_2_), channel_id=1, source_target_pairs={{0,2},{2,0},{1,3},{3,1},{4,6},{6,4},{5,7},{7,5},{8,10},{10,8},{9,1... | collective-permute-start | bytes 983048 | tf_op jit(solution)/shard_map/ppermute | solution.py:208
  60.2 0.8 slice.8
  60.9 1.3 %collective-permute-start.4 = (bf16[16,640]{1,0:T(8,128)(2,1)S(1)}, bf16[16,640]{1,0:T(8,128)(2,1)S(1)}, u32[]{:S(2)}, u32[]{:S(2)}) collective-permute-start(bf16[16,640]{1,0:T(8,128)(2,1)S(1)} %slice.8), channel_id=1, source_target_pairs={{0,1},{1,4},{4,5},{5,8},{8,9},{9,12},{12,13},{2,3},{3,6},{6,7},{7,... | collective-permute-start | bytes 61448 | tf_op jit(solution)/shard_map/ppermute | solution.py:208
  62.2 0.8 collective-permute-done.4.refs_0_
  63.0 0.6 collective-permute-start.5
  63.6 0.1 pad_add_fusion.where_ref
  63.7 4.9 %collective-permute-done.5.refs_1_ = bf16[16,640]{1,0:T(8,128)(2,1)S(1)} collective-permute-done((bf16[16,640]{1,0:T(8,128)(2,1)S(1)}, bf16[16,640]{1,0:T(8,128)(2,1)S(1)}, u32[]{:S(2)}, u32[]{:S(2)}) %collective-permute-start.5) | collective-permute-done | bytes 20512 | tf_op jit(solution)/shard_map/ppermute | solution.py:208
  68.6 0.0 collective-permute-done.7.refs_8_
  68.6 0.0 collective-permute-done.8.refs_9_
  68.6 0.0 collective-permute-done.6.refs_3_
  68.6 0.0 copy-done
  68.7 0.0 copy-start.1
  68.7 1.8 %copy-done.1 = bf16[1280,1152]{1,0:T(8,128)(2,1)S(1)} copy-done((bf16[1280,1152]{1,0:T(8,128)(2,1)S(1)}, bf16[1280,1152]{1,0:T(8,128)(2,1)}, u32[]{:S(2)}) %copy-start.1) | copy-done | bytes 2949144
  70.5 0.0 copy-start.2
  70.5 1.8 %copy-done.2 = bf16[1280,1152]{1,0:T(8,128)(2,1)S(1)} copy-done((bf16[1280,1152]{1,0:T(8,128)(2,1)S(1)}, bf16[1280,1152]{1,0:T(8,128)(2,1)}, u32[]{:S(2)}) %copy-start.2) | copy-done | bytes 2949144
  72.3 1.0 copy-done.6
  73.3 7.9 %project.1 = (f32[2,272,1152]{2,1,0:T(8,128)S(1)}, f32[8,272]{1,0:T(8,128)S(1)}) custom-call(s32[2]{0:T(128)S(1)} %pad_add_fusion.where_ref, bf16[16,640]{1,0:T(8,128)(2,1)S(1)} %collective-permute-done.4.refs_0_, bf16[16,640]{1,0:T(8,128)(2,1)S(1)} %collective-permute-done.5.refs_1_, bf16[256,640]{1,0:T(8,128)(2,1)S(1)} %copy-done.6, ...), custom_call_target="tpu_custom_call" | custom-call | tf_op jit(solution)/shard_map/project/pallas_call | solution.py:258
  81.2 1.5 %copy-done.3 = f32[2,272,1152]{2,1,0:T(8,128)} copy-done((f32[2,272,1152]{2,1,0:T(8,128)}, f32[2,272,1152]{2,1,0:T(8,128)S(1)}, u32[]{:S(2)}) %copy-start.3) | copy-done | bytes 2506776
  82.7 1.5 %collective-permute-start.9 = (f32[8,272]{1,0:T(8,128)S(1)}, f32[8,272]{1,0:T(8,128)S(1)}, u32[]{:S(2)}, u32[]{:S(2)}) collective-permute-start(f32[8,272]{1,0:T(8,128)S(1)} %get-tuple-element.17.refs_0_), channel_id=1, source_target_pairs={{0,2},{2,0},{1,3},{3,1},{4,6},{6,4},{5,7},{7,5},{8,10},{10,8},{9,1... | collective-permute-start | bytes 26120 | tf_op jit(solution)/shard_map/ppermute | solution.py:208
  84.2 2.2 %collective-permute-done.9.refs_1_ = f32[8,272]{1,0:T(8,128)S(1)} collective-permute-done((f32[8,272]{1,0:T(8,128)S(1)}, f32[8,272]{1,0:T(8,128)S(1)}, u32[]{:S(2)}, u32[]{:S(2)}) %collective-permute-start.9) | collective-permute-done | bytes 8736 | tf_op jit(solution)/shard_map/ppermute | solution.py:208
  86.4 0.0 copy-done.8
  86.4 1.7 %copy-done.4 = f32[2,272,1152]{2,1,0:T(8,128)S(1)} copy-done((f32[2,272,1152]{2,1,0:T(8,128)S(1)}, f32[2,272,1152]{2,1,0:T(8,128)}, u32[]{:S(2)}) %copy-start.4) | copy-done | bytes 2506776
  88.1 4.3 %finish.1 = bf16[256,2304]{1,0:T(8,128)(2,1)} custom-call(s32[1]{0:T(128)} %bitcast.keep_ref, f32[8,272]{1,0:T(8,128)S(1)} %get-tuple-element.17.refs_0_, f32[8,272]{1,0:T(8,128)S(1)} %collective-permute-done.9.refs_1_, f32[2,272,1152]{2,1,0:T(8,128)S(1)} %copy-done.4, bf16[256,2304]{1,0:T(8,128)(2,1)S(1)} %copy-done, f32[4,2304]{1,0:T(4,128)S(1)} %copy-done.8), custom_call_target="tpu_custom_call" | custom-call | tf_op jit(solution)/shard_map/finish/pallas_call | solution.py:287
  (4 shorter events, 0.0 us)
Async XLA Ops:
  6.5 52.2 %reduce-scatter.2.cloned.1.call-start = ((), (), s32[]{:S(2)}) async-start(), calls=%async_computation.1 | async-start | bytes 1638400 | tf_op jit(solution)/shard_map/reduce_scatter | solution.py:247
  7.4 13.7 %collective-permute-start.3 = (bf16[16,2304]{1,0:T(8,128)(2,1)S(1)}, bf16[16,2304]{1,0:T(8,128)(2,1)S(1)}, u32[]{:S(2)}, u32[]{:S(2)}) collective-permute-start(bf16[16,2304]{1,0:T(8,128)(2,1)S(1)} %slice.6), channel_id=1, source_target_pairs={{0,1},{1,4},{4,5},{5,8},{8,9},{9,12},{12,13},{2,3},{3,6},{6,7},{7,... | collective-permute-start | bytes 221192 | tf_op jit(solution)/shard_map/ppermute | solution.py:208
  11.7 9.5 %copy-start.9 = (s32[8,256]{1,0:T(8,128)S(1)}, s32[8,256]{1,0:T(8,128)}, u32[]{:S(2)}) copy-start(s32[8,256]{1,0:T(8,128)} %place_rows.1.refs_0_) | copy-start | bytes 24580
  11.7 9.4 %collective-permute-start.2 = (s32[8,256]{1,0:T(8,128)}, s32[8,256]{1,0:T(8,128)S(1)}, u32[]{:S(2)}, u32[]{:S(2)}) collective-permute-start(s32[8,256]{1,0:T(8,128)} %place_rows.1.refs_0_), channel_id=1, source_target_pairs={{0,12},{4,8},{8,4},{12,0},{1,13},{5,9},{9,5},{13,1},{2,14},{6,10},... | collective-permute-start | bytes 24584 | tf_op jit(solution)/shard_map/ppermute | solution.py:218
  16.3 4.8 %collective-permute-start.1 = (s32[8,256]{1,0:T(8,128)}, s32[8,256]{1,0:T(8,128)S(1)}, u32[]{:S(2)}, u32[]{:S(2)}) collective-permute-start(s32[8,256]{1,0:T(8,128)} %place_rows.1.refs_0_), channel_id=1, source_target_pairs={{0,8},{4,12},{8,0},{12,4},{1,9},{5,13},{9,1},{13,5},{2,10},{6,14},... | collective-permute-start | bytes 24584 | tf_op jit(solution)/shard_map/ppermute | solution.py:218
  16.3 4.8 %collective-permute-start = (s32[8,256]{1,0:T(8,128)}, s32[8,256]{1,0:T(8,128)S(1)}, u32[]{:S(2)}, u32[]{:S(2)}) collective-permute-start(s32[8,256]{1,0:T(8,128)} %place_rows.1.refs_0_), channel_id=1, source_target_pairs={{0,4},{4,0},{8,12},{12,8},{1,5},{5,1},{9,13},{13,9},{2,6},{6,2},{1... | collective-permute-start | bytes 24584 | tf_op jit(solution)/shard_map/ppermute | solution.py:218
  16.9 51.8 %collective-permute-start.7 = (bf16[1280,1152]{1,0:T(8,128)(2,1)}, bf16[1280,1152]{1,0:T(8,128)(2,1)}, u32[]{:S(2)}, u32[]{:S(2)}) collective-permute-start(bf16[1280,1152]{1,0:T(8,128)(2,1)} %refs_6_.1), channel_id=1, source_target_pairs={{0,1},{1,0},{2,3},{3,2},{4,5},{5,4},{6,7},{7,6},{8,9},{9,8},{10,11... | collective-permute-start | bytes 8847368 | tf_op jit(solution)/shard_map/ppermute | solution.py:208
  17.9 1.3 %copy-start.5 = (bf16[8,1024,80]{1,2,0:T(8,128)(2,1)S(1)}, bf16[8,1024,80]{1,2,0:T(8,128)(2,1)}, u32[]{:S(2)}) copy-start(bf16[8,1024,80]{1,2,0:T(8,128)(2,1)} %param.11) | copy-start | bytes 3932164
  19.3 0.9 copy-start.7
  21.0 47.6 %copy-start = (bf16[256,2304]{1,0:T(8,128)(2,1)S(1)}, bf16[256,2304]{1,0:T(8,128)(2,1)}, u32[]{:S(2)}) copy-start(bf16[256,2304]{1,0:T(8,128)(2,1)} %refs_3_.1) | copy-start | bytes 3538948
  21.1 47.5 %collective-permute-start.8 = (bf16[1280,1152]{1,0:T(8,128)(2,1)}, bf16[1280,1152]{1,0:T(8,128)(2,1)}, u32[]{:S(2)}, u32[]{:S(2)}) collective-permute-start(bf16[1280,1152]{1,0:T(8,128)(2,1)} %refs_7_.1), channel_id=1, source_target_pairs={{0,1},{1,0},{2,3},{3,2},{4,5},{5,4},{6,7},{7,6},{8,9},{9,8},{10,11... | collective-permute-start | bytes 8847368 | tf_op jit(solution)/shard_map/ppermute | solution.py:208
  58.7 9.9 %collective-permute-start.6 = (bf16[256,640]{1,0:T(8,128)(2,1)}, bf16[256,640]{1,0:T(8,128)(2,1)S(1)}, u32[]{:S(2)}, u32[]{:S(2)}) collective-permute-start(bf16[256,640]{1,0:T(8,128)(2,1)} %reduce-scatter.2.cloned.1.call-done.refs_2_), channel_id=1, source_target_pairs={{0,2},{2,0},{1,3},{3,1},{4,6},{6,4},{5,7},{7,5},{8,10},{10,8},{9,1... | collective-permute-start | bytes 983048 | tf_op jit(solution)/shard_map/ppermute | solution.py:208
  60.9 2.1 %collective-permute-start.4 = (bf16[16,640]{1,0:T(8,128)(2,1)S(1)}, bf16[16,640]{1,0:T(8,128)(2,1)S(1)}, u32[]{:S(2)}, u32[]{:S(2)}) collective-permute-start(bf16[16,640]{1,0:T(8,128)(2,1)S(1)} %slice.8), channel_id=1, source_target_pairs={{0,1},{1,4},{4,5},{5,8},{8,9},{9,12},{12,13},{2,3},{3,6},{6,7},{7,... | collective-permute-start | bytes 61448 | tf_op jit(solution)/shard_map/ppermute | solution.py:208
  63.0 5.6 %collective-permute-start.5 = (bf16[16,640]{1,0:T(8,128)(2,1)S(1)}, bf16[16,640]{1,0:T(8,128)(2,1)S(1)}, u32[]{:S(2)}, u32[]{:S(2)}) collective-permute-start(bf16[16,640]{1,0:T(8,128)(2,1)S(1)} %collective-permute-done.4.refs_0_), channel_id=1, source_target_pairs={{0,2},{2,0},{1,3},{3,1},{4,6},{6,4},{5,7},{7,5},{8,10},{10,8},{9,1... | collective-permute-start | bytes 61448 | tf_op jit(solution)/shard_map/ppermute | solution.py:208
  68.7 1.8 %copy-start.1 = (bf16[1280,1152]{1,0:T(8,128)(2,1)S(1)}, bf16[1280,1152]{1,0:T(8,128)(2,1)}, u32[]{:S(2)}) copy-start(bf16[1280,1152]{1,0:T(8,128)(2,1)} %refs_6_.1) | copy-start | bytes 8847364
  70.5 1.8 %copy-start.2 = (bf16[1280,1152]{1,0:T(8,128)(2,1)S(1)}, bf16[1280,1152]{1,0:T(8,128)(2,1)}, u32[]{:S(2)}) copy-start(bf16[1280,1152]{1,0:T(8,128)(2,1)} %refs_7_.1) | copy-start | bytes 8847364
  72.3 1.0 copy-start.6
  73.3 13.1 %copy-start.8 = (f32[4,2304]{1,0:T(4,128)S(1)}, f32[4,2304]{1,0:T(4,128)}, u32[]{:S(2)}) copy-start(f32[4,2304]{1,0:T(4,128)} %refs_4_.1) | copy-start | bytes 110596
  81.2 1.5 %copy-start.3 = (f32[2,272,1152]{2,1,0:T(8,128)}, f32[2,272,1152]{2,1,0:T(8,128)S(1)}, u32[]{:S(2)}) copy-start(f32[2,272,1152]{2,1,0:T(8,128)S(1)} %get-tuple-element.18.refs_2_) | copy-start | bytes 7520260
  82.7 3.7 %collective-permute-start.9 = (f32[8,272]{1,0:T(8,128)S(1)}, f32[8,272]{1,0:T(8,128)S(1)}, u32[]{:S(2)}, u32[]{:S(2)}) collective-permute-start(f32[8,272]{1,0:T(8,128)S(1)} %get-tuple-element.17.refs_0_), channel_id=1, source_target_pairs={{0,2},{2,0},{1,3},{3,1},{4,6},{6,4},{5,7},{7,5},{8,10},{10,8},{9,1... | collective-permute-start | bytes 26120 | tf_op jit(solution)/shard_map/ppermute | solution.py:208
  86.4 1.7 %copy-start.4 = (f32[2,272,1152]{2,1,0:T(8,128)S(1)}, f32[2,272,1152]{2,1,0:T(8,128)}, u32[]{:S(2)}) copy-start(f32[2,272,1152]{2,1,0:T(8,128)} %copy-done.3) | copy-start | bytes 7520260
Sparse Core Ops, SparseCore 0:
  26.6 32.0 reduce-scatter.1

commit v3 on v2

--- a/solution.py
+++ b/solution.py
@@ -84,69 +84,107 @@
         out_ref[head] = dot(rotation, jnp.concatenate([upper, lower], axis=0)).astype(BF16)
 
 
-def pick_kernel(count, scalars_ref, *refs):
+def picked(local, table_ref, head):
+    rows = table_ref.shape[2]
+    hot = to_bf16(iota((rows, local.shape[1]), 0) == local[head : head + 1, :])
+    return dot(table_ref[head], hot).astype(BF16)
+
+
+def pick_all_kernel(base_ref, ids_ref, table_ref, out_ref):
+    heads, width, _ = table_ref.shape
+    local = ids_ref[...] - base_ref[0]
+    for head in range(heads):
+        out_ref[head * width : (head + 1) * width, :] = picked(local, table_ref, head)
+
+
+def pick_kernel(count, targets, scalars_ref, *refs):
     pieces = refs[:count]
-    table_ref, out_ref, stack = refs[count:]
-    heads, width, rows = table_ref.shape
-    tokens = out_ref.shape[0]
-    step = pl.program_id(0)
-    if count > 1:
-
-        @pl.when(step == 0)
-        def _():
-            for k in range(count):
-                stack[k] = pieces[k][...]
-
-        ids = stack[scalars_ref[1 + step]]
+    table_ref = refs[count]
+    outs = refs[count + 1 : -1]
+    stack = refs[-1]
+    heads, width, _ = table_ref.shape
+    for k in range(count):
+        stack[k] = pieces[k][...]
+    for n, target in enumerate(targets):
+        local = stack[scalars_ref[1 + target]] - scalars_ref[0]
+        for head in range(heads):
+            stream, at = divmod(head, heads // 2)
+            outs[2 * n + stream][at * width : (at + 1) * width, :] = picked(
+                local, table_ref, head
+            )
+
+
+def merge_kernel(middle_ref, inner_ref, outer_ref, *refs):
+    received = refs[:-2]
+    out_ref, rim_ref = refs[-2:]
+    total = jnp.where(middle_ref[0] == 1, inner_ref[...].astype(F32), outer_ref[...].astype(F32))
+    for other in received:
+        total = total + other[...].astype(F32)
+    total = total.astype(BF16)
+    out_ref[...] = total
+    rim_ref[...] = total[:, total.shape[1] - LANES :]
+
+
+def project_kernel(count, stream, where_ref, *refs):
+    rims = refs[:count]
+    pieces = refs[count : 2 * count]
+    refs = refs[2 * count :]
+    weights = refs[:4]
+    if stream == 0:
+        key_ref, value_ref, held, sems = refs[4:]
     else:
-        ids = pieces[0][step]
-    local = ids - scalars_ref[0]
-    found = []
-    for head in range(heads):
-        hot = to_bf16(iota((rows, tokens), 0) == local[head : head + 1, :])
-        found.append(dot(table_ref[head], hot))
-    out_ref[...] = jnp.concatenate(found, axis=0).T.astype(BF16)
-
-
-def project_kernel(count, where_ref, *refs):
-    halos = refs[:count]
-    pieces = refs[count : 2 * count]
-    hidden_halo, hidden = refs[2 * count : 2 * count + 2]
-    weights = refs[2 * count + 2 : 2 * count + 6]
-    value_ref, stats_ref = refs[2 * count + 6 : 2 * count + 8]
-    memory, states = refs[2 * count + 8 :]
+        begun_keys, begun_values, hidden_halo, hidden, value_ref, stats_ref = refs[4:10]
+        held, sems, states = refs[10:]
     half = value_ref.shape[-1]
-    depth = memory.shape[-1]
+    depth, tokens = pieces[0].shape
     rep = where_ref[0]
     tp = where_ref[1]
-    for s in range(count):
-        memory[s, :RIM] = halos[s][...]
-        memory[s, RIM:] = pieces[s][...]
-    for slot in range(2):
-        states[slot, :RIM] = hidden_halo[:, slot * half : (slot + 1) * half]
-        states[slot, RIM:] = hidden[:, slot * half : (slot + 1) * half]
+    copies = []
+    for far in range(2):
+        for which in range(2):
+            for s in range(count):
+                owner = lax.rem(tp + count - s, count)
+                at = pl.multiple_of((2 * owner + stream) * depth, depth)
+                copy = pltpu.make_async_copy(
+                    weights[2 * far + which].at[pl.ds(at, depth), :],
+                    held.at[far, which, pl.ds(s * depth, depth), :],
+                    sems.at[(2 * far + which) * count + s],
+                )
+                copy.start()
+                copies.append(copy)
+    body = jnp.concatenate([p[...].astype(F32) for p in pieces], axis=0).T.astype(BF16)
+    rim = jnp.concatenate([r[...].astype(F32) for r in rims], axis=0).T.astype(BF16)
+    memory = jnp.concatenate([rim[LANES - RIM :], body], axis=0)
+    if stream == 1:
+        for slot in range(2):
+            states[slot, :RIM] = hidden_halo[:, slot * half : (slot + 1) * half]
+            states[slot, RIM:] = hidden[:, slot * half : (slot + 1) * half]
     sums = [0.0] * 4
     for far in range(2):
         slot = rep if far == 0 else 1 - rep
         fields = []
         for which in range(2):
-            field = None
             for s in range(count):
-                at = pl.multiple_of(lax.rem(tp + count - s, count) * depth, depth)
-                part = dot(memory[s], weights[2 * far + which][pl.ds(at, depth), :])
-                field = part if field is None else field + part
-            fields.append(field)
+                copies[(2 * far + which) * count + s].wait()
+            fields.append(dot(memory, held[far, which]))
         keys, values = fields
-        here = states[slot].astype(F32)
-        terms = (here * here, keys * keys, here * keys, values * values)
-        sums = [a + jnp.sum(t, axis=1, keepdims=True) for a, t in zip(sums, terms)]
-        value_ref[slot] = values
-    rows = memory.shape[1]
-    lane = iota((rows, 8), 1)
-    packed = jnp.zeros((rows, 8), F32)
-    for k in range(4):
-        packed = jnp.where(lane == k, sums[k], packed)
-    stats_ref[...] = dot_nt(unit(8, F32), packed, lax.Precision.HIGHEST)
+        if stream == 0:
+            key_ref[slot] = keys
+            value_ref[slot] = values
+        else:
+            keys = keys + begun_keys[slot]
+            values = values + begun_values[slot]
+            here = states[slot].astype(F32)
+            terms = (here * here, keys * keys, here * keys, values * values)
+            sums = [a + jnp.sum(t, axis=1, keepdims=True) for a, t in zip(sums, terms)]
+            value_ref[slot] = values
+    if stream == 1:
+        rows = memory.shape[0]
+        lane = iota((rows, 8), 1)
+        packed = jnp.zeros((rows, 8), F32)
+        for k in range(4):
+            packed = jnp.where(lane == k, sums[k], packed)
+        stats_ref[...] = dot_nt(unit(8, F32), packed, lax.Precision.HIGHEST)
 
 
 def finish_kernel(count, keep_ref, *refs):
@@ -182,6 +220,87 @@
 
 def whole(array):
     return pl.BlockSpec(array.shape, lambda *_: (0,) * array.ndim)
+
+
+def in_vmem(array):
+    return pltpu.with_memory_space_constraint(array, pltpu.VMEM)
+
+
+def scattered_sum(stored, decoded, here):
+    mems = lax.axis_size("mem")
+    heads, width, rows = decoded.shape
+    tokens = stored.shape[1]
+    asked = lax.all_gather(stored, "mem", axis=0)
+    partial = pl.pallas_call(
+        pick_all_kernel,
+        grid=(mems,),
+        in_specs=[
+            pl.BlockSpec(memory_space=pltpu.SMEM),
+            pl.BlockSpec((None, heads, tokens), lambda m: (m, 0, 0)),
+            whole(decoded),
+        ],
+        out_specs=pl.BlockSpec((None, heads * width, tokens), lambda m: (m, 0, 0)),
+        out_shape=jax.ShapeDtypeStruct((mems, heads * width, tokens), BF16),
+        compiler_params=pltpu.CompilerParams(vmem_limit_bytes=16 << 20),
+        name="pick_all",
+    )((here * rows).astype(I32).reshape(1), asked, decoded)
+    total = lax.psum_scatter(partial, "mem", scatter_dimension=0, tiled=False)
+    memory = jnp.split(total, 2, axis=0)
+    return memory, [m[:, tokens - LANES :] for m in memory]
+
+
+def line_sum(stored, decoded, here):
+    heads, width, rows = decoded.shape
+    tokens = stored.shape[1]
+    asked = [stored] + [
+        lax.ppermute(stored, "mem", [(i, i ^ x) for i in range(4)]) for x in range(1, 4)
+    ]
+    right = here >= 2
+    order = [here ^ jnp.where(right, j, 3 - j) for j in range(4)]
+    scalars = jnp.stack([here * rows] + order).astype(I32)
+    block = jax.ShapeDtypeStruct((heads * width // 2, tokens), BF16)
+
+    def pick(*targets):
+        return pl.pallas_call(
+            functools.partial(pick_kernel, 4, targets),
+            in_specs=[pl.BlockSpec(memory_space=pltpu.SMEM)]
+            + [pl.BlockSpec(memory_space=pltpu.VMEM)] * 5,
+            out_shape=(block,) * (2 * len(targets)),
+            scratch_shapes=[pltpu.VMEM((4, heads, tokens), I32)],
+            compiler_params=pltpu.CompilerParams(vmem_limit_bytes=16 << 20),
+            name="pick_rows",
+        )(scalars, *asked, decoded)
+
+    def after(x, *others):
+        return lax.optimization_barrier((x, *others))[0]
+
+    inward = lambda x: lax.ppermute(x, "mem", [(0, 1), (3, 2)])
+    across = lambda x: lax.ppermute(x, "mem", [(1, 2), (2, 1)])
+    outward = lambda x: lax.ppermute(x, "mem", [(1, 0), (2, 3)])
+
+    farthest = pick(0)
+    first = [inward(x) for x in farthest]
+    second_own = pick(1)
+    rest = pick(2, 3)
+    inner, outer = rest[:2], rest[2:]
+    middle = ((here == 1) | (here == 2)).astype(I32).reshape(1)
+    memory, rims = [], []
+    for n in range(2):
+        crossed = across(farthest[n] + first[n])
+        second = inward(after(second_own[n], first[n]))
+        crossed_near = across(second_own[n] + second)
+        third = inward(after(inner[n], second))
+        last = outward(outer[n] + crossed)
+        total, rim = pl.pallas_call(
+            merge_kernel,
+            in_specs=[pl.BlockSpec(memory_space=pltpu.SMEM)]
+            + [pl.BlockSpec(memory_space=pltpu.VMEM)] * 5,
+            out_shape=(block, jax.ShapeDtypeStruct((block.shape[0], LANES), BF16)),
+            name="merge",
+        )(middle, inner[n], outer[n], third, crossed_near, last)
+        memory.append(total)
+        rims.append(rim)
+    return memory, rims
 
 
 def shards(
@@ -200,77 +319,78 @@
     block = lax.axis_index(("mem", "rep"))
     smem = pl.BlockSpec(memory_space=pltpu.SMEM)
 
-    def shift(x, axis, by, wrap):
-        size = lax.axis_size(axis)
-        pairs = [
-            (i, (i + by) % size) for i in range(size) if wrap or 0 <= i + by < size
-        ]
-        return lax.ppermute(x, axis, pairs)
-
     stored = pl.pallas_call(
         place_kernel,
         out_shape=jax.ShapeDtypeStruct((heads, tokens), I32),
         name="place_rows",
     )(row_ids.T, row_place.reshape(-1, LANES))
-    here = lax.axis_index("mem")
-    if mems <= 4:
-        asked = [stored] + [
-            lax.ppermute(stored, "mem", [(i, i ^ x) for i in range(mems)]) for x in range(1, mems)
-        ]
-        order = [here ^ m for m in range(mems)]
-    else:
-        asked = [lax.all_gather(stored, "mem", axis=0)]
-        order = list(range(mems))
-    hidden_halo = shift(hidden[tokens - RIM :], ("mem", "rep"), 1, False)
-    asked, hidden_halo = lax.optimization_barrier((asked, hidden_halo))
-    other_key = shift(key_weight, "rep", 1, True)
-    other_value = shift(value_weight, "rep", 1, True)
-
     decoded = pl.pallas_call(
         decode_kernel,
         out_shape=jax.ShapeDtypeStruct((heads, width, rows), BF16),
         compiler_params=pltpu.CompilerParams(vmem_limit_bytes=16 << 20),
         name="decode_tables",
     )(table_codes.transpose(0, 2, 1), table_scales.transpose(2, 0, 1))
-
-    scalars = jnp.stack([here * rows] + order).astype(I32)
-    partial = pl.pallas_call(
-        functools.partial(pick_kernel, len(asked)),
-        grid=(mems,),
-        in_specs=[smem] + [whole(a) for a in asked] + [whole(decoded)],
-        out_specs=pl.BlockSpec((tokens, depth), lambda m: (m, 0)),
-        out_shape=jax.ShapeDtypeStruct((mems * tokens, depth), BF16),
-        scratch_shapes=[pltpu.VMEM((len(asked), heads, tokens), I32)],
-        compiler_params=pltpu.CompilerParams(vmem_limit_bytes=16 << 20),
-        name="pick_rows",
-    )(scalars, *asked, decoded)
-    memory = lax.psum_scatter(partial, "mem", scatter_dimension=0, tiled=True)
-
-    halo = shift(memory[tokens - RIM :], ("mem", "rep"), 1, False)
-    pieces = [memory] + [shift(memory, "tp", s, True) for s in range(1, tps)]
-    halos = [halo] + [shift(halo, "tp", s, True) for s in range(1, tps)]
+    here = lax.axis_index("mem")
+    if mems == 4:
+        memory, rims = line_sum(stored, decoded, here)
+    else:
+        memory, rims = scattered_sum(stored, decoded, here)
+
+    _, tail = lax.optimization_barrier((stored, hidden[tokens - RIM :]))
+    needed = [(i, i + 1) for i in range(blocks - 1) if (i + 1) * tokens % seq_length]
+    hidden_halo = lax.ppermute(tail, ("mem", "rep"), needed)
+    other_key = lax.ppermute(key_weight, "rep", [(0, 1), (1, 0)])
+    other_value = lax.ppermute(value_weight, "rep", [(0, 1), (1, 0)])
+    weights = (key_weight, value_weight, other_key, other_value)
 
     where = jnp.stack([lax.axis_index("rep"), lax.axis_index("tp")]).astype(I32)
     extended = tokens + RIM
-    operands = (*halos, *pieces, hidden_halo, hidden)
-    weights = (key_weight, value_weight, other_key, other_value)
-    weights = [pltpu.with_memory_space_constraint(w, pltpu.VMEM) for w in weights]
+    part = depth // 2
+    field = jax.ShapeDtypeStruct((2, extended, half), F32)
+    held = pltpu.VMEM((2, 2, tps * part, half), BF16)
+    sems = pltpu.SemaphoreType.DMA((4 * tps,))
+    anywhere = pl.BlockSpec(memory_space=pl.ANY)
+    resident = pl.BlockSpec(memory_space=pltpu.VMEM)
+    limit = pltpu.CompilerParams(vmem_limit_bytes=16 << 20)
+    inputs = []
+    for stream in range(2):
+        inner = [memory[stream]] + [
+            lax.ppermute(memory[stream], "tp", [(i, (i + s) % tps) for i in range(tps)])
+            for s in range(1, tps)
+        ]
+        rim = [
+            lax.ppermute(
+                rims[stream],
+                ("mem", "tp", "rep"),
+                [
+                    ((a // reps * tps + i) * reps + a % reps, (b // reps * tps + (i + s) % tps) * reps + b % reps)
+                    for a, b in needed
+                    for i in range(tps)
+                ],
+            )
+            for s in range(tps)
+        ]
+        inputs.append((where, *rim, *inner, *weights))
+    begun = pl.pallas_call(
+        functools.partial(project_kernel, tps, 0),
+        in_specs=[smem] + [resident] * (2 * tps) + [anywhere] * 4,
+        out_shape=(field, field),
+        scratch_shapes=[held, sems],
+        compiler_params=limit,
+        name="project_first",
+    )(*inputs[0])
     values, stats = pl.pallas_call(
-        functools.partial(project_kernel, tps),
-        in_specs=[smem] + [pl.BlockSpec(memory_space=pltpu.VMEM)] * (len(operands) + 4),
-        out_shape=(
-            jax.ShapeDtypeStruct((2, extended, half), F32),
-            jax.ShapeDtypeStruct((8, extended), F32),
-        ),
-        scratch_shapes=[
-            pltpu.VMEM((tps, extended, depth), BF16),
-            pltpu.VMEM((2, extended, half), BF16),
-        ],
-        compiler_params=pltpu.CompilerParams(vmem_limit_bytes=24 << 20),
-        name="project",
-    )(where, *operands, *weights)
-
-    all_stats = [stats] + [shift(stats, "tp", s, True) for s in range(1, tps)]
+        functools.partial(project_kernel, tps, 1),
+        in_specs=[smem] + [resident] * (2 * tps) + [anywhere] * 4 + [resident] * 4,
+        out_shape=(field, jax.ShapeDtypeStruct((8, extended), F32)),
+        scratch_shapes=[held, sems, pltpu.VMEM((2, extended, half), BF16)],
+        compiler_params=limit,
+        name="project_second",
+    )(*inputs[1], *[in_vmem(b) for b in begun], hidden_halo, hidden)
+
+    all_stats = [stats] + [
+        lax.ppermute(stats, "tp", [(i, (i + s) % tps) for i in range(tps)]) for s in range(1, tps)
+    ]
     keep = (block * tokens % seq_length != 0).astype(I32).reshape(1)
     aligned = half % LANES == 0
     if aligned:
@@ -299,7 +419,7 @@
         scratch_shapes=[pltpu.VMEM((extended, 8), F32), pltpu.VMEM((extended, step), F32)],
         compiler_params=pltpu.CompilerParams(vmem_limit_bytes=16 << 20),
         name="finish",
-    )(keep, *all_stats, values, split(hidden), split(conv_weight))
+    )(keep, *all_stats, in_vmem(values), split(hidden), split(conv_weight))
     return out if aligned else jnp.concatenate([out[0], out[1]], axis=1)
 
 

time: 99.8 us -> 89.3 us (0.89)
  waiting for transfers between devices: 40.3 us -> 8.74 us
  starting transfers between devices: 13.4 us -> 41.6 us
  between operations: 13.5 us -> 0.49 us
  Pallas kernels: 20.3 us -> 27.3 us
  local copies, waits for them, and re-layouts: 11.8 us -> 10.1 us
    reduce_scatter x1 -> x0, waiting for transfers between devices: 32.3 us -> none  [shards(): memory = lax.psum_scatter(partial, 'mem', scatter_dimension=0, tiled=True)]
    ppermute x10 -> x25, starting transfers between devices: 13.4 us -> 41.6 us  [the longest x6 19.4 us: line_sum(): inward = lambda x: lax.ppermute(x, 'mem', [(0, 1), (3, 2)])]
    pallas_call x2 -> x7, Pallas kernels: 13.1 us -> 20.1 us  [the longest x1 5.6 us: shards(): pl.pallas_call(functools.partial(project_kernel, tps, 1), in_specs=[smem]...]
    slice x2 -> x1, local copies, waits for them, and re-layouts: 1.65 us -> 0.01 us  [shards(): _, tail = lax.optimization_barrier((stored, hidden[tokens - RIM:]))]
    ppermute x10 -> x25, waiting for transfers between devices: 8.01 us -> 8.74 us  [the longest x6 3.84 us: line_sum(): inward = lambda x: lax.ppermute(x, 'mem', [(0, 1), (3, 2)])]
    unnamed x20 -> x46, local copies, waits for them, and re-layouts: 10.1 us -> 10 us
  transfers between devices with their start and end apart: 11 -> 25, of which waited for: 4 -> 8; matrix products, arithmetic and copies ran while one was open for 1% -> 0% of each run, Pallas kernels for 8% -> 20%
where the time goes in v3:
time: 89.3 us; the launch traced here: 88.5 us
  starting transfers between devices  41.6 us (47%)
  Pallas kernels  27.3 us (31%)
  local copies, waits for them, and re-layouts  10.1 us (11%)
  waiting for transfers between devices  8.74 us (10%)
    ppermute x6, starting transfers between devices, line_sum(): inward = lambda x: lax.ppermute(x, 'mem', [(0, 1), (3, 2)])  19.4 us
    unnamed x46, local copies, waits for them, and re-layouts  10 us
    ppermute x3, starting transfers between devices, line_sum(): lax.ppermute(stored, 'mem', [(i, i ^ x) for i in range(4)])  5.62 us
    pallas_call x1, Pallas kernels, shards(): pl.pallas_call(functools.partial(project_kernel, tps, 1), in_specs=[smem]...  5.6 us
    pallas_call x1, Pallas kernels, shards(): pl.pallas_call(functools.partial(project_kernel, tps, 0), in_specs=[smem]...  5.47 us
    ppermute x4, starting transfers between devices, shards(): lax.ppermute(rims[stream], ('mem', 'tp', 'rep'), [((a // reps * tps + i)...  5.33 us
    pallas_call x3, Pallas kernels, pick(): pl.pallas_call(functools.partial(pick_kernel, 4, targets), in_specs=[pl.B...  4.98 us
    pallas_call x1, Pallas kernels, shards(): pl.pallas_call(functools.partial(finish_kernel, tps), grid=(2 * per,), in...  4.33 us
  transfers between devices with their start and end apart: 25, of which 8 were waited for; matrix products, arithmetic and copies ran while one was open for 0% of the time, Pallas kernels for 20%

profile of v3, /device:TPU:0, one launch (start us, length us, event | category | flops | bytes accessed | tf_op | source)
XLA Modules:
  0.0 88.5 jit_solution(2757627401134154820)
XLA Ops:
  0.0 0.5 collective-permute-start.12
  0.5 1.9 %place_rows.1.refs_0_ = s32[8,256]{1,0:T(8,128)} custom-call(s32[8,256]{1,0:T(8,128)} %bitcast.16, s32[32,128]{1,0:T(8,128)} %bitcast.15), custom_call_target="tpu_custom_call" | custom-call | tf_op jit(solution)/shard_map/place_rows/pallas_call | solution.py:322
  2.4 5.1 %collective-permute-start.2 = (s32[8,256]{1,0:T(8,128)}, s32[8,256]{1,0:T(8,128)S(1)}, u32[]{:S(2)}, u32[]{:S(2)}) collective-permute-start(s32[8,256]{1,0:T(8,128)} %place_rows.1.refs_0_), channel_id=1, source_target_pairs={{0,12},{4,8},{8,4},{12,0},{1,13},{5,9},{9,5},{13,1},{2,14},{6,10},... | collective-permute-start | bytes 24584 | tf_op jit(solution)/shard_map/ppermute | solution.py:256
  7.5 0.6 collective-permute-start
  8.0 1.3 %copy-done.7 = bf16[8,1024,80]{1,2,0:T(8,128)(2,1)S(1)} copy-done((bf16[8,1024,80]{1,2,0:T(8,128)(2,1)S(1)}, bf16[8,1024,80]{1,2,0:T(8,128)(2,1)}, u32[]{:S(2)}) %copy-start.7) | copy-done | bytes 1310744
  9.4 0.9 copy-done.15
  10.2 0.9 decode_tables.1.refs_4_
  11.2 1.0 %collective-permute-done.1.refs_2_ = s32[8,256]{1,0:T(8,128)S(1)} collective-permute-done((s32[8,256]{1,0:T(8,128)}, s32[8,256]{1,0:T(8,128)S(1)}, u32[]{:S(2)}, u32[]{:S(2)}) %collective-permute-start.1) | collective-permute-done | bytes 8224 | tf_op jit(solution)/shard_map/ppermute | solution.py:256
  12.2 1.4 %pick_rows.5 = (bf16[320,256]{1,0:T(8,128)(2,1)S(1)}, bf16[320,256]{1,0:T(8,128)(2,1)S(1)}) custom-call(s32[5]{0:T(128)S(1)} %stack.35.scalars_ref, s32[8,256]{1,0:T(8,128)S(1)} %copy-done.14, s32[8,256]{1,0:T(8,128)S(1)} %collective-permute-done.refs_1_, s32[8,256]{1,0:T(8,128)S(1)} %collective-permute-done.1.refs_2_, ...), custom_call_target="tpu_custom_call" | custom-call | tf_op jit(solution)/shard_map/pick_rows/pallas_call | solution.py:264
  13.7 2.4 %collective-permute-start.14 = (bf16[320,256]{1,0:T(8,128)(2,1)S(1)}, bf16[320,256]{1,0:T(8,128)(2,1)S(1)}, u32[]{:S(2)}, u32[]{:S(2)}) collective-permute-start(bf16[320,256]{1,0:T(8,128)(2,1)S(1)} %get-tuple-element.37), channel_id=1, source_target_pairs={{0,4},{12,8},{1,5},{13,9},{2,6},{14,10},{3,7},{15,11},{16,20},{28,... | collective-permute-start | bytes 491528 | tf_op jit(solution)/shard_map/ppermute | solution.py:277
  16.0 1.3 %collective-permute-start.3 = (bf16[320,256]{1,0:T(8,128)(2,1)S(1)}, bf16[320,256]{1,0:T(8,128)(2,1)S(1)}, u32[]{:S(2)}, u32[]{:S(2)}) collective-permute-start(bf16[320,256]{1,0:T(8,128)(2,1)S(1)} %get-tuple-element.29), channel_id=1, source_target_pairs={{0,4},{12,8},{1,5},{13,9},{2,6},{14,10},{3,7},{15,11},{16,20},{28,... | collective-permute-start | bytes 491528 | tf_op jit(solution)/shard_map/ppermute | solution.py:277
  17.3 1.4 %pick_rows.4 = (bf16[320,256]{1,0:T(8,128)(2,1)S(1)}, bf16[320,256]{1,0:T(8,128)(2,1)S(1)}) custom-call(s32[5]{0:T(128)S(1)} %stack.35.scalars_ref, s32[8,256]{1,0:T(8,128)S(1)} %copy-done.14, s32[8,256]{1,0:T(8,128)S(1)} %collective-permute-done.refs_1_, s32[8,256]{1,0:T(8,128)S(1)} %collective-permute-done.1.refs_2_, ...), custom_call_target="tpu_custom_call" | custom-call | tf_op jit(solution)/shard_map/pick_rows/pallas_call | solution.py:264
  18.8 1.9 %collective-permute-done.14 = bf16[320,256]{1,0:T(8,128)(2,1)S(1)} collective-permute-done((bf16[320,256]{1,0:T(8,128)(2,1)S(1)}, bf16[320,256]{1,0:T(8,128)(2,1)S(1)}, u32[]{:S(2)}, u32[]{:S(2)}) %collective-permute-start.14) | collective-permute-done | bytes 163872 | tf_op jit(solution)/shard_map/ppermute | solution.py:277
  20.7 4.4 %collective-permute-start.15 = (bf16[320,256]{1,0:T(8,128)(2,1)S(1)}, bf16[320,256]{1,0:T(8,128)(2,1)S(1)}, u32[]{:S(2)}, u32[]{:S(2)}) collective-permute-start(bf16[320,256]{1,0:T(8,128)(2,1)S(1)} %get-tuple-element.38), channel_id=1, source_target_pairs={{0,4},{12,8},{1,5},{13,9},{2,6},{14,10},{3,7},{15,11},{16,20},{28,... | collective-permute-start | bytes 491528 | tf_op jit(solution)/shard_map/ppermute | solution.py:277
  25.1 0.7 collective-permute-start.7
  25.9 0.8 collective-permute-start.18
  26.7 1.2 %collective-permute-done.15 = bf16[320,256]{1,0:T(8,128)(2,1)S(1)} collective-permute-done((bf16[320,256]{1,0:T(8,128)(2,1)S(1)}, bf16[320,256]{1,0:T(8,128)(2,1)S(1)}, u32[]{:S(2)}, u32[]{:S(2)}) %collective-permute-start.15) | collective-permute-done | bytes 163872 | tf_op jit(solution)/shard_map/ppermute | solution.py:277
  27.9 5.7 %collective-permute-start.4 = (bf16[320,256]{1,0:T(8,128)(2,1)S(1)}, bf16[320,256]{1,0:T(8,128)(2,1)S(1)}, u32[]{:S(2)}, u32[]{:S(2)}) collective-permute-start(bf16[320,256]{1,0:T(8,128)(2,1)S(1)} %get-tuple-element.30), channel_id=1, source_target_pairs={{0,4},{12,8},{1,5},{13,9},{2,6},{14,10},{3,7},{15,11},{16,20},{28,... | collective-permute-start | bytes 491528 | tf_op jit(solution)/shard_map/ppermute | solution.py:277
  33.5 2.2 %pick_rows.3 = (bf16[320,256]{1,0:T(8,128)(2,1)S(1)}, bf16[320,256]{1,0:T(8,128)(2,1)S(1)}, bf16[320,256]{1,0:T(8,128)(2,1)S(1)}, bf16[320,256]{1,0:T(8,128)(2,1)S(1)}) custom-call(s32[5]{0:T(128)S(1)} %stack.35.scalars_ref, s32[8,256]{1,0:T(8,128)S(1)} %copy-done.14, s32[8,256]{1,0:T(8,128)S(1)} %collective-permute-done.refs_1_, ...), custom_call_target="tpu_custom_call" | custom-call | tf_op jit(solution)/shard_map/pick_rows/pallas_call | solution.py:264
  35.7 1.3 %collective-permute-start.16 = (bf16[320,256]{1,0:T(8,128)(2,1)S(1)}, bf16[320,256]{1,0:T(8,128)(2,1)S(1)}, u32[]{:S(2)}, u32[]{:S(2)}) collective-permute-start(bf16[320,256]{1,0:T(8,128)(2,1)S(1)} %get-tuple-element.39.inner_ref), channel_id=1, source_target_pairs={{0,4},{12,8},{1,5},{13,9},{2,6},{14,10},{3,7},{15,11},{16,20},{28,... | collective-permute-start | bytes 491528 | tf_op jit(solution)/shard_map/ppermute | solution.py:277
  37.1 0.7 collective-permute-start.17
  37.8 0.2 collective-permute-done.4
  38.1 1.3 %collective-permute-start.19 = (bf16[320,256]{1,0:T(8,128)(2,1)S(1)}, bf16[320,256]{1,0:T(8,128)(2,1)S(1)}, u32[]{:S(2)}, u32[]{:S(2)}) collective-permute-start(bf16[320,256]{1,0:T(8,128)(2,1)S(1)} %add.32), channel_id=1, source_target_pairs={{4,0},{8,12},{5,1},{9,13},{6,2},{10,14},{7,3},{11,15},{20,16},{24,... | collective-permute-start | bytes 491528 | tf_op jit(solution)/shard_map/ppermute | solution.py:279
  39.3 0.5 collective-permute-done.16.refs_0_
  39.9 4.4 %collective-permute-start.5 = (bf16[320,256]{1,0:T(8,128)(2,1)S(1)}, bf16[320,256]{1,0:T(8,128)(2,1)S(1)}, u32[]{:S(2)}, u32[]{:S(2)}) collective-permute-start(bf16[320,256]{1,0:T(8,128)(2,1)S(1)} %get-tuple-element.31.inner_ref), channel_id=1, source_target_pairs={{0,4},{12,8},{1,5},{13,9},{2,6},{14,10},{3,7},{15,11},{16,20},{28,... | collective-permute-start | bytes 491528 | tf_op jit(solution)/shard_map/ppermute | solution.py:277
  44.3 0.7 collective-permute-start.6
  45.1 0.2 collective-permute-done.19.refs_2_
  45.3 1.3 %collective-permute-start.8 = (bf16[320,256]{1,0:T(8,128)(2,1)S(1)}, bf16[320,256]{1,0:T(8,128)(2,1)S(1)}, u32[]{:S(2)}, u32[]{:S(2)}) collective-permute-start(bf16[320,256]{1,0:T(8,128)(2,1)S(1)} %add.29), channel_id=1, source_target_pairs={{4,0},{8,12},{5,1},{9,13},{6,2},{10,14},{7,3},{11,15},{20,16},{24,... | collective-permute-start | bytes 491528 | tf_op jit(solution)/shard_map/ppermute | solution.py:279
  46.6 2.1 %merge.3 = (bf16[320,256]{1,0:T(8,128)(2,1)}, bf16[320,128]{1,0:T(8,128)(2,1)}) custom-call(s32[1]{0:T(128)} %bitcast.3.middle_ref, bf16[320,256]{1,0:T(8,128)(2,1)} %copy-done.12, bf16[320,256]{1,0:T(8,128)(2,1)} %copy-done.9, bf16[320,256]{1,0:T(8,128)(2,1)} %copy-done.18, bf16[320,256]{1,0:T(8,128)(2,1)} %copy-done.20, bf16[320,256]{1,0:T(8,128)(2,1)} %copy-done.22), custom_call_target="tpu_custom_call" | custom-call | tf_op jit(solution)/shard_map/merge/pallas_call | solution.py:294
  48.7 1.5 %collective-permute-start.22 = (bf16[320,256]{1,0:T(8,128)(2,1)}, bf16[320,256]{1,0:T(8,128)(2,1)S(1)}, u32[]{:S(2)}, u32[]{:S(2)}) collective-permute-start(bf16[320,256]{1,0:T(8,128)(2,1)} %get-tuple-element.41.refs_2_), channel_id=1, source_target_pairs={{0,2},{2,0},{1,3},{3,1},{4,6},{6,4},{5,7},{7,5},{8,10},{10,8},{9,1... | collective-permute-start | bytes 491528 | tf_op jit(solution)/shard_map/ppermute | solution.py:358
  50.2 1.3 %collective-permute-start.21 = (bf16[320,128]{1,0:T(8,128)(2,1)}, bf16[320,128]{1,0:T(8,128)(2,1)S(1)}, u32[]{:S(2)}, u32[]{:S(2)}) collective-permute-start(bf16[320,128]{1,0:T(8,128)(2,1)} %get-tuple-element.40), channel_id=1, source_target_pairs={{0,3},{2,1},{4,7},{6,5},{8,11},{10,9},{12,15},{14,13},{16,19},{18,... | collective-permute-start | bytes 245768 | tf_op jit(solution)/shard_map/ppermute | solution.py:362
  51.5 1.0 %collective-permute-done.8.refs_2_ = bf16[320,256]{1,0:T(8,128)(2,1)S(1)} collective-permute-done((bf16[320,256]{1,0:T(8,128)(2,1)S(1)}, bf16[320,256]{1,0:T(8,128)(2,1)S(1)}, u32[]{:S(2)}, u32[]{:S(2)}) %collective-permute-start.8) | collective-permute-done | bytes 163872 | tf_op jit(solution)/shard_map/ppermute | solution.py:279
  52.5 1.3 %collective-permute-start.20 = (bf16[320,128]{1,0:T(8,128)(2,1)}, bf16[320,128]{1,0:T(8,128)(2,1)S(1)}, u32[]{:S(2)}, u32[]{:S(2)}) collective-permute-start(bf16[320,128]{1,0:T(8,128)(2,1)} %get-tuple-element.40), channel_id=1, source_target_pairs={{0,1},{2,3},{4,5},{6,7},{8,9},{10,11},{12,13},{14,15},{16,17},{18,... | collective-permute-start | bytes 245768 | tf_op jit(solution)/shard_map/ppermute | solution.py:362
  53.8 2.1 %merge.2 = (bf16[320,256]{1,0:T(8,128)(2,1)}, bf16[320,128]{1,0:T(8,128)(2,1)}) custom-call(s32[1]{0:T(128)} %bitcast.3.middle_ref, bf16[320,256]{1,0:T(8,128)(2,1)} %copy-done.11, bf16[320,256]{1,0:T(8,128)(2,1)} %copy-done.8, bf16[320,256]{1,0:T(8,128)(2,1)} %copy-done.17, bf16[320,256]{1,0:T(8,128)(2,1)} %copy-done.19, bf16[320,256]{1,0:T(8,128)(2,1)} %copy-done.21), custom_call_target="tpu_custom_call" | custom-call | tf_op jit(solution)/shard_map/merge/pallas_call | solution.py:294
  55.9 1.5 %collective-permute-start.11 = (bf16[320,256]{1,0:T(8,128)(2,1)}, bf16[320,256]{1,0:T(8,128)(2,1)S(1)}, u32[]{:S(2)}, u32[]{:S(2)}) collective-permute-start(bf16[320,256]{1,0:T(8,128)(2,1)} %get-tuple-element.33.refs_2_), channel_id=1, source_target_pairs={{0,2},{2,0},{1,3},{3,1},{4,6},{6,4},{5,7},{7,5},{8,10},{10,8},{9,1... | collective-permute-start | bytes 491528 | tf_op jit(solution)/shard_map/ppermute | solution.py:358
  57.4 1.3 %collective-permute-start.23 = (bf16[16,2304]{1,0:T(8,128)(2,1)S(1)}, bf16[16,2304]{1,0:T(8,128)(2,1)S(1)}, u32[]{:S(2)}, u32[]{:S(2)}) collective-permute-start(bf16[16,2304]{1,0:T(8,128)(2,1)S(1)} %slice.3), channel_id=1, source_target_pairs={{0,1},{4,5},{8,9},{12,13},{2,3},{6,7},{10,11},{14,15},{16,17},{20,... | collective-permute-start | bytes 221192 | tf_op jit(solution)/shard_map/ppermute | solution.py:341
  58.7 1.3 %collective-permute-start.10 = (bf16[320,128]{1,0:T(8,128)(2,1)}, bf16[320,128]{1,0:T(8,128)(2,1)S(1)}, u32[]{:S(2)}, u32[]{:S(2)}) collective-permute-start(bf16[320,128]{1,0:T(8,128)(2,1)} %get-tuple-element.32), channel_id=1, source_target_pairs={{0,3},{2,1},{4,7},{6,5},{8,11},{10,9},{12,15},{14,13},{16,19},{18,... | collective-permute-start | bytes 245768 | tf_op jit(solution)/shard_map/ppermute | solution.py:362
  60.0 1.5 %collective-permute-start.9 = (bf16[320,128]{1,0:T(8,128)(2,1)}, bf16[320,128]{1,0:T(8,128)(2,1)S(1)}, u32[]{:S(2)}, u32[]{:S(2)}) collective-permute-start(bf16[320,128]{1,0:T(8,128)(2,1)} %get-tuple-element.32), channel_id=1, source_target_pairs={{0,1},{2,3},{4,5},{6,7},{8,9},{10,11},{12,13},{14,15},{16,17},{18,... | collective-permute-start | bytes 245768 | tf_op jit(solution)/shard_map/ppermute | solution.py:362
  61.6 1.8 %copy-done = bf16[1280,1152]{1,0:T(8,128)(2,1)S(1)} copy-done((bf16[1280,1152]{1,0:T(8,128)(2,1)S(1)}, bf16[1280,1152]{1,0:T(8,128)(2,1)}, u32[]{:S(2)}) %copy-start) | copy-done | bytes 2949144
  63.4 1.8 %copy-done.2 = bf16[1280,1152]{1,0:T(8,128)(2,1)S(1)} copy-done((bf16[1280,1152]{1,0:T(8,128)(2,1)S(1)}, bf16[1280,1152]{1,0:T(8,128)(2,1)}, u32[]{:S(2)}) %copy-start.2) | copy-done | bytes 2949144
  65.2 0.9 %copy-done.13 = bf16[320,256]{1,0:T(8,128)(2,1)S(1)} copy-done((bf16[320,256]{1,0:T(8,128)(2,1)S(1)}, bf16[320,256]{1,0:T(8,128)(2,1)}, u32[]{:S(2)}) %copy-start.13) | copy-done | bytes 163864
  66.1 5.5 %project_first.1 = (f32[2,272,1152]{2,1,0:T(8,128)S(1)}, f32[2,272,1152]{2,1,0:T(8,128)S(1)}) custom-call(s32[2]{0:T(128)S(1)} %pad_add_fusion.where_ref, bf16[320,128]{1,0:T(8,128)(2,1)S(1)} %collective-permute-done.20.refs_0_, bf16[320,128]{1,0:T(8,128)(2,1)S(1)} %collective-permute-done.21.refs_1_, bf16[320,256]{1,0:T(8,128)(2,1)S(1)} %copy-done.13, ...), custom_call_target="tpu_custom_call" | custom-call | tf_op jit(solution)/shard_map/project_first/pallas_call | solution.py:374
  71.7 5.6 %project_second.1 = (f32[2,272,1152]{2,1,0:T(8,128)S(1)}, f32[8,272]{1,0:T(8,128)S(1)}) custom-call(s32[2]{0:T(128)S(1)} %pad_add_fusion.where_ref, bf16[320,128]{1,0:T(8,128)(2,1)S(1)} %collective-permute-done.9.refs_0_, bf16[320,128]{1,0:T(8,128)(2,1)S(1)} %collective-permute-done.10.refs_1_, bf16[320,256]{1,0:T(8,128)(2,1)S(1)} %copy-done.10, ...), custom_call_target="tpu_custom_call" | custom-call | tf_op jit(solution)/shard_map/project_second/pallas_call | solution.py:382
  77.3 1.4 %copy-done.5 = f32[2,272,1152]{2,1,0:T(8,128)} copy-done((f32[2,272,1152]{2,1,0:T(8,128)}, f32[2,272,1152]{2,1,0:T(8,128)S(1)}, u32[]{:S(2)}) %copy-start.5) | copy-done | bytes 2506776
  78.8 1.0 %collective-permute-start.24 = (f32[8,272]{1,0:T(8,128)S(1)}, f32[8,272]{1,0:T(8,128)S(1)}, u32[]{:S(2)}, u32[]{:S(2)}) collective-permute-start(f32[8,272]{1,0:T(8,128)S(1)} %get-tuple-element.45.refs_0_), channel_id=1, source_target_pairs={{0,2},{2,0},{1,3},{3,1},{4,6},{6,4},{5,7},{7,5},{8,10},{10,8},{9,1... | collective-permute-start | bytes 26120 | tf_op jit(solution)/shard_map/ppermute | solution.py:392
  79.8 2.7 %collective-permute-done.24.refs_1_ = f32[8,272]{1,0:T(8,128)S(1)} collective-permute-done((f32[8,272]{1,0:T(8,128)S(1)}, f32[8,272]{1,0:T(8,128)S(1)}, u32[]{:S(2)}, u32[]{:S(2)}) %collective-permute-start.24) | collective-permute-done | bytes 8736 | tf_op jit(solution)/shard_map/ppermute | solution.py:392
  82.5 1.7 %copy-done.6 = f32[2,272,1152]{2,1,0:T(8,128)S(1)} copy-done((f32[2,272,1152]{2,1,0:T(8,128)S(1)}, f32[2,272,1152]{2,1,0:T(8,128)}, u32[]{:S(2)}) %copy-start.6) | copy-done | bytes 2506776
  84.2 4.3 %finish.1 = bf16[256,2304]{1,0:T(8,128)(2,1)} custom-call(s32[1]{0:T(128)} %bitcast.keep_ref, f32[8,272]{1,0:T(8,128)S(1)} %get-tuple-element.45.refs_0_, f32[8,272]{1,0:T(8,128)S(1)} %collective-permute-done.24.refs_1_, f32[2,272,1152]{2,1,0:T(8,128)S(1)} %copy-done.6, bf16[256,2304]{1,0:T(8,128)(2,1)S(1)} %copy-done.4, f32[4,2304]{1,0:T(4,128)S(1)} %copy-done.16), custom_call_target="tpu_custom_call" | custom-call | tf_op jit(solution)/shard_map/finish/pallas_call | solution.py:407
  (67 shorter events, 0.6 us)
Async XLA Ops:
  0.0 60.0 %collective-permute-start.12 = (bf16[1280,1152]{1,0:T(8,128)(2,1)}, bf16[1280,1152]{1,0:T(8,128)(2,1)}, u32[]{:S(2)}, u32[]{:S(2)}) collective-permute-start(bf16[1280,1152]{1,0:T(8,128)(2,1)} %refs_4_.4), channel_id=1, source_target_pairs={{0,1},{1,0},{2,3},{3,2},{4,5},{5,4},{6,7},{7,6},{8,9},{9,8},{10,11... | collective-permute-start | bytes 8847368 | tf_op jit(solution)/shard_map/ppermute | solution.py:342
  0.5 61.1 %collective-permute-start.13 = (bf16[1280,1152]{1,0:T(8,128)(2,1)}, bf16[1280,1152]{1,0:T(8,128)(2,1)}, u32[]{:S(2)}, u32[]{:S(2)}) collective-permute-start(bf16[1280,1152]{1,0:T(8,128)(2,1)} %refs_5_.3), channel_id=1, source_target_pairs={{0,1},{1,0},{2,3},{3,2},{4,5},{5,4},{6,7},{7,6},{8,9},{9,8},{10,11... | collective-permute-start | bytes 8847368 | tf_op jit(solution)/shard_map/ppermute | solution.py:343
  2.4 9.8 %copy-start.14 = (s32[8,256]{1,0:T(8,128)S(1)}, s32[8,256]{1,0:T(8,128)}, u32[]{:S(2)}) copy-start(s32[8,256]{1,0:T(8,128)} %place_rows.1.refs_0_) | copy-start | bytes 24580
  2.4 8.8 %collective-permute-start.2 = (s32[8,256]{1,0:T(8,128)}, s32[8,256]{1,0:T(8,128)S(1)}, u32[]{:S(2)}, u32[]{:S(2)}) collective-permute-start(s32[8,256]{1,0:T(8,128)} %place_rows.1.refs_0_), channel_id=1, source_target_pairs={{0,12},{4,8},{8,4},{12,0},{1,13},{5,9},{9,5},{13,1},{2,14},{6,10},... | collective-permute-start | bytes 24584 | tf_op jit(solution)/shard_map/ppermute | solution.py:256
  7.5 4.8 %collective-permute-start.1 = (s32[8,256]{1,0:T(8,128)}, s32[8,256]{1,0:T(8,128)S(1)}, u32[]{:S(2)}, u32[]{:S(2)}) collective-permute-start(s32[8,256]{1,0:T(8,128)} %place_rows.1.refs_0_), channel_id=1, source_target_pairs={{0,8},{4,12},{8,0},{12,4},{1,9},{5,13},{9,1},{13,5},{2,10},{6,14},... | collective-permute-start | bytes 24584 | tf_op jit(solution)/shard_map/ppermute | solution.py:256
  7.5 4.8 %collective-permute-start = (s32[8,256]{1,0:T(8,128)}, s32[8,256]{1,0:T(8,128)S(1)}, u32[]{:S(2)}, u32[]{:S(2)}) collective-permute-start(s32[8,256]{1,0:T(8,128)} %place_rows.1.refs_0_), channel_id=1, source_target_pairs={{0,4},{4,0},{8,12},{12,8},{1,5},{5,1},{9,13},{13,9},{2,6},{6,2},{1... | collective-permute-start | bytes 24584 | tf_op jit(solution)/shard_map/ppermute | solution.py:256
  8.0 1.3 %copy-start.7 = (bf16[8,1024,80]{1,2,0:T(8,128)(2,1)S(1)}, bf16[8,1024,80]{1,2,0:T(8,128)(2,1)}, u32[]{:S(2)}) copy-start(bf16[8,1024,80]{1,2,0:T(8,128)(2,1)} %param.11) | copy-start | bytes 3932164
  9.4 0.9 %copy-start.15 = (bf16[8,1024,5]{1,0,2:T(8,128)(2,1)S(1)}, bf16[8,1024,5]{1,0,2:T(8,128)(2,1)}, u32[]{:S(2)}) copy-start(bf16[8,1024,5]{1,0,2:T(8,128)(2,1)} %param.12) | copy-start | bytes 245764
  13.7 7.0 %collective-permute-start.14 = (bf16[320,256]{1,0:T(8,128)(2,1)S(1)}, bf16[320,256]{1,0:T(8,128)(2,1)S(1)}, u32[]{:S(2)}, u32[]{:S(2)}) collective-permute-start(bf16[320,256]{1,0:T(8,128)(2,1)S(1)} %get-tuple-element.37), channel_id=1, source_target_pairs={{0,4},{12,8},{1,5},{13,9},{2,6},{14,10},{3,7},{15,11},{16,20},{28,... | collective-permute-start | bytes 491528 | tf_op jit(solution)/shard_map/ppermute | solution.py:277
  16.0 9.0 %collective-permute-start.3 = (bf16[320,256]{1,0:T(8,128)(2,1)S(1)}, bf16[320,256]{1,0:T(8,128)(2,1)S(1)}, u32[]{:S(2)}, u32[]{:S(2)}) collective-permute-start(bf16[320,256]{1,0:T(8,128)(2,1)S(1)} %get-tuple-element.29), channel_id=1, source_target_pairs={{0,4},{12,8},{1,5},{13,9},{2,6},{14,10},{3,7},{15,11},{16,20},{28,... | collective-permute-start | bytes 491528 | tf_op jit(solution)/shard_map/ppermute | solution.py:277
  20.7 7.2 %collective-permute-start.15 = (bf16[320,256]{1,0:T(8,128)(2,1)S(1)}, bf16[320,256]{1,0:T(8,128)(2,1)S(1)}, u32[]{:S(2)}, u32[]{:S(2)}) collective-permute-start(bf16[320,256]{1,0:T(8,128)(2,1)S(1)} %get-tuple-element.38), channel_id=1, source_target_pairs={{0,4},{12,8},{1,5},{13,9},{2,6},{14,10},{3,7},{15,11},{16,20},{28,... | collective-permute-start | bytes 491528 | tf_op jit(solution)/shard_map/ppermute | solution.py:277
  25.1 10.6 %collective-permute-start.7 = (bf16[320,256]{1,0:T(8,128)(2,1)S(1)}, bf16[320,256]{1,0:T(8,128)(2,1)S(1)}, u32[]{:S(2)}, u32[]{:S(2)}) collective-permute-start(bf16[320,256]{1,0:T(8,128)(2,1)S(1)} %add.28), channel_id=1, source_target_pairs={{4,8},{8,4},{5,9},{9,5},{6,10},{10,6},{7,11},{11,7},{20,24},{24,20... | collective-permute-start | bytes 491528 | tf_op jit(solution)/shard_map/ppermute | solution.py:278
  25.8 31.5 %copy-start.4 = (bf16[256,2304]{1,0:T(8,128)(2,1)S(1)}, bf16[256,2304]{1,0:T(8,128)(2,1)}, u32[]{:S(2)}) copy-start(bf16[256,2304]{1,0:T(8,128)(2,1)} %refs_3_.1) | copy-start | bytes 3538948
  25.9 11.3 %collective-permute-start.18 = (bf16[320,256]{1,0:T(8,128)(2,1)S(1)}, bf16[320,256]{1,0:T(8,128)(2,1)S(1)}, u32[]{:S(2)}, u32[]{:S(2)}) collective-permute-start(bf16[320,256]{1,0:T(8,128)(2,1)S(1)} %add.31), channel_id=1, source_target_pairs={{4,8},{8,4},{5,9},{9,5},{6,10},{10,6},{7,11},{11,7},{20,24},{24,20... | collective-permute-start | bytes 491528 | tf_op jit(solution)/shard_map/ppermute | solution.py:278
  27.9 10.2 %collective-permute-start.4 = (bf16[320,256]{1,0:T(8,128)(2,1)S(1)}, bf16[320,256]{1,0:T(8,128)(2,1)S(1)}, u32[]{:S(2)}, u32[]{:S(2)}) collective-permute-start(bf16[320,256]{1,0:T(8,128)(2,1)S(1)} %get-tuple-element.30), channel_id=1, source_target_pairs={{0,4},{12,8},{1,5},{13,9},{2,6},{14,10},{3,7},{15,11},{16,20},{28,... | collective-permute-start | bytes 491528 | tf_op jit(solution)/shard_map/ppermute | solution.py:277
  35.7 10.9 %copy-start.9 = (bf16[320,256]{1,0:T(8,128)(2,1)}, bf16[320,256]{1,0:T(8,128)(2,1)S(1)}, u32[]{:S(2)}) copy-start(bf16[320,256]{1,0:T(8,128)(2,1)S(1)} %get-tuple-element.35.outer_ref) | copy-start | bytes 491524
  35.7 10.9 %copy-start.12 = (bf16[320,256]{1,0:T(8,128)(2,1)}, bf16[320,256]{1,0:T(8,128)(2,1)S(1)}, u32[]{:S(2)}) copy-start(bf16[320,256]{1,0:T(8,128)(2,1)S(1)} %get-tuple-element.39.inner_ref) | copy-start | bytes 491524
  35.7 18.0 %copy-start.8 = (bf16[320,256]{1,0:T(8,128)(2,1)}, bf16[320,256]{1,0:T(8,128)(2,1)S(1)}, u32[]{:S(2)}) copy-start(bf16[320,256]{1,0:T(8,128)(2,1)S(1)} %get-tuple-element.27.outer_ref) | copy-start | bytes 491524
  35.7 18.0 %copy-start.11 = (bf16[320,256]{1,0:T(8,128)(2,1)}, bf16[320,256]{1,0:T(8,128)(2,1)S(1)}, u32[]{:S(2)}) copy-start(bf16[320,256]{1,0:T(8,128)(2,1)S(1)} %get-tuple-element.31.inner_ref) | copy-start | bytes 491524
  35.7 4.1 %collective-permute-start.16 = (bf16[320,256]{1,0:T(8,128)(2,1)S(1)}, bf16[320,256]{1,0:T(8,128)(2,1)S(1)}, u32[]{:S(2)}, u32[]{:S(2)}) collective-permute-start(bf16[320,256]{1,0:T(8,128)(2,1)S(1)} %get-tuple-element.39.inner_ref), channel_id=1, source_target_pairs={{0,4},{12,8},{1,5},{13,9},{2,6},{14,10},{3,7},{15,11},{16,20},{28,... | collective-permute-start | bytes 491528 | tf_op jit(solution)/shard_map/ppermute | solution.py:277
  37.1 7.2 %collective-permute-start.17 = (bf16[320,256]{1,0:T(8,128)(2,1)S(1)}, bf16[320,256]{1,0:T(8,128)(2,1)S(1)}, u32[]{:S(2)}, u32[]{:S(2)}) collective-permute-start(bf16[320,256]{1,0:T(8,128)(2,1)S(1)} %add.30), channel_id=1, source_target_pairs={{4,8},{8,4},{5,9},{9,5},{6,10},{10,6},{7,11},{11,7},{20,24},{24,20... | collective-permute-start | bytes 491528 | tf_op jit(solution)/shard_map/ppermute | solution.py:278
  38.1 7.2 %collective-permute-start.19 = (bf16[320,256]{1,0:T(8,128)(2,1)S(1)}, bf16[320,256]{1,0:T(8,128)(2,1)S(1)}, u32[]{:S(2)}, u32[]{:S(2)}) collective-permute-start(bf16[320,256]{1,0:T(8,128)(2,1)S(1)} %add.32), channel_id=1, source_target_pairs={{4,0},{8,12},{5,1},{9,13},{6,2},{10,14},{7,3},{11,15},{20,16},{24,... | collective-permute-start | bytes 491528 | tf_op jit(solution)/shard_map/ppermute | solution.py:279
  39.9 6.7 %copy-start.18 = (bf16[320,256]{1,0:T(8,128)(2,1)}, bf16[320,256]{1,0:T(8,128)(2,1)S(1)}, u32[]{:S(2)}) copy-start(bf16[320,256]{1,0:T(8,128)(2,1)S(1)} %collective-permute-done.16.refs_0_) | copy-start | bytes 491524
  39.9 8.8 %collective-permute-start.5 = (bf16[320,256]{1,0:T(8,128)(2,1)S(1)}, bf16[320,256]{1,0:T(8,128)(2,1)S(1)}, u32[]{:S(2)}, u32[]{:S(2)}) collective-permute-start(bf16[320,256]{1,0:T(8,128)(2,1)S(1)} %get-tuple-element.31.inner_ref), channel_id=1, source_target_pairs={{0,4},{12,8},{1,5},{13,9},{2,6},{14,10},{3,7},{15,11},{16,20},{28,... | collective-permute-start | bytes 491528 | tf_op jit(solution)/shard_map/ppermute | solution.py:277
  44.3 2.3 %copy-start.20 = (bf16[320,256]{1,0:T(8,128)(2,1)}, bf16[320,256]{1,0:T(8,128)(2,1)S(1)}, u32[]{:S(2)}) copy-start(bf16[320,256]{1,0:T(8,128)(2,1)S(1)} %collective-permute-done.17.refs_1_) | copy-start | bytes 491524
  44.3 5.9 %collective-permute-start.6 = (bf16[320,256]{1,0:T(8,128)(2,1)S(1)}, bf16[320,256]{1,0:T(8,128)(2,1)S(1)}, u32[]{:S(2)}, u32[]{:S(2)}) collective-permute-start(bf16[320,256]{1,0:T(8,128)(2,1)S(1)} %add.27), channel_id=1, source_target_pairs={{4,8},{8,4},{5,9},{9,5},{6,10},{10,6},{7,11},{11,7},{20,24},{24,20... | collective-permute-start | bytes 491528 | tf_op jit(solution)/shard_map/ppermute | solution.py:278
  45.3 1.3 %copy-start.22 = (bf16[320,256]{1,0:T(8,128)(2,1)}, bf16[320,256]{1,0:T(8,128)(2,1)S(1)}, u32[]{:S(2)}) copy-start(bf16[320,256]{1,0:T(8,128)(2,1)S(1)} %collective-permute-done.19.refs_2_) | copy-start | bytes 491524
  45.3 7.2 %collective-permute-start.8 = (bf16[320,256]{1,0:T(8,128)(2,1)S(1)}, bf16[320,256]{1,0:T(8,128)(2,1)S(1)}, u32[]{:S(2)}, u32[]{:S(2)}) collective-permute-start(bf16[320,256]{1,0:T(8,128)(2,1)S(1)} %add.29), channel_id=1, source_target_pairs={{4,0},{8,12},{5,1},{9,13},{6,2},{10,14},{7,3},{11,15},{20,16},{24,... | collective-permute-start | bytes 491528 | tf_op jit(solution)/shard_map/ppermute | solution.py:279
  48.7 5.1 %copy-start.17 = (bf16[320,256]{1,0:T(8,128)(2,1)}, bf16[320,256]{1,0:T(8,128)(2,1)S(1)}, u32[]{:S(2)}) copy-start(bf16[320,256]{1,0:T(8,128)(2,1)S(1)} %collective-permute-done.5.refs_0_) | copy-start | bytes 491524
  48.7 10.0 %collective-permute-start.22 = (bf16[320,256]{1,0:T(8,128)(2,1)}, bf16[320,256]{1,0:T(8,128)(2,1)S(1)}, u32[]{:S(2)}, u32[]{:S(2)}) collective-permute-start(bf16[320,256]{1,0:T(8,128)(2,1)} %get-tuple-element.41.refs_2_), channel_id=1, source_target_pairs={{0,2},{2,0},{1,3},{3,1},{4,6},{6,4},{5,7},{7,5},{8,10},{10,8},{9,1... | collective-permute-start | bytes 491528 | tf_op jit(solution)/shard_map/ppermute | solution.py:358
  50.2 3.6 %copy-start.19 = (bf16[320,256]{1,0:T(8,128)(2,1)}, bf16[320,256]{1,0:T(8,128)(2,1)S(1)}, u32[]{:S(2)}) copy-start(bf16[320,256]{1,0:T(8,128)(2,1)S(1)} %collective-permute-done.6.refs_1_) | copy-start | bytes 491524
  50.2 5.7 %collective-permute-start.21 = (bf16[320,128]{1,0:T(8,128)(2,1)}, bf16[320,128]{1,0:T(8,128)(2,1)S(1)}, u32[]{:S(2)}, u32[]{:S(2)}) collective-permute-start(bf16[320,128]{1,0:T(8,128)(2,1)} %get-tuple-element.40), channel_id=1, source_target_pairs={{0,3},{2,1},{4,7},{6,5},{8,11},{10,9},{12,15},{14,13},{16,19},{18,... | collective-permute-start | bytes 245768 | tf_op jit(solution)/shard_map/ppermute | solution.py:362
  52.5 1.3 %copy-start.21 = (bf16[320,256]{1,0:T(8,128)(2,1)}, bf16[320,256]{1,0:T(8,128)(2,1)S(1)}, u32[]{:S(2)}) copy-start(bf16[320,256]{1,0:T(8,128)(2,1)S(1)} %collective-permute-done.8.refs_2_) | copy-start | bytes 491524
  52.5 4.9 %collective-permute-start.20 = (bf16[320,128]{1,0:T(8,128)(2,1)}, bf16[320,128]{1,0:T(8,128)(2,1)S(1)}, u32[]{:S(2)}, u32[]{:S(2)}) collective-permute-start(bf16[320,128]{1,0:T(8,128)(2,1)} %get-tuple-element.40), channel_id=1, source_target_pairs={{0,1},{2,3},{4,5},{6,7},{8,9},{10,11},{12,13},{14,15},{16,17},{18,... | collective-permute-start | bytes 245768 | tf_op jit(solution)/shard_map/ppermute | solution.py:362
  55.9 15.8 %collective-permute-start.11 = (bf16[320,256]{1,0:T(8,128)(2,1)}, bf16[320,256]{1,0:T(8,128)(2,1)S(1)}, u32[]{:S(2)}, u32[]{:S(2)}) collective-permute-start(bf16[320,256]{1,0:T(8,128)(2,1)} %get-tuple-element.33.refs_2_), channel_id=1, source_target_pairs={{0,2},{2,0},{1,3},{3,1},{4,6},{6,4},{5,7},{7,5},{8,10},{10,8},{9,1... | collective-permute-start | bytes 491528 | tf_op jit(solution)/shard_map/ppermute | solution.py:358
  57.4 14.3 %collective-permute-start.23 = (bf16[16,2304]{1,0:T(8,128)(2,1)S(1)}, bf16[16,2304]{1,0:T(8,128)(2,1)S(1)}, u32[]{:S(2)}, u32[]{:S(2)}) collective-permute-start(bf16[16,2304]{1,0:T(8,128)(2,1)S(1)} %slice.3), channel_id=1, source_target_pairs={{0,1},{4,5},{8,9},{12,13},{2,3},{6,7},{10,11},{14,15},{16,17},{20,... | collective-permute-start | bytes 221192 | tf_op jit(solution)/shard_map/ppermute | solution.py:341
  58.7 13.0 %collective-permute-start.10 = (bf16[320,128]{1,0:T(8,128)(2,1)}, bf16[320,128]{1,0:T(8,128)(2,1)S(1)}, u32[]{:S(2)}, u32[]{:S(2)}) collective-permute-start(bf16[320,128]{1,0:T(8,128)(2,1)} %get-tuple-element.32), channel_id=1, source_target_pairs={{0,3},{2,1},{4,7},{6,5},{8,11},{10,9},{12,15},{14,13},{16,19},{18,... | collective-permute-start | bytes 245768 | tf_op jit(solution)/shard_map/ppermute | solution.py:362
  60.0 11.7 %collective-permute-start.9 = (bf16[320,128]{1,0:T(8,128)(2,1)}, bf16[320,128]{1,0:T(8,128)(2,1)S(1)}, u32[]{:S(2)}, u32[]{:S(2)}) collective-permute-start(bf16[320,128]{1,0:T(8,128)(2,1)} %get-tuple-element.32), channel_id=1, source_target_pairs={{0,1},{2,3},{4,5},{6,7},{8,9},{10,11},{12,13},{14,15},{16,17},{18,... | collective-permute-start | bytes 245768 | tf_op jit(solution)/shard_map/ppermute | solution.py:362
  61.6 1.8 %copy-start = (bf16[1280,1152]{1,0:T(8,128)(2,1)S(1)}, bf16[1280,1152]{1,0:T(8,128)(2,1)}, u32[]{:S(2)}) copy-start(bf16[1280,1152]{1,0:T(8,128)(2,1)} %refs_4_.4) | copy-start | bytes 8847364
  63.4 1.8 %copy-start.2 = (bf16[1280,1152]{1,0:T(8,128)(2,1)S(1)}, bf16[1280,1152]{1,0:T(8,128)(2,1)}, u32[]{:S(2)}) copy-start(bf16[1280,1152]{1,0:T(8,128)(2,1)} %refs_5_.3) | copy-start | bytes 8847364
  65.2 0.9 %copy-start.13 = (bf16[320,256]{1,0:T(8,128)(2,1)S(1)}, bf16[320,256]{1,0:T(8,128)(2,1)}, u32[]{:S(2)}) copy-start(bf16[320,256]{1,0:T(8,128)(2,1)} %get-tuple-element.41.refs_2_) | copy-start | bytes 491524
  66.1 5.5 %copy-start.1 = (bf16[1280,1152]{1,0:T(8,128)(2,1)S(1)}, bf16[1280,1152]{1,0:T(8,128)(2,1)}, u32[]{:S(2)}) copy-start(bf16[1280,1152]{1,0:T(8,128)(2,1)} %refs_4_.4) | copy-start | bytes 8847364
  66.1 5.5 %copy-start.3 = (bf16[1280,1152]{1,0:T(8,128)(2,1)S(1)}, bf16[1280,1152]{1,0:T(8,128)(2,1)}, u32[]{:S(2)}) copy-start(bf16[1280,1152]{1,0:T(8,128)(2,1)} %refs_5_.3) | copy-start | bytes 8847364
  66.1 5.5 %copy-start.10 = (bf16[320,256]{1,0:T(8,128)(2,1)S(1)}, bf16[320,256]{1,0:T(8,128)(2,1)}, u32[]{:S(2)}) copy-start(bf16[320,256]{1,0:T(8,128)(2,1)} %get-tuple-element.33.refs_2_) | copy-start | bytes 491524
  71.7 10.8 %copy-start.16 = (f32[4,2304]{1,0:T(4,128)S(1)}, f32[4,2304]{1,0:T(4,128)}, u32[]{:S(2)}) copy-start(f32[4,2304]{1,0:T(4,128)} %refs_4_.5) | copy-start | bytes 110596
  77.3 1.5 %copy-start.5 = (f32[2,272,1152]{2,1,0:T(8,128)}, f32[2,272,1152]{2,1,0:T(8,128)S(1)}, u32[]{:S(2)}) copy-start(f32[2,272,1152]{2,1,0:T(8,128)S(1)} %get-tuple-element.46.refs_2_) | copy-start | bytes 7520260
  78.8 3.7 %collective-permute-start.24 = (f32[8,272]{1,0:T(8,128)S(1)}, f32[8,272]{1,0:T(8,128)S(1)}, u32[]{:S(2)}, u32[]{:S(2)}) collective-permute-start(f32[8,272]{1,0:T(8,128)S(1)} %get-tuple-element.45.refs_0_), channel_id=1, source_target_pairs={{0,2},{2,0},{1,3},{3,1},{4,6},{6,4},{5,7},{7,5},{8,10},{10,8},{9,1... | collective-permute-start | bytes 26120 | tf_op jit(solution)/shard_map/ppermute | solution.py:392
  82.5 1.7 %copy-start.6 = (f32[2,272,1152]{2,1,0:T(8,128)S(1)}, f32[2,272,1152]{2,1,0:T(8,128)}, u32[]{:S(2)}) copy-start(f32[2,272,1152]{2,1,0:T(8,128)} %copy-done.5) | copy-start | bytes 7520260

commit v4 on v3

--- a/solution.py
+++ b/solution.py
@@ -108,10 +108,7 @@
     for n, target in enumerate(targets):
         local = stack[scalars_ref[1 + target]] - scalars_ref[0]
         for head in range(heads):
-            stream, at = divmod(head, heads // 2)
-            outs[2 * n + stream][at * width : (at + 1) * width, :] = picked(
-                local, table_ref, head
-            )
+            outs[n][head * width : (head + 1) * width, :] = picked(local, table_ref, head)
 
 
 def merge_kernel(middle_ref, inner_ref, outer_ref, *refs):
@@ -125,73 +122,80 @@
     rim_ref[...] = total[:, total.shape[1] - LANES :]
 
 
-def project_kernel(count, stream, where_ref, *refs):
-    rims = refs[:count]
-    pieces = refs[count : 2 * count]
-    refs = refs[2 * count :]
+def project_kernel(shifts, count, where_ref, *refs):
+    pieces = len(shifts)
+    first = 0 in shifts
+    rims = refs[:pieces]
+    bodies = refs[pieces : 2 * pieces]
+    refs = refs[2 * pieces :]
     weights = refs[:4]
-    if stream == 0:
+    if first:
         key_ref, value_ref, held, sems = refs[4:]
     else:
         begun_keys, begun_values, hidden_halo, hidden, value_ref, stats_ref = refs[4:10]
-        held, sems, states = refs[10:]
-    half = value_ref.shape[-1]
-    depth, tokens = pieces[0].shape
+        held, sems, states, done, done_sems = refs[10:]
+    half = held.shape[-1]
+    depth, tokens = bodies[0].shape
     rep = where_ref[0]
     tp = where_ref[1]
     copies = []
     for far in range(2):
         for which in range(2):
-            for s in range(count):
-                owner = lax.rem(tp + count - s, count)
-                at = pl.multiple_of((2 * owner + stream) * depth, depth)
+            for n, s in enumerate(shifts):
+                at = pl.multiple_of(lax.rem(tp + count - s, count) * depth, depth)
                 copy = pltpu.make_async_copy(
                     weights[2 * far + which].at[pl.ds(at, depth), :],
-                    held.at[far, which, pl.ds(s * depth, depth), :],
-                    sems.at[(2 * far + which) * count + s],
+                    held.at[far, which, pl.ds(n * depth, depth), :],
+                    sems.at[(2 * far + which) * pieces + n],
                 )
                 copy.start()
                 copies.append(copy)
-    body = jnp.concatenate([p[...].astype(F32) for p in pieces], axis=0).T.astype(BF16)
+    body = jnp.concatenate([b[...].astype(F32) for b in bodies], axis=0).T.astype(BF16)
     rim = jnp.concatenate([r[...].astype(F32) for r in rims], axis=0).T.astype(BF16)
     memory = jnp.concatenate([rim[LANES - RIM :], body], axis=0)
-    if stream == 1:
+    if not first:
         for slot in range(2):
             states[slot, :RIM] = hidden_halo[:, slot * half : (slot + 1) * half]
             states[slot, RIM:] = hidden[:, slot * half : (slot + 1) * half]
     sums = [0.0] * 4
+    out_copies = []
     for far in range(2):
         slot = rep if far == 0 else 1 - rep
         fields = []
         for which in range(2):
-            for s in range(count):
-                copies[(2 * far + which) * count + s].wait()
+            for n in range(pieces):
+                copies[(2 * far + which) * pieces + n].wait()
             fields.append(dot(memory, held[far, which]))
         keys, values = fields
-        if stream == 0:
+        if first:
             key_ref[slot] = keys
             value_ref[slot] = values
         else:
             keys = keys + begun_keys[slot]
             values = values + begun_values[slot]
+            done[far] = values
+            copy = pltpu.make_async_copy(done.at[far], value_ref.at[slot], done_sems.at[far])
+            copy.start()
+            out_copies.append(copy)
             here = states[slot].astype(F32)
             terms = (here * here, keys * keys, here * keys, values * values)
             sums = [a + jnp.sum(t, axis=1, keepdims=True) for a, t in zip(sums, terms)]
-            value_ref[slot] = values
-    if stream == 1:
+    if not first:
         rows = memory.shape[0]
         lane = iota((rows, 8), 1)
         packed = jnp.zeros((rows, 8), F32)
         for k in range(4):
             packed = jnp.where(lane == k, sums[k], packed)
         stats_ref[...] = dot_nt(unit(8, F32), packed, lax.Precision.HIGHEST)
+        for copy in out_copies:
+            copy.wait()
 
 
 def finish_kernel(count, keep_ref, *refs):
     stats = refs[:count]
-    value_ref, hidden_ref, taps_ref, out_ref, columns, normed = refs[count:]
+    value_ref, hidden_ref, taps_ref, out_ref, gates, factors, normed = refs[count:]
     rows = normed.shape[0]
-    tokens = out_ref.shape[0]
+    tokens, step = out_ref.shape
 
     @pl.when(pl.program_id(0) == 0)
     def _():
@@ -205,25 +209,36 @@
         factor = jnp.where((iota(factor.shape, 1) < RIM) & (keep_ref[0] == 0), 0.0, factor)
         line = iota(total.shape, 0)
         both = jnp.where(line == 0, gate, jnp.where(line == 1, factor, 0.0))
-        columns[...] = dot_nt(unit(rows, F32), both, lax.Precision.HIGHEST)
-
-    values = value_ref[...]
-    normed[...] = values * columns[:, 1:2]
-    conv = None
-    for tap in range(KERNEL):
-        lag = DILATION * tap
-        term = taps_ref[tap : tap + 1, :] * normed[RIM - lag : RIM - lag + tokens, :]
-        conv = term if conv is None else conv + term
-    gated = values[RIM:] * columns[RIM:, 0:1]
-    out_ref[...] = (hidden_ref[...].astype(F32) + jax.nn.silu(conv) + gated).astype(BF16)
+        columns = dot_nt(unit(rows, F32), both, lax.Precision.HIGHEST)
+        gates[...] = jnp.broadcast_to(columns[RIM:, 0:1], gates.shape)
+        factors[...] = jnp.broadcast_to(columns[:, 1:2], factors.shape)
+
+    for start in range(0, step, LANES):
+        size = min(LANES, step - start)
+        span = slice(start, start + size)
+        values = value_ref[:, span]
+        normed[:, span] = values * factors[:, :size]
+        conv = None
+        for tap in range(KERNEL):
+            lag = DILATION * tap
+            term = taps_ref[tap : tap + 1, span] * normed[RIM - lag : RIM - lag + tokens, span]
+            conv = term if conv is None else conv + term
+        gated = values[RIM:] * gates[:, :size]
+        out_ref[:, span] = (
+            hidden_ref[:, span].astype(F32) + jax.nn.silu(conv) + gated
+        ).astype(BF16)
 
 
 def whole(array):
     return pl.BlockSpec(array.shape, lambda *_: (0,) * array.ndim)
 
 
-def in_vmem(array):
-    return pltpu.with_memory_space_constraint(array, pltpu.VMEM)
+def in_hbm(array):
+    return pltpu.with_memory_space_constraint(array, pltpu.HBM)
+
+
+def limit(mib):
+    return pltpu.CompilerParams(vmem_limit_bytes=mib << 20)
 
 
 def scattered_sum(stored, decoded, here):
@@ -241,12 +256,11 @@
         ],
         out_specs=pl.BlockSpec((None, heads * width, tokens), lambda m: (m, 0, 0)),
         out_shape=jax.ShapeDtypeStruct((mems, heads * width, tokens), BF16),
-        compiler_params=pltpu.CompilerParams(vmem_limit_bytes=16 << 20),
+        compiler_params=limit(16),
         name="pick_all",
     )((here * rows).astype(I32).reshape(1), asked, decoded)
     total = lax.psum_scatter(partial, "mem", scatter_dimension=0, tiled=False)
-    memory = jnp.split(total, 2, axis=0)
-    return memory, [m[:, tokens - LANES :] for m in memory]
+    return total, total[:, tokens - LANES :]
 
 
 def line_sum(stored, decoded, here):
@@ -258,49 +272,50 @@
     right = here >= 2
     order = [here ^ jnp.where(right, j, 3 - j) for j in range(4)]
     scalars = jnp.stack([here * rows] + order).astype(I32)
-    block = jax.ShapeDtypeStruct((heads * width // 2, tokens), BF16)
+    block = jax.ShapeDtypeStruct((heads * width, tokens), BF16)
 
     def pick(*targets):
         return pl.pallas_call(
             functools.partial(pick_kernel, 4, targets),
             in_specs=[pl.BlockSpec(memory_space=pltpu.SMEM)]
             + [pl.BlockSpec(memory_space=pltpu.VMEM)] * 5,
-            out_shape=(block,) * (2 * len(targets)),
+            out_shape=(block,) * len(targets),
             scratch_shapes=[pltpu.VMEM((4, heads, tokens), I32)],
-            compiler_params=pltpu.CompilerParams(vmem_limit_bytes=16 << 20),
+            compiler_params=limit(8),
             name="pick_rows",
         )(scalars, *asked, decoded)
 
     def after(x, *others):
         return lax.optimization_barrier((x, *others))[0]
 
-    inward = lambda x: lax.ppermute(x, "mem", [(0, 1), (3, 2)])
-    across = lambda x: lax.ppermute(x, "mem", [(1, 2), (2, 1)])
-    outward = lambda x: lax.ppermute(x, "mem", [(1, 0), (2, 3)])
-
-    farthest = pick(0)
-    first = [inward(x) for x in farthest]
-    second_own = pick(1)
-    rest = pick(2, 3)
-    inner, outer = rest[:2], rest[2:]
+    def inward(x):
+        return lax.ppermute(x, "mem", [(0, 1), (3, 2)])
+
+    def across(x):
+        return lax.ppermute(x, "mem", [(1, 2), (2, 1)])
+
+    def outward(x):
+        return lax.ppermute(x, "mem", [(1, 0), (2, 3)])
+
+    (farthest,) = pick(0)
+    first = inward(farthest)
+    far_own, inner, outer = pick(1, 2, 3)
+    far_own, crossing = lax.optimization_barrier((far_own, farthest + first))
+    second = inward(far_own)
+    crossed = across(crossing)
+    inner, near, leaving = lax.optimization_barrier((inner, far_own + second, outer + crossed))
+    third = inward(inner)
+    crossed_near = across(near)
+    last = outward(leaving)
     middle = ((here == 1) | (here == 2)).astype(I32).reshape(1)
-    memory, rims = [], []
-    for n in range(2):
-        crossed = across(farthest[n] + first[n])
-        second = inward(after(second_own[n], first[n]))
-        crossed_near = across(second_own[n] + second)
-        third = inward(after(inner[n], second))
-        last = outward(outer[n] + crossed)
-        total, rim = pl.pallas_call(
-            merge_kernel,
-            in_specs=[pl.BlockSpec(memory_space=pltpu.SMEM)]
-            + [pl.BlockSpec(memory_space=pltpu.VMEM)] * 5,
-            out_shape=(block, jax.ShapeDtypeStruct((block.shape[0], LANES), BF16)),
-            name="merge",
-        )(middle, inner[n], outer[n], third, crossed_near, last)
-        memory.append(total)
-        rims.append(rim)
-    return memory, rims
+    return pl.pallas_call(
+        merge_kernel,
+        in_specs=[pl.BlockSpec(memory_space=pltpu.SMEM)]
+        + [pl.BlockSpec(memory_space=pltpu.VMEM)] * 5,
+        out_shape=(block, jax.ShapeDtypeStruct((block.shape[0], LANES), BF16)),
+        compiler_params=limit(4),
+        name="merge",
+    )(middle, inner, outer, third, crossed_near, last)
 
 
 def shards(
@@ -322,71 +337,76 @@
     stored = pl.pallas_call(
         place_kernel,
         out_shape=jax.ShapeDtypeStruct((heads, tokens), I32),
+        compiler_params=limit(4),
         name="place_rows",
     )(row_ids.T, row_place.reshape(-1, LANES))
     decoded = pl.pallas_call(
         decode_kernel,
         out_shape=jax.ShapeDtypeStruct((heads, width, rows), BF16),
-        compiler_params=pltpu.CompilerParams(vmem_limit_bytes=16 << 20),
+        compiler_params=limit(16),
         name="decode_tables",
     )(table_codes.transpose(0, 2, 1), table_scales.transpose(2, 0, 1))
     here = lax.axis_index("mem")
     if mems == 4:
-        memory, rims = line_sum(stored, decoded, here)
+        memory, rim = line_sum(stored, decoded, here)
     else:
-        memory, rims = scattered_sum(stored, decoded, here)
+        memory, rim = scattered_sum(stored, decoded, here)
 
     _, tail = lax.optimization_barrier((stored, hidden[tokens - RIM :]))
     needed = [(i, i + 1) for i in range(blocks - 1) if (i + 1) * tokens % seq_length]
     hidden_halo = lax.ppermute(tail, ("mem", "rep"), needed)
     other_key = lax.ppermute(key_weight, "rep", [(0, 1), (1, 0)])
     other_value = lax.ppermute(value_weight, "rep", [(0, 1), (1, 0)])
-    weights = (key_weight, value_weight, other_key, other_value)
+    weights = [in_hbm(w) for w in (key_weight, value_weight, other_key, other_value)]
 
     where = jnp.stack([lax.axis_index("rep"), lax.axis_index("tp")]).astype(I32)
     extended = tokens + RIM
-    part = depth // 2
+    bodies = [memory] + [
+        lax.ppermute(memory, "tp", [(i, (i + s) % tps) for i in range(tps)])
+        for s in range(1, tps)
+    ]
+    rims = [
+        lax.ppermute(
+            rim,
+            ("mem", "tp", "rep"),
+            [
+                (
+                    (a // reps * tps + i) * reps + a % reps,
+                    (b // reps * tps + (i + s) % tps) * reps + b % reps,
+                )
+                for a, b in needed
+                for i in range(tps)
+            ],
+        )
+        for s in range(tps)
+    ]
     field = jax.ShapeDtypeStruct((2, extended, half), F32)
-    held = pltpu.VMEM((2, 2, tps * part, half), BF16)
-    sems = pltpu.SemaphoreType.DMA((4 * tps,))
     anywhere = pl.BlockSpec(memory_space=pl.ANY)
     resident = pl.BlockSpec(memory_space=pltpu.VMEM)
-    limit = pltpu.CompilerParams(vmem_limit_bytes=16 << 20)
-    inputs = []
-    for stream in range(2):
-        inner = [memory[stream]] + [
-            lax.ppermute(memory[stream], "tp", [(i, (i + s) % tps) for i in range(tps)])
-            for s in range(1, tps)
-        ]
-        rim = [
-            lax.ppermute(
-                rims[stream],
-                ("mem", "tp", "rep"),
-                [
-                    ((a // reps * tps + i) * reps + a % reps, (b // reps * tps + (i + s) % tps) * reps + b % reps)
-                    for a, b in needed
-                    for i in range(tps)
-                ],
-            )
-            for s in range(tps)
-        ]
-        inputs.append((where, *rim, *inner, *weights))
     begun = pl.pallas_call(
-        functools.partial(project_kernel, tps, 0),
-        in_specs=[smem] + [resident] * (2 * tps) + [anywhere] * 4,
+        functools.partial(project_kernel, (0,), tps),
+        in_specs=[smem] + [resident] * 2 + [anywhere] * 4,
         out_shape=(field, field),
-        scratch_shapes=[held, sems],
-        compiler_params=limit,
-        name="project_first",
-    )(*inputs[0])
+        scratch_shapes=[pltpu.VMEM((2, 2, depth, half), BF16), pltpu.SemaphoreType.DMA((4,))],
+        compiler_params=limit(16),
+        name="project_own",
+    )(where, rims[0], memory, *weights)
+    others = tps - 1
     values, stats = pl.pallas_call(
-        functools.partial(project_kernel, tps, 1),
-        in_specs=[smem] + [resident] * (2 * tps) + [anywhere] * 4 + [resident] * 4,
-        out_shape=(field, jax.ShapeDtypeStruct((8, extended), F32)),
-        scratch_shapes=[held, sems, pltpu.VMEM((2, extended, half), BF16)],
-        compiler_params=limit,
-        name="project_second",
-    )(*inputs[1], *[in_vmem(b) for b in begun], hidden_halo, hidden)
+        functools.partial(project_kernel, tuple(range(1, tps)), tps),
+        in_specs=[smem] + [resident] * (2 * others) + [anywhere] * 4 + [resident] * 4,
+        out_specs=(pl.BlockSpec(memory_space=pltpu.HBM), resident),
+        out_shape=(pltpu.HBM(field.shape, F32), jax.ShapeDtypeStruct((8, extended), F32)),
+        scratch_shapes=[
+            pltpu.VMEM((2, 2, others * depth, half), BF16),
+            pltpu.SemaphoreType.DMA((4 * others,)),
+            pltpu.VMEM((2, extended, half), BF16),
+            pltpu.VMEM((2, extended, half), F32),
+            pltpu.SemaphoreType.DMA((2,)),
+        ],
+        compiler_params=limit(20),
+        name="project_others",
+    )(where, *rims[1:], *bodies[1:], *weights, *begun, hidden_halo, hidden)
 
     all_stats = [stats] + [
         lax.ppermute(stats, "tp", [(i, (i + s) % tps) for i in range(tps)]) for s in range(1, tps)
@@ -416,10 +436,14 @@
         ],
         out_specs=spec(tokens),
         out_shape=out_shape,
-        scratch_shapes=[pltpu.VMEM((extended, 8), F32), pltpu.VMEM((extended, step), F32)],
-        compiler_params=pltpu.CompilerParams(vmem_limit_bytes=16 << 20),
+        scratch_shapes=[
+            pltpu.VMEM((tokens, LANES), F32),
+            pltpu.VMEM((extended, LANES), F32),
+            pltpu.VMEM((extended, step), F32),
+        ],
+        compiler_params=limit(16),
         name="finish",
-    )(keep, *all_stats, in_vmem(values), split(hidden), split(conv_weight))
+    )(keep, *all_stats, in_hbm(values), split(hidden), split(conv_weight))
     return out if aligned else jnp.concatenate([out[0], out[1]], axis=1)
 
 

time: 89.3 us -> 76.8 us (0.86)
  starting transfers between devices: 41.6 us -> 29.9 us
  waiting for transfers between devices: 8.74 us -> 17 us
  local copies, waits for them, and re-layouts: 10.1 us -> 3.72 us
  Pallas kernels: 27.3 us -> 24.4 us
    ppermute x18 -> x9, starting transfers between devices: 33.1 us -> 20.9 us  [the longest x3 14.1 us: inward(): return lax.ppermute(x, 'mem', [(0, 1), (3, 2)])]
    ppermute x18 -> x9, waiting for transfers between devices: 5.05 us -> 13.1 us  [the longest x3 10 us: inward(): return lax.ppermute(x, 'mem', [(0, 1), (3, 2)])]
    unnamed x46 -> x12, local copies, waits for them, and re-layouts: 10 us -> 3.63 us
    pallas_call x2 -> x1, Pallas kernels: 4.11 us -> 0.21 us  [line_sum(): pl.pallas_call(merge_kernel, in_specs=[pl.BlockSpec(memory_space=pltpu.SM...]
    pallas_call x1, Pallas kernels: 4.33 us -> 6.23 us  [shards(): pl.pallas_call(functools.partial(finish_kernel, tps), grid=(2 * per,), in...]
    pallas_call x1, Pallas kernels: 1.91 us -> 0.57 us  [shards(): pl.pallas_call(place_kernel, out_shape=jax.ShapeDtypeStruct((heads, token...]
    pallas_call x2, Pallas kernels: 11.1 us -> 12.2 us  [the longest x1 6.7 us: shards(): pl.pallas_call(functools.partial(project_kernel, tuple(range(1, tps)), tp...]
    pallas_call x3 -> x2, Pallas kernels: 4.98 us -> 4.31 us  [pick(): pl.pallas_call(functools.partial(pick_kernel, 4, targets), in_specs=[pl.B...]
  transfers between devices with their start and end apart: 25 -> 16, of which waited for: 8 -> 6; matrix products, arithmetic and copies ran while one was open for 0% -> 2% of each run, Pallas kernels for 20% -> 15%
where the time goes in v4:
time: 76.8 us; the launch traced here: 76.3 us
  starting transfers between devices  29.9 us (39%)
  Pallas kernels  24.4 us (32%)
  waiting for transfers between devices  17 us (22%)
  local copies, waits for them, and re-layouts  3.72 us (5%)
  other arithmetic  1.06 us (1%)
    ppermute x3, starting transfers between devices, inward(): return lax.ppermute(x, 'mem', [(0, 1), (3, 2)])  14.1 us
    ppermute x3, waiting for transfers between devices, inward(): return lax.ppermute(x, 'mem', [(0, 1), (3, 2)])  10 us
    pallas_call x1, Pallas kernels, shards(): pl.pallas_call(functools.partial(project_kernel, tuple(range(1, tps)), tp...  6.7 us
    pallas_call x1, Pallas kernels, shards(): pl.pallas_call(functools.partial(finish_kernel, tps), grid=(2 * per,), in...  6.23 us
    ppermute x3, starting transfers between devices, line_sum(): lax.ppermute(stored, 'mem', [(i, i ^ x) for i in range(4)])  5.76 us
    pallas_call x1, Pallas kernels, shards(): pl.pallas_call(functools.partial(project_kernel, (0,), tps), in_specs=[sm...  5.47 us
    pallas_call x2, Pallas kernels, pick(): pl.pallas_call(functools.partial(pick_kernel, 4, targets), in_specs=[pl.B...  4.31 us
    unnamed x12, local copies, waits for them, and re-layouts  3.63 us
  transfers between devices with their start and end apart: 16, of which 6 were waited for; matrix products, arithmetic and copies ran while one was open for 2% of the time, Pallas kernels for 15%

profile of v4, /device:TPU:0, one launch (start us, length us, event | category | flops | bytes accessed | tf_op | source)
XLA Modules:
  0.0 76.3 jit_solution(17711715549826702623)
XLA Ops:
  0.0 0.5 collective-permute-start.11
  0.5 0.1 collective-permute-start.12
  0.5 0.7 copy-done.4
  1.2 0.7 copy-done.5
  1.9 0.6 place_rows.1.refs_0_
  2.5 5.1 %collective-permute-start.2 = (s32[8,256]{1,0:T(8,128)S(1)}, s32[8,256]{1,0:T(8,128)S(1)}, u32[]{:S(2)}, u32[]{:S(2)}) collective-permute-start(s32[8,256]{1,0:T(8,128)S(1)} %place_rows.1.refs_0_), channel_id=1, source_target_pairs={{0,12},{4,8},{8,4},{12,0},{1,13},{5,9},{9,5},{13,1},{2,14},{6,10},... | collective-permute-start | bytes 24584 | tf_op jit(solution)/shard_map/ppermute | solution.py:270
  7.6 0.0 collective-permute-start.1
  7.6 0.6 collective-permute-start
  8.3 1.3 %copy-done.1 = bf16[8,1024,80]{1,2,0:T(8,128)(2,1)S(1)} copy-done((bf16[8,1024,80]{1,2,0:T(8,128)(2,1)S(1)}, bf16[8,1024,80]{1,2,0:T(8,128)(2,1)}, u32[]{:S(2)}) %copy-start.1) | copy-done | bytes 1310744
  9.6 0.9 %copy-done.2 = bf16[8,1024,5]{1,0,2:T(8,128)(2,1)S(1)} copy-done((bf16[8,1024,5]{1,0,2:T(8,128)(2,1)S(1)}, bf16[8,1024,5]{1,0,2:T(8,128)(2,1)}, u32[]{:S(2)}) %copy-start.2) | copy-done | bytes 81944
  10.5 0.9 %decode_tables.1.refs_4_ = bf16[8,80,1024]{2,1,0:T(8,128)(2,1)S(1)} custom-call(bf16[8,80,1024]{2,1,0:T(8,128)(2,1)S(1)} %bitcast.13, bf16[5,8,1024]{2,1,0:T(8,128)(2,1)S(1)} %bitcast.14), custom_call_target="tpu_custom_call" | custom-call | tf_op jit(solution)/shard_map/decode_tables/pallas_call | solution.py:343
  11.3 0.1 stack.35.scalars_ref
  11.4 0.0 collective-permute-done.2.refs_3_
  11.4 0.7 collective-permute-done.1.refs_2_
  12.2 0.0 collective-permute-done.refs_1_
  12.2 1.4 %pick_rows.3 = bf16[640,256]{1,0:T(8,128)(2,1)S(1)} custom-call(s32[5]{0:T(128)S(1)} %stack.35.scalars_ref, s32[8,256]{1,0:T(8,128)S(1)} %place_rows.1.refs_0_, s32[8,256]{1,0:T(8,128)S(1)} %collective-permute-done.refs_1_, s32[8,256]{1,0:T(8,128)S(1)} %collective-permute-done.1.refs_2_, s32[8,256]{1,0:T(8,128)S(1)} %collective-permute-done.2.refs_3_, ...), custom_call_target="tpu_custom_call" | custom-call | tf_op jit(solution)/shard_map/pick_rows/pallas_call | solution.py:278
  13.6 2.6 %collective-permute-start.3 = (bf16[640,256]{1,0:T(8,128)(2,1)S(1)}, bf16[640,256]{1,0:T(8,128)(2,1)S(1)}, u32[]{:S(2)}, u32[]{:S(2)}) collective-permute-start(bf16[640,256]{1,0:T(8,128)(2,1)S(1)} %pick_rows.3), channel_id=1, source_target_pairs={{0,4},{12,8},{1,5},{13,9},{2,6},{14,10},{3,7},{15,11},{16,20},{28,... | collective-permute-start | bytes 983048 | tf_op jit(solution)/shard_map/ppermute | solution.py:292
  16.2 2.9 %pick_rows.2 = (bf16[640,256]{1,0:T(8,128)(2,1)S(1)}, bf16[640,256]{1,0:T(8,128)(2,1)S(1)}, bf16[640,256]{1,0:T(8,128)(2,1)S(1)}) custom-call(s32[5]{0:T(128)S(1)} %stack.35.scalars_ref, s32[8,256]{1,0:T(8,128)S(1)} %place_rows.1.refs_0_, s32[8,256]{1,0:T(8,128)S(1)} %collective-permute-done.refs_1_, s32[8,256]{1,0:T(8,128)S(1)} %collective-permute-done.1.refs_2_, ...), custom_call_target="tpu_custom_call" | custom-call | tf_op jit(solution)/shard_map/pick_rows/pallas_call | solution.py:278
  19.1 0.0 copy-start
  19.1 3.6 %collective-permute-done.3 = bf16[640,256]{1,0:T(8,128)(2,1)S(1)} collective-permute-done((bf16[640,256]{1,0:T(8,128)(2,1)S(1)}, bf16[640,256]{1,0:T(8,128)(2,1)S(1)}, u32[]{:S(2)}, u32[]{:S(2)}) %collective-permute-start.3) | collective-permute-done | bytes 327712 | tf_op jit(solution)/shard_map/ppermute | solution.py:292
  22.7 0.1 add.18
  22.8 4.4 %collective-permute-start.4 = (bf16[640,256]{1,0:T(8,128)(2,1)S(1)}, bf16[640,256]{1,0:T(8,128)(2,1)S(1)}, u32[]{:S(2)}, u32[]{:S(2)}) collective-permute-start(bf16[640,256]{1,0:T(8,128)(2,1)S(1)} %get-tuple-element.22), channel_id=1, source_target_pairs={{0,4},{12,8},{1,5},{13,9},{2,6},{14,10},{3,7},{15,11},{16,20},{28,... | collective-permute-start | bytes 983048 | tf_op jit(solution)/shard_map/ppermute | solution.py:292
  27.2 0.7 collective-permute-start.5
  27.9 4.9 %collective-permute-done.4 = bf16[640,256]{1,0:T(8,128)(2,1)S(1)} collective-permute-done((bf16[640,256]{1,0:T(8,128)(2,1)S(1)}, bf16[640,256]{1,0:T(8,128)(2,1)S(1)}, u32[]{:S(2)}, u32[]{:S(2)}) %collective-permute-start.4) | collective-permute-done | bytes 327712 | tf_op jit(solution)/shard_map/ppermute | solution.py:292
  32.8 0.8 %add.19 = bf16[640,256]{1,0:T(8,128)(2,1)} add(bf16[640,256]{1,0:T(8,128)(2,1)S(1)} %get-tuple-element.22, bf16[640,256]{1,0:T(8,128)(2,1)S(1)} %collective-permute-done.4) | non-fusion elementwise | flops 163840 | bytes 983040 | tf_op jit(solution)/shard_map/add | solution.py:306
  33.6 0.0 collective-permute-done.5
  33.6 0.1 add.20
  33.7 0.7 collective-permute-start.7
  34.4 1.3 %collective-permute-start.8 = (bf16[640,256]{1,0:T(8,128)(2,1)S(1)}, bf16[640,256]{1,0:T(8,128)(2,1)S(1)}, u32[]{:S(2)}, u32[]{:S(2)}) collective-permute-start(bf16[640,256]{1,0:T(8,128)(2,1)S(1)} %add.20), channel_id=1, source_target_pairs={{4,0},{8,12},{5,1},{9,13},{6,2},{10,14},{7,3},{11,15},{20,16},{24,... | collective-permute-start | bytes 983048 | tf_op jit(solution)/shard_map/ppermute | solution.py:298
  35.7 7.1 %collective-permute-start.6 = (bf16[640,256]{1,0:T(8,128)(2,1)S(1)}, bf16[640,256]{1,0:T(8,128)(2,1)S(1)}, u32[]{:S(2)}, u32[]{:S(2)}) collective-permute-start(bf16[640,256]{1,0:T(8,128)(2,1)S(1)} %get-tuple-element.25.inner_ref), channel_id=1, source_target_pairs={{0,4},{12,8},{1,5},{13,9},{2,6},{14,10},{3,7},{15,11},{16,20},{28,... | collective-permute-start | bytes 983048 | tf_op jit(solution)/shard_map/ppermute | solution.py:292
  42.9 0.0 collective-permute-done.7.refs_1_
  42.9 3.1 %collective-permute-done.8.refs_2_ = bf16[640,256]{1,0:T(8,128)(2,1)S(1)} collective-permute-done((bf16[640,256]{1,0:T(8,128)(2,1)S(1)}, bf16[640,256]{1,0:T(8,128)(2,1)S(1)}, u32[]{:S(2)}, u32[]{:S(2)}) %collective-permute-start.8) | collective-permute-done | bytes 327712 | tf_op jit(solution)/shard_map/ppermute | solution.py:298
  45.9 1.5 %collective-permute-done.6.refs_0_ = bf16[640,256]{1,0:T(8,128)(2,1)S(1)} collective-permute-done((bf16[640,256]{1,0:T(8,128)(2,1)S(1)}, bf16[640,256]{1,0:T(8,128)(2,1)S(1)}, u32[]{:S(2)}, u32[]{:S(2)}) %collective-permute-start.6) | collective-permute-done | bytes 327712 | tf_op jit(solution)/shard_map/ppermute | solution.py:292
  47.4 0.2 merge.1
  47.6 1.6 %collective-permute-start.10 = (bf16[640,256]{1,0:T(8,128)(2,1)S(1)}, bf16[640,256]{1,0:T(8,128)(2,1)S(1)}, u32[]{:S(2)}, u32[]{:S(2)}) collective-permute-start(bf16[640,256]{1,0:T(8,128)(2,1)S(1)} %get-tuple-element.29.refs_1_), channel_id=1, source_target_pairs={{0,2},{2,0},{1,3},{3,1},{4,6},{6,4},{5,7},{7,5},{8,10},{10,8},{9,1... | collective-permute-start | bytes 983048 | tf_op jit(solution)/shard_map/ppermute | solution.py:365
  49.2 1.3 %collective-permute-start.13 = (bf16[640,128]{1,0:T(8,128)(2,1)S(1)}, bf16[640,128]{1,0:T(8,128)(2,1)S(1)}, u32[]{:S(2)}, u32[]{:S(2)}) collective-permute-start(bf16[640,128]{1,0:T(8,128)(2,1)S(1)} %get-tuple-element.28), channel_id=1, source_target_pairs={{0,1},{2,3},{4,5},{6,7},{8,9},{10,11},{12,13},{14,15},{16,17},{18,... | collective-permute-start | bytes 491528 | tf_op jit(solution)/shard_map/ppermute | solution.py:369
  50.5 1.3 %collective-permute-start.9 = (bf16[640,128]{1,0:T(8,128)(2,1)S(1)}, bf16[640,128]{1,0:T(8,128)(2,1)S(1)}, u32[]{:S(2)}, u32[]{:S(2)}) collective-permute-start(bf16[640,128]{1,0:T(8,128)(2,1)S(1)} %get-tuple-element.28), channel_id=1, source_target_pairs={{0,3},{2,1},{4,7},{6,5},{8,11},{10,9},{12,15},{14,13},{16,19},{18,... | collective-permute-start | bytes 491528 | tf_op jit(solution)/shard_map/ppermute | solution.py:369
  51.8 2.1 %collective-permute-start.14 = (bf16[16,2304]{1,0:T(8,128)(2,1)S(1)}, bf16[16,2304]{1,0:T(8,128)(2,1)S(1)}, u32[]{:S(2)}, u32[]{:S(2)}) collective-permute-start(bf16[16,2304]{1,0:T(8,128)(2,1)S(1)} %slice.3), channel_id=1, source_target_pairs={{0,1},{4,5},{8,9},{12,13},{2,3},{6,7},{10,11},{14,15},{16,17},{20,... | collective-permute-start | bytes 221192 | tf_op jit(solution)/shard_map/ppermute | solution.py:357
  53.9 0.1 pad_add_fusion.where_ref
  54.0 0.0 collective-permute-done.12.refs_5_
  54.0 5.5 %project_own.1 = (f32[2,272,1152]{2,1,0:T(8,128)S(1)}, f32[2,272,1152]{2,1,0:T(8,128)S(1)}) custom-call(s32[2]{0:T(128)S(1)} %pad_add_fusion.where_ref, bf16[640,128]{1,0:T(8,128)(2,1)S(1)} %collective-permute-done.13.refs_0_, bf16[640,256]{1,0:T(8,128)(2,1)S(1)} %get-tuple-element.29.refs_1_, bf16[1280,1152]{1,0:T(8,128)(2,1)} %refs_2_.3, ...), custom_call_target="tpu_custom_call" | custom-call | tf_op jit(solution)/shard_map/project_own/pallas_call | solution.py:386
  59.5 0.0 collective-permute-done.14.refs_8_
  59.5 0.0 collective-permute-done.9.refs_0_
  59.5 0.0 copy-start.3
  59.6 6.7 %project_others.1 = (f32[2,272,1152]{2,1,0:T(8,128)}, f32[8,272]{1,0:T(8,128)S(1)}) custom-call(s32[2]{0:T(128)S(1)} %pad_add_fusion.where_ref, bf16[640,128]{1,0:T(8,128)(2,1)S(1)} %collective-permute-done.9.refs_0_, bf16[640,256]{1,0:T(8,128)(2,1)S(1)} %collective-permute-done.10.refs_1_, bf16[1280,1152]{1,0:T(8,128)(2,1)} %refs_2_.3, ...), custom_call_target="tpu_custom_call" | custom-call | tf_op jit(solution)/shard_map/project_others/pallas_call | solution.py:395
  66.3 0.6 collective-permute-start.15
  66.9 3.2 %collective-permute-done.15.refs_1_ = f32[8,272]{1,0:T(8,128)S(1)} collective-permute-done((f32[8,272]{1,0:T(8,128)S(1)}, f32[8,272]{1,0:T(8,128)S(1)}, u32[]{:S(2)}, u32[]{:S(2)}) %collective-permute-start.15) | collective-permute-done | bytes 8736 | tf_op jit(solution)/shard_map/ppermute | solution.py:412
  70.0 6.2 %finish.1 = bf16[256,2304]{1,0:T(8,128)(2,1)} custom-call(s32[1]{0:T(128)} %bitcast.keep_ref, f32[8,272]{1,0:T(8,128)S(1)} %get-tuple-element.33.refs_0_, f32[8,272]{1,0:T(8,128)S(1)} %collective-permute-done.15.refs_1_, f32[2,272,1152]{2,1,0:T(8,128)} %get-tuple-element.34.refs_2_, bf16[256,2304]{1,0:T(8,128)(2,1)S(1)} %copy-done, f32[4,2304]{1,0:T(4,128)S(1)} %copy-done.3), custom_call_target="tpu_custom_call" | custom-call | tf_op jit(solution)/shard_map/finish/pallas_call | solution.py:427
  (10 shorter events, 0.0 us)
Async XLA Ops:
  0.0 54.0 %collective-permute-start.11 = (bf16[1280,1152]{1,0:T(8,128)(2,1)}, bf16[1280,1152]{1,0:T(8,128)(2,1)}, u32[]{:S(2)}, u32[]{:S(2)}) collective-permute-start(bf16[1280,1152]{1,0:T(8,128)(2,1)} %refs_2_.3), channel_id=1, source_target_pairs={{0,1},{1,0},{2,3},{3,2},{4,5},{5,4},{6,7},{7,6},{8,9},{9,8},{10,11... | collective-permute-start | bytes 8847368 | tf_op jit(solution)/shard_map/ppermute | solution.py:358
  0.5 53.6 %collective-permute-start.12 = (bf16[1280,1152]{1,0:T(8,128)(2,1)}, bf16[1280,1152]{1,0:T(8,128)(2,1)}, u32[]{:S(2)}, u32[]{:S(2)}) collective-permute-start(bf16[1280,1152]{1,0:T(8,128)(2,1)} %refs_3_.4), channel_id=1, source_target_pairs={{0,1},{1,0},{2,3},{3,2},{4,5},{5,4},{6,7},{7,6},{8,9},{9,8},{10,11... | collective-permute-start | bytes 8847368 | tf_op jit(solution)/shard_map/ppermute | solution.py:359
  0.5 0.7 copy-start.4
  1.2 0.7 copy-start.5
  2.5 8.9 %collective-permute-start.2 = (s32[8,256]{1,0:T(8,128)S(1)}, s32[8,256]{1,0:T(8,128)S(1)}, u32[]{:S(2)}, u32[]{:S(2)}) collective-permute-start(s32[8,256]{1,0:T(8,128)S(1)} %place_rows.1.refs_0_), channel_id=1, source_target_pairs={{0,12},{4,8},{8,4},{12,0},{1,13},{5,9},{9,5},{13,1},{2,14},{6,10},... | collective-permute-start | bytes 24584 | tf_op jit(solution)/shard_map/ppermute | solution.py:270
  7.6 4.5 %collective-permute-start.1 = (s32[8,256]{1,0:T(8,128)S(1)}, s32[8,256]{1,0:T(8,128)S(1)}, u32[]{:S(2)}, u32[]{:S(2)}) collective-permute-start(s32[8,256]{1,0:T(8,128)S(1)} %place_rows.1.refs_0_), channel_id=1, source_target_pairs={{0,8},{4,12},{8,0},{12,4},{1,9},{5,13},{9,1},{13,5},{2,10},{6,14},... | collective-permute-start | bytes 24584 | tf_op jit(solution)/shard_map/ppermute | solution.py:270
  7.6 4.5 %collective-permute-start = (s32[8,256]{1,0:T(8,128)S(1)}, s32[8,256]{1,0:T(8,128)S(1)}, u32[]{:S(2)}, u32[]{:S(2)}) collective-permute-start(s32[8,256]{1,0:T(8,128)S(1)} %place_rows.1.refs_0_), channel_id=1, source_target_pairs={{0,4},{4,0},{8,12},{12,8},{1,5},{5,1},{9,13},{13,9},{2,6},{6,2},{1... | collective-permute-start | bytes 24584 | tf_op jit(solution)/shard_map/ppermute | solution.py:270
  8.3 1.3 %copy-start.1 = (bf16[8,1024,80]{1,2,0:T(8,128)(2,1)S(1)}, bf16[8,1024,80]{1,2,0:T(8,128)(2,1)}, u32[]{:S(2)}) copy-start(bf16[8,1024,80]{1,2,0:T(8,128)(2,1)} %param.11) | copy-start | bytes 3932164
  9.6 0.9 %copy-start.2 = (bf16[8,1024,5]{1,0,2:T(8,128)(2,1)S(1)}, bf16[8,1024,5]{1,0,2:T(8,128)(2,1)}, u32[]{:S(2)}) copy-start(bf16[8,1024,5]{1,0,2:T(8,128)(2,1)} %param.12) | copy-start | bytes 245764
  13.6 9.1 %collective-permute-start.3 = (bf16[640,256]{1,0:T(8,128)(2,1)S(1)}, bf16[640,256]{1,0:T(8,128)(2,1)S(1)}, u32[]{:S(2)}, u32[]{:S(2)}) collective-permute-start(bf16[640,256]{1,0:T(8,128)(2,1)S(1)} %pick_rows.3), channel_id=1, source_target_pairs={{0,4},{12,8},{1,5},{13,9},{2,6},{14,10},{3,7},{15,11},{16,20},{28,... | collective-permute-start | bytes 983048 | tf_op jit(solution)/shard_map/ppermute | solution.py:292
  19.1 32.7 %copy-start = (bf16[256,2304]{1,0:T(8,128)(2,1)S(1)}, bf16[256,2304]{1,0:T(8,128)(2,1)}, u32[]{:S(2)}) copy-start(bf16[256,2304]{1,0:T(8,128)(2,1)} %refs_3_.5) | copy-start | bytes 3538948
  22.8 10.0 %collective-permute-start.4 = (bf16[640,256]{1,0:T(8,128)(2,1)S(1)}, bf16[640,256]{1,0:T(8,128)(2,1)S(1)}, u32[]{:S(2)}, u32[]{:S(2)}) collective-permute-start(bf16[640,256]{1,0:T(8,128)(2,1)S(1)} %get-tuple-element.22), channel_id=1, source_target_pairs={{0,4},{12,8},{1,5},{13,9},{2,6},{14,10},{3,7},{15,11},{16,20},{28,... | collective-permute-start | bytes 983048 | tf_op jit(solution)/shard_map/ppermute | solution.py:292
  27.2 6.4 %collective-permute-start.5 = (bf16[640,256]{1,0:T(8,128)(2,1)S(1)}, bf16[640,256]{1,0:T(8,128)(2,1)S(1)}, u32[]{:S(2)}, u32[]{:S(2)}) collective-permute-start(bf16[640,256]{1,0:T(8,128)(2,1)S(1)} %add.18), channel_id=1, source_target_pairs={{4,8},{8,4},{5,9},{9,5},{6,10},{10,6},{7,11},{11,7},{20,24},{24,20... | collective-permute-start | bytes 983048 | tf_op jit(solution)/shard_map/ppermute | solution.py:295
  33.7 9.1 %collective-permute-start.7 = (bf16[640,256]{1,0:T(8,128)(2,1)}, bf16[640,256]{1,0:T(8,128)(2,1)S(1)}, u32[]{:S(2)}, u32[]{:S(2)}) collective-permute-start(bf16[640,256]{1,0:T(8,128)(2,1)} %add.19), channel_id=1, source_target_pairs={{4,8},{8,4},{5,9},{9,5},{6,10},{10,6},{7,11},{11,7},{20,24},{24,20... | collective-permute-start | bytes 983048 | tf_op jit(solution)/shard_map/ppermute | solution.py:295
  34.4 11.5 %collective-permute-start.8 = (bf16[640,256]{1,0:T(8,128)(2,1)S(1)}, bf16[640,256]{1,0:T(8,128)(2,1)S(1)}, u32[]{:S(2)}, u32[]{:S(2)}) collective-permute-start(bf16[640,256]{1,0:T(8,128)(2,1)S(1)} %add.20), channel_id=1, source_target_pairs={{4,0},{8,12},{5,1},{9,13},{6,2},{10,14},{7,3},{11,15},{20,16},{24,... | collective-permute-start | bytes 983048 | tf_op jit(solution)/shard_map/ppermute | solution.py:298
  35.7 11.7 %collective-permute-start.6 = (bf16[640,256]{1,0:T(8,128)(2,1)S(1)}, bf16[640,256]{1,0:T(8,128)(2,1)S(1)}, u32[]{:S(2)}, u32[]{:S(2)}) collective-permute-start(bf16[640,256]{1,0:T(8,128)(2,1)S(1)} %get-tuple-element.25.inner_ref), channel_id=1, source_target_pairs={{0,4},{12,8},{1,5},{13,9},{2,6},{14,10},{3,7},{15,11},{16,20},{28,... | collective-permute-start | bytes 983048 | tf_op jit(solution)/shard_map/ppermute | solution.py:292
  47.6 11.9 %collective-permute-start.10 = (bf16[640,256]{1,0:T(8,128)(2,1)S(1)}, bf16[640,256]{1,0:T(8,128)(2,1)S(1)}, u32[]{:S(2)}, u32[]{:S(2)}) collective-permute-start(bf16[640,256]{1,0:T(8,128)(2,1)S(1)} %get-tuple-element.29.refs_1_), channel_id=1, source_target_pairs={{0,2},{2,0},{1,3},{3,1},{4,6},{6,4},{5,7},{7,5},{8,10},{10,8},{9,1... | collective-permute-start | bytes 983048 | tf_op jit(solution)/shard_map/ppermute | solution.py:365
  49.2 2.6 %collective-permute-start.13 = (bf16[640,128]{1,0:T(8,128)(2,1)S(1)}, bf16[640,128]{1,0:T(8,128)(2,1)S(1)}, u32[]{:S(2)}, u32[]{:S(2)}) collective-permute-start(bf16[640,128]{1,0:T(8,128)(2,1)S(1)} %get-tuple-element.28), channel_id=1, source_target_pairs={{0,1},{2,3},{4,5},{6,7},{8,9},{10,11},{12,13},{14,15},{16,17},{18,... | collective-permute-start | bytes 491528 | tf_op jit(solution)/shard_map/ppermute | solution.py:369
  50.5 9.0 %collective-permute-start.9 = (bf16[640,128]{1,0:T(8,128)(2,1)S(1)}, bf16[640,128]{1,0:T(8,128)(2,1)S(1)}, u32[]{:S(2)}, u32[]{:S(2)}) collective-permute-start(bf16[640,128]{1,0:T(8,128)(2,1)S(1)} %get-tuple-element.28), channel_id=1, source_target_pairs={{0,3},{2,1},{4,7},{6,5},{8,11},{10,9},{12,15},{14,13},{16,19},{18,... | collective-permute-start | bytes 491528 | tf_op jit(solution)/shard_map/ppermute | solution.py:369
  51.8 7.7 %collective-permute-start.14 = (bf16[16,2304]{1,0:T(8,128)(2,1)S(1)}, bf16[16,2304]{1,0:T(8,128)(2,1)S(1)}, u32[]{:S(2)}, u32[]{:S(2)}) collective-permute-start(bf16[16,2304]{1,0:T(8,128)(2,1)S(1)} %slice.3), channel_id=1, source_target_pairs={{0,1},{4,5},{8,9},{12,13},{2,3},{6,7},{10,11},{14,15},{16,17},{20,... | collective-permute-start | bytes 221192 | tf_op jit(solution)/shard_map/ppermute | solution.py:357
  59.5 10.5 %copy-start.3 = (f32[4,2304]{1,0:T(4,128)S(1)}, f32[4,2304]{1,0:T(4,128)}, u32[]{:S(2)}) copy-start(f32[4,2304]{1,0:T(4,128)} %refs_4_.1) | copy-start | bytes 110596
  66.3 3.8 %collective-permute-start.15 = (f32[8,272]{1,0:T(8,128)S(1)}, f32[8,272]{1,0:T(8,128)S(1)}, u32[]{:S(2)}, u32[]{:S(2)}) collective-permute-start(f32[8,272]{1,0:T(8,128)S(1)} %get-tuple-element.33.refs_0_), channel_id=1, source_target_pairs={{0,2},{2,0},{1,3},{3,1},{4,6},{6,4},{5,7},{7,5},{8,10},{10,8},{9,1... | collective-permute-start | bytes 26120 | tf_op jit(solution)/shard_map/ppermute | solution.py:412

commit v5 on v4

v5 whole, which is shorter than its diff:
```python
import functools

import jax
import jax.numpy as jnp
from jax import lax
from jax.experimental import pallas as pl
from jax.experimental.pallas import tpu as pltpu
from jax.sharding import PartitionSpec as P

D = 4608
KERNEL = 4
DILATION = 3
SEQS = 4
EPSILON = 1e-06
RIM = 16
LANES = 128

F32 = jnp.float32
BF16 = jnp.bfloat16
I32 = jnp.int32


def iota(shape, axis):
    return lax.broadcasted_iota(I32, shape, axis)


def dot(a, b):
    return jnp.dot(a, b, preferred_element_type=F32)


def dot_nt(a, b, precision=None):
    return lax.dot_general(
        a, b, (((1,), (1,)), ((), ())), precision=precision, preferred_element_type=F32
    )


def unit(n, dtype):
    return (iota((n, n), 0) == iota((n, n), 1)).astype(F32).astype(dtype)


def to_bf16(x):
    return x.astype(F32).astype(BF16)


def place_kernel(ids_hbm, place_hbm, out_ref, ids_ref, place_ref, sems):
    copies = [
        pltpu.make_async_copy(place_hbm, place_ref, sems.at[0]),
        pltpu.make_async_copy(ids_hbm, ids_ref, sems.at[1]),
    ]
    for copy in copies:
        copy.start()
    copies[0].wait()
    place = place_ref[...]
    rows = place.shape[0]
    heads, tokens = ids_ref.shape
    eye = unit(LANES, BF16)
    table = jnp.concatenate(
        [dot_nt(eye, to_bf16(place >> 8)), dot_nt(eye, to_bf16(place & 255))], axis=0
    ).astype(BF16)
    copies[1].wait()
    for head in range(heads):
        row = ids_ref[head : head + 1, :]
        hot = to_bf16(iota((rows, tokens), 0) == (row >> 7))
        both = dot(table, hot)
        value = both[:LANES] * 256.0 + both[LANES:]
        chosen = jnp.where(iota(value.shape, 0) == (row & 127), value, 0.0)
        out_ref[head : head + 1, :] = jnp.sum(chosen, axis=0, keepdims=True).astype(I32)


def decode_kernel(codes_hbm, scales_hbm, out_ref, codes_ref, scales_ref, sems):
    heads, width, rows = codes_ref.shape
    blocks = scales_ref.shape[0]
    scales_copy = pltpu.make_async_copy(scales_hbm, scales_ref, sems.at[heads])
    scales_copy.start()
    copies = []
    for head in range(heads):
        copies.append(
            pltpu.make_async_copy(codes_hbm.at[head], codes_ref.at[head], sems.at[head])
        )
        copies[-1].start()
    entry = iota((width, 2 * width), 0)
    column = iota((width, 2 * width), 1)
    column = jnp.where(column < width, column, column - width)
    parity = entry & column & 15
    parity = parity ^ (parity >> 2)
    parity = (parity ^ (parity >> 1)) & 1
    same = (entry >> 4) == (column >> 4)
    rotation = jnp.where(same, 0.25 - 0.5 * parity.astype(F32), 0.0).astype(BF16)
    scales_copy.wait()
    for head in range(heads):
        copies[head].wait()
        factors = jnp.concatenate(
            [
                jnp.broadcast_to(scales_ref[b, head : head + 1, :].astype(F32), (16, rows))
                for b in range(blocks)
            ],
            axis=0,
        )
        scaled = codes_ref[head].astype(F32) * factors
        upper = scaled.astype(BF16)
        lower = (scaled - upper.astype(F32)).astype(BF16)
        out_ref[head] = dot(rotation, jnp.concatenate([upper, lower], axis=0)).astype(BF16)


def picked(local, table_ref, head):
    rows = table_ref.shape[2]
    hot = to_bf16(iota((rows, local.shape[1]), 0) == local[head : head + 1, :])
    return dot(table_ref[head], hot).astype(BF16)


def pick_all_kernel(base_ref, ids_ref, table_ref, out_ref):
    heads, width, _ = table_ref.shape
    local = ids_ref[...] - base_ref[0]
    for head in range(heads):
        out_ref[head * width : (head + 1) * width, :] = picked(local, table_ref, head)


def pick_kernel(count, targets, scalars_ref, *refs):
    pieces = refs[:count]
    table_ref = refs[count]
    outs = refs[count + 1 : -1]
    stack = refs[-1]
    heads, width, _ = table_ref.shape
    for k in range(count):
        stack[k] = pieces[k][...]
    for n, target in enumerate(targets):
        local = stack[scalars_ref[1 + target]] - scalars_ref[0]
        for head in range(heads):
            outs[n][head * width : (head + 1) * width, :] = picked(local, table_ref, head)


def merge_kernel(middle_ref, inner_ref, outer_ref, *refs):
    received = refs[:-2]
    out_ref, rim_ref = refs[-2:]
    total = jnp.where(middle_ref[0] == 1, inner_ref[...].astype(F32), outer_ref[...].astype(F32))
    for other in received:
        total = total + other[...].astype(F32)
    total = total.astype(BF16)
    out_ref[...] = total
    rim_ref[...] = total[:, total.shape[1] - LANES :]


def load_kernel(*refs):
    sources, targets, sems = refs[:2], refs[2:4], refs[4]
    rows = sources[0].shape[0]
    pieces = sems.shape[0] // 2
    step = rows // pieces
    copies = []
    for n in range(pieces):
        for which in range(2):
            span = pl.ds(n * step, step)
            copy = pltpu.make_async_copy(
                sources[which].at[span, :], targets[which].at[span, :], sems.at[2 * n + which]
            )
            copy.start()
            copies.append(copy)
    for copy in copies:
        copy.wait()


def project_kernel(shifts, count, where_ref, *refs):
    pieces = len(shifts)
    first = 0 in shifts
    rims = refs[:pieces]
    bodies = refs[pieces : 2 * pieces]
    refs = refs[2 * pieces :]
    weights = refs[:4]
    if first:
        key_ref, value_ref = refs[4:]
    else:
        begun_keys, begun_values, hidden_halo, hidden, value_ref, stats_ref, states = refs[4:]
    half = value_ref.shape[-1]
    depth, tokens = bodies[0].shape
    rep = where_ref[0]
    tp = where_ref[1]
    body = jnp.concatenate([b[...].astype(F32) for b in bodies], axis=0).T.astype(BF16)
    rim = jnp.concatenate([r[...].astype(F32) for r in rims], axis=0).T.astype(BF16)
    memory = jnp.concatenate([rim[LANES - RIM :], body], axis=0)
    if not first:
        for slot in range(2):
            states[slot, :RIM] = hidden_halo[:, slot * half : (slot + 1) * half]
            states[slot, RIM:] = hidden[:, slot * half : (slot + 1) * half]
    sums = [0.0] * 4
    for far in range(2):
        slot = rep if far == 0 else 1 - rep
        fields = []
        for which in range(2):
            field = None
            for n, s in enumerate(shifts):
                at = pl.multiple_of(lax.rem(tp + count - s, count) * depth, depth)
                part = dot(
                    memory[:, n * depth : (n + 1) * depth],
                    weights[2 * far + which][pl.ds(at, depth), :],
                )
                field = part if field is None else field + part
            fields.append(field)
        keys, values = fields
        if first:
            key_ref[slot] = keys
            value_ref[slot] = values
        else:
            keys = keys + begun_keys[slot]
            values = values + begun_values[slot]
            value_ref[slot] = values
            here = states[slot].astype(F32)
            terms = (here * here, keys * keys, here * keys, values * values)
            sums = [a + jnp.sum(t, axis=1, keepdims=True) for a, t in zip(sums, terms)]
    if not first:
        rows = memory.shape[0]
        lane = iota((rows, 8), 1)
        packed = jnp.zeros((rows, 8), F32)
        for k in range(4):
            packed = jnp.where(lane == k, sums[k], packed)
        stats_ref[...] = dot_nt(unit(8, F32), packed, lax.Precision.HIGHEST)


def finish_kernel(count, step, keep_ref, *refs):
    stats = refs[:count]
    value_ref, hidden_ref, taps_ref, out_hbm, gates, factors, normed, out_ref, sems = refs[count:]
    rows, half = normed.shape
    tokens, width = out_ref.shape
    total = stats[0][...]
    for other in stats[1:]:
        total = total + other[...]
    inverse_states = lax.rsqrt(total[0:1] / D + EPSILON)
    inverse_keys = lax.rsqrt(total[1:2] / D + EPSILON)
    gate = jax.nn.sigmoid(total[2:3] * inverse_states * inverse_keys / D**0.5)
    factor = gate * lax.rsqrt(gate * gate * total[3:4] / D + EPSILON)
    factor = jnp.where((iota(factor.shape, 1) < RIM) & (keep_ref[0] == 0), 0.0, factor)
    line = iota(total.shape, 0)
    both = jnp.where(line == 0, gate, jnp.where(line == 1, factor, 0.0))
    columns = dot_nt(unit(rows, F32), both, lax.Precision.HIGHEST)
    gates[...] = jnp.broadcast_to(columns[RIM:, 0:1], gates.shape)
    factors[...] = jnp.broadcast_to(columns[:, 1:2], factors.shape)
    copies = []
    for slot in range(2):
        for start in range(0, half, LANES):
            size = min(LANES, half - start)
            span = slice(start, start + size)
            there = slice(slot * half + start, slot * half + start + size)
            values = value_ref[slot, :, span]
            normed[:, span] = values * factors[:, :size]
            conv = None
            for tap in range(KERNEL):
                lag = DILATION * tap
                term = taps_ref[tap : tap + 1, there] * normed[RIM - lag : RIM - lag + tokens, span]
                conv = term if conv is None else conv + term
            gated = values[RIM:] * gates[:, :size]
            out_ref[:, there] = (
                hidden_ref[:, there].astype(F32) + jax.nn.silu(conv) + gated
            ).astype(BF16)
            if there.stop % step == 0:
                ready = pl.ds(there.stop - step, step)
                copy = pltpu.make_async_copy(
                    out_ref.at[:, ready], out_hbm.at[:, ready], sems.at[len(copies)]
                )
                copy.start()
                copies.append(copy)
    for copy in copies:
        copy.wait()


def whole(array):
    return pl.BlockSpec(array.shape, lambda *_: (0,) * array.ndim)


def in_hbm(array):
    return pltpu.with_memory_space_constraint(array, pltpu.HBM)


def in_vmem(array):
    return pltpu.with_memory_space_constraint(array, pltpu.VMEM)


def after(array, *others):
    return lax.optimization_barrier((array, *others))[0]


def load(pair):
    target = pltpu.VMEM(pair[0].shape, pair[0].dtype)
    return pl.pallas_call(
        load_kernel,
        in_specs=[pl.BlockSpec(memory_space=pl.ANY)] * 2,
        out_specs=(pl.BlockSpec(memory_space=pltpu.VMEM),) * 2,
        out_shape=(target, target),
        scratch_shapes=[pltpu.SemaphoreType.DMA((8,))],
        compiler_params=limit(4),
        name="load_weights",
    )(*pair)


def limit(mib):
    return pltpu.CompilerParams(vmem_limit_bytes=mib << 20)


def scattered_sum(stored, decoded, here, early, late):
    mems = lax.axis_size("mem")
    heads, width, rows = decoded.shape
    tokens = stored.shape[1]
    asked = lax.all_gather(stored, "mem", axis=0)
    partial = pl.pallas_call(
        pick_all_kernel,
        grid=(mems,),
        in_specs=[
            pl.BlockSpec(memory_space=pltpu.SMEM),
            pl.BlockSpec((None, heads, tokens), lambda m: (m, 0, 0)),
            whole(decoded),
        ],
        out_specs=pl.BlockSpec((None, heads * width, tokens), lambda m: (m, 0, 0)),
        out_shape=jax.ShapeDtypeStruct((mems, heads * width, tokens), BF16),
        compiler_params=limit(16),
        name="pick_all",
    )((here * rows).astype(I32).reshape(1), asked, decoded)
    total = lax.psum_scatter(partial, "mem", scatter_dimension=0, tiled=False)
    return total, total[:, tokens - LANES :], early(partial), late(total)


def line_sum(stored, decoded, here, early, late):
    heads, width, rows = decoded.shape
    tokens = stored.shape[1]
    asked = [stored] + [
        lax.ppermute(stored, "mem", [(i, i ^ x) for i in range(4)]) for x in range(1, 4)
    ]
    right = here >= 2
    order = [here ^ jnp.where(right, j, 3 - j) for j in range(4)]
    scalars = jnp.stack([here * rows] + order).astype(I32)
    block = jax.ShapeDtypeStruct((heads * width, tokens), BF16)

    def pick(*targets):
        return pl.pallas_call(
            functools.partial(pick_kernel, 4, targets),
            in_specs=[pl.BlockSpec(memory_space=pltpu.SMEM)]
            + [pl.BlockSpec(memory_space=pltpu.VMEM)] * 5,
            out_shape=(block,) * len(targets),
            scratch_shapes=[pltpu.VMEM((4, heads, tokens), I32)],
            compiler_params=limit(8),
            name="pick_rows",
        )(scalars, *asked, decoded)

    def inward(x):
        return lax.ppermute(x, "mem", [(0, 1), (3, 2)])

    def across(x):
        return lax.ppermute(x, "mem", [(1, 2), (2, 1)])

    def outward(x):
        return lax.ppermute(x, "mem", [(1, 0), (2, 3)])

    (farthest,) = pick(0)
    first = inward(farthest)
    begun = early(farthest)
    far_own, inner, outer = pick(1, 2, 3)
    far_own, begun = lax.optimization_barrier((far_own, begun))
    second = inward(far_own)
    crossed = across(farthest + first)
    ended = late(first)
    inner, ended = lax.optimization_barrier((inner, ended))
    third = inward(inner)
    crossed_near = across(far_own + after(second, *ended))
    last = outward(outer + crossed)
    middle = ((here == 1) | (here == 2)).astype(I32).reshape(1)
    memory, rim = pl.pallas_call(
        merge_kernel,
        in_specs=[pl.BlockSpec(memory_space=pltpu.SMEM)]
        + [pl.BlockSpec(memory_space=pltpu.VMEM)] * 5,
        out_shape=(block, jax.ShapeDtypeStruct((block.shape[0], LANES), BF16)),
        compiler_params=limit(4),
        name="merge",
    )(middle, inner, outer, third, crossed_near, last)
    return memory, rim, begun, ended


def shards(
    hidden, row_ids, row_place, table_codes, table_scales, key_weight, value_weight, conv_weight
):
    mems = lax.axis_size("mem")
    tps = lax.axis_size("tp")
    reps = lax.axis_size("rep")
    blocks = mems * reps
    tokens, heads = row_ids.shape
    rows, width = table_codes.shape[1:]
    depth = heads * width
    half = key_weight.shape[1]
    seq_length = tokens * blocks // SEQS
    assert reps == 2 and seq_length % tokens == 0 and row_place.shape[0] % LANES == 0
    block = lax.axis_index(("mem", "rep"))
    smem = pl.BlockSpec(memory_space=pltpu.SMEM)

    anywhere = pl.BlockSpec(memory_space=pl.ANY)
    resident = pl.BlockSpec(memory_space=pltpu.VMEM)
    places = row_place.reshape(-1, LANES)
    stored = pl.pallas_call(
        place_kernel,
        in_specs=[anywhere] * 2,
        out_shape=jax.ShapeDtypeStruct((heads, tokens), I32),
        scratch_shapes=[
            pltpu.VMEM((heads, tokens), I32),
            pltpu.VMEM(places.shape, I32),
            pltpu.SemaphoreType.DMA((2,)),
        ],
        compiler_params=limit(4),
        name="place_rows",
    )(in_hbm(row_ids.T), in_hbm(places))
    codes = table_codes.transpose(0, 2, 1)
    scales = table_scales.transpose(2, 0, 1)
    decoded = pl.pallas_call(
        decode_kernel,
        in_specs=[anywhere] * 2,
        out_shape=jax.ShapeDtypeStruct(codes.shape, BF16),
        scratch_shapes=[
            pltpu.VMEM(codes.shape, BF16),
            pltpu.VMEM(scales.shape, BF16),
            pltpu.SemaphoreType.DMA((heads + 1,)),
        ],
        compiler_params=limit(12),
        name="decode_tables",
    )(in_hbm(codes), in_hbm(scales))
    here = lax.axis_index("mem")
    other_key = lax.ppermute(key_weight, "rep", [(0, 1), (1, 0)])
    other_value = lax.ppermute(value_weight, "rep", [(0, 1), (1, 0)])
    needed = [(i, i + 1) for i in range(blocks - 1) if (i + 1) * tokens % seq_length]

    def early(token):
        tail = after(hidden[tokens - RIM :], token)
        halo = lax.ppermute(tail, ("mem", "rep"), needed)
        return halo, load([in_hbm(after(w, token)) for w in (key_weight, value_weight)])

    def late(token):
        return load([after(w, token) for w in (other_key, other_value)])

    summed = line_sum if mems == 4 else scattered_sum
    memory, rim, (hidden_halo, own_weights), other_weights = summed(
        stored, decoded, here, early, late
    )
    weights = [in_vmem(w) for w in (*own_weights, *other_weights)]

    where = jnp.stack([lax.axis_index("rep"), lax.axis_index("tp")]).astype(I32)
    extended = tokens + RIM
    bodies = [memory] + [
        lax.ppermute(memory, "tp", [(i, (i + s) % tps) for i in range(tps)])
        for s in range(1, tps)
    ]

    def next_rim(rim, s):
        pairs = [
            (
                (a // reps * tps + i) * reps + a % reps,
                (b // reps * tps + (i + s) % tps) * reps + b % reps,
            )
            for a, b in needed
            for i in range(tps)
        ]
        return lax.ppermute(rim, ("mem", "tp", "rep"), pairs)

    field = pltpu.VMEM((2, extended, half), F32)
    begun = pl.pallas_call(
        functools.partial(project_kernel, (0,), tps),
        in_specs=[smem] + [resident] * 6,
        out_specs=(resident,) * 2,
        out_shape=(field, field),
        compiler_params=limit(12),
        name="project_own",
    )(where, next_rim(rim, 0), memory, *weights)
    rim = after(rim, *begun)
    others = tps - 1
    values, stats = pl.pallas_call(
        functools.partial(project_kernel, tuple(range(1, tps)), tps),
        in_specs=[smem] + [resident] * (2 * others + 8),
        out_specs=(resident,) * 2,
        out_shape=(field, jax.ShapeDtypeStruct((8, extended), F32)),
        scratch_shapes=[pltpu.VMEM((2, extended, half), BF16)],
        compiler_params=limit(14),
        name="project_others",
    )(
        where,
        *[next_rim(rim, s) for s in range(1, tps)],
        *bodies[1:],
        *weights,
        *[in_vmem(b) for b in begun],
        hidden_halo,
        hidden,
    )

    all_stats = [stats] + [
        lax.ppermute(stats, "tp", [(i, (i + s) % tps) for i in range(tps)]) for s in range(1, tps)
    ]
    keep = (block * tokens % seq_length != 0).astype(I32).reshape(1)
    step = 2 * half
    if half % LANES == 0:
        step = next(c for c in (384, 256, 128) if half % c == 0)
    return pl.pallas_call(
        functools.partial(finish_kernel, tps, step),
        in_specs=[smem] + [resident] * (tps + 3),
        out_specs=anywhere,
        out_shape=jax.ShapeDtypeStruct((tokens, 2 * half), BF16),
        scratch_shapes=[
            pltpu.VMEM((tokens, LANES), F32),
            pltpu.VMEM((extended, LANES), F32),
            pltpu.VMEM((extended, half), F32),
            pltpu.VMEM((tokens, 2 * half), BF16),
            pltpu.SemaphoreType.DMA((2 * half // step,)),
        ],
        compiler_params=limit(12),
        name="finish",
    )(keep, *all_stats, in_vmem(values), hidden, conv_weight)


def solution(mesh):
    in_specs = (
        P(("parts", "mem", "rep"), "tp"),
        P(("parts", "mem", "rep"), "tp"),
        P("parts"),
        P(("parts", "tp"), "mem", None),
        P(("parts", "tp"), "mem", None),
        P(None, ("tp", "rep")),
        P(None, ("tp", "rep")),
        P(None, "tp"),
    )
    out_specs = P(("parts", "mem", "rep"), "tp")
    return jax.shard_map(shards, mesh=mesh, in_specs=in_specs, out_specs=out_specs, check_vma=False)
```

time: 76.8 us -> 93.3 us (1.21)
  the two profiles are of different devices: /device:TPU:0 before, /device:TPU:8 now
where the time goes in v5:
time: 93.3 us; the launch traced here: 92.6 us
  starting transfers between devices  27.4 us (29%)
  Pallas kernels  26.9 us (29%)
  waiting for transfers between devices  20.3 us (22%)
  local copies, waits for them, and re-layouts  15.8 us (17%)
  other arithmetic  1.79 us (2%)
    unnamed x28, local copies, waits for them, and re-layouts  14.8 us
    ppermute x3, waiting for transfers between devices, inward(): return lax.ppermute(x, 'mem', [(0, 1), (3, 2)])  12.1 us
    ppermute x2, starting transfers between devices, across(): return lax.ppermute(x, 'mem', [(1, 2), (2, 1)])  5.83 us
    pallas_call x2, Pallas kernels, load(): pl.pallas_call(load_kernel, in_specs=[pl.BlockSpec(memory_space=pl.ANY)]...  5.58 us
    ppermute x1, starting transfers between devices, outward(): return lax.ppermute(x, 'mem', [(1, 0), (2, 3)])  5.28 us
    ppermute x2, starting transfers between devices, next_rim(): return lax.ppermute(rim, ('mem', 'tp', 'rep'), pairs)  4.42 us
    pallas_call x2, Pallas kernels, pick(): pl.pallas_call(functools.partial(pick_kernel, 4, targets), in_specs=[pl.B...  4.34 us
    ppermute x3, starting transfers between devices, line_sum(): lax.ppermute(stored, 'mem', [(i, i ^ x) for i in range(4)])  4.12 us
  transfers between devices with their start and end apart: 16, of which 5 were waited for; matrix products, arithmetic and copies ran while one was open for 3% of the time, Pallas kernels for 19%

profile of v5, /device:TPU:8, one launch (start us, length us, event | category | flops | bytes accessed | tf_op | source)
XLA Modules:
  0.0 92.6 jit_solution(4367978543560809284)
XLA Ops:
  0.0 0.5 collective-permute-start.5
  0.5 1.3 %place_rows.1.refs_0_ = s32[8,256]{1,0:T(8,128)S(1)} custom-call(s32[8,256]{1,0:T(8,128)} %bitcast.16, s32[32,128]{1,0:T(8,128)} %bitcast.15), custom_call_target="tpu_custom_call" | custom-call | tf_op jit(solution)/shard_map/place_rows/pallas_call | solution.py:392
  1.9 1.6 %collective-permute-start.2 = (s32[8,256]{1,0:T(8,128)S(1)}, s32[8,256]{1,0:T(8,128)S(1)}, u32[]{:S(2)}, u32[]{:S(2)}) collective-permute-start(s32[8,256]{1,0:T(8,128)S(1)} %place_rows.1.refs_0_), channel_id=1, source_target_pairs={{0,12},{4,8},{8,4},{12,0},{1,13},{5,9},{9,5},{13,1},{2,14},{6,10},... | collective-permute-start | bytes 24584 | tf_op jit(solution)/shard_map/ppermute | solution.py:322
  3.5 1.1 %collective-permute-start.1 = (s32[8,256]{1,0:T(8,128)S(1)}, s32[8,256]{1,0:T(8,128)S(1)}, u32[]{:S(2)}, u32[]{:S(2)}) collective-permute-start(s32[8,256]{1,0:T(8,128)S(1)} %place_rows.1.refs_0_), channel_id=1, source_target_pairs={{0,8},{4,12},{8,0},{12,4},{1,9},{5,13},{9,1},{13,5},{2,10},{6,14},... | collective-permute-start | bytes 24584 | tf_op jit(solution)/shard_map/ppermute | solution.py:322
  4.6 1.4 %collective-permute-start = (s32[8,256]{1,0:T(8,128)S(1)}, s32[8,256]{1,0:T(8,128)S(1)}, u32[]{:S(2)}, u32[]{:S(2)}) collective-permute-start(s32[8,256]{1,0:T(8,128)S(1)} %place_rows.1.refs_0_), channel_id=1, source_target_pairs={{0,4},{4,0},{8,12},{12,8},{1,5},{5,1},{9,13},{13,9},{2,6},{6,2},{1... | collective-permute-start | bytes 24584 | tf_op jit(solution)/shard_map/ppermute | solution.py:322
  6.0 2.7 %decode_tables.1.refs_4_ = bf16[8,80,1024]{2,1,0:T(8,128)(2,1)S(1)} custom-call(bf16[8,80,1024]{2,1,0:T(8,128)(2,1)} %bitcast.13, bf16[5,8,1024]{2,1,0:T(8,128)(2,1)} %bitcast.14), custom_call_target="tpu_custom_call" | custom-call | tf_op jit(solution)/shard_map/decode_tables/pallas_call | solution.py:406
  8.7 0.1 stack.35.scalars_ref
  8.8 0.0 collective-permute-done.2.refs_3_
  8.8 0.0 collective-permute-done.1.refs_2_
  8.8 1.4 %pick_rows.3 = bf16[640,256]{1,0:T(8,128)(2,1)S(1)} custom-call(s32[5]{0:T(128)S(1)} %stack.35.scalars_ref, s32[8,256]{1,0:T(8,128)S(1)} %place_rows.1.refs_0_, s32[8,256]{1,0:T(8,128)S(1)} %collective-permute-done.refs_1_, s32[8,256]{1,0:T(8,128)S(1)} %collective-permute-done.1.refs_2_, s32[8,256]{1,0:T(8,128)S(1)} %collective-permute-done.2.refs_3_, ...), custom_call_target="tpu_custom_call" | custom-call | tf_op jit(solution)/shard_map/pick_rows/pallas_call | solution.py:330
  10.3 1.3 %collective-permute-start.4 = (bf16[640,256]{1,0:T(8,128)(2,1)S(1)}, bf16[640,256]{1,0:T(8,128)(2,1)S(1)}, u32[]{:S(2)}, u32[]{:S(2)}) collective-permute-start(bf16[640,256]{1,0:T(8,128)(2,1)S(1)} %pick_rows.3), channel_id=1, source_target_pairs={{0,4},{12,8},{1,5},{13,9},{2,6},{14,10},{3,7},{15,11},{16,20},{28,... | collective-permute-start | bytes 983048 | tf_op jit(solution)/shard_map/ppermute | solution.py:341
  11.6 0.9 slice.3
  12.4 1.3 %collective-permute-start.7 = (bf16[16,2304]{1,0:T(8,128)(2,1)S(1)}, bf16[16,2304]{1,0:T(8,128)(2,1)S(1)}, u32[]{:S(2)}, u32[]{:S(2)}) collective-permute-start(bf16[16,2304]{1,0:T(8,128)(2,1)S(1)} %slice.3), channel_id=1, source_target_pairs={{0,1},{4,5},{8,9},{12,13},{2,3},{6,7},{10,11},{14,15},{16,17},{20,... | collective-permute-start | bytes 221192 | tf_op jit(solution)/shard_map/ppermute | solution.py:425
  13.8 7.4 %collective-permute-done.4 = bf16[640,256]{1,0:T(8,128)(2,1)S(1)} collective-permute-done((bf16[640,256]{1,0:T(8,128)(2,1)S(1)}, bf16[640,256]{1,0:T(8,128)(2,1)S(1)}, u32[]{:S(2)}, u32[]{:S(2)}) %collective-permute-start.4) | collective-permute-done | bytes 327712 | tf_op jit(solution)/shard_map/ppermute | solution.py:341
  21.2 0.1 add.19
  21.3 3.4 %collective-permute-start.10 = (bf16[640,256]{1,0:T(8,128)(2,1)S(1)}, bf16[640,256]{1,0:T(8,128)(2,1)S(1)}, u32[]{:S(2)}, u32[]{:S(2)}) collective-permute-start(bf16[640,256]{1,0:T(8,128)(2,1)S(1)} %add.19), channel_id=1, source_target_pairs={{4,8},{8,4},{5,9},{9,5},{6,10},{10,6},{7,11},{11,7},{20,24},{24,20... | collective-permute-start | bytes 983048 | tf_op jit(solution)/shard_map/ppermute | solution.py:344
  24.7 2.8 %load_weights.3 = (bf16[1280,1152]{1,0:T(8,128)(2,1)S(1)}, bf16[1280,1152]{1,0:T(8,128)(2,1)S(1)}) custom-call(bf16[1280,1152]{1,0:T(8,128)(2,1)} %refs_0_, bf16[1280,1152]{1,0:T(8,128)(2,1)} %refs_1_), custom_call_target="tpu_custom_call" | custom-call | tf_op jit(solution)/shard_map/load_weights/pallas_call | solution.py:281
  27.6 1.6 %copy-done = bf16[1280,1152]{1,0:T(8,128)(2,1)} copy-done((bf16[1280,1152]{1,0:T(8,128)(2,1)}, bf16[1280,1152]{1,0:T(8,128)(2,1)S(1)}, u32[]{:S(2)}) %copy-start) | copy-done | bytes 2949144
  29.1 2.9 %pick_rows.2 = (bf16[640,256]{1,0:T(8,128)(2,1)S(1)}, bf16[640,256]{1,0:T(8,128)(2,1)}, bf16[640,256]{1,0:T(8,128)(2,1)S(1)}) custom-call(s32[5]{0:T(128)S(1)} %stack.35.scalars_ref, s32[8,256]{1,0:T(8,128)S(1)} %place_rows.1.refs_0_, s32[8,256]{1,0:T(8,128)S(1)} %collective-permute-done.refs_1_, s32[8,256]{1,0:T(8,128)S(1)} %collective-permute-done.1.refs_2_, ...), custom_call_target="tpu_custom_call" | custom-call | tf_op jit(solution)/shard_map/pick_rows/pallas_call | solution.py:330
  32.1 1.3 %collective-permute-start.8 = (bf16[640,256]{1,0:T(8,128)(2,1)S(1)}, bf16[640,256]{1,0:T(8,128)(2,1)S(1)}, u32[]{:S(2)}, u32[]{:S(2)}) collective-permute-start(bf16[640,256]{1,0:T(8,128)(2,1)S(1)} %get-tuple-element.45), channel_id=1, source_target_pairs={{0,4},{12,8},{1,5},{13,9},{2,6},{14,10},{3,7},{15,11},{16,20},{28,... | collective-permute-start | bytes 983048 | tf_op jit(solution)/shard_map/ppermute | solution.py:341
  33.4 0.8 add.20
  34.2 5.3 %collective-permute-start.11 = (bf16[640,256]{1,0:T(8,128)(2,1)}, bf16[640,256]{1,0:T(8,128)(2,1)}, u32[]{:S(2)}, u32[]{:S(2)}) collective-permute-start(bf16[640,256]{1,0:T(8,128)(2,1)} %add.20), channel_id=1, source_target_pairs={{4,0},{8,12},{5,1},{9,13},{6,2},{10,14},{7,3},{11,15},{20,16},{24,... | collective-permute-start | bytes 983048 | tf_op jit(solution)/shard_map/ppermute | solution.py:347
  39.5 2.7 %load_weights.2 = (bf16[1280,1152]{1,0:T(8,128)(2,1)S(1)}, bf16[1280,1152]{1,0:T(8,128)(2,1)S(1)}) custom-call(bf16[1280,1152]{1,0:T(8,128)(2,1)} %collective-permute-done.3.refs_0_, bf16[1280,1152]{1,0:T(8,128)(2,1)} %collective-permute-done.5.refs_1_), custom_call_target="tpu_custom_call" | custom-call | tf_op jit(solution)/shard_map/load_weights/pallas_call | solution.py:281
  42.2 1.6 %copy-done.3 = bf16[1280,1152]{1,0:T(8,128)(2,1)} copy-done((bf16[1280,1152]{1,0:T(8,128)(2,1)}, bf16[1280,1152]{1,0:T(8,128)(2,1)S(1)}, u32[]{:S(2)}) %copy-start.3) | copy-done | bytes 2949144
  43.8 1.6 %copy-done.5 = bf16[1280,1152]{1,0:T(8,128)(2,1)} copy-done((bf16[1280,1152]{1,0:T(8,128)(2,1)}, bf16[1280,1152]{1,0:T(8,128)(2,1)S(1)}, u32[]{:S(2)}) %copy-start.5) | copy-done | bytes 2949144
  45.5 1.3 %collective-permute-start.6 = (bf16[640,256]{1,0:T(8,128)(2,1)}, bf16[640,256]{1,0:T(8,128)(2,1)}, u32[]{:S(2)}, u32[]{:S(2)}) collective-permute-start(bf16[640,256]{1,0:T(8,128)(2,1)} %get-tuple-element.37.inner_ref), channel_id=1, source_target_pairs={{0,4},{12,8},{1,5},{13,9},{2,6},{14,10},{3,7},{15,11},{16,20},{28,... | collective-permute-start | bytes 983048 | tf_op jit(solution)/shard_map/ppermute | solution.py:341
  46.8 0.8 add.18
  47.6 2.5 %collective-permute-start.9 = (bf16[640,256]{1,0:T(8,128)(2,1)}, bf16[640,256]{1,0:T(8,128)(2,1)}, u32[]{:S(2)}, u32[]{:S(2)}) collective-permute-start(bf16[640,256]{1,0:T(8,128)(2,1)} %add.18), channel_id=1, source_target_pairs={{4,8},{8,4},{5,9},{9,5},{6,10},{10,6},{7,11},{11,7},{20,24},{24,20... | collective-permute-start | bytes 983048 | tf_op jit(solution)/shard_map/ppermute | solution.py:344
  50.1 4.7 %collective-permute-done.6.refs_0_ = bf16[640,256]{1,0:T(8,128)(2,1)} collective-permute-done((bf16[640,256]{1,0:T(8,128)(2,1)}, bf16[640,256]{1,0:T(8,128)(2,1)}, u32[]{:S(2)}, u32[]{:S(2)}) %collective-permute-start.6) | collective-permute-done | bytes 327712 | tf_op jit(solution)/shard_map/ppermute | solution.py:341
  54.7 2.1 %collective-permute-done.9.refs_1_ = bf16[640,256]{1,0:T(8,128)(2,1)} collective-permute-done((bf16[640,256]{1,0:T(8,128)(2,1)}, bf16[640,256]{1,0:T(8,128)(2,1)}, u32[]{:S(2)}, u32[]{:S(2)}) %collective-permute-start.9) | collective-permute-done | bytes 327712 | tf_op jit(solution)/shard_map/ppermute | solution.py:344
  56.9 2.3 %merge.1 = (bf16[640,256]{1,0:T(8,128)(2,1)}, bf16[640,128]{1,0:T(8,128)(2,1)}) custom-call(s32[1]{0:T(128)} %bitcast.3.middle_ref, bf16[640,256]{1,0:T(8,128)(2,1)} %get-tuple-element.37.inner_ref, bf16[640,256]{1,0:T(8,128)(2,1)S(1)} %get-tuple-element.38.outer_ref, bf16[640,256]{1,0:T(8,128)(2,1)} %collective-permute-done.6.refs_0_, ...), custom_call_target="tpu_custom_call" | custom-call | tf_op jit(solution)/shard_map/merge/pallas_call | solution.py:362
  59.1 1.3 %collective-permute-start.12 = (bf16[640,128]{1,0:T(8,128)(2,1)}, bf16[640,128]{1,0:T(8,128)(2,1)S(1)}, u32[]{:S(2)}, u32[]{:S(2)}) collective-permute-start(bf16[640,128]{1,0:T(8,128)(2,1)} %get-tuple-element.55), channel_id=1, source_target_pairs={{0,1},{2,3},{4,5},{6,7},{8,9},{10,11},{12,13},{14,15},{16,17},{18,... | collective-permute-start | bytes 491528 | tf_op jit(solution)/shard_map/ppermute | solution.py:453
  60.4 1.6 %collective-permute-start.14 = (bf16[640,256]{1,0:T(8,128)(2,1)}, bf16[640,256]{1,0:T(8,128)(2,1)S(1)}, u32[]{:S(2)}, u32[]{:S(2)}) collective-permute-start(bf16[640,256]{1,0:T(8,128)(2,1)} %get-tuple-element.50.refs_1_), channel_id=1, source_target_pairs={{0,2},{2,0},{1,3},{3,1},{4,6},{6,4},{5,7},{7,5},{8,10},{10,8},{9,1... | collective-permute-start | bytes 983048 | tf_op jit(solution)/shard_map/ppermute | solution.py:440
  62.0 0.1 pad_add_fusion.where_ref
  62.1 1.8 %copy-done.1 = bf16[1280,1152]{1,0:T(8,128)(2,1)S(1)} copy-done((bf16[1280,1152]{1,0:T(8,128)(2,1)S(1)}, bf16[1280,1152]{1,0:T(8,128)(2,1)}, u32[]{:S(2)}) %copy-start.1) | copy-done | bytes 2949144
  63.9 1.8 %copy-done.4 = bf16[1280,1152]{1,0:T(8,128)(2,1)S(1)} copy-done((bf16[1280,1152]{1,0:T(8,128)(2,1)S(1)}, bf16[1280,1152]{1,0:T(8,128)(2,1)}, u32[]{:S(2)}) %copy-start.4) | copy-done | bytes 2949144
  65.7 1.8 %copy-done.6 = bf16[1280,1152]{1,0:T(8,128)(2,1)S(1)} copy-done((bf16[1280,1152]{1,0:T(8,128)(2,1)S(1)}, bf16[1280,1152]{1,0:T(8,128)(2,1)}, u32[]{:S(2)}) %copy-start.6) | copy-done | bytes 2949144
  67.6 3.5 %project_own.1 = (f32[2,272,1152]{2,1,0:T(8,128)S(1)}, f32[2,272,1152]{2,1,0:T(8,128)S(1)}) custom-call(s32[2]{0:T(128)S(1)} %pad_add_fusion.where_ref, bf16[640,128]{1,0:T(8,128)(2,1)S(1)} %collective-permute-done.12.refs_0_, bf16[640,256]{1,0:T(8,128)(2,1)} %get-tuple-element.50.refs_1_, bf16[1280,1152]{1,0:T(8,128)(2,1)S(1)} %get-tuple-element.51.refs_2_, ...), custom_call_target="tpu_custom_call" | custom-call | tf_op jit(solution)/shard_map/project_own/pallas_call | solution.py:456
  71.1 0.0 copy-start.13
  71.1 3.1 %collective-permute-start.13 = (bf16[640,128]{1,0:T(8,128)(2,1)}, bf16[640,128]{1,0:T(8,128)(2,1)S(1)}, u32[]{:S(2)}, u32[]{:S(2)}) collective-permute-start(bf16[640,128]{1,0:T(8,128)(2,1)} %get-tuple-element.55), channel_id=1, source_target_pairs={{0,3},{2,1},{4,7},{6,5},{8,11},{10,9},{12,15},{14,13},{16,19},{18,... | collective-permute-start | bytes 491528 | tf_op jit(solution)/shard_map/ppermute | solution.py:453
  74.3 2.9 %collective-permute-done.13.refs_0_ = bf16[640,128]{1,0:T(8,128)(2,1)S(1)} collective-permute-done((bf16[640,128]{1,0:T(8,128)(2,1)}, bf16[640,128]{1,0:T(8,128)(2,1)S(1)}, u32[]{:S(2)}, u32[]{:S(2)}) %collective-permute-start.13) | collective-permute-done | bytes 163872 | tf_op jit(solution)/shard_map/ppermute | solution.py:453
  77.2 3.6 %project_others.1 = (f32[2,272,1152]{2,1,0:T(8,128)S(1)}, f32[8,272]{1,0:T(8,128)S(1)}) custom-call(s32[2]{0:T(128)S(1)} %pad_add_fusion.where_ref, bf16[640,128]{1,0:T(8,128)(2,1)S(1)} %collective-permute-done.13.refs_0_, bf16[640,256]{1,0:T(8,128)(2,1)S(1)} %collective-permute-done.14.refs_1_, bf16[1280,1152]{1,0:T(8,128)(2,1)S(1)} %get-tuple-element.51.refs_2_, ...), custom_call_target="tpu_custom_call" | custom-call | tf_op jit(solution)/shard_map/project_others/pallas_call | solution.py:466
  80.8 1.5 %copy-done.11 = f32[2,272,1152]{2,1,0:T(8,128)} copy-done((f32[2,272,1152]{2,1,0:T(8,128)}, f32[2,272,1152]{2,1,0:T(8,128)S(1)}, u32[]{:S(2)}) %copy-start.11) | copy-done | bytes 2506776
  82.3 0.5 collective-permute-start.15
  82.9 3.2 %collective-permute-done.15.refs_1_ = f32[8,272]{1,0:T(8,128)S(1)} collective-permute-done((f32[8,272]{1,0:T(8,128)S(1)}, f32[8,272]{1,0:T(8,128)S(1)}, u32[]{:S(2)}, u32[]{:S(2)}) %collective-permute-start.15) | collective-permute-done | bytes 8736 | tf_op jit(solution)/shard_map/ppermute | solution.py:485
  86.0 1.3 %copy-done.10 = bf16[256,2304]{1,0:T(8,128)(2,1)S(1)} copy-done((bf16[256,2304]{1,0:T(8,128)(2,1)S(1)}, bf16[256,2304]{1,0:T(8,128)(2,1)}, u32[]{:S(2)}) %copy-start.10) | copy-done | bytes 1179672
  87.3 1.7 %copy-done.12 = f32[2,272,1152]{2,1,0:T(8,128)S(1)} copy-done((f32[2,272,1152]{2,1,0:T(8,128)S(1)}, f32[2,272,1152]{2,1,0:T(8,128)}, u32[]{:S(2)}) %copy-start.12) | copy-done | bytes 2506776
  89.0 3.5 %finish.1 = bf16[256,2304]{1,0:T(8,128)(2,1)} custom-call(s32[1]{0:T(128)} %bitcast.keep_ref, f32[8,272]{1,0:T(8,128)S(1)} %get-tuple-element.57.refs_0_, f32[8,272]{1,0:T(8,128)S(1)} %collective-permute-done.15.refs_1_, f32[2,272,1152]{2,1,0:T(8,128)S(1)} %copy-done.12, bf16[256,2304]{1,0:T(8,128)(2,1)S(1)} %copy-done.10, f32[4,2304]{1,0:T(4,128)S(1)} %copy-done.13), custom_call_target="tpu_custom_call" | custom-call | tf_op jit(solution)/shard_map/finish/pallas_call | solution.py:491
  (28 shorter events, 0.1 us)
Async XLA Ops:
  0.0 39.5 %collective-permute-start.3 = (bf16[1280,1152]{1,0:T(8,128)(2,1)}, bf16[1280,1152]{1,0:T(8,128)(2,1)}, u32[]{:S(2)}, u32[]{:S(2)}) collective-permute-start(bf16[1280,1152]{1,0:T(8,128)(2,1)} %refs_0_), channel_id=1, source_target_pairs={{0,1},{1,0},{2,3},{3,2},{4,5},{5,4},{6,7},{7,6},{8,9},{9,8},{10,11... | collective-permute-start | bytes 8847368 | tf_op jit(solution)/shard_map/ppermute | solution.py:419
  0.0 39.5 %collective-permute-start.5 = (bf16[1280,1152]{1,0:T(8,128)(2,1)}, bf16[1280,1152]{1,0:T(8,128)(2,1)}, u32[]{:S(2)}, u32[]{:S(2)}) collective-permute-start(bf16[1280,1152]{1,0:T(8,128)(2,1)} %refs_1_), channel_id=1, source_target_pairs={{0,1},{1,0},{2,3},{3,2},{4,5},{5,4},{6,7},{7,6},{8,9},{9,8},{10,11... | collective-permute-start | bytes 8847368 | tf_op jit(solution)/shard_map/ppermute | solution.py:420
  1.9 7.0 %collective-permute-start.2 = (s32[8,256]{1,0:T(8,128)S(1)}, s32[8,256]{1,0:T(8,128)S(1)}, u32[]{:S(2)}, u32[]{:S(2)}) collective-permute-start(s32[8,256]{1,0:T(8,128)S(1)} %place_rows.1.refs_0_), channel_id=1, source_target_pairs={{0,12},{4,8},{8,4},{12,0},{1,13},{5,9},{9,5},{13,1},{2,14},{6,10},... | collective-permute-start | bytes 24584 | tf_op jit(solution)/shard_map/ppermute | solution.py:322
  3.5 5.3 %collective-permute-start.1 = (s32[8,256]{1,0:T(8,128)S(1)}, s32[8,256]{1,0:T(8,128)S(1)}, u32[]{:S(2)}, u32[]{:S(2)}) collective-permute-start(s32[8,256]{1,0:T(8,128)S(1)} %place_rows.1.refs_0_), channel_id=1, source_target_pairs={{0,8},{4,12},{8,0},{12,4},{1,9},{5,13},{9,1},{13,5},{2,10},{6,14},... | collective-permute-start | bytes 24584 | tf_op jit(solution)/shard_map/ppermute | solution.py:322
  4.6 4.2 %collective-permute-start = (s32[8,256]{1,0:T(8,128)S(1)}, s32[8,256]{1,0:T(8,128)S(1)}, u32[]{:S(2)}, u32[]{:S(2)}) collective-permute-start(s32[8,256]{1,0:T(8,128)S(1)} %place_rows.1.refs_0_), channel_id=1, source_target_pairs={{0,4},{4,0},{8,12},{12,8},{1,5},{5,1},{9,13},{13,9},{2,6},{6,2},{1... | collective-permute-start | bytes 24584 | tf_op jit(solution)/shard_map/ppermute | solution.py:322
  8.7 12.6 %copy-start.7 = (bf16[8,80,1024]{2,1,0:T(8,128)(2,1)}, bf16[8,80,1024]{2,1,0:T(8,128)(2,1)S(1)}, u32[]{:S(2)}) copy-start(bf16[8,80,1024]{2,1,0:T(8,128)(2,1)S(1)} %decode_tables.1.refs_4_) | copy-start | bytes 3932164
  10.3 11.0 %collective-permute-start.4 = (bf16[640,256]{1,0:T(8,128)(2,1)S(1)}, bf16[640,256]{1,0:T(8,128)(2,1)S(1)}, u32[]{:S(2)}, u32[]{:S(2)}) collective-permute-start(bf16[640,256]{1,0:T(8,128)(2,1)S(1)} %pick_rows.3), channel_id=1, source_target_pairs={{0,4},{12,8},{1,5},{13,9},{2,6},{14,10},{3,7},{15,11},{16,20},{28,... | collective-permute-start | bytes 983048 | tf_op jit(solution)/shard_map/ppermute | solution.py:341
  12.4 19.6 %collective-permute-start.7 = (bf16[16,2304]{1,0:T(8,128)(2,1)S(1)}, bf16[16,2304]{1,0:T(8,128)(2,1)S(1)}, u32[]{:S(2)}, u32[]{:S(2)}) collective-permute-start(bf16[16,2304]{1,0:T(8,128)(2,1)S(1)} %slice.3), channel_id=1, source_target_pairs={{0,1},{4,5},{8,9},{12,13},{2,3},{6,7},{10,11},{14,15},{16,17},{20,... | collective-permute-start | bytes 221192 | tf_op jit(solution)/shard_map/ppermute | solution.py:425
  21.3 12.0 %collective-permute-start.10 = (bf16[640,256]{1,0:T(8,128)(2,1)S(1)}, bf16[640,256]{1,0:T(8,128)(2,1)S(1)}, u32[]{:S(2)}, u32[]{:S(2)}) collective-permute-start(bf16[640,256]{1,0:T(8,128)(2,1)S(1)} %add.19), channel_id=1, source_target_pairs={{4,8},{8,4},{5,9},{9,5},{6,10},{10,6},{7,11},{11,7},{20,24},{24,20... | collective-permute-start | bytes 983048 | tf_op jit(solution)/shard_map/ppermute | solution.py:344
  24.7 4.4 %copy-start.8 = (bf16[8,80,1024]{2,1,0:T(8,128)(2,1)S(1)}, bf16[8,80,1024]{2,1,0:T(8,128)(2,1)}, u32[]{:S(2)}) copy-start(bf16[8,80,1024]{2,1,0:T(8,128)(2,1)} %copy-done.7) | copy-start | bytes 3932164
  27.6 1.6 %copy-start = (bf16[1280,1152]{1,0:T(8,128)(2,1)}, bf16[1280,1152]{1,0:T(8,128)(2,1)S(1)}, u32[]{:S(2)}) copy-start(bf16[1280,1152]{1,0:T(8,128)(2,1)S(1)} %get-tuple-element.52.refs_3_) | copy-start | bytes 8847364
  32.1 14.7 %collective-permute-start.8 = (bf16[640,256]{1,0:T(8,128)(2,1)S(1)}, bf16[640,256]{1,0:T(8,128)(2,1)S(1)}, u32[]{:S(2)}, u32[]{:S(2)}) collective-permute-start(bf16[640,256]{1,0:T(8,128)(2,1)S(1)} %get-tuple-element.45), channel_id=1, source_target_pairs={{0,4},{12,8},{1,5},{13,9},{2,6},{14,10},{3,7},{15,11},{16,20},{28,... | collective-permute-start | bytes 983048 | tf_op jit(solution)/shard_map/ppermute | solution.py:341
  34.2 15.9 %collective-permute-start.11 = (bf16[640,256]{1,0:T(8,128)(2,1)}, bf16[640,256]{1,0:T(8,128)(2,1)}, u32[]{:S(2)}, u32[]{:S(2)}) collective-permute-start(bf16[640,256]{1,0:T(8,128)(2,1)} %add.20), channel_id=1, source_target_pairs={{4,0},{8,12},{5,1},{9,13},{6,2},{10,14},{7,3},{11,15},{20,16},{24,... | collective-permute-start | bytes 983048 | tf_op jit(solution)/shard_map/ppermute | solution.py:347
  42.2 1.6 %copy-start.3 = (bf16[1280,1152]{1,0:T(8,128)(2,1)}, bf16[1280,1152]{1,0:T(8,128)(2,1)S(1)}, u32[]{:S(2)}) copy-start(bf16[1280,1152]{1,0:T(8,128)(2,1)S(1)} %get-tuple-element.46.refs_4_) | copy-start | bytes 8847364
  43.8 1.6 %copy-start.5 = (bf16[1280,1152]{1,0:T(8,128)(2,1)}, bf16[1280,1152]{1,0:T(8,128)(2,1)S(1)}, u32[]{:S(2)}) copy-start(bf16[1280,1152]{1,0:T(8,128)(2,1)S(1)} %get-tuple-element.47.refs_5_) | copy-start | bytes 8847364
  45.5 9.3 %collective-permute-start.6 = (bf16[640,256]{1,0:T(8,128)(2,1)}, bf16[640,256]{1,0:T(8,128)(2,1)}, u32[]{:S(2)}, u32[]{:S(2)}) collective-permute-start(bf16[640,256]{1,0:T(8,128)(2,1)} %get-tuple-element.37.inner_ref), channel_id=1, source_target_pairs={{0,4},{12,8},{1,5},{13,9},{2,6},{14,10},{3,7},{15,11},{16,20},{28,... | collective-permute-start | bytes 983048 | tf_op jit(solution)/shard_map/ppermute | solution.py:341
  47.6 9.3 %collective-permute-start.9 = (bf16[640,256]{1,0:T(8,128)(2,1)}, bf16[640,256]{1,0:T(8,128)(2,1)}, u32[]{:S(2)}, u32[]{:S(2)}) collective-permute-start(bf16[640,256]{1,0:T(8,128)(2,1)} %add.18), channel_id=1, source_target_pairs={{4,8},{8,4},{5,9},{9,5},{6,10},{10,6},{7,11},{11,7},{20,24},{24,20... | collective-permute-start | bytes 983048 | tf_op jit(solution)/shard_map/ppermute | solution.py:344
  59.1 2.9 %collective-permute-start.12 = (bf16[640,128]{1,0:T(8,128)(2,1)}, bf16[640,128]{1,0:T(8,128)(2,1)S(1)}, u32[]{:S(2)}, u32[]{:S(2)}) collective-permute-start(bf16[640,128]{1,0:T(8,128)(2,1)} %get-tuple-element.55), channel_id=1, source_target_pairs={{0,1},{2,3},{4,5},{6,7},{8,9},{10,11},{12,13},{14,15},{16,17},{18,... | collective-permute-start | bytes 491528 | tf_op jit(solution)/shard_map/ppermute | solution.py:453
  60.4 13.8 %collective-permute-start.14 = (bf16[640,256]{1,0:T(8,128)(2,1)}, bf16[640,256]{1,0:T(8,128)(2,1)S(1)}, u32[]{:S(2)}, u32[]{:S(2)}) collective-permute-start(bf16[640,256]{1,0:T(8,128)(2,1)} %get-tuple-element.50.refs_1_), channel_id=1, source_target_pairs={{0,2},{2,0},{1,3},{3,1},{4,6},{6,4},{5,7},{7,5},{8,10},{10,8},{9,1... | collective-permute-start | bytes 983048 | tf_op jit(solution)/shard_map/ppermute | solution.py:440
  62.1 1.8 %copy-start.1 = (bf16[1280,1152]{1,0:T(8,128)(2,1)S(1)}, bf16[1280,1152]{1,0:T(8,128)(2,1)}, u32[]{:S(2)}) copy-start(bf16[1280,1152]{1,0:T(8,128)(2,1)} %copy-done) | copy-start | bytes 8847364
  63.9 1.8 %copy-start.4 = (bf16[1280,1152]{1,0:T(8,128)(2,1)S(1)}, bf16[1280,1152]{1,0:T(8,128)(2,1)}, u32[]{:S(2)}) copy-start(bf16[1280,1152]{1,0:T(8,128)(2,1)} %copy-done.3) | copy-start | bytes 8847364
  65.7 1.8 %copy-start.6 = (bf16[1280,1152]{1,0:T(8,128)(2,1)S(1)}, bf16[1280,1152]{1,0:T(8,128)(2,1)}, u32[]{:S(2)}) copy-start(bf16[1280,1152]{1,0:T(8,128)(2,1)} %copy-done.5) | copy-start | bytes 8847364
  67.6 9.6 %copy-start.2 = (bf16[1280,1152]{1,0:T(8,128)(2,1)S(1)}, bf16[1280,1152]{1,0:T(8,128)(2,1)}, u32[]{:S(2)}) copy-start(bf16[1280,1152]{1,0:T(8,128)(2,1)} %copy-done) | copy-start | bytes 8847364
  67.6 9.6 %copy-start.9 = (bf16[256,2304]{1,0:T(8,128)(2,1)S(1)}, bf16[256,2304]{1,0:T(8,128)(2,1)}, u32[]{:S(2)}) copy-start(bf16[256,2304]{1,0:T(8,128)(2,1)} %refs_3_.1) | copy-start | bytes 3538948
  71.1 14.9 %copy-start.13 = (f32[4,2304]{1,0:T(4,128)S(1)}, f32[4,2304]{1,0:T(4,128)}, u32[]{:S(2)}) copy-start(f32[4,2304]{1,0:T(4,128)} %refs_4_.1) | copy-start | bytes 110596
  71.1 6.1 %collective-permute-start.13 = (bf16[640,128]{1,0:T(8,128)(2,1)}, bf16[640,128]{1,0:T(8,128)(2,1)S(1)}, u32[]{:S(2)}, u32[]{:S(2)}) collective-permute-start(bf16[640,128]{1,0:T(8,128)(2,1)} %get-tuple-element.55), channel_id=1, source_target_pairs={{0,3},{2,1},{4,7},{6,5},{8,11},{10,9},{12,15},{14,13},{16,19},{18,... | collective-permute-start | bytes 491528 | tf_op jit(solution)/shard_map/ppermute | solution.py:453
  80.8 1.5 %copy-start.11 = (f32[2,272,1152]{2,1,0:T(8,128)}, f32[2,272,1152]{2,1,0:T(8,128)S(1)}, u32[]{:S(2)}) copy-start(f32[2,272,1152]{2,1,0:T(8,128)S(1)} %get-tuple-element.58.refs_2_) | copy-start | bytes 7520260
  82.3 3.7 %collective-permute-start.15 = (f32[8,272]{1,0:T(8,128)S(1)}, f32[8,272]{1,0:T(8,128)S(1)}, u32[]{:S(2)}, u32[]{:S(2)}) collective-permute-start(f32[8,272]{1,0:T(8,128)S(1)} %get-tuple-element.57.refs_0_), channel_id=1, source_target_pairs={{0,2},{2,0},{1,3},{3,1},{4,6},{6,4},{5,7},{7,5},{8,10},{10,8},{9,1... | collective-permute-start | bytes 26120 | tf_op jit(solution)/shard_map/ppermute | solution.py:485
  86.0 1.3 %copy-start.10 = (bf16[256,2304]{1,0:T(8,128)(2,1)S(1)}, bf16[256,2304]{1,0:T(8,128)(2,1)}, u32[]{:S(2)}) copy-start(bf16[256,2304]{1,0:T(8,128)(2,1)} %refs_3_.1) | copy-start | bytes 3538948
  87.3 1.7 %copy-start.12 = (f32[2,272,1152]{2,1,0:T(8,128)S(1)}, f32[2,272,1152]{2,1,0:T(8,128)}, u32[]{:S(2)}) copy-start(f32[2,272,1152]{2,1,0:T(8,128)} %copy-done.11) | copy-start | bytes 7520260

commit v6 on v5

--- a/solution.py
+++ b/solution.py
@@ -130,32 +130,11 @@
 
 
 def merge_kernel(middle_ref, inner_ref, outer_ref, *refs):
-    received = refs[:-2]
-    out_ref, rim_ref = refs[-2:]
+    received = refs[:-1]
     total = jnp.where(middle_ref[0] == 1, inner_ref[...].astype(F32), outer_ref[...].astype(F32))
     for other in received:
         total = total + other[...].astype(F32)
-    total = total.astype(BF16)
-    out_ref[...] = total
-    rim_ref[...] = total[:, total.shape[1] - LANES :]
-
-
-def load_kernel(*refs):
-    sources, targets, sems = refs[:2], refs[2:4], refs[4]
-    rows = sources[0].shape[0]
-    pieces = sems.shape[0] // 2
-    step = rows // pieces
-    copies = []
-    for n in range(pieces):
-        for which in range(2):
-            span = pl.ds(n * step, step)
-            copy = pltpu.make_async_copy(
-                sources[which].at[span, :], targets[which].at[span, :], sems.at[2 * n + which]
-            )
-            copy.start()
-            copies.append(copy)
-    for copy in copies:
-        copy.wait()
+    refs[-1][...] = total.astype(BF16)
 
 
 def project_kernel(shifts, count, where_ref, *refs):
@@ -164,44 +143,65 @@
     rims = refs[:pieces]
     bodies = refs[pieces : 2 * pieces]
     refs = refs[2 * pieces :]
-    weights = refs[:4]
-    if first:
-        key_ref, value_ref = refs[4:]
-    else:
-        begun_keys, begun_values, hidden_halo, hidden, value_ref, stats_ref, states = refs[4:]
-    half = value_ref.shape[-1]
     depth, tokens = bodies[0].shape
     rep = where_ref[0]
     tp = where_ref[1]
+    if first:
+        weights = refs[:4]
+        key_ref, value_ref, rest, held, sems, rest_sems = refs[4:]
+        half = held.shape[-1]
+
+        def bring(target, far, which, n, s, sem):
+            owner = lax.rem(tp + count - s, count)
+            rows = pl.ds(pl.multiple_of(owner * depth, depth), depth)
+            copy = pltpu.make_async_copy(
+                weights[2 * far + which].at[rows, :],
+                target.at[far, which, pl.ds(n * depth, depth), :],
+                sem,
+            )
+            copy.start()
+            return copy
+
+        copies = [
+            bring(held, far, which, 0, 0, sems.at[2 * far + which])
+            for far in range(2)
+            for which in range(2)
+        ]
+    else:
+        rest, begun_keys, begun_values, hidden_halo, hidden = refs[:5]
+        value_hbm, stats_ref, states, done, done_sems = refs[5:]
+        held = rest
+        half = held.shape[-1]
+        for slot in range(2):
+            states[slot, :RIM] = hidden_halo[:, slot * half : (slot + 1) * half]
+            states[slot, RIM:] = hidden[:, slot * half : (slot + 1) * half]
     body = jnp.concatenate([b[...].astype(F32) for b in bodies], axis=0).T.astype(BF16)
     rim = jnp.concatenate([r[...].astype(F32) for r in rims], axis=0).T.astype(BF16)
     memory = jnp.concatenate([rim[LANES - RIM :], body], axis=0)
-    if not first:
-        for slot in range(2):
-            states[slot, :RIM] = hidden_halo[:, slot * half : (slot + 1) * half]
-            states[slot, RIM:] = hidden[:, slot * half : (slot + 1) * half]
     sums = [0.0] * 4
+    later = []
     for far in range(2):
         slot = rep if far == 0 else 1 - rep
-        fields = []
-        for which in range(2):
-            field = None
-            for n, s in enumerate(shifts):
-                at = pl.multiple_of(lax.rem(tp + count - s, count) * depth, depth)
-                part = dot(
-                    memory[:, n * depth : (n + 1) * depth],
-                    weights[2 * far + which][pl.ds(at, depth), :],
-                )
-                field = part if field is None else field + part
-            fields.append(field)
-        keys, values = fields
+        fields = [None, None]
+        for which in (1, 0):
+            if first:
+                copies[2 * far + which].wait()
+            fields[which] = dot(memory, held[far, which])
+            if not first and which == 1:
+                done[far] = fields[1] + begun_values[slot]
+                copy = pltpu.make_async_copy(done.at[far], value_hbm.at[slot], done_sems.at[far])
+                copy.start()
+                later.append(copy)
         if first:
-            key_ref[slot] = keys
-            value_ref[slot] = values
+            value_ref[slot] = fields[1]
+            key_ref[slot] = fields[0]
+            for which in range(2):
+                for n in range(count - 1):
+                    sem = rest_sems.at[(2 * far + which) * (count - 1) + n]
+                    later.append(bring(rest, far, which, n, n + 1, sem))
         else:
-            keys = keys + begun_keys[slot]
-            values = values + begun_values[slot]
-            value_ref[slot] = values
+            keys = fields[0] + begun_keys[slot]
+            values = done[far]
             here = states[slot].astype(F32)
             terms = (here * here, keys * keys, here * keys, values * values)
             sums = [a + jnp.sum(t, axis=1, keepdims=True) for a, t in zip(sums, terms)]
@@ -212,13 +212,26 @@
         for k in range(4):
             packed = jnp.where(lane == k, sums[k], packed)
         stats_ref[...] = dot_nt(unit(8, F32), packed, lax.Precision.HIGHEST)
+    for copy in later:
+        copy.wait()
 
 
 def finish_kernel(count, step, keep_ref, *refs):
     stats = refs[:count]
-    value_ref, hidden_ref, taps_ref, out_hbm, gates, factors, normed, out_ref, sems = refs[count:]
+    value_hbm, hidden_ref, taps_ref, out_hbm = refs[count : count + 4]
+    gates, factors, value_ref, normed, out_ref, in_sems, sems = refs[count + 4 :]
     rows, half = normed.shape
     tokens, width = out_ref.shape
+    arrivals = {}
+    chunk = min(step, half)
+    for slot in range(2):
+        for start in range(0, half, chunk):
+            span = pl.ds(start, chunk)
+            copy = pltpu.make_async_copy(
+                value_hbm.at[slot, :, span], value_ref.at[slot, :, span], in_sems.at[len(arrivals)]
+            )
+            copy.start()
+            arrivals[slot, start] = copy
     total = stats[0][...]
     for other in stats[1:]:
         total = total + other[...]
@@ -238,6 +251,8 @@
             size = min(LANES, half - start)
             span = slice(start, start + size)
             there = slice(slot * half + start, slot * half + start + size)
+            if start % chunk == 0:
+                arrivals[slot, start].wait()
             values = value_ref[slot, :, span]
             normed[:, span] = values * factors[:, :size]
             conv = None
@@ -268,32 +283,15 @@
     return pltpu.with_memory_space_constraint(array, pltpu.HBM)
 
 
-def in_vmem(array):
-    return pltpu.with_memory_space_constraint(array, pltpu.VMEM)
-
-
 def after(array, *others):
     return lax.optimization_barrier((array, *others))[0]
 
 
-def load(pair):
-    target = pltpu.VMEM(pair[0].shape, pair[0].dtype)
-    return pl.pallas_call(
-        load_kernel,
-        in_specs=[pl.BlockSpec(memory_space=pl.ANY)] * 2,
-        out_specs=(pl.BlockSpec(memory_space=pltpu.VMEM),) * 2,
-        out_shape=(target, target),
-        scratch_shapes=[pltpu.SemaphoreType.DMA((8,))],
-        compiler_params=limit(4),
-        name="load_weights",
-    )(*pair)
-
-
 def limit(mib):
     return pltpu.CompilerParams(vmem_limit_bytes=mib << 20)
 
 
-def scattered_sum(stored, decoded, here, early, late):
+def scattered_sum(stored, decoded, here, meanwhile):
     mems = lax.axis_size("mem")
     heads, width, rows = decoded.shape
     tokens = stored.shape[1]
@@ -312,10 +310,10 @@
         name="pick_all",
     )((here * rows).astype(I32).reshape(1), asked, decoded)
     total = lax.psum_scatter(partial, "mem", scatter_dimension=0, tiled=False)
-    return total, total[:, tokens - LANES :], early(partial), late(total)
-
-
-def line_sum(stored, decoded, here, early, late):
+    return total, meanwhile(partial)
+
+
+def line_sum(stored, decoded, here, meanwhile):
     heads, width, rows = decoded.shape
     tokens = stored.shape[1]
     asked = [stored] + [
@@ -337,37 +335,29 @@
             name="pick_rows",
         )(scalars, *asked, decoded)
 
-    def inward(x):
-        return lax.ppermute(x, "mem", [(0, 1), (3, 2)])
-
-    def across(x):
-        return lax.ppermute(x, "mem", [(1, 2), (2, 1)])
-
-    def outward(x):
-        return lax.ppermute(x, "mem", [(1, 0), (2, 3)])
-
+    def send(x, *pairs):
+        return lax.ppermute(x, "mem", pairs)
+
+    middle = ((here == 1) | (here == 2)).astype(I32)
     (farthest,) = pick(0)
-    first = inward(farthest)
-    begun = early(farthest)
-    far_own, inner, outer = pick(1, 2, 3)
-    far_own, begun = lax.optimization_barrier((far_own, begun))
-    second = inward(far_own)
-    crossed = across(farthest + first)
-    ended = late(first)
-    inner, ended = lax.optimization_barrier((inner, ended))
-    third = inward(inner)
-    crossed_near = across(far_own + after(second, *ended))
-    last = outward(outer + crossed)
-    middle = ((here == 1) | (here == 2)).astype(I32).reshape(1)
-    memory, rim = pl.pallas_call(
+    inward = send(farthest, (0, 1), (3, 2))
+    other = meanwhile(farthest)
+    (far,) = pick(1)
+    across = send(far, (1, 2), (2, 1))
+    inner, outer = pick(2, 3)
+    beside = send(jnp.where(middle == 1, outer, inner), (0, 1), (1, 0), (2, 3), (3, 2))
+    onward, other = lax.optimization_barrier((farthest + inward, other))
+    onward = send(onward, (1, 3), (2, 0))
+    past = send(after(far, inward), (0, 2), (3, 1))
+    memory = pl.pallas_call(
         merge_kernel,
         in_specs=[pl.BlockSpec(memory_space=pltpu.SMEM)]
-        + [pl.BlockSpec(memory_space=pltpu.VMEM)] * 5,
-        out_shape=(block, jax.ShapeDtypeStruct((block.shape[0], LANES), BF16)),
+        + [pl.BlockSpec(memory_space=pltpu.VMEM)] * 6,
+        out_shape=block,
         compiler_params=limit(4),
         name="merge",
-    )(middle, inner, outer, third, crossed_near, last)
-    return memory, rim, begun, ended
+    )(middle.reshape(1), inner, outer, across, beside, onward, past)
+    return memory, other
 
 
 def shards(
@@ -420,19 +410,13 @@
     other_value = lax.ppermute(value_weight, "rep", [(0, 1), (1, 0)])
     needed = [(i, i + 1) for i in range(blocks - 1) if (i + 1) * tokens % seq_length]
 
-    def early(token):
+    def meanwhile(token):
         tail = after(hidden[tokens - RIM :], token)
-        halo = lax.ppermute(tail, ("mem", "rep"), needed)
-        return halo, load([in_hbm(after(w, token)) for w in (key_weight, value_weight)])
-
-    def late(token):
-        return load([after(w, token) for w in (other_key, other_value)])
+        return lax.ppermute(tail, ("mem", "rep"), needed)
 
     summed = line_sum if mems == 4 else scattered_sum
-    memory, rim, (hidden_halo, own_weights), other_weights = summed(
-        stored, decoded, here, early, late
-    )
-    weights = [in_vmem(w) for w in (*own_weights, *other_weights)]
+    memory, hidden_halo = summed(stored, decoded, here, meanwhile)
+    weights = [in_hbm(w) for w in (key_weight, value_weight, other_key, other_value)]
 
     where = jnp.stack([lax.axis_index("rep"), lax.axis_index("tp")]).astype(I32)
     extended = tokens + RIM
@@ -452,31 +436,41 @@
         ]
         return lax.ppermute(rim, ("mem", "tp", "rep"), pairs)
 
-    field = pltpu.VMEM((2, extended, half), F32)
-    begun = pl.pallas_call(
+    rim = memory[:, tokens - LANES :]
+    others = tps - 1
+    field = jax.ShapeDtypeStruct((2, extended, half), F32)
+    *begun, rest = pl.pallas_call(
         functools.partial(project_kernel, (0,), tps),
-        in_specs=[smem] + [resident] * 6,
-        out_specs=(resident,) * 2,
-        out_shape=(field, field),
+        in_specs=[smem] + [resident] * 2 + [anywhere] * 4,
+        out_specs=(resident,) * 3,
+        out_shape=(field, field, pltpu.VMEM((2, 2, others * depth, half), BF16)),
+        scratch_shapes=[
+            pltpu.VMEM((2, 2, depth, half), BF16),
+            pltpu.SemaphoreType.DMA((4,)),
+            pltpu.SemaphoreType.DMA((4 * others,)),
+        ],
         compiler_params=limit(12),
         name="project_own",
     )(where, next_rim(rim, 0), memory, *weights)
     rim = after(rim, *begun)
-    others = tps - 1
     values, stats = pl.pallas_call(
         functools.partial(project_kernel, tuple(range(1, tps)), tps),
-        in_specs=[smem] + [resident] * (2 * others + 8),
-        out_specs=(resident,) * 2,
-        out_shape=(field, jax.ShapeDtypeStruct((8, extended), F32)),
-        scratch_shapes=[pltpu.VMEM((2, extended, half), BF16)],
+        in_specs=[smem] + [resident] * (2 * others + 5),
+        out_specs=(pl.BlockSpec(memory_space=pltpu.HBM), resident),
+        out_shape=(pltpu.HBM(field.shape, F32), jax.ShapeDtypeStruct((8, extended), F32)),
+        scratch_shapes=[
+            pltpu.VMEM((2, extended, half), BF16),
+            pltpu.VMEM((2, extended, half), F32),
+            pltpu.SemaphoreType.DMA((2,)),
+        ],
         compiler_params=limit(14),
         name="project_others",
     )(
         where,
         *[next_rim(rim, s) for s in range(1, tps)],
         *bodies[1:],
-        *weights,
-        *[in_vmem(b) for b in begun],
+        rest,
+        *begun,
         hidden_halo,
         hidden,
     )
@@ -490,19 +484,21 @@
         step = next(c for c in (384, 256, 128) if half % c == 0)
     return pl.pallas_call(
         functools.partial(finish_kernel, tps, step),
-        in_specs=[smem] + [resident] * (tps + 3),
+        in_specs=[smem] + [resident] * tps + [anywhere] + [resident] * 2,
         out_specs=anywhere,
         out_shape=jax.ShapeDtypeStruct((tokens, 2 * half), BF16),
         scratch_shapes=[
             pltpu.VMEM((tokens, LANES), F32),
             pltpu.VMEM((extended, LANES), F32),
+            pltpu.VMEM((2, extended, half), F32),
             pltpu.VMEM((extended, half), F32),
             pltpu.VMEM((tokens, 2 * half), BF16),
+            pltpu.SemaphoreType.DMA((2 * half // min(step, half),)),
             pltpu.SemaphoreType.DMA((2 * half // step,)),
         ],
         compiler_params=limit(12),
         name="finish",
-    )(keep, *all_stats, in_vmem(values), hidden, conv_weight)
+    )(keep, *all_stats, in_hbm(values), hidden, conv_weight)
 
 
 def solution(mesh):

time: 93.3 us -> 70.2 us (0.75)
  the two profiles are of different devices: /device:TPU:8 before, /device:TPU:0 now
where the time goes in v6:
time: 70.2 us; the launch traced here: 69.8 us
  starting transfers between devices  25.2 us (36%)
  Pallas kernels  24.5 us (35%)
  waiting for transfers between devices  18.4 us (26%)
  other arithmetic  1.17 us (2%)
    ppermute x5, starting transfers between devices, send(): return lax.ppermute(x, 'mem', pairs)  11.4 us
    ppermute x5, waiting for transfers between devices, send(): return lax.ppermute(x, 'mem', pairs)  10.1 us
    pallas_call x1, Pallas kernels, shards(): pl.pallas_call(functools.partial(project_kernel, (0,), tps), in_specs=[sm...  6.94 us
    ppermute x3, starting transfers between devices, line_sum(): lax.ppermute(stored, 'mem', [(i, i ^ x) for i in range(4)])  5.68 us
    pallas_call x3, Pallas kernels, pick(): pl.pallas_call(functools.partial(pick_kernel, 4, targets), in_specs=[pl.B...  4.97 us
    pallas_call x1, Pallas kernels, shards(): pl.pallas_call(functools.partial(project_kernel, tuple(range(1, tps)), tp...  4.24 us
    ppermute x2, starting transfers between devices, next_rim(): return lax.ppermute(rim, ('mem', 'tp', 'rep'), pairs)  4.21 us
    pallas_call x1, Pallas kernels, shards(): pl.pallas_call(functools.partial(finish_kernel, tps, step), in_specs=[sme...  3.96 us
  transfers between devices with their start and end apart: 15, of which 5 were waited for; matrix products, arithmetic and copies ran while one was open for 2% of the time, Pallas kernels for 23%

profile of v6, /device:TPU:0, one launch (start us, length us, event | category | flops | bytes accessed | tf_op | source)
XLA Modules:
  0.0 69.8 jit_solution(13717921387842552507)
XLA Ops:
  0.0 0.5 collective-permute-start.10
  0.5 0.1 collective-permute-start.11
  0.5 1.3 %place_rows.1.refs_0_ = s32[8,256]{1,0:T(8,128)S(1)} custom-call(s32[8,256]{1,0:T(8,128)} %bitcast.16, s32[32,128]{1,0:T(8,128)} %bitcast.15), custom_call_target="tpu_custom_call" | custom-call | tf_op jit(solution)/shard_map/place_rows/pallas_call | solution.py:382
  1.9 3.1 %collective-permute-start = (s32[8,256]{1,0:T(8,128)S(1)}, s32[8,256]{1,0:T(8,128)S(1)}, u32[]{:S(2)}, u32[]{:S(2)}) collective-permute-start(s32[8,256]{1,0:T(8,128)S(1)} %place_rows.1.refs_0_), channel_id=1, source_target_pairs={{0,4},{4,0},{8,12},{12,8},{1,5},{5,1},{9,13},{13,9},{2,6},{6,2},{1... | collective-permute-start | bytes 24584 | tf_op jit(solution)/shard_map/ppermute | solution.py:320
  4.9 2.6 %collective-permute-start.1 = (s32[8,256]{1,0:T(8,128)S(1)}, s32[8,256]{1,0:T(8,128)S(1)}, u32[]{:S(2)}, u32[]{:S(2)}) collective-permute-start(s32[8,256]{1,0:T(8,128)S(1)} %place_rows.1.refs_0_), channel_id=1, source_target_pairs={{0,8},{4,12},{8,0},{12,4},{1,9},{5,13},{9,1},{13,5},{2,10},{6,14},... | collective-permute-start | bytes 24584 | tf_op jit(solution)/shard_map/ppermute | solution.py:320
  7.5 0.0 collective-permute-start.2
  7.5 0.0 copy-start
  7.5 2.8 %decode_tables.1.refs_4_ = bf16[8,80,1024]{2,1,0:T(8,128)(2,1)S(1)} custom-call(bf16[8,80,1024]{2,1,0:T(8,128)(2,1)} %bitcast.13, bf16[5,8,1024]{2,1,0:T(8,128)(2,1)} %bitcast.14), custom_call_target="tpu_custom_call" | custom-call | tf_op jit(solution)/shard_map/decode_tables/pallas_call | solution.py:396
  10.4 0.1 stack.35.scalars_ref
  10.5 0.0 collective-permute-done.refs_1_
  10.5 0.0 collective-permute-done.1.refs_2_
  10.5 2.5 %collective-permute-done.2.refs_3_ = s32[8,256]{1,0:T(8,128)S(1)} collective-permute-done((s32[8,256]{1,0:T(8,128)S(1)}, s32[8,256]{1,0:T(8,128)S(1)}, u32[]{:S(2)}, u32[]{:S(2)}) %collective-permute-start.2) | collective-permute-done | bytes 8224 | tf_op jit(solution)/shard_map/ppermute | solution.py:320
  13.0 1.4 %pick_rows.5 = bf16[640,256]{1,0:T(8,128)(2,1)S(1)} custom-call(s32[5]{0:T(128)S(1)} %stack.35.scalars_ref, s32[8,256]{1,0:T(8,128)S(1)} %place_rows.1.refs_0_, s32[8,256]{1,0:T(8,128)S(1)} %collective-permute-done.refs_1_, s32[8,256]{1,0:T(8,128)S(1)} %collective-permute-done.1.refs_2_, s32[8,256]{1,0:T(8,128)S(1)} %collective-permute-done.2.refs_3_, ...), custom_call_target="tpu_custom_call" | custom-call | tf_op jit(solution)/shard_map/pick_rows/pallas_call | solution.py:328
  14.4 2.0 %collective-permute-start.5 = (bf16[640,256]{1,0:T(8,128)(2,1)S(1)}, bf16[640,256]{1,0:T(8,128)(2,1)}, u32[]{:S(2)}, u32[]{:S(2)}) collective-permute-start(bf16[640,256]{1,0:T(8,128)(2,1)S(1)} %pick_rows.5), channel_id=1, source_target_pairs={{0,4},{12,8},{1,5},{13,9},{2,6},{14,10},{3,7},{15,11},{16,20},{28,... | collective-permute-start | bytes 983048 | tf_op jit(solution)/shard_map/ppermute | solution.py:339
  16.4 1.4 %pick_rows.4 = bf16[640,256]{1,0:T(8,128)(2,1)S(1)} custom-call(s32[5]{0:T(128)S(1)} %stack.35.scalars_ref, s32[8,256]{1,0:T(8,128)S(1)} %place_rows.1.refs_0_, s32[8,256]{1,0:T(8,128)S(1)} %collective-permute-done.refs_1_, s32[8,256]{1,0:T(8,128)S(1)} %collective-permute-done.1.refs_2_, s32[8,256]{1,0:T(8,128)S(1)} %collective-permute-done.2.refs_3_, ...), custom_call_target="tpu_custom_call" | custom-call | tf_op jit(solution)/shard_map/pick_rows/pallas_call | solution.py:328
  17.8 0.7 collective-permute-start.3
  18.5 0.0 copy-done
  18.6 1.3 %collective-permute-start.6 = (bf16[16,2304]{1,0:T(8,128)(2,1)S(1)}, bf16[16,2304]{1,0:T(8,128)(2,1)S(1)}, u32[]{:S(2)}, u32[]{:S(2)}) collective-permute-start(bf16[16,2304]{1,0:T(8,128)(2,1)S(1)} %slice.6), channel_id=1, source_target_pairs={{0,1},{4,5},{8,9},{12,13},{2,3},{6,7},{10,11},{14,15},{16,17},{20,... | collective-permute-start | bytes 221192 | tf_op jit(solution)/shard_map/ppermute | solution.py:415
  19.9 2.2 %pick_rows.3 = (bf16[640,256]{1,0:T(8,128)(2,1)S(1)}, bf16[640,256]{1,0:T(8,128)(2,1)S(1)}) custom-call(s32[5]{0:T(128)S(1)} %stack.35.scalars_ref, s32[8,256]{1,0:T(8,128)S(1)} %place_rows.1.refs_0_, s32[8,256]{1,0:T(8,128)S(1)} %collective-permute-done.refs_1_, s32[8,256]{1,0:T(8,128)S(1)} %collective-permute-done.1.refs_2_, ...), custom_call_target="tpu_custom_call" | custom-call | tf_op jit(solution)/shard_map/pick_rows/pallas_call | solution.py:328
  22.1 0.0 collective-permute-done.5
  22.1 1.9 %collective-permute-start.4 = (bf16[640,256]{1,0:T(8,128)(2,1)S(1)}, bf16[640,256]{1,0:T(8,128)(2,1)S(1)}, u32[]{:S(2)}, u32[]{:S(2)}) collective-permute-start(bf16[640,256]{1,0:T(8,128)(2,1)S(1)} %broadcast_select_fusion), channel_id=1, source_target_pairs={{0,4},{4,0},{8,12},{12,8},{1,5},{5,1},{9,13},{13,9},{2,6},{6,2},{1... | collective-permute-start | bytes 983048 | tf_op jit(solution)/shard_map/ppermute | solution.py:339
  24.0 1.1 %add.12 = bf16[640,256]{1,0:T(8,128)(2,1)S(1)} add(bf16[640,256]{1,0:T(8,128)(2,1)S(1)} %pick_rows.5, bf16[640,256]{1,0:T(8,128)(2,1)} %collective-permute-done.5) | non-fusion elementwise | flops 163840 | bytes 983040 | tf_op jit(solution)/shard_map/add | solution.py:349
  25.0 0.0 collective-permute-done.6.refs_5_
  25.0 0.0 copy-start.1
  25.0 1.3 %collective-permute-start.7 = (bf16[640,256]{1,0:T(8,128)(2,1)S(1)}, bf16[640,256]{1,0:T(8,128)(2,1)S(1)}, u32[]{:S(2)}, u32[]{:S(2)}) collective-permute-start(bf16[640,256]{1,0:T(8,128)(2,1)S(1)} %add.12), channel_id=1, source_target_pairs={{4,12},{8,0},{5,13},{9,1},{6,14},{10,2},{7,15},{11,3},{20,28},{24,... | collective-permute-start | bytes 983048 | tf_op jit(solution)/shard_map/ppermute | solution.py:339
  26.3 0.0 collective-permute-done.3.refs_0_
  26.4 5.5 %collective-permute-start.8 = (bf16[640,256]{1,0:T(8,128)(2,1)S(1)}, bf16[640,256]{1,0:T(8,128)(2,1)S(1)}, u32[]{:S(2)}, u32[]{:S(2)}) collective-permute-start(bf16[640,256]{1,0:T(8,128)(2,1)S(1)} %pick_rows.4), channel_id=1, source_target_pairs={{0,8},{12,4},{1,9},{13,5},{2,10},{14,6},{3,11},{15,7},{16,24},{28,... | collective-permute-start | bytes 983048 | tf_op jit(solution)/shard_map/ppermute | solution.py:339
  31.8 2.8 %collective-permute-done.4.refs_1_ = bf16[640,256]{1,0:T(8,128)(2,1)S(1)} collective-permute-done((bf16[640,256]{1,0:T(8,128)(2,1)S(1)}, bf16[640,256]{1,0:T(8,128)(2,1)S(1)}, u32[]{:S(2)}, u32[]{:S(2)}) %collective-permute-start.4) | collective-permute-done | bytes 327712 | tf_op jit(solution)/shard_map/ppermute | solution.py:339
  34.6 7.3 %collective-permute-done.7.refs_2_ = bf16[640,256]{1,0:T(8,128)(2,1)S(1)} collective-permute-done((bf16[640,256]{1,0:T(8,128)(2,1)S(1)}, bf16[640,256]{1,0:T(8,128)(2,1)S(1)}, u32[]{:S(2)}, u32[]{:S(2)}) %collective-permute-start.7) | collective-permute-done | bytes 327712 | tf_op jit(solution)/shard_map/ppermute | solution.py:339
  41.9 0.0 collective-permute-done.8.refs_3_
  41.9 0.2 merge.1.refs_1_
  42.2 0.0 copy-done.1
  42.2 1.3 %collective-permute-start.9 = (bf16[640,128]{1,0:T(8,128)(2,1)S(1)}, bf16[640,128]{1,0:T(8,128)(2,1)S(1)}, u32[]{:S(2)}, u32[]{:S(2)}) collective-permute-start(bf16[640,128]{1,0:T(8,128)(2,1)S(1)} %slice.8), channel_id=1, source_target_pairs={{0,1},{2,3},{4,5},{6,7},{8,9},{10,11},{12,13},{14,15},{16,17},{18,... | collective-permute-start | bytes 491528 | tf_op jit(solution)/shard_map/ppermute | solution.py:437
  43.5 1.6 %collective-permute-start.13 = (bf16[640,256]{1,0:T(8,128)(2,1)S(1)}, bf16[640,256]{1,0:T(8,128)(2,1)S(1)}, u32[]{:S(2)}, u32[]{:S(2)}) collective-permute-start(bf16[640,256]{1,0:T(8,128)(2,1)S(1)} %merge.1.refs_1_), channel_id=1, source_target_pairs={{0,2},{2,0},{1,3},{3,1},{4,6},{6,4},{5,7},{7,5},{8,10},{10,8},{9,1... | collective-permute-start | bytes 983048 | tf_op jit(solution)/shard_map/ppermute | solution.py:424
  45.1 0.1 pad_add_fusion.where_ref
  45.2 0.0 collective-permute-done.9.refs_0_
  45.2 0.0 collective-permute-done.10.refs_4_
  45.2 0.0 collective-permute-done.11.refs_5_
  45.2 6.9 %project_own.1 = (f32[2,272,1152]{2,1,0:T(8,128)S(1)}, f32[2,272,1152]{2,1,0:T(8,128)S(1)}, bf16[2,2,640,1152]{3,2,1,0:T(8,128)(2,1)S(1)}) custom-call(s32[2]{0:T(128)S(1)} %pad_add_fusion.where_ref, bf16[640,128]{1,0:T(8,128)(2,1)S(1)} %collective-permute-done.9.refs_0_, bf16[640,256]{1,0:T(8,128)(2,1)S(1)} %merge.1.refs_1_, bf16[1280,1152]{1,0:T(8,128)(2,1)} %refs_2_.1, ...), custom_call_target="tpu_custom_call" | custom-call | tf_op jit(solution)/shard_map/project_own/pallas_call | solution.py:442
  52.1 2.9 %collective-permute-start.12 = (bf16[640,128]{1,0:T(8,128)(2,1)S(1)}, bf16[640,128]{1,0:T(8,128)(2,1)S(1)}, u32[]{:S(2)}, u32[]{:S(2)}) collective-permute-start(bf16[640,128]{1,0:T(8,128)(2,1)S(1)} %slice.8), channel_id=1, source_target_pairs={{0,3},{2,1},{4,7},{6,5},{8,11},{10,9},{12,15},{14,13},{16,19},{18,... | collective-permute-start | bytes 491528 | tf_op jit(solution)/shard_map/ppermute | solution.py:437
  55.1 0.0 collective-permute-done.13.refs_1_
  55.1 2.6 %collective-permute-done.12.refs_0_ = bf16[640,128]{1,0:T(8,128)(2,1)S(1)} collective-permute-done((bf16[640,128]{1,0:T(8,128)(2,1)S(1)}, bf16[640,128]{1,0:T(8,128)(2,1)S(1)}, u32[]{:S(2)}, u32[]{:S(2)}) %collective-permute-start.12) | collective-permute-done | bytes 163872 | tf_op jit(solution)/shard_map/ppermute | solution.py:437
  57.7 0.0 copy-done.2
  57.7 4.2 %project_others.1 = (f32[2,272,1152]{2,1,0:T(8,128)}, f32[8,272]{1,0:T(8,128)S(1)}) custom-call(s32[2]{0:T(128)S(1)} %pad_add_fusion.where_ref, bf16[640,128]{1,0:T(8,128)(2,1)S(1)} %collective-permute-done.12.refs_0_, bf16[640,256]{1,0:T(8,128)(2,1)S(1)} %collective-permute-done.13.refs_1_, bf16[2,2,640,1152]{3,2,1,0:T(8,128)(2,1)S(1)} %get-tuple-element.25.refs_2_, ...), custom_call_target="tpu_custom_call" | custom-call | tf_op jit(solution)/shard_map/project_others/pallas_call | solution.py:456
  61.9 0.6 collective-permute-start.14
  62.5 3.2 %collective-permute-done.14.refs_1_ = f32[8,272]{1,0:T(8,128)S(1)} collective-permute-done((f32[8,272]{1,0:T(8,128)S(1)}, f32[8,272]{1,0:T(8,128)S(1)}, u32[]{:S(2)}, u32[]{:S(2)}) %collective-permute-start.14) | collective-permute-done | bytes 8736 | tf_op jit(solution)/shard_map/ppermute | solution.py:479
  65.7 0.0 copy-done.3
  65.7 4.0 %finish.1 = bf16[256,2304]{1,0:T(8,128)(2,1)} custom-call(s32[1]{0:T(128)} %bitcast.keep_ref, f32[8,272]{1,0:T(8,128)S(1)} %get-tuple-element.27.refs_0_, f32[8,272]{1,0:T(8,128)S(1)} %collective-permute-done.14.refs_1_, f32[2,272,1152]{2,1,0:T(8,128)} %get-tuple-element.28.refs_2_, bf16[256,2304]{1,0:T(8,128)(2,1)S(1)} %copy-done, f32[4,2304]{1,0:T(4,128)S(1)} %copy-done.3), custom_call_target="tpu_custom_call" | custom-call | tf_op jit(solution)/shard_map/finish/pallas_call | solution.py:485
  (5 shorter events, 0.1 us)
Async XLA Ops:
  0.0 45.2 %collective-permute-start.10 = (bf16[1280,1152]{1,0:T(8,128)(2,1)}, bf16[1280,1152]{1,0:T(8,128)(2,1)}, u32[]{:S(2)}, u32[]{:S(2)}) collective-permute-start(bf16[1280,1152]{1,0:T(8,128)(2,1)} %refs_2_.1), channel_id=1, source_target_pairs={{0,1},{1,0},{2,3},{3,2},{4,5},{5,4},{6,7},{7,6},{8,9},{9,8},{10,11... | collective-permute-start | bytes 8847368 | tf_op jit(solution)/shard_map/ppermute | solution.py:409
  0.5 44.7 %collective-permute-start.11 = (bf16[1280,1152]{1,0:T(8,128)(2,1)}, bf16[1280,1152]{1,0:T(8,128)(2,1)}, u32[]{:S(2)}, u32[]{:S(2)}) collective-permute-start(bf16[1280,1152]{1,0:T(8,128)(2,1)} %refs_3_.2), channel_id=1, source_target_pairs={{0,1},{1,0},{2,3},{3,2},{4,5},{5,4},{6,7},{7,6},{8,9},{9,8},{10,11... | collective-permute-start | bytes 8847368 | tf_op jit(solution)/shard_map/ppermute | solution.py:410
  1.9 8.6 %collective-permute-start = (s32[8,256]{1,0:T(8,128)S(1)}, s32[8,256]{1,0:T(8,128)S(1)}, u32[]{:S(2)}, u32[]{:S(2)}) collective-permute-start(s32[8,256]{1,0:T(8,128)S(1)} %place_rows.1.refs_0_), channel_id=1, source_target_pairs={{0,4},{4,0},{8,12},{12,8},{1,5},{5,1},{9,13},{13,9},{2,6},{6,2},{1... | collective-permute-start | bytes 24584 | tf_op jit(solution)/shard_map/ppermute | solution.py:320
  4.9 5.5 %collective-permute-start.1 = (s32[8,256]{1,0:T(8,128)S(1)}, s32[8,256]{1,0:T(8,128)S(1)}, u32[]{:S(2)}, u32[]{:S(2)}) collective-permute-start(s32[8,256]{1,0:T(8,128)S(1)} %place_rows.1.refs_0_), channel_id=1, source_target_pairs={{0,8},{4,12},{8,0},{12,4},{1,9},{5,13},{9,1},{13,5},{2,10},{6,14},... | collective-permute-start | bytes 24584 | tf_op jit(solution)/shard_map/ppermute | solution.py:320
  7.5 5.4 %collective-permute-start.2 = (s32[8,256]{1,0:T(8,128)S(1)}, s32[8,256]{1,0:T(8,128)S(1)}, u32[]{:S(2)}, u32[]{:S(2)}) collective-permute-start(s32[8,256]{1,0:T(8,128)S(1)} %place_rows.1.refs_0_), channel_id=1, source_target_pairs={{0,12},{4,8},{8,4},{12,0},{1,13},{5,9},{9,5},{13,1},{2,14},{6,10},... | collective-permute-start | bytes 24584 | tf_op jit(solution)/shard_map/ppermute | solution.py:320
  7.5 11.0 %copy-start = (bf16[256,2304]{1,0:T(8,128)(2,1)S(1)}, bf16[256,2304]{1,0:T(8,128)(2,1)}, u32[]{:S(2)}) copy-start(bf16[256,2304]{1,0:T(8,128)(2,1)} %refs_3_.3) | copy-start | bytes 3538948
  14.4 7.7 %collective-permute-start.5 = (bf16[640,256]{1,0:T(8,128)(2,1)S(1)}, bf16[640,256]{1,0:T(8,128)(2,1)}, u32[]{:S(2)}, u32[]{:S(2)}) collective-permute-start(bf16[640,256]{1,0:T(8,128)(2,1)S(1)} %pick_rows.5), channel_id=1, source_target_pairs={{0,4},{12,8},{1,5},{13,9},{2,6},{14,10},{3,7},{15,11},{16,20},{28,... | collective-permute-start | bytes 983048 | tf_op jit(solution)/shard_map/ppermute | solution.py:339
  17.8 8.5 %collective-permute-start.3 = (bf16[640,256]{1,0:T(8,128)(2,1)S(1)}, bf16[640,256]{1,0:T(8,128)(2,1)S(1)}, u32[]{:S(2)}, u32[]{:S(2)}) collective-permute-start(bf16[640,256]{1,0:T(8,128)(2,1)S(1)} %pick_rows.4), channel_id=1, source_target_pairs={{4,8},{8,4},{5,9},{9,5},{6,10},{10,6},{7,11},{11,7},{20,24},{24,20... | collective-permute-start | bytes 983048 | tf_op jit(solution)/shard_map/ppermute | solution.py:339
  18.6 6.5 %collective-permute-start.6 = (bf16[16,2304]{1,0:T(8,128)(2,1)S(1)}, bf16[16,2304]{1,0:T(8,128)(2,1)S(1)}, u32[]{:S(2)}, u32[]{:S(2)}) collective-permute-start(bf16[16,2304]{1,0:T(8,128)(2,1)S(1)} %slice.6), channel_id=1, source_target_pairs={{0,1},{4,5},{8,9},{12,13},{2,3},{6,7},{10,11},{14,15},{16,17},{20,... | collective-permute-start | bytes 221192 | tf_op jit(solution)/shard_map/ppermute | solution.py:415
  22.1 12.6 %collective-permute-start.4 = (bf16[640,256]{1,0:T(8,128)(2,1)S(1)}, bf16[640,256]{1,0:T(8,128)(2,1)S(1)}, u32[]{:S(2)}, u32[]{:S(2)}) collective-permute-start(bf16[640,256]{1,0:T(8,128)(2,1)S(1)} %broadcast_select_fusion), channel_id=1, source_target_pairs={{0,4},{4,0},{8,12},{12,8},{1,5},{5,1},{9,13},{13,9},{2,6},{6,2},{1... | collective-permute-start | bytes 983048 | tf_op jit(solution)/shard_map/ppermute | solution.py:339
  25.0 17.2 %copy-start.1 = (bf16[16,2304]{1,0:T(8,128)(2,1)}, bf16[16,2304]{1,0:T(8,128)(2,1)S(1)}, u32[]{:S(2)}) copy-start(bf16[16,2304]{1,0:T(8,128)(2,1)S(1)} %collective-permute-done.6.refs_5_) | copy-start | bytes 221188
  25.0 16.9 %collective-permute-start.7 = (bf16[640,256]{1,0:T(8,128)(2,1)S(1)}, bf16[640,256]{1,0:T(8,128)(2,1)S(1)}, u32[]{:S(2)}, u32[]{:S(2)}) collective-permute-start(bf16[640,256]{1,0:T(8,128)(2,1)S(1)} %add.12), channel_id=1, source_target_pairs={{4,12},{8,0},{5,13},{9,1},{6,14},{10,2},{7,15},{11,3},{20,28},{24,... | collective-permute-start | bytes 983048 | tf_op jit(solution)/shard_map/ppermute | solution.py:339
  26.4 15.6 %collective-permute-start.8 = (bf16[640,256]{1,0:T(8,128)(2,1)S(1)}, bf16[640,256]{1,0:T(8,128)(2,1)S(1)}, u32[]{:S(2)}, u32[]{:S(2)}) collective-permute-start(bf16[640,256]{1,0:T(8,128)(2,1)S(1)} %pick_rows.4), channel_id=1, source_target_pairs={{0,8},{12,4},{1,9},{13,5},{2,10},{14,6},{3,11},{15,7},{16,24},{28,... | collective-permute-start | bytes 983048 | tf_op jit(solution)/shard_map/ppermute | solution.py:339
  42.2 2.9 %collective-permute-start.9 = (bf16[640,128]{1,0:T(8,128)(2,1)S(1)}, bf16[640,128]{1,0:T(8,128)(2,1)S(1)}, u32[]{:S(2)}, u32[]{:S(2)}) collective-permute-start(bf16[640,128]{1,0:T(8,128)(2,1)S(1)} %slice.8), channel_id=1, source_target_pairs={{0,1},{2,3},{4,5},{6,7},{8,9},{10,11},{12,13},{14,15},{16,17},{18,... | collective-permute-start | bytes 491528 | tf_op jit(solution)/shard_map/ppermute | solution.py:437
  43.5 11.5 %collective-permute-start.13 = (bf16[640,256]{1,0:T(8,128)(2,1)S(1)}, bf16[640,256]{1,0:T(8,128)(2,1)S(1)}, u32[]{:S(2)}, u32[]{:S(2)}) collective-permute-start(bf16[640,256]{1,0:T(8,128)(2,1)S(1)} %merge.1.refs_1_), channel_id=1, source_target_pairs={{0,2},{2,0},{1,3},{3,1},{4,6},{6,4},{5,7},{7,5},{8,10},{10,8},{9,1... | collective-permute-start | bytes 983048 | tf_op jit(solution)/shard_map/ppermute | solution.py:424
  45.2 12.5 %copy-start.2 = (bf16[16,2304]{1,0:T(8,128)(2,1)S(1)}, bf16[16,2304]{1,0:T(8,128)(2,1)}, u32[]{:S(2)}) copy-start(bf16[16,2304]{1,0:T(8,128)(2,1)} %copy-done.1) | copy-start | bytes 221188
  52.1 5.6 %collective-permute-start.12 = (bf16[640,128]{1,0:T(8,128)(2,1)S(1)}, bf16[640,128]{1,0:T(8,128)(2,1)S(1)}, u32[]{:S(2)}, u32[]{:S(2)}) collective-permute-start(bf16[640,128]{1,0:T(8,128)(2,1)S(1)} %slice.8), channel_id=1, source_target_pairs={{0,3},{2,1},{4,7},{6,5},{8,11},{10,9},{12,15},{14,13},{16,19},{18,... | collective-permute-start | bytes 491528 | tf_op jit(solution)/shard_map/ppermute | solution.py:437
  57.7 8.0 %copy-start.3 = (f32[4,2304]{1,0:T(4,128)S(1)}, f32[4,2304]{1,0:T(4,128)}, u32[]{:S(2)}) copy-start(f32[4,2304]{1,0:T(4,128)} %refs_4_.1) | copy-start | bytes 110596
  61.9 3.8 %collective-permute-start.14 = (f32[8,272]{1,0:T(8,128)S(1)}, f32[8,272]{1,0:T(8,128)S(1)}, u32[]{:S(2)}, u32[]{:S(2)}) collective-permute-start(f32[8,272]{1,0:T(8,128)S(1)} %get-tuple-element.27.refs_0_), channel_id=1, source_target_pairs={{0,2},{2,0},{1,3},{3,1},{4,6},{6,4},{5,7},{7,5},{8,10},{10,8},{9,1... | collective-permute-start | bytes 26120 | tf_op jit(solution)/shard_map/ppermute | solution.py:479

commit v7 on v6

--- a/solution.py
+++ b/solution.py
@@ -165,9 +165,16 @@
         copies = [
             bring(held, far, which, 0, 0, sems.at[2 * far + which])
             for far in range(2)
-            for which in range(2)
+            for which in (1, 0)
+        ]
+        later = [
+            bring(rest, far, which, n, n + 1, rest_sems.at[(2 * far + which) * (count - 1) + n])
+            for far in range(2)
+            for which in (1, 0)
+            for n in range(count - 1)
         ]
     else:
+        later = []
         rest, begun_keys, begun_values, hidden_halo, hidden = refs[:5]
         value_hbm, stats_ref, states, done, done_sems = refs[5:]
         held = rest
@@ -179,13 +186,12 @@
     rim = jnp.concatenate([r[...].astype(F32) for r in rims], axis=0).T.astype(BF16)
     memory = jnp.concatenate([rim[LANES - RIM :], body], axis=0)
     sums = [0.0] * 4
-    later = []
     for far in range(2):
         slot = rep if far == 0 else 1 - rep
         fields = [None, None]
         for which in (1, 0):
             if first:
-                copies[2 * far + which].wait()
+                copies[2 * far + 1 - which].wait()
             fields[which] = dot(memory, held[far, which])
             if not first and which == 1:
                 done[far] = fields[1] + begun_values[slot]
@@ -195,10 +201,6 @@
         if first:
             value_ref[slot] = fields[1]
             key_ref[slot] = fields[0]
-            for which in range(2):
-                for n in range(count - 1):
-                    sem = rest_sems.at[(2 * far + which) * (count - 1) + n]
-                    later.append(bring(rest, far, which, n, n + 1, sem))
         else:
             keys = fields[0] + begun_keys[slot]
             values = done[far]
@@ -291,7 +293,7 @@
     return pltpu.CompilerParams(vmem_limit_bytes=mib << 20)
 
 
-def scattered_sum(stored, decoded, here, meanwhile):
+def scattered_sum(stored, decoded, here, meanwhile, settled):
     mems = lax.axis_size("mem")
     heads, width, rows = decoded.shape
     tokens = stored.shape[1]
@@ -310,15 +312,16 @@
         name="pick_all",
     )((here * rows).astype(I32).reshape(1), asked, decoded)
     total = lax.psum_scatter(partial, "mem", scatter_dimension=0, tiled=False)
-    return total, meanwhile(partial)
-
-
-def line_sum(stored, decoded, here, meanwhile):
+    return total, meanwhile(partial), settled
+
+
+def line_sum(stored, decoded, here, meanwhile, settled):
     heads, width, rows = decoded.shape
     tokens = stored.shape[1]
     asked = [stored] + [
         lax.ppermute(stored, "mem", [(i, i ^ x) for i in range(4)]) for x in range(1, 4)
     ]
+    asked, settled = lax.optimization_barrier((asked, settled))
     right = here >= 2
     order = [here ^ jnp.where(right, j, 3 - j) for j in range(4)]
     scalars = jnp.stack([here * rows] + order).astype(I32)
@@ -341,14 +344,14 @@
     middle = ((here == 1) | (here == 2)).astype(I32)
     (farthest,) = pick(0)
     inward = send(farthest, (0, 1), (3, 2))
-    other = meanwhile(farthest)
     (far,) = pick(1)
     across = send(far, (1, 2), (2, 1))
     inner, outer = pick(2, 3)
     beside = send(jnp.where(middle == 1, outer, inner), (0, 1), (1, 0), (2, 3), (3, 2))
-    onward, other = lax.optimization_barrier((farthest + inward, other))
+    past = send(far, (0, 2), (3, 1))
+    onward = farthest + inward
+    other = meanwhile(onward)
     onward = send(onward, (1, 3), (2, 0))
-    past = send(after(far, inward), (0, 2), (3, 1))
     memory = pl.pallas_call(
         merge_kernel,
         in_specs=[pl.BlockSpec(memory_space=pltpu.SMEM)]
@@ -357,7 +360,7 @@
         compiler_params=limit(4),
         name="merge",
     )(middle.reshape(1), inner, outer, across, beside, onward, past)
-    return memory, other
+    return memory, other, settled
 
 
 def shards(
@@ -415,8 +418,10 @@
         return lax.ppermute(tail, ("mem", "rep"), needed)
 
     summed = line_sum if mems == 4 else scattered_sum
-    memory, hidden_halo = summed(stored, decoded, here, meanwhile)
-    weights = [in_hbm(w) for w in (key_weight, value_weight, other_key, other_value)]
+    memory, hidden_halo, others = summed(
+        stored, decoded, here, meanwhile, (other_key, other_value)
+    )
+    weights = [in_hbm(w) for w in (key_weight, value_weight, *others)]
 
     where = jnp.stack([lax.axis_index("rep"), lax.axis_index("tp")]).astype(I32)
     extended = tokens + RIM
@@ -437,6 +442,7 @@
         return lax.ppermute(rim, ("mem", "tp", "rep"), pairs)
 
     rim = memory[:, tokens - LANES :]
+    rims = [next_rim(rim, s) for s in range(tps)]
     others = tps - 1
     field = jax.ShapeDtypeStruct((2, extended, half), F32)
     *begun, rest = pl.pallas_call(
@@ -451,8 +457,7 @@
         ],
         compiler_params=limit(12),
         name="project_own",
-    )(where, next_rim(rim, 0), memory, *weights)
-    rim = after(rim, *begun)
+    )(where, rims[0], memory, *weights)
     values, stats = pl.pallas_call(
         functools.partial(project_kernel, tuple(range(1, tps)), tps),
         in_specs=[smem] + [resident] * (2 * others + 5),
@@ -467,7 +472,7 @@
         name="project_others",
     )(
         where,
-        *[next_rim(rim, s) for s in range(1, tps)],
+        *rims[1:],
         *bodies[1:],
         rest,
         *begun,

time: 70.2 us -> 68.7 us (0.979)
  waiting for transfers between devices: 18.4 us -> 23.3 us
  starting transfers between devices: 25.2 us -> 21.2 us
  Pallas kernels: 24.5 us -> 23.1 us
  other arithmetic: 1.17 us -> 0.21 us
    ppermute x5, waiting for transfers between devices: 10.1 us -> 18.3 us  [send(): return lax.ppermute(x, 'mem', pairs)]
    ppermute x5, starting transfers between devices: 11.4 us -> 8.05 us  [send(): return lax.ppermute(x, 'mem', pairs)]
    ppermute x2, waiting for transfers between devices: 2.62 us -> 0.01 us  [next_rim(): return lax.ppermute(rim, ('mem', 'tp', 'rep'), pairs)]
    ppermute x2, starting transfers between devices: 4.21 us -> 2.6 us  [next_rim(): return lax.ppermute(rim, ('mem', 'tp', 'rep'), pairs)]
    pallas_call x1, Pallas kernels: 6.94 us -> 5.6 us  [shards(): pl.pallas_call(functools.partial(project_kernel, (0,), tps), in_specs=[sm...]
    add x1, other arithmetic: 1.05 us -> 0.09 us  [line_sum(): onward = farthest + inward]
    ppermute x1, starting transfers between devices: 0.6 us -> 1.33 us  [shards(): lax.ppermute(stats, 'tp', [(i, (i + s) % tps) for i in range(tps)])]
    ppermute x1, waiting for transfers between devices: 3.16 us -> 2.43 us  [shards(): lax.ppermute(stats, 'tp', [(i, (i + s) % tps) for i in range(tps)])]
  transfers between devices with their start and end apart: 15 -> 15, of which waited for: 5 -> 4; matrix products, arithmetic and copies ran while one was open for 2% -> 0% of each run, Pallas kernels for 23% -> 19%
where the time goes in v7:
time: 68.7 us; the launch traced here: 68.4 us
  waiting for transfers between devices  23.3 us (34%)
  Pallas kernels  23.1 us (34%)
  starting transfers between devices  21.2 us (31%)
    ppermute x5, waiting for transfers between devices, send(): return lax.ppermute(x, 'mem', pairs)  18.3 us
    ppermute x5, starting transfers between devices, send(): return lax.ppermute(x, 'mem', pairs)  8.05 us
    ppermute x3, starting transfers between devices, line_sum(): lax.ppermute(stored, 'mem', [(i, i ^ x) for i in range(4)])  5.68 us
    pallas_call x1, Pallas kernels, shards(): pl.pallas_call(functools.partial(project_kernel, (0,), tps), in_specs=[sm...  5.6 us
    pallas_call x3, Pallas kernels, pick(): pl.pallas_call(functools.partial(pick_kernel, 4, targets), in_specs=[pl.B...  4.99 us
    pallas_call x1, Pallas kernels, shards(): pl.pallas_call(functools.partial(project_kernel, tuple(range(1, tps)), tp...  4.26 us
    pallas_call x1, Pallas kernels, shards(): pl.pallas_call(functools.partial(finish_kernel, tps, step), in_specs=[sme...  3.96 us
    pallas_call x1, Pallas kernels, shards(): pl.pallas_call(decode_kernel, in_specs=[anywhere] * 2, out_shape=jax.Shap...  2.74 us
  transfers between devices with their start and end apart: 15, of which 4 were waited for; matrix products, arithmetic and copies ran while one was open for 0% of the time, Pallas kernels for 19%

profile of v7, /device:TPU:0, one launch (start us, length us, event | category | flops | bytes accessed | tf_op | source)
XLA Modules:
  0.0 68.4 jit_solution(5842715823115012526)
XLA Ops:
  0.0 0.5 collective-permute-start.3
  0.5 0.1 collective-permute-start.4
  0.5 1.3 %place_rows.1.refs_0_ = s32[8,256]{1,0:T(8,128)S(1)} custom-call(s32[8,256]{1,0:T(8,128)} %bitcast.16, s32[32,128]{1,0:T(8,128)} %bitcast.15), custom_call_target="tpu_custom_call" | custom-call | tf_op jit(solution)/shard_map/place_rows/pallas_call | solution.py:385
  1.9 3.1 %collective-permute-start = (s32[8,256]{1,0:T(8,128)S(1)}, s32[8,256]{1,0:T(8,128)S(1)}, u32[]{:S(2)}, u32[]{:S(2)}) collective-permute-start(s32[8,256]{1,0:T(8,128)S(1)} %place_rows.1.refs_0_), channel_id=1, source_target_pairs={{0,4},{4,0},{8,12},{12,8},{1,5},{5,1},{9,13},{13,9},{2,6},{6,2},{1... | collective-permute-start | bytes 24584 | tf_op jit(solution)/shard_map/ppermute | solution.py:322
  4.9 2.6 %collective-permute-start.1 = (s32[8,256]{1,0:T(8,128)S(1)}, s32[8,256]{1,0:T(8,128)S(1)}, u32[]{:S(2)}, u32[]{:S(2)}) collective-permute-start(s32[8,256]{1,0:T(8,128)S(1)} %place_rows.1.refs_0_), channel_id=1, source_target_pairs={{0,8},{4,12},{8,0},{12,4},{1,9},{5,13},{9,1},{13,5},{2,10},{6,14},... | collective-permute-start | bytes 24584 | tf_op jit(solution)/shard_map/ppermute | solution.py:322
  7.5 0.0 collective-permute-start.2
  7.5 2.7 %decode_tables.1.refs_4_ = bf16[8,80,1024]{2,1,0:T(8,128)(2,1)S(1)} custom-call(bf16[8,80,1024]{2,1,0:T(8,128)(2,1)} %bitcast.13, bf16[5,8,1024]{2,1,0:T(8,128)(2,1)} %bitcast.14), custom_call_target="tpu_custom_call" | custom-call | tf_op jit(solution)/shard_map/decode_tables/pallas_call | solution.py:399
  10.3 0.1 stack.35.scalars_ref
  10.4 0.0 collective-permute-done.refs_1_
  10.4 0.0 collective-permute-done.1.refs_2_
  10.4 2.6 %collective-permute-done.2.refs_3_ = s32[8,256]{1,0:T(8,128)S(1)} collective-permute-done((s32[8,256]{1,0:T(8,128)S(1)}, s32[8,256]{1,0:T(8,128)S(1)}, u32[]{:S(2)}, u32[]{:S(2)}) %collective-permute-start.2) | collective-permute-done | bytes 8224 | tf_op jit(solution)/shard_map/ppermute | solution.py:322
  13.0 0.0 collective-permute-done.3.refs_4_
  13.0 0.0 collective-permute-done.4.refs_5_
  13.0 1.4 %pick_rows.5 = bf16[640,256]{1,0:T(8,128)(2,1)S(1)} custom-call(s32[5]{0:T(128)S(1)} %stack.35.scalars_ref, s32[8,256]{1,0:T(8,128)S(1)} %place_rows.1.refs_0_, s32[8,256]{1,0:T(8,128)S(1)} %collective-permute-done.refs_1_, s32[8,256]{1,0:T(8,128)S(1)} %collective-permute-done.1.refs_2_, s32[8,256]{1,0:T(8,128)S(1)} %collective-permute-done.2.refs_3_, ...), custom_call_target="tpu_custom_call" | custom-call | tf_op jit(solution)/shard_map/pick_rows/pallas_call | solution.py:331
  14.4 1.9 %collective-permute-start.7 = (bf16[640,256]{1,0:T(8,128)(2,1)S(1)}, bf16[640,256]{1,0:T(8,128)(2,1)S(1)}, u32[]{:S(2)}, u32[]{:S(2)}) collective-permute-start(bf16[640,256]{1,0:T(8,128)(2,1)S(1)} %pick_rows.5), channel_id=1, source_target_pairs={{0,4},{12,8},{1,5},{13,9},{2,6},{14,10},{3,7},{15,11},{16,20},{28,... | collective-permute-start | bytes 983048 | tf_op jit(solution)/shard_map/ppermute | solution.py:342
  16.3 2.2 %pick_rows.3 = (bf16[640,256]{1,0:T(8,128)(2,1)S(1)}, bf16[640,256]{1,0:T(8,128)(2,1)S(1)}) custom-call(s32[5]{0:T(128)S(1)} %stack.35.scalars_ref, s32[8,256]{1,0:T(8,128)S(1)} %place_rows.1.refs_0_, s32[8,256]{1,0:T(8,128)S(1)} %collective-permute-done.refs_1_, s32[8,256]{1,0:T(8,128)S(1)} %collective-permute-done.1.refs_2_, ...), custom_call_target="tpu_custom_call" | custom-call | tf_op jit(solution)/shard_map/pick_rows/pallas_call | solution.py:331
  18.5 1.4 %pick_rows.4 = bf16[640,256]{1,0:T(8,128)(2,1)S(1)} custom-call(s32[5]{0:T(128)S(1)} %stack.35.scalars_ref, s32[8,256]{1,0:T(8,128)S(1)} %place_rows.1.refs_0_, s32[8,256]{1,0:T(8,128)S(1)} %collective-permute-done.refs_1_, s32[8,256]{1,0:T(8,128)S(1)} %collective-permute-done.1.refs_2_, s32[8,256]{1,0:T(8,128)S(1)} %collective-permute-done.2.refs_3_, ...), custom_call_target="tpu_custom_call" | custom-call | tf_op jit(solution)/shard_map/pick_rows/pallas_call | solution.py:331
  19.9 0.0 copy-start
  19.9 0.8 %collective-permute-start.5 = (bf16[640,256]{1,0:T(8,128)(2,1)S(1)}, bf16[640,256]{1,0:T(8,128)(2,1)S(1)}, u32[]{:S(2)}, u32[]{:S(2)}) collective-permute-start(bf16[640,256]{1,0:T(8,128)(2,1)S(1)} %pick_rows.4), channel_id=1, source_target_pairs={{4,8},{8,4},{5,9},{9,5},{6,10},{10,6},{7,11},{11,7},{20,24},{24,20... | collective-permute-start | bytes 983048 | tf_op jit(solution)/shard_map/ppermute | solution.py:342
  20.7 4.0 %collective-permute-start.9 = (bf16[640,256]{1,0:T(8,128)(2,1)S(1)}, bf16[640,256]{1,0:T(8,128)(2,1)S(1)}, u32[]{:S(2)}, u32[]{:S(2)}) collective-permute-start(bf16[640,256]{1,0:T(8,128)(2,1)S(1)} %pick_rows.4), channel_id=1, source_target_pairs={{0,8},{12,4},{1,9},{13,5},{2,10},{14,6},{3,11},{15,7},{16,24},{28,... | collective-permute-start | bytes 983048 | tf_op jit(solution)/shard_map/ppermute | solution.py:342
  24.8 0.1 collective-permute-start.6
  24.8 0.0 collective-permute-done.7
  24.8 0.1 add.12
  24.9 1.3 %collective-permute-start.8 = (bf16[640,256]{1,0:T(8,128)(2,1)S(1)}, bf16[640,256]{1,0:T(8,128)(2,1)S(1)}, u32[]{:S(2)}, u32[]{:S(2)}) collective-permute-start(bf16[640,256]{1,0:T(8,128)(2,1)S(1)} %add.12), channel_id=1, source_target_pairs={{4,12},{8,0},{5,13},{9,1},{6,14},{10,2},{7,15},{11,3},{20,28},{24,... | collective-permute-start | bytes 983048 | tf_op jit(solution)/shard_map/ppermute | solution.py:342
  26.2 12.5 %collective-permute-done.6.refs_1_ = bf16[640,256]{1,0:T(8,128)(2,1)S(1)} collective-permute-done((bf16[640,256]{1,0:T(8,128)(2,1)S(1)}, bf16[640,256]{1,0:T(8,128)(2,1)S(1)}, u32[]{:S(2)}, u32[]{:S(2)}) %collective-permute-start.6) | collective-permute-done | bytes 327712 | tf_op jit(solution)/shard_map/ppermute | solution.py:342
  38.7 0.0 collective-permute-done.5.refs_0_
  38.7 0.0 collective-permute-done.9.refs_3_
  38.7 5.8 %collective-permute-done.8.refs_2_ = bf16[640,256]{1,0:T(8,128)(2,1)S(1)} collective-permute-done((bf16[640,256]{1,0:T(8,128)(2,1)S(1)}, bf16[640,256]{1,0:T(8,128)(2,1)S(1)}, u32[]{:S(2)}, u32[]{:S(2)}) %collective-permute-start.8) | collective-permute-done | bytes 327712 | tf_op jit(solution)/shard_map/ppermute | solution.py:342
  44.5 0.2 merge.1.refs_1_
  44.8 1.6 %collective-permute-start.11 = (bf16[640,256]{1,0:T(8,128)(2,1)S(1)}, bf16[640,256]{1,0:T(8,128)(2,1)S(1)}, u32[]{:S(2)}, u32[]{:S(2)}) collective-permute-start(bf16[640,256]{1,0:T(8,128)(2,1)S(1)} %merge.1.refs_1_), channel_id=1, source_target_pairs={{0,2},{2,0},{1,3},{3,1},{4,6},{6,4},{5,7},{7,5},{8,10},{10,8},{9,1... | collective-permute-start | bytes 983048 | tf_op jit(solution)/shard_map/ppermute | solution.py:429
  46.3 1.3 %collective-permute-start.12 = (bf16[640,128]{1,0:T(8,128)(2,1)S(1)}, bf16[640,128]{1,0:T(8,128)(2,1)S(1)}, u32[]{:S(2)}, u32[]{:S(2)}) collective-permute-start(bf16[640,128]{1,0:T(8,128)(2,1)S(1)} %slice.8), channel_id=1, source_target_pairs={{0,1},{2,3},{4,5},{6,7},{8,9},{10,11},{12,13},{14,15},{16,17},{18,... | collective-permute-start | bytes 491528 | tf_op jit(solution)/shard_map/ppermute | solution.py:442
  47.7 1.3 %collective-permute-start.10 = (bf16[640,128]{1,0:T(8,128)(2,1)S(1)}, bf16[640,128]{1,0:T(8,128)(2,1)S(1)}, u32[]{:S(2)}, u32[]{:S(2)}) collective-permute-start(bf16[640,128]{1,0:T(8,128)(2,1)S(1)} %slice.8), channel_id=1, source_target_pairs={{0,3},{2,1},{4,7},{6,5},{8,11},{10,9},{12,15},{14,13},{16,19},{18,... | collective-permute-start | bytes 491528 | tf_op jit(solution)/shard_map/ppermute | solution.py:442
  49.0 0.0 copy-done
  49.0 1.5 %collective-permute-start.13 = (bf16[16,2304]{1,0:T(8,128)(2,1)S(1)}, bf16[16,2304]{1,0:T(8,128)(2,1)S(1)}, u32[]{:S(2)}, u32[]{:S(2)}) collective-permute-start(bf16[16,2304]{1,0:T(8,128)(2,1)S(1)} %slice.7), channel_id=1, source_target_pairs={{0,1},{4,5},{8,9},{12,13},{2,3},{6,7},{10,11},{14,15},{16,17},{20,... | collective-permute-start | bytes 221192 | tf_op jit(solution)/shard_map/ppermute | solution.py:418
  50.5 0.1 pad_add_fusion.where_ref
  50.6 0.0 collective-permute-done.12.refs_0_
  50.6 5.6 %project_own.1 = (f32[2,272,1152]{2,1,0:T(8,128)S(1)}, f32[2,272,1152]{2,1,0:T(8,128)S(1)}, bf16[2,2,640,1152]{3,2,1,0:T(8,128)(2,1)S(1)}) custom-call(s32[2]{0:T(128)S(1)} %pad_add_fusion.where_ref, bf16[640,128]{1,0:T(8,128)(2,1)S(1)} %collective-permute-done.12.refs_0_, bf16[640,256]{1,0:T(8,128)(2,1)S(1)} %merge.1.refs_1_, bf16[1280,1152]{1,0:T(8,128)(2,1)} %refs_2_.1, ...), custom_call_target="tpu_custom_call" | custom-call | tf_op jit(solution)/shard_map/project_own/pallas_call | solution.py:448
  56.2 0.0 collective-permute-done.13.refs_5_
  56.2 0.0 collective-permute-done.10.refs_0_
  56.2 0.0 collective-permute-done.11.refs_1_
  56.2 0.0 copy-start.1
  56.2 4.3 %project_others.1 = (f32[2,272,1152]{2,1,0:T(8,128)}, f32[8,272]{1,0:T(8,128)S(1)}) custom-call(s32[2]{0:T(128)S(1)} %pad_add_fusion.where_ref, bf16[640,128]{1,0:T(8,128)(2,1)S(1)} %collective-permute-done.10.refs_0_, bf16[640,256]{1,0:T(8,128)(2,1)S(1)} %collective-permute-done.11.refs_1_, bf16[2,2,640,1152]{3,2,1,0:T(8,128)(2,1)S(1)} %get-tuple-element.27.refs_2_, ...), custom_call_target="tpu_custom_call" | custom-call | tf_op jit(solution)/shard_map/project_others/pallas_call | solution.py:461
  60.5 1.3 %collective-permute-start.14 = (f32[8,272]{1,0:T(8,128)S(1)}, f32[8,272]{1,0:T(8,128)S(1)}, u32[]{:S(2)}, u32[]{:S(2)}) collective-permute-start(f32[8,272]{1,0:T(8,128)S(1)} %get-tuple-element.31.refs_0_), channel_id=1, source_target_pairs={{0,2},{2,0},{1,3},{3,1},{4,6},{6,4},{5,7},{7,5},{8,10},{10,8},{9,1... | collective-permute-start | bytes 26120 | tf_op jit(solution)/shard_map/ppermute | solution.py:484
  61.8 2.4 %collective-permute-done.14.refs_1_ = f32[8,272]{1,0:T(8,128)S(1)} collective-permute-done((f32[8,272]{1,0:T(8,128)S(1)}, f32[8,272]{1,0:T(8,128)S(1)}, u32[]{:S(2)}, u32[]{:S(2)}) %collective-permute-start.14) | collective-permute-done | bytes 8736 | tf_op jit(solution)/shard_map/ppermute | solution.py:484
  64.2 0.0 copy-done.1
  64.2 4.0 %finish.1 = bf16[256,2304]{1,0:T(8,128)(2,1)} custom-call(s32[1]{0:T(128)} %bitcast.keep_ref, f32[8,272]{1,0:T(8,128)S(1)} %get-tuple-element.31.refs_0_, f32[8,272]{1,0:T(8,128)S(1)} %collective-permute-done.14.refs_1_, f32[2,272,1152]{2,1,0:T(8,128)} %get-tuple-element.32.refs_2_, bf16[256,2304]{1,0:T(8,128)(2,1)S(1)} %copy-done, f32[4,2304]{1,0:T(4,128)S(1)} %copy-done.1), custom_call_target="tpu_custom_call" | custom-call | tf_op jit(solution)/shard_map/finish/pallas_call | solution.py:490
  (3 shorter events, 0.1 us)
Async XLA Ops:
  0.0 13.0 %collective-permute-start.3 = (bf16[1280,1152]{1,0:T(8,128)(2,1)}, bf16[1280,1152]{1,0:T(8,128)(2,1)}, u32[]{:S(2)}, u32[]{:S(2)}) collective-permute-start(bf16[1280,1152]{1,0:T(8,128)(2,1)} %refs_2_.1), channel_id=1, source_target_pairs={{0,1},{1,0},{2,3},{3,2},{4,5},{5,4},{6,7},{7,6},{8,9},{9,8},{10,11... | collective-permute-start | bytes 8847368 | tf_op jit(solution)/shard_map/ppermute | solution.py:412
  0.5 12.5 %collective-permute-start.4 = (bf16[1280,1152]{1,0:T(8,128)(2,1)}, bf16[1280,1152]{1,0:T(8,128)(2,1)}, u32[]{:S(2)}, u32[]{:S(2)}) collective-permute-start(bf16[1280,1152]{1,0:T(8,128)(2,1)} %refs_3_.2), channel_id=1, source_target_pairs={{0,1},{1,0},{2,3},{3,2},{4,5},{5,4},{6,7},{7,6},{8,9},{9,8},{10,11... | collective-permute-start | bytes 8847368 | tf_op jit(solution)/shard_map/ppermute | solution.py:413
  1.9 8.5 %collective-permute-start = (s32[8,256]{1,0:T(8,128)S(1)}, s32[8,256]{1,0:T(8,128)S(1)}, u32[]{:S(2)}, u32[]{:S(2)}) collective-permute-start(s32[8,256]{1,0:T(8,128)S(1)} %place_rows.1.refs_0_), channel_id=1, source_target_pairs={{0,4},{4,0},{8,12},{12,8},{1,5},{5,1},{9,13},{13,9},{2,6},{6,2},{1... | collective-permute-start | bytes 24584 | tf_op jit(solution)/shard_map/ppermute | solution.py:322
  4.9 5.4 %collective-permute-start.1 = (s32[8,256]{1,0:T(8,128)S(1)}, s32[8,256]{1,0:T(8,128)S(1)}, u32[]{:S(2)}, u32[]{:S(2)}) collective-permute-start(s32[8,256]{1,0:T(8,128)S(1)} %place_rows.1.refs_0_), channel_id=1, source_target_pairs={{0,8},{4,12},{8,0},{12,4},{1,9},{5,13},{9,1},{13,5},{2,10},{6,14},... | collective-permute-start | bytes 24584 | tf_op jit(solution)/shard_map/ppermute | solution.py:322
  7.5 5.4 %collective-permute-start.2 = (s32[8,256]{1,0:T(8,128)S(1)}, s32[8,256]{1,0:T(8,128)S(1)}, u32[]{:S(2)}, u32[]{:S(2)}) collective-permute-start(s32[8,256]{1,0:T(8,128)S(1)} %place_rows.1.refs_0_), channel_id=1, source_target_pairs={{0,12},{4,8},{8,4},{12,0},{1,13},{5,9},{9,5},{13,1},{2,14},{6,10},... | collective-permute-start | bytes 24584 | tf_op jit(solution)/shard_map/ppermute | solution.py:322
  14.4 10.4 %collective-permute-start.7 = (bf16[640,256]{1,0:T(8,128)(2,1)S(1)}, bf16[640,256]{1,0:T(8,128)(2,1)S(1)}, u32[]{:S(2)}, u32[]{:S(2)}) collective-permute-start(bf16[640,256]{1,0:T(8,128)(2,1)S(1)} %pick_rows.5), channel_id=1, source_target_pairs={{0,4},{12,8},{1,5},{13,9},{2,6},{14,10},{3,7},{15,11},{16,20},{28,... | collective-permute-start | bytes 983048 | tf_op jit(solution)/shard_map/ppermute | solution.py:342
  19.9 29.1 %copy-start = (bf16[256,2304]{1,0:T(8,128)(2,1)S(1)}, bf16[256,2304]{1,0:T(8,128)(2,1)}, u32[]{:S(2)}) copy-start(bf16[256,2304]{1,0:T(8,128)(2,1)} %refs_3_.3) | copy-start | bytes 3538948
  19.9 18.8 %collective-permute-start.5 = (bf16[640,256]{1,0:T(8,128)(2,1)S(1)}, bf16[640,256]{1,0:T(8,128)(2,1)S(1)}, u32[]{:S(2)}, u32[]{:S(2)}) collective-permute-start(bf16[640,256]{1,0:T(8,128)(2,1)S(1)} %pick_rows.4), channel_id=1, source_target_pairs={{4,8},{8,4},{5,9},{9,5},{6,10},{10,6},{7,11},{11,7},{20,24},{24,20... | collective-permute-start | bytes 983048 | tf_op jit(solution)/shard_map/ppermute | solution.py:342
  20.7 18.0 %collective-permute-start.9 = (bf16[640,256]{1,0:T(8,128)(2,1)S(1)}, bf16[640,256]{1,0:T(8,128)(2,1)S(1)}, u32[]{:S(2)}, u32[]{:S(2)}) collective-permute-start(bf16[640,256]{1,0:T(8,128)(2,1)S(1)} %pick_rows.4), channel_id=1, source_target_pairs={{0,8},{12,4},{1,9},{13,5},{2,10},{14,6},{3,11},{15,7},{16,24},{28,... | collective-permute-start | bytes 983048 | tf_op jit(solution)/shard_map/ppermute | solution.py:342
  24.8 14.0 %collective-permute-start.6 = (bf16[640,256]{1,0:T(8,128)(2,1)S(1)}, bf16[640,256]{1,0:T(8,128)(2,1)S(1)}, u32[]{:S(2)}, u32[]{:S(2)}) collective-permute-start(bf16[640,256]{1,0:T(8,128)(2,1)S(1)} %broadcast_select_fusion), channel_id=1, source_target_pairs={{0,4},{4,0},{8,12},{12,8},{1,5},{5,1},{9,13},{13,9},{2,6},{6,2},{1... | collective-permute-start | bytes 983048 | tf_op jit(solution)/shard_map/ppermute | solution.py:342
  24.9 19.6 %collective-permute-start.8 = (bf16[640,256]{1,0:T(8,128)(2,1)S(1)}, bf16[640,256]{1,0:T(8,128)(2,1)S(1)}, u32[]{:S(2)}, u32[]{:S(2)}) collective-permute-start(bf16[640,256]{1,0:T(8,128)(2,1)S(1)} %add.12), channel_id=1, source_target_pairs={{4,12},{8,0},{5,13},{9,1},{6,14},{10,2},{7,15},{11,3},{20,28},{24,... | collective-permute-start | bytes 983048 | tf_op jit(solution)/shard_map/ppermute | solution.py:342
  44.8 11.4 %collective-permute-start.11 = (bf16[640,256]{1,0:T(8,128)(2,1)S(1)}, bf16[640,256]{1,0:T(8,128)(2,1)S(1)}, u32[]{:S(2)}, u32[]{:S(2)}) collective-permute-start(bf16[640,256]{1,0:T(8,128)(2,1)S(1)} %merge.1.refs_1_), channel_id=1, source_target_pairs={{0,2},{2,0},{1,3},{3,1},{4,6},{6,4},{5,7},{7,5},{8,10},{10,8},{9,1... | collective-permute-start | bytes 983048 | tf_op jit(solution)/shard_map/ppermute | solution.py:429
  46.3 4.2 %collective-permute-start.12 = (bf16[640,128]{1,0:T(8,128)(2,1)S(1)}, bf16[640,128]{1,0:T(8,128)(2,1)S(1)}, u32[]{:S(2)}, u32[]{:S(2)}) collective-permute-start(bf16[640,128]{1,0:T(8,128)(2,1)S(1)} %slice.8), channel_id=1, source_target_pairs={{0,1},{2,3},{4,5},{6,7},{8,9},{10,11},{12,13},{14,15},{16,17},{18,... | collective-permute-start | bytes 491528 | tf_op jit(solution)/shard_map/ppermute | solution.py:442
  47.7 8.5 %collective-permute-start.10 = (bf16[640,128]{1,0:T(8,128)(2,1)S(1)}, bf16[640,128]{1,0:T(8,128)(2,1)S(1)}, u32[]{:S(2)}, u32[]{:S(2)}) collective-permute-start(bf16[640,128]{1,0:T(8,128)(2,1)S(1)} %slice.8), channel_id=1, source_target_pairs={{0,3},{2,1},{4,7},{6,5},{8,11},{10,9},{12,15},{14,13},{16,19},{18,... | collective-permute-start | bytes 491528 | tf_op jit(solution)/shard_map/ppermute | solution.py:442
  49.0 7.2 %collective-permute-start.13 = (bf16[16,2304]{1,0:T(8,128)(2,1)S(1)}, bf16[16,2304]{1,0:T(8,128)(2,1)S(1)}, u32[]{:S(2)}, u32[]{:S(2)}) collective-permute-start(bf16[16,2304]{1,0:T(8,128)(2,1)S(1)} %slice.7), channel_id=1, source_target_pairs={{0,1},{4,5},{8,9},{12,13},{2,3},{6,7},{10,11},{14,15},{16,17},{20,... | collective-permute-start | bytes 221192 | tf_op jit(solution)/shard_map/ppermute | solution.py:418
  56.2 8.0 %copy-start.1 = (f32[4,2304]{1,0:T(4,128)S(1)}, f32[4,2304]{1,0:T(4,128)}, u32[]{:S(2)}) copy-start(f32[4,2304]{1,0:T(4,128)} %refs_4_.1) | copy-start | bytes 110596
  60.5 3.8 %collective-permute-start.14 = (f32[8,272]{1,0:T(8,128)S(1)}, f32[8,272]{1,0:T(8,128)S(1)}, u32[]{:S(2)}, u32[]{:S(2)}) collective-permute-start(f32[8,272]{1,0:T(8,128)S(1)} %get-tuple-element.31.refs_0_), channel_id=1, source_target_pairs={{0,2},{2,0},{1,3},{3,1},{4,6},{6,4},{5,7},{7,5},{8,10},{10,8},{9,1... | collective-permute-start | bytes 26120 | tf_op jit(solution)/shard_map/ppermute | solution.py:484

commit v8 on v7

--- a/solution.py
+++ b/solution.py
@@ -108,31 +108,16 @@
     return dot(table_ref[head], hot).astype(BF16)
 
 
-def pick_all_kernel(base_ref, ids_ref, table_ref, out_ref):
+def pick_kernel(base_ref, ids_ref, table_ref, out_ref):
     heads, width, _ = table_ref.shape
     local = ids_ref[...] - base_ref[0]
     for head in range(heads):
         out_ref[head * width : (head + 1) * width, :] = picked(local, table_ref, head)
 
 
-def pick_kernel(count, targets, scalars_ref, *refs):
-    pieces = refs[:count]
-    table_ref = refs[count]
-    outs = refs[count + 1 : -1]
-    stack = refs[-1]
-    heads, width, _ = table_ref.shape
-    for k in range(count):
-        stack[k] = pieces[k][...]
-    for n, target in enumerate(targets):
-        local = stack[scalars_ref[1 + target]] - scalars_ref[0]
-        for head in range(heads):
-            outs[n][head * width : (head + 1) * width, :] = picked(local, table_ref, head)
-
-
-def merge_kernel(middle_ref, inner_ref, outer_ref, *refs):
-    received = refs[:-1]
-    total = jnp.where(middle_ref[0] == 1, inner_ref[...].astype(F32), outer_ref[...].astype(F32))
-    for other in received:
+def merge_kernel(*refs):
+    total = refs[0][...].astype(F32)
+    for other in refs[1:-1]:
         total = total + other[...].astype(F32)
     refs[-1][...] = total.astype(BF16)
 
@@ -299,7 +284,7 @@
     tokens = stored.shape[1]
     asked = lax.all_gather(stored, "mem", axis=0)
     partial = pl.pallas_call(
-        pick_all_kernel,
+        pick_kernel,
         grid=(mems,),
         in_specs=[
             pl.BlockSpec(memory_space=pltpu.SMEM),
@@ -318,48 +303,46 @@
 def line_sum(stored, decoded, here, meanwhile, settled):
     heads, width, rows = decoded.shape
     tokens = stored.shape[1]
-    asked = [stored] + [
-        lax.ppermute(stored, "mem", [(i, i ^ x) for i in range(4)]) for x in range(1, 4)
-    ]
-    asked, settled = lax.optimization_barrier((asked, settled))
-    right = here >= 2
-    order = [here ^ jnp.where(right, j, 3 - j) for j in range(4)]
-    scalars = jnp.stack([here * rows] + order).astype(I32)
+    base = (here * rows).astype(I32).reshape(1)
     block = jax.ShapeDtypeStruct((heads * width, tokens), BF16)
 
-    def pick(*targets):
+    def ask(ids, x):
+        return lax.ppermute(ids, "mem", [(i, i ^ x) for i in range(4)])
+
+    def pick(ids):
         return pl.pallas_call(
-            functools.partial(pick_kernel, 4, targets),
+            pick_kernel,
             in_specs=[pl.BlockSpec(memory_space=pltpu.SMEM)]
-            + [pl.BlockSpec(memory_space=pltpu.VMEM)] * 5,
-            out_shape=(block,) * len(targets),
-            scratch_shapes=[pltpu.VMEM((4, heads, tokens), I32)],
+            + [pl.BlockSpec(memory_space=pltpu.VMEM)] * 2,
+            out_shape=block,
             compiler_params=limit(8),
             name="pick_rows",
-        )(scalars, *asked, decoded)
+        )(base, ids, decoded)
 
     def send(x, *pairs):
         return lax.ppermute(x, "mem", pairs)
 
-    middle = ((here == 1) | (here == 2)).astype(I32)
-    (farthest,) = pick(0)
-    inward = send(farthest, (0, 1), (3, 2))
-    (far,) = pick(1)
-    across = send(far, (1, 2), (2, 1))
-    inner, outer = pick(2, 3)
-    beside = send(jnp.where(middle == 1, outer, inner), (0, 1), (1, 0), (2, 3), (3, 2))
-    past = send(far, (0, 2), (3, 1))
-    onward = farthest + inward
+    rows_3 = pick(ask(stored, 3))
+    inward = send(rows_3, (0, 1), (3, 2))
+    across = send(rows_3, (1, 2), (2, 1))
+    own = pick(after(stored, rows_3))
+    stored, settled = lax.optimization_barrier((after(stored, own), settled))
+    asked = ask(stored, 2), ask(stored, 1)
+    rows_2 = pick(asked[0])
+    past = send(rows_2, (0, 2), (3, 1))
+    rows_1 = pick(asked[1])
+    onward = after(rows_2, rows_1, across) + inward
     other = meanwhile(onward)
     onward = send(onward, (1, 3), (2, 0))
+    beside = send(after(rows_1, inward), (0, 1), (1, 0), (2, 3), (3, 2))
+    own, other = lax.optimization_barrier((own + past, other))
     memory = pl.pallas_call(
         merge_kernel,
-        in_specs=[pl.BlockSpec(memory_space=pltpu.SMEM)]
-        + [pl.BlockSpec(memory_space=pltpu.VMEM)] * 6,
+        in_specs=[pl.BlockSpec(memory_space=pltpu.VMEM)] * 4,
         out_shape=block,
         compiler_params=limit(4),
         name="merge",
-    )(middle.reshape(1), inner, outer, across, beside, onward, past)
+    )(own, across, beside, onward)
     return memory, other, settled
 
 

time: 68.7 us -> 68.6 us (level)
  starting transfers between devices: 21.2 us -> 29.1 us
  waiting for transfers between devices: 23.3 us -> 17 us
  Pallas kernels: 23.1 us -> 21.5 us
    ppermute x5, waiting for transfers between devices: 18.3 us -> 10.2 us  [send(): return lax.ppermute(x, 'mem', pairs)]
    ppermute x5, starting transfers between devices: 8.05 us -> 14.6 us  [send(): return lax.ppermute(x, 'mem', pairs)]
    ppermute x3, starting transfers between devices: 5.68 us -> 7.77 us  [ask(): return lax.ppermute(ids, 'mem', [(i, i ^ x) for i in range(4)])]
    pallas_call x4 -> x5, Pallas kernels: 5.23 us -> 3.62 us  [the longest x4 3.46 us: pick(): pl.pallas_call(pick_kernel, in_specs=[pl.BlockSpec(memory_space=pltpu.SME...]
    ppermute x1, waiting for transfers between devices: 0.01 us -> 0.79 us  [meanwhile(): return lax.ppermute(tail, ('mem', 'rep'), needed)]
    ppermute x1, starting transfers between devices: 1.33 us -> 0.6 us  [shards(): lax.ppermute(stats, 'tp', [(i, (i + s) % tps) for i in range(tps)])]
    ppermute x1, waiting for transfers between devices: 2.43 us -> 3.16 us  [shards(): lax.ppermute(stats, 'tp', [(i, (i + s) % tps) for i in range(tps)])]
  transfers between devices with their start and end apart: 15 -> 15, of which waited for: 4 -> 5; matrix products, arithmetic and copies ran while one was open for 0% -> 0% of each run, Pallas kernels for 19% -> 19%
where the time goes in v8:
time: 68.6 us; the launch traced here: 68.2 us
  starting transfers between devices  29.1 us (42%)
  Pallas kernels  21.5 us (31%)
  waiting for transfers between devices  17 us (25%)
    ppermute x5, starting transfers between devices, send(): return lax.ppermute(x, 'mem', pairs)  14.6 us
    ppermute x5, waiting for transfers between devices, send(): return lax.ppermute(x, 'mem', pairs)  10.2 us
    ppermute x3, starting transfers between devices, ask(): return lax.ppermute(ids, 'mem', [(i, i ^ x) for i in range(4)])  7.77 us
    pallas_call x1, Pallas kernels, shards(): pl.pallas_call(functools.partial(project_kernel, (0,), tps), in_specs=[sm...  5.6 us
    pallas_call x1, Pallas kernels, shards(): pl.pallas_call(functools.partial(project_kernel, tuple(range(1, tps)), tp...  4.24 us
    pallas_call x1, Pallas kernels, shards(): pl.pallas_call(functools.partial(finish_kernel, tps, step), in_specs=[sme...  3.96 us
    pallas_call x4, Pallas kernels, pick(): pl.pallas_call(pick_kernel, in_specs=[pl.BlockSpec(memory_space=pltpu.SME...  3.46 us
    ppermute x1, waiting for transfers between devices, shards(): lax.ppermute(stats, 'tp', [(i, (i + s) % tps) for i in range(tps)])  3.16 us
  transfers between devices with their start and end apart: 15, of which 5 were waited for; matrix products, arithmetic and copies ran while one was open for 0% of the time, Pallas kernels for 19%

profile of v8, /device:TPU:0, one launch (start us, length us, event | category | flops | bytes accessed | tf_op | source)
XLA Modules:
  0.0 68.2 jit_solution(17227414913662599770)
XLA Ops:
  0.0 0.5 collective-permute-start.1
  0.5 0.1 collective-permute-start.2
  0.5 1.3 %place_rows.1.ids_ref = s32[8,256]{1,0:T(8,128)S(1)} custom-call(s32[8,256]{1,0:T(8,128)} %bitcast.11, s32[32,128]{1,0:T(8,128)} %bitcast.10), custom_call_target="tpu_custom_call" | custom-call | tf_op jit(solution)/shard_map/place_rows/pallas_call | solution.py:368
  1.9 5.1 %collective-permute-start = (s32[8,256]{1,0:T(8,128)S(1)}, s32[8,256]{1,0:T(8,128)S(1)}, u32[]{:S(2)}, u32[]{:S(2)}) collective-permute-start(s32[8,256]{1,0:T(8,128)S(1)} %place_rows.1.ids_ref), channel_id=1, source_target_pairs={{0,12},{4,8},{8,4},{12,0},{1,13},{5,9},{9,5},{13,1},{2,14},{6,10},... | collective-permute-start | bytes 24584 | tf_op jit(solution)/shard_map/ppermute | solution.py:310
  7.0 2.7 %decode_tables.1.table_ref = bf16[8,80,1024]{2,1,0:T(8,128)(2,1)S(1)} custom-call(bf16[8,80,1024]{2,1,0:T(8,128)(2,1)} %bitcast.8, bf16[5,8,1024]{2,1,0:T(8,128)(2,1)} %bitcast.9), custom_call_target="tpu_custom_call" | custom-call | tf_op jit(solution)/shard_map/decode_tables/pallas_call | solution.py:382
  9.7 0.0 collective-permute-done.ids_ref
  9.7 0.9 %pick_rows.4 = bf16[640,256]{1,0:T(8,128)(2,1)S(1)} custom-call(s32[1]{0:T(128)} %bitcast.3.base_ref, s32[8,256]{1,0:T(8,128)S(1)} %collective-permute-done.ids_ref, bf16[8,80,1024]{2,1,0:T(8,128)(2,1)S(1)} %decode_tables.1.table_ref), custom_call_target="tpu_custom_call" | custom-call | tf_op jit(solution)/shard_map/pick_rows/pallas_call | solution.py:313
  10.6 0.7 collective-permute-start.6
  11.3 3.6 %collective-permute-start.7 = (bf16[640,256]{1,0:T(8,128)(2,1)S(1)}, bf16[640,256]{1,0:T(8,128)(2,1)S(1)}, u32[]{:S(2)}, u32[]{:S(2)}) collective-permute-start(bf16[640,256]{1,0:T(8,128)(2,1)S(1)} %pick_rows.4), channel_id=1, source_target_pairs={{0,4},{12,8},{1,5},{13,9},{2,6},{14,10},{3,7},{15,11},{16,20},{28,... | collective-permute-start | bytes 983048 | tf_op jit(solution)/shard_map/ppermute | solution.py:323
  14.9 0.9 %pick_rows.5 = bf16[640,256]{1,0:T(8,128)(2,1)S(1)} custom-call(s32[1]{0:T(128)} %bitcast.3.base_ref, s32[8,256]{1,0:T(8,128)S(1)} %place_rows.1.ids_ref, bf16[8,80,1024]{2,1,0:T(8,128)(2,1)S(1)} %decode_tables.1.table_ref), custom_call_target="tpu_custom_call" | custom-call | tf_op jit(solution)/shard_map/pick_rows/pallas_call | solution.py:313
  15.8 0.0 copy-start
  15.8 0.0 collective-permute-done.1.refs_4_
  15.8 0.0 collective-permute-done.2.refs_5_
  15.8 0.1 collective-permute-start.3
  15.9 2.6 %collective-permute-start.5 = (s32[8,256]{1,0:T(8,128)S(1)}, s32[8,256]{1,0:T(8,128)S(1)}, u32[]{:S(2)}, u32[]{:S(2)}) collective-permute-start(s32[8,256]{1,0:T(8,128)S(1)} %place_rows.1.ids_ref), channel_id=1, source_target_pairs={{0,4},{4,0},{8,12},{12,8},{1,5},{5,1},{9,13},{13,9},{2,6},{6,2},{1... | collective-permute-start | bytes 24584 | tf_op jit(solution)/shard_map/ppermute | solution.py:310
  18.4 2.8 %collective-permute-done.3.ids_ref = s32[8,256]{1,0:T(8,128)S(1)} collective-permute-done((s32[8,256]{1,0:T(8,128)S(1)}, s32[8,256]{1,0:T(8,128)S(1)}, u32[]{:S(2)}, u32[]{:S(2)}) %collective-permute-start.3) | collective-permute-done | bytes 8224 | tf_op jit(solution)/shard_map/ppermute | solution.py:310
  21.2 0.9 %pick_rows.6 = bf16[640,256]{1,0:T(8,128)(2,1)S(1)} custom-call(s32[1]{0:T(128)} %bitcast.3.base_ref, s32[8,256]{1,0:T(8,128)S(1)} %collective-permute-done.3.ids_ref, bf16[8,80,1024]{2,1,0:T(8,128)(2,1)S(1)} %decode_tables.1.table_ref), custom_call_target="tpu_custom_call" | custom-call | tf_op jit(solution)/shard_map/pick_rows/pallas_call | solution.py:313
  22.1 5.3 %collective-permute-start.4 = (bf16[640,256]{1,0:T(8,128)(2,1)S(1)}, bf16[640,256]{1,0:T(8,128)(2,1)S(1)}, u32[]{:S(2)}, u32[]{:S(2)}) collective-permute-start(bf16[640,256]{1,0:T(8,128)(2,1)S(1)} %pick_rows.6), channel_id=1, source_target_pairs={{0,8},{12,4},{1,9},{13,5},{2,10},{14,6},{3,11},{15,7},{16,24},{28,... | collective-permute-start | bytes 983048 | tf_op jit(solution)/shard_map/ppermute | solution.py:323
  27.4 0.0 collective-permute-done.5.ids_ref
  27.4 0.9 %pick_rows.7 = bf16[640,256]{1,0:T(8,128)(2,1)S(1)} custom-call(s32[1]{0:T(128)} %bitcast.3.base_ref, s32[8,256]{1,0:T(8,128)S(1)} %collective-permute-done.5.ids_ref, bf16[8,80,1024]{2,1,0:T(8,128)(2,1)S(1)} %decode_tables.1.table_ref), custom_call_target="tpu_custom_call" | custom-call | tf_op jit(solution)/shard_map/pick_rows/pallas_call | solution.py:313
  28.3 0.0 collective-permute-done.6.refs_1_
  28.3 0.0 collective-permute-done.7
  28.3 0.1 add.16
  28.4 1.3 %collective-permute-start.10 = (bf16[640,256]{1,0:T(8,128)(2,1)S(1)}, bf16[640,256]{1,0:T(8,128)(2,1)S(1)}, u32[]{:S(2)}, u32[]{:S(2)}) collective-permute-start(bf16[640,256]{1,0:T(8,128)(2,1)S(1)} %add.16), channel_id=1, source_target_pairs={{4,12},{8,0},{5,13},{9,1},{6,14},{10,2},{7,15},{11,3},{20,28},{24,... | collective-permute-start | bytes 983048 | tf_op jit(solution)/shard_map/ppermute | solution.py:323
  29.7 3.7 %collective-permute-start.9 = (bf16[640,256]{1,0:T(8,128)(2,1)S(1)}, bf16[640,256]{1,0:T(8,128)(2,1)S(1)}, u32[]{:S(2)}, u32[]{:S(2)}) collective-permute-start(bf16[640,256]{1,0:T(8,128)(2,1)S(1)} %pick_rows.7), channel_id=1, source_target_pairs={{0,4},{4,0},{8,12},{12,8},{1,5},{5,1},{9,13},{13,9},{2,6},{6,2},{1... | collective-permute-start | bytes 983048 | tf_op jit(solution)/shard_map/ppermute | solution.py:323
  33.4 0.0 copy-done
  33.5 1.3 %collective-permute-start.8 = (bf16[16,2304]{1,0:T(8,128)(2,1)S(1)}, bf16[16,2304]{1,0:T(8,128)(2,1)S(1)}, u32[]{:S(2)}, u32[]{:S(2)}) collective-permute-start(bf16[16,2304]{1,0:T(8,128)(2,1)S(1)} %slice.6), channel_id=1, source_target_pairs={{0,1},{4,5},{8,9},{12,13},{2,3},{6,7},{10,11},{14,15},{16,17},{20,... | collective-permute-start | bytes 221192 | tf_op jit(solution)/shard_map/ppermute | solution.py:401
  34.8 0.0 collective-permute-done.4
  34.8 0.1 add.15.refs_0_
  34.9 0.8 %collective-permute-done.8.refs_5_ = bf16[16,2304]{1,0:T(8,128)(2,1)S(1)} collective-permute-done((bf16[16,2304]{1,0:T(8,128)(2,1)S(1)}, bf16[16,2304]{1,0:T(8,128)(2,1)S(1)}, u32[]{:S(2)}, u32[]{:S(2)}) %collective-permute-start.8) | collective-permute-done | bytes 73760 | tf_op jit(solution)/shard_map/ppermute | solution.py:401
  35.7 7.1 %collective-permute-done.10.refs_3_ = bf16[640,256]{1,0:T(8,128)(2,1)S(1)} collective-permute-done((bf16[640,256]{1,0:T(8,128)(2,1)S(1)}, bf16[640,256]{1,0:T(8,128)(2,1)S(1)}, u32[]{:S(2)}, u32[]{:S(2)}) %collective-permute-start.10) | collective-permute-done | bytes 327712 | tf_op jit(solution)/shard_map/ppermute | solution.py:323
  42.7 3.1 %collective-permute-done.9.refs_2_ = bf16[640,256]{1,0:T(8,128)(2,1)S(1)} collective-permute-done((bf16[640,256]{1,0:T(8,128)(2,1)S(1)}, bf16[640,256]{1,0:T(8,128)(2,1)S(1)}, u32[]{:S(2)}, u32[]{:S(2)}) %collective-permute-start.9) | collective-permute-done | bytes 327712 | tf_op jit(solution)/shard_map/ppermute | solution.py:323
  45.9 0.2 merge.1.refs_1_
  46.0 1.6 %collective-permute-start.12 = (bf16[640,256]{1,0:T(8,128)(2,1)S(1)}, bf16[640,256]{1,0:T(8,128)(2,1)S(1)}, u32[]{:S(2)}, u32[]{:S(2)}) collective-permute-start(bf16[640,256]{1,0:T(8,128)(2,1)S(1)} %merge.1.refs_1_), channel_id=1, source_target_pairs={{0,2},{2,0},{1,3},{3,1},{4,6},{6,4},{5,7},{7,5},{8,10},{10,8},{9,1... | collective-permute-start | bytes 983048 | tf_op jit(solution)/shard_map/ppermute | solution.py:412
  47.6 1.3 %collective-permute-start.13 = (bf16[640,128]{1,0:T(8,128)(2,1)S(1)}, bf16[640,128]{1,0:T(8,128)(2,1)S(1)}, u32[]{:S(2)}, u32[]{:S(2)}) collective-permute-start(bf16[640,128]{1,0:T(8,128)(2,1)S(1)} %slice.8), channel_id=1, source_target_pairs={{0,1},{2,3},{4,5},{6,7},{8,9},{10,11},{12,13},{14,15},{16,17},{18,... | collective-permute-start | bytes 491528 | tf_op jit(solution)/shard_map/ppermute | solution.py:425
  48.9 1.5 %collective-permute-start.11 = (bf16[640,128]{1,0:T(8,128)(2,1)S(1)}, bf16[640,128]{1,0:T(8,128)(2,1)S(1)}, u32[]{:S(2)}, u32[]{:S(2)}) collective-permute-start(bf16[640,128]{1,0:T(8,128)(2,1)S(1)} %slice.8), channel_id=1, source_target_pairs={{0,3},{2,1},{4,7},{6,5},{8,11},{10,9},{12,15},{14,13},{16,19},{18,... | collective-permute-start | bytes 491528 | tf_op jit(solution)/shard_map/ppermute | solution.py:425
  50.4 0.1 pad_add_fusion.where_ref
  50.5 0.0 collective-permute-done.13.refs_0_
  50.5 5.6 %project_own.1 = (f32[2,272,1152]{2,1,0:T(8,128)S(1)}, f32[2,272,1152]{2,1,0:T(8,128)S(1)}, bf16[2,2,640,1152]{3,2,1,0:T(8,128)(2,1)S(1)}) custom-call(s32[2]{0:T(128)S(1)} %pad_add_fusion.where_ref, bf16[640,128]{1,0:T(8,128)(2,1)S(1)} %collective-permute-done.13.refs_0_, bf16[640,256]{1,0:T(8,128)(2,1)S(1)} %merge.1.refs_1_, bf16[1280,1152]{1,0:T(8,128)(2,1)} %refs_2_.1, ...), custom_call_target="tpu_custom_call" | custom-call | tf_op jit(solution)/shard_map/project_own/pallas_call | solution.py:431
  56.1 0.0 collective-permute-done.11.refs_0_
  56.1 0.0 collective-permute-done.12.refs_1_
  56.1 0.0 copy-start.1
  56.1 4.2 %project_others.1 = (f32[2,272,1152]{2,1,0:T(8,128)}, f32[8,272]{1,0:T(8,128)S(1)}) custom-call(s32[2]{0:T(128)S(1)} %pad_add_fusion.where_ref, bf16[640,128]{1,0:T(8,128)(2,1)S(1)} %collective-permute-done.11.refs_0_, bf16[640,256]{1,0:T(8,128)(2,1)S(1)} %collective-permute-done.12.refs_1_, bf16[2,2,640,1152]{3,2,1,0:T(8,128)(2,1)S(1)} %get-tuple-element.29.refs_2_, ...), custom_call_target="tpu_custom_call" | custom-call | tf_op jit(solution)/shard_map/project_others/pallas_call | solution.py:444
  60.4 0.6 collective-permute-start.14
  61.0 3.2 %collective-permute-done.14.refs_1_ = f32[8,272]{1,0:T(8,128)S(1)} collective-permute-done((f32[8,272]{1,0:T(8,128)S(1)}, f32[8,272]{1,0:T(8,128)S(1)}, u32[]{:S(2)}, u32[]{:S(2)}) %collective-permute-start.14) | collective-permute-done | bytes 8736 | tf_op jit(solution)/shard_map/ppermute | solution.py:467
  64.1 0.0 copy-done.1
  64.1 4.0 %finish.1 = bf16[256,2304]{1,0:T(8,128)(2,1)} custom-call(s32[1]{0:T(128)} %bitcast.keep_ref, f32[8,272]{1,0:T(8,128)S(1)} %get-tuple-element.33.refs_0_, f32[8,272]{1,0:T(8,128)S(1)} %collective-permute-done.14.refs_1_, f32[2,272,1152]{2,1,0:T(8,128)} %get-tuple-element.34.refs_2_, bf16[256,2304]{1,0:T(8,128)(2,1)S(1)} %copy-done, f32[4,2304]{1,0:T(4,128)S(1)} %copy-done.1), custom_call_target="tpu_custom_call" | custom-call | tf_op jit(solution)/shard_map/finish/pallas_call | solution.py:473
  (2 shorter events, 0.0 us)
Async XLA Ops:
  0.0 15.8 %collective-permute-start.1 = (bf16[1280,1152]{1,0:T(8,128)(2,1)}, bf16[1280,1152]{1,0:T(8,128)(2,1)}, u32[]{:S(2)}, u32[]{:S(2)}) collective-permute-start(bf16[1280,1152]{1,0:T(8,128)(2,1)} %refs_2_.1), channel_id=1, source_target_pairs={{0,1},{1,0},{2,3},{3,2},{4,5},{5,4},{6,7},{7,6},{8,9},{9,8},{10,11... | collective-permute-start | bytes 8847368 | tf_op jit(solution)/shard_map/ppermute | solution.py:395
  0.5 15.3 %collective-permute-start.2 = (bf16[1280,1152]{1,0:T(8,128)(2,1)}, bf16[1280,1152]{1,0:T(8,128)(2,1)}, u32[]{:S(2)}, u32[]{:S(2)}) collective-permute-start(bf16[1280,1152]{1,0:T(8,128)(2,1)} %refs_3_.2), channel_id=1, source_target_pairs={{0,1},{1,0},{2,3},{3,2},{4,5},{5,4},{6,7},{7,6},{8,9},{9,8},{10,11... | collective-permute-start | bytes 8847368 | tf_op jit(solution)/shard_map/ppermute | solution.py:396
  1.9 7.9 %collective-permute-start = (s32[8,256]{1,0:T(8,128)S(1)}, s32[8,256]{1,0:T(8,128)S(1)}, u32[]{:S(2)}, u32[]{:S(2)}) collective-permute-start(s32[8,256]{1,0:T(8,128)S(1)} %place_rows.1.ids_ref), channel_id=1, source_target_pairs={{0,12},{4,8},{8,4},{12,0},{1,13},{5,9},{9,5},{13,1},{2,14},{6,10},... | collective-permute-start | bytes 24584 | tf_op jit(solution)/shard_map/ppermute | solution.py:310
  10.6 17.7 %collective-permute-start.6 = (bf16[640,256]{1,0:T(8,128)(2,1)S(1)}, bf16[640,256]{1,0:T(8,128)(2,1)S(1)}, u32[]{:S(2)}, u32[]{:S(2)}) collective-permute-start(bf16[640,256]{1,0:T(8,128)(2,1)S(1)} %pick_rows.4), channel_id=1, source_target_pairs={{4,8},{8,4},{5,9},{9,5},{6,10},{10,6},{7,11},{11,7},{20,24},{24,20... | collective-permute-start | bytes 983048 | tf_op jit(solution)/shard_map/ppermute | solution.py:323
  11.3 17.0 %collective-permute-start.7 = (bf16[640,256]{1,0:T(8,128)(2,1)S(1)}, bf16[640,256]{1,0:T(8,128)(2,1)S(1)}, u32[]{:S(2)}, u32[]{:S(2)}) collective-permute-start(bf16[640,256]{1,0:T(8,128)(2,1)S(1)} %pick_rows.4), channel_id=1, source_target_pairs={{0,4},{12,8},{1,5},{13,9},{2,6},{14,10},{3,7},{15,11},{16,20},{28,... | collective-permute-start | bytes 983048 | tf_op jit(solution)/shard_map/ppermute | solution.py:323
  15.8 17.7 %copy-start = (bf16[256,2304]{1,0:T(8,128)(2,1)S(1)}, bf16[256,2304]{1,0:T(8,128)(2,1)}, u32[]{:S(2)}) copy-start(bf16[256,2304]{1,0:T(8,128)(2,1)} %refs_3_.3) | copy-start | bytes 3538948
  15.8 5.5 %collective-permute-start.3 = (s32[8,256]{1,0:T(8,128)S(1)}, s32[8,256]{1,0:T(8,128)S(1)}, u32[]{:S(2)}, u32[]{:S(2)}) collective-permute-start(s32[8,256]{1,0:T(8,128)S(1)} %place_rows.1.ids_ref), channel_id=1, source_target_pairs={{0,8},{4,12},{8,0},{12,4},{1,9},{5,13},{9,1},{13,5},{2,10},{6,14},... | collective-permute-start | bytes 24584 | tf_op jit(solution)/shard_map/ppermute | solution.py:310
  15.9 11.6 %collective-permute-start.5 = (s32[8,256]{1,0:T(8,128)S(1)}, s32[8,256]{1,0:T(8,128)S(1)}, u32[]{:S(2)}, u32[]{:S(2)}) collective-permute-start(s32[8,256]{1,0:T(8,128)S(1)} %place_rows.1.ids_ref), channel_id=1, source_target_pairs={{0,4},{4,0},{8,12},{12,8},{1,5},{5,1},{9,13},{13,9},{2,6},{6,2},{1... | collective-permute-start | bytes 24584 | tf_op jit(solution)/shard_map/ppermute | solution.py:310
  22.1 12.7 %collective-permute-start.4 = (bf16[640,256]{1,0:T(8,128)(2,1)S(1)}, bf16[640,256]{1,0:T(8,128)(2,1)S(1)}, u32[]{:S(2)}, u32[]{:S(2)}) collective-permute-start(bf16[640,256]{1,0:T(8,128)(2,1)S(1)} %pick_rows.6), channel_id=1, source_target_pairs={{0,8},{12,4},{1,9},{13,5},{2,10},{14,6},{3,11},{15,7},{16,24},{28,... | collective-permute-start | bytes 983048 | tf_op jit(solution)/shard_map/ppermute | solution.py:323
  28.4 14.3 %collective-permute-start.10 = (bf16[640,256]{1,0:T(8,128)(2,1)S(1)}, bf16[640,256]{1,0:T(8,128)(2,1)S(1)}, u32[]{:S(2)}, u32[]{:S(2)}) collective-permute-start(bf16[640,256]{1,0:T(8,128)(2,1)S(1)} %add.16), channel_id=1, source_target_pairs={{4,12},{8,0},{5,13},{9,1},{6,14},{10,2},{7,15},{11,3},{20,28},{24,... | collective-permute-start | bytes 983048 | tf_op jit(solution)/shard_map/ppermute | solution.py:323
  29.7 16.1 %collective-permute-start.9 = (bf16[640,256]{1,0:T(8,128)(2,1)S(1)}, bf16[640,256]{1,0:T(8,128)(2,1)S(1)}, u32[]{:S(2)}, u32[]{:S(2)}) collective-permute-start(bf16[640,256]{1,0:T(8,128)(2,1)S(1)} %pick_rows.7), channel_id=1, source_target_pairs={{0,4},{4,0},{8,12},{12,8},{1,5},{5,1},{9,13},{13,9},{2,6},{6,2},{1... | collective-permute-start | bytes 983048 | tf_op jit(solution)/shard_map/ppermute | solution.py:323
  33.5 2.2 %collective-permute-start.8 = (bf16[16,2304]{1,0:T(8,128)(2,1)S(1)}, bf16[16,2304]{1,0:T(8,128)(2,1)S(1)}, u32[]{:S(2)}, u32[]{:S(2)}) collective-permute-start(bf16[16,2304]{1,0:T(8,128)(2,1)S(1)} %slice.6), channel_id=1, source_target_pairs={{0,1},{4,5},{8,9},{12,13},{2,3},{6,7},{10,11},{14,15},{16,17},{20,... | collective-permute-start | bytes 221192 | tf_op jit(solution)/shard_map/ppermute | solution.py:401
  46.0 10.1 %collective-permute-start.12 = (bf16[640,256]{1,0:T(8,128)(2,1)S(1)}, bf16[640,256]{1,0:T(8,128)(2,1)S(1)}, u32[]{:S(2)}, u32[]{:S(2)}) collective-permute-start(bf16[640,256]{1,0:T(8,128)(2,1)S(1)} %merge.1.refs_1_), channel_id=1, source_target_pairs={{0,2},{2,0},{1,3},{3,1},{4,6},{6,4},{5,7},{7,5},{8,10},{10,8},{9,1... | collective-permute-start | bytes 983048 | tf_op jit(solution)/shard_map/ppermute | solution.py:412
  47.6 2.9 %collective-permute-start.13 = (bf16[640,128]{1,0:T(8,128)(2,1)S(1)}, bf16[640,128]{1,0:T(8,128)(2,1)S(1)}, u32[]{:S(2)}, u32[]{:S(2)}) collective-permute-start(bf16[640,128]{1,0:T(8,128)(2,1)S(1)} %slice.8), channel_id=1, source_target_pairs={{0,1},{2,3},{4,5},{6,7},{8,9},{10,11},{12,13},{14,15},{16,17},{18,... | collective-permute-start | bytes 491528 | tf_op jit(solution)/shard_map/ppermute | solution.py:425
  48.9 7.2 %collective-permute-start.11 = (bf16[640,128]{1,0:T(8,128)(2,1)S(1)}, bf16[640,128]{1,0:T(8,128)(2,1)S(1)}, u32[]{:S(2)}, u32[]{:S(2)}) collective-permute-start(bf16[640,128]{1,0:T(8,128)(2,1)S(1)} %slice.8), channel_id=1, source_target_pairs={{0,3},{2,1},{4,7},{6,5},{8,11},{10,9},{12,15},{14,13},{16,19},{18,... | collective-permute-start | bytes 491528 | tf_op jit(solution)/shard_map/ppermute | solution.py:425
  56.1 8.0 %copy-start.1 = (f32[4,2304]{1,0:T(4,128)S(1)}, f32[4,2304]{1,0:T(4,128)}, u32[]{:S(2)}) copy-start(f32[4,2304]{1,0:T(4,128)} %refs_4_.1) | copy-start | bytes 110596
  60.4 3.8 %collective-permute-start.14 = (f32[8,272]{1,0:T(8,128)S(1)}, f32[8,272]{1,0:T(8,128)S(1)}, u32[]{:S(2)}, u32[]{:S(2)}) collective-permute-start(f32[8,272]{1,0:T(8,128)S(1)} %get-tuple-element.33.refs_0_), channel_id=1, source_target_pairs={{0,2},{2,0},{1,3},{3,1},{4,6},{6,4},{5,7},{7,5},{8,10},{10,8},{9,1... | collective-permute-start | bytes 26120 | tf_op jit(solution)/shard_map/ppermute | solution.py:467

commit v9 on v8

--- a/solution.py
+++ b/solution.py
@@ -309,6 +309,9 @@
     def ask(ids, x):
         return lax.ppermute(ids, "mem", [(i, i ^ x) for i in range(4)])
 
+    def crossing(x, pairs):
+        return lax.ppermute(x, ("mem", "rep"), [(2 * a + b, 2 * c + d) for a, b, c, d in pairs])
+
     def pick(ids):
         return pl.pallas_call(
             pick_kernel,
@@ -322,19 +325,24 @@
     def send(x, *pairs):
         return lax.ppermute(x, "mem", pairs)
 
-    rows_3 = pick(ask(stored, 3))
+    first = ask(stored, 3)
+    second = crossing(
+        stored,
+        [(m, r, m ^ 2, r ^ int(m in (1, 2))) for m in range(4) for r in range(2)],
+    )
+    first, second = lax.optimization_barrier((first, second))
+    rows_3 = pick(first)
     inward = send(rows_3, (0, 1), (3, 2))
     across = send(rows_3, (1, 2), (2, 1))
-    own = pick(after(stored, rows_3))
-    stored, settled = lax.optimization_barrier((after(stored, own), settled))
-    asked = ask(stored, 2), ask(stored, 1)
-    rows_2 = pick(asked[0])
-    past = send(rows_2, (0, 2), (3, 1))
-    rows_1 = pick(asked[1])
-    onward = after(rows_2, rows_1, across) + inward
+    rows_2 = pick(after(second, rows_3))
+    past = crossing(rows_2, [(m, r, m ^ 2, r ^ 1) for m in (0, 3) for r in range(2)])
+    stored, settled = lax.optimization_barrier((after(stored, rows_2), settled))
+    rows_1 = pick(ask(stored, 1))
+    own = pick(stored)
+    onward = after(rows_2, own, across) + inward
     other = meanwhile(onward)
     onward = send(onward, (1, 3), (2, 0))
-    beside = send(after(rows_1, inward), (0, 1), (1, 0), (2, 3), (3, 2))
+    beside = send(rows_1, (0, 1), (1, 0), (2, 3), (3, 2))
     own, other = lax.optimization_barrier((own + past, other))
     memory = pl.pallas_call(
         merge_kernel,
@@ -390,7 +398,7 @@
         ],
         compiler_params=limit(12),
         name="decode_tables",
-    )(in_hbm(codes), in_hbm(scales))
+    )(in_hbm(after(codes, stored)), in_hbm(scales))
     here = lax.axis_index("mem")
     other_key = lax.ppermute(key_weight, "rep", [(0, 1), (1, 0)])
     other_value = lax.ppermute(value_weight, "rep", [(0, 1), (1, 0)])

time: 68.6 us -> 67 us (0.977)
  starting transfers between devices: 29.1 us -> 24.6 us
  waiting for transfers between devices: 17 us -> 19.9 us
    ppermute x5 -> x4, starting transfers between devices: 14.6 us -> 9.47 us  [send(): return lax.ppermute(x, 'mem', pairs)]
    ppermute x5 -> x4, waiting for transfers between devices: 10.2 us -> 14.6 us  [send(): return lax.ppermute(x, 'mem', pairs)]
    ppermute x0 -> x2, starting transfers between devices: none -> 3.21 us  [crossing(): lax.ppermute(x, ('mem', 'rep'), [(2 * a + b, 2 * c + d) for a, b, c, d in...]
    ppermute x3 -> x2, waiting for transfers between devices: 2.81 us -> 0.01 us  [ask(): return lax.ppermute(ids, 'mem', [(i, i ^ x) for i in range(4)])]
    ppermute x3 -> x2, starting transfers between devices: 7.77 us -> 5.19 us  [ask(): return lax.ppermute(ids, 'mem', [(i, i ^ x) for i in range(4)])]
    ppermute x0 -> x2, waiting for transfers between devices: none -> 2.15 us  [crossing(): lax.ppermute(x, ('mem', 'rep'), [(2 * a + b, 2 * c + d) for a, b, c, d in...]
    ppermute x1, waiting for transfers between devices: 0.79 us -> 0.01 us  [meanwhile(): return lax.ppermute(tail, ('mem', 'rep'), needed)]
  transfers between devices with their start and end apart: 15 -> 15, of which waited for: 5 -> 6; matrix products, arithmetic and copies ran while one was open for 0% -> 0% of each run, Pallas kernels for 19% -> 20%
where the time goes in v9:
time: 67 us; the launch traced here: 66.7 us
  starting transfers between devices  24.6 us (37%)
  Pallas kernels  21.5 us (32%)
  waiting for transfers between devices  19.9 us (30%)
    ppermute x4, waiting for transfers between devices, send(): return lax.ppermute(x, 'mem', pairs)  14.6 us
    ppermute x4, starting transfers between devices, send(): return lax.ppermute(x, 'mem', pairs)  9.47 us
    pallas_call x1, Pallas kernels, shards(): pl.pallas_call(functools.partial(project_kernel, (0,), tps), in_specs=[sm...  5.61 us
    ppermute x2, starting transfers between devices, ask(): return lax.ppermute(ids, 'mem', [(i, i ^ x) for i in range(4)])  5.19 us
    pallas_call x1, Pallas kernels, shards(): pl.pallas_call(functools.partial(project_kernel, tuple(range(1, tps)), tp...  4.24 us
    pallas_call x1, Pallas kernels, shards(): pl.pallas_call(functools.partial(finish_kernel, tps, step), in_specs=[sme...  3.96 us
    pallas_call x4, Pallas kernels, pick(): pl.pallas_call(pick_kernel, in_specs=[pl.BlockSpec(memory_space=pltpu.SME...  3.45 us
    ppermute x2, starting transfers between devices, crossing(): lax.ppermute(x, ('mem', 'rep'), [(2 * a + b, 2 * c + d) for a, b, c, d in...  3.21 us
  transfers between devices with their start and end apart: 15, of which 6 were waited for; matrix products, arithmetic and copies ran while one was open for 0% of the time, Pallas kernels for 20%

profile of v9, /device:TPU:0, one launch (start us, length us, event | category | flops | bytes accessed | tf_op | source)
XLA Modules:
  0.0 66.7 jit_solution(7353717932335911796)
XLA Ops:
  0.0 0.5 collective-permute-start.2
  0.5 0.1 collective-permute-start.3
  0.5 1.3 %place_rows.1.ids_ref = s32[8,256]{1,0:T(8,128)S(1)} custom-call(s32[8,256]{1,0:T(8,128)} %bitcast.11, s32[32,128]{1,0:T(8,128)} %bitcast.10), custom_call_target="tpu_custom_call" | custom-call | tf_op jit(solution)/shard_map/place_rows/pallas_call | solution.py:376
  1.9 5.1 %collective-permute-start = (s32[8,256]{1,0:T(8,128)S(1)}, s32[8,256]{1,0:T(8,128)S(1)}, u32[]{:S(2)}, u32[]{:S(2)}) collective-permute-start(s32[8,256]{1,0:T(8,128)S(1)} %place_rows.1.ids_ref), channel_id=1, source_target_pairs={{0,12},{4,8},{8,4},{12,0},{1,13},{5,9},{9,5},{13,1},{2,14},{6,10},... | collective-permute-start | bytes 24584 | tf_op jit(solution)/shard_map/ppermute | solution.py:310
  7.0 0.0 collective-permute-start.1
  7.0 2.7 %decode_tables.1.table_ref = bf16[8,80,1024]{2,1,0:T(8,128)(2,1)S(1)} custom-call(bf16[8,80,1024]{2,1,0:T(8,128)(2,1)} %bitcast.8, bf16[5,8,1024]{2,1,0:T(8,128)(2,1)} %bitcast.9), custom_call_target="tpu_custom_call" | custom-call | tf_op jit(solution)/shard_map/decode_tables/pallas_call | solution.py:390
  9.7 0.0 collective-permute-done.ids_ref
  9.7 1.2 %collective-permute-done.1.ids_ref = s32[8,256]{1,0:T(8,128)S(1)} collective-permute-done((s32[8,256]{1,0:T(8,128)S(1)}, s32[8,256]{1,0:T(8,128)S(1)}, u32[]{:S(2)}, u32[]{:S(2)}) %collective-permute-start.1) | collective-permute-done | bytes 8224 | tf_op jit(solution)/shard_map/ppermute | solution.py:313
  10.9 0.9 %pick_rows.4 = bf16[640,256]{1,0:T(8,128)(2,1)S(1)} custom-call(s32[1]{0:T(128)} %bitcast.3.base_ref, s32[8,256]{1,0:T(8,128)S(1)} %collective-permute-done.ids_ref, bf16[8,80,1024]{2,1,0:T(8,128)(2,1)S(1)} %decode_tables.1.table_ref), custom_call_target="tpu_custom_call" | custom-call | tf_op jit(solution)/shard_map/pick_rows/pallas_call | solution.py:316
  11.8 0.7 %collective-permute-start.5 = (bf16[640,256]{1,0:T(8,128)(2,1)S(1)}, bf16[640,256]{1,0:T(8,128)(2,1)S(1)}, u32[]{:S(2)}, u32[]{:S(2)}) collective-permute-start(bf16[640,256]{1,0:T(8,128)(2,1)S(1)} %pick_rows.4), channel_id=1, source_target_pairs={{4,8},{8,4},{5,9},{9,5},{6,10},{10,6},{7,11},{11,7},{20,24},{24,20... | collective-permute-start | bytes 983048 | tf_op jit(solution)/shard_map/ppermute | solution.py:326
  12.5 4.8 %collective-permute-start.6 = (bf16[640,256]{1,0:T(8,128)(2,1)S(1)}, bf16[640,256]{1,0:T(8,128)(2,1)S(1)}, u32[]{:S(2)}, u32[]{:S(2)}) collective-permute-start(bf16[640,256]{1,0:T(8,128)(2,1)S(1)} %pick_rows.4), channel_id=1, source_target_pairs={{0,4},{12,8},{1,5},{13,9},{2,6},{14,10},{3,7},{15,11},{16,20},{28,... | collective-permute-start | bytes 983048 | tf_op jit(solution)/shard_map/ppermute | solution.py:326
  17.3 0.9 %pick_rows.5 = bf16[640,256]{1,0:T(8,128)(2,1)S(1)} custom-call(s32[1]{0:T(128)} %bitcast.3.base_ref, s32[8,256]{1,0:T(8,128)S(1)} %collective-permute-done.1.ids_ref, bf16[8,80,1024]{2,1,0:T(8,128)(2,1)S(1)} %decode_tables.1.table_ref), custom_call_target="tpu_custom_call" | custom-call | tf_op jit(solution)/shard_map/pick_rows/pallas_call | solution.py:316
  18.1 0.0 copy-start
  18.2 0.0 collective-permute-done.2.refs_4_
  18.2 0.0 collective-permute-done.3.refs_5_
  18.2 0.1 collective-permute-start.8
  18.3 3.2 %collective-permute-start.4 = (bf16[640,256]{1,0:T(8,128)(2,1)S(1)}, bf16[640,256]{1,0:T(8,128)(2,1)S(1)}, u32[]{:S(2)}, u32[]{:S(2)}) collective-permute-start(bf16[640,256]{1,0:T(8,128)(2,1)S(1)} %pick_rows.5), channel_id=1, source_target_pairs={{0,9},{1,8},{12,5},{13,4},{2,11},{3,10},{14,7},{15,6},{16,25},{17,... | collective-permute-start | bytes 983048 | tf_op jit(solution)/shard_map/ppermute | solution.py:313
  21.5 0.9 %pick_rows.6 = bf16[640,256]{1,0:T(8,128)(2,1)S(1)} custom-call(s32[1]{0:T(128)} %bitcast.3.base_ref, s32[8,256]{1,0:T(8,128)S(1)} %place_rows.1.ids_ref, bf16[8,80,1024]{2,1,0:T(8,128)(2,1)S(1)} %decode_tables.1.table_ref), custom_call_target="tpu_custom_call" | custom-call | tf_op jit(solution)/shard_map/pick_rows/pallas_call | solution.py:316
  22.3 0.0 collective-permute-done.5.refs_1_
  22.3 2.9 %collective-permute-done.6 = bf16[640,256]{1,0:T(8,128)(2,1)S(1)} collective-permute-done((bf16[640,256]{1,0:T(8,128)(2,1)S(1)}, bf16[640,256]{1,0:T(8,128)(2,1)S(1)}, u32[]{:S(2)}, u32[]{:S(2)}) %collective-permute-start.6) | collective-permute-done | bytes 327712 | tf_op jit(solution)/shard_map/ppermute | solution.py:326
  25.3 0.1 add.16
  25.3 1.3 %collective-permute-start.10 = (bf16[640,256]{1,0:T(8,128)(2,1)S(1)}, bf16[640,256]{1,0:T(8,128)(2,1)S(1)}, u32[]{:S(2)}, u32[]{:S(2)}) collective-permute-start(bf16[640,256]{1,0:T(8,128)(2,1)S(1)} %add.16), channel_id=1, source_target_pairs={{4,12},{8,0},{5,13},{9,1},{6,14},{10,2},{7,15},{11,3},{20,28},{24,... | collective-permute-start | bytes 983048 | tf_op jit(solution)/shard_map/ppermute | solution.py:326
  26.6 0.0 collective-permute-done.8.ids_ref
  26.7 0.9 %pick_rows.7 = bf16[640,256]{1,0:T(8,128)(2,1)S(1)} custom-call(s32[1]{0:T(128)} %bitcast.3.base_ref, s32[8,256]{1,0:T(8,128)S(1)} %collective-permute-done.8.ids_ref, bf16[8,80,1024]{2,1,0:T(8,128)(2,1)S(1)} %decode_tables.1.table_ref), custom_call_target="tpu_custom_call" | custom-call | tf_op jit(solution)/shard_map/pick_rows/pallas_call | solution.py:316
  27.5 2.7 %collective-permute-start.9 = (bf16[640,256]{1,0:T(8,128)(2,1)S(1)}, bf16[640,256]{1,0:T(8,128)(2,1)S(1)}, u32[]{:S(2)}, u32[]{:S(2)}) collective-permute-start(bf16[640,256]{1,0:T(8,128)(2,1)S(1)} %pick_rows.7), channel_id=1, source_target_pairs={{0,4},{4,0},{8,12},{12,8},{1,5},{5,1},{9,13},{13,9},{2,6},{6,2},{1... | collective-permute-start | bytes 983048 | tf_op jit(solution)/shard_map/ppermute | solution.py:326
  30.2 0.0 copy-done
  30.3 1.3 %collective-permute-start.7 = (bf16[16,2304]{1,0:T(8,128)(2,1)S(1)}, bf16[16,2304]{1,0:T(8,128)(2,1)S(1)}, u32[]{:S(2)}, u32[]{:S(2)}) collective-permute-start(bf16[16,2304]{1,0:T(8,128)(2,1)S(1)} %slice.6), channel_id=1, source_target_pairs={{0,1},{4,5},{8,9},{12,13},{2,3},{6,7},{10,11},{14,15},{16,17},{20,... | collective-permute-start | bytes 221192 | tf_op jit(solution)/shard_map/ppermute | solution.py:409
  31.6 0.9 %collective-permute-done.4 = bf16[640,256]{1,0:T(8,128)(2,1)S(1)} collective-permute-done((bf16[640,256]{1,0:T(8,128)(2,1)S(1)}, bf16[640,256]{1,0:T(8,128)(2,1)S(1)}, u32[]{:S(2)}, u32[]{:S(2)}) %collective-permute-start.4) | collective-permute-done | bytes 327712 | tf_op jit(solution)/shard_map/ppermute | solution.py:313
  32.5 0.1 add.15.refs_0_
  32.6 0.0 collective-permute-done.7.refs_5_
  32.6 8.2 %collective-permute-done.10.refs_3_ = bf16[640,256]{1,0:T(8,128)(2,1)S(1)} collective-permute-done((bf16[640,256]{1,0:T(8,128)(2,1)S(1)}, bf16[640,256]{1,0:T(8,128)(2,1)S(1)}, u32[]{:S(2)}, u32[]{:S(2)}) %collective-permute-start.10) | collective-permute-done | bytes 327712 | tf_op jit(solution)/shard_map/ppermute | solution.py:326
  40.9 3.5 %collective-permute-done.9.refs_2_ = bf16[640,256]{1,0:T(8,128)(2,1)S(1)} collective-permute-done((bf16[640,256]{1,0:T(8,128)(2,1)S(1)}, bf16[640,256]{1,0:T(8,128)(2,1)S(1)}, u32[]{:S(2)}, u32[]{:S(2)}) %collective-permute-start.9) | collective-permute-done | bytes 327712 | tf_op jit(solution)/shard_map/ppermute | solution.py:326
  44.3 0.2 merge.1.refs_1_
  44.5 1.6 %collective-permute-start.12 = (bf16[640,256]{1,0:T(8,128)(2,1)S(1)}, bf16[640,256]{1,0:T(8,128)(2,1)S(1)}, u32[]{:S(2)}, u32[]{:S(2)}) collective-permute-start(bf16[640,256]{1,0:T(8,128)(2,1)S(1)} %merge.1.refs_1_), channel_id=1, source_target_pairs={{0,2},{2,0},{1,3},{3,1},{4,6},{6,4},{5,7},{7,5},{8,10},{10,8},{9,1... | collective-permute-start | bytes 983048 | tf_op jit(solution)/shard_map/ppermute | solution.py:420
  46.0 1.3 %collective-permute-start.13 = (bf16[640,128]{1,0:T(8,128)(2,1)S(1)}, bf16[640,128]{1,0:T(8,128)(2,1)S(1)}, u32[]{:S(2)}, u32[]{:S(2)}) collective-permute-start(bf16[640,128]{1,0:T(8,128)(2,1)S(1)} %slice.8), channel_id=1, source_target_pairs={{0,1},{2,3},{4,5},{6,7},{8,9},{10,11},{12,13},{14,15},{16,17},{18,... | collective-permute-start | bytes 491528 | tf_op jit(solution)/shard_map/ppermute | solution.py:433
  47.4 1.5 %collective-permute-start.11 = (bf16[640,128]{1,0:T(8,128)(2,1)S(1)}, bf16[640,128]{1,0:T(8,128)(2,1)S(1)}, u32[]{:S(2)}, u32[]{:S(2)}) collective-permute-start(bf16[640,128]{1,0:T(8,128)(2,1)S(1)} %slice.8), channel_id=1, source_target_pairs={{0,3},{2,1},{4,7},{6,5},{8,11},{10,9},{12,15},{14,13},{16,19},{18,... | collective-permute-start | bytes 491528 | tf_op jit(solution)/shard_map/ppermute | solution.py:433
  48.8 0.1 pad_add_fusion.where_ref
  48.9 0.0 collective-permute-done.13.refs_0_
  48.9 5.6 %project_own.1 = (f32[2,272,1152]{2,1,0:T(8,128)S(1)}, f32[2,272,1152]{2,1,0:T(8,128)S(1)}, bf16[2,2,640,1152]{3,2,1,0:T(8,128)(2,1)S(1)}) custom-call(s32[2]{0:T(128)S(1)} %pad_add_fusion.where_ref, bf16[640,128]{1,0:T(8,128)(2,1)S(1)} %collective-permute-done.13.refs_0_, bf16[640,256]{1,0:T(8,128)(2,1)S(1)} %merge.1.refs_1_, bf16[1280,1152]{1,0:T(8,128)(2,1)} %refs_2_.1, ...), custom_call_target="tpu_custom_call" | custom-call | tf_op jit(solution)/shard_map/project_own/pallas_call | solution.py:439
  54.5 0.0 collective-permute-done.11.refs_0_
  54.5 0.0 collective-permute-done.12.refs_1_
  54.6 0.0 copy-start.1
  54.6 4.2 %project_others.1 = (f32[2,272,1152]{2,1,0:T(8,128)}, f32[8,272]{1,0:T(8,128)S(1)}) custom-call(s32[2]{0:T(128)S(1)} %pad_add_fusion.where_ref, bf16[640,128]{1,0:T(8,128)(2,1)S(1)} %collective-permute-done.11.refs_0_, bf16[640,256]{1,0:T(8,128)(2,1)S(1)} %collective-permute-done.12.refs_1_, bf16[2,2,640,1152]{3,2,1,0:T(8,128)(2,1)S(1)} %get-tuple-element.33.refs_2_, ...), custom_call_target="tpu_custom_call" | custom-call | tf_op jit(solution)/shard_map/project_others/pallas_call | solution.py:452
  58.8 0.6 collective-permute-start.14
  59.5 3.1 %collective-permute-done.14.refs_1_ = f32[8,272]{1,0:T(8,128)S(1)} collective-permute-done((f32[8,272]{1,0:T(8,128)S(1)}, f32[8,272]{1,0:T(8,128)S(1)}, u32[]{:S(2)}, u32[]{:S(2)}) %collective-permute-start.14) | collective-permute-done | bytes 8736 | tf_op jit(solution)/shard_map/ppermute | solution.py:475
  62.6 0.0 copy-done.1
  62.6 4.0 %finish.1 = bf16[256,2304]{1,0:T(8,128)(2,1)} custom-call(s32[1]{0:T(128)} %bitcast.keep_ref, f32[8,272]{1,0:T(8,128)S(1)} %get-tuple-element.37.refs_0_, f32[8,272]{1,0:T(8,128)S(1)} %collective-permute-done.14.refs_1_, f32[2,272,1152]{2,1,0:T(8,128)} %get-tuple-element.38.refs_2_, bf16[256,2304]{1,0:T(8,128)(2,1)S(1)} %copy-done, f32[4,2304]{1,0:T(4,128)S(1)} %copy-done.1), custom_call_target="tpu_custom_call" | custom-call | tf_op jit(solution)/shard_map/finish/pallas_call | solution.py:481
  (2 shorter events, 0.0 us)
Async XLA Ops:
  0.0 18.2 %collective-permute-start.2 = (bf16[1280,1152]{1,0:T(8,128)(2,1)}, bf16[1280,1152]{1,0:T(8,128)(2,1)}, u32[]{:S(2)}, u32[]{:S(2)}) collective-permute-start(bf16[1280,1152]{1,0:T(8,128)(2,1)} %refs_2_.1), channel_id=1, source_target_pairs={{0,1},{1,0},{2,3},{3,2},{4,5},{5,4},{6,7},{7,6},{8,9},{9,8},{10,11... | collective-permute-start | bytes 8847368 | tf_op jit(solution)/shard_map/ppermute | solution.py:403
  0.5 17.7 %collective-permute-start.3 = (bf16[1280,1152]{1,0:T(8,128)(2,1)}, bf16[1280,1152]{1,0:T(8,128)(2,1)}, u32[]{:S(2)}, u32[]{:S(2)}) collective-permute-start(bf16[1280,1152]{1,0:T(8,128)(2,1)} %refs_3_.2), channel_id=1, source_target_pairs={{0,1},{1,0},{2,3},{3,2},{4,5},{5,4},{6,7},{7,6},{8,9},{9,8},{10,11... | collective-permute-start | bytes 8847368 | tf_op jit(solution)/shard_map/ppermute | solution.py:404
  1.9 7.9 %collective-permute-start = (s32[8,256]{1,0:T(8,128)S(1)}, s32[8,256]{1,0:T(8,128)S(1)}, u32[]{:S(2)}, u32[]{:S(2)}) collective-permute-start(s32[8,256]{1,0:T(8,128)S(1)} %place_rows.1.ids_ref), channel_id=1, source_target_pairs={{0,12},{4,8},{8,4},{12,0},{1,13},{5,9},{9,5},{13,1},{2,14},{6,10},... | collective-permute-start | bytes 24584 | tf_op jit(solution)/shard_map/ppermute | solution.py:310
  7.0 4.0 %collective-permute-start.1 = (s32[8,256]{1,0:T(8,128)S(1)}, s32[8,256]{1,0:T(8,128)S(1)}, u32[]{:S(2)}, u32[]{:S(2)}) collective-permute-start(s32[8,256]{1,0:T(8,128)S(1)} %place_rows.1.ids_ref), channel_id=1, source_target_pairs={{0,8},{1,9},{4,13},{5,12},{8,1},{9,0},{12,4},{13,5},{2,10},{3,11},... | collective-permute-start | bytes 24584 | tf_op jit(solution)/shard_map/ppermute | solution.py:313
  11.8 10.5 %collective-permute-start.5 = (bf16[640,256]{1,0:T(8,128)(2,1)S(1)}, bf16[640,256]{1,0:T(8,128)(2,1)S(1)}, u32[]{:S(2)}, u32[]{:S(2)}) collective-permute-start(bf16[640,256]{1,0:T(8,128)(2,1)S(1)} %pick_rows.4), channel_id=1, source_target_pairs={{4,8},{8,4},{5,9},{9,5},{6,10},{10,6},{7,11},{11,7},{20,24},{24,20... | collective-permute-start | bytes 983048 | tf_op jit(solution)/shard_map/ppermute | solution.py:326
  12.5 12.8 %collective-permute-start.6 = (bf16[640,256]{1,0:T(8,128)(2,1)S(1)}, bf16[640,256]{1,0:T(8,128)(2,1)S(1)}, u32[]{:S(2)}, u32[]{:S(2)}) collective-permute-start(bf16[640,256]{1,0:T(8,128)(2,1)S(1)} %pick_rows.4), channel_id=1, source_target_pairs={{0,4},{12,8},{1,5},{13,9},{2,6},{14,10},{3,7},{15,11},{16,20},{28,... | collective-permute-start | bytes 983048 | tf_op jit(solution)/shard_map/ppermute | solution.py:326
  18.1 12.1 %copy-start = (bf16[256,2304]{1,0:T(8,128)(2,1)S(1)}, bf16[256,2304]{1,0:T(8,128)(2,1)}, u32[]{:S(2)}) copy-start(bf16[256,2304]{1,0:T(8,128)(2,1)} %refs_3_.3) | copy-start | bytes 3538948
  18.2 8.5 %collective-permute-start.8 = (s32[8,256]{1,0:T(8,128)S(1)}, s32[8,256]{1,0:T(8,128)S(1)}, u32[]{:S(2)}, u32[]{:S(2)}) collective-permute-start(s32[8,256]{1,0:T(8,128)S(1)} %place_rows.1.ids_ref), channel_id=1, source_target_pairs={{0,4},{4,0},{8,12},{12,8},{1,5},{5,1},{9,13},{13,9},{2,6},{6,2},{1... | collective-permute-start | bytes 24584 | tf_op jit(solution)/shard_map/ppermute | solution.py:310
  18.3 14.2 %collective-permute-start.4 = (bf16[640,256]{1,0:T(8,128)(2,1)S(1)}, bf16[640,256]{1,0:T(8,128)(2,1)S(1)}, u32[]{:S(2)}, u32[]{:S(2)}) collective-permute-start(bf16[640,256]{1,0:T(8,128)(2,1)S(1)} %pick_rows.5), channel_id=1, source_target_pairs={{0,9},{1,8},{12,5},{13,4},{2,11},{3,10},{14,7},{15,6},{16,25},{17,... | collective-permute-start | bytes 983048 | tf_op jit(solution)/shard_map/ppermute | solution.py:313
  25.3 15.5 %collective-permute-start.10 = (bf16[640,256]{1,0:T(8,128)(2,1)S(1)}, bf16[640,256]{1,0:T(8,128)(2,1)S(1)}, u32[]{:S(2)}, u32[]{:S(2)}) collective-permute-start(bf16[640,256]{1,0:T(8,128)(2,1)S(1)} %add.16), channel_id=1, source_target_pairs={{4,12},{8,0},{5,13},{9,1},{6,14},{10,2},{7,15},{11,3},{20,28},{24,... | collective-permute-start | bytes 983048 | tf_op jit(solution)/shard_map/ppermute | solution.py:326
  27.5 16.8 %collective-permute-start.9 = (bf16[640,256]{1,0:T(8,128)(2,1)S(1)}, bf16[640,256]{1,0:T(8,128)(2,1)S(1)}, u32[]{:S(2)}, u32[]{:S(2)}) collective-permute-start(bf16[640,256]{1,0:T(8,128)(2,1)S(1)} %pick_rows.7), channel_id=1, source_target_pairs={{0,4},{4,0},{8,12},{12,8},{1,5},{5,1},{9,13},{13,9},{2,6},{6,2},{1... | collective-permute-start | bytes 983048 | tf_op jit(solution)/shard_map/ppermute | solution.py:326
  30.3 2.3 %collective-permute-start.7 = (bf16[16,2304]{1,0:T(8,128)(2,1)S(1)}, bf16[16,2304]{1,0:T(8,128)(2,1)S(1)}, u32[]{:S(2)}, u32[]{:S(2)}) collective-permute-start(bf16[16,2304]{1,0:T(8,128)(2,1)S(1)} %slice.6), channel_id=1, source_target_pairs={{0,1},{4,5},{8,9},{12,13},{2,3},{6,7},{10,11},{14,15},{16,17},{20,... | collective-permute-start | bytes 221192 | tf_op jit(solution)/shard_map/ppermute | solution.py:409
  44.5 10.1 %collective-permute-start.12 = (bf16[640,256]{1,0:T(8,128)(2,1)S(1)}, bf16[640,256]{1,0:T(8,128)(2,1)S(1)}, u32[]{:S(2)}, u32[]{:S(2)}) collective-permute-start(bf16[640,256]{1,0:T(8,128)(2,1)S(1)} %merge.1.refs_1_), channel_id=1, source_target_pairs={{0,2},{2,0},{1,3},{3,1},{4,6},{6,4},{5,7},{7,5},{8,10},{10,8},{9,1... | collective-permute-start | bytes 983048 | tf_op jit(solution)/shard_map/ppermute | solution.py:420
  46.0 2.9 %collective-permute-start.13 = (bf16[640,128]{1,0:T(8,128)(2,1)S(1)}, bf16[640,128]{1,0:T(8,128)(2,1)S(1)}, u32[]{:S(2)}, u32[]{:S(2)}) collective-permute-start(bf16[640,128]{1,0:T(8,128)(2,1)S(1)} %slice.8), channel_id=1, source_target_pairs={{0,1},{2,3},{4,5},{6,7},{8,9},{10,11},{12,13},{14,15},{16,17},{18,... | collective-permute-start | bytes 491528 | tf_op jit(solution)/shard_map/ppermute | solution.py:433
  47.4 7.2 %collective-permute-start.11 = (bf16[640,128]{1,0:T(8,128)(2,1)S(1)}, bf16[640,128]{1,0:T(8,128)(2,1)S(1)}, u32[]{:S(2)}, u32[]{:S(2)}) collective-permute-start(bf16[640,128]{1,0:T(8,128)(2,1)S(1)} %slice.8), channel_id=1, source_target_pairs={{0,3},{2,1},{4,7},{6,5},{8,11},{10,9},{12,15},{14,13},{16,19},{18,... | collective-permute-start | bytes 491528 | tf_op jit(solution)/shard_map/ppermute | solution.py:433
  54.6 8.0 %copy-start.1 = (f32[4,2304]{1,0:T(4,128)S(1)}, f32[4,2304]{1,0:T(4,128)}, u32[]{:S(2)}) copy-start(f32[4,2304]{1,0:T(4,128)} %refs_4_.1) | copy-start | bytes 110596
  58.8 3.8 %collective-permute-start.14 = (f32[8,272]{1,0:T(8,128)S(1)}, f32[8,272]{1,0:T(8,128)S(1)}, u32[]{:S(2)}, u32[]{:S(2)}) collective-permute-start(f32[8,272]{1,0:T(8,128)S(1)} %get-tuple-element.37.refs_0_), channel_id=1, source_target_pairs={{0,2},{2,0},{1,3},{3,1},{4,6},{6,4},{5,7},{7,5},{8,10},{10,8},{9,1... | collective-permute-start | bytes 26120 | tf_op jit(solution)/shard_map/ppermute | solution.py:475

commit v10 on v9

--- a/solution.py
+++ b/solution.py
@@ -335,22 +335,24 @@
     inward = send(rows_3, (0, 1), (3, 2))
     across = send(rows_3, (1, 2), (2, 1))
     rows_2 = pick(after(second, rows_3))
-    past = crossing(rows_2, [(m, r, m ^ 2, r ^ 1) for m in (0, 3) for r in range(2)])
     stored, settled = lax.optimization_barrier((after(stored, rows_2), settled))
     rows_1 = pick(ask(stored, 1))
     own = pick(stored)
-    onward = after(rows_2, own, across) + inward
+    onward = after(rows_2, rows_1, own) + inward
+    onward = after(onward, across)
+    rows_1, rows_2 = after(rows_1, onward), after(rows_2, onward)
     other = meanwhile(onward)
     onward = send(onward, (1, 3), (2, 0))
     beside = send(rows_1, (0, 1), (1, 0), (2, 3), (3, 2))
-    own, other = lax.optimization_barrier((own + past, other))
+    past = crossing(rows_2, [(m, r, m ^ 2, r ^ 1) for m in (0, 3) for r in range(2)])
+    own, other = lax.optimization_barrier((own + onward, other))
     memory = pl.pallas_call(
         merge_kernel,
         in_specs=[pl.BlockSpec(memory_space=pltpu.VMEM)] * 4,
         out_shape=block,
         compiler_params=limit(4),
         name="merge",
-    )(own, across, beside, onward)
+    )(own, across, beside, past)
     return memory, other, settled
 
 

time: 67 us -> 67.5 us (level)
  starting transfers between devices: 24.6 us -> 27.1 us
  waiting for transfers between devices: 19.9 us -> 17.8 us
    ppermute x4, starting transfers between devices: 9.47 us -> 4.09 us  [send(): return lax.ppermute(x, 'mem', pairs)]
    ppermute x2, starting transfers between devices: 3.21 us -> 6.39 us  [crossing(): lax.ppermute(x, ('mem', 'rep'), [(2 * a + b, 2 * c + d) for a, b, c, d in...]
    ppermute x4, waiting for transfers between devices: 14.6 us -> 12.3 us  [send(): return lax.ppermute(x, 'mem', pairs)]
    ppermute x2, waiting for transfers between devices: 0.01 us -> 2.09 us  [ask(): return lax.ppermute(ids, 'mem', [(i, i ^ x) for i in range(4)])]
    ppermute x2, starting transfers between devices: 5.19 us -> 7.27 us  [ask(): return lax.ppermute(ids, 'mem', [(i, i ^ x) for i in range(4)])]
    ppermute x1, starting transfers between devices: 1.29 us -> 2.49 us  [meanwhile(): return lax.ppermute(tail, ('mem', 'rep'), needed)]
    ppermute x2, waiting for transfers between devices: 2.15 us -> 1.21 us  [crossing(): lax.ppermute(x, ('mem', 'rep'), [(2 * a + b, 2 * c + d) for a, b, c, d in...]
    ppermute x1, waiting for transfers between devices: 3.12 us -> 2.21 us  [shards(): lax.ppermute(stats, 'tp', [(i, (i + s) % tps) for i in range(tps)])]
  transfers between devices with their start and end apart: 15 -> 15, of which waited for: 6 -> 5; matrix products, arithmetic and copies ran while one was open for 0% -> 0% of each run, Pallas kernels for 20% -> 20%
where the time goes in v10:
time: 67.5 us; the launch traced here: 67.1 us
  starting transfers between devices  27.1 us (40%)
  Pallas kernels  21.5 us (32%)
  waiting for transfers between devices  17.8 us (26%)
    ppermute x4, waiting for transfers between devices, send(): return lax.ppermute(x, 'mem', pairs)  12.3 us
    ppermute x2, starting transfers between devices, ask(): return lax.ppermute(ids, 'mem', [(i, i ^ x) for i in range(4)])  7.27 us
    ppermute x2, starting transfers between devices, crossing(): lax.ppermute(x, ('mem', 'rep'), [(2 * a + b, 2 * c + d) for a, b, c, d in...  6.39 us
    pallas_call x1, Pallas kernels, shards(): pl.pallas_call(functools.partial(project_kernel, (0,), tps), in_specs=[sm...  5.6 us
    pallas_call x1, Pallas kernels, shards(): pl.pallas_call(functools.partial(project_kernel, tuple(range(1, tps)), tp...  4.24 us
    ppermute x4, starting transfers between devices, send(): return lax.ppermute(x, 'mem', pairs)  4.09 us
    pallas_call x1, Pallas kernels, shards(): pl.pallas_call(functools.partial(finish_kernel, tps, step), in_specs=[sme...  3.96 us
    pallas_call x4, Pallas kernels, pick(): pl.pallas_call(pick_kernel, in_specs=[pl.BlockSpec(memory_space=pltpu.SME...  3.45 us
  transfers between devices with their start and end apart: 15, of which 5 were waited for; matrix products, arithmetic and copies ran while one was open for 0% of the time, Pallas kernels for 20%

profile of v10, /device:TPU:0, one launch (start us, length us, event | category | flops | bytes accessed | tf_op | source)
XLA Modules:
  0.0 67.1 jit_solution(15097332838779638210)
XLA Ops:
  0.0 0.5 collective-permute-start.2
  0.5 0.1 collective-permute-start.3
  0.5 1.3 %place_rows.1.ids_ref = s32[8,256]{1,0:T(8,128)S(1)} custom-call(s32[8,256]{1,0:T(8,128)} %bitcast.11, s32[32,128]{1,0:T(8,128)} %bitcast.10), custom_call_target="tpu_custom_call" | custom-call | tf_op jit(solution)/shard_map/place_rows/pallas_call | solution.py:378
  1.9 5.1 %collective-permute-start = (s32[8,256]{1,0:T(8,128)S(1)}, s32[8,256]{1,0:T(8,128)S(1)}, u32[]{:S(2)}, u32[]{:S(2)}) collective-permute-start(s32[8,256]{1,0:T(8,128)S(1)} %place_rows.1.ids_ref), channel_id=1, source_target_pairs={{0,12},{4,8},{8,4},{12,0},{1,13},{5,9},{9,5},{13,1},{2,14},{6,10},... | collective-permute-start | bytes 24584 | tf_op jit(solution)/shard_map/ppermute | solution.py:310
  7.0 0.0 collective-permute-start.1
  7.0 2.7 %decode_tables.1.table_ref = bf16[8,80,1024]{2,1,0:T(8,128)(2,1)S(1)} custom-call(bf16[8,80,1024]{2,1,0:T(8,128)(2,1)} %bitcast.8, bf16[5,8,1024]{2,1,0:T(8,128)(2,1)} %bitcast.9), custom_call_target="tpu_custom_call" | custom-call | tf_op jit(solution)/shard_map/decode_tables/pallas_call | solution.py:392
  9.7 0.0 collective-permute-done.ids_ref
  9.7 1.2 %collective-permute-done.1.ids_ref = s32[8,256]{1,0:T(8,128)S(1)} collective-permute-done((s32[8,256]{1,0:T(8,128)S(1)}, s32[8,256]{1,0:T(8,128)S(1)}, u32[]{:S(2)}, u32[]{:S(2)}) %collective-permute-start.1) | collective-permute-done | bytes 8224 | tf_op jit(solution)/shard_map/ppermute | solution.py:313
  10.9 0.9 %pick_rows.4 = bf16[640,256]{1,0:T(8,128)(2,1)S(1)} custom-call(s32[1]{0:T(128)} %bitcast.3.base_ref, s32[8,256]{1,0:T(8,128)S(1)} %collective-permute-done.ids_ref, bf16[8,80,1024]{2,1,0:T(8,128)(2,1)S(1)} %decode_tables.1.table_ref), custom_call_target="tpu_custom_call" | custom-call | tf_op jit(solution)/shard_map/pick_rows/pallas_call | solution.py:316
  11.8 2.0 %collective-permute-start.5 = (bf16[640,256]{1,0:T(8,128)(2,1)S(1)}, bf16[640,256]{1,0:T(8,128)(2,1)S(1)}, u32[]{:S(2)}, u32[]{:S(2)}) collective-permute-start(bf16[640,256]{1,0:T(8,128)(2,1)S(1)} %pick_rows.4), channel_id=1, source_target_pairs={{0,4},{12,8},{1,5},{13,9},{2,6},{14,10},{3,7},{15,11},{16,20},{28,... | collective-permute-start | bytes 983048 | tf_op jit(solution)/shard_map/ppermute | solution.py:326
  13.9 0.7 %collective-permute-start.6 = (bf16[640,256]{1,0:T(8,128)(2,1)S(1)}, bf16[640,256]{1,0:T(8,128)(2,1)S(1)}, u32[]{:S(2)}, u32[]{:S(2)}) collective-permute-start(bf16[640,256]{1,0:T(8,128)(2,1)S(1)} %pick_rows.4), channel_id=1, source_target_pairs={{4,8},{8,4},{5,9},{9,5},{6,10},{10,6},{7,11},{11,7},{20,24},{24,20... | collective-permute-start | bytes 983048 | tf_op jit(solution)/shard_map/ppermute | solution.py:326
  14.6 0.9 %pick_rows.5 = bf16[640,256]{1,0:T(8,128)(2,1)S(1)} custom-call(s32[1]{0:T(128)} %bitcast.3.base_ref, s32[8,256]{1,0:T(8,128)S(1)} %collective-permute-done.1.ids_ref, bf16[8,80,1024]{2,1,0:T(8,128)(2,1)S(1)} %decode_tables.1.table_ref), custom_call_target="tpu_custom_call" | custom-call | tf_op jit(solution)/shard_map/pick_rows/pallas_call | solution.py:316
  15.4 0.0 copy-start
  15.4 0.0 collective-permute-done.2.refs_4_
  15.4 0.0 collective-permute-done.3.refs_5_
  15.5 2.2 %collective-permute-start.4 = (s32[8,256]{1,0:T(8,128)S(1)}, s32[8,256]{1,0:T(8,128)S(1)}, u32[]{:S(2)}, u32[]{:S(2)}) collective-permute-start(s32[8,256]{1,0:T(8,128)S(1)} %place_rows.1.ids_ref), channel_id=1, source_target_pairs={{0,4},{4,0},{8,12},{12,8},{1,5},{5,1},{9,13},{13,9},{2,6},{6,2},{1... | collective-permute-start | bytes 24584 | tf_op jit(solution)/shard_map/ppermute | solution.py:310
  17.6 0.9 %pick_rows.6 = bf16[640,256]{1,0:T(8,128)(2,1)S(1)} custom-call(s32[1]{0:T(128)} %bitcast.3.base_ref, s32[8,256]{1,0:T(8,128)S(1)} %place_rows.1.ids_ref, bf16[8,80,1024]{2,1,0:T(8,128)(2,1)S(1)} %decode_tables.1.table_ref), custom_call_target="tpu_custom_call" | custom-call | tf_op jit(solution)/shard_map/pick_rows/pallas_call | solution.py:316
  18.5 2.1 %collective-permute-done.4.ids_ref = s32[8,256]{1,0:T(8,128)S(1)} collective-permute-done((s32[8,256]{1,0:T(8,128)S(1)}, s32[8,256]{1,0:T(8,128)S(1)}, u32[]{:S(2)}, u32[]{:S(2)}) %collective-permute-start.4) | collective-permute-done | bytes 8224 | tf_op jit(solution)/shard_map/ppermute | solution.py:310
  20.6 0.9 %pick_rows.7 = bf16[640,256]{1,0:T(8,128)(2,1)S(1)} custom-call(s32[1]{0:T(128)} %bitcast.3.base_ref, s32[8,256]{1,0:T(8,128)S(1)} %collective-permute-done.4.ids_ref, bf16[8,80,1024]{2,1,0:T(8,128)(2,1)S(1)} %decode_tables.1.table_ref), custom_call_target="tpu_custom_call" | custom-call | tf_op jit(solution)/shard_map/pick_rows/pallas_call | solution.py:316
  21.4 0.0 collective-permute-done.5
  21.4 0.1 add.15
  21.5 0.0 collective-permute-done.6.refs_1_
  21.5 1.3 %collective-permute-start.7 = (bf16[640,256]{1,0:T(8,128)(2,1)S(1)}, bf16[640,256]{1,0:T(8,128)(2,1)S(1)}, u32[]{:S(2)}, u32[]{:S(2)}) collective-permute-start(bf16[640,256]{1,0:T(8,128)(2,1)S(1)} %add.15), channel_id=1, source_target_pairs={{4,12},{8,0},{5,13},{9,1},{6,14},{10,2},{7,15},{11,3},{20,28},{24,... | collective-permute-start | bytes 983048 | tf_op jit(solution)/shard_map/ppermute | solution.py:326
  22.8 6.4 %collective-permute-start.10 = (bf16[640,256]{1,0:T(8,128)(2,1)S(1)}, bf16[640,256]{1,0:T(8,128)(2,1)S(1)}, u32[]{:S(2)}, u32[]{:S(2)}) collective-permute-start(bf16[640,256]{1,0:T(8,128)(2,1)S(1)} %pick_rows.5), channel_id=1, source_target_pairs={{0,9},{1,8},{12,5},{13,4},{2,11},{3,10},{14,7},{15,6},{16,25},{17,... | collective-permute-start | bytes 983048 | tf_op jit(solution)/shard_map/ppermute | solution.py:313
  29.2 0.1 collective-permute-start.9
  29.3 0.0 copy-done
  29.3 2.5 %collective-permute-start.8 = (bf16[16,2304]{1,0:T(8,128)(2,1)S(1)}, bf16[16,2304]{1,0:T(8,128)(2,1)S(1)}, u32[]{:S(2)}, u32[]{:S(2)}) collective-permute-start(bf16[16,2304]{1,0:T(8,128)(2,1)S(1)} %slice.6), channel_id=1, source_target_pairs={{0,1},{4,5},{8,9},{12,13},{2,3},{6,7},{10,11},{14,15},{16,17},{20,... | collective-permute-start | bytes 221192 | tf_op jit(solution)/shard_map/ppermute | solution.py:411
  31.8 10.7 %collective-permute-done.7 = bf16[640,256]{1,0:T(8,128)(2,1)S(1)} collective-permute-done((bf16[640,256]{1,0:T(8,128)(2,1)S(1)}, bf16[640,256]{1,0:T(8,128)(2,1)S(1)}, u32[]{:S(2)}, u32[]{:S(2)}) %collective-permute-start.7) | collective-permute-done | bytes 327712 | tf_op jit(solution)/shard_map/ppermute | solution.py:326
  42.5 0.1 add.16.refs_0_
  42.6 0.0 collective-permute-done.8.refs_5_
  42.6 0.0 collective-permute-done.10.refs_3_
  42.7 1.6 %collective-permute-done.9.refs_2_ = bf16[640,256]{1,0:T(8,128)(2,1)S(1)} collective-permute-done((bf16[640,256]{1,0:T(8,128)(2,1)S(1)}, bf16[640,256]{1,0:T(8,128)(2,1)S(1)}, u32[]{:S(2)}, u32[]{:S(2)}) %collective-permute-start.9) | collective-permute-done | bytes 327712 | tf_op jit(solution)/shard_map/ppermute | solution.py:326
  44.3 0.2 merge.1.refs_1_
  44.4 1.6 %collective-permute-start.12 = (bf16[640,256]{1,0:T(8,128)(2,1)S(1)}, bf16[640,256]{1,0:T(8,128)(2,1)S(1)}, u32[]{:S(2)}, u32[]{:S(2)}) collective-permute-start(bf16[640,256]{1,0:T(8,128)(2,1)S(1)} %merge.1.refs_1_), channel_id=1, source_target_pairs={{0,2},{2,0},{1,3},{3,1},{4,6},{6,4},{5,7},{7,5},{8,10},{10,8},{9,1... | collective-permute-start | bytes 983048 | tf_op jit(solution)/shard_map/ppermute | solution.py:422
  46.0 1.6 %collective-permute-start.13 = (bf16[640,128]{1,0:T(8,128)(2,1)S(1)}, bf16[640,128]{1,0:T(8,128)(2,1)S(1)}, u32[]{:S(2)}, u32[]{:S(2)}) collective-permute-start(bf16[640,128]{1,0:T(8,128)(2,1)S(1)} %slice.8), channel_id=1, source_target_pairs={{0,1},{2,3},{4,5},{6,7},{8,9},{10,11},{12,13},{14,15},{16,17},{18,... | collective-permute-start | bytes 491528 | tf_op jit(solution)/shard_map/ppermute | solution.py:435
  47.6 1.6 %collective-permute-start.11 = (bf16[640,128]{1,0:T(8,128)(2,1)S(1)}, bf16[640,128]{1,0:T(8,128)(2,1)S(1)}, u32[]{:S(2)}, u32[]{:S(2)}) collective-permute-start(bf16[640,128]{1,0:T(8,128)(2,1)S(1)} %slice.8), channel_id=1, source_target_pairs={{0,3},{2,1},{4,7},{6,5},{8,11},{10,9},{12,15},{14,13},{16,19},{18,... | collective-permute-start | bytes 491528 | tf_op jit(solution)/shard_map/ppermute | solution.py:435
  49.3 0.1 pad_add_fusion.where_ref
  49.3 0.0 collective-permute-done.13.refs_0_
  49.3 5.6 %project_own.1 = (f32[2,272,1152]{2,1,0:T(8,128)S(1)}, f32[2,272,1152]{2,1,0:T(8,128)S(1)}, bf16[2,2,640,1152]{3,2,1,0:T(8,128)(2,1)S(1)}) custom-call(s32[2]{0:T(128)S(1)} %pad_add_fusion.where_ref, bf16[640,128]{1,0:T(8,128)(2,1)S(1)} %collective-permute-done.13.refs_0_, bf16[640,256]{1,0:T(8,128)(2,1)S(1)} %merge.1.refs_1_, bf16[1280,1152]{1,0:T(8,128)(2,1)} %refs_2_.1, ...), custom_call_target="tpu_custom_call" | custom-call | tf_op jit(solution)/shard_map/project_own/pallas_call | solution.py:441
  55.0 0.0 collective-permute-done.11.refs_0_
  55.0 0.0 collective-permute-done.12.refs_1_
  55.0 0.0 copy-start.1
  55.0 4.2 %project_others.1 = (f32[2,272,1152]{2,1,0:T(8,128)}, f32[8,272]{1,0:T(8,128)S(1)}) custom-call(s32[2]{0:T(128)S(1)} %pad_add_fusion.where_ref, bf16[640,128]{1,0:T(8,128)(2,1)S(1)} %collective-permute-done.11.refs_0_, bf16[640,256]{1,0:T(8,128)(2,1)S(1)} %collective-permute-done.12.refs_1_, bf16[2,2,640,1152]{3,2,1,0:T(8,128)(2,1)S(1)} %get-tuple-element.39.refs_2_, ...), custom_call_target="tpu_custom_call" | custom-call | tf_op jit(solution)/shard_map/project_others/pallas_call | solution.py:454
  59.2 1.6 %collective-permute-start.14 = (f32[8,272]{1,0:T(8,128)S(1)}, f32[8,272]{1,0:T(8,128)S(1)}, u32[]{:S(2)}, u32[]{:S(2)}) collective-permute-start(f32[8,272]{1,0:T(8,128)S(1)} %get-tuple-element.43.refs_0_), channel_id=1, source_target_pairs={{0,2},{2,0},{1,3},{3,1},{4,6},{6,4},{5,7},{7,5},{8,10},{10,8},{9,1... | collective-permute-start | bytes 26120 | tf_op jit(solution)/shard_map/ppermute | solution.py:477
  60.8 2.2 %collective-permute-done.14.refs_1_ = f32[8,272]{1,0:T(8,128)S(1)} collective-permute-done((f32[8,272]{1,0:T(8,128)S(1)}, f32[8,272]{1,0:T(8,128)S(1)}, u32[]{:S(2)}, u32[]{:S(2)}) %collective-permute-start.14) | collective-permute-done | bytes 8736 | tf_op jit(solution)/shard_map/ppermute | solution.py:477
  63.0 0.0 copy-done.1
  63.0 4.0 %finish.1 = bf16[256,2304]{1,0:T(8,128)(2,1)} custom-call(s32[1]{0:T(128)} %bitcast.keep_ref, f32[8,272]{1,0:T(8,128)S(1)} %get-tuple-element.43.refs_0_, f32[8,272]{1,0:T(8,128)S(1)} %collective-permute-done.14.refs_1_, f32[2,272,1152]{2,1,0:T(8,128)} %get-tuple-element.44.refs_2_, bf16[256,2304]{1,0:T(8,128)(2,1)S(1)} %copy-done, f32[4,2304]{1,0:T(4,128)S(1)} %copy-done.1), custom_call_target="tpu_custom_call" | custom-call | tf_op jit(solution)/shard_map/finish/pallas_call | solution.py:483
  (2 shorter events, 0.0 us)
Async XLA Ops:
  0.0 15.4 %collective-permute-start.2 = (bf16[1280,1152]{1,0:T(8,128)(2,1)}, bf16[1280,1152]{1,0:T(8,128)(2,1)}, u32[]{:S(2)}, u32[]{:S(2)}) collective-permute-start(bf16[1280,1152]{1,0:T(8,128)(2,1)} %refs_2_.1), channel_id=1, source_target_pairs={{0,1},{1,0},{2,3},{3,2},{4,5},{5,4},{6,7},{7,6},{8,9},{9,8},{10,11... | collective-permute-start | bytes 8847368 | tf_op jit(solution)/shard_map/ppermute | solution.py:405
  0.5 15.0 %collective-permute-start.3 = (bf16[1280,1152]{1,0:T(8,128)(2,1)}, bf16[1280,1152]{1,0:T(8,128)(2,1)}, u32[]{:S(2)}, u32[]{:S(2)}) collective-permute-start(bf16[1280,1152]{1,0:T(8,128)(2,1)} %refs_3_.2), channel_id=1, source_target_pairs={{0,1},{1,0},{2,3},{3,2},{4,5},{5,4},{6,7},{7,6},{8,9},{9,8},{10,11... | collective-permute-start | bytes 8847368 | tf_op jit(solution)/shard_map/ppermute | solution.py:406
  1.9 7.9 %collective-permute-start = (s32[8,256]{1,0:T(8,128)S(1)}, s32[8,256]{1,0:T(8,128)S(1)}, u32[]{:S(2)}, u32[]{:S(2)}) collective-permute-start(s32[8,256]{1,0:T(8,128)S(1)} %place_rows.1.ids_ref), channel_id=1, source_target_pairs={{0,12},{4,8},{8,4},{12,0},{1,13},{5,9},{9,5},{13,1},{2,14},{6,10},... | collective-permute-start | bytes 24584 | tf_op jit(solution)/shard_map/ppermute | solution.py:310
  7.0 4.0 %collective-permute-start.1 = (s32[8,256]{1,0:T(8,128)S(1)}, s32[8,256]{1,0:T(8,128)S(1)}, u32[]{:S(2)}, u32[]{:S(2)}) collective-permute-start(s32[8,256]{1,0:T(8,128)S(1)} %place_rows.1.ids_ref), channel_id=1, source_target_pairs={{0,8},{1,9},{4,13},{5,12},{8,1},{9,0},{12,4},{13,5},{2,10},{3,11},... | collective-permute-start | bytes 24584 | tf_op jit(solution)/shard_map/ppermute | solution.py:313
  11.8 9.6 %collective-permute-start.5 = (bf16[640,256]{1,0:T(8,128)(2,1)S(1)}, bf16[640,256]{1,0:T(8,128)(2,1)S(1)}, u32[]{:S(2)}, u32[]{:S(2)}) collective-permute-start(bf16[640,256]{1,0:T(8,128)(2,1)S(1)} %pick_rows.4), channel_id=1, source_target_pairs={{0,4},{12,8},{1,5},{13,9},{2,6},{14,10},{3,7},{15,11},{16,20},{28,... | collective-permute-start | bytes 983048 | tf_op jit(solution)/shard_map/ppermute | solution.py:326
  13.9 7.7 %collective-permute-start.6 = (bf16[640,256]{1,0:T(8,128)(2,1)S(1)}, bf16[640,256]{1,0:T(8,128)(2,1)S(1)}, u32[]{:S(2)}, u32[]{:S(2)}) collective-permute-start(bf16[640,256]{1,0:T(8,128)(2,1)S(1)} %pick_rows.4), channel_id=1, source_target_pairs={{4,8},{8,4},{5,9},{9,5},{6,10},{10,6},{7,11},{11,7},{20,24},{24,20... | collective-permute-start | bytes 983048 | tf_op jit(solution)/shard_map/ppermute | solution.py:326
  15.4 13.9 %copy-start = (bf16[256,2304]{1,0:T(8,128)(2,1)S(1)}, bf16[256,2304]{1,0:T(8,128)(2,1)}, u32[]{:S(2)}) copy-start(bf16[256,2304]{1,0:T(8,128)(2,1)} %refs_3_.3) | copy-start | bytes 3538948
  15.5 5.1 %collective-permute-start.4 = (s32[8,256]{1,0:T(8,128)S(1)}, s32[8,256]{1,0:T(8,128)S(1)}, u32[]{:S(2)}, u32[]{:S(2)}) collective-permute-start(s32[8,256]{1,0:T(8,128)S(1)} %place_rows.1.ids_ref), channel_id=1, source_target_pairs={{0,4},{4,0},{8,12},{12,8},{1,5},{5,1},{9,13},{13,9},{2,6},{6,2},{1... | collective-permute-start | bytes 24584 | tf_op jit(solution)/shard_map/ppermute | solution.py:310
  21.5 21.0 %collective-permute-start.7 = (bf16[640,256]{1,0:T(8,128)(2,1)S(1)}, bf16[640,256]{1,0:T(8,128)(2,1)S(1)}, u32[]{:S(2)}, u32[]{:S(2)}) collective-permute-start(bf16[640,256]{1,0:T(8,128)(2,1)S(1)} %add.15), channel_id=1, source_target_pairs={{4,12},{8,0},{5,13},{9,1},{6,14},{10,2},{7,15},{11,3},{20,28},{24,... | collective-permute-start | bytes 983048 | tf_op jit(solution)/shard_map/ppermute | solution.py:326
  22.8 19.8 %collective-permute-start.10 = (bf16[640,256]{1,0:T(8,128)(2,1)S(1)}, bf16[640,256]{1,0:T(8,128)(2,1)S(1)}, u32[]{:S(2)}, u32[]{:S(2)}) collective-permute-start(bf16[640,256]{1,0:T(8,128)(2,1)S(1)} %pick_rows.5), channel_id=1, source_target_pairs={{0,9},{1,8},{12,5},{13,4},{2,11},{3,10},{14,7},{15,6},{16,25},{17,... | collective-permute-start | bytes 983048 | tf_op jit(solution)/shard_map/ppermute | solution.py:313
  29.2 15.0 %collective-permute-start.9 = (bf16[640,256]{1,0:T(8,128)(2,1)S(1)}, bf16[640,256]{1,0:T(8,128)(2,1)S(1)}, u32[]{:S(2)}, u32[]{:S(2)}) collective-permute-start(bf16[640,256]{1,0:T(8,128)(2,1)S(1)} %pick_rows.7), channel_id=1, source_target_pairs={{0,4},{4,0},{8,12},{12,8},{1,5},{5,1},{9,13},{13,9},{2,6},{6,2},{1... | collective-permute-start | bytes 983048 | tf_op jit(solution)/shard_map/ppermute | solution.py:326
  29.3 13.3 %collective-permute-start.8 = (bf16[16,2304]{1,0:T(8,128)(2,1)S(1)}, bf16[16,2304]{1,0:T(8,128)(2,1)S(1)}, u32[]{:S(2)}, u32[]{:S(2)}) collective-permute-start(bf16[16,2304]{1,0:T(8,128)(2,1)S(1)} %slice.6), channel_id=1, source_target_pairs={{0,1},{4,5},{8,9},{12,13},{2,3},{6,7},{10,11},{14,15},{16,17},{20,... | collective-permute-start | bytes 221192 | tf_op jit(solution)/shard_map/ppermute | solution.py:411
  44.4 10.5 %collective-permute-start.12 = (bf16[640,256]{1,0:T(8,128)(2,1)S(1)}, bf16[640,256]{1,0:T(8,128)(2,1)S(1)}, u32[]{:S(2)}, u32[]{:S(2)}) collective-permute-start(bf16[640,256]{1,0:T(8,128)(2,1)S(1)} %merge.1.refs_1_), channel_id=1, source_target_pairs={{0,2},{2,0},{1,3},{3,1},{4,6},{6,4},{5,7},{7,5},{8,10},{10,8},{9,1... | collective-permute-start | bytes 983048 | tf_op jit(solution)/shard_map/ppermute | solution.py:422
  46.0 3.4 %collective-permute-start.13 = (bf16[640,128]{1,0:T(8,128)(2,1)S(1)}, bf16[640,128]{1,0:T(8,128)(2,1)S(1)}, u32[]{:S(2)}, u32[]{:S(2)}) collective-permute-start(bf16[640,128]{1,0:T(8,128)(2,1)S(1)} %slice.8), channel_id=1, source_target_pairs={{0,1},{2,3},{4,5},{6,7},{8,9},{10,11},{12,13},{14,15},{16,17},{18,... | collective-permute-start | bytes 491528 | tf_op jit(solution)/shard_map/ppermute | solution.py:435
  47.6 7.3 %collective-permute-start.11 = (bf16[640,128]{1,0:T(8,128)(2,1)S(1)}, bf16[640,128]{1,0:T(8,128)(2,1)S(1)}, u32[]{:S(2)}, u32[]{:S(2)}) collective-permute-start(bf16[640,128]{1,0:T(8,128)(2,1)S(1)} %slice.8), channel_id=1, source_target_pairs={{0,3},{2,1},{4,7},{6,5},{8,11},{10,9},{12,15},{14,13},{16,19},{18,... | collective-permute-start | bytes 491528 | tf_op jit(solution)/shard_map/ppermute | solution.py:435
  55.0 8.0 %copy-start.1 = (f32[4,2304]{1,0:T(4,128)S(1)}, f32[4,2304]{1,0:T(4,128)}, u32[]{:S(2)}) copy-start(f32[4,2304]{1,0:T(4,128)} %refs_4_.1) | copy-start | bytes 110596
  59.2 3.8 %collective-permute-start.14 = (f32[8,272]{1,0:T(8,128)S(1)}, f32[8,272]{1,0:T(8,128)S(1)}, u32[]{:S(2)}, u32[]{:S(2)}) collective-permute-start(f32[8,272]{1,0:T(8,128)S(1)} %get-tuple-element.43.refs_0_), channel_id=1, source_target_pairs={{0,2},{2,0},{1,3},{3,1},{4,6},{6,4},{5,7},{7,5},{8,10},{10,8},{9,1... | collective-permute-start | bytes 26120 | tf_op jit(solution)/shard_map/ppermute | solution.py:477

commit v11 on v8

--- a/solution.py
+++ b/solution.py
@@ -67,8 +67,49 @@
         out_ref[head : head + 1, :] = jnp.sum(chosen, axis=0, keepdims=True).astype(I32)
 
 
-def decode_kernel(codes_hbm, scales_hbm, out_ref, codes_ref, scales_ref, sems):
-    heads, width, rows = codes_ref.shape
+def rotation_twice(width):
+    entry = iota((width, 2 * width), 0)
+    column = iota((width, 2 * width), 1)
+    column = jnp.where(column < width, column, column - width)
+    parity = entry & column & 15
+    parity = parity ^ (parity >> 2)
+    parity = (parity ^ (parity >> 1)) & 1
+    same = (entry >> 4) == (column >> 4)
+    return jnp.where(same, 0.25 - 0.5 * parity.astype(F32), 0.0).astype(BF16)
+
+
+def decoded_table(rotation, codes, scales):
+    spread = [jnp.broadcast_to(s, (16, codes.shape[1])) for s in scales]
+    scaled = codes.astype(F32) * jnp.concatenate(spread, axis=0)
+    upper = scaled.astype(BF16)
+    lower = (scaled - upper.astype(F32)).astype(BF16)
+    return dot(rotation, jnp.concatenate([upper, lower], axis=0)).astype(BF16)
+
+
+def lend_kernel(rep_ref, codes_hbm, scales_hbm, out_ref, codes_ref, scales_ref, wide_ref, sems):
+    count, width, _ = out_ref.shape
+    blocks = scales_ref.shape[0]
+    begin = rep_ref[0] * count
+    scales_copy = pltpu.make_async_copy(scales_hbm, scales_ref, sems.at[count])
+    scales_copy.start()
+    copies = []
+    for n in range(count):
+        copies.append(
+            pltpu.make_async_copy(codes_hbm.at[begin + n], codes_ref.at[n], sems.at[n])
+        )
+        copies[-1].start()
+    rotation = rotation_twice(width)
+    scales_copy.wait()
+    wide_ref[...] = scales_ref[...].astype(F32)
+    for n in range(count):
+        copies[n].wait()
+        scales = [wide_ref[b, pl.ds(begin + n, 1), :] for b in range(blocks)]
+        out_ref[n] = decoded_table(rotation, codes_ref[n], scales)
+
+
+def decode_kernel(lend, rep_ref, codes_hbm, scales_hbm, out_ref, *refs):
+    codes_ref, scales_ref, sems = refs[-3:]
+    heads, width, _ = codes_ref.shape
     blocks = scales_ref.shape[0]
     scales_copy = pltpu.make_async_copy(scales_hbm, scales_ref, sems.at[heads])
     scales_copy.start()
@@ -78,48 +119,52 @@
             pltpu.make_async_copy(codes_hbm.at[head], codes_ref.at[head], sems.at[head])
         )
         copies[-1].start()
-    entry = iota((width, 2 * width), 0)
-    column = iota((width, 2 * width), 1)
-    column = jnp.where(column < width, column, column - width)
-    parity = entry & column & 15
-    parity = parity ^ (parity >> 2)
-    parity = (parity ^ (parity >> 1)) & 1
-    same = (entry >> 4) == (column >> 4)
-    rotation = jnp.where(same, 0.25 - 0.5 * parity.astype(F32), 0.0).astype(BF16)
+    rotation = rotation_twice(width)
     scales_copy.wait()
     for head in range(heads):
         copies[head].wait()
-        factors = jnp.concatenate(
-            [
-                jnp.broadcast_to(scales_ref[b, head : head + 1, :].astype(F32), (16, rows))
-                for b in range(blocks)
-            ],
-            axis=0,
-        )
-        scaled = codes_ref[head].astype(F32) * factors
-        upper = scaled.astype(BF16)
-        lower = (scaled - upper.astype(F32)).astype(BF16)
-        out_ref[head] = dot(rotation, jnp.concatenate([upper, lower], axis=0)).astype(BF16)
-
-
-def picked(local, table_ref, head):
-    rows = table_ref.shape[2]
-    hot = to_bf16(iota((rows, local.shape[1]), 0) == local[head : head + 1, :])
-    return dot(table_ref[head], hot).astype(BF16)
-
-
-def pick_kernel(base_ref, ids_ref, table_ref, out_ref):
-    heads, width, _ = table_ref.shape
-    local = ids_ref[...] - base_ref[0]
-    for head in range(heads):
-        out_ref[head * width : (head + 1) * width, :] = picked(local, table_ref, head)
-
-
-def merge_kernel(*refs):
-    total = refs[0][...].astype(F32)
-    for other in refs[1:-1]:
-        total = total + other[...].astype(F32)
-    refs[-1][...] = total.astype(BF16)
+        scales = [scales_ref[b, head : head + 1, :].astype(F32) for b in range(blocks)]
+        table = decoded_table(rotation, codes_ref[head], scales)
+        out_ref[head] = table
+        if lend and head >= heads // 2:
+            count = heads // 4
+            owner, at = divmod(head - heads // 2, count)
+
+            @pl.when(rep_ref[0] == owner)
+            def _(table=table, at=at):
+                refs[0][at] = table
+
+
+def picked(local, table):
+    hot = to_bf16(iota((table.shape[1], local.shape[1]), 0) == local)
+    return dot(table, hot)
+
+
+def pick_kernel(first, count, scalars_ref, ids_ref, table_ref, *refs):
+    out_ref = refs[-1]
+    width = table_ref.shape[1]
+    ids = ids_ref[...]
+    for n in range(count):
+        row = ids[first + n : first + n + 1, :]
+        value = picked(row - scalars_ref[0], table_ref[first + n])
+        if len(refs) > 1:
+            side, at = divmod(n, count // 2)
+            straight, swapped = refs[0][at], refs[1][at]
+            table = jnp.where(scalars_ref[2] == side, straight, swapped)
+            value = value + picked(row - scalars_ref[1], table)
+        out_ref[n * width : (n + 1) * width, :] = value.astype(BF16)
+
+
+def merge_kernel(beside_ref, *refs):
+    out_ref = refs[-1]
+    part = refs[0].shape[0]
+    parts = out_ref.shape[0] // part
+    for k in range(parts):
+        span = slice(k * part, (k + 1) * part)
+        total = beside_ref[span, :].astype(F32)
+        for other in refs[k:-1:parts]:
+            total = total + other[...].astype(F32)
+        out_ref[span, :] = total.astype(BF16)
 
 
 def project_kernel(shifts, count, where_ref, *refs):
@@ -278,13 +323,44 @@
     return pltpu.CompilerParams(vmem_limit_bytes=mib << 20)
 
 
-def scattered_sum(stored, decoded, here, meanwhile, settled):
+def pick(ids, table, scalars, *near, first=0, count=None):
+    heads, width, _ = table.shape
+    count = count or heads
+    return pl.pallas_call(
+        functools.partial(pick_kernel, first, count),
+        in_specs=[pl.BlockSpec(memory_space=pltpu.SMEM)]
+        + [pl.BlockSpec(memory_space=pltpu.VMEM)] * (2 + len(near)),
+        out_shape=jax.ShapeDtypeStruct((count * width, ids.shape[1]), BF16),
+        compiler_params=limit(8),
+        name="pick_rows",
+    )(scalars, ids, table, *near)
+
+
+def decode(codes, scales, rep, lend):
+    heads, width, rows = codes.shape
+    shapes = [jax.ShapeDtypeStruct((n, width, rows), BF16) for n in (heads, heads // 4)]
+    return pl.pallas_call(
+        functools.partial(decode_kernel, lend),
+        in_specs=[pl.BlockSpec(memory_space=pltpu.SMEM)] + [pl.BlockSpec(memory_space=pl.ANY)] * 2,
+        out_shape=shapes[: 1 + lend],
+        scratch_shapes=[
+            pltpu.VMEM(codes.shape, BF16),
+            pltpu.VMEM(scales.shape, BF16),
+            pltpu.SemaphoreType.DMA((heads + 1,)),
+        ],
+        compiler_params=limit(12),
+        name="decode_tables",
+    )(rep, in_hbm(codes), in_hbm(scales))
+
+
+def scattered_sum(stored, codes, scales, here, rep, meanwhile, settled):
     mems = lax.axis_size("mem")
-    heads, width, rows = decoded.shape
+    heads, width, rows = codes.shape
     tokens = stored.shape[1]
+    (decoded,) = decode(codes, scales, rep, False)
     asked = lax.all_gather(stored, "mem", axis=0)
     partial = pl.pallas_call(
-        pick_kernel,
+        functools.partial(pick_kernel, 0, heads),
         grid=(mems,),
         in_specs=[
             pl.BlockSpec(memory_space=pltpu.SMEM),
@@ -300,49 +376,66 @@
     return total, meanwhile(partial), settled
 
 
-def line_sum(stored, decoded, here, meanwhile, settled):
-    heads, width, rows = decoded.shape
-    tokens = stored.shape[1]
-    base = (here * rows).astype(I32).reshape(1)
-    block = jax.ShapeDtypeStruct((heads * width, tokens), BF16)
-
-    def ask(ids, x):
-        return lax.ppermute(ids, "mem", [(i, i ^ x) for i in range(4)])
-
-    def pick(ids):
-        return pl.pallas_call(
-            pick_kernel,
-            in_specs=[pl.BlockSpec(memory_space=pltpu.SMEM)]
-            + [pl.BlockSpec(memory_space=pltpu.VMEM)] * 2,
-            out_shape=block,
-            compiler_params=limit(8),
-            name="pick_rows",
-        )(base, ids, decoded)
+def line_sum(stored, codes, scales, here, rep, meanwhile, settled):
+    heads, width, rows = codes.shape
+    part = heads // 2
+    middle = (here == 1) | (here == 2)
+    outer = jnp.where(here < 2, 0, 3)
+    scalars = jnp.stack([here * rows, outer * rows, rep[0]]).astype(I32)
 
     def send(x, *pairs):
         return lax.ppermute(x, "mem", pairs)
 
-    rows_3 = pick(ask(stored, 3))
-    inward = send(rows_3, (0, 1), (3, 2))
-    across = send(rows_3, (1, 2), (2, 1))
-    own = pick(after(stored, rows_3))
-    stored, settled = lax.optimization_barrier((after(stored, own), settled))
-    asked = ask(stored, 2), ask(stored, 1)
-    rows_2 = pick(asked[0])
-    past = send(rows_2, (0, 2), (3, 1))
-    rows_1 = pick(asked[1])
-    onward = after(rows_2, rows_1, across) + inward
-    other = meanwhile(onward)
-    onward = send(onward, (1, 3), (2, 0))
-    beside = send(after(rows_1, inward), (0, 1), (1, 0), (2, 3), (3, 2))
-    own, other = lax.optimization_barrier((own + past, other))
+    def swap(x):
+        return lax.ppermute(x, "rep", [(0, 1), (1, 0)])
+
+    lent = pl.pallas_call(
+        lend_kernel,
+        in_specs=[pl.BlockSpec(memory_space=pltpu.SMEM)] + [pl.BlockSpec(memory_space=pl.ANY)] * 2,
+        out_shape=jax.ShapeDtypeStruct((heads // 4, width, rows), BF16),
+        scratch_shapes=[
+            pltpu.VMEM((heads // 4, width, rows), BF16),
+            pltpu.VMEM(scales.shape, BF16),
+            pltpu.VMEM(scales.shape, F32),
+            pltpu.SemaphoreType.DMA((heads // 4 + 1,)),
+        ],
+        compiler_params=limit(4),
+        name="lend_tables",
+    )(rep, in_hbm(codes), in_hbm(scales))
+    near = [send(lent, (0, 1), (3, 2))]
+    ids = stored(lent)
+    ids_3 = send(ids, (1, 2), (2, 1))
+    ids_2 = send(ids, (0, 2), (3, 1))
+    decoded, lent = decode(after(codes, ids), scales, rep, True)
+    ids_1 = send(after(ids, ids_3), (0, 1), (3, 2))
+    lent, settled, ids_1, ids_2, ids_3 = lax.optimization_barrier(
+        (lent, settled, ids_1, ids_2, ids_3)
+    )
+    near.append(send(lent, (0, 1), (3, 2)))
+
+    beside = pick(ids_1, decoded, scalars)
+    other = meanwhile(beside)
+    beside = send(beside, (1, 0), (2, 3))
+    across, onward, own = [], [], []
+    for n in range(2):
+        near_n = near[n] if n == 0 else after(near[n], own[0])
+        held = (near_n, swap(near_n))
+        half = dict(first=n * part, count=part)
+        rows_3 = pick(ids_3, decoded, scalars, *held, **half)
+        across.append(send(rows_3, (1, 2), (2, 1)))
+        rows_2 = pick(after(ids_2, rows_3), decoded, scalars, *held, **half)
+        if n:
+            rows_2 = after(rows_2, across[0], onward[0])
+        onward.append(send(rows_2, (1, 3), (2, 0)))
+        own.append(pick(after(ids, rows_2), decoded, scalars, *held, **half))
+    own[1], other = lax.optimization_barrier((own[1], other))
     memory = pl.pallas_call(
         merge_kernel,
-        in_specs=[pl.BlockSpec(memory_space=pltpu.VMEM)] * 4,
-        out_shape=block,
+        in_specs=[pl.BlockSpec(memory_space=pltpu.VMEM)] * 7,
+        out_shape=jax.ShapeDtypeStruct((heads * width, ids.shape[1]), BF16),
         compiler_params=limit(4),
         name="merge",
-    )(own, across, beside, onward)
+    )(beside, *own, *across, *onward)
     return memory, other, settled
 
 
@@ -365,33 +458,26 @@
     anywhere = pl.BlockSpec(memory_space=pl.ANY)
     resident = pl.BlockSpec(memory_space=pltpu.VMEM)
     places = row_place.reshape(-1, LANES)
-    stored = pl.pallas_call(
-        place_kernel,
-        in_specs=[anywhere] * 2,
-        out_shape=jax.ShapeDtypeStruct((heads, tokens), I32),
-        scratch_shapes=[
-            pltpu.VMEM((heads, tokens), I32),
-            pltpu.VMEM(places.shape, I32),
-            pltpu.SemaphoreType.DMA((2,)),
-        ],
-        compiler_params=limit(4),
-        name="place_rows",
-    )(in_hbm(row_ids.T), in_hbm(places))
+
+    def stored(token=None):
+        ids = row_ids.T if token is None else after(row_ids.T, token)
+        return pl.pallas_call(
+            place_kernel,
+            in_specs=[anywhere] * 2,
+            out_shape=jax.ShapeDtypeStruct((heads, tokens), I32),
+            scratch_shapes=[
+                pltpu.VMEM((heads, tokens), I32),
+                pltpu.VMEM(places.shape, I32),
+                pltpu.SemaphoreType.DMA((2,)),
+            ],
+            compiler_params=limit(4),
+            name="place_rows",
+        )(in_hbm(ids), in_hbm(places))
+
     codes = table_codes.transpose(0, 2, 1)
     scales = table_scales.transpose(2, 0, 1)
-    decoded = pl.pallas_call(
-        decode_kernel,
-        in_specs=[anywhere] * 2,
-        out_shape=jax.ShapeDtypeStruct(codes.shape, BF16),
-        scratch_shapes=[
-            pltpu.VMEM(codes.shape, BF16),
-            pltpu.VMEM(scales.shape, BF16),
-            pltpu.SemaphoreType.DMA((heads + 1,)),
-        ],
-        compiler_params=limit(12),
-        name="decode_tables",
-    )(in_hbm(codes), in_hbm(scales))
     here = lax.axis_index("mem")
+    rep = lax.axis_index("rep").astype(I32).reshape(1)
     other_key = lax.ppermute(key_weight, "rep", [(0, 1), (1, 0)])
     other_value = lax.ppermute(value_weight, "rep", [(0, 1), (1, 0)])
     needed = [(i, i + 1) for i in range(blocks - 1) if (i + 1) * tokens % seq_length]
@@ -400,9 +486,15 @@
         tail = after(hidden[tokens - RIM :], token)
         return lax.ppermute(tail, ("mem", "rep"), needed)
 
-    summed = line_sum if mems == 4 else scattered_sum
-    memory, hidden_halo, others = summed(
-        stored, decoded, here, meanwhile, (other_key, other_value)
+    line = mems == 4 and heads % 4 == 0
+    memory, hidden_halo, others = (line_sum if line else scattered_sum)(
+        stored if line else stored(),
+        codes,
+        scales,
+        here,
+        rep,
+        meanwhile,
+        (other_key, other_value),
     )
     weights = [in_hbm(w) for w in (key_weight, value_weight, *others)]
 

time: 68.6 us -> 73.6 us (1.073)
  Pallas kernels: 21.5 us -> 29.4 us
  waiting for transfers between devices: 17 us -> 14.6 us
    pallas_call x6 -> x10, Pallas kernels: 7.53 us -> 15.4 us  [the longest x7 9.9 us: pick(): pl.pallas_call(functools.partial(pick_kernel, first, count), in_specs=[pl...]
    ppermute x3 -> x2, starting transfers between devices: 7.77 us -> 0.07 us  [swap(): return lax.ppermute(x, 'rep', [(0, 1), (1, 0)])]
    ppermute x5 -> x10, starting transfers between devices: 14.6 us -> 20.4 us  [send(): return lax.ppermute(x, 'mem', pairs)]
    ppermute x3 -> x2, waiting for transfers between devices: 2.81 us -> 0.01 us  [swap(): return lax.ppermute(x, 'rep', [(0, 1), (1, 0)])]
    ppermute x5 -> x10, waiting for transfers between devices: 10.2 us -> 12.3 us  [send(): return lax.ppermute(x, 'mem', pairs)]
    ppermute x1, starting transfers between devices: 0.6 us -> 1.56 us  [shards(): lax.ppermute(stats, 'tp', [(i, (i + s) % tps) for i in range(tps)])]
    ppermute x1, waiting for transfers between devices: 3.16 us -> 2.2 us  [shards(): lax.ppermute(stats, 'tp', [(i, (i + s) % tps) for i in range(tps)])]
    ppermute x1, waiting for transfers between devices: 0.79 us -> 0.01 us  [meanwhile(): return lax.ppermute(tail, ('mem', 'rep'), needed)]
  transfers between devices with their start and end apart: 15 -> 19, of which waited for: 5 -> 4; matrix products, arithmetic and copies ran while one was open for 0% -> 0% of each run, Pallas kernels for 19% -> 29%
where the time goes in v11:
time: 73.6 us; the launch traced here: 73.2 us
  Pallas kernels  29.4 us (40%)
  starting transfers between devices  28.6 us (39%)
  waiting for transfers between devices  14.6 us (20%)
    ppermute x10, starting transfers between devices, send(): return lax.ppermute(x, 'mem', pairs)  20.4 us
    ppermute x10, waiting for transfers between devices, send(): return lax.ppermute(x, 'mem', pairs)  12.3 us
    pallas_call x7, Pallas kernels, pick(): pl.pallas_call(functools.partial(pick_kernel, first, count), in_specs=[pl...  9.9 us
    pallas_call x1, Pallas kernels, shards(): pl.pallas_call(functools.partial(project_kernel, (0,), tps), in_specs=[sm...  5.6 us
    pallas_call x1, Pallas kernels, shards(): pl.pallas_call(functools.partial(project_kernel, tuple(range(1, tps)), tp...  4.27 us
    pallas_call x1, Pallas kernels, shards(): pl.pallas_call(functools.partial(finish_kernel, tps, step), in_specs=[sme...  3.96 us
    ppermute x2, starting transfers between devices, next_rim(): return lax.ppermute(rim, ('mem', 'tp', 'rep'), pairs)  2.92 us
    pallas_call x1, Pallas kernels, decode(): pl.pallas_call(functools.partial(decode_kernel, lend), in_specs=[pl.Block...  2.75 us
  transfers between devices with their start and end apart: 19, of which 4 were waited for; matrix products, arithmetic and copies ran while one was open for 0% of the time, Pallas kernels for 29%

profile of v11, /device:TPU:0, one launch (start us, length us, event | category | flops | bytes accessed | tf_op | source)
XLA Modules:
  0.0 73.2 jit_solution(7214292510183419463)
XLA Ops:
  0.0 0.5 collective-permute-start
  0.5 0.1 collective-permute-start.1
  0.5 1.4 %lend_tables.1 = bf16[2,80,1024]{2,1,0:T(8,128)(2,1)S(1)} custom-call(s32[1]{0:T(128)} %bitcast.1.rep_ref, bf16[8,80,1024]{2,1,0:T(8,128)(2,1)} %bitcast.9, bf16[5,8,1024]{2,1,0:T(8,128)(2,1)} %bitcast.11), custom_call_target="tpu_custom_call" | custom-call | tf_op jit(solution)/shard_map/lend_tables/pallas_call | solution.py:392
  1.9 4.9 %collective-permute-start.6 = (bf16[2,80,1024]{2,1,0:T(8,128)(2,1)S(1)}, bf16[2,80,1024]{2,1,0:T(8,128)(2,1)S(1)}, u32[]{:S(2)}, u32[]{:S(2)}) collective-permute-start(bf16[2,80,1024]{2,1,0:T(8,128)(2,1)S(1)} %lend_tables.1), channel_id=1, source_target_pairs={{0,4},{12,8},{1,5},{13,9},{2,6},{14,10},{3,7},{15,11},{16,20},{28,... | collective-permute-start | bytes 983048 | tf_op jit(solution)/shard_map/ppermute | solution.py:387
  6.9 1.3 %place_rows.1.ids_ref = s32[8,256]{1,0:T(8,128)S(1)} custom-call(s32[8,256]{1,0:T(8,128)} %bitcast.14, s32[32,128]{1,0:T(8,128)} %bitcast.13), custom_call_target="tpu_custom_call" | custom-call | tf_op jit(solution)/shard_map/place_rows/pallas_call | solution.py:464
  8.2 0.7 collective-permute-start.2
  8.9 4.0 %collective-permute-start.4 = (s32[8,256]{1,0:T(8,128)S(1)}, s32[8,256]{1,0:T(8,128)S(1)}, u32[]{:S(2)}, u32[]{:S(2)}) collective-permute-start(s32[8,256]{1,0:T(8,128)S(1)} %place_rows.1.ids_ref), channel_id=1, source_target_pairs={{0,8},{12,4},{1,9},{13,5},{2,10},{14,6},{3,11},{15,7},{16,24},{28,... | collective-permute-start | bytes 24584 | tf_op jit(solution)/shard_map/ppermute | solution.py:387
  12.9 2.1 %collective-permute-start.3 = (s32[8,256]{1,0:T(8,128)S(1)}, s32[8,256]{1,0:T(8,128)S(1)}, u32[]{:S(2)}, u32[]{:S(2)}) collective-permute-start(s32[8,256]{1,0:T(8,128)S(1)} %place_rows.1.ids_ref), channel_id=1, source_target_pairs={{0,4},{12,8},{1,5},{13,9},{2,6},{14,10},{3,7},{15,11},{16,20},{28,... | collective-permute-start | bytes 24584 | tf_op jit(solution)/shard_map/ppermute | solution.py:387
  15.0 0.1 collective-permute-start.7
  15.1 2.7 %decode_tables.1 = (bf16[8,80,1024]{2,1,0:T(8,128)(2,1)S(1)}, bf16[2,80,1024]{2,1,0:T(8,128)(2,1)S(1)}) custom-call(s32[1]{0:T(128)} %bitcast.1.rep_ref, bf16[8,80,1024]{2,1,0:T(8,128)(2,1)} %bitcast.10, bf16[5,8,1024]{2,1,0:T(8,128)(2,1)} %bitcast.12), custom_call_target="tpu_custom_call" | custom-call | tf_op jit(solution)/shard_map/decode_tables/pallas_call | solution.py:342
  17.9 0.0 collective-permute-done.4.ids_ref
  17.9 0.0 collective-permute-done.refs_4_
  17.9 0.0 collective-permute-done.1.refs_5_
  17.9 3.3 %collective-permute-start.8 = (bf16[2,80,1024]{2,1,0:T(8,128)(2,1)S(1)}, bf16[2,80,1024]{2,1,0:T(8,128)(2,1)S(1)}, u32[]{:S(2)}, u32[]{:S(2)}) collective-permute-start(bf16[2,80,1024]{2,1,0:T(8,128)(2,1)S(1)} %get-tuple-element.40), channel_id=1, source_target_pairs={{0,4},{12,8},{1,5},{13,9},{2,6},{14,10},{3,7},{15,11},{16,20},{28,... | collective-permute-start | bytes 983048 | tf_op jit(solution)/shard_map/ppermute | solution.py:387
  21.3 0.1 pad_add_fusion.1.scalars_ref
  21.4 1.4 %pick_rows.8 = bf16[320,256]{1,0:T(8,128)(2,1)S(1)} custom-call(s32[3]{0:T(128)S(1)} %pad_add_fusion.1.scalars_ref, s32[8,256]{1,0:T(8,128)S(1)} %collective-permute-done.2.ids_ref, bf16[8,80,1024]{2,1,0:T(8,128)(2,1)S(1)} %get-tuple-element.35.table_ref, bf16[2,80,1024]{2,1,0:T(8,128)(2,1)S(1)} %collective-permute-done.6.refs_0_, ...), custom_call_target="tpu_custom_call" | custom-call | tf_op jit(solution)/shard_map/pick_rows/pallas_call | solution.py:329
  22.8 1.4 %pick_rows.9 = bf16[320,256]{1,0:T(8,128)(2,1)S(1)} custom-call(s32[3]{0:T(128)S(1)} %pad_add_fusion.1.scalars_ref, s32[8,256]{1,0:T(8,128)S(1)} %collective-permute-done.4.ids_ref, bf16[8,80,1024]{2,1,0:T(8,128)(2,1)S(1)} %get-tuple-element.35.table_ref, bf16[2,80,1024]{2,1,0:T(8,128)(2,1)S(1)} %collective-permute-done.6.refs_0_, ...), custom_call_target="tpu_custom_call" | custom-call | tf_op jit(solution)/shard_map/pick_rows/pallas_call | solution.py:329
  24.2 1.4 %pick_rows.10.refs_0_ = bf16[320,256]{1,0:T(8,128)(2,1)S(1)} custom-call(s32[3]{0:T(128)S(1)} %pad_add_fusion.1.scalars_ref, s32[8,256]{1,0:T(8,128)S(1)} %place_rows.1.ids_ref, bf16[8,80,1024]{2,1,0:T(8,128)(2,1)S(1)} %get-tuple-element.35.table_ref, bf16[2,80,1024]{2,1,0:T(8,128)(2,1)S(1)} %collective-permute-done.6.refs_0_, ...), custom_call_target="tpu_custom_call" | custom-call | tf_op jit(solution)/shard_map/pick_rows/pallas_call | solution.py:329
  25.6 3.3 %collective-permute-done.8.refs_0_ = bf16[2,80,1024]{2,1,0:T(8,128)(2,1)S(1)} collective-permute-done((bf16[2,80,1024]{2,1,0:T(8,128)(2,1)S(1)}, bf16[2,80,1024]{2,1,0:T(8,128)(2,1)S(1)}, u32[]{:S(2)}, u32[]{:S(2)}) %collective-permute-start.8) | collective-permute-done | bytes 327712 | tf_op jit(solution)/shard_map/ppermute | solution.py:387
  28.9 0.0 collective-permute-start.9
  28.9 1.3 %collective-permute-start.11 = (bf16[320,256]{1,0:T(8,128)(2,1)S(1)}, bf16[320,256]{1,0:T(8,128)(2,1)S(1)}, u32[]{:S(2)}, u32[]{:S(2)}) collective-permute-start(bf16[320,256]{1,0:T(8,128)(2,1)S(1)} %pick_rows.9), channel_id=1, source_target_pairs={{4,12},{8,0},{5,13},{9,1},{6,14},{10,2},{7,15},{11,3},{20,28},{24,... | collective-permute-start | bytes 491528 | tf_op jit(solution)/shard_map/ppermute | solution.py:387
  30.2 0.7 collective-permute-start.10
  30.8 1.4 %pick_rows.7 = bf16[640,256]{1,0:T(8,128)(2,1)S(1)} custom-call(s32[3]{0:T(128)S(1)} %pad_add_fusion.1.scalars_ref, s32[8,256]{1,0:T(8,128)S(1)} %collective-permute-done.3.ids_ref, bf16[8,80,1024]{2,1,0:T(8,128)(2,1)S(1)} %get-tuple-element.35.table_ref), custom_call_target="tpu_custom_call" | custom-call | tf_op jit(solution)/shard_map/pick_rows/pallas_call | solution.py:329
  32.3 0.0 copy-start
  32.3 1.4 %collective-permute-start.5 = (bf16[640,256]{1,0:T(8,128)(2,1)S(1)}, bf16[640,256]{1,0:T(8,128)(2,1)S(1)}, u32[]{:S(2)}, u32[]{:S(2)}) collective-permute-start(bf16[640,256]{1,0:T(8,128)(2,1)S(1)} %pick_rows.7), channel_id=1, source_target_pairs={{4,0},{8,12},{5,1},{9,13},{6,2},{10,14},{7,3},{11,15},{20,16},{24,... | collective-permute-start | bytes 983048 | tf_op jit(solution)/shard_map/ppermute | solution.py:387
  33.7 1.4 %pick_rows.11 = bf16[320,256]{1,0:T(8,128)(2,1)S(1)} custom-call(s32[3]{0:T(128)S(1)} %pad_add_fusion.1.scalars_ref, s32[8,256]{1,0:T(8,128)S(1)} %collective-permute-done.2.ids_ref, bf16[8,80,1024]{2,1,0:T(8,128)(2,1)S(1)} %get-tuple-element.35.table_ref, bf16[2,80,1024]{2,1,0:T(8,128)(2,1)S(1)} %collective-permute-done.8.refs_0_, ...), custom_call_target="tpu_custom_call" | custom-call | tf_op jit(solution)/shard_map/pick_rows/pallas_call | solution.py:329
  35.1 1.4 %pick_rows.12 = bf16[320,256]{1,0:T(8,128)(2,1)S(1)} custom-call(s32[3]{0:T(128)S(1)} %pad_add_fusion.1.scalars_ref, s32[8,256]{1,0:T(8,128)S(1)} %collective-permute-done.4.ids_ref, bf16[8,80,1024]{2,1,0:T(8,128)(2,1)S(1)} %get-tuple-element.35.table_ref, bf16[2,80,1024]{2,1,0:T(8,128)(2,1)S(1)} %collective-permute-done.8.refs_0_, ...), custom_call_target="tpu_custom_call" | custom-call | tf_op jit(solution)/shard_map/pick_rows/pallas_call | solution.py:329
  36.5 2.2 %collective-permute-done.11.refs_4_ = bf16[320,256]{1,0:T(8,128)(2,1)S(1)} collective-permute-done((bf16[320,256]{1,0:T(8,128)(2,1)S(1)}, bf16[320,256]{1,0:T(8,128)(2,1)S(1)}, u32[]{:S(2)}, u32[]{:S(2)}) %collective-permute-start.11) | collective-permute-done | bytes 163872 | tf_op jit(solution)/shard_map/ppermute | solution.py:387
  38.7 1.3 %collective-permute-start.14 = (bf16[320,256]{1,0:T(8,128)(2,1)S(1)}, bf16[320,256]{1,0:T(8,128)(2,1)S(1)}, u32[]{:S(2)}, u32[]{:S(2)}) collective-permute-start(bf16[320,256]{1,0:T(8,128)(2,1)S(1)} %pick_rows.12), channel_id=1, source_target_pairs={{4,12},{8,0},{5,13},{9,1},{6,14},{10,2},{7,15},{11,3},{20,28},{24,... | collective-permute-start | bytes 491528 | tf_op jit(solution)/shard_map/ppermute | solution.py:387
  40.0 0.7 collective-permute-start.13
  40.7 1.6 %collective-permute-start.12 = (bf16[16,2304]{1,0:T(8,128)(2,1)S(1)}, bf16[16,2304]{1,0:T(8,128)(2,1)S(1)}, u32[]{:S(2)}, u32[]{:S(2)}) collective-permute-start(bf16[16,2304]{1,0:T(8,128)(2,1)S(1)} %slice.6), channel_id=1, source_target_pairs={{0,1},{4,5},{8,9},{12,13},{2,3},{6,7},{10,11},{14,15},{16,17},{20,... | collective-permute-start | bytes 221192 | tf_op jit(solution)/shard_map/ppermute | solution.py:487
  42.3 1.4 %pick_rows.13.refs_1_ = bf16[320,256]{1,0:T(8,128)(2,1)S(1)} custom-call(s32[3]{0:T(128)S(1)} %pad_add_fusion.1.scalars_ref, s32[8,256]{1,0:T(8,128)S(1)} %place_rows.1.ids_ref, bf16[8,80,1024]{2,1,0:T(8,128)(2,1)S(1)} %get-tuple-element.35.table_ref, bf16[2,80,1024]{2,1,0:T(8,128)(2,1)S(1)} %collective-permute-done.8.refs_0_, ...), custom_call_target="tpu_custom_call" | custom-call | tf_op jit(solution)/shard_map/pick_rows/pallas_call | solution.py:329
  43.7 0.0 collective-permute-done.12.refs_5_
  43.7 6.9 %collective-permute-done.5.beside_ref = bf16[640,256]{1,0:T(8,128)(2,1)S(1)} collective-permute-done((bf16[640,256]{1,0:T(8,128)(2,1)S(1)}, bf16[640,256]{1,0:T(8,128)(2,1)S(1)}, u32[]{:S(2)}, u32[]{:S(2)}) %collective-permute-start.5) | collective-permute-done | bytes 327712 | tf_op jit(solution)/shard_map/ppermute | solution.py:387
  50.6 0.0 collective-permute-done.13.refs_3_
  50.6 0.2 merge.1.refs_1_
  50.8 1.6 %collective-permute-start.16 = (bf16[640,256]{1,0:T(8,128)(2,1)S(1)}, bf16[640,256]{1,0:T(8,128)(2,1)S(1)}, u32[]{:S(2)}, u32[]{:S(2)}) collective-permute-start(bf16[640,256]{1,0:T(8,128)(2,1)S(1)} %merge.1.refs_1_), channel_id=1, source_target_pairs={{0,2},{2,0},{1,3},{3,1},{4,6},{6,4},{5,7},{7,5},{8,10},{10,8},{9,1... | collective-permute-start | bytes 983048 | tf_op jit(solution)/shard_map/ppermute | solution.py:504
  52.3 1.3 %collective-permute-start.17 = (bf16[640,128]{1,0:T(8,128)(2,1)S(1)}, bf16[640,128]{1,0:T(8,128)(2,1)S(1)}, u32[]{:S(2)}, u32[]{:S(2)}) collective-permute-start(bf16[640,128]{1,0:T(8,128)(2,1)S(1)} %slice.8), channel_id=1, source_target_pairs={{0,1},{2,3},{4,5},{6,7},{8,9},{10,11},{12,13},{14,15},{16,17},{18,... | collective-permute-start | bytes 491528 | tf_op jit(solution)/shard_map/ppermute | solution.py:517
  53.7 1.6 %collective-permute-start.15 = (bf16[640,128]{1,0:T(8,128)(2,1)S(1)}, bf16[640,128]{1,0:T(8,128)(2,1)S(1)}, u32[]{:S(2)}, u32[]{:S(2)}) collective-permute-start(bf16[640,128]{1,0:T(8,128)(2,1)S(1)} %slice.8), channel_id=1, source_target_pairs={{0,3},{2,1},{4,7},{6,5},{8,11},{10,9},{12,15},{14,13},{16,19},{18,... | collective-permute-start | bytes 491528 | tf_op jit(solution)/shard_map/ppermute | solution.py:517
  55.3 0.1 pad_add_fusion.where_ref
  55.4 0.0 collective-permute-done.17.refs_0_
  55.4 5.6 %project_own.1 = (f32[2,272,1152]{2,1,0:T(8,128)S(1)}, f32[2,272,1152]{2,1,0:T(8,128)S(1)}, bf16[2,2,640,1152]{3,2,1,0:T(8,128)(2,1)S(1)}) custom-call(s32[2]{0:T(128)S(1)} %pad_add_fusion.where_ref, bf16[640,128]{1,0:T(8,128)(2,1)S(1)} %collective-permute-done.17.refs_0_, bf16[640,256]{1,0:T(8,128)(2,1)S(1)} %merge.1.refs_1_, bf16[1280,1152]{1,0:T(8,128)(2,1)} %refs_2_.1, ...), custom_call_target="tpu_custom_call" | custom-call | tf_op jit(solution)/shard_map/project_own/pallas_call | solution.py:523
  61.0 0.0 collective-permute-done.16.refs_1_
  61.0 0.0 copy-start.1
  61.0 4.3 %project_others.1 = (f32[2,272,1152]{2,1,0:T(8,128)}, f32[8,272]{1,0:T(8,128)S(1)}) custom-call(s32[2]{0:T(128)S(1)} %pad_add_fusion.where_ref, bf16[640,128]{1,0:T(8,128)(2,1)S(1)} %collective-permute-done.15.refs_0_, bf16[640,256]{1,0:T(8,128)(2,1)S(1)} %collective-permute-done.16.refs_1_, bf16[2,2,640,1152]{3,2,1,0:T(8,128)(2,1)S(1)} %get-tuple-element.49.refs_2_, ...), custom_call_target="tpu_custom_call" | custom-call | tf_op jit(solution)/shard_map/project_others/pallas_call | solution.py:536
  65.3 1.6 %collective-permute-start.18 = (f32[8,272]{1,0:T(8,128)S(1)}, f32[8,272]{1,0:T(8,128)S(1)}, u32[]{:S(2)}, u32[]{:S(2)}) collective-permute-start(f32[8,272]{1,0:T(8,128)S(1)} %get-tuple-element.53.refs_0_), channel_id=1, source_target_pairs={{0,2},{2,0},{1,3},{3,1},{4,6},{6,4},{5,7},{7,5},{8,10},{10,8},{9,1... | collective-permute-start | bytes 26120 | tf_op jit(solution)/shard_map/ppermute | solution.py:559
  66.8 2.2 %collective-permute-done.18.refs_1_ = f32[8,272]{1,0:T(8,128)S(1)} collective-permute-done((f32[8,272]{1,0:T(8,128)S(1)}, f32[8,272]{1,0:T(8,128)S(1)}, u32[]{:S(2)}, u32[]{:S(2)}) %collective-permute-start.18) | collective-permute-done | bytes 8736 | tf_op jit(solution)/shard_map/ppermute | solution.py:559
  69.0 4.0 %finish.1 = bf16[256,2304]{1,0:T(8,128)(2,1)} custom-call(s32[1]{0:T(128)} %bitcast.keep_ref, f32[8,272]{1,0:T(8,128)S(1)} %get-tuple-element.53.refs_0_, f32[8,272]{1,0:T(8,128)S(1)} %collective-permute-done.18.refs_1_, f32[2,272,1152]{2,1,0:T(8,128)} %get-tuple-element.54.refs_2_, bf16[256,2304]{1,0:T(8,128)(2,1)S(1)} %copy-done, f32[4,2304]{1,0:T(4,128)S(1)} %copy-done.1), custom_call_target="tpu_custom_call" | custom-call | tf_op jit(solution)/shard_map/finish/pallas_call | solution.py:565
  (12 shorter events, 0.0 us)
Async XLA Ops:
  0.0 17.9 %collective-permute-start = (bf16[1280,1152]{1,0:T(8,128)(2,1)}, bf16[1280,1152]{1,0:T(8,128)(2,1)}, u32[]{:S(2)}, u32[]{:S(2)}) collective-permute-start(bf16[1280,1152]{1,0:T(8,128)(2,1)} %refs_2_.1), channel_id=1, source_target_pairs={{0,1},{1,0},{2,3},{3,2},{4,5},{5,4},{6,7},{7,6},{8,9},{9,8},{10,11... | collective-permute-start | bytes 8847368 | tf_op jit(solution)/shard_map/ppermute | solution.py:481
  0.5 17.5 %collective-permute-start.1 = (bf16[1280,1152]{1,0:T(8,128)(2,1)}, bf16[1280,1152]{1,0:T(8,128)(2,1)}, u32[]{:S(2)}, u32[]{:S(2)}) collective-permute-start(bf16[1280,1152]{1,0:T(8,128)(2,1)} %refs_3_.2), channel_id=1, source_target_pairs={{0,1},{1,0},{2,3},{3,2},{4,5},{5,4},{6,7},{7,6},{8,9},{9,8},{10,11... | collective-permute-start | bytes 8847368 | tf_op jit(solution)/shard_map/ppermute | solution.py:482
  1.9 13.1 %collective-permute-start.6 = (bf16[2,80,1024]{2,1,0:T(8,128)(2,1)S(1)}, bf16[2,80,1024]{2,1,0:T(8,128)(2,1)S(1)}, u32[]{:S(2)}, u32[]{:S(2)}) collective-permute-start(bf16[2,80,1024]{2,1,0:T(8,128)(2,1)S(1)} %lend_tables.1), channel_id=1, source_target_pairs={{0,4},{12,8},{1,5},{13,9},{2,6},{14,10},{3,7},{15,11},{16,20},{28,... | collective-permute-start | bytes 983048 | tf_op jit(solution)/shard_map/ppermute | solution.py:387
  8.2 4.7 %collective-permute-start.2 = (s32[8,256]{1,0:T(8,128)S(1)}, s32[8,256]{1,0:T(8,128)S(1)}, u32[]{:S(2)}, u32[]{:S(2)}) collective-permute-start(s32[8,256]{1,0:T(8,128)S(1)} %place_rows.1.ids_ref), channel_id=1, source_target_pairs={{4,8},{8,4},{5,9},{9,5},{6,10},{10,6},{7,11},{11,7},{20,24},{24,20... | collective-permute-start | bytes 24584 | tf_op jit(solution)/shard_map/ppermute | solution.py:387
  8.9 9.0 %collective-permute-start.4 = (s32[8,256]{1,0:T(8,128)S(1)}, s32[8,256]{1,0:T(8,128)S(1)}, u32[]{:S(2)}, u32[]{:S(2)}) collective-permute-start(s32[8,256]{1,0:T(8,128)S(1)} %place_rows.1.ids_ref), channel_id=1, source_target_pairs={{0,8},{12,4},{1,9},{13,5},{2,10},{14,6},{3,11},{15,7},{16,24},{28,... | collective-permute-start | bytes 24584 | tf_op jit(solution)/shard_map/ppermute | solution.py:387
  12.9 5.0 %collective-permute-start.3 = (s32[8,256]{1,0:T(8,128)S(1)}, s32[8,256]{1,0:T(8,128)S(1)}, u32[]{:S(2)}, u32[]{:S(2)}) collective-permute-start(s32[8,256]{1,0:T(8,128)S(1)} %place_rows.1.ids_ref), channel_id=1, source_target_pairs={{0,4},{12,8},{1,5},{13,9},{2,6},{14,10},{3,7},{15,11},{16,20},{28,... | collective-permute-start | bytes 24584 | tf_op jit(solution)/shard_map/ppermute | solution.py:387
  15.0 6.3 %collective-permute-start.7 = (bf16[2,80,1024]{2,1,0:T(8,128)(2,1)S(1)}, bf16[2,80,1024]{2,1,0:T(8,128)(2,1)S(1)}, u32[]{:S(2)}, u32[]{:S(2)}) collective-permute-start(bf16[2,80,1024]{2,1,0:T(8,128)(2,1)S(1)} %collective-permute-done.6.refs_0_), channel_id=1, source_target_pairs={{0,1},{1,0},{2,3},{3,2},{4,5},{5,4},{6,7},{7,6},{8,9},{9,8},{10,11... | collective-permute-start | bytes 983048 | tf_op jit(solution)/shard_map/ppermute | solution.py:390
  17.9 11.0 %collective-permute-start.8 = (bf16[2,80,1024]{2,1,0:T(8,128)(2,1)S(1)}, bf16[2,80,1024]{2,1,0:T(8,128)(2,1)S(1)}, u32[]{:S(2)}, u32[]{:S(2)}) collective-permute-start(bf16[2,80,1024]{2,1,0:T(8,128)(2,1)S(1)} %get-tuple-element.40), channel_id=1, source_target_pairs={{0,4},{12,8},{1,5},{13,9},{2,6},{14,10},{3,7},{15,11},{16,20},{28,... | collective-permute-start | bytes 983048 | tf_op jit(solution)/shard_map/ppermute | solution.py:387
  28.9 4.8 %collective-permute-start.9 = (bf16[2,80,1024]{2,1,0:T(8,128)(2,1)S(1)}, bf16[2,80,1024]{2,1,0:T(8,128)(2,1)S(1)}, u32[]{:S(2)}, u32[]{:S(2)}) collective-permute-start(bf16[2,80,1024]{2,1,0:T(8,128)(2,1)S(1)} %collective-permute-done.8.refs_0_), channel_id=1, source_target_pairs={{0,1},{1,0},{2,3},{3,2},{4,5},{5,4},{6,7},{7,6},{8,9},{9,8},{10,11... | collective-permute-start | bytes 983048 | tf_op jit(solution)/shard_map/ppermute | solution.py:390
  28.9 9.9 %collective-permute-start.11 = (bf16[320,256]{1,0:T(8,128)(2,1)S(1)}, bf16[320,256]{1,0:T(8,128)(2,1)S(1)}, u32[]{:S(2)}, u32[]{:S(2)}) collective-permute-start(bf16[320,256]{1,0:T(8,128)(2,1)S(1)} %pick_rows.9), channel_id=1, source_target_pairs={{4,12},{8,0},{5,13},{9,1},{6,14},{10,2},{7,15},{11,3},{20,28},{24,... | collective-permute-start | bytes 491528 | tf_op jit(solution)/shard_map/ppermute | solution.py:387
  30.2 8.6 %collective-permute-start.10 = (bf16[320,256]{1,0:T(8,128)(2,1)S(1)}, bf16[320,256]{1,0:T(8,128)(2,1)S(1)}, u32[]{:S(2)}, u32[]{:S(2)}) collective-permute-start(bf16[320,256]{1,0:T(8,128)(2,1)S(1)} %pick_rows.8), channel_id=1, source_target_pairs={{4,8},{8,4},{5,9},{9,5},{6,10},{10,6},{7,11},{11,7},{20,24},{24,20... | collective-permute-start | bytes 491528 | tf_op jit(solution)/shard_map/ppermute | solution.py:387
  32.3 8.4 %copy-start = (bf16[256,2304]{1,0:T(8,128)(2,1)S(1)}, bf16[256,2304]{1,0:T(8,128)(2,1)}, u32[]{:S(2)}) copy-start(bf16[256,2304]{1,0:T(8,128)(2,1)} %refs_3_.3) | copy-start | bytes 3538948
  32.3 18.3 %collective-permute-start.5 = (bf16[640,256]{1,0:T(8,128)(2,1)S(1)}, bf16[640,256]{1,0:T(8,128)(2,1)S(1)}, u32[]{:S(2)}, u32[]{:S(2)}) collective-permute-start(bf16[640,256]{1,0:T(8,128)(2,1)S(1)} %pick_rows.7), channel_id=1, source_target_pairs={{4,0},{8,12},{5,1},{9,13},{6,2},{10,14},{7,3},{11,15},{20,16},{24,... | collective-permute-start | bytes 983048 | tf_op jit(solution)/shard_map/ppermute | solution.py:387
  38.7 11.9 %collective-permute-start.14 = (bf16[320,256]{1,0:T(8,128)(2,1)S(1)}, bf16[320,256]{1,0:T(8,128)(2,1)S(1)}, u32[]{:S(2)}, u32[]{:S(2)}) collective-permute-start(bf16[320,256]{1,0:T(8,128)(2,1)S(1)} %pick_rows.12), channel_id=1, source_target_pairs={{4,12},{8,0},{5,13},{9,1},{6,14},{10,2},{7,15},{11,3},{20,28},{24,... | collective-permute-start | bytes 491528 | tf_op jit(solution)/shard_map/ppermute | solution.py:387
  40.0 10.6 %collective-permute-start.13 = (bf16[320,256]{1,0:T(8,128)(2,1)S(1)}, bf16[320,256]{1,0:T(8,128)(2,1)S(1)}, u32[]{:S(2)}, u32[]{:S(2)}) collective-permute-start(bf16[320,256]{1,0:T(8,128)(2,1)S(1)} %pick_rows.11), channel_id=1, source_target_pairs={{4,8},{8,4},{5,9},{9,5},{6,10},{10,6},{7,11},{11,7},{20,24},{24,20... | collective-permute-start | bytes 491528 | tf_op jit(solution)/shard_map/ppermute | solution.py:387
  40.7 3.0 %collective-permute-start.12 = (bf16[16,2304]{1,0:T(8,128)(2,1)S(1)}, bf16[16,2304]{1,0:T(8,128)(2,1)S(1)}, u32[]{:S(2)}, u32[]{:S(2)}) collective-permute-start(bf16[16,2304]{1,0:T(8,128)(2,1)S(1)} %slice.6), channel_id=1, source_target_pairs={{0,1},{4,5},{8,9},{12,13},{2,3},{6,7},{10,11},{14,15},{16,17},{20,... | collective-permute-start | bytes 221192 | tf_op jit(solution)/shard_map/ppermute | solution.py:487
  50.8 10.2 %collective-permute-start.16 = (bf16[640,256]{1,0:T(8,128)(2,1)S(1)}, bf16[640,256]{1,0:T(8,128)(2,1)S(1)}, u32[]{:S(2)}, u32[]{:S(2)}) collective-permute-start(bf16[640,256]{1,0:T(8,128)(2,1)S(1)} %merge.1.refs_1_), channel_id=1, source_target_pairs={{0,2},{2,0},{1,3},{3,1},{4,6},{6,4},{5,7},{7,5},{8,10},{10,8},{9,1... | collective-permute-start | bytes 983048 | tf_op jit(solution)/shard_map/ppermute | solution.py:504
  52.3 3.0 %collective-permute-start.17 = (bf16[640,128]{1,0:T(8,128)(2,1)S(1)}, bf16[640,128]{1,0:T(8,128)(2,1)S(1)}, u32[]{:S(2)}, u32[]{:S(2)}) collective-permute-start(bf16[640,128]{1,0:T(8,128)(2,1)S(1)} %slice.8), channel_id=1, source_target_pairs={{0,1},{2,3},{4,5},{6,7},{8,9},{10,11},{12,13},{14,15},{16,17},{18,... | collective-permute-start | bytes 491528 | tf_op jit(solution)/shard_map/ppermute | solution.py:517
  53.7 7.3 %collective-permute-start.15 = (bf16[640,128]{1,0:T(8,128)(2,1)S(1)}, bf16[640,128]{1,0:T(8,128)(2,1)S(1)}, u32[]{:S(2)}, u32[]{:S(2)}) collective-permute-start(bf16[640,128]{1,0:T(8,128)(2,1)S(1)} %slice.8), channel_id=1, source_target_pairs={{0,3},{2,1},{4,7},{6,5},{8,11},{10,9},{12,15},{14,13},{16,19},{18,... | collective-permute-start | bytes 491528 | tf_op jit(solution)/shard_map/ppermute | solution.py:517
  61.0 8.1 %copy-start.1 = (f32[4,2304]{1,0:T(4,128)S(1)}, f32[4,2304]{1,0:T(4,128)}, u32[]{:S(2)}) copy-start(f32[4,2304]{1,0:T(4,128)} %refs_4_.1) | copy-start | bytes 110596
  65.3 3.8 %collective-permute-start.18 = (f32[8,272]{1,0:T(8,128)S(1)}, f32[8,272]{1,0:T(8,128)S(1)}, u32[]{:S(2)}, u32[]{:S(2)}) collective-permute-start(f32[8,272]{1,0:T(8,128)S(1)} %get-tuple-element.53.refs_0_), channel_id=1, source_target_pairs={{0,2},{2,0},{1,3},{3,1},{4,6},{6,4},{5,7},{7,5},{8,10},{10,8},{9,1... | collective-permute-start | bytes 26120 | tf_op jit(solution)/shard_map/ppermute | solution.py:559

commit v12 on v10

--- a/solution.py
+++ b/solution.py
@@ -336,23 +336,22 @@
     across = send(rows_3, (1, 2), (2, 1))
     rows_2 = pick(after(second, rows_3))
     stored, settled = lax.optimization_barrier((after(stored, rows_2), settled))
+    past = crossing(rows_2, [(m, r, m ^ 2, r ^ 1) for m in (0, 3) for r in range(2)])
     rows_1 = pick(ask(stored, 1))
     own = pick(stored)
+    beside = send(rows_1, (0, 1), (1, 0), (2, 3), (3, 2))
     onward = after(rows_2, rows_1, own) + inward
     onward = after(onward, across)
-    rows_1, rows_2 = after(rows_1, onward), after(rows_2, onward)
     other = meanwhile(onward)
     onward = send(onward, (1, 3), (2, 0))
-    beside = send(rows_1, (0, 1), (1, 0), (2, 3), (3, 2))
-    past = crossing(rows_2, [(m, r, m ^ 2, r ^ 1) for m in (0, 3) for r in range(2)])
-    own, other = lax.optimization_barrier((own + onward, other))
+    own, other = lax.optimization_barrier((own + past + beside, other))
     memory = pl.pallas_call(
         merge_kernel,
-        in_specs=[pl.BlockSpec(memory_space=pltpu.VMEM)] * 4,
+        in_specs=[pl.BlockSpec(memory_space=pltpu.VMEM)] * 3,
         out_shape=block,
         compiler_params=limit(4),
         name="merge",
-    )(own, across, beside, past)
+    )(own, across, onward)
     return memory, other, settled
 
 

time: 67.5 us -> 65.3 us (0.967)
  starting transfers between devices: 27.1 us -> 24 us
  waiting for transfers between devices: 17.8 us -> 18.8 us
    ppermute x2, starting transfers between devices: 6.39 us -> 2.61 us  [crossing(): lax.ppermute(x, ('mem', 'rep'), [(2 * a + b, 2 * c + d) for a, b, c, d in...]
    ppermute x4, starting transfers between devices: 4.09 us -> 6.57 us  [send(): return lax.ppermute(x, 'mem', pairs)]
    ppermute x4, waiting for transfers between devices: 12.3 us -> 14.2 us  [send(): return lax.ppermute(x, 'mem', pairs)]
    ppermute x2, waiting for transfers between devices: 2.09 us -> 0.34 us  [ask(): return lax.ppermute(ids, 'mem', [(i, i ^ x) for i in range(4)])]
    ppermute x1, starting transfers between devices: 2.49 us -> 1.29 us  [meanwhile(): return lax.ppermute(tail, ('mem', 'rep'), needed)]
  transfers between devices with their start and end apart: 15 -> 15, of which waited for: 5 -> 6; matrix products, arithmetic and copies ran while one was open for 0% -> 0% of each run, Pallas kernels for 20% -> 20%
where the time goes in v12:
time: 65.3 us; the launch traced here: 64.9 us
  starting transfers between devices  24 us (37%)
  Pallas kernels  21.5 us (33%)
  waiting for transfers between devices  18.8 us (29%)
    ppermute x4, waiting for transfers between devices, send(): return lax.ppermute(x, 'mem', pairs)  14.2 us
    ppermute x2, starting transfers between devices, ask(): return lax.ppermute(ids, 'mem', [(i, i ^ x) for i in range(4)])  7.27 us
    ppermute x4, starting transfers between devices, send(): return lax.ppermute(x, 'mem', pairs)  6.57 us
    pallas_call x1, Pallas kernels, shards(): pl.pallas_call(functools.partial(project_kernel, (0,), tps), in_specs=[sm...  5.61 us
    pallas_call x1, Pallas kernels, shards(): pl.pallas_call(functools.partial(project_kernel, tuple(range(1, tps)), tp...  4.24 us
    pallas_call x1, Pallas kernels, shards(): pl.pallas_call(functools.partial(finish_kernel, tps, step), in_specs=[sme...  3.96 us
    pallas_call x4, Pallas kernels, pick(): pl.pallas_call(pick_kernel, in_specs=[pl.BlockSpec(memory_space=pltpu.SME...  3.45 us
    ppermute x2, starting transfers between devices, next_rim(): return lax.ppermute(rim, ('mem', 'tp', 'rep'), pairs)  2.78 us
  transfers between devices with their start and end apart: 15, of which 6 were waited for; matrix products, arithmetic and copies ran while one was open for 0% of the time, Pallas kernels for 20%

profile of v12, /device:TPU:0, one launch (start us, length us, event | category | flops | bytes accessed | tf_op | source)
XLA Modules:
  0.0 64.9 jit_solution(11905463162907916079)
XLA Ops:
  0.0 0.5 collective-permute-start.2
  0.5 0.1 collective-permute-start.3
  0.5 1.3 %place_rows.1.ids_ref = s32[8,256]{1,0:T(8,128)S(1)} custom-call(s32[8,256]{1,0:T(8,128)} %bitcast.11, s32[32,128]{1,0:T(8,128)} %bitcast.10), custom_call_target="tpu_custom_call" | custom-call | tf_op jit(solution)/shard_map/place_rows/pallas_call | solution.py:377
  1.9 5.1 %collective-permute-start = (s32[8,256]{1,0:T(8,128)S(1)}, s32[8,256]{1,0:T(8,128)S(1)}, u32[]{:S(2)}, u32[]{:S(2)}) collective-permute-start(s32[8,256]{1,0:T(8,128)S(1)} %place_rows.1.ids_ref), channel_id=1, source_target_pairs={{0,12},{4,8},{8,4},{12,0},{1,13},{5,9},{9,5},{13,1},{2,14},{6,10},... | collective-permute-start | bytes 24584 | tf_op jit(solution)/shard_map/ppermute | solution.py:310
  7.0 0.0 collective-permute-start.1
  7.0 2.7 %decode_tables.1.table_ref = bf16[8,80,1024]{2,1,0:T(8,128)(2,1)S(1)} custom-call(bf16[8,80,1024]{2,1,0:T(8,128)(2,1)} %bitcast.8, bf16[5,8,1024]{2,1,0:T(8,128)(2,1)} %bitcast.9), custom_call_target="tpu_custom_call" | custom-call | tf_op jit(solution)/shard_map/decode_tables/pallas_call | solution.py:391
  9.7 0.0 collective-permute-done.ids_ref
  9.7 1.2 %collective-permute-done.1.ids_ref = s32[8,256]{1,0:T(8,128)S(1)} collective-permute-done((s32[8,256]{1,0:T(8,128)S(1)}, s32[8,256]{1,0:T(8,128)S(1)}, u32[]{:S(2)}, u32[]{:S(2)}) %collective-permute-start.1) | collective-permute-done | bytes 8224 | tf_op jit(solution)/shard_map/ppermute | solution.py:313
  10.9 0.9 %pick_rows.4 = bf16[640,256]{1,0:T(8,128)(2,1)S(1)} custom-call(s32[1]{0:T(128)} %bitcast.3.base_ref, s32[8,256]{1,0:T(8,128)S(1)} %collective-permute-done.ids_ref, bf16[8,80,1024]{2,1,0:T(8,128)(2,1)S(1)} %decode_tables.1.table_ref), custom_call_target="tpu_custom_call" | custom-call | tf_op jit(solution)/shard_map/pick_rows/pallas_call | solution.py:316
  11.8 2.0 %collective-permute-start.7 = (bf16[640,256]{1,0:T(8,128)(2,1)S(1)}, bf16[640,256]{1,0:T(8,128)(2,1)S(1)}, u32[]{:S(2)}, u32[]{:S(2)}) collective-permute-start(bf16[640,256]{1,0:T(8,128)(2,1)S(1)} %pick_rows.4), channel_id=1, source_target_pairs={{0,4},{12,8},{1,5},{13,9},{2,6},{14,10},{3,7},{15,11},{16,20},{28,... | collective-permute-start | bytes 983048 | tf_op jit(solution)/shard_map/ppermute | solution.py:326
  13.9 0.7 %collective-permute-start.8 = (bf16[640,256]{1,0:T(8,128)(2,1)S(1)}, bf16[640,256]{1,0:T(8,128)(2,1)S(1)}, u32[]{:S(2)}, u32[]{:S(2)}) collective-permute-start(bf16[640,256]{1,0:T(8,128)(2,1)S(1)} %pick_rows.4), channel_id=1, source_target_pairs={{4,8},{8,4},{5,9},{9,5},{6,10},{10,6},{7,11},{11,7},{20,24},{24,20... | collective-permute-start | bytes 983048 | tf_op jit(solution)/shard_map/ppermute | solution.py:326
  14.6 0.9 %pick_rows.5 = bf16[640,256]{1,0:T(8,128)(2,1)S(1)} custom-call(s32[1]{0:T(128)} %bitcast.3.base_ref, s32[8,256]{1,0:T(8,128)S(1)} %collective-permute-done.1.ids_ref, bf16[8,80,1024]{2,1,0:T(8,128)(2,1)S(1)} %decode_tables.1.table_ref), custom_call_target="tpu_custom_call" | custom-call | tf_op jit(solution)/shard_map/pick_rows/pallas_call | solution.py:316
  15.4 0.0 copy-start
  15.4 0.0 collective-permute-done.2.refs_4_
  15.4 0.0 collective-permute-done.3.refs_5_
  15.5 2.2 %collective-permute-start.5 = (s32[8,256]{1,0:T(8,128)S(1)}, s32[8,256]{1,0:T(8,128)S(1)}, u32[]{:S(2)}, u32[]{:S(2)}) collective-permute-start(s32[8,256]{1,0:T(8,128)S(1)} %place_rows.1.ids_ref), channel_id=1, source_target_pairs={{0,4},{4,0},{8,12},{12,8},{1,5},{5,1},{9,13},{13,9},{2,6},{6,2},{1... | collective-permute-start | bytes 24584 | tf_op jit(solution)/shard_map/ppermute | solution.py:310
  17.6 2.6 %collective-permute-start.4 = (bf16[640,256]{1,0:T(8,128)(2,1)S(1)}, bf16[640,256]{1,0:T(8,128)(2,1)S(1)}, u32[]{:S(2)}, u32[]{:S(2)}) collective-permute-start(bf16[640,256]{1,0:T(8,128)(2,1)S(1)} %pick_rows.5), channel_id=1, source_target_pairs={{0,9},{1,8},{12,5},{13,4},{2,11},{3,10},{14,7},{15,6},{16,25},{17,... | collective-permute-start | bytes 983048 | tf_op jit(solution)/shard_map/ppermute | solution.py:313
  20.2 0.3 collective-permute-done.5.ids_ref
  20.6 0.9 %pick_rows.7 = bf16[640,256]{1,0:T(8,128)(2,1)S(1)} custom-call(s32[1]{0:T(128)} %bitcast.3.base_ref, s32[8,256]{1,0:T(8,128)S(1)} %collective-permute-done.5.ids_ref, bf16[8,80,1024]{2,1,0:T(8,128)(2,1)S(1)} %decode_tables.1.table_ref), custom_call_target="tpu_custom_call" | custom-call | tf_op jit(solution)/shard_map/pick_rows/pallas_call | solution.py:316
  21.4 2.5 %collective-permute-start.6 = (bf16[640,256]{1,0:T(8,128)(2,1)S(1)}, bf16[640,256]{1,0:T(8,128)(2,1)S(1)}, u32[]{:S(2)}, u32[]{:S(2)}) collective-permute-start(bf16[640,256]{1,0:T(8,128)(2,1)S(1)} %pick_rows.7), channel_id=1, source_target_pairs={{0,4},{4,0},{8,12},{12,8},{1,5},{5,1},{9,13},{13,9},{2,6},{6,2},{1... | collective-permute-start | bytes 983048 | tf_op jit(solution)/shard_map/ppermute | solution.py:326
  24.0 0.9 %pick_rows.6 = bf16[640,256]{1,0:T(8,128)(2,1)S(1)} custom-call(s32[1]{0:T(128)} %bitcast.3.base_ref, s32[8,256]{1,0:T(8,128)S(1)} %place_rows.1.ids_ref, bf16[8,80,1024]{2,1,0:T(8,128)(2,1)S(1)} %decode_tables.1.table_ref), custom_call_target="tpu_custom_call" | custom-call | tf_op jit(solution)/shard_map/pick_rows/pallas_call | solution.py:316
  24.8 0.0 collective-permute-done.7
  24.8 0.1 add.20
  24.9 0.0 collective-permute-done.8.refs_1_
  24.9 1.3 %collective-permute-start.10 = (bf16[640,256]{1,0:T(8,128)(2,1)S(1)}, bf16[640,256]{1,0:T(8,128)(2,1)S(1)}, u32[]{:S(2)}, u32[]{:S(2)}) collective-permute-start(bf16[640,256]{1,0:T(8,128)(2,1)S(1)} %add.20), channel_id=1, source_target_pairs={{4,12},{8,0},{5,13},{9,1},{6,14},{10,2},{7,15},{11,3},{20,28},{24,... | collective-permute-start | bytes 983048 | tf_op jit(solution)/shard_map/ppermute | solution.py:326
  26.2 0.0 copy-done
  26.3 1.3 %collective-permute-start.9 = (bf16[16,2304]{1,0:T(8,128)(2,1)S(1)}, bf16[16,2304]{1,0:T(8,128)(2,1)S(1)}, u32[]{:S(2)}, u32[]{:S(2)}) collective-permute-start(bf16[16,2304]{1,0:T(8,128)(2,1)S(1)} %slice.6), channel_id=1, source_target_pairs={{0,1},{4,5},{8,9},{12,13},{2,3},{6,7},{10,11},{14,15},{16,17},{20,... | collective-permute-start | bytes 221192 | tf_op jit(solution)/shard_map/ppermute | solution.py:410
  27.6 0.7 %collective-permute-done.4 = bf16[640,256]{1,0:T(8,128)(2,1)S(1)} collective-permute-done((bf16[640,256]{1,0:T(8,128)(2,1)S(1)}, bf16[640,256]{1,0:T(8,128)(2,1)S(1)}, u32[]{:S(2)}, u32[]{:S(2)}) %collective-permute-start.4) | collective-permute-done | bytes 327712 | tf_op jit(solution)/shard_map/ppermute | solution.py:313
  28.3 6.7 %collective-permute-done.6 = bf16[640,256]{1,0:T(8,128)(2,1)S(1)} collective-permute-done((bf16[640,256]{1,0:T(8,128)(2,1)S(1)}, bf16[640,256]{1,0:T(8,128)(2,1)S(1)}, u32[]{:S(2)}, u32[]{:S(2)}) %collective-permute-start.6) | collective-permute-done | bytes 327712 | tf_op jit(solution)/shard_map/ppermute | solution.py:326
  35.0 0.0 collective-permute-done.9.refs_5_
  35.0 7.5 %collective-permute-done.10.refs_2_ = bf16[640,256]{1,0:T(8,128)(2,1)S(1)} collective-permute-done((bf16[640,256]{1,0:T(8,128)(2,1)S(1)}, bf16[640,256]{1,0:T(8,128)(2,1)S(1)}, u32[]{:S(2)}, u32[]{:S(2)}) %collective-permute-start.10) | collective-permute-done | bytes 327712 | tf_op jit(solution)/shard_map/ppermute | solution.py:326
  42.5 0.1 merge.1.refs_1_
  42.7 1.6 %collective-permute-start.12 = (bf16[640,256]{1,0:T(8,128)(2,1)S(1)}, bf16[640,256]{1,0:T(8,128)(2,1)S(1)}, u32[]{:S(2)}, u32[]{:S(2)}) collective-permute-start(bf16[640,256]{1,0:T(8,128)(2,1)S(1)} %merge.1.refs_1_), channel_id=1, source_target_pairs={{0,2},{2,0},{1,3},{3,1},{4,6},{6,4},{5,7},{7,5},{8,10},{10,8},{9,1... | collective-permute-start | bytes 983048 | tf_op jit(solution)/shard_map/ppermute | solution.py:421
  44.2 1.3 %collective-permute-start.13 = (bf16[640,128]{1,0:T(8,128)(2,1)S(1)}, bf16[640,128]{1,0:T(8,128)(2,1)S(1)}, u32[]{:S(2)}, u32[]{:S(2)}) collective-permute-start(bf16[640,128]{1,0:T(8,128)(2,1)S(1)} %slice.8), channel_id=1, source_target_pairs={{0,1},{2,3},{4,5},{6,7},{8,9},{10,11},{12,13},{14,15},{16,17},{18,... | collective-permute-start | bytes 491528 | tf_op jit(solution)/shard_map/ppermute | solution.py:434
  45.5 1.5 %collective-permute-start.11 = (bf16[640,128]{1,0:T(8,128)(2,1)S(1)}, bf16[640,128]{1,0:T(8,128)(2,1)S(1)}, u32[]{:S(2)}, u32[]{:S(2)}) collective-permute-start(bf16[640,128]{1,0:T(8,128)(2,1)S(1)} %slice.8), channel_id=1, source_target_pairs={{0,3},{2,1},{4,7},{6,5},{8,11},{10,9},{12,15},{14,13},{16,19},{18,... | collective-permute-start | bytes 491528 | tf_op jit(solution)/shard_map/ppermute | solution.py:434
  47.0 0.1 pad_add_fusion.where_ref
  47.1 0.0 collective-permute-done.13.refs_0_
  47.1 5.6 %project_own.1 = (f32[2,272,1152]{2,1,0:T(8,128)S(1)}, f32[2,272,1152]{2,1,0:T(8,128)S(1)}, bf16[2,2,640,1152]{3,2,1,0:T(8,128)(2,1)S(1)}) custom-call(s32[2]{0:T(128)S(1)} %pad_add_fusion.where_ref, bf16[640,128]{1,0:T(8,128)(2,1)S(1)} %collective-permute-done.13.refs_0_, bf16[640,256]{1,0:T(8,128)(2,1)S(1)} %merge.1.refs_1_, bf16[1280,1152]{1,0:T(8,128)(2,1)} %refs_2_.1, ...), custom_call_target="tpu_custom_call" | custom-call | tf_op jit(solution)/shard_map/project_own/pallas_call | solution.py:440
  52.7 0.0 collective-permute-done.11.refs_0_
  52.7 0.0 collective-permute-done.12.refs_1_
  52.8 0.0 copy-start.1
  52.8 4.2 %project_others.1 = (f32[2,272,1152]{2,1,0:T(8,128)}, f32[8,272]{1,0:T(8,128)S(1)}) custom-call(s32[2]{0:T(128)S(1)} %pad_add_fusion.where_ref, bf16[640,128]{1,0:T(8,128)(2,1)S(1)} %collective-permute-done.11.refs_0_, bf16[640,256]{1,0:T(8,128)(2,1)S(1)} %collective-permute-done.12.refs_1_, bf16[2,2,640,1152]{3,2,1,0:T(8,128)(2,1)S(1)} %get-tuple-element.35.refs_2_, ...), custom_call_target="tpu_custom_call" | custom-call | tf_op jit(solution)/shard_map/project_others/pallas_call | solution.py:453
  57.0 1.4 %collective-permute-start.14 = (f32[8,272]{1,0:T(8,128)S(1)}, f32[8,272]{1,0:T(8,128)S(1)}, u32[]{:S(2)}, u32[]{:S(2)}) collective-permute-start(f32[8,272]{1,0:T(8,128)S(1)} %get-tuple-element.39.refs_0_), channel_id=1, source_target_pairs={{0,2},{2,0},{1,3},{3,1},{4,6},{6,4},{5,7},{7,5},{8,10},{10,8},{9,1... | collective-permute-start | bytes 26120 | tf_op jit(solution)/shard_map/ppermute | solution.py:476
  58.4 2.3 %collective-permute-done.14.refs_1_ = f32[8,272]{1,0:T(8,128)S(1)} collective-permute-done((f32[8,272]{1,0:T(8,128)S(1)}, f32[8,272]{1,0:T(8,128)S(1)}, u32[]{:S(2)}, u32[]{:S(2)}) %collective-permute-start.14) | collective-permute-done | bytes 8736 | tf_op jit(solution)/shard_map/ppermute | solution.py:476
  60.8 0.0 copy-done.1
  60.8 4.0 %finish.1 = bf16[256,2304]{1,0:T(8,128)(2,1)} custom-call(s32[1]{0:T(128)} %bitcast.keep_ref, f32[8,272]{1,0:T(8,128)S(1)} %get-tuple-element.39.refs_0_, f32[8,272]{1,0:T(8,128)S(1)} %collective-permute-done.14.refs_1_, f32[2,272,1152]{2,1,0:T(8,128)} %get-tuple-element.40.refs_2_, bf16[256,2304]{1,0:T(8,128)(2,1)S(1)} %copy-done, f32[4,2304]{1,0:T(4,128)S(1)} %copy-done.1), custom_call_target="tpu_custom_call" | custom-call | tf_op jit(solution)/shard_map/finish/pallas_call | solution.py:482
  (3 shorter events, 0.1 us)
Async XLA Ops:
  0.0 15.4 %collective-permute-start.2 = (bf16[1280,1152]{1,0:T(8,128)(2,1)}, bf16[1280,1152]{1,0:T(8,128)(2,1)}, u32[]{:S(2)}, u32[]{:S(2)}) collective-permute-start(bf16[1280,1152]{1,0:T(8,128)(2,1)} %refs_2_.1), channel_id=1, source_target_pairs={{0,1},{1,0},{2,3},{3,2},{4,5},{5,4},{6,7},{7,6},{8,9},{9,8},{10,11... | collective-permute-start | bytes 8847368 | tf_op jit(solution)/shard_map/ppermute | solution.py:404
  0.5 15.0 %collective-permute-start.3 = (bf16[1280,1152]{1,0:T(8,128)(2,1)}, bf16[1280,1152]{1,0:T(8,128)(2,1)}, u32[]{:S(2)}, u32[]{:S(2)}) collective-permute-start(bf16[1280,1152]{1,0:T(8,128)(2,1)} %refs_3_.2), channel_id=1, source_target_pairs={{0,1},{1,0},{2,3},{3,2},{4,5},{5,4},{6,7},{7,6},{8,9},{9,8},{10,11... | collective-permute-start | bytes 8847368 | tf_op jit(solution)/shard_map/ppermute | solution.py:405
  1.9 7.9 %collective-permute-start = (s32[8,256]{1,0:T(8,128)S(1)}, s32[8,256]{1,0:T(8,128)S(1)}, u32[]{:S(2)}, u32[]{:S(2)}) collective-permute-start(s32[8,256]{1,0:T(8,128)S(1)} %place_rows.1.ids_ref), channel_id=1, source_target_pairs={{0,12},{4,8},{8,4},{12,0},{1,13},{5,9},{9,5},{13,1},{2,14},{6,10},... | collective-permute-start | bytes 24584 | tf_op jit(solution)/shard_map/ppermute | solution.py:310
  7.0 4.0 %collective-permute-start.1 = (s32[8,256]{1,0:T(8,128)S(1)}, s32[8,256]{1,0:T(8,128)S(1)}, u32[]{:S(2)}, u32[]{:S(2)}) collective-permute-start(s32[8,256]{1,0:T(8,128)S(1)} %place_rows.1.ids_ref), channel_id=1, source_target_pairs={{0,8},{1,9},{4,13},{5,12},{8,1},{9,0},{12,4},{13,5},{2,10},{3,11},... | collective-permute-start | bytes 24584 | tf_op jit(solution)/shard_map/ppermute | solution.py:313
  11.8 13.0 %collective-permute-start.7 = (bf16[640,256]{1,0:T(8,128)(2,1)S(1)}, bf16[640,256]{1,0:T(8,128)(2,1)S(1)}, u32[]{:S(2)}, u32[]{:S(2)}) collective-permute-start(bf16[640,256]{1,0:T(8,128)(2,1)S(1)} %pick_rows.4), channel_id=1, source_target_pairs={{0,4},{12,8},{1,5},{13,9},{2,6},{14,10},{3,7},{15,11},{16,20},{28,... | collective-permute-start | bytes 983048 | tf_op jit(solution)/shard_map/ppermute | solution.py:326
  13.9 11.1 %collective-permute-start.8 = (bf16[640,256]{1,0:T(8,128)(2,1)S(1)}, bf16[640,256]{1,0:T(8,128)(2,1)S(1)}, u32[]{:S(2)}, u32[]{:S(2)}) collective-permute-start(bf16[640,256]{1,0:T(8,128)(2,1)S(1)} %pick_rows.4), channel_id=1, source_target_pairs={{4,8},{8,4},{5,9},{9,5},{6,10},{10,6},{7,11},{11,7},{20,24},{24,20... | collective-permute-start | bytes 983048 | tf_op jit(solution)/shard_map/ppermute | solution.py:326
  15.4 10.8 %copy-start = (bf16[256,2304]{1,0:T(8,128)(2,1)S(1)}, bf16[256,2304]{1,0:T(8,128)(2,1)}, u32[]{:S(2)}) copy-start(bf16[256,2304]{1,0:T(8,128)(2,1)} %refs_3_.3) | copy-start | bytes 3538948
  15.5 5.1 %collective-permute-start.5 = (s32[8,256]{1,0:T(8,128)S(1)}, s32[8,256]{1,0:T(8,128)S(1)}, u32[]{:S(2)}, u32[]{:S(2)}) collective-permute-start(s32[8,256]{1,0:T(8,128)S(1)} %place_rows.1.ids_ref), channel_id=1, source_target_pairs={{0,4},{4,0},{8,12},{12,8},{1,5},{5,1},{9,13},{13,9},{2,6},{6,2},{1... | collective-permute-start | bytes 24584 | tf_op jit(solution)/shard_map/ppermute | solution.py:310
  17.6 10.6 %collective-permute-start.4 = (bf16[640,256]{1,0:T(8,128)(2,1)S(1)}, bf16[640,256]{1,0:T(8,128)(2,1)S(1)}, u32[]{:S(2)}, u32[]{:S(2)}) collective-permute-start(bf16[640,256]{1,0:T(8,128)(2,1)S(1)} %pick_rows.5), channel_id=1, source_target_pairs={{0,9},{1,8},{12,5},{13,4},{2,11},{3,10},{14,7},{15,6},{16,25},{17,... | collective-permute-start | bytes 983048 | tf_op jit(solution)/shard_map/ppermute | solution.py:313
  21.4 13.5 %collective-permute-start.6 = (bf16[640,256]{1,0:T(8,128)(2,1)S(1)}, bf16[640,256]{1,0:T(8,128)(2,1)S(1)}, u32[]{:S(2)}, u32[]{:S(2)}) collective-permute-start(bf16[640,256]{1,0:T(8,128)(2,1)S(1)} %pick_rows.7), channel_id=1, source_target_pairs={{0,4},{4,0},{8,12},{12,8},{1,5},{5,1},{9,13},{13,9},{2,6},{6,2},{1... | collective-permute-start | bytes 983048 | tf_op jit(solution)/shard_map/ppermute | solution.py:326
  24.9 17.6 %collective-permute-start.10 = (bf16[640,256]{1,0:T(8,128)(2,1)S(1)}, bf16[640,256]{1,0:T(8,128)(2,1)S(1)}, u32[]{:S(2)}, u32[]{:S(2)}) collective-permute-start(bf16[640,256]{1,0:T(8,128)(2,1)S(1)} %add.20), channel_id=1, source_target_pairs={{4,12},{8,0},{5,13},{9,1},{6,14},{10,2},{7,15},{11,3},{20,28},{24,... | collective-permute-start | bytes 983048 | tf_op jit(solution)/shard_map/ppermute | solution.py:326
  26.3 8.7 %collective-permute-start.9 = (bf16[16,2304]{1,0:T(8,128)(2,1)S(1)}, bf16[16,2304]{1,0:T(8,128)(2,1)S(1)}, u32[]{:S(2)}, u32[]{:S(2)}) collective-permute-start(bf16[16,2304]{1,0:T(8,128)(2,1)S(1)} %slice.6), channel_id=1, source_target_pairs={{0,1},{4,5},{8,9},{12,13},{2,3},{6,7},{10,11},{14,15},{16,17},{20,... | collective-permute-start | bytes 221192 | tf_op jit(solution)/shard_map/ppermute | solution.py:410
  42.7 10.1 %collective-permute-start.12 = (bf16[640,256]{1,0:T(8,128)(2,1)S(1)}, bf16[640,256]{1,0:T(8,128)(2,1)S(1)}, u32[]{:S(2)}, u32[]{:S(2)}) collective-permute-start(bf16[640,256]{1,0:T(8,128)(2,1)S(1)} %merge.1.refs_1_), channel_id=1, source_target_pairs={{0,2},{2,0},{1,3},{3,1},{4,6},{6,4},{5,7},{7,5},{8,10},{10,8},{9,1... | collective-permute-start | bytes 983048 | tf_op jit(solution)/shard_map/ppermute | solution.py:421
  44.2 2.9 %collective-permute-start.13 = (bf16[640,128]{1,0:T(8,128)(2,1)S(1)}, bf16[640,128]{1,0:T(8,128)(2,1)S(1)}, u32[]{:S(2)}, u32[]{:S(2)}) collective-permute-start(bf16[640,128]{1,0:T(8,128)(2,1)S(1)} %slice.8), channel_id=1, source_target_pairs={{0,1},{2,3},{4,5},{6,7},{8,9},{10,11},{12,13},{14,15},{16,17},{18,... | collective-permute-start | bytes 491528 | tf_op jit(solution)/shard_map/ppermute | solution.py:434
  45.5 7.2 %collective-permute-start.11 = (bf16[640,128]{1,0:T(8,128)(2,1)S(1)}, bf16[640,128]{1,0:T(8,128)(2,1)S(1)}, u32[]{:S(2)}, u32[]{:S(2)}) collective-permute-start(bf16[640,128]{1,0:T(8,128)(2,1)S(1)} %slice.8), channel_id=1, source_target_pairs={{0,3},{2,1},{4,7},{6,5},{8,11},{10,9},{12,15},{14,13},{16,19},{18,... | collective-permute-start | bytes 491528 | tf_op jit(solution)/shard_map/ppermute | solution.py:434
  52.8 8.0 %copy-start.1 = (f32[4,2304]{1,0:T(4,128)S(1)}, f32[4,2304]{1,0:T(4,128)}, u32[]{:S(2)}) copy-start(f32[4,2304]{1,0:T(4,128)} %refs_4_.1) | copy-start | bytes 110596
  57.0 3.8 %collective-permute-start.14 = (f32[8,272]{1,0:T(8,128)S(1)}, f32[8,272]{1,0:T(8,128)S(1)}, u32[]{:S(2)}, u32[]{:S(2)}) collective-permute-start(f32[8,272]{1,0:T(8,128)S(1)} %get-tuple-element.39.refs_0_), channel_id=1, source_target_pairs={{0,2},{2,0},{1,3},{3,1},{4,6},{6,4},{5,7},{7,5},{8,10},{10,8},{9,1... | collective-permute-start | bytes 26120 | tf_op jit(solution)/shard_map/ppermute | solution.py:476

commit v13 on v12

--- a/solution.py
+++ b/solution.py
@@ -340,8 +340,7 @@
     rows_1 = pick(ask(stored, 1))
     own = pick(stored)
     beside = send(rows_1, (0, 1), (1, 0), (2, 3), (3, 2))
-    onward = after(rows_2, rows_1, own) + inward
-    onward = after(onward, across)
+    onward = after(rows_2, rows_1, own, across) + inward
     other = meanwhile(onward)
     onward = send(onward, (1, 3), (2, 0))
     own, other = lax.optimization_barrier((own + past + beside, other))

time: 65.3 us -> 65.9 us (level)
    ppermute x2, waiting for transfers between devices: 0.34 us -> 3.98 us  [ask(): return lax.ppermute(ids, 'mem', [(i, i ^ x) for i in range(4)])]
    ppermute x4, waiting for transfers between devices: 14.2 us -> 10.6 us  [send(): return lax.ppermute(x, 'mem', pairs)]
    ppermute x4, starting transfers between devices: 6.57 us -> 9.29 us  [send(): return lax.ppermute(x, 'mem', pairs)]
    ppermute x2, starting transfers between devices: 7.27 us -> 5.19 us  [ask(): return lax.ppermute(ids, 'mem', [(i, i ^ x) for i in range(4)])]
    ppermute x2, waiting for transfers between devices: 1.88 us -> 1.21 us  [crossing(): lax.ppermute(x, ('mem', 'rep'), [(2 * a + b, 2 * c + d) for a, b, c, d in...]
    ppermute x1, waiting for transfers between devices: 2.35 us -> 3.01 us  [shards(): lax.ppermute(stats, 'tp', [(i, (i + s) % tps) for i in range(tps)])]
    ppermute x1, starting transfers between devices: 1.41 us -> 0.75 us  [shards(): lax.ppermute(stats, 'tp', [(i, (i + s) % tps) for i in range(tps)])]
  transfers between devices with their start and end apart: 15 -> 15, of which waited for: 6 -> 4; matrix products, arithmetic and copies ran while one was open for 0% -> 0% of each run, Pallas kernels for 20% -> 20%
where the time goes in v13:
time: 65.9 us; the launch traced here: 65.5 us
  starting transfers between devices  24.6 us (37%)
  Pallas kernels  21.4 us (32%)
  waiting for transfers between devices  18.9 us (29%)
    ppermute x4, waiting for transfers between devices, send(): return lax.ppermute(x, 'mem', pairs)  10.6 us
    ppermute x4, starting transfers between devices, send(): return lax.ppermute(x, 'mem', pairs)  9.29 us
    pallas_call x1, Pallas kernels, shards(): pl.pallas_call(functools.partial(project_kernel, (0,), tps), in_specs=[sm...  5.6 us
    ppermute x2, starting transfers between devices, ask(): return lax.ppermute(ids, 'mem', [(i, i ^ x) for i in range(4)])  5.19 us
    pallas_call x1, Pallas kernels, shards(): pl.pallas_call(functools.partial(project_kernel, tuple(range(1, tps)), tp...  4.24 us
    ppermute x2, waiting for transfers between devices, ask(): return lax.ppermute(ids, 'mem', [(i, i ^ x) for i in range(4)])  3.98 us
    pallas_call x1, Pallas kernels, shards(): pl.pallas_call(functools.partial(finish_kernel, tps, step), in_specs=[sme...  3.96 us
    pallas_call x4, Pallas kernels, pick(): pl.pallas_call(pick_kernel, in_specs=[pl.BlockSpec(memory_space=pltpu.SME...  3.45 us
  transfers between devices with their start and end apart: 15, of which 4 were waited for; matrix products, arithmetic and copies ran while one was open for 0% of the time, Pallas kernels for 20%

profile of v13, /device:TPU:0, one launch (start us, length us, event | category | flops | bytes accessed | tf_op | source)
XLA Modules:
  0.0 65.5 jit_solution(7440927847200999493)
XLA Ops:
  0.0 0.5 collective-permute-start.2
  0.5 0.1 collective-permute-start.3
  0.5 1.3 %place_rows.1.ids_ref = s32[8,256]{1,0:T(8,128)S(1)} custom-call(s32[8,256]{1,0:T(8,128)} %bitcast.11, s32[32,128]{1,0:T(8,128)} %bitcast.10), custom_call_target="tpu_custom_call" | custom-call | tf_op jit(solution)/shard_map/place_rows/pallas_call | solution.py:376
  1.9 5.1 %collective-permute-start = (s32[8,256]{1,0:T(8,128)S(1)}, s32[8,256]{1,0:T(8,128)S(1)}, u32[]{:S(2)}, u32[]{:S(2)}) collective-permute-start(s32[8,256]{1,0:T(8,128)S(1)} %place_rows.1.ids_ref), channel_id=1, source_target_pairs={{0,12},{4,8},{8,4},{12,0},{1,13},{5,9},{9,5},{13,1},{2,14},{6,10},... | collective-permute-start | bytes 24584 | tf_op jit(solution)/shard_map/ppermute | solution.py:310
  7.0 0.0 collective-permute-start.1
  7.0 2.7 %decode_tables.1.table_ref = bf16[8,80,1024]{2,1,0:T(8,128)(2,1)S(1)} custom-call(bf16[8,80,1024]{2,1,0:T(8,128)(2,1)} %bitcast.8, bf16[5,8,1024]{2,1,0:T(8,128)(2,1)} %bitcast.9), custom_call_target="tpu_custom_call" | custom-call | tf_op jit(solution)/shard_map/decode_tables/pallas_call | solution.py:390
  9.7 0.0 collective-permute-done.ids_ref
  9.7 1.2 %collective-permute-done.1.ids_ref = s32[8,256]{1,0:T(8,128)S(1)} collective-permute-done((s32[8,256]{1,0:T(8,128)S(1)}, s32[8,256]{1,0:T(8,128)S(1)}, u32[]{:S(2)}, u32[]{:S(2)}) %collective-permute-start.1) | collective-permute-done | bytes 8224 | tf_op jit(solution)/shard_map/ppermute | solution.py:313
  10.9 0.9 %pick_rows.4 = bf16[640,256]{1,0:T(8,128)(2,1)S(1)} custom-call(s32[1]{0:T(128)} %bitcast.3.base_ref, s32[8,256]{1,0:T(8,128)S(1)} %collective-permute-done.ids_ref, bf16[8,80,1024]{2,1,0:T(8,128)(2,1)S(1)} %decode_tables.1.table_ref), custom_call_target="tpu_custom_call" | custom-call | tf_op jit(solution)/shard_map/pick_rows/pallas_call | solution.py:316
  11.8 0.7 %collective-permute-start.7 = (bf16[640,256]{1,0:T(8,128)(2,1)S(1)}, bf16[640,256]{1,0:T(8,128)(2,1)S(1)}, u32[]{:S(2)}, u32[]{:S(2)}) collective-permute-start(bf16[640,256]{1,0:T(8,128)(2,1)S(1)} %pick_rows.4), channel_id=1, source_target_pairs={{4,8},{8,4},{5,9},{9,5},{6,10},{10,6},{7,11},{11,7},{20,24},{24,20... | collective-permute-start | bytes 983048 | tf_op jit(solution)/shard_map/ppermute | solution.py:326
  12.5 4.8 %collective-permute-start.8 = (bf16[640,256]{1,0:T(8,128)(2,1)S(1)}, bf16[640,256]{1,0:T(8,128)(2,1)S(1)}, u32[]{:S(2)}, u32[]{:S(2)}) collective-permute-start(bf16[640,256]{1,0:T(8,128)(2,1)S(1)} %pick_rows.4), channel_id=1, source_target_pairs={{0,4},{12,8},{1,5},{13,9},{2,6},{14,10},{3,7},{15,11},{16,20},{28,... | collective-permute-start | bytes 983048 | tf_op jit(solution)/shard_map/ppermute | solution.py:326
  17.3 0.9 %pick_rows.5 = bf16[640,256]{1,0:T(8,128)(2,1)S(1)} custom-call(s32[1]{0:T(128)} %bitcast.3.base_ref, s32[8,256]{1,0:T(8,128)S(1)} %collective-permute-done.1.ids_ref, bf16[8,80,1024]{2,1,0:T(8,128)(2,1)S(1)} %decode_tables.1.table_ref), custom_call_target="tpu_custom_call" | custom-call | tf_op jit(solution)/shard_map/pick_rows/pallas_call | solution.py:316
  18.1 0.0 copy-start
  18.2 0.0 collective-permute-done.2.refs_4_
  18.2 0.0 collective-permute-done.3.refs_5_
  18.2 0.1 collective-permute-start.5
  18.3 3.2 %collective-permute-start.4 = (bf16[640,256]{1,0:T(8,128)(2,1)S(1)}, bf16[640,256]{1,0:T(8,128)(2,1)S(1)}, u32[]{:S(2)}, u32[]{:S(2)}) collective-permute-start(bf16[640,256]{1,0:T(8,128)(2,1)S(1)} %pick_rows.5), channel_id=1, source_target_pairs={{0,9},{1,8},{12,5},{13,4},{2,11},{3,10},{14,7},{15,6},{16,25},{17,... | collective-permute-start | bytes 983048 | tf_op jit(solution)/shard_map/ppermute | solution.py:313
  21.5 4.0 %collective-permute-done.5.ids_ref = s32[8,256]{1,0:T(8,128)S(1)} collective-permute-done((s32[8,256]{1,0:T(8,128)S(1)}, s32[8,256]{1,0:T(8,128)S(1)}, u32[]{:S(2)}, u32[]{:S(2)}) %collective-permute-start.5) | collective-permute-done | bytes 8224 | tf_op jit(solution)/shard_map/ppermute | solution.py:310
  25.4 0.9 %pick_rows.7 = bf16[640,256]{1,0:T(8,128)(2,1)S(1)} custom-call(s32[1]{0:T(128)} %bitcast.3.base_ref, s32[8,256]{1,0:T(8,128)S(1)} %collective-permute-done.5.ids_ref, bf16[8,80,1024]{2,1,0:T(8,128)(2,1)S(1)} %decode_tables.1.table_ref), custom_call_target="tpu_custom_call" | custom-call | tf_op jit(solution)/shard_map/pick_rows/pallas_call | solution.py:316
  26.3 2.5 %collective-permute-start.6 = (bf16[640,256]{1,0:T(8,128)(2,1)S(1)}, bf16[640,256]{1,0:T(8,128)(2,1)S(1)}, u32[]{:S(2)}, u32[]{:S(2)}) collective-permute-start(bf16[640,256]{1,0:T(8,128)(2,1)S(1)} %pick_rows.7), channel_id=1, source_target_pairs={{0,4},{4,0},{8,12},{12,8},{1,5},{5,1},{9,13},{13,9},{2,6},{6,2},{1... | collective-permute-start | bytes 983048 | tf_op jit(solution)/shard_map/ppermute | solution.py:326
  28.8 0.9 %pick_rows.6 = bf16[640,256]{1,0:T(8,128)(2,1)S(1)} custom-call(s32[1]{0:T(128)} %bitcast.3.base_ref, s32[8,256]{1,0:T(8,128)S(1)} %place_rows.1.ids_ref, bf16[8,80,1024]{2,1,0:T(8,128)(2,1)S(1)} %decode_tables.1.table_ref), custom_call_target="tpu_custom_call" | custom-call | tf_op jit(solution)/shard_map/pick_rows/pallas_call | solution.py:316
  29.7 0.0 collective-permute-done.7.refs_1_
  29.7 0.0 collective-permute-done.8
  29.7 0.1 add.20
  29.8 1.3 %collective-permute-start.10 = (bf16[640,256]{1,0:T(8,128)(2,1)S(1)}, bf16[640,256]{1,0:T(8,128)(2,1)S(1)}, u32[]{:S(2)}, u32[]{:S(2)}) collective-permute-start(bf16[640,256]{1,0:T(8,128)(2,1)S(1)} %add.20), channel_id=1, source_target_pairs={{4,12},{8,0},{5,13},{9,1},{6,14},{10,2},{7,15},{11,3},{20,28},{24,... | collective-permute-start | bytes 983048 | tf_op jit(solution)/shard_map/ppermute | solution.py:326
  31.1 0.0 copy-done
  31.2 1.3 %collective-permute-start.9 = (bf16[16,2304]{1,0:T(8,128)(2,1)S(1)}, bf16[16,2304]{1,0:T(8,128)(2,1)S(1)}, u32[]{:S(2)}, u32[]{:S(2)}) collective-permute-start(bf16[16,2304]{1,0:T(8,128)(2,1)S(1)} %slice.6), channel_id=1, source_target_pairs={{0,1},{4,5},{8,9},{12,13},{2,3},{6,7},{10,11},{14,15},{16,17},{20,... | collective-permute-start | bytes 221192 | tf_op jit(solution)/shard_map/ppermute | solution.py:409
  32.5 0.0 collective-permute-done.4
  32.5 10.6 %collective-permute-done.6 = bf16[640,256]{1,0:T(8,128)(2,1)S(1)} collective-permute-done((bf16[640,256]{1,0:T(8,128)(2,1)S(1)}, bf16[640,256]{1,0:T(8,128)(2,1)S(1)}, u32[]{:S(2)}, u32[]{:S(2)}) %collective-permute-start.6) | collective-permute-done | bytes 327712 | tf_op jit(solution)/shard_map/ppermute | solution.py:326
  43.1 0.0 collective-permute-done.9.refs_5_
  43.2 0.0 collective-permute-done.10.refs_2_
  43.2 0.1 merge.1.refs_1_
  43.3 1.6 %collective-permute-start.12 = (bf16[640,256]{1,0:T(8,128)(2,1)S(1)}, bf16[640,256]{1,0:T(8,128)(2,1)S(1)}, u32[]{:S(2)}, u32[]{:S(2)}) collective-permute-start(bf16[640,256]{1,0:T(8,128)(2,1)S(1)} %merge.1.refs_1_), channel_id=1, source_target_pairs={{0,2},{2,0},{1,3},{3,1},{4,6},{6,4},{5,7},{7,5},{8,10},{10,8},{9,1... | collective-permute-start | bytes 983048 | tf_op jit(solution)/shard_map/ppermute | solution.py:420
  44.9 1.3 %collective-permute-start.13 = (bf16[640,128]{1,0:T(8,128)(2,1)S(1)}, bf16[640,128]{1,0:T(8,128)(2,1)S(1)}, u32[]{:S(2)}, u32[]{:S(2)}) collective-permute-start(bf16[640,128]{1,0:T(8,128)(2,1)S(1)} %slice.8), channel_id=1, source_target_pairs={{0,1},{2,3},{4,5},{6,7},{8,9},{10,11},{12,13},{14,15},{16,17},{18,... | collective-permute-start | bytes 491528 | tf_op jit(solution)/shard_map/ppermute | solution.py:433
  46.2 1.5 %collective-permute-start.11 = (bf16[640,128]{1,0:T(8,128)(2,1)S(1)}, bf16[640,128]{1,0:T(8,128)(2,1)S(1)}, u32[]{:S(2)}, u32[]{:S(2)}) collective-permute-start(bf16[640,128]{1,0:T(8,128)(2,1)S(1)} %slice.8), channel_id=1, source_target_pairs={{0,3},{2,1},{4,7},{6,5},{8,11},{10,9},{12,15},{14,13},{16,19},{18,... | collective-permute-start | bytes 491528 | tf_op jit(solution)/shard_map/ppermute | solution.py:433
  47.7 0.1 pad_add_fusion.where_ref
  47.7 0.0 collective-permute-done.13.refs_0_
  47.7 5.6 %project_own.1 = (f32[2,272,1152]{2,1,0:T(8,128)S(1)}, f32[2,272,1152]{2,1,0:T(8,128)S(1)}, bf16[2,2,640,1152]{3,2,1,0:T(8,128)(2,1)S(1)}) custom-call(s32[2]{0:T(128)S(1)} %pad_add_fusion.where_ref, bf16[640,128]{1,0:T(8,128)(2,1)S(1)} %collective-permute-done.13.refs_0_, bf16[640,256]{1,0:T(8,128)(2,1)S(1)} %merge.1.refs_1_, bf16[1280,1152]{1,0:T(8,128)(2,1)} %refs_2_.1, ...), custom_call_target="tpu_custom_call" | custom-call | tf_op jit(solution)/shard_map/project_own/pallas_call | solution.py:439
  53.4 0.0 collective-permute-done.11.refs_0_
  53.4 0.0 collective-permute-done.12.refs_1_
  53.4 0.0 copy-start.1
  53.4 4.2 %project_others.1 = (f32[2,272,1152]{2,1,0:T(8,128)}, f32[8,272]{1,0:T(8,128)S(1)}) custom-call(s32[2]{0:T(128)S(1)} %pad_add_fusion.where_ref, bf16[640,128]{1,0:T(8,128)(2,1)S(1)} %collective-permute-done.11.refs_0_, bf16[640,256]{1,0:T(8,128)(2,1)S(1)} %collective-permute-done.12.refs_1_, bf16[2,2,640,1152]{3,2,1,0:T(8,128)(2,1)S(1)} %get-tuple-element.33.refs_2_, ...), custom_call_target="tpu_custom_call" | custom-call | tf_op jit(solution)/shard_map/project_others/pallas_call | solution.py:452
  57.6 0.7 %collective-permute-start.14 = (f32[8,272]{1,0:T(8,128)S(1)}, f32[8,272]{1,0:T(8,128)S(1)}, u32[]{:S(2)}, u32[]{:S(2)}) collective-permute-start(f32[8,272]{1,0:T(8,128)S(1)} %get-tuple-element.37.refs_0_), channel_id=1, source_target_pairs={{0,2},{2,0},{1,3},{3,1},{4,6},{6,4},{5,7},{7,5},{8,10},{10,8},{9,1... | collective-permute-start | bytes 26120 | tf_op jit(solution)/shard_map/ppermute | solution.py:475
  58.4 3.0 %collective-permute-done.14.refs_1_ = f32[8,272]{1,0:T(8,128)S(1)} collective-permute-done((f32[8,272]{1,0:T(8,128)S(1)}, f32[8,272]{1,0:T(8,128)S(1)}, u32[]{:S(2)}, u32[]{:S(2)}) %collective-permute-start.14) | collective-permute-done | bytes 8736 | tf_op jit(solution)/shard_map/ppermute | solution.py:475
  61.4 0.0 copy-done.1
  61.4 4.0 %finish.1 = bf16[256,2304]{1,0:T(8,128)(2,1)} custom-call(s32[1]{0:T(128)} %bitcast.keep_ref, f32[8,272]{1,0:T(8,128)S(1)} %get-tuple-element.37.refs_0_, f32[8,272]{1,0:T(8,128)S(1)} %collective-permute-done.14.refs_1_, f32[2,272,1152]{2,1,0:T(8,128)} %get-tuple-element.38.refs_2_, bf16[256,2304]{1,0:T(8,128)(2,1)S(1)} %copy-done, f32[4,2304]{1,0:T(4,128)S(1)} %copy-done.1), custom_call_target="tpu_custom_call" | custom-call | tf_op jit(solution)/shard_map/finish/pallas_call | solution.py:481
  (3 shorter events, 0.1 us)
Async XLA Ops:
  0.0 18.2 %collective-permute-start.2 = (bf16[1280,1152]{1,0:T(8,128)(2,1)}, bf16[1280,1152]{1,0:T(8,128)(2,1)}, u32[]{:S(2)}, u32[]{:S(2)}) collective-permute-start(bf16[1280,1152]{1,0:T(8,128)(2,1)} %refs_2_.1), channel_id=1, source_target_pairs={{0,1},{1,0},{2,3},{3,2},{4,5},{5,4},{6,7},{7,6},{8,9},{9,8},{10,11... | collective-permute-start | bytes 8847368 | tf_op jit(solution)/shard_map/ppermute | solution.py:403
  0.5 17.7 %collective-permute-start.3 = (bf16[1280,1152]{1,0:T(8,128)(2,1)}, bf16[1280,1152]{1,0:T(8,128)(2,1)}, u32[]{:S(2)}, u32[]{:S(2)}) collective-permute-start(bf16[1280,1152]{1,0:T(8,128)(2,1)} %refs_3_.2), channel_id=1, source_target_pairs={{0,1},{1,0},{2,3},{3,2},{4,5},{5,4},{6,7},{7,6},{8,9},{9,8},{10,11... | collective-permute-start | bytes 8847368 | tf_op jit(solution)/shard_map/ppermute | solution.py:404
  1.9 7.9 %collective-permute-start = (s32[8,256]{1,0:T(8,128)S(1)}, s32[8,256]{1,0:T(8,128)S(1)}, u32[]{:S(2)}, u32[]{:S(2)}) collective-permute-start(s32[8,256]{1,0:T(8,128)S(1)} %place_rows.1.ids_ref), channel_id=1, source_target_pairs={{0,12},{4,8},{8,4},{12,0},{1,13},{5,9},{9,5},{13,1},{2,14},{6,10},... | collective-permute-start | bytes 24584 | tf_op jit(solution)/shard_map/ppermute | solution.py:310
  7.0 4.0 %collective-permute-start.1 = (s32[8,256]{1,0:T(8,128)S(1)}, s32[8,256]{1,0:T(8,128)S(1)}, u32[]{:S(2)}, u32[]{:S(2)}) collective-permute-start(s32[8,256]{1,0:T(8,128)S(1)} %place_rows.1.ids_ref), channel_id=1, source_target_pairs={{0,8},{1,9},{4,13},{5,12},{8,1},{9,0},{12,4},{13,5},{2,10},{3,11},... | collective-permute-start | bytes 24584 | tf_op jit(solution)/shard_map/ppermute | solution.py:313
  11.8 17.9 %collective-permute-start.7 = (bf16[640,256]{1,0:T(8,128)(2,1)S(1)}, bf16[640,256]{1,0:T(8,128)(2,1)S(1)}, u32[]{:S(2)}, u32[]{:S(2)}) collective-permute-start(bf16[640,256]{1,0:T(8,128)(2,1)S(1)} %pick_rows.4), channel_id=1, source_target_pairs={{4,8},{8,4},{5,9},{9,5},{6,10},{10,6},{7,11},{11,7},{20,24},{24,20... | collective-permute-start | bytes 983048 | tf_op jit(solution)/shard_map/ppermute | solution.py:326
  12.5 17.2 %collective-permute-start.8 = (bf16[640,256]{1,0:T(8,128)(2,1)S(1)}, bf16[640,256]{1,0:T(8,128)(2,1)S(1)}, u32[]{:S(2)}, u32[]{:S(2)}) collective-permute-start(bf16[640,256]{1,0:T(8,128)(2,1)S(1)} %pick_rows.4), channel_id=1, source_target_pairs={{0,4},{12,8},{1,5},{13,9},{2,6},{14,10},{3,7},{15,11},{16,20},{28,... | collective-permute-start | bytes 983048 | tf_op jit(solution)/shard_map/ppermute | solution.py:326
  18.1 13.0 %copy-start = (bf16[256,2304]{1,0:T(8,128)(2,1)S(1)}, bf16[256,2304]{1,0:T(8,128)(2,1)}, u32[]{:S(2)}) copy-start(bf16[256,2304]{1,0:T(8,128)(2,1)} %refs_3_.3) | copy-start | bytes 3538948
  18.2 7.3 %collective-permute-start.5 = (s32[8,256]{1,0:T(8,128)S(1)}, s32[8,256]{1,0:T(8,128)S(1)}, u32[]{:S(2)}, u32[]{:S(2)}) collective-permute-start(s32[8,256]{1,0:T(8,128)S(1)} %place_rows.1.ids_ref), channel_id=1, source_target_pairs={{0,4},{4,0},{8,12},{12,8},{1,5},{5,1},{9,13},{13,9},{2,6},{6,2},{1... | collective-permute-start | bytes 24584 | tf_op jit(solution)/shard_map/ppermute | solution.py:310
  18.3 14.2 %collective-permute-start.4 = (bf16[640,256]{1,0:T(8,128)(2,1)S(1)}, bf16[640,256]{1,0:T(8,128)(2,1)S(1)}, u32[]{:S(2)}, u32[]{:S(2)}) collective-permute-start(bf16[640,256]{1,0:T(8,128)(2,1)S(1)} %pick_rows.5), channel_id=1, source_target_pairs={{0,9},{1,8},{12,5},{13,4},{2,11},{3,10},{14,7},{15,6},{16,25},{17,... | collective-permute-start | bytes 983048 | tf_op jit(solution)/shard_map/ppermute | solution.py:313
  26.3 16.8 %collective-permute-start.6 = (bf16[640,256]{1,0:T(8,128)(2,1)S(1)}, bf16[640,256]{1,0:T(8,128)(2,1)S(1)}, u32[]{:S(2)}, u32[]{:S(2)}) collective-permute-start(bf16[640,256]{1,0:T(8,128)(2,1)S(1)} %pick_rows.7), channel_id=1, source_target_pairs={{0,4},{4,0},{8,12},{12,8},{1,5},{5,1},{9,13},{13,9},{2,6},{6,2},{1... | collective-permute-start | bytes 983048 | tf_op jit(solution)/shard_map/ppermute | solution.py:326
  29.8 13.3 %collective-permute-start.10 = (bf16[640,256]{1,0:T(8,128)(2,1)S(1)}, bf16[640,256]{1,0:T(8,128)(2,1)S(1)}, u32[]{:S(2)}, u32[]{:S(2)}) collective-permute-start(bf16[640,256]{1,0:T(8,128)(2,1)S(1)} %add.20), channel_id=1, source_target_pairs={{4,12},{8,0},{5,13},{9,1},{6,14},{10,2},{7,15},{11,3},{20,28},{24,... | collective-permute-start | bytes 983048 | tf_op jit(solution)/shard_map/ppermute | solution.py:326
  31.2 12.0 %collective-permute-start.9 = (bf16[16,2304]{1,0:T(8,128)(2,1)S(1)}, bf16[16,2304]{1,0:T(8,128)(2,1)S(1)}, u32[]{:S(2)}, u32[]{:S(2)}) collective-permute-start(bf16[16,2304]{1,0:T(8,128)(2,1)S(1)} %slice.6), channel_id=1, source_target_pairs={{0,1},{4,5},{8,9},{12,13},{2,3},{6,7},{10,11},{14,15},{16,17},{20,... | collective-permute-start | bytes 221192 | tf_op jit(solution)/shard_map/ppermute | solution.py:409
  43.3 10.1 %collective-permute-start.12 = (bf16[640,256]{1,0:T(8,128)(2,1)S(1)}, bf16[640,256]{1,0:T(8,128)(2,1)S(1)}, u32[]{:S(2)}, u32[]{:S(2)}) collective-permute-start(bf16[640,256]{1,0:T(8,128)(2,1)S(1)} %merge.1.refs_1_), channel_id=1, source_target_pairs={{0,2},{2,0},{1,3},{3,1},{4,6},{6,4},{5,7},{7,5},{8,10},{10,8},{9,1... | collective-permute-start | bytes 983048 | tf_op jit(solution)/shard_map/ppermute | solution.py:420
  44.9 2.9 %collective-permute-start.13 = (bf16[640,128]{1,0:T(8,128)(2,1)S(1)}, bf16[640,128]{1,0:T(8,128)(2,1)S(1)}, u32[]{:S(2)}, u32[]{:S(2)}) collective-permute-start(bf16[640,128]{1,0:T(8,128)(2,1)S(1)} %slice.8), channel_id=1, source_target_pairs={{0,1},{2,3},{4,5},{6,7},{8,9},{10,11},{12,13},{14,15},{16,17},{18,... | collective-permute-start | bytes 491528 | tf_op jit(solution)/shard_map/ppermute | solution.py:433
  46.2 7.2 %collective-permute-start.11 = (bf16[640,128]{1,0:T(8,128)(2,1)S(1)}, bf16[640,128]{1,0:T(8,128)(2,1)S(1)}, u32[]{:S(2)}, u32[]{:S(2)}) collective-permute-start(bf16[640,128]{1,0:T(8,128)(2,1)S(1)} %slice.8), channel_id=1, source_target_pairs={{0,3},{2,1},{4,7},{6,5},{8,11},{10,9},{12,15},{14,13},{16,19},{18,... | collective-permute-start | bytes 491528 | tf_op jit(solution)/shard_map/ppermute | solution.py:433
  53.4 8.0 %copy-start.1 = (f32[4,2304]{1,0:T(4,128)S(1)}, f32[4,2304]{1,0:T(4,128)}, u32[]{:S(2)}) copy-start(f32[4,2304]{1,0:T(4,128)} %refs_4_.1) | copy-start | bytes 110596
  57.6 3.8 %collective-permute-start.14 = (f32[8,272]{1,0:T(8,128)S(1)}, f32[8,272]{1,0:T(8,128)S(1)}, u32[]{:S(2)}, u32[]{:S(2)}) collective-permute-start(f32[8,272]{1,0:T(8,128)S(1)} %get-tuple-element.37.refs_0_), channel_id=1, source_target_pairs={{0,2},{2,0},{1,3},{3,1},{4,6},{6,4},{5,7},{7,5},{8,10},{10,8},{9,1... | collective-permute-start | bytes 26120 | tf_op jit(solution)/shard_map/ppermute | solution.py:475

commit v14 on v12

--- a/solution.py
+++ b/solution.py
@@ -330,20 +330,20 @@
         stored,
         [(m, r, m ^ 2, r ^ int(m in (1, 2))) for m in range(4) for r in range(2)],
     )
-    first, second = lax.optimization_barrier((first, second))
+    third = ask(stored, 1)
+    first, second, third = lax.optimization_barrier((first, second, third))
     rows_3 = pick(first)
     inward = send(rows_3, (0, 1), (3, 2))
     across = send(rows_3, (1, 2), (2, 1))
     rows_2 = pick(after(second, rows_3))
-    stored, settled = lax.optimization_barrier((after(stored, rows_2), settled))
+    third, settled = lax.optimization_barrier((after(third, rows_2), settled))
     past = crossing(rows_2, [(m, r, m ^ 2, r ^ 1) for m in (0, 3) for r in range(2)])
-    rows_1 = pick(ask(stored, 1))
-    own = pick(stored)
+    rows_1 = pick(third)
+    own = pick(after(stored, rows_1))
     beside = send(rows_1, (0, 1), (1, 0), (2, 3), (3, 2))
     onward = after(rows_2, rows_1, own) + inward
-    onward = after(onward, across)
-    other = meanwhile(onward)
     onward = send(onward, (1, 3), (2, 0))
+    other = meanwhile(across)
     own, other = lax.optimization_barrier((own + past + beside, other))
     memory = pl.pallas_call(
         merge_kernel,

time: 65.3 us -> 62 us (0.949)
  waiting for transfers between devices: 18.8 us -> 16.3 us
  starting transfers between devices: 24 us -> 23.3 us
    ppermute x4, waiting for transfers between devices: 14.2 us -> 10.2 us  [send(): return lax.ppermute(x, 'mem', pairs)]
    ppermute x2, waiting for transfers between devices: 1.88 us -> 3.92 us  [crossing(): lax.ppermute(x, ('mem', 'rep'), [(2 * a + b, 2 * c + d) for a, b, c, d in...]
    ppermute x2, starting transfers between devices: 7.27 us -> 5.35 us  [ask(): return lax.ppermute(ids, 'mem', [(i, i ^ x) for i in range(4)])]
    ppermute x4, starting transfers between devices: 6.57 us -> 5.19 us  [send(): return lax.ppermute(x, 'mem', pairs)]
    ppermute x1, starting transfers between devices: 1.29 us -> 2.48 us  [meanwhile(): return lax.ppermute(tail, ('mem', 'rep'), needed)]
    ppermute x2, starting transfers between devices: 2.61 us -> 3.28 us  [crossing(): lax.ppermute(x, ('mem', 'rep'), [(2 * a + b, 2 * c + d) for a, b, c, d in...]
  transfers between devices with their start and end apart: 15 -> 15, of which waited for: 6 -> 5; matrix products, arithmetic and copies ran while one was open for 0% -> 0% of each run, Pallas kernels for 20% -> 21%
where the time goes in v14:
time: 62 us; the launch traced here: 61.7 us
  starting transfers between devices  23.3 us (38%)
  Pallas kernels  21.4 us (35%)
  waiting for transfers between devices  16.3 us (26%)
    ppermute x4, waiting for transfers between devices, send(): return lax.ppermute(x, 'mem', pairs)  10.2 us
    pallas_call x1, Pallas kernels, shards(): pl.pallas_call(functools.partial(project_kernel, (0,), tps), in_specs=[sm...  5.6 us
    ppermute x2, starting transfers between devices, ask(): return lax.ppermute(ids, 'mem', [(i, i ^ x) for i in range(4)])  5.35 us
    ppermute x4, starting transfers between devices, send(): return lax.ppermute(x, 'mem', pairs)  5.19 us
    pallas_call x1, Pallas kernels, shards(): pl.pallas_call(functools.partial(project_kernel, tuple(range(1, tps)), tp...  4.24 us
    pallas_call x1, Pallas kernels, shards(): pl.pallas_call(functools.partial(finish_kernel, tps, step), in_specs=[sme...  3.96 us
    ppermute x2, waiting for transfers between devices, crossing(): lax.ppermute(x, ('mem', 'rep'), [(2 * a + b, 2 * c + d) for a, b, c, d in...  3.92 us
    pallas_call x4, Pallas kernels, pick(): pl.pallas_call(pick_kernel, in_specs=[pl.BlockSpec(memory_space=pltpu.SME...  3.46 us
  transfers between devices with their start and end apart: 15, of which 5 were waited for; matrix products, arithmetic and copies ran while one was open for 0% of the time, Pallas kernels for 21%

profile of v14, /device:TPU:0, one launch (start us, length us, event | category | flops | bytes accessed | tf_op | source)
XLA Modules:
  0.0 61.7 jit_solution(13309902917091518727)
XLA Ops:
  0.0 0.5 collective-permute-start.3
  0.5 0.1 collective-permute-start.4
  0.5 1.3 %place_rows.1.ids_ref = s32[8,256]{1,0:T(8,128)S(1)} custom-call(s32[8,256]{1,0:T(8,128)} %bitcast.11, s32[32,128]{1,0:T(8,128)} %bitcast.10), custom_call_target="tpu_custom_call" | custom-call | tf_op jit(solution)/shard_map/place_rows/pallas_call | solution.py:377
  1.9 5.1 %collective-permute-start = (s32[8,256]{1,0:T(8,128)S(1)}, s32[8,256]{1,0:T(8,128)S(1)}, u32[]{:S(2)}, u32[]{:S(2)}) collective-permute-start(s32[8,256]{1,0:T(8,128)S(1)} %place_rows.1.ids_ref), channel_id=1, source_target_pairs={{0,12},{4,8},{8,4},{12,0},{1,13},{5,9},{9,5},{13,1},{2,14},{6,10},... | collective-permute-start | bytes 24584 | tf_op jit(solution)/shard_map/ppermute | solution.py:310
  7.0 0.0 collective-permute-start.1
  7.0 0.2 collective-permute-start.2
  7.2 2.7 %decode_tables.1.table_ref = bf16[8,80,1024]{2,1,0:T(8,128)(2,1)S(1)} custom-call(bf16[8,80,1024]{2,1,0:T(8,128)(2,1)} %bitcast.8, bf16[5,8,1024]{2,1,0:T(8,128)(2,1)} %bitcast.9), custom_call_target="tpu_custom_call" | custom-call | tf_op jit(solution)/shard_map/decode_tables/pallas_call | solution.py:391
  10.0 0.0 collective-permute-done.ids_ref
  10.0 1.0 %collective-permute-done.1.ids_ref = s32[8,256]{1,0:T(8,128)S(1)} collective-permute-done((s32[8,256]{1,0:T(8,128)S(1)}, s32[8,256]{1,0:T(8,128)S(1)}, u32[]{:S(2)}, u32[]{:S(2)}) %collective-permute-start.1) | collective-permute-done | bytes 8224 | tf_op jit(solution)/shard_map/ppermute | solution.py:313
  10.9 0.0 collective-permute-done.2.ids_ref
  11.0 0.9 %pick_rows.4 = bf16[640,256]{1,0:T(8,128)(2,1)S(1)} custom-call(s32[1]{0:T(128)} %bitcast.3.base_ref, s32[8,256]{1,0:T(8,128)S(1)} %collective-permute-done.ids_ref, bf16[8,80,1024]{2,1,0:T(8,128)(2,1)S(1)} %decode_tables.1.table_ref), custom_call_target="tpu_custom_call" | custom-call | tf_op jit(solution)/shard_map/pick_rows/pallas_call | solution.py:316
  11.8 2.8 %collective-permute-start.9 = (bf16[640,256]{1,0:T(8,128)(2,1)S(1)}, bf16[640,256]{1,0:T(8,128)(2,1)S(1)}, u32[]{:S(2)}, u32[]{:S(2)}) collective-permute-start(bf16[640,256]{1,0:T(8,128)(2,1)S(1)} %pick_rows.4), channel_id=1, source_target_pairs={{0,4},{12,8},{1,5},{13,9},{2,6},{14,10},{3,7},{15,11},{16,20},{28,... | collective-permute-start | bytes 983048 | tf_op jit(solution)/shard_map/ppermute | solution.py:326
  14.6 0.7 %collective-permute-start.7 = (bf16[640,256]{1,0:T(8,128)(2,1)S(1)}, bf16[640,256]{1,0:T(8,128)(2,1)S(1)}, u32[]{:S(2)}, u32[]{:S(2)}) collective-permute-start(bf16[640,256]{1,0:T(8,128)(2,1)S(1)} %pick_rows.4), channel_id=1, source_target_pairs={{4,8},{8,4},{5,9},{9,5},{6,10},{10,6},{7,11},{11,7},{20,24},{24,20... | collective-permute-start | bytes 983048 | tf_op jit(solution)/shard_map/ppermute | solution.py:326
  15.3 0.9 %pick_rows.5 = bf16[640,256]{1,0:T(8,128)(2,1)S(1)} custom-call(s32[1]{0:T(128)} %bitcast.3.base_ref, s32[8,256]{1,0:T(8,128)S(1)} %collective-permute-done.1.ids_ref, bf16[8,80,1024]{2,1,0:T(8,128)(2,1)S(1)} %decode_tables.1.table_ref), custom_call_target="tpu_custom_call" | custom-call | tf_op jit(solution)/shard_map/pick_rows/pallas_call | solution.py:316
  16.1 0.0 copy-start
  16.1 3.3 %collective-permute-start.5 = (bf16[640,256]{1,0:T(8,128)(2,1)S(1)}, bf16[640,256]{1,0:T(8,128)(2,1)S(1)}, u32[]{:S(2)}, u32[]{:S(2)}) collective-permute-start(bf16[640,256]{1,0:T(8,128)(2,1)S(1)} %pick_rows.5), channel_id=1, source_target_pairs={{0,9},{1,8},{12,5},{13,4},{2,11},{3,10},{14,7},{15,6},{16,25},{17,... | collective-permute-start | bytes 983048 | tf_op jit(solution)/shard_map/ppermute | solution.py:313
  19.4 0.0 collective-permute-done.3.refs_4_
  19.4 0.0 collective-permute-done.4.refs_5_
  19.5 0.9 %pick_rows.6 = bf16[640,256]{1,0:T(8,128)(2,1)S(1)} custom-call(s32[1]{0:T(128)} %bitcast.3.base_ref, s32[8,256]{1,0:T(8,128)S(1)} %collective-permute-done.2.ids_ref, bf16[8,80,1024]{2,1,0:T(8,128)(2,1)S(1)} %decode_tables.1.table_ref), custom_call_target="tpu_custom_call" | custom-call | tf_op jit(solution)/shard_map/pick_rows/pallas_call | solution.py:316
  20.3 0.5 collective-permute-start.6
  20.8 0.9 %pick_rows.7 = bf16[640,256]{1,0:T(8,128)(2,1)S(1)} custom-call(s32[1]{0:T(128)} %bitcast.3.base_ref, s32[8,256]{1,0:T(8,128)S(1)} %place_rows.1.ids_ref, bf16[8,80,1024]{2,1,0:T(8,128)(2,1)S(1)} %decode_tables.1.table_ref), custom_call_target="tpu_custom_call" | custom-call | tf_op jit(solution)/shard_map/pick_rows/pallas_call | solution.py:316
  21.6 0.0 collective-permute-done.9
  21.7 0.1 add.20
  21.7 1.3 %collective-permute-start.10 = (bf16[640,256]{1,0:T(8,128)(2,1)S(1)}, bf16[640,256]{1,0:T(8,128)(2,1)S(1)}, u32[]{:S(2)}, u32[]{:S(2)}) collective-permute-start(bf16[640,256]{1,0:T(8,128)(2,1)S(1)} %add.20), channel_id=1, source_target_pairs={{4,12},{8,0},{5,13},{9,1},{6,14},{10,2},{7,15},{11,3},{20,28},{24,... | collective-permute-start | bytes 983048 | tf_op jit(solution)/shard_map/ppermute | solution.py:326
  23.0 0.0 copy-done
  23.1 0.0 collective-permute-done.7.refs_1_
  23.1 2.5 %collective-permute-start.8 = (bf16[16,2304]{1,0:T(8,128)(2,1)S(1)}, bf16[16,2304]{1,0:T(8,128)(2,1)S(1)}, u32[]{:S(2)}, u32[]{:S(2)}) collective-permute-start(bf16[16,2304]{1,0:T(8,128)(2,1)S(1)} %slice.6), channel_id=1, source_target_pairs={{0,1},{4,5},{8,9},{12,13},{2,3},{6,7},{10,11},{14,15},{16,17},{20,... | collective-permute-start | bytes 221192 | tf_op jit(solution)/shard_map/ppermute | solution.py:410
  25.6 2.9 %collective-permute-done.5 = bf16[640,256]{1,0:T(8,128)(2,1)S(1)} collective-permute-done((bf16[640,256]{1,0:T(8,128)(2,1)S(1)}, bf16[640,256]{1,0:T(8,128)(2,1)S(1)}, u32[]{:S(2)}, u32[]{:S(2)}) %collective-permute-start.5) | collective-permute-done | bytes 327712 | tf_op jit(solution)/shard_map/ppermute | solution.py:313
  28.5 6.7 %collective-permute-done.6 = bf16[640,256]{1,0:T(8,128)(2,1)S(1)} collective-permute-done((bf16[640,256]{1,0:T(8,128)(2,1)S(1)}, bf16[640,256]{1,0:T(8,128)(2,1)S(1)}, u32[]{:S(2)}, u32[]{:S(2)}) %collective-permute-start.6) | collective-permute-done | bytes 327712 | tf_op jit(solution)/shard_map/ppermute | solution.py:326
  35.3 0.0 collective-permute-done.8.refs_5_
  35.3 3.5 %collective-permute-done.10.refs_2_ = bf16[640,256]{1,0:T(8,128)(2,1)S(1)} collective-permute-done((bf16[640,256]{1,0:T(8,128)(2,1)S(1)}, bf16[640,256]{1,0:T(8,128)(2,1)S(1)}, u32[]{:S(2)}, u32[]{:S(2)}) %collective-permute-start.10) | collective-permute-done | bytes 327712 | tf_op jit(solution)/shard_map/ppermute | solution.py:326
  38.7 0.1 merge.1.refs_1_
  38.9 1.6 %collective-permute-start.12 = (bf16[640,256]{1,0:T(8,128)(2,1)S(1)}, bf16[640,256]{1,0:T(8,128)(2,1)S(1)}, u32[]{:S(2)}, u32[]{:S(2)}) collective-permute-start(bf16[640,256]{1,0:T(8,128)(2,1)S(1)} %merge.1.refs_1_), channel_id=1, source_target_pairs={{0,2},{2,0},{1,3},{3,1},{4,6},{6,4},{5,7},{7,5},{8,10},{10,8},{9,1... | collective-permute-start | bytes 983048 | tf_op jit(solution)/shard_map/ppermute | solution.py:421
  40.4 1.7 %collective-permute-start.13 = (bf16[640,128]{1,0:T(8,128)(2,1)S(1)}, bf16[640,128]{1,0:T(8,128)(2,1)S(1)}, u32[]{:S(2)}, u32[]{:S(2)}) collective-permute-start(bf16[640,128]{1,0:T(8,128)(2,1)S(1)} %slice.8), channel_id=1, source_target_pairs={{0,1},{2,3},{4,5},{6,7},{8,9},{10,11},{12,13},{14,15},{16,17},{18,... | collective-permute-start | bytes 491528 | tf_op jit(solution)/shard_map/ppermute | solution.py:434
  42.2 1.6 %collective-permute-start.11 = (bf16[640,128]{1,0:T(8,128)(2,1)S(1)}, bf16[640,128]{1,0:T(8,128)(2,1)S(1)}, u32[]{:S(2)}, u32[]{:S(2)}) collective-permute-start(bf16[640,128]{1,0:T(8,128)(2,1)S(1)} %slice.8), channel_id=1, source_target_pairs={{0,3},{2,1},{4,7},{6,5},{8,11},{10,9},{12,15},{14,13},{16,19},{18,... | collective-permute-start | bytes 491528 | tf_op jit(solution)/shard_map/ppermute | solution.py:434
  43.8 0.1 pad_add_fusion.where_ref
  43.9 0.0 collective-permute-done.13.refs_0_
  43.9 5.6 %project_own.1 = (f32[2,272,1152]{2,1,0:T(8,128)S(1)}, f32[2,272,1152]{2,1,0:T(8,128)S(1)}, bf16[2,2,640,1152]{3,2,1,0:T(8,128)(2,1)S(1)}) custom-call(s32[2]{0:T(128)S(1)} %pad_add_fusion.where_ref, bf16[640,128]{1,0:T(8,128)(2,1)S(1)} %collective-permute-done.13.refs_0_, bf16[640,256]{1,0:T(8,128)(2,1)S(1)} %merge.1.refs_1_, bf16[1280,1152]{1,0:T(8,128)(2,1)} %refs_2_.1, ...), custom_call_target="tpu_custom_call" | custom-call | tf_op jit(solution)/shard_map/project_own/pallas_call | solution.py:440
  49.5 0.0 collective-permute-done.11.refs_0_
  49.5 0.0 collective-permute-done.12.refs_1_
  49.5 0.0 copy-start.1
  49.5 4.2 %project_others.1 = (f32[2,272,1152]{2,1,0:T(8,128)}, f32[8,272]{1,0:T(8,128)S(1)}) custom-call(s32[2]{0:T(128)S(1)} %pad_add_fusion.where_ref, bf16[640,128]{1,0:T(8,128)(2,1)S(1)} %collective-permute-done.11.refs_0_, bf16[640,256]{1,0:T(8,128)(2,1)S(1)} %collective-permute-done.12.refs_1_, bf16[2,2,640,1152]{3,2,1,0:T(8,128)(2,1)S(1)} %get-tuple-element.37.refs_2_, ...), custom_call_target="tpu_custom_call" | custom-call | tf_op jit(solution)/shard_map/project_others/pallas_call | solution.py:453
  53.8 1.6 %collective-permute-start.14 = (f32[8,272]{1,0:T(8,128)S(1)}, f32[8,272]{1,0:T(8,128)S(1)}, u32[]{:S(2)}, u32[]{:S(2)}) collective-permute-start(f32[8,272]{1,0:T(8,128)S(1)} %get-tuple-element.41.refs_0_), channel_id=1, source_target_pairs={{0,2},{2,0},{1,3},{3,1},{4,6},{6,4},{5,7},{7,5},{8,10},{10,8},{9,1... | collective-permute-start | bytes 26120 | tf_op jit(solution)/shard_map/ppermute | solution.py:476
  55.3 2.2 %collective-permute-done.14.refs_1_ = f32[8,272]{1,0:T(8,128)S(1)} collective-permute-done((f32[8,272]{1,0:T(8,128)S(1)}, f32[8,272]{1,0:T(8,128)S(1)}, u32[]{:S(2)}, u32[]{:S(2)}) %collective-permute-start.14) | collective-permute-done | bytes 8736 | tf_op jit(solution)/shard_map/ppermute | solution.py:476
  57.6 0.0 copy-done.1
  57.6 4.0 %finish.1 = bf16[256,2304]{1,0:T(8,128)(2,1)} custom-call(s32[1]{0:T(128)} %bitcast.keep_ref, f32[8,272]{1,0:T(8,128)S(1)} %get-tuple-element.41.refs_0_, f32[8,272]{1,0:T(8,128)S(1)} %collective-permute-done.14.refs_1_, f32[2,272,1152]{2,1,0:T(8,128)} %get-tuple-element.42.refs_2_, bf16[256,2304]{1,0:T(8,128)(2,1)S(1)} %copy-done, f32[4,2304]{1,0:T(4,128)S(1)} %copy-done.1), custom_call_target="tpu_custom_call" | custom-call | tf_op jit(solution)/shard_map/finish/pallas_call | solution.py:482
  (3 shorter events, 0.1 us)
Async XLA Ops:
  0.0 19.4 %collective-permute-start.3 = (bf16[1280,1152]{1,0:T(8,128)(2,1)}, bf16[1280,1152]{1,0:T(8,128)(2,1)}, u32[]{:S(2)}, u32[]{:S(2)}) collective-permute-start(bf16[1280,1152]{1,0:T(8,128)(2,1)} %refs_2_.1), channel_id=1, source_target_pairs={{0,1},{1,0},{2,3},{3,2},{4,5},{5,4},{6,7},{7,6},{8,9},{9,8},{10,11... | collective-permute-start | bytes 8847368 | tf_op jit(solution)/shard_map/ppermute | solution.py:404
  0.5 19.0 %collective-permute-start.4 = (bf16[1280,1152]{1,0:T(8,128)(2,1)}, bf16[1280,1152]{1,0:T(8,128)(2,1)}, u32[]{:S(2)}, u32[]{:S(2)}) collective-permute-start(bf16[1280,1152]{1,0:T(8,128)(2,1)} %refs_3_.2), channel_id=1, source_target_pairs={{0,1},{1,0},{2,3},{3,2},{4,5},{5,4},{6,7},{7,6},{8,9},{9,8},{10,11... | collective-permute-start | bytes 8847368 | tf_op jit(solution)/shard_map/ppermute | solution.py:405
  1.9 8.1 %collective-permute-start = (s32[8,256]{1,0:T(8,128)S(1)}, s32[8,256]{1,0:T(8,128)S(1)}, u32[]{:S(2)}, u32[]{:S(2)}) collective-permute-start(s32[8,256]{1,0:T(8,128)S(1)} %place_rows.1.ids_ref), channel_id=1, source_target_pairs={{0,12},{4,8},{8,4},{12,0},{1,13},{5,9},{9,5},{13,1},{2,14},{6,10},... | collective-permute-start | bytes 24584 | tf_op jit(solution)/shard_map/ppermute | solution.py:310
  7.0 4.0 %collective-permute-start.1 = (s32[8,256]{1,0:T(8,128)S(1)}, s32[8,256]{1,0:T(8,128)S(1)}, u32[]{:S(2)}, u32[]{:S(2)}) collective-permute-start(s32[8,256]{1,0:T(8,128)S(1)} %place_rows.1.ids_ref), channel_id=1, source_target_pairs={{0,8},{1,9},{4,13},{5,12},{8,1},{9,0},{12,4},{13,5},{2,10},{3,11},... | collective-permute-start | bytes 24584 | tf_op jit(solution)/shard_map/ppermute | solution.py:313
  7.0 4.0 %collective-permute-start.2 = (s32[8,256]{1,0:T(8,128)S(1)}, s32[8,256]{1,0:T(8,128)S(1)}, u32[]{:S(2)}, u32[]{:S(2)}) collective-permute-start(s32[8,256]{1,0:T(8,128)S(1)} %place_rows.1.ids_ref), channel_id=1, source_target_pairs={{0,4},{4,0},{8,12},{12,8},{1,5},{5,1},{9,13},{13,9},{2,6},{6,2},{1... | collective-permute-start | bytes 24584 | tf_op jit(solution)/shard_map/ppermute | solution.py:310
  11.8 9.8 %collective-permute-start.9 = (bf16[640,256]{1,0:T(8,128)(2,1)S(1)}, bf16[640,256]{1,0:T(8,128)(2,1)S(1)}, u32[]{:S(2)}, u32[]{:S(2)}) collective-permute-start(bf16[640,256]{1,0:T(8,128)(2,1)S(1)} %pick_rows.4), channel_id=1, source_target_pairs={{0,4},{12,8},{1,5},{13,9},{2,6},{14,10},{3,7},{15,11},{16,20},{28,... | collective-permute-start | bytes 983048 | tf_op jit(solution)/shard_map/ppermute | solution.py:326
  14.6 8.5 %collective-permute-start.7 = (bf16[640,256]{1,0:T(8,128)(2,1)S(1)}, bf16[640,256]{1,0:T(8,128)(2,1)S(1)}, u32[]{:S(2)}, u32[]{:S(2)}) collective-permute-start(bf16[640,256]{1,0:T(8,128)(2,1)S(1)} %pick_rows.4), channel_id=1, source_target_pairs={{4,8},{8,4},{5,9},{9,5},{6,10},{10,6},{7,11},{11,7},{20,24},{24,20... | collective-permute-start | bytes 983048 | tf_op jit(solution)/shard_map/ppermute | solution.py:326
  16.1 6.9 %copy-start = (bf16[256,2304]{1,0:T(8,128)(2,1)S(1)}, bf16[256,2304]{1,0:T(8,128)(2,1)}, u32[]{:S(2)}) copy-start(bf16[256,2304]{1,0:T(8,128)(2,1)} %refs_3_.3) | copy-start | bytes 3538948
  16.1 12.4 %collective-permute-start.5 = (bf16[640,256]{1,0:T(8,128)(2,1)S(1)}, bf16[640,256]{1,0:T(8,128)(2,1)S(1)}, u32[]{:S(2)}, u32[]{:S(2)}) collective-permute-start(bf16[640,256]{1,0:T(8,128)(2,1)S(1)} %pick_rows.5), channel_id=1, source_target_pairs={{0,9},{1,8},{12,5},{13,4},{2,11},{3,10},{14,7},{15,6},{16,25},{17,... | collective-permute-start | bytes 983048 | tf_op jit(solution)/shard_map/ppermute | solution.py:313
  20.3 14.9 %collective-permute-start.6 = (bf16[640,256]{1,0:T(8,128)(2,1)S(1)}, bf16[640,256]{1,0:T(8,128)(2,1)S(1)}, u32[]{:S(2)}, u32[]{:S(2)}) collective-permute-start(bf16[640,256]{1,0:T(8,128)(2,1)S(1)} %pick_rows.6), channel_id=1, source_target_pairs={{0,4},{4,0},{8,12},{12,8},{1,5},{5,1},{9,13},{13,9},{2,6},{6,2},{1... | collective-permute-start | bytes 983048 | tf_op jit(solution)/shard_map/ppermute | solution.py:326
  21.7 17.0 %collective-permute-start.10 = (bf16[640,256]{1,0:T(8,128)(2,1)S(1)}, bf16[640,256]{1,0:T(8,128)(2,1)S(1)}, u32[]{:S(2)}, u32[]{:S(2)}) collective-permute-start(bf16[640,256]{1,0:T(8,128)(2,1)S(1)} %add.20), channel_id=1, source_target_pairs={{4,12},{8,0},{5,13},{9,1},{6,14},{10,2},{7,15},{11,3},{20,28},{24,... | collective-permute-start | bytes 983048 | tf_op jit(solution)/shard_map/ppermute | solution.py:326
  23.1 12.2 %collective-permute-start.8 = (bf16[16,2304]{1,0:T(8,128)(2,1)S(1)}, bf16[16,2304]{1,0:T(8,128)(2,1)S(1)}, u32[]{:S(2)}, u32[]{:S(2)}) collective-permute-start(bf16[16,2304]{1,0:T(8,128)(2,1)S(1)} %slice.6), channel_id=1, source_target_pairs={{0,1},{4,5},{8,9},{12,13},{2,3},{6,7},{10,11},{14,15},{16,17},{20,... | collective-permute-start | bytes 221192 | tf_op jit(solution)/shard_map/ppermute | solution.py:410
  38.9 10.7 %collective-permute-start.12 = (bf16[640,256]{1,0:T(8,128)(2,1)S(1)}, bf16[640,256]{1,0:T(8,128)(2,1)S(1)}, u32[]{:S(2)}, u32[]{:S(2)}) collective-permute-start(bf16[640,256]{1,0:T(8,128)(2,1)S(1)} %merge.1.refs_1_), channel_id=1, source_target_pairs={{0,2},{2,0},{1,3},{3,1},{4,6},{6,4},{5,7},{7,5},{8,10},{10,8},{9,1... | collective-permute-start | bytes 983048 | tf_op jit(solution)/shard_map/ppermute | solution.py:421
  40.4 3.5 %collective-permute-start.13 = (bf16[640,128]{1,0:T(8,128)(2,1)S(1)}, bf16[640,128]{1,0:T(8,128)(2,1)S(1)}, u32[]{:S(2)}, u32[]{:S(2)}) collective-permute-start(bf16[640,128]{1,0:T(8,128)(2,1)S(1)} %slice.8), channel_id=1, source_target_pairs={{0,1},{2,3},{4,5},{6,7},{8,9},{10,11},{12,13},{14,15},{16,17},{18,... | collective-permute-start | bytes 491528 | tf_op jit(solution)/shard_map/ppermute | solution.py:434
  42.2 7.3 %collective-permute-start.11 = (bf16[640,128]{1,0:T(8,128)(2,1)S(1)}, bf16[640,128]{1,0:T(8,128)(2,1)S(1)}, u32[]{:S(2)}, u32[]{:S(2)}) collective-permute-start(bf16[640,128]{1,0:T(8,128)(2,1)S(1)} %slice.8), channel_id=1, source_target_pairs={{0,3},{2,1},{4,7},{6,5},{8,11},{10,9},{12,15},{14,13},{16,19},{18,... | collective-permute-start | bytes 491528 | tf_op jit(solution)/shard_map/ppermute | solution.py:434
  49.5 8.0 %copy-start.1 = (f32[4,2304]{1,0:T(4,128)S(1)}, f32[4,2304]{1,0:T(4,128)}, u32[]{:S(2)}) copy-start(f32[4,2304]{1,0:T(4,128)} %refs_4_.1) | copy-start | bytes 110596
  53.8 3.8 %collective-permute-start.14 = (f32[8,272]{1,0:T(8,128)S(1)}, f32[8,272]{1,0:T(8,128)S(1)}, u32[]{:S(2)}, u32[]{:S(2)}) collective-permute-start(f32[8,272]{1,0:T(8,128)S(1)} %get-tuple-element.41.refs_0_), channel_id=1, source_target_pairs={{0,2},{2,0},{1,3},{3,1},{4,6},{6,4},{5,7},{7,5},{8,10},{10,8},{9,1... | collective-permute-start | bytes 26120 | tf_op jit(solution)/shard_map/ppermute | solution.py:476

commit v15 on v14

--- a/solution.py
+++ b/solution.py
@@ -203,22 +203,38 @@
         copy.wait()
 
 
-def finish_kernel(count, step, keep_ref, *refs):
-    stats = refs[:count]
-    value_hbm, hidden_ref, taps_ref, out_hbm = refs[count : count + 4]
-    gates, factors, value_ref, normed, out_ref, in_sems, sems = refs[count + 4 :]
-    rows, half = normed.shape
-    tokens, width = out_ref.shape
-    arrivals = {}
-    chunk = min(step, half)
+def prepare_kernel(chunk, taps_ref, value_hbm, value_ref, tap_ref, rows_ref, sems):
+    half = rows_ref.shape[-1]
+    tokens = value_ref.shape[1]
+    copies = []
     for slot in range(2):
         for start in range(0, half, chunk):
             span = pl.ds(start, chunk)
             copy = pltpu.make_async_copy(
-                value_hbm.at[slot, :, span], value_ref.at[slot, :, span], in_sems.at[len(arrivals)]
+                value_hbm.at[slot, :, span], rows_ref.at[slot, :, span], sems.at[len(copies)]
             )
             copy.start()
-            arrivals[slot, start] = copy
+            copies.append(copy)
+    for slot in range(2):
+        for start in range(0, half, LANES):
+            size = min(LANES, half - start)
+            span = slice(start, start + size)
+            there = slice(slot * half + start, slot * half + start + size)
+            if start % chunk == 0:
+                copies[(slot * half + start) // chunk].wait()
+            value_ref[slot, :, span] = rows_ref[slot, RIM:, span]
+            for tap in range(1, KERNEL):
+                lag = DILATION * tap
+                rows = rows_ref[slot, RIM - lag : RIM - lag + tokens, span]
+                tap_ref[tap - 1, slot, :, span] = taps_ref[tap : tap + 1, there] * rows
+
+
+def finish_kernel(count, step, keep_ref, *refs):
+    stats = refs[:count]
+    value_ref, tap_ref, hidden_ref, taps_ref, out_hbm = refs[count : count + 5]
+    columns, gates, factors, out_ref, sems = refs[count + 5 :]
+    half = value_ref.shape[-1]
+    tokens, width = out_ref.shape
     total = stats[0][...]
     for other in stats[1:]:
         total = total + other[...]
@@ -229,25 +245,24 @@
     factor = jnp.where((iota(factor.shape, 1) < RIM) & (keep_ref[0] == 0), 0.0, factor)
     line = iota(total.shape, 0)
     both = jnp.where(line == 0, gate, jnp.where(line == 1, factor, 0.0))
-    columns = dot_nt(unit(rows, F32), both, lax.Precision.HIGHEST)
+    columns[...] = dot_nt(unit(total.shape[1], F32), both, lax.Precision.HIGHEST)
     gates[...] = jnp.broadcast_to(columns[RIM:, 0:1], gates.shape)
-    factors[...] = jnp.broadcast_to(columns[:, 1:2], factors.shape)
+    for tap in range(KERNEL):
+        lag = DILATION * tap
+        factors[tap] = jnp.broadcast_to(
+            columns[RIM - lag : RIM - lag + tokens, 1:2], factors.shape[1:]
+        )
     copies = []
     for slot in range(2):
         for start in range(0, half, LANES):
             size = min(LANES, half - start)
             span = slice(start, start + size)
             there = slice(slot * half + start, slot * half + start + size)
-            if start % chunk == 0:
-                arrivals[slot, start].wait()
             values = value_ref[slot, :, span]
-            normed[:, span] = values * factors[:, :size]
-            conv = None
-            for tap in range(KERNEL):
-                lag = DILATION * tap
-                term = taps_ref[tap : tap + 1, there] * normed[RIM - lag : RIM - lag + tokens, span]
-                conv = term if conv is None else conv + term
-            gated = values[RIM:] * gates[:, :size]
+            conv = taps_ref[0:1, there] * values * factors[0, :, :size]
+            for tap in range(1, KERNEL):
+                conv = conv + tap_ref[tap - 1, slot, :, span] * factors[tap, :, :size]
+            gated = values * gates[:, :size]
             out_ref[:, there] = (
                 hidden_ref[:, there].astype(F32) + jax.nn.silu(conv) + gated
             ).astype(BF16)
@@ -479,23 +494,38 @@
     step = 2 * half
     if half % LANES == 0:
         step = next(c for c in (384, 256, 128) if half % c == 0)
+    chunk = min(step, half)
+    body = (2, tokens, half)
+    values, products = pl.pallas_call(
+        functools.partial(prepare_kernel, chunk),
+        in_specs=[resident, anywhere],
+        out_specs=(resident,) * 2,
+        out_shape=(
+            jax.ShapeDtypeStruct(body, F32),
+            jax.ShapeDtypeStruct((KERNEL - 1, *body), F32),
+        ),
+        scratch_shapes=[
+            pltpu.VMEM((2, extended, half), F32),
+            pltpu.SemaphoreType.DMA((2 * half // chunk,)),
+        ],
+        compiler_params=limit(6),
+        name="prepare",
+    )(conv_weight, in_hbm(values))
     return pl.pallas_call(
         functools.partial(finish_kernel, tps, step),
-        in_specs=[smem] + [resident] * tps + [anywhere] + [resident] * 2,
+        in_specs=[smem] + [resident] * (tps + 4),
         out_specs=anywhere,
         out_shape=jax.ShapeDtypeStruct((tokens, 2 * half), BF16),
         scratch_shapes=[
+            pltpu.VMEM((extended, 8), F32),
             pltpu.VMEM((tokens, LANES), F32),
-            pltpu.VMEM((extended, LANES), F32),
-            pltpu.VMEM((2, extended, half), F32),
-            pltpu.VMEM((extended, half), F32),
+            pltpu.VMEM((KERNEL, tokens, LANES), F32),
             pltpu.VMEM((tokens, 2 * half), BF16),
-            pltpu.SemaphoreType.DMA((2 * half // min(step, half),)),
             pltpu.SemaphoreType.DMA((2 * half // step,)),
         ],
-        compiler_params=limit(12),
+        compiler_params=limit(6),
         name="finish",
-    )(keep, *all_stats, in_hbm(values), hidden, conv_weight)
+    )(keep, *all_stats, values, products, hidden, conv_weight)
 
 
 def solution(mesh):

time: 62 us -> 60.9 us (0.982)
  waiting for transfers between devices: 16.3 us -> 14.4 us
  Pallas kernels: 21.4 us -> 22.3 us
    ppermute x1, waiting for transfers between devices: 2.21 us -> 0.27 us  [shards(): lax.ppermute(stats, 'tp', [(i, (i + s) % tps) for i in range(tps)])]
    pallas_call x0 -> x1, Pallas kernels: none -> 1.93 us  [shards(): pl.pallas_call(functools.partial(prepare_kernel, chunk), in_specs=[reside...]
    pallas_call x1, Pallas kernels: 3.96 us -> 2.84 us  [shards(): pl.pallas_call(functools.partial(finish_kernel, tps, step), in_specs=[sme...]
  transfers between devices with their start and end apart: 15 -> 15, of which waited for: 5 -> 5; matrix products, arithmetic and copies ran while one was open for 0% -> 0% of each run, Pallas kernels for 21% -> 25%
where the time goes in v15:
time: 60.9 us; the launch traced here: 60.6 us
  starting transfers between devices  23.3 us (38%)
  Pallas kernels  22.3 us (37%)
  waiting for transfers between devices  14.4 us (24%)
    ppermute x4, waiting for transfers between devices, send(): return lax.ppermute(x, 'mem', pairs)  10.2 us
    pallas_call x1, Pallas kernels, shards(): pl.pallas_call(functools.partial(project_kernel, (0,), tps), in_specs=[sm...  5.6 us
    ppermute x2, starting transfers between devices, ask(): return lax.ppermute(ids, 'mem', [(i, i ^ x) for i in range(4)])  5.35 us
    ppermute x4, starting transfers between devices, send(): return lax.ppermute(x, 'mem', pairs)  5.19 us
    pallas_call x1, Pallas kernels, shards(): pl.pallas_call(functools.partial(project_kernel, tuple(range(1, tps)), tp...  4.25 us
    ppermute x2, waiting for transfers between devices, crossing(): lax.ppermute(x, ('mem', 'rep'), [(2 * a + b, 2 * c + d) for a, b, c, d in...  3.92 us
    pallas_call x4, Pallas kernels, pick(): pl.pallas_call(pick_kernel, in_specs=[pl.BlockSpec(memory_space=pltpu.SME...  3.46 us
    ppermute x2, starting transfers between devices, next_rim(): return lax.ppermute(rim, ('mem', 'tp', 'rep'), pairs)  3.36 us
  transfers between devices with their start and end apart: 15, of which 5 were waited for; matrix products, arithmetic and copies ran while one was open for 0% of the time, Pallas kernels for 25%

profile of v15, /device:TPU:0, one launch (start us, length us, event | category | flops | bytes accessed | tf_op | source)
XLA Modules:
  0.0 60.6 jit_solution(13456104494009705996)
XLA Ops:
  0.0 0.5 collective-permute-start.3
  0.5 0.1 collective-permute-start.4
  0.5 1.3 %place_rows.1.ids_ref = s32[8,256]{1,0:T(8,128)S(1)} custom-call(s32[8,256]{1,0:T(8,128)} %bitcast.11, s32[32,128]{1,0:T(8,128)} %bitcast.10), custom_call_target="tpu_custom_call" | custom-call | tf_op jit(solution)/shard_map/place_rows/pallas_call | solution.py:392
  1.9 5.1 %collective-permute-start = (s32[8,256]{1,0:T(8,128)S(1)}, s32[8,256]{1,0:T(8,128)S(1)}, u32[]{:S(2)}, u32[]{:S(2)}) collective-permute-start(s32[8,256]{1,0:T(8,128)S(1)} %place_rows.1.ids_ref), channel_id=1, source_target_pairs={{0,12},{4,8},{8,4},{12,0},{1,13},{5,9},{9,5},{13,1},{2,14},{6,10},... | collective-permute-start | bytes 24584 | tf_op jit(solution)/shard_map/ppermute | solution.py:325
  7.0 0.0 collective-permute-start.1
  7.0 0.2 collective-permute-start.2
  7.2 2.7 %decode_tables.1.table_ref = bf16[8,80,1024]{2,1,0:T(8,128)(2,1)S(1)} custom-call(bf16[8,80,1024]{2,1,0:T(8,128)(2,1)} %bitcast.8, bf16[5,8,1024]{2,1,0:T(8,128)(2,1)} %bitcast.9), custom_call_target="tpu_custom_call" | custom-call | tf_op jit(solution)/shard_map/decode_tables/pallas_call | solution.py:406
  10.0 0.0 collective-permute-done.ids_ref
  10.0 1.0 %collective-permute-done.1.ids_ref = s32[8,256]{1,0:T(8,128)S(1)} collective-permute-done((s32[8,256]{1,0:T(8,128)S(1)}, s32[8,256]{1,0:T(8,128)S(1)}, u32[]{:S(2)}, u32[]{:S(2)}) %collective-permute-start.1) | collective-permute-done | bytes 8224 | tf_op jit(solution)/shard_map/ppermute | solution.py:328
  10.9 0.0 collective-permute-done.2.ids_ref
  11.0 0.9 %pick_rows.4 = bf16[640,256]{1,0:T(8,128)(2,1)S(1)} custom-call(s32[1]{0:T(128)} %bitcast.3.base_ref, s32[8,256]{1,0:T(8,128)S(1)} %collective-permute-done.ids_ref, bf16[8,80,1024]{2,1,0:T(8,128)(2,1)S(1)} %decode_tables.1.table_ref), custom_call_target="tpu_custom_call" | custom-call | tf_op jit(solution)/shard_map/pick_rows/pallas_call | solution.py:331
  11.8 2.8 %collective-permute-start.9 = (bf16[640,256]{1,0:T(8,128)(2,1)S(1)}, bf16[640,256]{1,0:T(8,128)(2,1)S(1)}, u32[]{:S(2)}, u32[]{:S(2)}) collective-permute-start(bf16[640,256]{1,0:T(8,128)(2,1)S(1)} %pick_rows.4), channel_id=1, source_target_pairs={{0,4},{12,8},{1,5},{13,9},{2,6},{14,10},{3,7},{15,11},{16,20},{28,... | collective-permute-start | bytes 983048 | tf_op jit(solution)/shard_map/ppermute | solution.py:341
  14.6 0.7 %collective-permute-start.7 = (bf16[640,256]{1,0:T(8,128)(2,1)S(1)}, bf16[640,256]{1,0:T(8,128)(2,1)S(1)}, u32[]{:S(2)}, u32[]{:S(2)}) collective-permute-start(bf16[640,256]{1,0:T(8,128)(2,1)S(1)} %pick_rows.4), channel_id=1, source_target_pairs={{4,8},{8,4},{5,9},{9,5},{6,10},{10,6},{7,11},{11,7},{20,24},{24,20... | collective-permute-start | bytes 983048 | tf_op jit(solution)/shard_map/ppermute | solution.py:341
  15.3 0.9 %pick_rows.5 = bf16[640,256]{1,0:T(8,128)(2,1)S(1)} custom-call(s32[1]{0:T(128)} %bitcast.3.base_ref, s32[8,256]{1,0:T(8,128)S(1)} %collective-permute-done.1.ids_ref, bf16[8,80,1024]{2,1,0:T(8,128)(2,1)S(1)} %decode_tables.1.table_ref), custom_call_target="tpu_custom_call" | custom-call | tf_op jit(solution)/shard_map/pick_rows/pallas_call | solution.py:331
  16.1 0.0 copy-start
  16.1 3.3 %collective-permute-start.5 = (bf16[640,256]{1,0:T(8,128)(2,1)S(1)}, bf16[640,256]{1,0:T(8,128)(2,1)S(1)}, u32[]{:S(2)}, u32[]{:S(2)}) collective-permute-start(bf16[640,256]{1,0:T(8,128)(2,1)S(1)} %pick_rows.5), channel_id=1, source_target_pairs={{0,9},{1,8},{12,5},{13,4},{2,11},{3,10},{14,7},{15,6},{16,25},{17,... | collective-permute-start | bytes 983048 | tf_op jit(solution)/shard_map/ppermute | solution.py:328
  19.4 0.0 collective-permute-done.3.refs_4_
  19.4 0.0 collective-permute-done.4.refs_5_
  19.5 0.9 %pick_rows.6 = bf16[640,256]{1,0:T(8,128)(2,1)S(1)} custom-call(s32[1]{0:T(128)} %bitcast.3.base_ref, s32[8,256]{1,0:T(8,128)S(1)} %collective-permute-done.2.ids_ref, bf16[8,80,1024]{2,1,0:T(8,128)(2,1)S(1)} %decode_tables.1.table_ref), custom_call_target="tpu_custom_call" | custom-call | tf_op jit(solution)/shard_map/pick_rows/pallas_call | solution.py:331
  20.3 0.5 collective-permute-start.6
  20.8 0.9 %pick_rows.7 = bf16[640,256]{1,0:T(8,128)(2,1)S(1)} custom-call(s32[1]{0:T(128)} %bitcast.3.base_ref, s32[8,256]{1,0:T(8,128)S(1)} %place_rows.1.ids_ref, bf16[8,80,1024]{2,1,0:T(8,128)(2,1)S(1)} %decode_tables.1.table_ref), custom_call_target="tpu_custom_call" | custom-call | tf_op jit(solution)/shard_map/pick_rows/pallas_call | solution.py:331
  21.6 0.0 collective-permute-done.9
  21.7 0.1 add.20
  21.7 1.3 %collective-permute-start.10 = (bf16[640,256]{1,0:T(8,128)(2,1)S(1)}, bf16[640,256]{1,0:T(8,128)(2,1)S(1)}, u32[]{:S(2)}, u32[]{:S(2)}) collective-permute-start(bf16[640,256]{1,0:T(8,128)(2,1)S(1)} %add.20), channel_id=1, source_target_pairs={{4,12},{8,0},{5,13},{9,1},{6,14},{10,2},{7,15},{11,3},{20,28},{24,... | collective-permute-start | bytes 983048 | tf_op jit(solution)/shard_map/ppermute | solution.py:341
  23.0 0.0 copy-done
  23.1 0.0 collective-permute-done.7.refs_1_
  23.1 2.5 %collective-permute-start.8 = (bf16[16,2304]{1,0:T(8,128)(2,1)S(1)}, bf16[16,2304]{1,0:T(8,128)(2,1)S(1)}, u32[]{:S(2)}, u32[]{:S(2)}) collective-permute-start(bf16[16,2304]{1,0:T(8,128)(2,1)S(1)} %slice.6), channel_id=1, source_target_pairs={{0,1},{4,5},{8,9},{12,13},{2,3},{6,7},{10,11},{14,15},{16,17},{20,... | collective-permute-start | bytes 221192 | tf_op jit(solution)/shard_map/ppermute | solution.py:425
  25.6 2.9 %collective-permute-done.5 = bf16[640,256]{1,0:T(8,128)(2,1)S(1)} collective-permute-done((bf16[640,256]{1,0:T(8,128)(2,1)S(1)}, bf16[640,256]{1,0:T(8,128)(2,1)S(1)}, u32[]{:S(2)}, u32[]{:S(2)}) %collective-permute-start.5) | collective-permute-done | bytes 327712 | tf_op jit(solution)/shard_map/ppermute | solution.py:328
  28.5 6.7 %collective-permute-done.6 = bf16[640,256]{1,0:T(8,128)(2,1)S(1)} collective-permute-done((bf16[640,256]{1,0:T(8,128)(2,1)S(1)}, bf16[640,256]{1,0:T(8,128)(2,1)S(1)}, u32[]{:S(2)}, u32[]{:S(2)}) %collective-permute-start.6) | collective-permute-done | bytes 327712 | tf_op jit(solution)/shard_map/ppermute | solution.py:341
  35.3 0.0 collective-permute-done.8.refs_5_
  35.3 3.5 %collective-permute-done.10.refs_2_ = bf16[640,256]{1,0:T(8,128)(2,1)S(1)} collective-permute-done((bf16[640,256]{1,0:T(8,128)(2,1)S(1)}, bf16[640,256]{1,0:T(8,128)(2,1)S(1)}, u32[]{:S(2)}, u32[]{:S(2)}) %collective-permute-start.10) | collective-permute-done | bytes 327712 | tf_op jit(solution)/shard_map/ppermute | solution.py:341
  38.7 0.1 merge.1.refs_1_
  38.9 1.6 %collective-permute-start.12 = (bf16[640,256]{1,0:T(8,128)(2,1)S(1)}, bf16[640,256]{1,0:T(8,128)(2,1)S(1)}, u32[]{:S(2)}, u32[]{:S(2)}) collective-permute-start(bf16[640,256]{1,0:T(8,128)(2,1)S(1)} %merge.1.refs_1_), channel_id=1, source_target_pairs={{0,2},{2,0},{1,3},{3,1},{4,6},{6,4},{5,7},{7,5},{8,10},{10,8},{9,1... | collective-permute-start | bytes 983048 | tf_op jit(solution)/shard_map/ppermute | solution.py:436
  40.4 1.7 %collective-permute-start.13 = (bf16[640,128]{1,0:T(8,128)(2,1)S(1)}, bf16[640,128]{1,0:T(8,128)(2,1)S(1)}, u32[]{:S(2)}, u32[]{:S(2)}) collective-permute-start(bf16[640,128]{1,0:T(8,128)(2,1)S(1)} %slice.8), channel_id=1, source_target_pairs={{0,1},{2,3},{4,5},{6,7},{8,9},{10,11},{12,13},{14,15},{16,17},{18,... | collective-permute-start | bytes 491528 | tf_op jit(solution)/shard_map/ppermute | solution.py:449
  42.2 1.6 %collective-permute-start.11 = (bf16[640,128]{1,0:T(8,128)(2,1)S(1)}, bf16[640,128]{1,0:T(8,128)(2,1)S(1)}, u32[]{:S(2)}, u32[]{:S(2)}) collective-permute-start(bf16[640,128]{1,0:T(8,128)(2,1)S(1)} %slice.8), channel_id=1, source_target_pairs={{0,3},{2,1},{4,7},{6,5},{8,11},{10,9},{12,15},{14,13},{16,19},{18,... | collective-permute-start | bytes 491528 | tf_op jit(solution)/shard_map/ppermute | solution.py:449
  43.8 0.1 pad_add_fusion.where_ref
  43.9 0.0 collective-permute-done.13.refs_0_
  43.9 5.6 %project_own.1 = (f32[2,272,1152]{2,1,0:T(8,128)S(1)}, f32[2,272,1152]{2,1,0:T(8,128)S(1)}, bf16[2,2,640,1152]{3,2,1,0:T(8,128)(2,1)S(1)}) custom-call(s32[2]{0:T(128)S(1)} %pad_add_fusion.where_ref, bf16[640,128]{1,0:T(8,128)(2,1)S(1)} %collective-permute-done.13.refs_0_, bf16[640,256]{1,0:T(8,128)(2,1)S(1)} %merge.1.refs_1_, bf16[1280,1152]{1,0:T(8,128)(2,1)} %refs_2_.1, ...), custom_call_target="tpu_custom_call" | custom-call | tf_op jit(solution)/shard_map/project_own/pallas_call | solution.py:455
  49.5 0.0 collective-permute-done.11.refs_0_
  49.5 0.0 collective-permute-done.12.refs_1_
  49.5 0.0 copy-start.1
  49.5 4.2 %project_others.1 = (f32[2,272,1152]{2,1,0:T(8,128)}, f32[8,272]{1,0:T(8,128)S(1)}) custom-call(s32[2]{0:T(128)S(1)} %pad_add_fusion.where_ref, bf16[640,128]{1,0:T(8,128)(2,1)S(1)} %collective-permute-done.11.refs_0_, bf16[640,256]{1,0:T(8,128)(2,1)S(1)} %collective-permute-done.12.refs_1_, bf16[2,2,640,1152]{3,2,1,0:T(8,128)(2,1)S(1)} %get-tuple-element.39.refs_2_, ...), custom_call_target="tpu_custom_call" | custom-call | tf_op jit(solution)/shard_map/project_others/pallas_call | solution.py:468
  53.8 1.6 %collective-permute-start.14 = (f32[8,272]{1,0:T(8,128)S(1)}, f32[8,272]{1,0:T(8,128)S(1)}, u32[]{:S(2)}, u32[]{:S(2)}) collective-permute-start(f32[8,272]{1,0:T(8,128)S(1)} %get-tuple-element.43.refs_0_), channel_id=1, source_target_pairs={{0,2},{2,0},{1,3},{3,1},{4,6},{6,4},{5,7},{7,5},{8,10},{10,8},{9,1... | collective-permute-start | bytes 26120 | tf_op jit(solution)/shard_map/ppermute | solution.py:491
  55.4 0.0 copy-done.1
  55.4 1.9 %prepare.1 = (f32[2,256,1152]{2,1,0:T(8,128)S(1)}, f32[3,2,256,1152]{3,2,1,0:T(8,128)S(1)}) custom-call(f32[4,2304]{1,0:T(4,128)S(1)} %copy-done.1, f32[2,272,1152]{2,1,0:T(8,128)} %get-tuple-element.44.value_hbm), custom_call_target="tpu_custom_call" | custom-call | tf_op jit(solution)/shard_map/prepare/pallas_call | solution.py:499
  57.3 0.3 collective-permute-done.14.refs_1_
  57.6 2.8 %finish.1 = bf16[256,2304]{1,0:T(8,128)(2,1)} custom-call(s32[1]{0:T(128)} %bitcast.keep_ref, f32[8,272]{1,0:T(8,128)S(1)} %get-tuple-element.43.refs_0_, f32[8,272]{1,0:T(8,128)S(1)} %collective-permute-done.14.refs_1_, f32[2,256,1152]{2,1,0:T(8,128)S(1)} %get-tuple-element.45.refs_2_, f32[3,2,256,1152]{3,2,1,0:T(8,128)S(1)} %get-tuple-element.46.refs_3_, ...), custom_call_target="tpu_custom_call" | custom-call | tf_op jit(solution)/shard_map/finish/pallas_call | solution.py:514
  (3 shorter events, 0.1 us)
Async XLA Ops:
  0.0 19.4 %collective-permute-start.3 = (bf16[1280,1152]{1,0:T(8,128)(2,1)}, bf16[1280,1152]{1,0:T(8,128)(2,1)}, u32[]{:S(2)}, u32[]{:S(2)}) collective-permute-start(bf16[1280,1152]{1,0:T(8,128)(2,1)} %refs_2_.1), channel_id=1, source_target_pairs={{0,1},{1,0},{2,3},{3,2},{4,5},{5,4},{6,7},{7,6},{8,9},{9,8},{10,11... | collective-permute-start | bytes 8847368 | tf_op jit(solution)/shard_map/ppermute | solution.py:419
  0.5 19.0 %collective-permute-start.4 = (bf16[1280,1152]{1,0:T(8,128)(2,1)}, bf16[1280,1152]{1,0:T(8,128)(2,1)}, u32[]{:S(2)}, u32[]{:S(2)}) collective-permute-start(bf16[1280,1152]{1,0:T(8,128)(2,1)} %refs_3_.1), channel_id=1, source_target_pairs={{0,1},{1,0},{2,3},{3,2},{4,5},{5,4},{6,7},{7,6},{8,9},{9,8},{10,11... | collective-permute-start | bytes 8847368 | tf_op jit(solution)/shard_map/ppermute | solution.py:420
  1.9 8.1 %collective-permute-start = (s32[8,256]{1,0:T(8,128)S(1)}, s32[8,256]{1,0:T(8,128)S(1)}, u32[]{:S(2)}, u32[]{:S(2)}) collective-permute-start(s32[8,256]{1,0:T(8,128)S(1)} %place_rows.1.ids_ref), channel_id=1, source_target_pairs={{0,12},{4,8},{8,4},{12,0},{1,13},{5,9},{9,5},{13,1},{2,14},{6,10},... | collective-permute-start | bytes 24584 | tf_op jit(solution)/shard_map/ppermute | solution.py:325
  7.0 4.0 %collective-permute-start.1 = (s32[8,256]{1,0:T(8,128)S(1)}, s32[8,256]{1,0:T(8,128)S(1)}, u32[]{:S(2)}, u32[]{:S(2)}) collective-permute-start(s32[8,256]{1,0:T(8,128)S(1)} %place_rows.1.ids_ref), channel_id=1, source_target_pairs={{0,8},{1,9},{4,13},{5,12},{8,1},{9,0},{12,4},{13,5},{2,10},{3,11},... | collective-permute-start | bytes 24584 | tf_op jit(solution)/shard_map/ppermute | solution.py:328
  7.0 4.0 %collective-permute-start.2 = (s32[8,256]{1,0:T(8,128)S(1)}, s32[8,256]{1,0:T(8,128)S(1)}, u32[]{:S(2)}, u32[]{:S(2)}) collective-permute-start(s32[8,256]{1,0:T(8,128)S(1)} %place_rows.1.ids_ref), channel_id=1, source_target_pairs={{0,4},{4,0},{8,12},{12,8},{1,5},{5,1},{9,13},{13,9},{2,6},{6,2},{1... | collective-permute-start | bytes 24584 | tf_op jit(solution)/shard_map/ppermute | solution.py:325
  11.8 9.8 %collective-permute-start.9 = (bf16[640,256]{1,0:T(8,128)(2,1)S(1)}, bf16[640,256]{1,0:T(8,128)(2,1)S(1)}, u32[]{:S(2)}, u32[]{:S(2)}) collective-permute-start(bf16[640,256]{1,0:T(8,128)(2,1)S(1)} %pick_rows.4), channel_id=1, source_target_pairs={{0,4},{12,8},{1,5},{13,9},{2,6},{14,10},{3,7},{15,11},{16,20},{28,... | collective-permute-start | bytes 983048 | tf_op jit(solution)/shard_map/ppermute | solution.py:341
  14.6 8.5 %collective-permute-start.7 = (bf16[640,256]{1,0:T(8,128)(2,1)S(1)}, bf16[640,256]{1,0:T(8,128)(2,1)S(1)}, u32[]{:S(2)}, u32[]{:S(2)}) collective-permute-start(bf16[640,256]{1,0:T(8,128)(2,1)S(1)} %pick_rows.4), channel_id=1, source_target_pairs={{4,8},{8,4},{5,9},{9,5},{6,10},{10,6},{7,11},{11,7},{20,24},{24,20... | collective-permute-start | bytes 983048 | tf_op jit(solution)/shard_map/ppermute | solution.py:341
  16.1 6.9 %copy-start = (bf16[256,2304]{1,0:T(8,128)(2,1)S(1)}, bf16[256,2304]{1,0:T(8,128)(2,1)}, u32[]{:S(2)}) copy-start(bf16[256,2304]{1,0:T(8,128)(2,1)} %refs_4_.1) | copy-start | bytes 3538948
  16.1 12.4 %collective-permute-start.5 = (bf16[640,256]{1,0:T(8,128)(2,1)S(1)}, bf16[640,256]{1,0:T(8,128)(2,1)S(1)}, u32[]{:S(2)}, u32[]{:S(2)}) collective-permute-start(bf16[640,256]{1,0:T(8,128)(2,1)S(1)} %pick_rows.5), channel_id=1, source_target_pairs={{0,9},{1,8},{12,5},{13,4},{2,11},{3,10},{14,7},{15,6},{16,25},{17,... | collective-permute-start | bytes 983048 | tf_op jit(solution)/shard_map/ppermute | solution.py:328
  20.3 14.9 %collective-permute-start.6 = (bf16[640,256]{1,0:T(8,128)(2,1)S(1)}, bf16[640,256]{1,0:T(8,128)(2,1)S(1)}, u32[]{:S(2)}, u32[]{:S(2)}) collective-permute-start(bf16[640,256]{1,0:T(8,128)(2,1)S(1)} %pick_rows.6), channel_id=1, source_target_pairs={{0,4},{4,0},{8,12},{12,8},{1,5},{5,1},{9,13},{13,9},{2,6},{6,2},{1... | collective-permute-start | bytes 983048 | tf_op jit(solution)/shard_map/ppermute | solution.py:341
  21.7 17.0 %collective-permute-start.10 = (bf16[640,256]{1,0:T(8,128)(2,1)S(1)}, bf16[640,256]{1,0:T(8,128)(2,1)S(1)}, u32[]{:S(2)}, u32[]{:S(2)}) collective-permute-start(bf16[640,256]{1,0:T(8,128)(2,1)S(1)} %add.20), channel_id=1, source_target_pairs={{4,12},{8,0},{5,13},{9,1},{6,14},{10,2},{7,15},{11,3},{20,28},{24,... | collective-permute-start | bytes 983048 | tf_op jit(solution)/shard_map/ppermute | solution.py:341
  23.1 12.2 %collective-permute-start.8 = (bf16[16,2304]{1,0:T(8,128)(2,1)S(1)}, bf16[16,2304]{1,0:T(8,128)(2,1)S(1)}, u32[]{:S(2)}, u32[]{:S(2)}) collective-permute-start(bf16[16,2304]{1,0:T(8,128)(2,1)S(1)} %slice.6), channel_id=1, source_target_pairs={{0,1},{4,5},{8,9},{12,13},{2,3},{6,7},{10,11},{14,15},{16,17},{20,... | collective-permute-start | bytes 221192 | tf_op jit(solution)/shard_map/ppermute | solution.py:425
  38.9 10.7 %collective-permute-start.12 = (bf16[640,256]{1,0:T(8,128)(2,1)S(1)}, bf16[640,256]{1,0:T(8,128)(2,1)S(1)}, u32[]{:S(2)}, u32[]{:S(2)}) collective-permute-start(bf16[640,256]{1,0:T(8,128)(2,1)S(1)} %merge.1.refs_1_), channel_id=1, source_target_pairs={{0,2},{2,0},{1,3},{3,1},{4,6},{6,4},{5,7},{7,5},{8,10},{10,8},{9,1... | collective-permute-start | bytes 983048 | tf_op jit(solution)/shard_map/ppermute | solution.py:436
  40.4 3.5 %collective-permute-start.13 = (bf16[640,128]{1,0:T(8,128)(2,1)S(1)}, bf16[640,128]{1,0:T(8,128)(2,1)S(1)}, u32[]{:S(2)}, u32[]{:S(2)}) collective-permute-start(bf16[640,128]{1,0:T(8,128)(2,1)S(1)} %slice.8), channel_id=1, source_target_pairs={{0,1},{2,3},{4,5},{6,7},{8,9},{10,11},{12,13},{14,15},{16,17},{18,... | collective-permute-start | bytes 491528 | tf_op jit(solution)/shard_map/ppermute | solution.py:449
  42.2 7.3 %collective-permute-start.11 = (bf16[640,128]{1,0:T(8,128)(2,1)S(1)}, bf16[640,128]{1,0:T(8,128)(2,1)S(1)}, u32[]{:S(2)}, u32[]{:S(2)}) collective-permute-start(bf16[640,128]{1,0:T(8,128)(2,1)S(1)} %slice.8), channel_id=1, source_target_pairs={{0,3},{2,1},{4,7},{6,5},{8,11},{10,9},{12,15},{14,13},{16,19},{18,... | collective-permute-start | bytes 491528 | tf_op jit(solution)/shard_map/ppermute | solution.py:449
  49.5 5.8 %copy-start.1 = (f32[4,2304]{1,0:T(4,128)S(1)}, f32[4,2304]{1,0:T(4,128)}, u32[]{:S(2)}) copy-start(f32[4,2304]{1,0:T(4,128)} %refs_5_.1) | copy-start | bytes 110596
  53.8 3.8 %collective-permute-start.14 = (f32[8,272]{1,0:T(8,128)S(1)}, f32[8,272]{1,0:T(8,128)S(1)}, u32[]{:S(2)}, u32[]{:S(2)}) collective-permute-start(f32[8,272]{1,0:T(8,128)S(1)} %get-tuple-element.43.refs_0_), channel_id=1, source_target_pairs={{0,2},{2,0},{1,3},{3,1},{4,6},{6,4},{5,7},{7,5},{8,10},{10,8},{9,1... | collective-permute-start | bytes 26120 | tf_op jit(solution)/shard_map/ppermute | solution.py:491

commit v16 on v15

--- a/solution.py
+++ b/solution.py
@@ -122,73 +122,68 @@
     refs[-1][...] = total.astype(BF16)
 
 
+def load_kernel(*refs):
+    count = len(refs) // 2
+    sources, targets, sems = refs[:count], refs[count : 2 * count], refs[-1]
+    pieces = sems.shape[0] // count
+    step = sources[0].shape[0] // pieces
+    copies = []
+    for k in range(count):
+        for n in range(pieces):
+            span = pl.ds(n * step, step)
+            copy = pltpu.make_async_copy(
+                sources[k].at[span, :], targets[k].at[span, :], sems.at[k * pieces + n]
+            )
+            copy.start()
+            copies.append(copy)
+    for copy in copies:
+        copy.wait()
+
+
 def project_kernel(shifts, count, where_ref, *refs):
     pieces = len(shifts)
     first = 0 in shifts
     rims = refs[:pieces]
     bodies = refs[pieces : 2 * pieces]
-    refs = refs[2 * pieces :]
+    weights = refs[2 * pieces : 2 * pieces + 4]
+    refs = refs[2 * pieces + 4 :]
     depth, tokens = bodies[0].shape
     rep = where_ref[0]
     tp = where_ref[1]
     if first:
-        weights = refs[:4]
-        key_ref, value_ref, rest, held, sems, rest_sems = refs[4:]
-        half = held.shape[-1]
-
-        def bring(target, far, which, n, s, sem):
-            owner = lax.rem(tp + count - s, count)
-            rows = pl.ds(pl.multiple_of(owner * depth, depth), depth)
-            copy = pltpu.make_async_copy(
-                weights[2 * far + which].at[rows, :],
-                target.at[far, which, pl.ds(n * depth, depth), :],
-                sem,
-            )
-            copy.start()
-            return copy
-
-        copies = [
-            bring(held, far, which, 0, 0, sems.at[2 * far + which])
-            for far in range(2)
-            for which in (1, 0)
-        ]
-        later = [
-            bring(rest, far, which, n, n + 1, rest_sems.at[(2 * far + which) * (count - 1) + n])
-            for far in range(2)
-            for which in (1, 0)
-            for n in range(count - 1)
-        ]
+        key_ref, value_ref = refs
+        half = value_ref.shape[-1]
     else:
-        later = []
-        rest, begun_keys, begun_values, hidden_halo, hidden = refs[:5]
-        value_hbm, stats_ref, states, done, done_sems = refs[5:]
-        held = rest
-        half = held.shape[-1]
+        begun_keys, begun_values, hidden_halo, hidden, value_ref, stats_ref, states = refs
+        half = value_ref.shape[-1]
         for slot in range(2):
             states[slot, :RIM] = hidden_halo[:, slot * half : (slot + 1) * half]
             states[slot, RIM:] = hidden[:, slot * half : (slot + 1) * half]
     body = jnp.concatenate([b[...].astype(F32) for b in bodies], axis=0).T.astype(BF16)
     rim = jnp.concatenate([r[...].astype(F32) for r in rims], axis=0).T.astype(BF16)
     memory = jnp.concatenate([rim[LANES - RIM :], body], axis=0)
+
+    def project(far, which):
+        field = None
+        for n, s in enumerate(shifts):
+            owner = lax.rem(tp + count - s, count)
+            rows = pl.ds(pl.multiple_of(owner * depth, depth), depth)
+            part = dot(
+                memory[:, n * depth : (n + 1) * depth], weights[2 * far + which][rows, :]
+            )
+            field = part if field is None else field + part
+        return field
+
     sums = [0.0] * 4
     for far in range(2):
         slot = rep if far == 0 else 1 - rep
-        fields = [None, None]
-        for which in (1, 0):
-            if first:
-                copies[2 * far + 1 - which].wait()
-            fields[which] = dot(memory, held[far, which])
-            if not first and which == 1:
-                done[far] = fields[1] + begun_values[slot]
-                copy = pltpu.make_async_copy(done.at[far], value_hbm.at[slot], done_sems.at[far])
-                copy.start()
-                later.append(copy)
         if first:
-            value_ref[slot] = fields[1]
-            key_ref[slot] = fields[0]
+            value_ref[slot] = project(far, 1)
+            key_ref[slot] = project(far, 0)
         else:
-            keys = fields[0] + begun_keys[slot]
-            values = done[far]
+            values = project(far, 1) + begun_values[slot]
+            value_ref[slot] = values
+            keys = project(far, 0) + begun_keys[slot]
             here = states[slot].astype(F32)
             terms = (here * here, keys * keys, here * keys, values * values)
             sums = [a + jnp.sum(t, axis=1, keepdims=True) for a, t in zip(sums, terms)]
@@ -199,30 +194,16 @@
         for k in range(4):
             packed = jnp.where(lane == k, sums[k], packed)
         stats_ref[...] = dot_nt(unit(8, F32), packed, lax.Precision.HIGHEST)
-    for copy in later:
-        copy.wait()
-
-
-def prepare_kernel(chunk, taps_ref, value_hbm, value_ref, tap_ref, rows_ref, sems):
+
+
+def prepare_kernel(taps_ref, rows_ref, tap_ref):
     half = rows_ref.shape[-1]
-    tokens = value_ref.shape[1]
-    copies = []
-    for slot in range(2):
-        for start in range(0, half, chunk):
-            span = pl.ds(start, chunk)
-            copy = pltpu.make_async_copy(
-                value_hbm.at[slot, :, span], rows_ref.at[slot, :, span], sems.at[len(copies)]
-            )
-            copy.start()
-            copies.append(copy)
+    tokens = tap_ref.shape[2]
     for slot in range(2):
         for start in range(0, half, LANES):
             size = min(LANES, half - start)
             span = slice(start, start + size)
             there = slice(slot * half + start, slot * half + start + size)
-            if start % chunk == 0:
-                copies[(slot * half + start) // chunk].wait()
-            value_ref[slot, :, span] = rows_ref[slot, RIM:, span]
             for tap in range(1, KERNEL):
                 lag = DILATION * tap
                 rows = rows_ref[slot, RIM - lag : RIM - lag + tokens, span]
@@ -258,7 +239,7 @@
             size = min(LANES, half - start)
             span = slice(start, start + size)
             there = slice(slot * half + start, slot * half + start + size)
-            values = value_ref[slot, :, span]
+            values = value_ref[slot, RIM:, span]
             conv = taps_ref[0:1, there] * values * factors[0, :, :size]
             for tap in range(1, KERNEL):
                 conv = conv + tap_ref[tap - 1, slot, :, span] * factors[tap, :, :size]
@@ -312,7 +293,7 @@
         name="pick_all",
     )((here * rows).astype(I32).reshape(1), asked, decoded)
     total = lax.psum_scatter(partial, "mem", scatter_dimension=0, tiled=False)
-    return total, meanwhile(partial), settled
+    return total, meanwhile(partial, partial, settled)
 
 
 def line_sum(stored, decoded, here, meanwhile, settled):
@@ -357,8 +338,8 @@
     own = pick(after(stored, rows_1))
     beside = send(rows_1, (0, 1), (1, 0), (2, 3), (3, 2))
     onward = after(rows_2, rows_1, own) + inward
+    other = meanwhile(across, onward, settled)
     onward = send(onward, (1, 3), (2, 0))
-    other = meanwhile(across)
     own, other = lax.optimization_barrier((own + past + beside, other))
     memory = pl.pallas_call(
         merge_kernel,
@@ -367,7 +348,7 @@
         compiler_params=limit(4),
         name="merge",
     )(own, across, onward)
-    return memory, other, settled
+    return memory, other
 
 
 def shards(
@@ -420,15 +401,29 @@
     other_value = lax.ppermute(value_weight, "rep", [(0, 1), (1, 0)])
     needed = [(i, i + 1) for i in range(blocks - 1) if (i + 1) * tokens % seq_length]
 
-    def meanwhile(token):
+    def meanwhile(token, later, weights):
         tail = after(hidden[tokens - RIM :], token)
-        return lax.ppermute(tail, ("mem", "rep"), needed)
+        halo = lax.ppermute(tail, ("mem", "rep"), needed)
+        weights = lax.optimization_barrier((*weights, later))[:-1]
+        held = pl.pallas_call(
+            load_kernel,
+            in_specs=[anywhere] * 4,
+            out_specs=(resident,) * 4,
+            out_shape=(pltpu.VMEM(key_weight.shape, BF16),) * 4,
+            scratch_shapes=[pltpu.SemaphoreType.DMA((8,))],
+            compiler_params=limit(4),
+            name="load_weights",
+        )(*[in_hbm(w) for w in weights])
+        return halo, held
 
     summed = line_sum if mems == 4 else scattered_sum
-    memory, hidden_halo, others = summed(
-        stored, decoded, here, meanwhile, (other_key, other_value)
+    memory, (hidden_halo, weights) = summed(
+        stored,
+        decoded,
+        here,
+        meanwhile,
+        (key_weight, value_weight, other_key, other_value),
     )
-    weights = [in_hbm(w) for w in (key_weight, value_weight, *others)]
 
     where = jnp.stack([lax.axis_index("rep"), lax.axis_index("tp")]).astype(I32)
     extended = tokens + RIM
@@ -452,40 +447,23 @@
     rims = [next_rim(rim, s) for s in range(tps)]
     others = tps - 1
     field = jax.ShapeDtypeStruct((2, extended, half), F32)
-    *begun, rest = pl.pallas_call(
+    begun = pl.pallas_call(
         functools.partial(project_kernel, (0,), tps),
-        in_specs=[smem] + [resident] * 2 + [anywhere] * 4,
-        out_specs=(resident,) * 3,
-        out_shape=(field, field, pltpu.VMEM((2, 2, others * depth, half), BF16)),
-        scratch_shapes=[
-            pltpu.VMEM((2, 2, depth, half), BF16),
-            pltpu.SemaphoreType.DMA((4,)),
-            pltpu.SemaphoreType.DMA((4 * others,)),
-        ],
-        compiler_params=limit(12),
+        in_specs=[smem] + [resident] * 6,
+        out_specs=(resident,) * 2,
+        out_shape=(field, field),
+        compiler_params=limit(8),
         name="project_own",
     )(where, rims[0], memory, *weights)
     values, stats = pl.pallas_call(
         functools.partial(project_kernel, tuple(range(1, tps)), tps),
-        in_specs=[smem] + [resident] * (2 * others + 5),
-        out_specs=(pl.BlockSpec(memory_space=pltpu.HBM), resident),
-        out_shape=(pltpu.HBM(field.shape, F32), jax.ShapeDtypeStruct((8, extended), F32)),
-        scratch_shapes=[
-            pltpu.VMEM((2, extended, half), BF16),
-            pltpu.VMEM((2, extended, half), F32),
-            pltpu.SemaphoreType.DMA((2,)),
-        ],
-        compiler_params=limit(14),
+        in_specs=[smem] + [resident] * (2 * others + 8),
+        out_specs=(resident,) * 2,
+        out_shape=(field, jax.ShapeDtypeStruct((8, extended), F32)),
+        scratch_shapes=[pltpu.VMEM((2, extended, half), BF16)],
+        compiler_params=limit(8),
         name="project_others",
-    )(
-        where,
-        *rims[1:],
-        *bodies[1:],
-        rest,
-        *begun,
-        hidden_halo,
-        hidden,
-    )
+    )(where, *rims[1:], *bodies[1:], *weights, *begun, hidden_halo, hidden)
 
     all_stats = [stats] + [
         lax.ppermute(stats, "tp", [(i, (i + s) % tps) for i in range(tps)]) for s in range(1, tps)
@@ -494,23 +472,14 @@
     step = 2 * half
     if half % LANES == 0:
         step = next(c for c in (384, 256, 128) if half % c == 0)
-    chunk = min(step, half)
-    body = (2, tokens, half)
-    values, products = pl.pallas_call(
-        functools.partial(prepare_kernel, chunk),
-        in_specs=[resident, anywhere],
-        out_specs=(resident,) * 2,
-        out_shape=(
-            jax.ShapeDtypeStruct(body, F32),
-            jax.ShapeDtypeStruct((KERNEL - 1, *body), F32),
-        ),
-        scratch_shapes=[
-            pltpu.VMEM((2, extended, half), F32),
-            pltpu.SemaphoreType.DMA((2 * half // chunk,)),
-        ],
-        compiler_params=limit(6),
+    products = pl.pallas_call(
+        prepare_kernel,
+        in_specs=[resident] * 2,
+        out_specs=resident,
+        out_shape=jax.ShapeDtypeStruct((KERNEL - 1, 2, tokens, half), F32),
+        compiler_params=limit(4),
         name="prepare",
-    )(conv_weight, in_hbm(values))
+    )(conv_weight, values)
     return pl.pallas_call(
         functools.partial(finish_kernel, tps, step),
         in_specs=[smem] + [resident] * (tps + 4),

time: 60.9 us -> 68.8 us (1.13)
  the two profiles are of different devices: /device:TPU:0 before, /device:TPU:18 now
where the time goes in v16:
time: 68.8 us; the launch traced here: 68.2 us
  Pallas kernels  23.3 us (34%)
  starting transfers between devices  19.6 us (28%)
  local copies, waits for them, and re-layouts  16.4 us (24%)
  waiting for transfers between devices  8.3 us (12%)
    unnamed x26, local copies, waits for them, and re-layouts  14.8 us
    ppermute x4, starting transfers between devices, send(): return lax.ppermute(x, 'mem', pairs)  8.15 us
    ppermute x4, waiting for transfers between devices, send(): return lax.ppermute(x, 'mem', pairs)  7.73 us
    pallas_call x1, Pallas kernels, meanwhile(): pl.pallas_call(load_kernel, in_specs=[anywhere] * 4, out_specs=(resident,...  4.47 us
    pallas_call x1, Pallas kernels, shards(): pl.pallas_call(functools.partial(project_kernel, tuple(range(1, tps)), tp...  4.2 us
    pallas_call x4, Pallas kernels, pick(): pl.pallas_call(pick_kernel, in_specs=[pl.BlockSpec(memory_space=pltpu.SME...  3.45 us
    pallas_call x1, Pallas kernels, shards(): pl.pallas_call(functools.partial(project_kernel, (0,), tps), in_specs=[sm...  3.42 us
    ppermute x2, starting transfers between devices, next_rim(): return lax.ppermute(rim, ('mem', 'tp', 'rep'), pairs)  3.42 us
  transfers between devices with their start and end apart: 15, of which 3 were waited for; matrix products, arithmetic and copies ran while one was open for 3% of the time, Pallas kernels for 24%

profile of v16, /device:TPU:18, one launch (start us, length us, event | category | flops | bytes accessed | tf_op | source)
XLA Modules:
  0.0 68.2 jit_solution(2170277662052260847)
XLA Ops:
  0.0 0.0 collective-permute-start.3
  0.0 0.5 collective-permute-start.4
  0.5 1.3 %place_rows.1.ids_ref = s32[8,256]{1,0:T(8,128)S(1)} custom-call(s32[8,256]{1,0:T(8,128)} %bitcast.11, s32[32,128]{1,0:T(8,128)} %bitcast.10), custom_call_target="tpu_custom_call" | custom-call | tf_op jit(solution)/shard_map/place_rows/pallas_call | solution.py:373
  1.9 1.6 %collective-permute-start.2 = (s32[8,256]{1,0:T(8,128)S(1)}, s32[8,256]{1,0:T(8,128)S(1)}, u32[]{:S(2)}, u32[]{:S(2)}) collective-permute-start(s32[8,256]{1,0:T(8,128)S(1)} %place_rows.1.ids_ref), channel_id=1, source_target_pairs={{0,4},{4,0},{8,12},{12,8},{1,5},{5,1},{9,13},{13,9},{2,6},{6,2},{1... | collective-permute-start | bytes 24584 | tf_op jit(solution)/shard_map/ppermute | solution.py:306
  3.5 0.0 collective-permute-start.1
  3.5 1.2 %collective-permute-start = (s32[8,256]{1,0:T(8,128)S(1)}, s32[8,256]{1,0:T(8,128)S(1)}, u32[]{:S(2)}, u32[]{:S(2)}) collective-permute-start(s32[8,256]{1,0:T(8,128)S(1)} %place_rows.1.ids_ref), channel_id=1, source_target_pairs={{0,12},{4,8},{8,4},{12,0},{1,13},{5,9},{9,5},{13,1},{2,14},{6,10},... | collective-permute-start | bytes 24584 | tf_op jit(solution)/shard_map/ppermute | solution.py:306
  4.7 2.7 %decode_tables.1.table_ref = bf16[8,80,1024]{2,1,0:T(8,128)(2,1)S(1)} custom-call(bf16[8,80,1024]{2,1,0:T(8,128)(2,1)} %bitcast.8, bf16[5,8,1024]{2,1,0:T(8,128)(2,1)} %bitcast.9), custom_call_target="tpu_custom_call" | custom-call | tf_op jit(solution)/shard_map/decode_tables/pallas_call | solution.py:387
  7.5 0.0 collective-permute-done.2.ids_ref
  7.5 0.5 collective-permute-done.1.ids_ref
  8.0 0.0 collective-permute-done.ids_ref
  8.1 0.9 %pick_rows.4 = bf16[640,256]{1,0:T(8,128)(2,1)S(1)} custom-call(s32[1]{0:T(128)} %bitcast.3.base_ref, s32[8,256]{1,0:T(8,128)S(1)} %collective-permute-done.ids_ref, bf16[8,80,1024]{2,1,0:T(8,128)(2,1)S(1)} %decode_tables.1.table_ref), custom_call_target="tpu_custom_call" | custom-call | tf_op jit(solution)/shard_map/pick_rows/pallas_call | solution.py:312
  8.9 1.3 %collective-permute-start.9 = (bf16[640,256]{1,0:T(8,128)(2,1)S(1)}, bf16[640,256]{1,0:T(8,128)(2,1)S(1)}, u32[]{:S(2)}, u32[]{:S(2)}) collective-permute-start(bf16[640,256]{1,0:T(8,128)(2,1)S(1)} %pick_rows.4), channel_id=1, source_target_pairs={{0,4},{12,8},{1,5},{13,9},{2,6},{14,10},{3,7},{15,11},{16,20},{28,... | collective-permute-start | bytes 983048 | tf_op jit(solution)/shard_map/ppermute | solution.py:322
  10.2 2.2 %collective-permute-start.7 = (bf16[640,256]{1,0:T(8,128)(2,1)S(1)}, bf16[640,256]{1,0:T(8,128)(2,1)S(1)}, u32[]{:S(2)}, u32[]{:S(2)}) collective-permute-start(bf16[640,256]{1,0:T(8,128)(2,1)S(1)} %pick_rows.4), channel_id=1, source_target_pairs={{4,8},{8,4},{5,9},{9,5},{6,10},{10,6},{7,11},{11,7},{20,24},{24,20... | collective-permute-start | bytes 983048 | tf_op jit(solution)/shard_map/ppermute | solution.py:322
  12.5 0.9 %pick_rows.5 = bf16[640,256]{1,0:T(8,128)(2,1)S(1)} custom-call(s32[1]{0:T(128)} %bitcast.3.base_ref, s32[8,256]{1,0:T(8,128)S(1)} %collective-permute-done.1.ids_ref, bf16[8,80,1024]{2,1,0:T(8,128)(2,1)S(1)} %decode_tables.1.table_ref), custom_call_target="tpu_custom_call" | custom-call | tf_op jit(solution)/shard_map/pick_rows/pallas_call | solution.py:312
  13.3 1.3 %collective-permute-start.5 = (bf16[640,256]{1,0:T(8,128)(2,1)S(1)}, bf16[640,256]{1,0:T(8,128)(2,1)S(1)}, u32[]{:S(2)}, u32[]{:S(2)}) collective-permute-start(bf16[640,256]{1,0:T(8,128)(2,1)S(1)} %pick_rows.5), channel_id=1, source_target_pairs={{0,9},{1,8},{12,5},{13,4},{2,11},{3,10},{14,7},{15,6},{16,25},{17,... | collective-permute-start | bytes 983048 | tf_op jit(solution)/shard_map/ppermute | solution.py:309
  14.6 0.0 collective-permute-done.3.refs_2_
  14.7 0.9 %pick_rows.6 = bf16[640,256]{1,0:T(8,128)(2,1)S(1)} custom-call(s32[1]{0:T(128)} %bitcast.3.base_ref, s32[8,256]{1,0:T(8,128)S(1)} %collective-permute-done.2.ids_ref, bf16[8,80,1024]{2,1,0:T(8,128)(2,1)S(1)} %decode_tables.1.table_ref), custom_call_target="tpu_custom_call" | custom-call | tf_op jit(solution)/shard_map/pick_rows/pallas_call | solution.py:312
  15.5 3.1 %collective-permute-start.6 = (bf16[640,256]{1,0:T(8,128)(2,1)S(1)}, bf16[640,256]{1,0:T(8,128)(2,1)S(1)}, u32[]{:S(2)}, u32[]{:S(2)}) collective-permute-start(bf16[640,256]{1,0:T(8,128)(2,1)S(1)} %pick_rows.6), channel_id=1, source_target_pairs={{0,4},{4,0},{8,12},{12,8},{1,5},{5,1},{9,13},{13,9},{2,6},{6,2},{1... | collective-permute-start | bytes 983048 | tf_op jit(solution)/shard_map/ppermute | solution.py:322
  18.7 0.9 %pick_rows.7 = bf16[640,256]{1,0:T(8,128)(2,1)S(1)} custom-call(s32[1]{0:T(128)} %bitcast.3.base_ref, s32[8,256]{1,0:T(8,128)S(1)} %place_rows.1.ids_ref, bf16[8,80,1024]{2,1,0:T(8,128)(2,1)S(1)} %decode_tables.1.table_ref), custom_call_target="tpu_custom_call" | custom-call | tf_op jit(solution)/shard_map/pick_rows/pallas_call | solution.py:312
  19.5 1.9 %collective-permute-done.9 = bf16[640,256]{1,0:T(8,128)(2,1)S(1)} collective-permute-done((bf16[640,256]{1,0:T(8,128)(2,1)S(1)}, bf16[640,256]{1,0:T(8,128)(2,1)S(1)}, u32[]{:S(2)}, u32[]{:S(2)}) %collective-permute-start.9) | collective-permute-done | bytes 327712 | tf_op jit(solution)/shard_map/ppermute | solution.py:322
  21.4 0.1 add.20
  21.5 1.5 %collective-permute-start.10 = (bf16[640,256]{1,0:T(8,128)(2,1)S(1)}, bf16[640,256]{1,0:T(8,128)(2,1)S(1)}, u32[]{:S(2)}, u32[]{:S(2)}) collective-permute-start(bf16[640,256]{1,0:T(8,128)(2,1)S(1)} %add.20), channel_id=1, source_target_pairs={{4,12},{8,0},{5,13},{9,1},{6,14},{10,2},{7,15},{11,3},{20,28},{24,... | collective-permute-start | bytes 983048 | tf_op jit(solution)/shard_map/ppermute | solution.py:322
  22.9 0.9 %slice.6 = bf16[16,2304]{1,0:T(8,128)(2,1)S(1)} slice(bf16[256,2304]{1,0:T(8,128)(2,1)} %refs_4_.1), slice={[240:256], [0:2304]} | slice | bytes 147456 | tf_op jit(solution)/shard_map/slice | solution.py:405
  23.8 5.9 %collective-permute-done.7.refs_1_ = bf16[640,256]{1,0:T(8,128)(2,1)S(1)} collective-permute-done((bf16[640,256]{1,0:T(8,128)(2,1)S(1)}, bf16[640,256]{1,0:T(8,128)(2,1)S(1)}, u32[]{:S(2)}, u32[]{:S(2)}) %collective-permute-start.7) | collective-permute-done | bytes 327712 | tf_op jit(solution)/shard_map/ppermute | solution.py:322
  29.7 1.3 %collective-permute-start.8 = (bf16[16,2304]{1,0:T(8,128)(2,1)S(1)}, bf16[16,2304]{1,0:T(8,128)(2,1)S(1)}, u32[]{:S(2)}, u32[]{:S(2)}) collective-permute-start(bf16[16,2304]{1,0:T(8,128)(2,1)S(1)} %slice.6), channel_id=1, source_target_pairs={{0,1},{4,5},{8,9},{12,13},{2,3},{6,7},{10,11},{14,15},{16,17},{20,... | collective-permute-start | bytes 221192 | tf_op jit(solution)/shard_map/ppermute | solution.py:406
  31.0 4.5 %load_weights.1 = (bf16[1280,1152]{1,0:T(8,128)(2,1)S(1)}, bf16[1280,1152]{1,0:T(8,128)(2,1)S(1)}, bf16[1280,1152]{1,0:T(8,128)(2,1)S(1)}, bf16[1280,1152]{1,0:T(8,128)(2,1)S(1)}) custom-call(bf16[1280,1152]{1,0:T(8,128)(2,1)} %refs_0_, bf16[1280,1152]{1,0:T(8,128)(2,1)} %refs_1_, bf16[1280,1152]{1,0:T(8,128)(2,1)} %copy-done.12, ...), custom_call_target="tpu_custom_call" | custom-call | tf_op jit(solution)/shard_map/load_weights/pallas_call | solution.py:408
  35.5 1.6 %copy-done = bf16[1280,1152]{1,0:T(8,128)(2,1)} copy-done((bf16[1280,1152]{1,0:T(8,128)(2,1)}, bf16[1280,1152]{1,0:T(8,128)(2,1)S(1)}, u32[]{:S(2)}) %copy-start) | copy-done | bytes 2949144
  37.1 1.6 %copy-done.2 = bf16[1280,1152]{1,0:T(8,128)(2,1)} copy-done((bf16[1280,1152]{1,0:T(8,128)(2,1)}, bf16[1280,1152]{1,0:T(8,128)(2,1)S(1)}, u32[]{:S(2)}) %copy-start.2) | copy-done | bytes 2949144
  38.7 1.6 %copy-done.4 = bf16[1280,1152]{1,0:T(8,128)(2,1)} copy-done((bf16[1280,1152]{1,0:T(8,128)(2,1)}, bf16[1280,1152]{1,0:T(8,128)(2,1)S(1)}, u32[]{:S(2)}) %copy-start.4) | copy-done | bytes 2949144
  40.4 0.1 merge.1.refs_1_
  40.5 0.6 collective-permute-start.12
  41.1 0.7 slice.8
  41.8 2.0 %collective-permute-start.13 = (bf16[640,128]{1,0:T(8,128)(2,1)}, bf16[640,128]{1,0:T(8,128)(2,1)}, u32[]{:S(2)}, u32[]{:S(2)}) collective-permute-start(bf16[640,128]{1,0:T(8,128)(2,1)} %slice.8), channel_id=1, source_target_pairs={{0,1},{2,3},{4,5},{6,7},{8,9},{10,11},{12,13},{14,15},{16,17},{18,... | collective-permute-start | bytes 491528 | tf_op jit(solution)/shard_map/ppermute | solution.py:444
  43.8 1.5 %collective-permute-start.11 = (bf16[640,128]{1,0:T(8,128)(2,1)}, bf16[640,128]{1,0:T(8,128)(2,1)S(1)}, u32[]{:S(2)}, u32[]{:S(2)}) collective-permute-start(bf16[640,128]{1,0:T(8,128)(2,1)} %slice.8), channel_id=1, source_target_pairs={{0,3},{2,1},{4,7},{6,5},{8,11},{10,9},{12,15},{14,13},{16,19},{18,... | collective-permute-start | bytes 491528 | tf_op jit(solution)/shard_map/ppermute | solution.py:444
  45.2 0.1 pad_add_fusion.where_ref
  45.3 1.8 %copy-done.1 = bf16[1280,1152]{1,0:T(8,128)(2,1)S(1)} copy-done((bf16[1280,1152]{1,0:T(8,128)(2,1)S(1)}, bf16[1280,1152]{1,0:T(8,128)(2,1)}, u32[]{:S(2)}) %copy-start.1) | copy-done | bytes 2949144
  47.2 1.8 %copy-done.3 = bf16[1280,1152]{1,0:T(8,128)(2,1)S(1)} copy-done((bf16[1280,1152]{1,0:T(8,128)(2,1)S(1)}, bf16[1280,1152]{1,0:T(8,128)(2,1)}, u32[]{:S(2)}) %copy-start.3) | copy-done | bytes 2949144
  49.0 1.8 %copy-done.5 = bf16[1280,1152]{1,0:T(8,128)(2,1)S(1)} copy-done((bf16[1280,1152]{1,0:T(8,128)(2,1)S(1)}, bf16[1280,1152]{1,0:T(8,128)(2,1)}, u32[]{:S(2)}) %copy-start.5) | copy-done | bytes 2949144
  50.8 3.4 %project_own.1 = (f32[2,272,1152]{2,1,0:T(8,128)S(1)}, f32[2,272,1152]{2,1,0:T(8,128)S(1)}) custom-call(s32[2]{0:T(128)S(1)} %pad_add_fusion.where_ref, bf16[640,128]{1,0:T(8,128)(2,1)} %collective-permute-done.13.refs_0_, bf16[640,256]{1,0:T(8,128)(2,1)S(1)} %merge.1.refs_1_, bf16[1280,1152]{1,0:T(8,128)(2,1)S(1)} %get-tuple-element.60.refs_2_, ...), custom_call_target="tpu_custom_call" | custom-call | tf_op jit(solution)/shard_map/project_own/pallas_call | solution.py:450
  54.3 0.0 copy-start.11
  54.3 4.2 %project_others.1 = (f32[2,272,1152]{2,1,0:T(8,128)S(1)}, f32[8,272]{1,0:T(8,128)S(1)}) custom-call(s32[2]{0:T(128)S(1)} %pad_add_fusion.where_ref, bf16[640,128]{1,0:T(8,128)(2,1)S(1)} %collective-permute-done.11.refs_0_, bf16[640,256]{1,0:T(8,128)(2,1)} %collective-permute-done.12.refs_1_, bf16[1280,1152]{1,0:T(8,128)(2,1)S(1)} %get-tuple-element.60.refs_2_, ...), custom_call_target="tpu_custom_call" | custom-call | tf_op jit(solution)/shard_map/project_others/pallas_call | solution.py:458
  58.5 1.5 %copy-done.6 = f32[2,272,1152]{2,1,0:T(8,128)} copy-done((f32[2,272,1152]{2,1,0:T(8,128)}, f32[2,272,1152]{2,1,0:T(8,128)S(1)}, u32[]{:S(2)}) %copy-start.6) | copy-done | bytes 2506776
  60.0 1.5 %collective-permute-start.14 = (f32[8,272]{1,0:T(8,128)S(1)}, f32[8,272]{1,0:T(8,128)S(1)}, u32[]{:S(2)}, u32[]{:S(2)}) collective-permute-start(f32[8,272]{1,0:T(8,128)S(1)} %get-tuple-element.67.refs_0_), channel_id=1, source_target_pairs={{0,2},{2,0},{1,3},{3,1},{4,6},{6,4},{5,7},{7,5},{8,10},{10,8},{9,1... | collective-permute-start | bytes 26120 | tf_op jit(solution)/shard_map/ppermute | solution.py:469
  61.5 1.7 %copy-done.7 = f32[2,272,1152]{2,1,0:T(8,128)S(1)} copy-done((f32[2,272,1152]{2,1,0:T(8,128)S(1)}, f32[2,272,1152]{2,1,0:T(8,128)}, u32[]{:S(2)}) %copy-start.7) | copy-done | bytes 2506776
  63.2 0.7 %prepare.1.refs_3_ = f32[3,2,256,1152]{3,2,1,0:T(8,128)S(1)} custom-call(f32[4,2304]{1,0:T(4,128)S(1)} %copy-done.11, f32[2,272,1152]{2,1,0:T(8,128)S(1)} %copy-done.7), custom_call_target="tpu_custom_call" | custom-call | tf_op jit(solution)/shard_map/prepare/pallas_call | solution.py:475
  64.0 1.0 %copy-done.8 = f32[2,272,1152]{2,1,0:T(8,128)S(1)} copy-done((f32[2,272,1152]{2,1,0:T(8,128)S(1)}, f32[2,272,1152]{2,1,0:T(8,128)}, u32[]{:S(2)}) %copy-start.8) | copy-done | bytes 2506776
  64.9 0.3 copy-done.10
  65.2 2.8 %finish.1 = bf16[256,2304]{1,0:T(8,128)(2,1)} custom-call(s32[1]{0:T(128)} %bitcast.keep_ref, f32[8,272]{1,0:T(8,128)S(1)} %get-tuple-element.67.refs_0_, f32[8,272]{1,0:T(8,128)S(1)} %collective-permute-done.14.refs_1_, f32[2,272,1152]{2,1,0:T(8,128)S(1)} %copy-done.8, f32[3,2,256,1152]{3,2,1,0:T(8,128)S(1)} %prepare.1.refs_3_, ...), custom_call_target="tpu_custom_call" | custom-call | tf_op jit(solution)/shard_map/finish/pallas_call | solution.py:483
  (25 shorter events, 0.1 us)
Async XLA Ops:
  0.0 14.6 %collective-permute-start.3 = (bf16[1280,1152]{1,0:T(8,128)(2,1)}, bf16[1280,1152]{1,0:T(8,128)(2,1)S(1)}, u32[]{:S(2)}, u32[]{:S(2)}) collective-permute-start(bf16[1280,1152]{1,0:T(8,128)(2,1)} %refs_0_), channel_id=1, source_target_pairs={{0,1},{1,0},{2,3},{3,2},{4,5},{5,4},{6,7},{7,6},{8,9},{9,8},{10,11... | collective-permute-start | bytes 8847368 | tf_op jit(solution)/shard_map/ppermute | solution.py:400
  0.0 14.7 %collective-permute-start.4 = (bf16[1280,1152]{1,0:T(8,128)(2,1)}, bf16[1280,1152]{1,0:T(8,128)(2,1)}, u32[]{:S(2)}, u32[]{:S(2)}) collective-permute-start(bf16[1280,1152]{1,0:T(8,128)(2,1)} %refs_1_), channel_id=1, source_target_pairs={{0,1},{1,0},{2,3},{3,2},{4,5},{5,4},{6,7},{7,6},{8,9},{9,8},{10,11... | collective-permute-start | bytes 8847368 | tf_op jit(solution)/shard_map/ppermute | solution.py:401
  1.9 5.6 %collective-permute-start.2 = (s32[8,256]{1,0:T(8,128)S(1)}, s32[8,256]{1,0:T(8,128)S(1)}, u32[]{:S(2)}, u32[]{:S(2)}) collective-permute-start(s32[8,256]{1,0:T(8,128)S(1)} %place_rows.1.ids_ref), channel_id=1, source_target_pairs={{0,4},{4,0},{8,12},{12,8},{1,5},{5,1},{9,13},{13,9},{2,6},{6,2},{1... | collective-permute-start | bytes 24584 | tf_op jit(solution)/shard_map/ppermute | solution.py:306
  3.5 4.5 %collective-permute-start.1 = (s32[8,256]{1,0:T(8,128)S(1)}, s32[8,256]{1,0:T(8,128)S(1)}, u32[]{:S(2)}, u32[]{:S(2)}) collective-permute-start(s32[8,256]{1,0:T(8,128)S(1)} %place_rows.1.ids_ref), channel_id=1, source_target_pairs={{0,8},{1,9},{4,13},{5,12},{8,1},{9,0},{12,4},{13,5},{2,10},{3,11},... | collective-permute-start | bytes 24584 | tf_op jit(solution)/shard_map/ppermute | solution.py:309
  3.5 4.5 %collective-permute-start = (s32[8,256]{1,0:T(8,128)S(1)}, s32[8,256]{1,0:T(8,128)S(1)}, u32[]{:S(2)}, u32[]{:S(2)}) collective-permute-start(s32[8,256]{1,0:T(8,128)S(1)} %place_rows.1.ids_ref), channel_id=1, source_target_pairs={{0,12},{4,8},{8,4},{12,0},{1,13},{5,9},{9,5},{13,1},{2,14},{6,10},... | collective-permute-start | bytes 24584 | tf_op jit(solution)/shard_map/ppermute | solution.py:306
  8.9 12.5 %collective-permute-start.9 = (bf16[640,256]{1,0:T(8,128)(2,1)S(1)}, bf16[640,256]{1,0:T(8,128)(2,1)S(1)}, u32[]{:S(2)}, u32[]{:S(2)}) collective-permute-start(bf16[640,256]{1,0:T(8,128)(2,1)S(1)} %pick_rows.4), channel_id=1, source_target_pairs={{0,4},{12,8},{1,5},{13,9},{2,6},{14,10},{3,7},{15,11},{16,20},{28,... | collective-permute-start | bytes 983048 | tf_op jit(solution)/shard_map/ppermute | solution.py:322
  10.2 19.5 %collective-permute-start.7 = (bf16[640,256]{1,0:T(8,128)(2,1)S(1)}, bf16[640,256]{1,0:T(8,128)(2,1)S(1)}, u32[]{:S(2)}, u32[]{:S(2)}) collective-permute-start(bf16[640,256]{1,0:T(8,128)(2,1)S(1)} %pick_rows.4), channel_id=1, source_target_pairs={{4,8},{8,4},{5,9},{9,5},{6,10},{10,6},{7,11},{11,7},{20,24},{24,20... | collective-permute-start | bytes 983048 | tf_op jit(solution)/shard_map/ppermute | solution.py:322
  13.3 27.0 %collective-permute-start.5 = (bf16[640,256]{1,0:T(8,128)(2,1)S(1)}, bf16[640,256]{1,0:T(8,128)(2,1)S(1)}, u32[]{:S(2)}, u32[]{:S(2)}) collective-permute-start(bf16[640,256]{1,0:T(8,128)(2,1)S(1)} %pick_rows.5), channel_id=1, source_target_pairs={{0,9},{1,8},{12,5},{13,4},{2,11},{3,10},{14,7},{15,6},{16,25},{17,... | collective-permute-start | bytes 983048 | tf_op jit(solution)/shard_map/ppermute | solution.py:309
  14.6 15.1 %copy-start.12 = (bf16[1280,1152]{1,0:T(8,128)(2,1)}, bf16[1280,1152]{1,0:T(8,128)(2,1)S(1)}, u32[]{:S(2)}) copy-start(bf16[1280,1152]{1,0:T(8,128)(2,1)S(1)} %collective-permute-done.3.refs_2_) | copy-start | bytes 8847364
  15.5 24.8 %collective-permute-start.6 = (bf16[640,256]{1,0:T(8,128)(2,1)S(1)}, bf16[640,256]{1,0:T(8,128)(2,1)S(1)}, u32[]{:S(2)}, u32[]{:S(2)}) collective-permute-start(bf16[640,256]{1,0:T(8,128)(2,1)S(1)} %pick_rows.6), channel_id=1, source_target_pairs={{0,4},{4,0},{8,12},{12,8},{1,5},{5,1},{9,13},{13,9},{2,6},{6,2},{1... | collective-permute-start | bytes 983048 | tf_op jit(solution)/shard_map/ppermute | solution.py:322
  21.5 18.9 %collective-permute-start.10 = (bf16[640,256]{1,0:T(8,128)(2,1)S(1)}, bf16[640,256]{1,0:T(8,128)(2,1)S(1)}, u32[]{:S(2)}, u32[]{:S(2)}) collective-permute-start(bf16[640,256]{1,0:T(8,128)(2,1)S(1)} %add.20), channel_id=1, source_target_pairs={{4,12},{8,0},{5,13},{9,1},{6,14},{10,2},{7,15},{11,3},{20,28},{24,... | collective-permute-start | bytes 983048 | tf_op jit(solution)/shard_map/ppermute | solution.py:322
  29.7 10.7 %collective-permute-start.8 = (bf16[16,2304]{1,0:T(8,128)(2,1)S(1)}, bf16[16,2304]{1,0:T(8,128)(2,1)S(1)}, u32[]{:S(2)}, u32[]{:S(2)}) collective-permute-start(bf16[16,2304]{1,0:T(8,128)(2,1)S(1)} %slice.6), channel_id=1, source_target_pairs={{0,1},{4,5},{8,9},{12,13},{2,3},{6,7},{10,11},{14,15},{16,17},{20,... | collective-permute-start | bytes 221192 | tf_op jit(solution)/shard_map/ppermute | solution.py:406
  35.5 1.6 %copy-start = (bf16[1280,1152]{1,0:T(8,128)(2,1)}, bf16[1280,1152]{1,0:T(8,128)(2,1)S(1)}, u32[]{:S(2)}) copy-start(bf16[1280,1152]{1,0:T(8,128)(2,1)S(1)} %get-tuple-element.61.refs_3_) | copy-start | bytes 8847364
  37.1 1.6 %copy-start.2 = (bf16[1280,1152]{1,0:T(8,128)(2,1)}, bf16[1280,1152]{1,0:T(8,128)(2,1)S(1)}, u32[]{:S(2)}) copy-start(bf16[1280,1152]{1,0:T(8,128)(2,1)S(1)} %get-tuple-element.62.refs_4_) | copy-start | bytes 8847364
  38.7 1.6 %copy-start.4 = (bf16[1280,1152]{1,0:T(8,128)(2,1)}, bf16[1280,1152]{1,0:T(8,128)(2,1)S(1)}, u32[]{:S(2)}) copy-start(bf16[1280,1152]{1,0:T(8,128)(2,1)S(1)} %get-tuple-element.63.refs_5_) | copy-start | bytes 8847364
  40.5 13.7 %collective-permute-start.12 = (bf16[640,256]{1,0:T(8,128)(2,1)S(1)}, bf16[640,256]{1,0:T(8,128)(2,1)}, u32[]{:S(2)}, u32[]{:S(2)}) collective-permute-start(bf16[640,256]{1,0:T(8,128)(2,1)S(1)} %merge.1.refs_1_), channel_id=1, source_target_pairs={{0,2},{2,0},{1,3},{3,1},{4,6},{6,4},{5,7},{7,5},{8,10},{10,8},{9,1... | collective-permute-start | bytes 983048 | tf_op jit(solution)/shard_map/ppermute | solution.py:431
  41.8 3.5 %collective-permute-start.13 = (bf16[640,128]{1,0:T(8,128)(2,1)}, bf16[640,128]{1,0:T(8,128)(2,1)}, u32[]{:S(2)}, u32[]{:S(2)}) collective-permute-start(bf16[640,128]{1,0:T(8,128)(2,1)} %slice.8), channel_id=1, source_target_pairs={{0,1},{2,3},{4,5},{6,7},{8,9},{10,11},{12,13},{14,15},{16,17},{18,... | collective-permute-start | bytes 491528 | tf_op jit(solution)/shard_map/ppermute | solution.py:444
  43.8 10.5 %collective-permute-start.11 = (bf16[640,128]{1,0:T(8,128)(2,1)}, bf16[640,128]{1,0:T(8,128)(2,1)S(1)}, u32[]{:S(2)}, u32[]{:S(2)}) collective-permute-start(bf16[640,128]{1,0:T(8,128)(2,1)} %slice.8), channel_id=1, source_target_pairs={{0,3},{2,1},{4,7},{6,5},{8,11},{10,9},{12,15},{14,13},{16,19},{18,... | collective-permute-start | bytes 491528 | tf_op jit(solution)/shard_map/ppermute | solution.py:444
  45.3 1.8 %copy-start.1 = (bf16[1280,1152]{1,0:T(8,128)(2,1)S(1)}, bf16[1280,1152]{1,0:T(8,128)(2,1)}, u32[]{:S(2)}) copy-start(bf16[1280,1152]{1,0:T(8,128)(2,1)} %copy-done) | copy-start | bytes 8847364
  47.2 1.8 %copy-start.3 = (bf16[1280,1152]{1,0:T(8,128)(2,1)S(1)}, bf16[1280,1152]{1,0:T(8,128)(2,1)}, u32[]{:S(2)}) copy-start(bf16[1280,1152]{1,0:T(8,128)(2,1)} %copy-done.2) | copy-start | bytes 8847364
  49.0 1.8 %copy-start.5 = (bf16[1280,1152]{1,0:T(8,128)(2,1)S(1)}, bf16[1280,1152]{1,0:T(8,128)(2,1)}, u32[]{:S(2)}) copy-start(bf16[1280,1152]{1,0:T(8,128)(2,1)} %copy-done.4) | copy-start | bytes 8847364
  50.8 3.5 %copy-start.9 = (bf16[256,2304]{1,0:T(8,128)(2,1)S(1)}, bf16[256,2304]{1,0:T(8,128)(2,1)}, u32[]{:S(2)}) copy-start(bf16[256,2304]{1,0:T(8,128)(2,1)} %refs_4_.1) | copy-start | bytes 3538948
  54.3 7.2 %copy-start.11 = (f32[4,2304]{1,0:T(4,128)S(1)}, f32[4,2304]{1,0:T(4,128)}, u32[]{:S(2)}) copy-start(f32[4,2304]{1,0:T(4,128)} %refs_5_.1) | copy-start | bytes 110596
  58.5 1.5 %copy-start.6 = (f32[2,272,1152]{2,1,0:T(8,128)}, f32[2,272,1152]{2,1,0:T(8,128)S(1)}, u32[]{:S(2)}) copy-start(f32[2,272,1152]{2,1,0:T(8,128)S(1)} %get-tuple-element.68.rows_ref.refs_2_) | copy-start | bytes 7520260
  60.0 3.9 %collective-permute-start.14 = (f32[8,272]{1,0:T(8,128)S(1)}, f32[8,272]{1,0:T(8,128)S(1)}, u32[]{:S(2)}, u32[]{:S(2)}) collective-permute-start(f32[8,272]{1,0:T(8,128)S(1)} %get-tuple-element.67.refs_0_), channel_id=1, source_target_pairs={{0,2},{2,0},{1,3},{3,1},{4,6},{6,4},{5,7},{7,5},{8,10},{10,8},{9,1... | collective-permute-start | bytes 26120 | tf_op jit(solution)/shard_map/ppermute | solution.py:469
  61.5 1.7 %copy-start.7 = (f32[2,272,1152]{2,1,0:T(8,128)S(1)}, f32[2,272,1152]{2,1,0:T(8,128)}, u32[]{:S(2)}) copy-start(f32[2,272,1152]{2,1,0:T(8,128)} %copy-done.6) | copy-start | bytes 7520260
  63.2 1.7 %copy-start.8 = (f32[2,272,1152]{2,1,0:T(8,128)S(1)}, f32[2,272,1152]{2,1,0:T(8,128)}, u32[]{:S(2)}) copy-start(f32[2,272,1152]{2,1,0:T(8,128)} %copy-done.6) | copy-start | bytes 7520260
  63.2 2.0 %copy-start.10 = (bf16[256,2304]{1,0:T(8,128)(2,1)S(1)}, bf16[256,2304]{1,0:T(8,128)(2,1)}, u32[]{:S(2)}) copy-start(bf16[256,2304]{1,0:T(8,128)(2,1)} %refs_4_.1) | copy-start | bytes 3538948

commit v17 on v15

--- a/solution.py
+++ b/solution.py
@@ -42,11 +42,18 @@
     return x.astype(F32).astype(BF16)
 
 
-def place_kernel(ids_hbm, place_hbm, out_ref, ids_ref, place_ref, sems):
+def place_kernel(
+    ids_hbm, place_hbm, codes_hbm, scales_hbm, out_ref, codes_ref, scales_ref, ids_ref, place_ref, sems
+):
     copies = [
         pltpu.make_async_copy(place_hbm, place_ref, sems.at[0]),
         pltpu.make_async_copy(ids_hbm, ids_ref, sems.at[1]),
+        pltpu.make_async_copy(scales_hbm, scales_ref, sems.at[2]),
     ]
+    for n in range(codes_ref.shape[0]):
+        copies.append(
+            pltpu.make_async_copy(codes_hbm.at[n], codes_ref.at[n], sems.at[3 + n])
+        )
     for copy in copies:
         copy.start()
     copies[0].wait()
@@ -65,19 +72,13 @@
         value = both[:LANES] * 256.0 + both[LANES:]
         chosen = jnp.where(iota(value.shape, 0) == (row & 127), value, 0.0)
         out_ref[head : head + 1, :] = jnp.sum(chosen, axis=0, keepdims=True).astype(I32)
-
-
-def decode_kernel(codes_hbm, scales_hbm, out_ref, codes_ref, scales_ref, sems):
+    for copy in copies[2:]:
+        copy.wait()
+
+
+def decode_kernel(codes_ref, scales_ref, out_ref):
     heads, width, rows = codes_ref.shape
     blocks = scales_ref.shape[0]
-    scales_copy = pltpu.make_async_copy(scales_hbm, scales_ref, sems.at[heads])
-    scales_copy.start()
-    copies = []
-    for head in range(heads):
-        copies.append(
-            pltpu.make_async_copy(codes_hbm.at[head], codes_ref.at[head], sems.at[head])
-        )
-        copies[-1].start()
     entry = iota((width, 2 * width), 0)
     column = iota((width, 2 * width), 1)
     column = jnp.where(column < width, column, column - width)
@@ -86,9 +87,7 @@
     parity = (parity ^ (parity >> 1)) & 1
     same = (entry >> 4) == (column >> 4)
     rotation = jnp.where(same, 0.25 - 0.5 * parity.astype(F32), 0.0).astype(BF16)
-    scales_copy.wait()
     for head in range(heads):
-        copies[head].wait()
         factors = jnp.concatenate(
             [
                 jnp.broadcast_to(scales_ref[b, head : head + 1, :].astype(F32), (16, rows))
@@ -136,28 +135,34 @@
         key_ref, value_ref, rest, held, sems, rest_sems = refs[4:]
         half = held.shape[-1]
 
+        split = sems.shape[-1]
+        size = depth // split
+
         def bring(target, far, which, n, s, sem):
             owner = lax.rem(tp + count - s, count)
-            rows = pl.ds(pl.multiple_of(owner * depth, depth), depth)
-            copy = pltpu.make_async_copy(
-                weights[2 * far + which].at[rows, :],
-                target.at[far, which, pl.ds(n * depth, depth), :],
-                sem,
-            )
-            copy.start()
-            return copy
+            copies = []
+            for k in range(split):
+                rows = pl.ds(pl.multiple_of(owner * depth + k * size, size), size)
+                copy = pltpu.make_async_copy(
+                    weights[2 * far + which].at[rows, :],
+                    target.at[far, which, pl.ds(n * depth + k * size, size), :],
+                    sem.at[k],
+                )
+                copy.start()
+                copies.append(copy)
+            return copies
 
         copies = [
             bring(held, far, which, 0, 0, sems.at[2 * far + which])
             for far in range(2)
             for which in (1, 0)
         ]
-        later = [
-            bring(rest, far, which, n, n + 1, rest_sems.at[(2 * far + which) * (count - 1) + n])
-            for far in range(2)
-            for which in (1, 0)
-            for n in range(count - 1)
-        ]
+        later = []
+        for far in range(2):
+            for which in (1, 0):
+                for n in range(count - 1):
+                    sem = rest_sems.at[(2 * far + which) * (count - 1) + n]
+                    later += bring(rest, far, which, n, n + 1, sem)
     else:
         later = []
         rest, begun_keys, begun_values, hidden_halo, hidden = refs[:5]
@@ -176,7 +181,8 @@
         fields = [None, None]
         for which in (1, 0):
             if first:
-                copies[2 * far + 1 - which].wait()
+                for copy in copies[2 * far + 1 - which]:
+                    copy.wait()
             fields[which] = dot(memory, held[far, which])
             if not first and which == 1:
                 done[far] = fields[1] + begun_values[slot]
@@ -389,32 +395,33 @@
     anywhere = pl.BlockSpec(memory_space=pl.ANY)
     resident = pl.BlockSpec(memory_space=pltpu.VMEM)
     places = row_place.reshape(-1, LANES)
-    stored = pl.pallas_call(
+    codes = table_codes.transpose(0, 2, 1)
+    scales = table_scales.transpose(2, 0, 1)
+    stored, codes, scales = pl.pallas_call(
         place_kernel,
-        in_specs=[anywhere] * 2,
-        out_shape=jax.ShapeDtypeStruct((heads, tokens), I32),
+        in_specs=[anywhere] * 4,
+        out_specs=(resident,) * 3,
+        out_shape=(
+            jax.ShapeDtypeStruct((heads, tokens), I32),
+            jax.ShapeDtypeStruct(codes.shape, BF16),
+            jax.ShapeDtypeStruct(scales.shape, BF16),
+        ),
         scratch_shapes=[
             pltpu.VMEM((heads, tokens), I32),
             pltpu.VMEM(places.shape, I32),
-            pltpu.SemaphoreType.DMA((2,)),
+            pltpu.SemaphoreType.DMA((heads + 3,)),
         ],
         compiler_params=limit(4),
         name="place_rows",
-    )(in_hbm(row_ids.T), in_hbm(places))
-    codes = table_codes.transpose(0, 2, 1)
-    scales = table_scales.transpose(2, 0, 1)
+    )(*[in_hbm(x) for x in (row_ids.T, places, codes, scales)])
     decoded = pl.pallas_call(
         decode_kernel,
-        in_specs=[anywhere] * 2,
+        in_specs=[resident] * 2,
+        out_specs=resident,
         out_shape=jax.ShapeDtypeStruct(codes.shape, BF16),
-        scratch_shapes=[
-            pltpu.VMEM(codes.shape, BF16),
-            pltpu.VMEM(scales.shape, BF16),
-            pltpu.SemaphoreType.DMA((heads + 1,)),
-        ],
-        compiler_params=limit(12),
+        compiler_params=limit(6),
         name="decode_tables",
-    )(in_hbm(after(codes, stored)), in_hbm(scales))
+    )(codes, scales)
     here = lax.axis_index("mem")
     other_key = lax.ppermute(key_weight, "rep", [(0, 1), (1, 0)])
     other_value = lax.ppermute(value_weight, "rep", [(0, 1), (1, 0)])
@@ -459,8 +466,8 @@
         out_shape=(field, field, pltpu.VMEM((2, 2, others * depth, half), BF16)),
         scratch_shapes=[
             pltpu.VMEM((2, 2, depth, half), BF16),
-            pltpu.SemaphoreType.DMA((4,)),
-            pltpu.SemaphoreType.DMA((4 * others,)),
+            pltpu.SemaphoreType.DMA((4, 4)),
+            pltpu.SemaphoreType.DMA((4 * others, 4)),
         ],
         compiler_params=limit(12),
         name="project_own",

time: 60.9 us -> 61.2 us (level)
  waiting for transfers between devices: 14.4 us -> 16.4 us
  Pallas kernels: 22.3 us -> 21 us
    pallas_call x2, Pallas kernels: 4.07 us -> 2.38 us  [the longest x1 1.51 us: shards(): pl.pallas_call(place_kernel, in_specs=[anywhere] * 4, out_specs=(resident...]
    ppermute x4, waiting for transfers between devices: 10.2 us -> 11.3 us  [send(): return lax.ppermute(x, 'mem', pairs)]
  transfers between devices with their start and end apart: 15 -> 15, of which waited for: 5 -> 6; matrix products, arithmetic and copies ran while one was open for 0% -> 0% of each run, Pallas kernels for 25% -> 23%
where the time goes in v17:
time: 61.2 us; the launch traced here: 60.9 us
  starting transfers between devices  22.9 us (37%)
  Pallas kernels  21 us (34%)
  waiting for transfers between devices  16.4 us (27%)
    ppermute x4, waiting for transfers between devices, send(): return lax.ppermute(x, 'mem', pairs)  11.3 us
    pallas_call x1, Pallas kernels, shards(): pl.pallas_call(functools.partial(project_kernel, (0,), tps), in_specs=[sm...  6.02 us
    ppermute x2, starting transfers between devices, ask(): return lax.ppermute(ids, 'mem', [(i, i ^ x) for i in range(4)])  5.35 us
    ppermute x4, starting transfers between devices, send(): return lax.ppermute(x, 'mem', pairs)  4.77 us
    pallas_call x1, Pallas kernels, shards(): pl.pallas_call(functools.partial(project_kernel, tuple(range(1, tps)), tp...  4.25 us
    ppermute x2, waiting for transfers between devices, crossing(): lax.ppermute(x, ('mem', 'rep'), [(2 * a + b, 2 * c + d) for a, b, c, d in...  4.23 us
    ppermute x2, starting transfers between devices, crossing(): lax.ppermute(x, ('mem', 'rep'), [(2 * a + b, 2 * c + d) for a, b, c, d in...  3.71 us
    pallas_call x4, Pallas kernels, pick(): pl.pallas_call(pick_kernel, in_specs=[pl.BlockSpec(memory_space=pltpu.SME...  3.46 us
  transfers between devices with their start and end apart: 15, of which 6 were waited for; matrix products, arithmetic and copies ran while one was open for 0% of the time, Pallas kernels for 23%

profile of v17, /device:TPU:0, one launch (start us, length us, event | category | flops | bytes accessed | tf_op | source)
XLA Modules:
  0.0 60.9 jit_solution(2560489875845254327)
XLA Ops:
  0.0 0.5 collective-permute-start.3
  0.5 0.1 collective-permute-start.4
  0.5 1.5 %place_rows.1 = (s32[8,256]{1,0:T(8,128)S(1)}, bf16[8,80,1024]{2,1,0:T(8,128)(2,1)S(1)}, bf16[5,8,1024]{2,1,0:T(8,128)(2,1)S(1)}) custom-call(s32[8,256]{1,0:T(8,128)} %bitcast.11, s32[32,128]{1,0:T(8,128)} %bitcast.10, bf16[8,80,1024]{2,1,0:T(8,128)(2,1)} %bitcast.8, bf16[5,8,1024]{2,1,0:T(8,128)(2,1)} %bitcast.9), custom_call_target="tpu_custom_call" | custom-call | tf_op jit(solution)/shard_map/place_rows/pallas_call | solution.py:400
  2.0 5.1 %collective-permute-start = (s32[8,256]{1,0:T(8,128)S(1)}, s32[8,256]{1,0:T(8,128)S(1)}, u32[]{:S(2)}, u32[]{:S(2)}) collective-permute-start(s32[8,256]{1,0:T(8,128)S(1)} %get-tuple-element.37.ids_ref), channel_id=1, source_target_pairs={{0,12},{4,8},{8,4},{12,0},{1,13},{5,9},{9,5},{13,1},{2,14},{6,10},... | collective-permute-start | bytes 24584 | tf_op jit(solution)/shard_map/ppermute | solution.py:331
  7.1 0.0 collective-permute-start.1
  7.2 0.2 collective-permute-start.2
  7.4 0.9 %decode_tables.1.table_ref = bf16[8,80,1024]{2,1,0:T(8,128)(2,1)S(1)} custom-call(bf16[8,80,1024]{2,1,0:T(8,128)(2,1)S(1)} %get-tuple-element.32.codes_ref, bf16[5,8,1024]{2,1,0:T(8,128)(2,1)S(1)} %get-tuple-element.33.scales_ref), custom_call_target="tpu_custom_call" | custom-call | tf_op jit(solution)/shard_map/decode_tables/pallas_call | solution.py:417
  8.3 0.5 collective-permute-done.ids_ref
  8.8 2.3 %collective-permute-done.1.ids_ref = s32[8,256]{1,0:T(8,128)S(1)} collective-permute-done((s32[8,256]{1,0:T(8,128)S(1)}, s32[8,256]{1,0:T(8,128)S(1)}, u32[]{:S(2)}, u32[]{:S(2)}) %collective-permute-start.1) | collective-permute-done | bytes 8224 | tf_op jit(solution)/shard_map/ppermute | solution.py:334
  11.1 0.0 collective-permute-done.2.ids_ref
  11.1 0.9 %pick_rows.4 = bf16[640,256]{1,0:T(8,128)(2,1)S(1)} custom-call(s32[1]{0:T(128)} %bitcast.3.base_ref, s32[8,256]{1,0:T(8,128)S(1)} %collective-permute-done.ids_ref, bf16[8,80,1024]{2,1,0:T(8,128)(2,1)S(1)} %decode_tables.1.table_ref), custom_call_target="tpu_custom_call" | custom-call | tf_op jit(solution)/shard_map/pick_rows/pallas_call | solution.py:337
  12.0 2.0 %collective-permute-start.9 = (bf16[640,256]{1,0:T(8,128)(2,1)S(1)}, bf16[640,256]{1,0:T(8,128)(2,1)S(1)}, u32[]{:S(2)}, u32[]{:S(2)}) collective-permute-start(bf16[640,256]{1,0:T(8,128)(2,1)S(1)} %pick_rows.4), channel_id=1, source_target_pairs={{0,4},{12,8},{1,5},{13,9},{2,6},{14,10},{3,7},{15,11},{16,20},{28,... | collective-permute-start | bytes 983048 | tf_op jit(solution)/shard_map/ppermute | solution.py:347
  14.0 0.7 %collective-permute-start.7 = (bf16[640,256]{1,0:T(8,128)(2,1)S(1)}, bf16[640,256]{1,0:T(8,128)(2,1)S(1)}, u32[]{:S(2)}, u32[]{:S(2)}) collective-permute-start(bf16[640,256]{1,0:T(8,128)(2,1)S(1)} %pick_rows.4), channel_id=1, source_target_pairs={{4,8},{8,4},{5,9},{9,5},{6,10},{10,6},{7,11},{11,7},{20,24},{24,20... | collective-permute-start | bytes 983048 | tf_op jit(solution)/shard_map/ppermute | solution.py:347
  14.7 0.9 %pick_rows.5 = bf16[640,256]{1,0:T(8,128)(2,1)S(1)} custom-call(s32[1]{0:T(128)} %bitcast.3.base_ref, s32[8,256]{1,0:T(8,128)S(1)} %collective-permute-done.1.ids_ref, bf16[8,80,1024]{2,1,0:T(8,128)(2,1)S(1)} %decode_tables.1.table_ref), custom_call_target="tpu_custom_call" | custom-call | tf_op jit(solution)/shard_map/pick_rows/pallas_call | solution.py:337
  15.6 0.0 copy-start
  15.6 3.7 %collective-permute-start.5 = (bf16[640,256]{1,0:T(8,128)(2,1)S(1)}, bf16[640,256]{1,0:T(8,128)(2,1)S(1)}, u32[]{:S(2)}, u32[]{:S(2)}) collective-permute-start(bf16[640,256]{1,0:T(8,128)(2,1)S(1)} %pick_rows.5), channel_id=1, source_target_pairs={{0,9},{1,8},{12,5},{13,4},{2,11},{3,10},{14,7},{15,6},{16,25},{17,... | collective-permute-start | bytes 983048 | tf_op jit(solution)/shard_map/ppermute | solution.py:334
  19.3 0.0 collective-permute-done.3.refs_4_
  19.3 0.0 collective-permute-done.4.refs_5_
  19.3 0.9 %pick_rows.6 = bf16[640,256]{1,0:T(8,128)(2,1)S(1)} custom-call(s32[1]{0:T(128)} %bitcast.3.base_ref, s32[8,256]{1,0:T(8,128)S(1)} %collective-permute-done.2.ids_ref, bf16[8,80,1024]{2,1,0:T(8,128)(2,1)S(1)} %decode_tables.1.table_ref), custom_call_target="tpu_custom_call" | custom-call | tf_op jit(solution)/shard_map/pick_rows/pallas_call | solution.py:337
  20.2 0.7 %collective-permute-start.6 = (bf16[640,256]{1,0:T(8,128)(2,1)S(1)}, bf16[640,256]{1,0:T(8,128)(2,1)S(1)}, u32[]{:S(2)}, u32[]{:S(2)}) collective-permute-start(bf16[640,256]{1,0:T(8,128)(2,1)S(1)} %pick_rows.6), channel_id=1, source_target_pairs={{0,4},{4,0},{8,12},{12,8},{1,5},{5,1},{9,13},{13,9},{2,6},{6,2},{1... | collective-permute-start | bytes 983048 | tf_op jit(solution)/shard_map/ppermute | solution.py:347
  21.0 0.9 %pick_rows.7 = bf16[640,256]{1,0:T(8,128)(2,1)S(1)} custom-call(s32[1]{0:T(128)} %bitcast.3.base_ref, s32[8,256]{1,0:T(8,128)S(1)} %get-tuple-element.37.ids_ref, bf16[8,80,1024]{2,1,0:T(8,128)(2,1)S(1)} %decode_tables.1.table_ref), custom_call_target="tpu_custom_call" | custom-call | tf_op jit(solution)/shard_map/pick_rows/pallas_call | solution.py:337
  21.8 0.0 collective-permute-done.9
  21.8 0.1 add.20
  21.9 1.3 %collective-permute-start.10 = (bf16[640,256]{1,0:T(8,128)(2,1)S(1)}, bf16[640,256]{1,0:T(8,128)(2,1)S(1)}, u32[]{:S(2)}, u32[]{:S(2)}) collective-permute-start(bf16[640,256]{1,0:T(8,128)(2,1)S(1)} %add.20), channel_id=1, source_target_pairs={{4,12},{8,0},{5,13},{9,1},{6,14},{10,2},{7,15},{11,3},{20,28},{24,... | collective-permute-start | bytes 983048 | tf_op jit(solution)/shard_map/ppermute | solution.py:347
  23.2 0.0 copy-done
  23.2 0.0 collective-permute-done.7.refs_1_
  23.3 2.1 %collective-permute-start.8 = (bf16[16,2304]{1,0:T(8,128)(2,1)S(1)}, bf16[16,2304]{1,0:T(8,128)(2,1)S(1)}, u32[]{:S(2)}, u32[]{:S(2)}) collective-permute-start(bf16[16,2304]{1,0:T(8,128)(2,1)S(1)} %slice.6), channel_id=1, source_target_pairs={{0,1},{4,5},{8,9},{12,13},{2,3},{6,7},{10,11},{14,15},{16,17},{20,... | collective-permute-start | bytes 221192 | tf_op jit(solution)/shard_map/ppermute | solution.py:432
  25.4 1.9 %collective-permute-done.5 = bf16[640,256]{1,0:T(8,128)(2,1)S(1)} collective-permute-done((bf16[640,256]{1,0:T(8,128)(2,1)S(1)}, bf16[640,256]{1,0:T(8,128)(2,1)S(1)}, u32[]{:S(2)}, u32[]{:S(2)}) %collective-permute-start.5) | collective-permute-done | bytes 327712 | tf_op jit(solution)/shard_map/ppermute | solution.py:334
  27.3 7.0 %collective-permute-done.6 = bf16[640,256]{1,0:T(8,128)(2,1)S(1)} collective-permute-done((bf16[640,256]{1,0:T(8,128)(2,1)S(1)}, bf16[640,256]{1,0:T(8,128)(2,1)S(1)}, u32[]{:S(2)}, u32[]{:S(2)}) %collective-permute-start.6) | collective-permute-done | bytes 327712 | tf_op jit(solution)/shard_map/ppermute | solution.py:347
  34.3 0.0 collective-permute-done.8.refs_5_
  34.3 4.3 %collective-permute-done.10.refs_2_ = bf16[640,256]{1,0:T(8,128)(2,1)S(1)} collective-permute-done((bf16[640,256]{1,0:T(8,128)(2,1)S(1)}, bf16[640,256]{1,0:T(8,128)(2,1)S(1)}, u32[]{:S(2)}, u32[]{:S(2)}) %collective-permute-start.10) | collective-permute-done | bytes 327712 | tf_op jit(solution)/shard_map/ppermute | solution.py:347
  38.6 0.1 merge.1.refs_1_
  38.8 1.6 %collective-permute-start.12 = (bf16[640,256]{1,0:T(8,128)(2,1)S(1)}, bf16[640,256]{1,0:T(8,128)(2,1)S(1)}, u32[]{:S(2)}, u32[]{:S(2)}) collective-permute-start(bf16[640,256]{1,0:T(8,128)(2,1)S(1)} %merge.1.refs_1_), channel_id=1, source_target_pairs={{0,2},{2,0},{1,3},{3,1},{4,6},{6,4},{5,7},{7,5},{8,10},{10,8},{9,1... | collective-permute-start | bytes 983048 | tf_op jit(solution)/shard_map/ppermute | solution.py:443
  40.3 1.7 %collective-permute-start.13 = (bf16[640,128]{1,0:T(8,128)(2,1)S(1)}, bf16[640,128]{1,0:T(8,128)(2,1)S(1)}, u32[]{:S(2)}, u32[]{:S(2)}) collective-permute-start(bf16[640,128]{1,0:T(8,128)(2,1)S(1)} %slice.8), channel_id=1, source_target_pairs={{0,1},{2,3},{4,5},{6,7},{8,9},{10,11},{12,13},{14,15},{16,17},{18,... | collective-permute-start | bytes 491528 | tf_op jit(solution)/shard_map/ppermute | solution.py:456
  42.1 1.6 %collective-permute-start.11 = (bf16[640,128]{1,0:T(8,128)(2,1)S(1)}, bf16[640,128]{1,0:T(8,128)(2,1)S(1)}, u32[]{:S(2)}, u32[]{:S(2)}) collective-permute-start(bf16[640,128]{1,0:T(8,128)(2,1)S(1)} %slice.8), channel_id=1, source_target_pairs={{0,3},{2,1},{4,7},{6,5},{8,11},{10,9},{12,15},{14,13},{16,19},{18,... | collective-permute-start | bytes 491528 | tf_op jit(solution)/shard_map/ppermute | solution.py:456
  43.7 0.1 pad_add_fusion.where_ref
  43.8 0.0 collective-permute-done.13.refs_0_
  43.8 6.0 %project_own.1 = (f32[2,272,1152]{2,1,0:T(8,128)S(1)}, f32[2,272,1152]{2,1,0:T(8,128)S(1)}, bf16[2,2,640,1152]{3,2,1,0:T(8,128)(2,1)S(1)}) custom-call(s32[2]{0:T(128)S(1)} %pad_add_fusion.where_ref, bf16[640,128]{1,0:T(8,128)(2,1)S(1)} %collective-permute-done.13.refs_0_, bf16[640,256]{1,0:T(8,128)(2,1)S(1)} %merge.1.refs_1_, bf16[1280,1152]{1,0:T(8,128)(2,1)} %refs_2_.1, ...), custom_call_target="tpu_custom_call" | custom-call | tf_op jit(solution)/shard_map/project_own/pallas_call | solution.py:462
  49.8 0.0 collective-permute-done.11.refs_0_
  49.8 0.0 collective-permute-done.12.refs_1_
  49.8 0.0 copy-start.1
  49.9 4.3 %project_others.1 = (f32[2,272,1152]{2,1,0:T(8,128)}, f32[8,272]{1,0:T(8,128)S(1)}) custom-call(s32[2]{0:T(128)S(1)} %pad_add_fusion.where_ref, bf16[640,128]{1,0:T(8,128)(2,1)S(1)} %collective-permute-done.11.refs_0_, bf16[640,256]{1,0:T(8,128)(2,1)S(1)} %collective-permute-done.12.refs_1_, bf16[2,2,640,1152]{3,2,1,0:T(8,128)(2,1)S(1)} %get-tuple-element.43.refs_2_, ...), custom_call_target="tpu_custom_call" | custom-call | tf_op jit(solution)/shard_map/project_others/pallas_call | solution.py:475
  54.1 1.5 %collective-permute-start.14 = (f32[8,272]{1,0:T(8,128)S(1)}, f32[8,272]{1,0:T(8,128)S(1)}, u32[]{:S(2)}, u32[]{:S(2)}) collective-permute-start(f32[8,272]{1,0:T(8,128)S(1)} %get-tuple-element.47.refs_0_), channel_id=1, source_target_pairs={{0,2},{2,0},{1,3},{3,1},{4,6},{6,4},{5,7},{7,5},{8,10},{10,8},{9,1... | collective-permute-start | bytes 26120 | tf_op jit(solution)/shard_map/ppermute | solution.py:498
  55.7 0.0 copy-done.1
  55.7 1.9 %prepare.1 = (f32[2,256,1152]{2,1,0:T(8,128)S(1)}, f32[3,2,256,1152]{3,2,1,0:T(8,128)S(1)}) custom-call(f32[4,2304]{1,0:T(4,128)S(1)} %copy-done.1, f32[2,272,1152]{2,1,0:T(8,128)} %get-tuple-element.48.value_hbm), custom_call_target="tpu_custom_call" | custom-call | tf_op jit(solution)/shard_map/prepare/pallas_call | solution.py:506
  57.6 0.3 collective-permute-done.14.refs_1_
  57.9 2.8 %finish.1 = bf16[256,2304]{1,0:T(8,128)(2,1)} custom-call(s32[1]{0:T(128)} %bitcast.keep_ref, f32[8,272]{1,0:T(8,128)S(1)} %get-tuple-element.47.refs_0_, f32[8,272]{1,0:T(8,128)S(1)} %collective-permute-done.14.refs_1_, f32[2,256,1152]{2,1,0:T(8,128)S(1)} %get-tuple-element.49.refs_2_, f32[3,2,256,1152]{3,2,1,0:T(8,128)S(1)} %get-tuple-element.50.refs_3_, ...), custom_call_target="tpu_custom_call" | custom-call | tf_op jit(solution)/shard_map/finish/pallas_call | solution.py:521
  (3 shorter events, 0.1 us)
Async XLA Ops:
  0.0 19.3 %collective-permute-start.3 = (bf16[1280,1152]{1,0:T(8,128)(2,1)}, bf16[1280,1152]{1,0:T(8,128)(2,1)}, u32[]{:S(2)}, u32[]{:S(2)}) collective-permute-start(bf16[1280,1152]{1,0:T(8,128)(2,1)} %refs_2_.1), channel_id=1, source_target_pairs={{0,1},{1,0},{2,3},{3,2},{4,5},{5,4},{6,7},{7,6},{8,9},{9,8},{10,11... | collective-permute-start | bytes 8847368 | tf_op jit(solution)/shard_map/ppermute | solution.py:426
  0.5 18.9 %collective-permute-start.4 = (bf16[1280,1152]{1,0:T(8,128)(2,1)}, bf16[1280,1152]{1,0:T(8,128)(2,1)}, u32[]{:S(2)}, u32[]{:S(2)}) collective-permute-start(bf16[1280,1152]{1,0:T(8,128)(2,1)} %refs_3_.1), channel_id=1, source_target_pairs={{0,1},{1,0},{2,3},{3,2},{4,5},{5,4},{6,7},{7,6},{8,9},{9,8},{10,11... | collective-permute-start | bytes 8847368 | tf_op jit(solution)/shard_map/ppermute | solution.py:427
  2.0 6.7 %collective-permute-start = (s32[8,256]{1,0:T(8,128)S(1)}, s32[8,256]{1,0:T(8,128)S(1)}, u32[]{:S(2)}, u32[]{:S(2)}) collective-permute-start(s32[8,256]{1,0:T(8,128)S(1)} %get-tuple-element.37.ids_ref), channel_id=1, source_target_pairs={{0,12},{4,8},{8,4},{12,0},{1,13},{5,9},{9,5},{13,1},{2,14},{6,10},... | collective-permute-start | bytes 24584 | tf_op jit(solution)/shard_map/ppermute | solution.py:331
  7.1 4.0 %collective-permute-start.1 = (s32[8,256]{1,0:T(8,128)S(1)}, s32[8,256]{1,0:T(8,128)S(1)}, u32[]{:S(2)}, u32[]{:S(2)}) collective-permute-start(s32[8,256]{1,0:T(8,128)S(1)} %get-tuple-element.37.ids_ref), channel_id=1, source_target_pairs={{0,8},{1,9},{4,13},{5,12},{8,1},{9,0},{12,4},{13,5},{2,10},{3,11},... | collective-permute-start | bytes 24584 | tf_op jit(solution)/shard_map/ppermute | solution.py:334
  7.2 4.0 %collective-permute-start.2 = (s32[8,256]{1,0:T(8,128)S(1)}, s32[8,256]{1,0:T(8,128)S(1)}, u32[]{:S(2)}, u32[]{:S(2)}) collective-permute-start(s32[8,256]{1,0:T(8,128)S(1)} %get-tuple-element.37.ids_ref), channel_id=1, source_target_pairs={{0,4},{4,0},{8,12},{12,8},{1,5},{5,1},{9,13},{13,9},{2,6},{6,2},{1... | collective-permute-start | bytes 24584 | tf_op jit(solution)/shard_map/ppermute | solution.py:331
  12.0 9.8 %collective-permute-start.9 = (bf16[640,256]{1,0:T(8,128)(2,1)S(1)}, bf16[640,256]{1,0:T(8,128)(2,1)S(1)}, u32[]{:S(2)}, u32[]{:S(2)}) collective-permute-start(bf16[640,256]{1,0:T(8,128)(2,1)S(1)} %pick_rows.4), channel_id=1, source_target_pairs={{0,4},{12,8},{1,5},{13,9},{2,6},{14,10},{3,7},{15,11},{16,20},{28,... | collective-permute-start | bytes 983048 | tf_op jit(solution)/shard_map/ppermute | solution.py:347
  14.0 9.2 %collective-permute-start.7 = (bf16[640,256]{1,0:T(8,128)(2,1)S(1)}, bf16[640,256]{1,0:T(8,128)(2,1)S(1)}, u32[]{:S(2)}, u32[]{:S(2)}) collective-permute-start(bf16[640,256]{1,0:T(8,128)(2,1)S(1)} %pick_rows.4), channel_id=1, source_target_pairs={{4,8},{8,4},{5,9},{9,5},{6,10},{10,6},{7,11},{11,7},{20,24},{24,20... | collective-permute-start | bytes 983048 | tf_op jit(solution)/shard_map/ppermute | solution.py:347
  15.6 7.6 %copy-start = (bf16[256,2304]{1,0:T(8,128)(2,1)S(1)}, bf16[256,2304]{1,0:T(8,128)(2,1)}, u32[]{:S(2)}) copy-start(bf16[256,2304]{1,0:T(8,128)(2,1)} %refs_4_.1) | copy-start | bytes 3538948
  15.6 11.6 %collective-permute-start.5 = (bf16[640,256]{1,0:T(8,128)(2,1)S(1)}, bf16[640,256]{1,0:T(8,128)(2,1)S(1)}, u32[]{:S(2)}, u32[]{:S(2)}) collective-permute-start(bf16[640,256]{1,0:T(8,128)(2,1)S(1)} %pick_rows.5), channel_id=1, source_target_pairs={{0,9},{1,8},{12,5},{13,4},{2,11},{3,10},{14,7},{15,6},{16,25},{17,... | collective-permute-start | bytes 983048 | tf_op jit(solution)/shard_map/ppermute | solution.py:334
  20.2 14.1 %collective-permute-start.6 = (bf16[640,256]{1,0:T(8,128)(2,1)S(1)}, bf16[640,256]{1,0:T(8,128)(2,1)S(1)}, u32[]{:S(2)}, u32[]{:S(2)}) collective-permute-start(bf16[640,256]{1,0:T(8,128)(2,1)S(1)} %pick_rows.6), channel_id=1, source_target_pairs={{0,4},{4,0},{8,12},{12,8},{1,5},{5,1},{9,13},{13,9},{2,6},{6,2},{1... | collective-permute-start | bytes 983048 | tf_op jit(solution)/shard_map/ppermute | solution.py:347
  21.9 16.7 %collective-permute-start.10 = (bf16[640,256]{1,0:T(8,128)(2,1)S(1)}, bf16[640,256]{1,0:T(8,128)(2,1)S(1)}, u32[]{:S(2)}, u32[]{:S(2)}) collective-permute-start(bf16[640,256]{1,0:T(8,128)(2,1)S(1)} %add.20), channel_id=1, source_target_pairs={{4,12},{8,0},{5,13},{9,1},{6,14},{10,2},{7,15},{11,3},{20,28},{24,... | collective-permute-start | bytes 983048 | tf_op jit(solution)/shard_map/ppermute | solution.py:347
  23.3 11.1 %collective-permute-start.8 = (bf16[16,2304]{1,0:T(8,128)(2,1)S(1)}, bf16[16,2304]{1,0:T(8,128)(2,1)S(1)}, u32[]{:S(2)}, u32[]{:S(2)}) collective-permute-start(bf16[16,2304]{1,0:T(8,128)(2,1)S(1)} %slice.6), channel_id=1, source_target_pairs={{0,1},{4,5},{8,9},{12,13},{2,3},{6,7},{10,11},{14,15},{16,17},{20,... | collective-permute-start | bytes 221192 | tf_op jit(solution)/shard_map/ppermute | solution.py:432
  38.8 11.1 %collective-permute-start.12 = (bf16[640,256]{1,0:T(8,128)(2,1)S(1)}, bf16[640,256]{1,0:T(8,128)(2,1)S(1)}, u32[]{:S(2)}, u32[]{:S(2)}) collective-permute-start(bf16[640,256]{1,0:T(8,128)(2,1)S(1)} %merge.1.refs_1_), channel_id=1, source_target_pairs={{0,2},{2,0},{1,3},{3,1},{4,6},{6,4},{5,7},{7,5},{8,10},{10,8},{9,1... | collective-permute-start | bytes 983048 | tf_op jit(solution)/shard_map/ppermute | solution.py:443
  40.3 3.5 %collective-permute-start.13 = (bf16[640,128]{1,0:T(8,128)(2,1)S(1)}, bf16[640,128]{1,0:T(8,128)(2,1)S(1)}, u32[]{:S(2)}, u32[]{:S(2)}) collective-permute-start(bf16[640,128]{1,0:T(8,128)(2,1)S(1)} %slice.8), channel_id=1, source_target_pairs={{0,1},{2,3},{4,5},{6,7},{8,9},{10,11},{12,13},{14,15},{16,17},{18,... | collective-permute-start | bytes 491528 | tf_op jit(solution)/shard_map/ppermute | solution.py:456
  42.1 7.7 %collective-permute-start.11 = (bf16[640,128]{1,0:T(8,128)(2,1)S(1)}, bf16[640,128]{1,0:T(8,128)(2,1)S(1)}, u32[]{:S(2)}, u32[]{:S(2)}) collective-permute-start(bf16[640,128]{1,0:T(8,128)(2,1)S(1)} %slice.8), channel_id=1, source_target_pairs={{0,3},{2,1},{4,7},{6,5},{8,11},{10,9},{12,15},{14,13},{16,19},{18,... | collective-permute-start | bytes 491528 | tf_op jit(solution)/shard_map/ppermute | solution.py:456
  49.8 5.8 %copy-start.1 = (f32[4,2304]{1,0:T(4,128)S(1)}, f32[4,2304]{1,0:T(4,128)}, u32[]{:S(2)}) copy-start(f32[4,2304]{1,0:T(4,128)} %refs_5_.1) | copy-start | bytes 110596
  54.1 3.8 %collective-permute-start.14 = (f32[8,272]{1,0:T(8,128)S(1)}, f32[8,272]{1,0:T(8,128)S(1)}, u32[]{:S(2)}, u32[]{:S(2)}) collective-permute-start(f32[8,272]{1,0:T(8,128)S(1)} %get-tuple-element.47.refs_0_), channel_id=1, source_target_pairs={{0,2},{2,0},{1,3},{3,1},{4,6},{6,4},{5,7},{7,5},{8,10},{10,8},{9,1... | collective-permute-start | bytes 26120 | tf_op jit(solution)/shard_map/ppermute | solution.py:498

commit v18 on v17

--- a/solution.py
+++ b/solution.py
@@ -135,22 +135,16 @@
         key_ref, value_ref, rest, held, sems, rest_sems = refs[4:]
         half = held.shape[-1]
 
-        split = sems.shape[-1]
-        size = depth // split
-
         def bring(target, far, which, n, s, sem):
             owner = lax.rem(tp + count - s, count)
-            copies = []
-            for k in range(split):
-                rows = pl.ds(pl.multiple_of(owner * depth + k * size, size), size)
-                copy = pltpu.make_async_copy(
-                    weights[2 * far + which].at[rows, :],
-                    target.at[far, which, pl.ds(n * depth + k * size, size), :],
-                    sem.at[k],
-                )
-                copy.start()
-                copies.append(copy)
-            return copies
+            rows = pl.ds(pl.multiple_of(owner * depth, depth), depth)
+            copy = pltpu.make_async_copy(
+                weights[2 * far + which].at[rows, :],
+                target.at[far, which, pl.ds(n * depth, depth), :],
+                sem,
+            )
+            copy.start()
+            return copy
 
         copies = [
             bring(held, far, which, 0, 0, sems.at[2 * far + which])
@@ -158,11 +152,6 @@
             for which in (1, 0)
         ]
         later = []
-        for far in range(2):
-            for which in (1, 0):
-                for n in range(count - 1):
-                    sem = rest_sems.at[(2 * far + which) * (count - 1) + n]
-                    later += bring(rest, far, which, n, n + 1, sem)
     else:
         later = []
         rest, begun_keys, begun_values, hidden_halo, hidden = refs[:5]
@@ -181,8 +170,14 @@
         fields = [None, None]
         for which in (1, 0):
             if first:
-                for copy in copies[2 * far + 1 - which]:
-                    copy.wait()
+                copies[2 * far + 1 - which].wait()
+                if far == 0 and which == 1:
+                    later = [
+                        bring(rest, f, w, n, n + 1, rest_sems.at[(2 * f + w) * (count - 1) + n])
+                        for f in range(2)
+                        for w in (1, 0)
+                        for n in range(count - 1)
+                    ]
             fields[which] = dot(memory, held[far, which])
             if not first and which == 1:
                 done[far] = fields[1] + begun_values[slot]
@@ -352,8 +347,8 @@
         [(m, r, m ^ 2, r ^ int(m in (1, 2))) for m in range(4) for r in range(2)],
     )
     third = ask(stored, 1)
-    first, second, third = lax.optimization_barrier((first, second, third))
     rows_3 = pick(first)
+    rows_3, second, third = lax.optimization_barrier((rows_3, second, third))
     inward = send(rows_3, (0, 1), (3, 2))
     across = send(rows_3, (1, 2), (2, 1))
     rows_2 = pick(after(second, rows_3))
@@ -466,8 +461,8 @@
         out_shape=(field, field, pltpu.VMEM((2, 2, others * depth, half), BF16)),
         scratch_shapes=[
             pltpu.VMEM((2, 2, depth, half), BF16),
-            pltpu.SemaphoreType.DMA((4, 4)),
-            pltpu.SemaphoreType.DMA((4 * others, 4)),
+            pltpu.SemaphoreType.DMA((4,)),
+            pltpu.SemaphoreType.DMA((4 * others,)),
         ],
         compiler_params=limit(12),
         name="project_own",

time: 61.2 us -> 59.8 us (0.977)
  waiting for transfers between devices: 16.4 us -> 15.5 us
    ppermute x2, waiting for transfers between devices: 4.23 us -> 3.36 us  [crossing(): lax.ppermute(x, ('mem', 'rep'), [(2 * a + b, 2 * c + d) for a, b, c, d in...]
  transfers between devices with their start and end apart: 15 -> 15, of which waited for: 6 -> 6; matrix products, arithmetic and copies ran while one was open for 0% -> 0% of each run, Pallas kernels for 23% -> 22%
where the time goes in v18:
time: 59.8 us; the launch traced here: 59.5 us
  starting transfers between devices  22.9 us (38%)
  Pallas kernels  20.5 us (34%)
  waiting for transfers between devices  15.5 us (26%)
    ppermute x4, waiting for transfers between devices, send(): return lax.ppermute(x, 'mem', pairs)  11.3 us
    pallas_call x1, Pallas kernels, shards(): pl.pallas_call(functools.partial(project_kernel, (0,), tps), in_specs=[sm...  5.51 us
    ppermute x2, starting transfers between devices, ask(): return lax.ppermute(ids, 'mem', [(i, i ^ x) for i in range(4)])  5.35 us
    ppermute x4, starting transfers between devices, send(): return lax.ppermute(x, 'mem', pairs)  4.76 us
    pallas_call x1, Pallas kernels, shards(): pl.pallas_call(functools.partial(project_kernel, tuple(range(1, tps)), tp...  4.24 us
    ppermute x2, starting transfers between devices, crossing(): lax.ppermute(x, ('mem', 'rep'), [(2 * a + b, 2 * c + d) for a, b, c, d in...  3.71 us
    pallas_call x4, Pallas kernels, pick(): pl.pallas_call(pick_kernel, in_specs=[pl.BlockSpec(memory_space=pltpu.SME...  3.46 us
    ppermute x2, waiting for transfers between devices, crossing(): lax.ppermute(x, ('mem', 'rep'), [(2 * a + b, 2 * c + d) for a, b, c, d in...  3.36 us
  transfers between devices with their start and end apart: 15, of which 6 were waited for; matrix products, arithmetic and copies ran while one was open for 0% of the time, Pallas kernels for 22%

profile of v18, /device:TPU:0, one launch (start us, length us, event | category | flops | bytes accessed | tf_op | source)
XLA Modules:
  0.0 59.5 jit_solution(14120256505080482536)
XLA Ops:
  0.0 0.5 collective-permute-start.3
  0.5 0.1 collective-permute-start.4
  0.5 1.5 %place_rows.1 = (s32[8,256]{1,0:T(8,128)S(1)}, bf16[8,80,1024]{2,1,0:T(8,128)(2,1)S(1)}, bf16[5,8,1024]{2,1,0:T(8,128)(2,1)S(1)}) custom-call(s32[8,256]{1,0:T(8,128)} %bitcast.11, s32[32,128]{1,0:T(8,128)} %bitcast.10, bf16[8,80,1024]{2,1,0:T(8,128)(2,1)} %bitcast.8, bf16[5,8,1024]{2,1,0:T(8,128)(2,1)} %bitcast.9), custom_call_target="tpu_custom_call" | custom-call | tf_op jit(solution)/shard_map/place_rows/pallas_call | solution.py:395
  2.0 5.1 %collective-permute-start = (s32[8,256]{1,0:T(8,128)S(1)}, s32[8,256]{1,0:T(8,128)S(1)}, u32[]{:S(2)}, u32[]{:S(2)}) collective-permute-start(s32[8,256]{1,0:T(8,128)S(1)} %get-tuple-element.37.ids_ref), channel_id=1, source_target_pairs={{0,12},{4,8},{8,4},{12,0},{1,13},{5,9},{9,5},{13,1},{2,14},{6,10},... | collective-permute-start | bytes 24584 | tf_op jit(solution)/shard_map/ppermute | solution.py:326
  7.1 0.0 collective-permute-start.1
  7.2 0.2 collective-permute-start.2
  7.4 0.9 %decode_tables.1.table_ref = bf16[8,80,1024]{2,1,0:T(8,128)(2,1)S(1)} custom-call(bf16[8,80,1024]{2,1,0:T(8,128)(2,1)S(1)} %get-tuple-element.29.codes_ref, bf16[5,8,1024]{2,1,0:T(8,128)(2,1)S(1)} %get-tuple-element.30.scales_ref), custom_call_target="tpu_custom_call" | custom-call | tf_op jit(solution)/shard_map/decode_tables/pallas_call | solution.py:412
  8.3 0.5 collective-permute-done.ids_ref
  8.8 0.9 %pick_rows.4 = bf16[640,256]{1,0:T(8,128)(2,1)S(1)} custom-call(s32[1]{0:T(128)} %bitcast.3.base_ref, s32[8,256]{1,0:T(8,128)S(1)} %collective-permute-done.ids_ref, bf16[8,80,1024]{2,1,0:T(8,128)(2,1)S(1)} %decode_tables.1.table_ref), custom_call_target="tpu_custom_call" | custom-call | tf_op jit(solution)/shard_map/pick_rows/pallas_call | solution.py:332
  9.6 1.5 %collective-permute-done.1.ids_ref = s32[8,256]{1,0:T(8,128)S(1)} collective-permute-done((s32[8,256]{1,0:T(8,128)S(1)}, s32[8,256]{1,0:T(8,128)S(1)}, u32[]{:S(2)}, u32[]{:S(2)}) %collective-permute-start.1) | collective-permute-done | bytes 8224 | tf_op jit(solution)/shard_map/ppermute | solution.py:329
  11.1 0.0 collective-permute-done.2.ids_ref
  11.1 2.0 %collective-permute-start.9 = (bf16[640,256]{1,0:T(8,128)(2,1)S(1)}, bf16[640,256]{1,0:T(8,128)(2,1)S(1)}, u32[]{:S(2)}, u32[]{:S(2)}) collective-permute-start(bf16[640,256]{1,0:T(8,128)(2,1)S(1)} %pick_rows.4), channel_id=1, source_target_pairs={{0,4},{12,8},{1,5},{13,9},{2,6},{14,10},{3,7},{15,11},{16,20},{28,... | collective-permute-start | bytes 983048 | tf_op jit(solution)/shard_map/ppermute | solution.py:342
  13.2 0.7 %collective-permute-start.7 = (bf16[640,256]{1,0:T(8,128)(2,1)S(1)}, bf16[640,256]{1,0:T(8,128)(2,1)S(1)}, u32[]{:S(2)}, u32[]{:S(2)}) collective-permute-start(bf16[640,256]{1,0:T(8,128)(2,1)S(1)} %pick_rows.4), channel_id=1, source_target_pairs={{4,8},{8,4},{5,9},{9,5},{6,10},{10,6},{7,11},{11,7},{20,24},{24,20... | collective-permute-start | bytes 983048 | tf_op jit(solution)/shard_map/ppermute | solution.py:342
  13.9 0.9 %pick_rows.5 = bf16[640,256]{1,0:T(8,128)(2,1)S(1)} custom-call(s32[1]{0:T(128)} %bitcast.3.base_ref, s32[8,256]{1,0:T(8,128)S(1)} %collective-permute-done.1.ids_ref, bf16[8,80,1024]{2,1,0:T(8,128)(2,1)S(1)} %decode_tables.1.table_ref), custom_call_target="tpu_custom_call" | custom-call | tf_op jit(solution)/shard_map/pick_rows/pallas_call | solution.py:332
  14.7 0.0 copy-start
  14.7 3.7 %collective-permute-start.5 = (bf16[640,256]{1,0:T(8,128)(2,1)S(1)}, bf16[640,256]{1,0:T(8,128)(2,1)S(1)}, u32[]{:S(2)}, u32[]{:S(2)}) collective-permute-start(bf16[640,256]{1,0:T(8,128)(2,1)S(1)} %pick_rows.5), channel_id=1, source_target_pairs={{0,9},{1,8},{12,5},{13,4},{2,11},{3,10},{14,7},{15,6},{16,25},{17,... | collective-permute-start | bytes 983048 | tf_op jit(solution)/shard_map/ppermute | solution.py:329
  18.5 0.0 collective-permute-done.3.refs_4_
  18.5 0.0 collective-permute-done.4.refs_5_
  18.5 0.9 %pick_rows.6 = bf16[640,256]{1,0:T(8,128)(2,1)S(1)} custom-call(s32[1]{0:T(128)} %bitcast.3.base_ref, s32[8,256]{1,0:T(8,128)S(1)} %collective-permute-done.2.ids_ref, bf16[8,80,1024]{2,1,0:T(8,128)(2,1)S(1)} %decode_tables.1.table_ref), custom_call_target="tpu_custom_call" | custom-call | tf_op jit(solution)/shard_map/pick_rows/pallas_call | solution.py:332
  19.3 0.7 %collective-permute-start.6 = (bf16[640,256]{1,0:T(8,128)(2,1)S(1)}, bf16[640,256]{1,0:T(8,128)(2,1)S(1)}, u32[]{:S(2)}, u32[]{:S(2)}) collective-permute-start(bf16[640,256]{1,0:T(8,128)(2,1)S(1)} %pick_rows.6), channel_id=1, source_target_pairs={{0,4},{4,0},{8,12},{12,8},{1,5},{5,1},{9,13},{13,9},{2,6},{6,2},{1... | collective-permute-start | bytes 983048 | tf_op jit(solution)/shard_map/ppermute | solution.py:342
  20.1 0.9 %pick_rows.7 = bf16[640,256]{1,0:T(8,128)(2,1)S(1)} custom-call(s32[1]{0:T(128)} %bitcast.3.base_ref, s32[8,256]{1,0:T(8,128)S(1)} %get-tuple-element.37.ids_ref, bf16[8,80,1024]{2,1,0:T(8,128)(2,1)S(1)} %decode_tables.1.table_ref), custom_call_target="tpu_custom_call" | custom-call | tf_op jit(solution)/shard_map/pick_rows/pallas_call | solution.py:332
  20.9 0.0 collective-permute-done.9
  21.0 0.1 add.20
  21.0 1.3 %collective-permute-start.10 = (bf16[640,256]{1,0:T(8,128)(2,1)S(1)}, bf16[640,256]{1,0:T(8,128)(2,1)S(1)}, u32[]{:S(2)}, u32[]{:S(2)}) collective-permute-start(bf16[640,256]{1,0:T(8,128)(2,1)S(1)} %add.20), channel_id=1, source_target_pairs={{4,12},{8,0},{5,13},{9,1},{6,14},{10,2},{7,15},{11,3},{20,28},{24,... | collective-permute-start | bytes 983048 | tf_op jit(solution)/shard_map/ppermute | solution.py:342
  22.3 0.0 copy-done
  22.4 0.0 collective-permute-done.7.refs_1_
  22.4 2.1 %collective-permute-start.8 = (bf16[16,2304]{1,0:T(8,128)(2,1)S(1)}, bf16[16,2304]{1,0:T(8,128)(2,1)S(1)}, u32[]{:S(2)}, u32[]{:S(2)}) collective-permute-start(bf16[16,2304]{1,0:T(8,128)(2,1)S(1)} %slice.6), channel_id=1, source_target_pairs={{0,1},{4,5},{8,9},{12,13},{2,3},{6,7},{10,11},{14,15},{16,17},{20,... | collective-permute-start | bytes 221192 | tf_op jit(solution)/shard_map/ppermute | solution.py:427
  24.5 1.9 %collective-permute-done.5 = bf16[640,256]{1,0:T(8,128)(2,1)S(1)} collective-permute-done((bf16[640,256]{1,0:T(8,128)(2,1)S(1)}, bf16[640,256]{1,0:T(8,128)(2,1)S(1)}, u32[]{:S(2)}, u32[]{:S(2)}) %collective-permute-start.5) | collective-permute-done | bytes 327712 | tf_op jit(solution)/shard_map/ppermute | solution.py:329
  26.4 7.0 %collective-permute-done.6 = bf16[640,256]{1,0:T(8,128)(2,1)S(1)} collective-permute-done((bf16[640,256]{1,0:T(8,128)(2,1)S(1)}, bf16[640,256]{1,0:T(8,128)(2,1)S(1)}, u32[]{:S(2)}, u32[]{:S(2)}) %collective-permute-start.6) | collective-permute-done | bytes 327712 | tf_op jit(solution)/shard_map/ppermute | solution.py:342
  33.5 0.0 collective-permute-done.8.refs_5_
  33.5 4.3 %collective-permute-done.10.refs_2_ = bf16[640,256]{1,0:T(8,128)(2,1)S(1)} collective-permute-done((bf16[640,256]{1,0:T(8,128)(2,1)S(1)}, bf16[640,256]{1,0:T(8,128)(2,1)S(1)}, u32[]{:S(2)}, u32[]{:S(2)}) %collective-permute-start.10) | collective-permute-done | bytes 327712 | tf_op jit(solution)/shard_map/ppermute | solution.py:342
  37.8 0.1 merge.1.refs_1_
  37.9 1.6 %collective-permute-start.12 = (bf16[640,256]{1,0:T(8,128)(2,1)S(1)}, bf16[640,256]{1,0:T(8,128)(2,1)S(1)}, u32[]{:S(2)}, u32[]{:S(2)}) collective-permute-start(bf16[640,256]{1,0:T(8,128)(2,1)S(1)} %merge.1.refs_1_), channel_id=1, source_target_pairs={{0,2},{2,0},{1,3},{3,1},{4,6},{6,4},{5,7},{7,5},{8,10},{10,8},{9,1... | collective-permute-start | bytes 983048 | tf_op jit(solution)/shard_map/ppermute | solution.py:438
  39.5 1.7 %collective-permute-start.13 = (bf16[640,128]{1,0:T(8,128)(2,1)S(1)}, bf16[640,128]{1,0:T(8,128)(2,1)S(1)}, u32[]{:S(2)}, u32[]{:S(2)}) collective-permute-start(bf16[640,128]{1,0:T(8,128)(2,1)S(1)} %slice.8), channel_id=1, source_target_pairs={{0,1},{2,3},{4,5},{6,7},{8,9},{10,11},{12,13},{14,15},{16,17},{18,... | collective-permute-start | bytes 491528 | tf_op jit(solution)/shard_map/ppermute | solution.py:451
  41.2 1.6 %collective-permute-start.11 = (bf16[640,128]{1,0:T(8,128)(2,1)S(1)}, bf16[640,128]{1,0:T(8,128)(2,1)S(1)}, u32[]{:S(2)}, u32[]{:S(2)}) collective-permute-start(bf16[640,128]{1,0:T(8,128)(2,1)S(1)} %slice.8), channel_id=1, source_target_pairs={{0,3},{2,1},{4,7},{6,5},{8,11},{10,9},{12,15},{14,13},{16,19},{18,... | collective-permute-start | bytes 491528 | tf_op jit(solution)/shard_map/ppermute | solution.py:451
  42.8 0.1 pad_add_fusion.where_ref
  42.9 0.0 collective-permute-done.13.refs_0_
  42.9 5.5 %project_own.1 = (f32[2,272,1152]{2,1,0:T(8,128)S(1)}, f32[2,272,1152]{2,1,0:T(8,128)S(1)}, bf16[2,2,640,1152]{3,2,1,0:T(8,128)(2,1)S(1)}) custom-call(s32[2]{0:T(128)S(1)} %pad_add_fusion.where_ref, bf16[640,128]{1,0:T(8,128)(2,1)S(1)} %collective-permute-done.13.refs_0_, bf16[640,256]{1,0:T(8,128)(2,1)S(1)} %merge.1.refs_1_, bf16[1280,1152]{1,0:T(8,128)(2,1)} %refs_2_.1, ...), custom_call_target="tpu_custom_call" | custom-call | tf_op jit(solution)/shard_map/project_own/pallas_call | solution.py:457
  48.4 0.0 collective-permute-done.11.refs_0_
  48.4 0.0 collective-permute-done.12.refs_1_
  48.5 0.0 copy-start.1
  48.5 4.2 %project_others.1 = (f32[2,272,1152]{2,1,0:T(8,128)}, f32[8,272]{1,0:T(8,128)S(1)}) custom-call(s32[2]{0:T(128)S(1)} %pad_add_fusion.where_ref, bf16[640,128]{1,0:T(8,128)(2,1)S(1)} %collective-permute-done.11.refs_0_, bf16[640,256]{1,0:T(8,128)(2,1)S(1)} %collective-permute-done.12.refs_1_, bf16[2,2,640,1152]{3,2,1,0:T(8,128)(2,1)S(1)} %get-tuple-element.43.refs_2_, ...), custom_call_target="tpu_custom_call" | custom-call | tf_op jit(solution)/shard_map/project_others/pallas_call | solution.py:470
  52.7 1.6 %collective-permute-start.14 = (f32[8,272]{1,0:T(8,128)S(1)}, f32[8,272]{1,0:T(8,128)S(1)}, u32[]{:S(2)}, u32[]{:S(2)}) collective-permute-start(f32[8,272]{1,0:T(8,128)S(1)} %get-tuple-element.47.refs_0_), channel_id=1, source_target_pairs={{0,2},{2,0},{1,3},{3,1},{4,6},{6,4},{5,7},{7,5},{8,10},{10,8},{9,1... | collective-permute-start | bytes 26120 | tf_op jit(solution)/shard_map/ppermute | solution.py:493
  54.3 0.0 copy-done.1
  54.3 1.9 %prepare.1 = (f32[2,256,1152]{2,1,0:T(8,128)S(1)}, f32[3,2,256,1152]{3,2,1,0:T(8,128)S(1)}) custom-call(f32[4,2304]{1,0:T(4,128)S(1)} %copy-done.1, f32[2,272,1152]{2,1,0:T(8,128)} %get-tuple-element.48.value_hbm), custom_call_target="tpu_custom_call" | custom-call | tf_op jit(solution)/shard_map/prepare/pallas_call | solution.py:501
  56.2 0.3 collective-permute-done.14.refs_1_
  56.5 2.8 %finish.1 = bf16[256,2304]{1,0:T(8,128)(2,1)} custom-call(s32[1]{0:T(128)} %bitcast.keep_ref, f32[8,272]{1,0:T(8,128)S(1)} %get-tuple-element.47.refs_0_, f32[8,272]{1,0:T(8,128)S(1)} %collective-permute-done.14.refs_1_, f32[2,256,1152]{2,1,0:T(8,128)S(1)} %get-tuple-element.49.refs_2_, f32[3,2,256,1152]{3,2,1,0:T(8,128)S(1)} %get-tuple-element.50.refs_3_, ...), custom_call_target="tpu_custom_call" | custom-call | tf_op jit(solution)/shard_map/finish/pallas_call | solution.py:516
  (3 shorter events, 0.1 us)
Async XLA Ops:
  0.0 18.5 %collective-permute-start.3 = (bf16[1280,1152]{1,0:T(8,128)(2,1)}, bf16[1280,1152]{1,0:T(8,128)(2,1)}, u32[]{:S(2)}, u32[]{:S(2)}) collective-permute-start(bf16[1280,1152]{1,0:T(8,128)(2,1)} %refs_2_.1), channel_id=1, source_target_pairs={{0,1},{1,0},{2,3},{3,2},{4,5},{5,4},{6,7},{7,6},{8,9},{9,8},{10,11... | collective-permute-start | bytes 8847368 | tf_op jit(solution)/shard_map/ppermute | solution.py:421
  0.5 18.0 %collective-permute-start.4 = (bf16[1280,1152]{1,0:T(8,128)(2,1)}, bf16[1280,1152]{1,0:T(8,128)(2,1)}, u32[]{:S(2)}, u32[]{:S(2)}) collective-permute-start(bf16[1280,1152]{1,0:T(8,128)(2,1)} %refs_3_.1), channel_id=1, source_target_pairs={{0,1},{1,0},{2,3},{3,2},{4,5},{5,4},{6,7},{7,6},{8,9},{9,8},{10,11... | collective-permute-start | bytes 8847368 | tf_op jit(solution)/shard_map/ppermute | solution.py:422
  2.0 6.7 %collective-permute-start = (s32[8,256]{1,0:T(8,128)S(1)}, s32[8,256]{1,0:T(8,128)S(1)}, u32[]{:S(2)}, u32[]{:S(2)}) collective-permute-start(s32[8,256]{1,0:T(8,128)S(1)} %get-tuple-element.37.ids_ref), channel_id=1, source_target_pairs={{0,12},{4,8},{8,4},{12,0},{1,13},{5,9},{9,5},{13,1},{2,14},{6,10},... | collective-permute-start | bytes 24584 | tf_op jit(solution)/shard_map/ppermute | solution.py:326
  7.1 4.0 %collective-permute-start.1 = (s32[8,256]{1,0:T(8,128)S(1)}, s32[8,256]{1,0:T(8,128)S(1)}, u32[]{:S(2)}, u32[]{:S(2)}) collective-permute-start(s32[8,256]{1,0:T(8,128)S(1)} %get-tuple-element.37.ids_ref), channel_id=1, source_target_pairs={{0,8},{1,9},{4,13},{5,12},{8,1},{9,0},{12,4},{13,5},{2,10},{3,11},... | collective-permute-start | bytes 24584 | tf_op jit(solution)/shard_map/ppermute | solution.py:329
  7.2 4.0 %collective-permute-start.2 = (s32[8,256]{1,0:T(8,128)S(1)}, s32[8,256]{1,0:T(8,128)S(1)}, u32[]{:S(2)}, u32[]{:S(2)}) collective-permute-start(s32[8,256]{1,0:T(8,128)S(1)} %get-tuple-element.37.ids_ref), channel_id=1, source_target_pairs={{0,4},{4,0},{8,12},{12,8},{1,5},{5,1},{9,13},{13,9},{2,6},{6,2},{1... | collective-permute-start | bytes 24584 | tf_op jit(solution)/shard_map/ppermute | solution.py:326
  11.1 9.8 %collective-permute-start.9 = (bf16[640,256]{1,0:T(8,128)(2,1)S(1)}, bf16[640,256]{1,0:T(8,128)(2,1)S(1)}, u32[]{:S(2)}, u32[]{:S(2)}) collective-permute-start(bf16[640,256]{1,0:T(8,128)(2,1)S(1)} %pick_rows.4), channel_id=1, source_target_pairs={{0,4},{12,8},{1,5},{13,9},{2,6},{14,10},{3,7},{15,11},{16,20},{28,... | collective-permute-start | bytes 983048 | tf_op jit(solution)/shard_map/ppermute | solution.py:342
  13.2 9.2 %collective-permute-start.7 = (bf16[640,256]{1,0:T(8,128)(2,1)S(1)}, bf16[640,256]{1,0:T(8,128)(2,1)S(1)}, u32[]{:S(2)}, u32[]{:S(2)}) collective-permute-start(bf16[640,256]{1,0:T(8,128)(2,1)S(1)} %pick_rows.4), channel_id=1, source_target_pairs={{4,8},{8,4},{5,9},{9,5},{6,10},{10,6},{7,11},{11,7},{20,24},{24,20... | collective-permute-start | bytes 983048 | tf_op jit(solution)/shard_map/ppermute | solution.py:342
  14.7 7.6 %copy-start = (bf16[256,2304]{1,0:T(8,128)(2,1)S(1)}, bf16[256,2304]{1,0:T(8,128)(2,1)}, u32[]{:S(2)}) copy-start(bf16[256,2304]{1,0:T(8,128)(2,1)} %refs_4_.1) | copy-start | bytes 3538948
  14.7 11.6 %collective-permute-start.5 = (bf16[640,256]{1,0:T(8,128)(2,1)S(1)}, bf16[640,256]{1,0:T(8,128)(2,1)S(1)}, u32[]{:S(2)}, u32[]{:S(2)}) collective-permute-start(bf16[640,256]{1,0:T(8,128)(2,1)S(1)} %pick_rows.5), channel_id=1, source_target_pairs={{0,9},{1,8},{12,5},{13,4},{2,11},{3,10},{14,7},{15,6},{16,25},{17,... | collective-permute-start | bytes 983048 | tf_op jit(solution)/shard_map/ppermute | solution.py:329
  19.3 14.1 %collective-permute-start.6 = (bf16[640,256]{1,0:T(8,128)(2,1)S(1)}, bf16[640,256]{1,0:T(8,128)(2,1)S(1)}, u32[]{:S(2)}, u32[]{:S(2)}) collective-permute-start(bf16[640,256]{1,0:T(8,128)(2,1)S(1)} %pick_rows.6), channel_id=1, source_target_pairs={{0,4},{4,0},{8,12},{12,8},{1,5},{5,1},{9,13},{13,9},{2,6},{6,2},{1... | collective-permute-start | bytes 983048 | tf_op jit(solution)/shard_map/ppermute | solution.py:342
  21.0 16.7 %collective-permute-start.10 = (bf16[640,256]{1,0:T(8,128)(2,1)S(1)}, bf16[640,256]{1,0:T(8,128)(2,1)S(1)}, u32[]{:S(2)}, u32[]{:S(2)}) collective-permute-start(bf16[640,256]{1,0:T(8,128)(2,1)S(1)} %add.20), channel_id=1, source_target_pairs={{4,12},{8,0},{5,13},{9,1},{6,14},{10,2},{7,15},{11,3},{20,28},{24,... | collective-permute-start | bytes 983048 | tf_op jit(solution)/shard_map/ppermute | solution.py:342
  22.4 11.1 %collective-permute-start.8 = (bf16[16,2304]{1,0:T(8,128)(2,1)S(1)}, bf16[16,2304]{1,0:T(8,128)(2,1)S(1)}, u32[]{:S(2)}, u32[]{:S(2)}) collective-permute-start(bf16[16,2304]{1,0:T(8,128)(2,1)S(1)} %slice.6), channel_id=1, source_target_pairs={{0,1},{4,5},{8,9},{12,13},{2,3},{6,7},{10,11},{14,15},{16,17},{20,... | collective-permute-start | bytes 221192 | tf_op jit(solution)/shard_map/ppermute | solution.py:427
  37.9 10.6 %collective-permute-start.12 = (bf16[640,256]{1,0:T(8,128)(2,1)S(1)}, bf16[640,256]{1,0:T(8,128)(2,1)S(1)}, u32[]{:S(2)}, u32[]{:S(2)}) collective-permute-start(bf16[640,256]{1,0:T(8,128)(2,1)S(1)} %merge.1.refs_1_), channel_id=1, source_target_pairs={{0,2},{2,0},{1,3},{3,1},{4,6},{6,4},{5,7},{7,5},{8,10},{10,8},{9,1... | collective-permute-start | bytes 983048 | tf_op jit(solution)/shard_map/ppermute | solution.py:438
  39.5 3.5 %collective-permute-start.13 = (bf16[640,128]{1,0:T(8,128)(2,1)S(1)}, bf16[640,128]{1,0:T(8,128)(2,1)S(1)}, u32[]{:S(2)}, u32[]{:S(2)}) collective-permute-start(bf16[640,128]{1,0:T(8,128)(2,1)S(1)} %slice.8), channel_id=1, source_target_pairs={{0,1},{2,3},{4,5},{6,7},{8,9},{10,11},{12,13},{14,15},{16,17},{18,... | collective-permute-start | bytes 491528 | tf_op jit(solution)/shard_map/ppermute | solution.py:451
  41.2 7.2 %collective-permute-start.11 = (bf16[640,128]{1,0:T(8,128)(2,1)S(1)}, bf16[640,128]{1,0:T(8,128)(2,1)S(1)}, u32[]{:S(2)}, u32[]{:S(2)}) collective-permute-start(bf16[640,128]{1,0:T(8,128)(2,1)S(1)} %slice.8), channel_id=1, source_target_pairs={{0,3},{2,1},{4,7},{6,5},{8,11},{10,9},{12,15},{14,13},{16,19},{18,... | collective-permute-start | bytes 491528 | tf_op jit(solution)/shard_map/ppermute | solution.py:451
  48.5 5.8 %copy-start.1 = (f32[4,2304]{1,0:T(4,128)S(1)}, f32[4,2304]{1,0:T(4,128)}, u32[]{:S(2)}) copy-start(f32[4,2304]{1,0:T(4,128)} %refs_5_.1) | copy-start | bytes 110596
  52.7 3.8 %collective-permute-start.14 = (f32[8,272]{1,0:T(8,128)S(1)}, f32[8,272]{1,0:T(8,128)S(1)}, u32[]{:S(2)}, u32[]{:S(2)}) collective-permute-start(f32[8,272]{1,0:T(8,128)S(1)} %get-tuple-element.47.refs_0_), channel_id=1, source_target_pairs={{0,2},{2,0},{1,3},{3,1},{4,6},{6,4},{5,7},{7,5},{8,10},{10,8},{9,1... | collective-permute-start | bytes 26120 | tf_op jit(solution)/shard_map/ppermute | solution.py:493

commit v19 on v18

--- a/solution.py
+++ b/solution.py
@@ -107,9 +107,9 @@
     return dot(table_ref[head], hot).astype(BF16)
 
 
-def pick_kernel(base_ref, ids_ref, table_ref, out_ref):
+def pick_kernel(begin, base_ref, ids_ref, table_ref, out_ref):
     heads, width, _ = table_ref.shape
-    local = ids_ref[...] - base_ref[0]
+    local = ids_ref[begin : begin + heads, :] - base_ref[0]
     for head in range(heads):
         out_ref[head * width : (head + 1) * width, :] = picked(local, table_ref, head)
 
@@ -300,7 +300,7 @@
     tokens = stored.shape[1]
     asked = lax.all_gather(stored, "mem", axis=0)
     partial = pl.pallas_call(
-        pick_kernel,
+        functools.partial(pick_kernel, 0),
         grid=(mems,),
         in_specs=[
             pl.BlockSpec(memory_space=pltpu.SMEM),
@@ -322,15 +322,12 @@
     base = (here * rows).astype(I32).reshape(1)
     block = jax.ShapeDtypeStruct((heads * width, tokens), BF16)
 
-    def ask(ids, x):
-        return lax.ppermute(ids, "mem", [(i, i ^ x) for i in range(4)])
-
     def crossing(x, pairs):
         return lax.ppermute(x, ("mem", "rep"), [(2 * a + b, 2 * c + d) for a, b, c, d in pairs])
 
-    def pick(ids):
+    def pick(ids, begin=0):
         return pl.pallas_call(
-            pick_kernel,
+            functools.partial(pick_kernel, begin),
             in_specs=[pl.BlockSpec(memory_space=pltpu.SMEM)]
             + [pl.BlockSpec(memory_space=pltpu.VMEM)] * 2,
             out_shape=block,
@@ -341,26 +338,27 @@
     def send(x, *pairs):
         return lax.ppermute(x, "mem", pairs)
 
-    first = ask(stored, 3)
-    second = crossing(
-        stored,
+    first = lax.ppermute(stored, "mem", [(m, m ^ 3) for m in range(4)])
+    both = crossing(
+        jnp.concatenate([stored, first]),
         [(m, r, m ^ 2, r ^ int(m in (1, 2))) for m in range(4) for r in range(2)],
     )
-    third = ask(stored, 1)
     rows_3 = pick(first)
-    rows_3, second, third = lax.optimization_barrier((rows_3, second, third))
+    rows_3, both = lax.optimization_barrier((rows_3, both))
     inward = send(rows_3, (0, 1), (3, 2))
     across = send(rows_3, (1, 2), (2, 1))
-    rows_2 = pick(after(second, rows_3))
-    third, settled = lax.optimization_barrier((after(third, rows_2), settled))
-    past = crossing(rows_2, [(m, r, m ^ 2, r ^ 1) for m in (0, 3) for r in range(2)])
-    rows_1 = pick(third)
+    rows_2 = pick(both)
+    ready, both, settled = lax.optimization_barrier((rows_2, both, settled))
+    past = crossing(ready, [(m, r, m ^ 2, r ^ 1) for m in (0, 3) for r in range(2)])
+    rows_1 = pick(both, heads)
     own = pick(after(stored, rows_1))
-    beside = send(rows_1, (0, 1), (1, 0), (2, 3), (3, 2))
+    beside = crossing(
+        rows_1, [(m, r, m ^ 1, r ^ int(m in (0, 3))) for m in range(4) for r in range(2)]
+    )
     onward = after(rows_2, rows_1, own) + inward
     onward = send(onward, (1, 3), (2, 0))
     other = meanwhile(across)
-    own, other = lax.optimization_barrier((own + past + beside, other))
+    own, other = lax.optimization_barrier((own + beside + past, other))
     memory = pl.pallas_call(
         merge_kernel,
         in_specs=[pl.BlockSpec(memory_space=pltpu.VMEM)] * 3,

time: 59.8 us -> 65.3 us (1.092)
  waiting for transfers between devices: 15.5 us -> 21.3 us
    ppermute x2 -> x3, waiting for transfers between devices: 3.36 us -> 11.8 us  [crossing(): lax.ppermute(x, ('mem', 'rep'), [(2 * a + b, 2 * c + d) for a, b, c, d in...]
    ppermute x4 -> x3, waiting for transfers between devices: 11.3 us -> 6.78 us  [send(): return lax.ppermute(x, 'mem', pairs)]
    ppermute x4 -> x3, starting transfers between devices: 4.76 us -> 5.92 us  [send(): return lax.ppermute(x, 'mem', pairs)]
    ppermute x2 -> x1, waiting for transfers between devices: 0.52 us -> 1.63 us  [line_sum(): first = lax.ppermute(stored, 'mem', [(m, m ^ 3) for m in range(4)])]
    ppermute x2 -> x3, starting transfers between devices: 3.71 us -> 4.54 us  [crossing(): lax.ppermute(x, ('mem', 'rep'), [(2 * a + b, 2 * c + d) for a, b, c, d in...]
    ppermute x1, starting transfers between devices: 1.56 us -> 0.77 us  [shards(): lax.ppermute(stats, 'tp', [(i, (i + s) % tps) for i in range(tps)])]
    ppermute x1, waiting for transfers between devices: 0.26 us -> 1.05 us  [shards(): lax.ppermute(stats, 'tp', [(i, (i + s) % tps) for i in range(tps)])]
    ppermute x1, starting transfers between devices: 2.12 us -> 1.37 us  [meanwhile(): return lax.ppermute(tail, ('mem', 'rep'), needed)]
  transfers between devices with their start and end apart: 15 -> 14, of which waited for: 6 -> 7; matrix products, arithmetic and copies ran while one was open for 0% -> 0% of each run, Pallas kernels for 22% -> 20%
where the time goes in v19:
time: 65.3 us; the launch traced here: 65 us
  starting transfers between devices  22.6 us (35%)
  waiting for transfers between devices  21.3 us (33%)
  Pallas kernels  20.5 us (31%)
    ppermute x3, waiting for transfers between devices, crossing(): lax.ppermute(x, ('mem', 'rep'), [(2 * a + b, 2 * c + d) for a, b, c, d in...  11.8 us
    ppermute x3, waiting for transfers between devices, send(): return lax.ppermute(x, 'mem', pairs)  6.78 us
    ppermute x3, starting transfers between devices, send(): return lax.ppermute(x, 'mem', pairs)  5.92 us
    pallas_call x1, Pallas kernels, shards(): pl.pallas_call(functools.partial(project_kernel, (0,), tps), in_specs=[sm...  5.51 us
    ppermute x1, starting transfers between devices, line_sum(): first = lax.ppermute(stored, 'mem', [(m, m ^ 3) for m in range(4)])  5.11 us
    ppermute x3, starting transfers between devices, crossing(): lax.ppermute(x, ('mem', 'rep'), [(2 * a + b, 2 * c + d) for a, b, c, d in...  4.54 us
    pallas_call x1, Pallas kernels, shards(): pl.pallas_call(functools.partial(project_kernel, tuple(range(1, tps)), tp...  4.25 us
    pallas_call x4, Pallas kernels, pick(): pl.pallas_call(functools.partial(pick_kernel, begin), in_specs=[pl.BlockS...  3.46 us
  transfers between devices with their start and end apart: 14, of which 7 were waited for; matrix products, arithmetic and copies ran while one was open for 0% of the time, Pallas kernels for 20%

profile of v19, /device:TPU:0, one launch (start us, length us, event | category | flops | bytes accessed | tf_op | source)
XLA Modules:
  0.0 65.0 jit_solution(13949826919389140838)
XLA Ops:
  0.0 0.5 collective-permute-start.2
  0.5 0.1 collective-permute-start.3
  0.5 1.5 %place_rows.1 = (s32[8,256]{1,0:T(8,128)S(1)}, bf16[8,80,1024]{2,1,0:T(8,128)(2,1)S(1)}, bf16[5,8,1024]{2,1,0:T(8,128)(2,1)S(1)}) custom-call(s32[8,256]{1,0:T(8,128)} %bitcast.11, s32[32,128]{1,0:T(8,128)} %bitcast.10, bf16[8,80,1024]{2,1,0:T(8,128)(2,1)} %bitcast.8, bf16[5,8,1024]{2,1,0:T(8,128)(2,1)} %bitcast.9), custom_call_target="tpu_custom_call" | custom-call | tf_op jit(solution)/shard_map/place_rows/pallas_call | solution.py:393
  2.0 5.1 %collective-permute-start = (s32[8,256]{1,0:T(8,128)S(1)}, s32[8,256]{1,0:T(8,128)S(1)}, u32[]{:S(2)}, u32[]{:S(2)}) collective-permute-start(s32[8,256]{1,0:T(8,128)S(1)} %get-tuple-element.31.ids_ref), channel_id=1, source_target_pairs={{0,12},{4,8},{8,4},{12,0},{1,13},{5,9},{9,5},{13,1},{2,14},{6,10},... | collective-permute-start | bytes 24584 | tf_op jit(solution)/shard_map/ppermute | solution.py:341
  7.1 1.6 %collective-permute-done.ids_ref = s32[8,256]{1,0:T(8,128)S(1)} collective-permute-done((s32[8,256]{1,0:T(8,128)S(1)}, s32[8,256]{1,0:T(8,128)S(1)}, u32[]{:S(2)}, u32[]{:S(2)}) %collective-permute-start) | collective-permute-done | bytes 8224 | tf_op jit(solution)/shard_map/ppermute | solution.py:341
  8.8 1.0 %collective-permute-start.1 = (s32[16,256]{1,0:T(8,128)S(1)}, s32[16,256]{1,0:T(8,128)S(1)}, u32[]{:S(2)}, u32[]{:S(2)}) collective-permute-start(s32[16,256]{1,0:T(8,128)S(1)} %pad_add_fusion), channel_id=1, source_target_pairs={{0,8},{1,9},{4,13},{5,12},{8,1},{9,0},{12,4},{13,5},{2,10},{3,11},... | collective-permute-start | bytes 49160 | tf_op jit(solution)/shard_map/ppermute | solution.py:326
  9.8 0.9 %decode_tables.1.table_ref = bf16[8,80,1024]{2,1,0:T(8,128)(2,1)S(1)} custom-call(bf16[8,80,1024]{2,1,0:T(8,128)(2,1)S(1)} %get-tuple-element.27.codes_ref, bf16[5,8,1024]{2,1,0:T(8,128)(2,1)S(1)} %get-tuple-element.28.scales_ref), custom_call_target="tpu_custom_call" | custom-call | tf_op jit(solution)/shard_map/decode_tables/pallas_call | solution.py:410
  10.7 0.9 %pick_rows.4 = bf16[640,256]{1,0:T(8,128)(2,1)S(1)} custom-call(s32[1]{0:T(128)} %bitcast.3.base_ref, s32[8,256]{1,0:T(8,128)S(1)} %collective-permute-done.ids_ref, bf16[8,80,1024]{2,1,0:T(8,128)(2,1)S(1)} %decode_tables.1.table_ref), custom_call_target="tpu_custom_call" | custom-call | tf_op jit(solution)/shard_map/pick_rows/pallas_call | solution.py:329
  11.5 1.3 %collective-permute-done.1.ids_ref = s32[16,256]{1,0:T(8,128)S(1)} collective-permute-done((s32[16,256]{1,0:T(8,128)S(1)}, s32[16,256]{1,0:T(8,128)S(1)}, u32[]{:S(2)}, u32[]{:S(2)}) %collective-permute-start.1) | collective-permute-done | bytes 16416 | tf_op jit(solution)/shard_map/ppermute | solution.py:326
  12.8 3.9 %collective-permute-start.8 = (bf16[640,256]{1,0:T(8,128)(2,1)S(1)}, bf16[640,256]{1,0:T(8,128)(2,1)S(1)}, u32[]{:S(2)}, u32[]{:S(2)}) collective-permute-start(bf16[640,256]{1,0:T(8,128)(2,1)S(1)} %pick_rows.4), channel_id=1, source_target_pairs={{0,4},{12,8},{1,5},{13,9},{2,6},{14,10},{3,7},{15,11},{16,20},{28,... | collective-permute-start | bytes 983048 | tf_op jit(solution)/shard_map/ppermute | solution.py:339
  16.8 0.7 %collective-permute-start.6 = (bf16[640,256]{1,0:T(8,128)(2,1)S(1)}, bf16[640,256]{1,0:T(8,128)(2,1)S(1)}, u32[]{:S(2)}, u32[]{:S(2)}) collective-permute-start(bf16[640,256]{1,0:T(8,128)(2,1)S(1)} %pick_rows.4), channel_id=1, source_target_pairs={{4,8},{8,4},{5,9},{9,5},{6,10},{10,6},{7,11},{11,7},{20,24},{24,20... | collective-permute-start | bytes 983048 | tf_op jit(solution)/shard_map/ppermute | solution.py:339
  17.5 0.9 %pick_rows.5 = bf16[640,256]{1,0:T(8,128)(2,1)S(1)} custom-call(s32[1]{0:T(128)} %bitcast.3.base_ref, s32[16,256]{1,0:T(8,128)S(1)} %collective-permute-done.1.ids_ref, bf16[8,80,1024]{2,1,0:T(8,128)(2,1)S(1)} %decode_tables.1.table_ref), custom_call_target="tpu_custom_call" | custom-call | tf_op jit(solution)/shard_map/pick_rows/pallas_call | solution.py:329
  18.4 0.0 copy-start
  18.4 0.0 collective-permute-done.2.refs_4_
  18.4 0.0 collective-permute-done.3.refs_5_
  18.4 0.9 %pick_rows.6 = bf16[640,256]{1,0:T(8,128)(2,1)S(1)} custom-call(s32[1]{0:T(128)} %bitcast.3.base_ref, s32[16,256]{1,0:T(8,128)S(1)} %collective-permute-done.1.ids_ref, bf16[8,80,1024]{2,1,0:T(8,128)(2,1)S(1)} %decode_tables.1.table_ref), custom_call_target="tpu_custom_call" | custom-call | tf_op jit(solution)/shard_map/pick_rows/pallas_call | solution.py:329
  19.3 0.4 collective-permute-start.4
  19.7 3.1 %collective-permute-start.5 = (bf16[640,256]{1,0:T(8,128)(2,1)S(1)}, bf16[640,256]{1,0:T(8,128)(2,1)S(1)}, u32[]{:S(2)}, u32[]{:S(2)}) collective-permute-start(bf16[640,256]{1,0:T(8,128)(2,1)S(1)} %pick_rows.5), channel_id=1, source_target_pairs={{0,9},{1,8},{12,5},{13,4},{2,11},{3,10},{14,7},{15,6},{16,25},{17,... | collective-permute-start | bytes 983048 | tf_op jit(solution)/shard_map/ppermute | solution.py:326
  22.8 0.9 %pick_rows.7 = bf16[640,256]{1,0:T(8,128)(2,1)S(1)} custom-call(s32[1]{0:T(128)} %bitcast.3.base_ref, s32[8,256]{1,0:T(8,128)S(1)} %get-tuple-element.31.ids_ref, bf16[8,80,1024]{2,1,0:T(8,128)(2,1)S(1)} %decode_tables.1.table_ref), custom_call_target="tpu_custom_call" | custom-call | tf_op jit(solution)/shard_map/pick_rows/pallas_call | solution.py:329
  23.7 1.2 %collective-permute-done.8 = bf16[640,256]{1,0:T(8,128)(2,1)S(1)} collective-permute-done((bf16[640,256]{1,0:T(8,128)(2,1)S(1)}, bf16[640,256]{1,0:T(8,128)(2,1)S(1)}, u32[]{:S(2)}, u32[]{:S(2)}) %collective-permute-start.8) | collective-permute-done | bytes 327712 | tf_op jit(solution)/shard_map/ppermute | solution.py:339
  24.8 0.1 add.20
  24.9 1.3 %collective-permute-start.9 = (bf16[640,256]{1,0:T(8,128)(2,1)S(1)}, bf16[640,256]{1,0:T(8,128)(2,1)S(1)}, u32[]{:S(2)}, u32[]{:S(2)}) collective-permute-start(bf16[640,256]{1,0:T(8,128)(2,1)S(1)} %add.20), channel_id=1, source_target_pairs={{4,12},{8,0},{5,13},{9,1},{6,14},{10,2},{7,15},{11,3},{20,28},{24,... | collective-permute-start | bytes 983048 | tf_op jit(solution)/shard_map/ppermute | solution.py:339
  26.2 0.0 copy-done
  26.2 0.0 collective-permute-done.6.refs_1_
  26.3 1.4 %collective-permute-start.7 = (bf16[16,2304]{1,0:T(8,128)(2,1)S(1)}, bf16[16,2304]{1,0:T(8,128)(2,1)S(1)}, u32[]{:S(2)}, u32[]{:S(2)}) collective-permute-start(bf16[16,2304]{1,0:T(8,128)(2,1)S(1)} %slice.6), channel_id=1, source_target_pairs={{0,1},{4,5},{8,9},{12,13},{2,3},{6,7},{10,11},{14,15},{16,17},{20,... | collective-permute-start | bytes 221192 | tf_op jit(solution)/shard_map/ppermute | solution.py:425
  27.6 4.2 %collective-permute-done.4 = bf16[640,256]{1,0:T(8,128)(2,1)S(1)} collective-permute-done((bf16[640,256]{1,0:T(8,128)(2,1)S(1)}, bf16[640,256]{1,0:T(8,128)(2,1)S(1)}, u32[]{:S(2)}, u32[]{:S(2)}) %collective-permute-start.4) | collective-permute-done | bytes 327712 | tf_op jit(solution)/shard_map/ppermute | solution.py:326
  31.9 6.3 %collective-permute-done.5 = bf16[640,256]{1,0:T(8,128)(2,1)S(1)} collective-permute-done((bf16[640,256]{1,0:T(8,128)(2,1)S(1)}, bf16[640,256]{1,0:T(8,128)(2,1)S(1)}, u32[]{:S(2)}, u32[]{:S(2)}) %collective-permute-start.5) | collective-permute-done | bytes 327712 | tf_op jit(solution)/shard_map/ppermute | solution.py:326
  38.2 0.0 collective-permute-done.7.refs_5_
  38.2 5.6 %collective-permute-done.9.refs_2_ = bf16[640,256]{1,0:T(8,128)(2,1)S(1)} collective-permute-done((bf16[640,256]{1,0:T(8,128)(2,1)S(1)}, bf16[640,256]{1,0:T(8,128)(2,1)S(1)}, u32[]{:S(2)}, u32[]{:S(2)}) %collective-permute-start.9) | collective-permute-done | bytes 327712 | tf_op jit(solution)/shard_map/ppermute | solution.py:339
  43.8 0.1 merge.1.refs_1_
  43.9 1.6 %collective-permute-start.11 = (bf16[640,256]{1,0:T(8,128)(2,1)S(1)}, bf16[640,256]{1,0:T(8,128)(2,1)S(1)}, u32[]{:S(2)}, u32[]{:S(2)}) collective-permute-start(bf16[640,256]{1,0:T(8,128)(2,1)S(1)} %merge.1.refs_1_), channel_id=1, source_target_pairs={{0,2},{2,0},{1,3},{3,1},{4,6},{6,4},{5,7},{7,5},{8,10},{10,8},{9,1... | collective-permute-start | bytes 983048 | tf_op jit(solution)/shard_map/ppermute | solution.py:436
  45.5 1.3 %collective-permute-start.12 = (bf16[640,128]{1,0:T(8,128)(2,1)S(1)}, bf16[640,128]{1,0:T(8,128)(2,1)S(1)}, u32[]{:S(2)}, u32[]{:S(2)}) collective-permute-start(bf16[640,128]{1,0:T(8,128)(2,1)S(1)} %slice.8), channel_id=1, source_target_pairs={{0,1},{2,3},{4,5},{6,7},{8,9},{10,11},{12,13},{14,15},{16,17},{18,... | collective-permute-start | bytes 491528 | tf_op jit(solution)/shard_map/ppermute | solution.py:449
  46.8 1.5 %collective-permute-start.10 = (bf16[640,128]{1,0:T(8,128)(2,1)S(1)}, bf16[640,128]{1,0:T(8,128)(2,1)S(1)}, u32[]{:S(2)}, u32[]{:S(2)}) collective-permute-start(bf16[640,128]{1,0:T(8,128)(2,1)S(1)} %slice.8), channel_id=1, source_target_pairs={{0,3},{2,1},{4,7},{6,5},{8,11},{10,9},{12,15},{14,13},{16,19},{18,... | collective-permute-start | bytes 491528 | tf_op jit(solution)/shard_map/ppermute | solution.py:449
  48.3 0.1 pad_add_fusion.1.where_ref
  48.4 0.0 collective-permute-done.12.refs_0_
  48.4 5.5 %project_own.1 = (f32[2,272,1152]{2,1,0:T(8,128)S(1)}, f32[2,272,1152]{2,1,0:T(8,128)S(1)}, bf16[2,2,640,1152]{3,2,1,0:T(8,128)(2,1)S(1)}) custom-call(s32[2]{0:T(128)S(1)} %pad_add_fusion.1.where_ref, bf16[640,128]{1,0:T(8,128)(2,1)S(1)} %collective-permute-done.12.refs_0_, bf16[640,256]{1,0:T(8,128)(2,1)S(1)} %merge.1.refs_1_, bf16[1280,1152]{1,0:T(8,128)(2,1)} %refs_2_.1, ...), custom_call_target="tpu_custom_call" | custom-call | tf_op jit(solution)/shard_map/project_own/pallas_call | solution.py:455
  53.9 0.0 collective-permute-done.10.refs_0_
  53.9 0.0 collective-permute-done.11.refs_1_
  53.9 0.0 copy-start.1
  53.9 4.2 %project_others.1 = (f32[2,272,1152]{2,1,0:T(8,128)}, f32[8,272]{1,0:T(8,128)S(1)}) custom-call(s32[2]{0:T(128)S(1)} %pad_add_fusion.1.where_ref, bf16[640,128]{1,0:T(8,128)(2,1)S(1)} %collective-permute-done.10.refs_0_, bf16[640,256]{1,0:T(8,128)(2,1)S(1)} %collective-permute-done.11.refs_1_, bf16[2,2,640,1152]{3,2,1,0:T(8,128)(2,1)S(1)} %get-tuple-element.39.refs_2_, ...), custom_call_target="tpu_custom_call" | custom-call | tf_op jit(solution)/shard_map/project_others/pallas_call | solution.py:468
  58.2 0.8 %collective-permute-start.13 = (f32[8,272]{1,0:T(8,128)S(1)}, f32[8,272]{1,0:T(8,128)S(1)}, u32[]{:S(2)}, u32[]{:S(2)}) collective-permute-start(f32[8,272]{1,0:T(8,128)S(1)} %get-tuple-element.43.refs_0_), channel_id=1, source_target_pairs={{0,2},{2,0},{1,3},{3,1},{4,6},{6,4},{5,7},{7,5},{8,10},{10,8},{9,1... | collective-permute-start | bytes 26120 | tf_op jit(solution)/shard_map/ppermute | solution.py:491
  59.0 0.0 copy-done.1
  59.0 1.9 %prepare.1 = (f32[2,256,1152]{2,1,0:T(8,128)S(1)}, f32[3,2,256,1152]{3,2,1,0:T(8,128)S(1)}) custom-call(f32[4,2304]{1,0:T(4,128)S(1)} %copy-done.1, f32[2,272,1152]{2,1,0:T(8,128)} %get-tuple-element.44.value_hbm), custom_call_target="tpu_custom_call" | custom-call | tf_op jit(solution)/shard_map/prepare/pallas_call | solution.py:499
  60.9 1.1 %collective-permute-done.13.refs_1_ = f32[8,272]{1,0:T(8,128)S(1)} collective-permute-done((f32[8,272]{1,0:T(8,128)S(1)}, f32[8,272]{1,0:T(8,128)S(1)}, u32[]{:S(2)}, u32[]{:S(2)}) %collective-permute-start.13) | collective-permute-done | bytes 8736 | tf_op jit(solution)/shard_map/ppermute | solution.py:491
  62.0 2.8 %finish.1 = bf16[256,2304]{1,0:T(8,128)(2,1)} custom-call(s32[1]{0:T(128)} %bitcast.keep_ref, f32[8,272]{1,0:T(8,128)S(1)} %get-tuple-element.43.refs_0_, f32[8,272]{1,0:T(8,128)S(1)} %collective-permute-done.13.refs_1_, f32[2,256,1152]{2,1,0:T(8,128)S(1)} %get-tuple-element.45.refs_2_, f32[3,2,256,1152]{3,2,1,0:T(8,128)S(1)} %get-tuple-element.46.refs_3_, ...), custom_call_target="tpu_custom_call" | custom-call | tf_op jit(solution)/shard_map/finish/pallas_call | solution.py:514
  (4 shorter events, 0.1 us)
Async XLA Ops:
  0.0 18.4 %collective-permute-start.2 = (bf16[1280,1152]{1,0:T(8,128)(2,1)}, bf16[1280,1152]{1,0:T(8,128)(2,1)}, u32[]{:S(2)}, u32[]{:S(2)}) collective-permute-start(bf16[1280,1152]{1,0:T(8,128)(2,1)} %refs_2_.1), channel_id=1, source_target_pairs={{0,1},{1,0},{2,3},{3,2},{4,5},{5,4},{6,7},{7,6},{8,9},{9,8},{10,11... | collective-permute-start | bytes 8847368 | tf_op jit(solution)/shard_map/ppermute | solution.py:419
  0.5 17.9 %collective-permute-start.3 = (bf16[1280,1152]{1,0:T(8,128)(2,1)}, bf16[1280,1152]{1,0:T(8,128)(2,1)}, u32[]{:S(2)}, u32[]{:S(2)}) collective-permute-start(bf16[1280,1152]{1,0:T(8,128)(2,1)} %refs_3_.1), channel_id=1, source_target_pairs={{0,1},{1,0},{2,3},{3,2},{4,5},{5,4},{6,7},{7,6},{8,9},{9,8},{10,11... | collective-permute-start | bytes 8847368 | tf_op jit(solution)/shard_map/ppermute | solution.py:420
  2.0 6.7 %collective-permute-start = (s32[8,256]{1,0:T(8,128)S(1)}, s32[8,256]{1,0:T(8,128)S(1)}, u32[]{:S(2)}, u32[]{:S(2)}) collective-permute-start(s32[8,256]{1,0:T(8,128)S(1)} %get-tuple-element.31.ids_ref), channel_id=1, source_target_pairs={{0,12},{4,8},{8,4},{12,0},{1,13},{5,9},{9,5},{13,1},{2,14},{6,10},... | collective-permute-start | bytes 24584 | tf_op jit(solution)/shard_map/ppermute | solution.py:341
  8.8 4.1 %collective-permute-start.1 = (s32[16,256]{1,0:T(8,128)S(1)}, s32[16,256]{1,0:T(8,128)S(1)}, u32[]{:S(2)}, u32[]{:S(2)}) collective-permute-start(s32[16,256]{1,0:T(8,128)S(1)} %pad_add_fusion), channel_id=1, source_target_pairs={{0,8},{1,9},{4,13},{5,12},{8,1},{9,0},{12,4},{13,5},{2,10},{3,11},... | collective-permute-start | bytes 49160 | tf_op jit(solution)/shard_map/ppermute | solution.py:326
  12.8 12.0 %collective-permute-start.8 = (bf16[640,256]{1,0:T(8,128)(2,1)S(1)}, bf16[640,256]{1,0:T(8,128)(2,1)S(1)}, u32[]{:S(2)}, u32[]{:S(2)}) collective-permute-start(bf16[640,256]{1,0:T(8,128)(2,1)S(1)} %pick_rows.4), channel_id=1, source_target_pairs={{0,4},{12,8},{1,5},{13,9},{2,6},{14,10},{3,7},{15,11},{16,20},{28,... | collective-permute-start | bytes 983048 | tf_op jit(solution)/shard_map/ppermute | solution.py:339
  16.8 9.5 %collective-permute-start.6 = (bf16[640,256]{1,0:T(8,128)(2,1)S(1)}, bf16[640,256]{1,0:T(8,128)(2,1)S(1)}, u32[]{:S(2)}, u32[]{:S(2)}) collective-permute-start(bf16[640,256]{1,0:T(8,128)(2,1)S(1)} %pick_rows.4), channel_id=1, source_target_pairs={{4,8},{8,4},{5,9},{9,5},{6,10},{10,6},{7,11},{11,7},{20,24},{24,20... | collective-permute-start | bytes 983048 | tf_op jit(solution)/shard_map/ppermute | solution.py:339
  18.4 7.9 %copy-start = (bf16[256,2304]{1,0:T(8,128)(2,1)S(1)}, bf16[256,2304]{1,0:T(8,128)(2,1)}, u32[]{:S(2)}) copy-start(bf16[256,2304]{1,0:T(8,128)(2,1)} %refs_4_.1) | copy-start | bytes 3538948
  19.3 12.6 %collective-permute-start.4 = (bf16[640,256]{1,0:T(8,128)(2,1)S(1)}, bf16[640,256]{1,0:T(8,128)(2,1)S(1)}, u32[]{:S(2)}, u32[]{:S(2)}) collective-permute-start(bf16[640,256]{1,0:T(8,128)(2,1)S(1)} %pick_rows.6), channel_id=1, source_target_pairs={{0,5},{1,4},{4,0},{5,1},{8,12},{9,13},{12,9},{13,8},{2,7},{3,6},{6... | collective-permute-start | bytes 983048 | tf_op jit(solution)/shard_map/ppermute | solution.py:326
  19.7 18.5 %collective-permute-start.5 = (bf16[640,256]{1,0:T(8,128)(2,1)S(1)}, bf16[640,256]{1,0:T(8,128)(2,1)S(1)}, u32[]{:S(2)}, u32[]{:S(2)}) collective-permute-start(bf16[640,256]{1,0:T(8,128)(2,1)S(1)} %pick_rows.5), channel_id=1, source_target_pairs={{0,9},{1,8},{12,5},{13,4},{2,11},{3,10},{14,7},{15,6},{16,25},{17,... | collective-permute-start | bytes 983048 | tf_op jit(solution)/shard_map/ppermute | solution.py:326
  24.9 18.9 %collective-permute-start.9 = (bf16[640,256]{1,0:T(8,128)(2,1)S(1)}, bf16[640,256]{1,0:T(8,128)(2,1)S(1)}, u32[]{:S(2)}, u32[]{:S(2)}) collective-permute-start(bf16[640,256]{1,0:T(8,128)(2,1)S(1)} %add.20), channel_id=1, source_target_pairs={{4,12},{8,0},{5,13},{9,1},{6,14},{10,2},{7,15},{11,3},{20,28},{24,... | collective-permute-start | bytes 983048 | tf_op jit(solution)/shard_map/ppermute | solution.py:339
  26.3 11.9 %collective-permute-start.7 = (bf16[16,2304]{1,0:T(8,128)(2,1)S(1)}, bf16[16,2304]{1,0:T(8,128)(2,1)S(1)}, u32[]{:S(2)}, u32[]{:S(2)}) collective-permute-start(bf16[16,2304]{1,0:T(8,128)(2,1)S(1)} %slice.6), channel_id=1, source_target_pairs={{0,1},{4,5},{8,9},{12,13},{2,3},{6,7},{10,11},{14,15},{16,17},{20,... | collective-permute-start | bytes 221192 | tf_op jit(solution)/shard_map/ppermute | solution.py:425
  43.9 10.0 %collective-permute-start.11 = (bf16[640,256]{1,0:T(8,128)(2,1)S(1)}, bf16[640,256]{1,0:T(8,128)(2,1)S(1)}, u32[]{:S(2)}, u32[]{:S(2)}) collective-permute-start(bf16[640,256]{1,0:T(8,128)(2,1)S(1)} %merge.1.refs_1_), channel_id=1, source_target_pairs={{0,2},{2,0},{1,3},{3,1},{4,6},{6,4},{5,7},{7,5},{8,10},{10,8},{9,1... | collective-permute-start | bytes 983048 | tf_op jit(solution)/shard_map/ppermute | solution.py:436
  45.5 2.9 %collective-permute-start.12 = (bf16[640,128]{1,0:T(8,128)(2,1)S(1)}, bf16[640,128]{1,0:T(8,128)(2,1)S(1)}, u32[]{:S(2)}, u32[]{:S(2)}) collective-permute-start(bf16[640,128]{1,0:T(8,128)(2,1)S(1)} %slice.8), channel_id=1, source_target_pairs={{0,1},{2,3},{4,5},{6,7},{8,9},{10,11},{12,13},{14,15},{16,17},{18,... | collective-permute-start | bytes 491528 | tf_op jit(solution)/shard_map/ppermute | solution.py:449
  46.8 7.1 %collective-permute-start.10 = (bf16[640,128]{1,0:T(8,128)(2,1)S(1)}, bf16[640,128]{1,0:T(8,128)(2,1)S(1)}, u32[]{:S(2)}, u32[]{:S(2)}) collective-permute-start(bf16[640,128]{1,0:T(8,128)(2,1)S(1)} %slice.8), channel_id=1, source_target_pairs={{0,3},{2,1},{4,7},{6,5},{8,11},{10,9},{12,15},{14,13},{16,19},{18,... | collective-permute-start | bytes 491528 | tf_op jit(solution)/shard_map/ppermute | solution.py:449
  53.9 5.0 %copy-start.1 = (f32[4,2304]{1,0:T(4,128)S(1)}, f32[4,2304]{1,0:T(4,128)}, u32[]{:S(2)}) copy-start(f32[4,2304]{1,0:T(4,128)} %refs_5_.1) | copy-start | bytes 110596
  58.2 3.8 %collective-permute-start.13 = (f32[8,272]{1,0:T(8,128)S(1)}, f32[8,272]{1,0:T(8,128)S(1)}, u32[]{:S(2)}, u32[]{:S(2)}) collective-permute-start(f32[8,272]{1,0:T(8,128)S(1)} %get-tuple-element.43.refs_0_), channel_id=1, source_target_pairs={{0,2},{2,0},{1,3},{3,1},{4,6},{6,4},{5,7},{7,5},{8,10},{10,8},{9,1... | collective-permute-start | bytes 26120 | tf_op jit(solution)/shard_map/ppermute | solution.py:491

commit v20 on v18

--- a/solution.py
+++ b/solution.py
@@ -121,87 +121,109 @@
     refs[-1][...] = total.astype(BF16)
 
 
-def project_kernel(shifts, count, where_ref, *refs):
-    pieces = len(shifts)
-    first = 0 in shifts
-    rims = refs[:pieces]
-    bodies = refs[pieces : 2 * pieces]
-    refs = refs[2 * pieces :]
-    depth, tokens = bodies[0].shape
+def fetch(count, tp, depth, source, target, shifts, sems):
+    copies = []
+    for n, s in enumerate(shifts):
+        owner = lax.rem(tp + count - s, count)
+        rows = pl.ds(pl.multiple_of(owner * depth, depth), depth)
+        copy = pltpu.make_async_copy(
+            source.at[rows, :], target.at[pl.ds(n * depth, depth), :], sems.at[n]
+        )
+        copy.start()
+        copies.append(copy)
+    return copies
+
+
+def await_all(copies):
+    for copy in copies:
+        copy.wait()
+
+
+def with_rim(rims, bodies):
+    body = jnp.concatenate([b[...].astype(F32) for b in bodies], axis=0).T.astype(BF16)
+    rim = jnp.concatenate([r[...].astype(F32) for r in rims], axis=0).T.astype(BF16)
+    return jnp.concatenate([rim[LANES - RIM :], body], axis=0)
+
+
+def project_own_kernel(count, where_ref, rim_ref, body_ref, *refs):
+    weights, hidden_halo, hidden = refs[:4], refs[4], refs[5]
+    key_ref, value_ref, next_ref, states_ref, power_ref, held, sems, next_sems = refs[6:]
+    half = value_ref.shape[-1]
+    depth = body_ref.shape[0]
     rep = where_ref[0]
     tp = where_ref[1]
-    if first:
-        weights = refs[:4]
-        key_ref, value_ref, rest, held, sems, rest_sems = refs[4:]
-        half = held.shape[-1]
-
-        def bring(target, far, which, n, s, sem):
-            owner = lax.rem(tp + count - s, count)
-            rows = pl.ds(pl.multiple_of(owner * depth, depth), depth)
-            copy = pltpu.make_async_copy(
-                weights[2 * far + which].at[rows, :],
-                target.at[far, which, pl.ds(n * depth, depth), :],
-                sem,
-            )
-            copy.start()
-            return copy
-
-        copies = [
-            bring(held, far, which, 0, 0, sems.at[2 * far + which])
-            for far in range(2)
-            for which in (1, 0)
-        ]
-        later = []
-    else:
-        later = []
-        rest, begun_keys, begun_values, hidden_halo, hidden = refs[:5]
-        value_hbm, stats_ref, states, done, done_sems = refs[5:]
-        held = rest
-        half = held.shape[-1]
-        for slot in range(2):
-            states[slot, :RIM] = hidden_halo[:, slot * half : (slot + 1) * half]
-            states[slot, RIM:] = hidden[:, slot * half : (slot + 1) * half]
-    body = jnp.concatenate([b[...].astype(F32) for b in bodies], axis=0).T.astype(BF16)
-    rim = jnp.concatenate([r[...].astype(F32) for r in rims], axis=0).T.astype(BF16)
-    memory = jnp.concatenate([rim[LANES - RIM :], body], axis=0)
-    sums = [0.0] * 4
+    order = [(far, which) for far in range(2) for which in (1, 0)]
+    copies = {
+        (far, which): fetch(
+            count, tp, depth, weights[2 * far + which], held.at[far, which], (0,),
+            sems.at[2 * far + which],
+        )
+        for far, which in order
+    }
+    power = 0.0
+    for slot in range(2):
+        span = slice(slot * half, (slot + 1) * half)
+        states_ref[slot, :RIM] = hidden_halo[:, span]
+        states_ref[slot, RIM:] = hidden[:, span]
+        here = states_ref[slot].astype(F32)
+        power = power + jnp.sum(here * here, axis=1, keepdims=True)
+    power_ref[...] = jnp.broadcast_to(power, power_ref.shape)
+    memory = with_rim([rim_ref], [body_ref])
+    later = []
+    for far, which in order:
+        slot = rep if far == 0 else 1 - rep
+        await_all(copies[far, which])
+        if not later:
+            for w in (1, 0):
+                later += fetch(
+                    count, tp, depth, weights[w], next_ref.at[w], range(1, count), next_sems.at[w]
+                )
+        target = value_ref if which == 1 else key_ref
+        target[slot] = dot(memory, held[far, which])
+    await_all(later)
+
+
+def project_others_kernel(count, where_ref, *refs):
+    pieces = count - 1
+    rims, bodies = refs[:pieces], refs[pieces : 2 * pieces]
+    weights = refs[2 * pieces : 2 * pieces + 2]
+    next_ref, begun_keys, begun_values, states_ref, power_ref = refs[2 * pieces + 2 :][:5]
+    value_hbm, stats_ref, held, sems, done, done_sems = refs[2 * pieces + 7 :]
+    half = held.shape[-1]
+    depth = bodies[0].shape[0]
+    rep = where_ref[0]
+    tp = where_ref[1]
+    copies = {
+        which: fetch(
+            count, tp, depth, weights[which], held.at[which], range(1, count), sems.at[which]
+        )
+        for which in (1, 0)
+    }
+    memory = with_rim(rims, bodies)
+    sums = [0.0] * 3
+    later = []
     for far in range(2):
         slot = rep if far == 0 else 1 - rep
         fields = [None, None]
         for which in (1, 0):
-            if first:
-                copies[2 * far + 1 - which].wait()
-                if far == 0 and which == 1:
-                    later = [
-                        bring(rest, f, w, n, n + 1, rest_sems.at[(2 * f + w) * (count - 1) + n])
-                        for f in range(2)
-                        for w in (1, 0)
-                        for n in range(count - 1)
-                    ]
-            fields[which] = dot(memory, held[far, which])
-            if not first and which == 1:
+            if far == 1:
+                await_all(copies[which])
+            fields[which] = dot(memory, next_ref[which] if far == 0 else held[which])
+            if which == 1:
                 done[far] = fields[1] + begun_values[slot]
                 copy = pltpu.make_async_copy(done.at[far], value_hbm.at[slot], done_sems.at[far])
                 copy.start()
                 later.append(copy)
-        if first:
-            value_ref[slot] = fields[1]
-            key_ref[slot] = fields[0]
-        else:
-            keys = fields[0] + begun_keys[slot]
-            values = done[far]
-            here = states[slot].astype(F32)
-            terms = (here * here, keys * keys, here * keys, values * values)
-            sums = [a + jnp.sum(t, axis=1, keepdims=True) for a, t in zip(sums, terms)]
-    if not first:
-        rows = memory.shape[0]
-        lane = iota((rows, 8), 1)
-        packed = jnp.zeros((rows, 8), F32)
-        for k in range(4):
-            packed = jnp.where(lane == k, sums[k], packed)
-        stats_ref[...] = dot_nt(unit(8, F32), packed, lax.Precision.HIGHEST)
-    for copy in later:
-        copy.wait()
+        keys = fields[0] + begun_keys[slot]
+        values = done[far]
+        terms = (keys * keys, states_ref[slot].astype(F32) * keys, values * values)
+        sums = [a + jnp.sum(t, axis=1, keepdims=True) for a, t in zip(sums, terms)]
+    packed = power_ref[...]
+    lane = iota(packed.shape, 1)
+    for k in range(3):
+        packed = jnp.where(lane == k + 1, sums[k], packed)
+    stats_ref[...] = dot_nt(unit(8, F32), packed, lax.Precision.HIGHEST)
+    await_all(later)
 
 
 def prepare_kernel(chunk, taps_ref, value_hbm, value_ref, tap_ref, rows_ref, sems):
@@ -454,40 +476,39 @@
     rims = [next_rim(rim, s) for s in range(tps)]
     others = tps - 1
     field = jax.ShapeDtypeStruct((2, extended, half), F32)
-    *begun, rest = pl.pallas_call(
-        functools.partial(project_kernel, (0,), tps),
-        in_specs=[smem] + [resident] * 2 + [anywhere] * 4,
-        out_specs=(resident,) * 3,
-        out_shape=(field, field, pltpu.VMEM((2, 2, others * depth, half), BF16)),
+    *begun, following, states, power = pl.pallas_call(
+        functools.partial(project_own_kernel, tps),
+        in_specs=[smem] + [resident] * 2 + [anywhere] * 4 + [resident] * 2,
+        out_specs=(resident,) * 5,
+        out_shape=(
+            field,
+            field,
+            pltpu.VMEM((2, others * depth, half), BF16),
+            jax.ShapeDtypeStruct((2, extended, half), BF16),
+            jax.ShapeDtypeStruct((extended, 8), F32),
+        ),
         scratch_shapes=[
             pltpu.VMEM((2, 2, depth, half), BF16),
-            pltpu.SemaphoreType.DMA((4,)),
-            pltpu.SemaphoreType.DMA((4 * others,)),
+            pltpu.SemaphoreType.DMA((4, 1)),
+            pltpu.SemaphoreType.DMA((2, others)),
         ],
         compiler_params=limit(12),
         name="project_own",
-    )(where, rims[0], memory, *weights)
+    )(where, rims[0], memory, *weights, hidden_halo, hidden)
     values, stats = pl.pallas_call(
-        functools.partial(project_kernel, tuple(range(1, tps)), tps),
-        in_specs=[smem] + [resident] * (2 * others + 5),
+        functools.partial(project_others_kernel, tps),
+        in_specs=[smem] + [resident] * (2 * others) + [anywhere] * 2 + [resident] * 5,
         out_specs=(pl.BlockSpec(memory_space=pltpu.HBM), resident),
         out_shape=(pltpu.HBM(field.shape, F32), jax.ShapeDtypeStruct((8, extended), F32)),
         scratch_shapes=[
-            pltpu.VMEM((2, extended, half), BF16),
+            pltpu.VMEM((2, others * depth, half), BF16),
+            pltpu.SemaphoreType.DMA((2, others)),
             pltpu.VMEM((2, extended, half), F32),
             pltpu.SemaphoreType.DMA((2,)),
         ],
         compiler_params=limit(14),
         name="project_others",
-    )(
-        where,
-        *rims[1:],
-        *bodies[1:],
-        rest,
-        *begun,
-        hidden_halo,
-        hidden,
-    )
+    )(where, *rims[1:], *bodies[1:], *weights[2:], following, *begun, states, power)
 
     all_stats = [stats] + [
         lax.ppermute(stats, "tp", [(i, (i + s) % tps) for i in range(tps)]) for s in range(1, tps)

time: 59.8 us -> 61.6 us (1.030)
  Pallas kernels: 20.5 us -> 22.3 us
  waiting for transfers between devices: 15.5 us -> 14.1 us
  starting transfers between devices: 22.9 us -> 24.2 us
    ppermute x2, waiting for transfers between devices: 3.36 us -> 0.97 us  [crossing(): lax.ppermute(x, ('mem', 'rep'), [(2 * a + b, 2 * c + d) for a, b, c, d in...]
    ppermute x4, starting transfers between devices: 4.76 us -> 6.85 us  [send(): return lax.ppermute(x, 'mem', pairs)]
    ppermute x1, starting transfers between devices: 2.12 us -> 4.12 us  [meanwhile(): return lax.ppermute(tail, ('mem', 'rep'), needed)]
    pallas_call x2, Pallas kernels: 9.75 us -> 11.5 us  [the longest x1 5.93 us: shards(): pl.pallas_call(functools.partial(project_others_kernel, tps), in_specs=[s...]
    ppermute x2, starting transfers between devices: 3.71 us -> 2.37 us  [crossing(): lax.ppermute(x, ('mem', 'rep'), [(2 * a + b, 2 * c + d) for a, b, c, d in...]
    ppermute x2, waiting for transfers between devices: 0.52 us -> 1.28 us  [ask(): return lax.ppermute(ids, 'mem', [(i, i ^ x) for i in range(4)])]
  transfers between devices with their start and end apart: 15 -> 15, of which waited for: 6 -> 7; matrix products, arithmetic and copies ran while one was open for 0% -> 0% of each run, Pallas kernels for 22% -> 22%
where the time goes in v20:
time: 61.6 us; the launch traced here: 61.2 us
  starting transfers between devices  24.2 us (39%)
  Pallas kernels  22.3 us (36%)
  waiting for transfers between devices  14.1 us (23%)
    ppermute x4, waiting for transfers between devices, send(): return lax.ppermute(x, 'mem', pairs)  11 us
    ppermute x4, starting transfers between devices, send(): return lax.ppermute(x, 'mem', pairs)  6.85 us
    pallas_call x1, Pallas kernels, shards(): pl.pallas_call(functools.partial(project_others_kernel, tps), in_specs=[s...  5.93 us
    pallas_call x1, Pallas kernels, shards(): pl.pallas_call(functools.partial(project_own_kernel, tps), in_specs=[smem...  5.62 us
    ppermute x2, starting transfers between devices, ask(): return lax.ppermute(ids, 'mem', [(i, i ^ x) for i in range(4)])  5.12 us
    ppermute x1, starting transfers between devices, meanwhile(): return lax.ppermute(tail, ('mem', 'rep'), needed)  4.12 us
    pallas_call x4, Pallas kernels, pick(): pl.pallas_call(pick_kernel, in_specs=[pl.BlockSpec(memory_space=pltpu.SME...  3.45 us
    pallas_call x1, Pallas kernels, shards(): pl.pallas_call(functools.partial(finish_kernel, tps, step), in_specs=[sme...  2.84 us
  transfers between devices with their start and end apart: 15, of which 7 were waited for; matrix products, arithmetic and copies ran while one was open for 0% of the time, Pallas kernels for 22%

profile of v20, /device:TPU:0, one launch (start us, length us, event | category | flops | bytes accessed | tf_op | source)
XLA Modules:
  0.0 61.2 jit_solution(6918115923976301368)
XLA Ops:
  0.0 0.5 collective-permute-start.3
  0.5 0.1 collective-permute-start.4
  0.5 1.5 %place_rows.1 = (s32[8,256]{1,0:T(8,128)S(1)}, bf16[8,80,1024]{2,1,0:T(8,128)(2,1)S(1)}, bf16[5,8,1024]{2,1,0:T(8,128)(2,1)S(1)}) custom-call(s32[8,256]{1,0:T(8,128)} %bitcast.11, s32[32,128]{1,0:T(8,128)} %bitcast.10, bf16[8,80,1024]{2,1,0:T(8,128)(2,1)} %bitcast.8, bf16[5,8,1024]{2,1,0:T(8,128)(2,1)} %bitcast.9), custom_call_target="tpu_custom_call" | custom-call | tf_op jit(solution)/shard_map/place_rows/pallas_call | solution.py:417
  2.0 5.1 %collective-permute-start = (s32[8,256]{1,0:T(8,128)S(1)}, s32[8,256]{1,0:T(8,128)S(1)}, u32[]{:S(2)}, u32[]{:S(2)}) collective-permute-start(s32[8,256]{1,0:T(8,128)S(1)} %get-tuple-element.39.ids_ref), channel_id=1, source_target_pairs={{0,12},{4,8},{8,4},{12,0},{1,13},{5,9},{9,5},{13,1},{2,14},{6,10},... | collective-permute-start | bytes 24584 | tf_op jit(solution)/shard_map/ppermute | solution.py:348
  7.1 0.0 collective-permute-start.2
  7.2 0.6 %collective-permute-start.1 = (s32[8,256]{1,0:T(8,128)S(1)}, s32[8,256]{1,0:T(8,128)S(1)}, u32[]{:S(2)}, u32[]{:S(2)}) collective-permute-start(s32[8,256]{1,0:T(8,128)S(1)} %get-tuple-element.39.ids_ref), channel_id=1, source_target_pairs={{0,8},{1,9},{4,13},{5,12},{8,1},{9,0},{12,4},{13,5},{2,10},{3,11},... | collective-permute-start | bytes 24584 | tf_op jit(solution)/shard_map/ppermute | solution.py:351
  7.8 0.9 %decode_tables.1.table_ref = bf16[8,80,1024]{2,1,0:T(8,128)(2,1)S(1)} custom-call(bf16[8,80,1024]{2,1,0:T(8,128)(2,1)S(1)} %get-tuple-element.31.codes_ref, bf16[5,8,1024]{2,1,0:T(8,128)(2,1)S(1)} %get-tuple-element.32.scales_ref), custom_call_target="tpu_custom_call" | custom-call | tf_op jit(solution)/shard_map/decode_tables/pallas_call | solution.py:434
  8.7 0.1 collective-permute-done.ids_ref
  8.8 0.9 %pick_rows.4 = bf16[640,256]{1,0:T(8,128)(2,1)S(1)} custom-call(s32[1]{0:T(128)} %bitcast.3.base_ref, s32[8,256]{1,0:T(8,128)S(1)} %collective-permute-done.ids_ref, bf16[8,80,1024]{2,1,0:T(8,128)(2,1)S(1)} %decode_tables.1.table_ref), custom_call_target="tpu_custom_call" | custom-call | tf_op jit(solution)/shard_map/pick_rows/pallas_call | solution.py:354
  9.6 1.2 %collective-permute-done.2.ids_ref = s32[8,256]{1,0:T(8,128)S(1)} collective-permute-done((s32[8,256]{1,0:T(8,128)S(1)}, s32[8,256]{1,0:T(8,128)S(1)}, u32[]{:S(2)}, u32[]{:S(2)}) %collective-permute-start.2) | collective-permute-done | bytes 8224 | tf_op jit(solution)/shard_map/ppermute | solution.py:348
  10.8 0.3 collective-permute-done.1.ids_ref
  11.1 4.5 %collective-permute-start.9 = (bf16[640,256]{1,0:T(8,128)(2,1)S(1)}, bf16[640,256]{1,0:T(8,128)(2,1)S(1)}, u32[]{:S(2)}, u32[]{:S(2)}) collective-permute-start(bf16[640,256]{1,0:T(8,128)(2,1)S(1)} %pick_rows.4), channel_id=1, source_target_pairs={{0,4},{12,8},{1,5},{13,9},{2,6},{14,10},{3,7},{15,11},{16,20},{28,... | collective-permute-start | bytes 983048 | tf_op jit(solution)/shard_map/ppermute | solution.py:364
  15.6 0.7 %collective-permute-start.7 = (bf16[640,256]{1,0:T(8,128)(2,1)S(1)}, bf16[640,256]{1,0:T(8,128)(2,1)S(1)}, u32[]{:S(2)}, u32[]{:S(2)}) collective-permute-start(bf16[640,256]{1,0:T(8,128)(2,1)S(1)} %pick_rows.4), channel_id=1, source_target_pairs={{4,8},{8,4},{5,9},{9,5},{6,10},{10,6},{7,11},{11,7},{20,24},{24,20... | collective-permute-start | bytes 983048 | tf_op jit(solution)/shard_map/ppermute | solution.py:364
  16.3 0.9 %pick_rows.5 = bf16[640,256]{1,0:T(8,128)(2,1)S(1)} custom-call(s32[1]{0:T(128)} %bitcast.3.base_ref, s32[8,256]{1,0:T(8,128)S(1)} %collective-permute-done.1.ids_ref, bf16[8,80,1024]{2,1,0:T(8,128)(2,1)S(1)} %decode_tables.1.table_ref), custom_call_target="tpu_custom_call" | custom-call | tf_op jit(solution)/shard_map/pick_rows/pallas_call | solution.py:354
  17.2 0.0 copy-start
  17.2 1.7 %collective-permute-start.5 = (bf16[640,256]{1,0:T(8,128)(2,1)S(1)}, bf16[640,256]{1,0:T(8,128)(2,1)S(1)}, u32[]{:S(2)}, u32[]{:S(2)}) collective-permute-start(bf16[640,256]{1,0:T(8,128)(2,1)S(1)} %pick_rows.5), channel_id=1, source_target_pairs={{0,9},{1,8},{12,5},{13,4},{2,11},{3,10},{14,7},{15,6},{16,25},{17,... | collective-permute-start | bytes 983048 | tf_op jit(solution)/shard_map/ppermute | solution.py:351
  19.0 0.0 collective-permute-done.3.refs_2_
  19.0 0.0 collective-permute-done.4.refs_3_
  19.0 0.9 %pick_rows.6 = bf16[640,256]{1,0:T(8,128)(2,1)S(1)} custom-call(s32[1]{0:T(128)} %bitcast.3.base_ref, s32[8,256]{1,0:T(8,128)S(1)} %collective-permute-done.2.ids_ref, bf16[8,80,1024]{2,1,0:T(8,128)(2,1)S(1)} %decode_tables.1.table_ref), custom_call_target="tpu_custom_call" | custom-call | tf_op jit(solution)/shard_map/pick_rows/pallas_call | solution.py:354
  19.8 0.4 collective-permute-start.6
  20.2 0.9 %pick_rows.7 = bf16[640,256]{1,0:T(8,128)(2,1)S(1)} custom-call(s32[1]{0:T(128)} %bitcast.3.base_ref, s32[8,256]{1,0:T(8,128)S(1)} %get-tuple-element.39.ids_ref, bf16[8,80,1024]{2,1,0:T(8,128)(2,1)S(1)} %decode_tables.1.table_ref), custom_call_target="tpu_custom_call" | custom-call | tf_op jit(solution)/shard_map/pick_rows/pallas_call | solution.py:354
  21.1 0.0 collective-permute-done.9
  21.1 0.1 add.20
  21.2 1.3 %collective-permute-start.10 = (bf16[640,256]{1,0:T(8,128)(2,1)S(1)}, bf16[640,256]{1,0:T(8,128)(2,1)S(1)}, u32[]{:S(2)}, u32[]{:S(2)}) collective-permute-start(bf16[640,256]{1,0:T(8,128)(2,1)S(1)} %add.20), channel_id=1, source_target_pairs={{4,12},{8,0},{5,13},{9,1},{6,14},{10,2},{7,15},{11,3},{20,28},{24,... | collective-permute-start | bytes 983048 | tf_op jit(solution)/shard_map/ppermute | solution.py:364
  22.5 0.0 copy-done
  22.5 0.0 collective-permute-done.7.refs_1_
  22.5 4.1 %collective-permute-start.8 = (bf16[16,2304]{1,0:T(8,128)(2,1)S(1)}, bf16[16,2304]{1,0:T(8,128)(2,1)S(1)}, u32[]{:S(2)}, u32[]{:S(2)}) collective-permute-start(bf16[16,2304]{1,0:T(8,128)(2,1)S(1)} %slice.6), channel_id=1, source_target_pairs={{0,1},{4,5},{8,9},{12,13},{2,3},{6,7},{10,11},{14,15},{16,17},{20,... | collective-permute-start | bytes 221192 | tf_op jit(solution)/shard_map/ppermute | solution.py:449
  26.6 0.6 %collective-permute-done.5 = bf16[640,256]{1,0:T(8,128)(2,1)S(1)} collective-permute-done((bf16[640,256]{1,0:T(8,128)(2,1)S(1)}, bf16[640,256]{1,0:T(8,128)(2,1)S(1)}, u32[]{:S(2)}, u32[]{:S(2)}) %collective-permute-start.5) | collective-permute-done | bytes 327712 | tf_op jit(solution)/shard_map/ppermute | solution.py:351
  27.3 7.0 %collective-permute-done.6 = bf16[640,256]{1,0:T(8,128)(2,1)S(1)} collective-permute-done((bf16[640,256]{1,0:T(8,128)(2,1)S(1)}, bf16[640,256]{1,0:T(8,128)(2,1)S(1)}, u32[]{:S(2)}, u32[]{:S(2)}) %collective-permute-start.6) | collective-permute-done | bytes 327712 | tf_op jit(solution)/shard_map/ppermute | solution.py:364
  34.3 0.0 collective-permute-done.8.refs_4_
  34.4 3.9 %collective-permute-done.10.refs_2_ = bf16[640,256]{1,0:T(8,128)(2,1)S(1)} collective-permute-done((bf16[640,256]{1,0:T(8,128)(2,1)S(1)}, bf16[640,256]{1,0:T(8,128)(2,1)S(1)}, u32[]{:S(2)}, u32[]{:S(2)}) %collective-permute-start.10) | collective-permute-done | bytes 327712 | tf_op jit(solution)/shard_map/ppermute | solution.py:364
  38.3 0.1 merge.1.body_ref
  38.4 1.6 %collective-permute-start.12 = (bf16[640,256]{1,0:T(8,128)(2,1)S(1)}, bf16[640,256]{1,0:T(8,128)(2,1)S(1)}, u32[]{:S(2)}, u32[]{:S(2)}) collective-permute-start(bf16[640,256]{1,0:T(8,128)(2,1)S(1)} %merge.1.body_ref), channel_id=1, source_target_pairs={{0,2},{2,0},{1,3},{3,1},{4,6},{6,4},{5,7},{7,5},{8,10},{10,8},{9,1... | collective-permute-start | bytes 983048 | tf_op jit(solution)/shard_map/ppermute | solution.py:460
  40.0 1.3 %collective-permute-start.13 = (bf16[640,128]{1,0:T(8,128)(2,1)S(1)}, bf16[640,128]{1,0:T(8,128)(2,1)S(1)}, u32[]{:S(2)}, u32[]{:S(2)}) collective-permute-start(bf16[640,128]{1,0:T(8,128)(2,1)S(1)} %slice.8), channel_id=1, source_target_pairs={{0,1},{2,3},{4,5},{6,7},{8,9},{10,11},{12,13},{14,15},{16,17},{18,... | collective-permute-start | bytes 491528 | tf_op jit(solution)/shard_map/ppermute | solution.py:473
  41.3 1.5 %collective-permute-start.11 = (bf16[640,128]{1,0:T(8,128)(2,1)S(1)}, bf16[640,128]{1,0:T(8,128)(2,1)S(1)}, u32[]{:S(2)}, u32[]{:S(2)}) collective-permute-start(bf16[640,128]{1,0:T(8,128)(2,1)S(1)} %slice.8), channel_id=1, source_target_pairs={{0,3},{2,1},{4,7},{6,5},{8,11},{10,9},{12,15},{14,13},{16,19},{18,... | collective-permute-start | bytes 491528 | tf_op jit(solution)/shard_map/ppermute | solution.py:473
  42.8 0.1 pad_add_fusion.where_ref
  42.9 0.0 collective-permute-done.13.rim_ref
  42.9 5.6 %project_own.1 = (f32[2,272,1152]{2,1,0:T(8,128)S(1)}, f32[2,272,1152]{2,1,0:T(8,128)S(1)}, bf16[2,640,1152]{2,1,0:T(8,128)(2,1)S(1)}, bf16[2,272,1152]{2,1,0:T(8,128)(2,1)S(1)}, f32[272,8]{1,0:T(8,128)S(1)}) custom-call(s32[2]{0:T(128)S(1)} %pad_add_fusion.where_ref, bf16[640,128]{1,0:T(8,128)(2,1)S(1)} %collective-permute-done.13.rim_ref, ...), custom_call_target="tpu_custom_call" | custom-call | tf_op jit(solution)/shard_map/project_own/pallas_call | solution.py:479
  48.5 0.0 collective-permute-done.11.refs_0_
  48.5 0.0 collective-permute-done.12.refs_1_
  48.5 0.0 copy-start.1
  48.5 5.9 %project_others.1 = (f32[2,272,1152]{2,1,0:T(8,128)}, f32[8,272]{1,0:T(8,128)S(1)}) custom-call(s32[2]{0:T(128)S(1)} %pad_add_fusion.where_ref, bf16[640,128]{1,0:T(8,128)(2,1)S(1)} %collective-permute-done.11.refs_0_, bf16[640,256]{1,0:T(8,128)(2,1)S(1)} %collective-permute-done.12.refs_1_, bf16[1280,1152]{1,0:T(8,128)(2,1)} %collective-permute-done.3.refs_2_, ...), custom_call_target="tpu_custom_call" | custom-call | tf_op jit(solution)/shard_map/project_others/pallas_call | solution.py:498
  54.5 0.9 %collective-permute-start.14 = (f32[8,272]{1,0:T(8,128)S(1)}, f32[8,272]{1,0:T(8,128)S(1)}, u32[]{:S(2)}, u32[]{:S(2)}) collective-permute-start(f32[8,272]{1,0:T(8,128)S(1)} %get-tuple-element.51.refs_0_), channel_id=1, source_target_pairs={{0,2},{2,0},{1,3},{3,1},{4,6},{6,4},{5,7},{7,5},{8,10},{10,8},{9,1... | collective-permute-start | bytes 26120 | tf_op jit(solution)/shard_map/ppermute | solution.py:514
  55.4 0.0 copy-done.1
  55.4 1.9 %prepare.1 = (f32[2,256,1152]{2,1,0:T(8,128)S(1)}, f32[3,2,256,1152]{3,2,1,0:T(8,128)S(1)}) custom-call(f32[4,2304]{1,0:T(4,128)S(1)} %copy-done.1, f32[2,272,1152]{2,1,0:T(8,128)} %get-tuple-element.52.value_hbm), custom_call_target="tpu_custom_call" | custom-call | tf_op jit(solution)/shard_map/prepare/pallas_call | solution.py:522
  57.3 0.9 %collective-permute-done.14.refs_1_ = f32[8,272]{1,0:T(8,128)S(1)} collective-permute-done((f32[8,272]{1,0:T(8,128)S(1)}, f32[8,272]{1,0:T(8,128)S(1)}, u32[]{:S(2)}, u32[]{:S(2)}) %collective-permute-start.14) | collective-permute-done | bytes 8736 | tf_op jit(solution)/shard_map/ppermute | solution.py:514
  58.2 2.8 %finish.1 = bf16[256,2304]{1,0:T(8,128)(2,1)} custom-call(s32[1]{0:T(128)} %bitcast.keep_ref, f32[8,272]{1,0:T(8,128)S(1)} %get-tuple-element.51.refs_0_, f32[8,272]{1,0:T(8,128)S(1)} %collective-permute-done.14.refs_1_, f32[2,256,1152]{2,1,0:T(8,128)S(1)} %get-tuple-element.53.refs_2_, f32[3,2,256,1152]{3,2,1,0:T(8,128)S(1)} %get-tuple-element.54.refs_3_, ...), custom_call_target="tpu_custom_call" | custom-call | tf_op jit(solution)/shard_map/finish/pallas_call | solution.py:537
  (3 shorter events, 0.1 us)
Async XLA Ops:
  0.0 19.0 %collective-permute-start.3 = (bf16[1280,1152]{1,0:T(8,128)(2,1)}, bf16[1280,1152]{1,0:T(8,128)(2,1)}, u32[]{:S(2)}, u32[]{:S(2)}) collective-permute-start(bf16[1280,1152]{1,0:T(8,128)(2,1)} %refs_0_.1), channel_id=1, source_target_pairs={{0,1},{1,0},{2,3},{3,2},{4,5},{5,4},{6,7},{7,6},{8,9},{9,8},{10,11... | collective-permute-start | bytes 8847368 | tf_op jit(solution)/shard_map/ppermute | solution.py:443
  0.5 18.5 %collective-permute-start.4 = (bf16[1280,1152]{1,0:T(8,128)(2,1)}, bf16[1280,1152]{1,0:T(8,128)(2,1)}, u32[]{:S(2)}, u32[]{:S(2)}) collective-permute-start(bf16[1280,1152]{1,0:T(8,128)(2,1)} %refs_1_.1), channel_id=1, source_target_pairs={{0,1},{1,0},{2,3},{3,2},{4,5},{5,4},{6,7},{7,6},{8,9},{9,8},{10,11... | collective-permute-start | bytes 8847368 | tf_op jit(solution)/shard_map/ppermute | solution.py:444
  2.0 6.7 %collective-permute-start = (s32[8,256]{1,0:T(8,128)S(1)}, s32[8,256]{1,0:T(8,128)S(1)}, u32[]{:S(2)}, u32[]{:S(2)}) collective-permute-start(s32[8,256]{1,0:T(8,128)S(1)} %get-tuple-element.39.ids_ref), channel_id=1, source_target_pairs={{0,12},{4,8},{8,4},{12,0},{1,13},{5,9},{9,5},{13,1},{2,14},{6,10},... | collective-permute-start | bytes 24584 | tf_op jit(solution)/shard_map/ppermute | solution.py:348
  7.1 3.7 %collective-permute-start.2 = (s32[8,256]{1,0:T(8,128)S(1)}, s32[8,256]{1,0:T(8,128)S(1)}, u32[]{:S(2)}, u32[]{:S(2)}) collective-permute-start(s32[8,256]{1,0:T(8,128)S(1)} %get-tuple-element.39.ids_ref), channel_id=1, source_target_pairs={{0,4},{4,0},{8,12},{12,8},{1,5},{5,1},{9,13},{13,9},{2,6},{6,2},{1... | collective-permute-start | bytes 24584 | tf_op jit(solution)/shard_map/ppermute | solution.py:348
  7.2 4.0 %collective-permute-start.1 = (s32[8,256]{1,0:T(8,128)S(1)}, s32[8,256]{1,0:T(8,128)S(1)}, u32[]{:S(2)}, u32[]{:S(2)}) collective-permute-start(s32[8,256]{1,0:T(8,128)S(1)} %get-tuple-element.39.ids_ref), channel_id=1, source_target_pairs={{0,8},{1,9},{4,13},{5,12},{8,1},{9,0},{12,4},{13,5},{2,10},{3,11},... | collective-permute-start | bytes 24584 | tf_op jit(solution)/shard_map/ppermute | solution.py:351
  11.1 9.9 %collective-permute-start.9 = (bf16[640,256]{1,0:T(8,128)(2,1)S(1)}, bf16[640,256]{1,0:T(8,128)(2,1)S(1)}, u32[]{:S(2)}, u32[]{:S(2)}) collective-permute-start(bf16[640,256]{1,0:T(8,128)(2,1)S(1)} %pick_rows.4), channel_id=1, source_target_pairs={{0,4},{12,8},{1,5},{13,9},{2,6},{14,10},{3,7},{15,11},{16,20},{28,... | collective-permute-start | bytes 983048 | tf_op jit(solution)/shard_map/ppermute | solution.py:364
  15.6 6.8 %collective-permute-start.7 = (bf16[640,256]{1,0:T(8,128)(2,1)S(1)}, bf16[640,256]{1,0:T(8,128)(2,1)S(1)}, u32[]{:S(2)}, u32[]{:S(2)}) collective-permute-start(bf16[640,256]{1,0:T(8,128)(2,1)S(1)} %pick_rows.4), channel_id=1, source_target_pairs={{4,8},{8,4},{5,9},{9,5},{6,10},{10,6},{7,11},{11,7},{20,24},{24,20... | collective-permute-start | bytes 983048 | tf_op jit(solution)/shard_map/ppermute | solution.py:364
  17.2 5.3 %copy-start = (bf16[256,2304]{1,0:T(8,128)(2,1)S(1)}, bf16[256,2304]{1,0:T(8,128)(2,1)}, u32[]{:S(2)}) copy-start(bf16[256,2304]{1,0:T(8,128)(2,1)} %refs_4_.1) | copy-start | bytes 3538948
  17.2 10.1 %collective-permute-start.5 = (bf16[640,256]{1,0:T(8,128)(2,1)S(1)}, bf16[640,256]{1,0:T(8,128)(2,1)S(1)}, u32[]{:S(2)}, u32[]{:S(2)}) collective-permute-start(bf16[640,256]{1,0:T(8,128)(2,1)S(1)} %pick_rows.5), channel_id=1, source_target_pairs={{0,9},{1,8},{12,5},{13,4},{2,11},{3,10},{14,7},{15,6},{16,25},{17,... | collective-permute-start | bytes 983048 | tf_op jit(solution)/shard_map/ppermute | solution.py:351
  19.8 14.5 %collective-permute-start.6 = (bf16[640,256]{1,0:T(8,128)(2,1)S(1)}, bf16[640,256]{1,0:T(8,128)(2,1)S(1)}, u32[]{:S(2)}, u32[]{:S(2)}) collective-permute-start(bf16[640,256]{1,0:T(8,128)(2,1)S(1)} %pick_rows.6), channel_id=1, source_target_pairs={{0,4},{4,0},{8,12},{12,8},{1,5},{5,1},{9,13},{13,9},{2,6},{6,2},{1... | collective-permute-start | bytes 983048 | tf_op jit(solution)/shard_map/ppermute | solution.py:364
  21.2 17.1 %collective-permute-start.10 = (bf16[640,256]{1,0:T(8,128)(2,1)S(1)}, bf16[640,256]{1,0:T(8,128)(2,1)S(1)}, u32[]{:S(2)}, u32[]{:S(2)}) collective-permute-start(bf16[640,256]{1,0:T(8,128)(2,1)S(1)} %add.20), channel_id=1, source_target_pairs={{4,12},{8,0},{5,13},{9,1},{6,14},{10,2},{7,15},{11,3},{20,28},{24,... | collective-permute-start | bytes 983048 | tf_op jit(solution)/shard_map/ppermute | solution.py:364
  22.5 11.8 %collective-permute-start.8 = (bf16[16,2304]{1,0:T(8,128)(2,1)S(1)}, bf16[16,2304]{1,0:T(8,128)(2,1)S(1)}, u32[]{:S(2)}, u32[]{:S(2)}) collective-permute-start(bf16[16,2304]{1,0:T(8,128)(2,1)S(1)} %slice.6), channel_id=1, source_target_pairs={{0,1},{4,5},{8,9},{12,13},{2,3},{6,7},{10,11},{14,15},{16,17},{20,... | collective-permute-start | bytes 221192 | tf_op jit(solution)/shard_map/ppermute | solution.py:449
  38.4 10.1 %collective-permute-start.12 = (bf16[640,256]{1,0:T(8,128)(2,1)S(1)}, bf16[640,256]{1,0:T(8,128)(2,1)S(1)}, u32[]{:S(2)}, u32[]{:S(2)}) collective-permute-start(bf16[640,256]{1,0:T(8,128)(2,1)S(1)} %merge.1.body_ref), channel_id=1, source_target_pairs={{0,2},{2,0},{1,3},{3,1},{4,6},{6,4},{5,7},{7,5},{8,10},{10,8},{9,1... | collective-permute-start | bytes 983048 | tf_op jit(solution)/shard_map/ppermute | solution.py:460
  40.0 2.9 %collective-permute-start.13 = (bf16[640,128]{1,0:T(8,128)(2,1)S(1)}, bf16[640,128]{1,0:T(8,128)(2,1)S(1)}, u32[]{:S(2)}, u32[]{:S(2)}) collective-permute-start(bf16[640,128]{1,0:T(8,128)(2,1)S(1)} %slice.8), channel_id=1, source_target_pairs={{0,1},{2,3},{4,5},{6,7},{8,9},{10,11},{12,13},{14,15},{16,17},{18,... | collective-permute-start | bytes 491528 | tf_op jit(solution)/shard_map/ppermute | solution.py:473
  41.3 7.2 %collective-permute-start.11 = (bf16[640,128]{1,0:T(8,128)(2,1)S(1)}, bf16[640,128]{1,0:T(8,128)(2,1)S(1)}, u32[]{:S(2)}, u32[]{:S(2)}) collective-permute-start(bf16[640,128]{1,0:T(8,128)(2,1)S(1)} %slice.8), channel_id=1, source_target_pairs={{0,3},{2,1},{4,7},{6,5},{8,11},{10,9},{12,15},{14,13},{16,19},{18,... | collective-permute-start | bytes 491528 | tf_op jit(solution)/shard_map/ppermute | solution.py:473
  48.5 6.9 %copy-start.1 = (f32[4,2304]{1,0:T(4,128)S(1)}, f32[4,2304]{1,0:T(4,128)}, u32[]{:S(2)}) copy-start(f32[4,2304]{1,0:T(4,128)} %refs_5_.3) | copy-start | bytes 110596
  54.5 3.8 %collective-permute-start.14 = (f32[8,272]{1,0:T(8,128)S(1)}, f32[8,272]{1,0:T(8,128)S(1)}, u32[]{:S(2)}, u32[]{:S(2)}) collective-permute-start(f32[8,272]{1,0:T(8,128)S(1)} %get-tuple-element.51.refs_0_), channel_id=1, source_target_pairs={{0,2},{2,0},{1,3},{3,1},{4,6},{6,4},{5,7},{7,5},{8,10},{10,8},{9,1... | collective-permute-start | bytes 26120 | tf_op jit(solution)/shard_map/ppermute | solution.py:514

commit v21 on v20

--- a/solution.py
+++ b/solution.py
@@ -174,9 +174,10 @@
         slot = rep if far == 0 else 1 - rep
         await_all(copies[far, which])
         if not later:
-            for w in (1, 0):
+            for f, w in order:
                 later += fetch(
-                    count, tp, depth, weights[w], next_ref.at[w], range(1, count), next_sems.at[w]
+                    count, tp, depth, weights[2 * f + w], next_ref.at[f, w], range(1, count),
+                    next_sems.at[2 * f + w],
                 )
         target = value_ref if which == 1 else key_ref
         target[slot] = dot(memory, held[far, which])
@@ -186,19 +187,9 @@
 def project_others_kernel(count, where_ref, *refs):
     pieces = count - 1
     rims, bodies = refs[:pieces], refs[pieces : 2 * pieces]
-    weights = refs[2 * pieces : 2 * pieces + 2]
-    next_ref, begun_keys, begun_values, states_ref, power_ref = refs[2 * pieces + 2 :][:5]
-    value_hbm, stats_ref, held, sems, done, done_sems = refs[2 * pieces + 7 :]
-    half = held.shape[-1]
-    depth = bodies[0].shape[0]
+    held, begun_keys, begun_values, states_ref, power_ref = refs[2 * pieces :][:5]
+    value_hbm, stats_ref, done, done_sems = refs[2 * pieces + 5 :]
     rep = where_ref[0]
-    tp = where_ref[1]
-    copies = {
-        which: fetch(
-            count, tp, depth, weights[which], held.at[which], range(1, count), sems.at[which]
-        )
-        for which in (1, 0)
-    }
     memory = with_rim(rims, bodies)
     sums = [0.0] * 3
     later = []
@@ -206,9 +197,7 @@
         slot = rep if far == 0 else 1 - rep
         fields = [None, None]
         for which in (1, 0):
-            if far == 1:
-                await_all(copies[which])
-            fields[which] = dot(memory, next_ref[which] if far == 0 else held[which])
+            fields[which] = dot(memory, held[far, which])
             if which == 1:
                 done[far] = fields[1] + begun_values[slot]
                 copy = pltpu.make_async_copy(done.at[far], value_hbm.at[slot], done_sems.at[far])
@@ -483,32 +472,30 @@
         out_shape=(
             field,
             field,
-            pltpu.VMEM((2, others * depth, half), BF16),
+            pltpu.VMEM((2, 2, others * depth, half), BF16),
             jax.ShapeDtypeStruct((2, extended, half), BF16),
             jax.ShapeDtypeStruct((extended, 8), F32),
         ),
         scratch_shapes=[
             pltpu.VMEM((2, 2, depth, half), BF16),
             pltpu.SemaphoreType.DMA((4, 1)),
-            pltpu.SemaphoreType.DMA((2, others)),
+            pltpu.SemaphoreType.DMA((4, others)),
         ],
         compiler_params=limit(12),
         name="project_own",
     )(where, rims[0], memory, *weights, hidden_halo, hidden)
     values, stats = pl.pallas_call(
         functools.partial(project_others_kernel, tps),
-        in_specs=[smem] + [resident] * (2 * others) + [anywhere] * 2 + [resident] * 5,
+        in_specs=[smem] + [resident] * (2 * others + 5),
         out_specs=(pl.BlockSpec(memory_space=pltpu.HBM), resident),
         out_shape=(pltpu.HBM(field.shape, F32), jax.ShapeDtypeStruct((8, extended), F32)),
         scratch_shapes=[
-            pltpu.VMEM((2, others * depth, half), BF16),
-            pltpu.SemaphoreType.DMA((2, others)),
             pltpu.VMEM((2, extended, half), F32),
             pltpu.SemaphoreType.DMA((2,)),
         ],
         compiler_params=limit(14),
         name="project_others",
-    )(where, *rims[1:], *bodies[1:], *weights[2:], following, *begun, states, power)
+    )(where, *rims[1:], *bodies[1:], following, *begun, states, power)
 
     all_stats = [stats] + [
         lax.ppermute(stats, "tp", [(i, (i + s) % tps) for i in range(tps)]) for s in range(1, tps)

time: 61.6 us -> 59.3 us (0.963)
  Pallas kernels: 22.3 us -> 20 us
  waiting for transfers between devices: 14.1 us -> 15.5 us
  starting transfers between devices: 24.2 us -> 22.9 us
    ppermute x2, waiting for transfers between devices: 0.97 us -> 3.36 us  [crossing(): lax.ppermute(x, ('mem', 'rep'), [(2 * a + b, 2 * c + d) for a, b, c, d in...]
    pallas_call x1, Pallas kernels: 5.93 us -> 3.6 us  [shards(): pl.pallas_call(functools.partial(project_others_kernel, tps), in_specs=[s...]
    ppermute x4, starting transfers between devices: 6.85 us -> 4.76 us  [send(): return lax.ppermute(x, 'mem', pairs)]
    ppermute x1, starting transfers between devices: 4.12 us -> 2.12 us  [meanwhile(): return lax.ppermute(tail, ('mem', 'rep'), needed)]
    ppermute x2, starting transfers between devices: 2.37 us -> 3.71 us  [crossing(): lax.ppermute(x, ('mem', 'rep'), [(2 * a + b, 2 * c + d) for a, b, c, d in...]
    ppermute x2, waiting for transfers between devices: 1.28 us -> 0.52 us  [ask(): return lax.ppermute(ids, 'mem', [(i, i ^ x) for i in range(4)])]
  transfers between devices with their start and end apart: 15 -> 15, of which waited for: 7 -> 6; matrix products, arithmetic and copies ran while one was open for 0% -> 0% of each run, Pallas kernels for 22% -> 23%
where the time goes in v21:
time: 59.3 us; the launch traced here: 59 us
  starting transfers between devices  22.9 us (39%)
  Pallas kernels  20 us (34%)
  waiting for transfers between devices  15.5 us (26%)
    ppermute x4, waiting for transfers between devices, send(): return lax.ppermute(x, 'mem', pairs)  11.3 us
    pallas_call x1, Pallas kernels, shards(): pl.pallas_call(functools.partial(project_own_kernel, tps), in_specs=[smem...  5.66 us
    ppermute x2, starting transfers between devices, ask(): return lax.ppermute(ids, 'mem', [(i, i ^ x) for i in range(4)])  5.35 us
    ppermute x4, starting transfers between devices, send(): return lax.ppermute(x, 'mem', pairs)  4.76 us
    ppermute x2, starting transfers between devices, crossing(): lax.ppermute(x, ('mem', 'rep'), [(2 * a + b, 2 * c + d) for a, b, c, d in...  3.71 us
    pallas_call x1, Pallas kernels, shards(): pl.pallas_call(functools.partial(project_others_kernel, tps), in_specs=[s...  3.6 us
    pallas_call x4, Pallas kernels, pick(): pl.pallas_call(pick_kernel, in_specs=[pl.BlockSpec(memory_space=pltpu.SME...  3.46 us
    ppermute x2, waiting for transfers between devices, crossing(): lax.ppermute(x, ('mem', 'rep'), [(2 * a + b, 2 * c + d) for a, b, c, d in...  3.36 us
  transfers between devices with their start and end apart: 15, of which 6 were waited for; matrix products, arithmetic and copies ran while one was open for 0% of the time, Pallas kernels for 23%

profile of v21, /device:TPU:0, one launch (start us, length us, event | category | flops | bytes accessed | tf_op | source)
XLA Modules:
  0.0 59.0 jit_solution(10464136241120908565)
XLA Ops:
  0.0 0.5 collective-permute-start.3
  0.5 0.1 collective-permute-start.4
  0.5 1.5 %place_rows.1 = (s32[8,256]{1,0:T(8,128)S(1)}, bf16[8,80,1024]{2,1,0:T(8,128)(2,1)S(1)}, bf16[5,8,1024]{2,1,0:T(8,128)(2,1)S(1)}) custom-call(s32[8,256]{1,0:T(8,128)} %bitcast.11, s32[32,128]{1,0:T(8,128)} %bitcast.10, bf16[8,80,1024]{2,1,0:T(8,128)(2,1)} %bitcast.8, bf16[5,8,1024]{2,1,0:T(8,128)(2,1)} %bitcast.9), custom_call_target="tpu_custom_call" | custom-call | tf_op jit(solution)/shard_map/place_rows/pallas_call | solution.py:406
  2.0 5.1 %collective-permute-start = (s32[8,256]{1,0:T(8,128)S(1)}, s32[8,256]{1,0:T(8,128)S(1)}, u32[]{:S(2)}, u32[]{:S(2)}) collective-permute-start(s32[8,256]{1,0:T(8,128)S(1)} %get-tuple-element.39.ids_ref), channel_id=1, source_target_pairs={{0,12},{4,8},{8,4},{12,0},{1,13},{5,9},{9,5},{13,1},{2,14},{6,10},... | collective-permute-start | bytes 24584 | tf_op jit(solution)/shard_map/ppermute | solution.py:337
  7.1 0.0 collective-permute-start.1
  7.2 0.2 collective-permute-start.2
  7.4 0.9 %decode_tables.1.table_ref = bf16[8,80,1024]{2,1,0:T(8,128)(2,1)S(1)} custom-call(bf16[8,80,1024]{2,1,0:T(8,128)(2,1)S(1)} %get-tuple-element.31.codes_ref, bf16[5,8,1024]{2,1,0:T(8,128)(2,1)S(1)} %get-tuple-element.32.scales_ref), custom_call_target="tpu_custom_call" | custom-call | tf_op jit(solution)/shard_map/decode_tables/pallas_call | solution.py:423
  8.3 0.5 collective-permute-done.ids_ref
  8.8 0.9 %pick_rows.4 = bf16[640,256]{1,0:T(8,128)(2,1)S(1)} custom-call(s32[1]{0:T(128)} %bitcast.3.base_ref, s32[8,256]{1,0:T(8,128)S(1)} %collective-permute-done.ids_ref, bf16[8,80,1024]{2,1,0:T(8,128)(2,1)S(1)} %decode_tables.1.table_ref), custom_call_target="tpu_custom_call" | custom-call | tf_op jit(solution)/shard_map/pick_rows/pallas_call | solution.py:343
  9.6 1.5 %collective-permute-done.1.ids_ref = s32[8,256]{1,0:T(8,128)S(1)} collective-permute-done((s32[8,256]{1,0:T(8,128)S(1)}, s32[8,256]{1,0:T(8,128)S(1)}, u32[]{:S(2)}, u32[]{:S(2)}) %collective-permute-start.1) | collective-permute-done | bytes 8224 | tf_op jit(solution)/shard_map/ppermute | solution.py:340
  11.1 0.0 collective-permute-done.2.ids_ref
  11.1 2.0 %collective-permute-start.9 = (bf16[640,256]{1,0:T(8,128)(2,1)S(1)}, bf16[640,256]{1,0:T(8,128)(2,1)S(1)}, u32[]{:S(2)}, u32[]{:S(2)}) collective-permute-start(bf16[640,256]{1,0:T(8,128)(2,1)S(1)} %pick_rows.4), channel_id=1, source_target_pairs={{0,4},{12,8},{1,5},{13,9},{2,6},{14,10},{3,7},{15,11},{16,20},{28,... | collective-permute-start | bytes 983048 | tf_op jit(solution)/shard_map/ppermute | solution.py:353
  13.2 0.7 %collective-permute-start.7 = (bf16[640,256]{1,0:T(8,128)(2,1)S(1)}, bf16[640,256]{1,0:T(8,128)(2,1)S(1)}, u32[]{:S(2)}, u32[]{:S(2)}) collective-permute-start(bf16[640,256]{1,0:T(8,128)(2,1)S(1)} %pick_rows.4), channel_id=1, source_target_pairs={{4,8},{8,4},{5,9},{9,5},{6,10},{10,6},{7,11},{11,7},{20,24},{24,20... | collective-permute-start | bytes 983048 | tf_op jit(solution)/shard_map/ppermute | solution.py:353
  13.9 0.9 %pick_rows.5 = bf16[640,256]{1,0:T(8,128)(2,1)S(1)} custom-call(s32[1]{0:T(128)} %bitcast.3.base_ref, s32[8,256]{1,0:T(8,128)S(1)} %collective-permute-done.1.ids_ref, bf16[8,80,1024]{2,1,0:T(8,128)(2,1)S(1)} %decode_tables.1.table_ref), custom_call_target="tpu_custom_call" | custom-call | tf_op jit(solution)/shard_map/pick_rows/pallas_call | solution.py:343
  14.7 0.0 copy-start
  14.7 3.7 %collective-permute-start.5 = (bf16[640,256]{1,0:T(8,128)(2,1)S(1)}, bf16[640,256]{1,0:T(8,128)(2,1)S(1)}, u32[]{:S(2)}, u32[]{:S(2)}) collective-permute-start(bf16[640,256]{1,0:T(8,128)(2,1)S(1)} %pick_rows.5), channel_id=1, source_target_pairs={{0,9},{1,8},{12,5},{13,4},{2,11},{3,10},{14,7},{15,6},{16,25},{17,... | collective-permute-start | bytes 983048 | tf_op jit(solution)/shard_map/ppermute | solution.py:340
  18.5 0.0 collective-permute-done.3.refs_2_
  18.5 0.0 collective-permute-done.4.refs_3_
  18.5 0.9 %pick_rows.6 = bf16[640,256]{1,0:T(8,128)(2,1)S(1)} custom-call(s32[1]{0:T(128)} %bitcast.3.base_ref, s32[8,256]{1,0:T(8,128)S(1)} %collective-permute-done.2.ids_ref, bf16[8,80,1024]{2,1,0:T(8,128)(2,1)S(1)} %decode_tables.1.table_ref), custom_call_target="tpu_custom_call" | custom-call | tf_op jit(solution)/shard_map/pick_rows/pallas_call | solution.py:343
  19.3 0.7 %collective-permute-start.6 = (bf16[640,256]{1,0:T(8,128)(2,1)S(1)}, bf16[640,256]{1,0:T(8,128)(2,1)S(1)}, u32[]{:S(2)}, u32[]{:S(2)}) collective-permute-start(bf16[640,256]{1,0:T(8,128)(2,1)S(1)} %pick_rows.6), channel_id=1, source_target_pairs={{0,4},{4,0},{8,12},{12,8},{1,5},{5,1},{9,13},{13,9},{2,6},{6,2},{1... | collective-permute-start | bytes 983048 | tf_op jit(solution)/shard_map/ppermute | solution.py:353
  20.1 0.9 %pick_rows.7 = bf16[640,256]{1,0:T(8,128)(2,1)S(1)} custom-call(s32[1]{0:T(128)} %bitcast.3.base_ref, s32[8,256]{1,0:T(8,128)S(1)} %get-tuple-element.39.ids_ref, bf16[8,80,1024]{2,1,0:T(8,128)(2,1)S(1)} %decode_tables.1.table_ref), custom_call_target="tpu_custom_call" | custom-call | tf_op jit(solution)/shard_map/pick_rows/pallas_call | solution.py:343
  20.9 0.0 collective-permute-done.9
  21.0 0.1 add.20
  21.0 1.3 %collective-permute-start.10 = (bf16[640,256]{1,0:T(8,128)(2,1)S(1)}, bf16[640,256]{1,0:T(8,128)(2,1)S(1)}, u32[]{:S(2)}, u32[]{:S(2)}) collective-permute-start(bf16[640,256]{1,0:T(8,128)(2,1)S(1)} %add.20), channel_id=1, source_target_pairs={{4,12},{8,0},{5,13},{9,1},{6,14},{10,2},{7,15},{11,3},{20,28},{24,... | collective-permute-start | bytes 983048 | tf_op jit(solution)/shard_map/ppermute | solution.py:353
  22.3 0.0 copy-done
  22.4 0.0 collective-permute-done.7.refs_1_
  22.4 2.1 %collective-permute-start.8 = (bf16[16,2304]{1,0:T(8,128)(2,1)S(1)}, bf16[16,2304]{1,0:T(8,128)(2,1)S(1)}, u32[]{:S(2)}, u32[]{:S(2)}) collective-permute-start(bf16[16,2304]{1,0:T(8,128)(2,1)S(1)} %slice.6), channel_id=1, source_target_pairs={{0,1},{4,5},{8,9},{12,13},{2,3},{6,7},{10,11},{14,15},{16,17},{20,... | collective-permute-start | bytes 221192 | tf_op jit(solution)/shard_map/ppermute | solution.py:438
  24.5 1.9 %collective-permute-done.5 = bf16[640,256]{1,0:T(8,128)(2,1)S(1)} collective-permute-done((bf16[640,256]{1,0:T(8,128)(2,1)S(1)}, bf16[640,256]{1,0:T(8,128)(2,1)S(1)}, u32[]{:S(2)}, u32[]{:S(2)}) %collective-permute-start.5) | collective-permute-done | bytes 327712 | tf_op jit(solution)/shard_map/ppermute | solution.py:340
  26.4 7.0 %collective-permute-done.6 = bf16[640,256]{1,0:T(8,128)(2,1)S(1)} collective-permute-done((bf16[640,256]{1,0:T(8,128)(2,1)S(1)}, bf16[640,256]{1,0:T(8,128)(2,1)S(1)}, u32[]{:S(2)}, u32[]{:S(2)}) %collective-permute-start.6) | collective-permute-done | bytes 327712 | tf_op jit(solution)/shard_map/ppermute | solution.py:353
  33.5 0.0 collective-permute-done.8.refs_4_
  33.5 4.3 %collective-permute-done.10.refs_2_ = bf16[640,256]{1,0:T(8,128)(2,1)S(1)} collective-permute-done((bf16[640,256]{1,0:T(8,128)(2,1)S(1)}, bf16[640,256]{1,0:T(8,128)(2,1)S(1)}, u32[]{:S(2)}, u32[]{:S(2)}) %collective-permute-start.10) | collective-permute-done | bytes 327712 | tf_op jit(solution)/shard_map/ppermute | solution.py:353
  37.8 0.1 merge.1.body_ref
  37.9 1.6 %collective-permute-start.12 = (bf16[640,256]{1,0:T(8,128)(2,1)S(1)}, bf16[640,256]{1,0:T(8,128)(2,1)S(1)}, u32[]{:S(2)}, u32[]{:S(2)}) collective-permute-start(bf16[640,256]{1,0:T(8,128)(2,1)S(1)} %merge.1.body_ref), channel_id=1, source_target_pairs={{0,2},{2,0},{1,3},{3,1},{4,6},{6,4},{5,7},{7,5},{8,10},{10,8},{9,1... | collective-permute-start | bytes 983048 | tf_op jit(solution)/shard_map/ppermute | solution.py:449
  39.5 1.7 %collective-permute-start.13 = (bf16[640,128]{1,0:T(8,128)(2,1)S(1)}, bf16[640,128]{1,0:T(8,128)(2,1)S(1)}, u32[]{:S(2)}, u32[]{:S(2)}) collective-permute-start(bf16[640,128]{1,0:T(8,128)(2,1)S(1)} %slice.8), channel_id=1, source_target_pairs={{0,1},{2,3},{4,5},{6,7},{8,9},{10,11},{12,13},{14,15},{16,17},{18,... | collective-permute-start | bytes 491528 | tf_op jit(solution)/shard_map/ppermute | solution.py:462
  41.2 1.6 %collective-permute-start.11 = (bf16[640,128]{1,0:T(8,128)(2,1)S(1)}, bf16[640,128]{1,0:T(8,128)(2,1)S(1)}, u32[]{:S(2)}, u32[]{:S(2)}) collective-permute-start(bf16[640,128]{1,0:T(8,128)(2,1)S(1)} %slice.8), channel_id=1, source_target_pairs={{0,3},{2,1},{4,7},{6,5},{8,11},{10,9},{12,15},{14,13},{16,19},{18,... | collective-permute-start | bytes 491528 | tf_op jit(solution)/shard_map/ppermute | solution.py:462
  42.8 0.1 pad_add_fusion.where_ref
  42.9 0.0 collective-permute-done.13.rim_ref
  42.9 5.7 %project_own.1 = (f32[2,272,1152]{2,1,0:T(8,128)S(1)}, f32[2,272,1152]{2,1,0:T(8,128)S(1)}, bf16[2,2,640,1152]{3,2,1,0:T(8,128)(2,1)S(1)}, bf16[2,272,1152]{2,1,0:T(8,128)(2,1)S(1)}, f32[272,8]{1,0:T(8,128)S(1)}) custom-call(s32[2]{0:T(128)S(1)} %pad_add_fusion.where_ref, bf16[640,128]{1,0:T(8,128)(2,1)S(1)} %collective-permute-done.13.rim_ref, ...), custom_call_target="tpu_custom_call" | custom-call | tf_op jit(solution)/shard_map/project_own/pallas_call | solution.py:468
  48.6 0.0 collective-permute-done.11.refs_0_
  48.6 0.0 collective-permute-done.12.refs_1_
  48.6 0.0 copy-start.1
  48.6 3.6 %project_others.1 = (f32[2,272,1152]{2,1,0:T(8,128)}, f32[8,272]{1,0:T(8,128)S(1)}) custom-call(s32[2]{0:T(128)S(1)} %pad_add_fusion.where_ref, bf16[640,128]{1,0:T(8,128)(2,1)S(1)} %collective-permute-done.11.refs_0_, bf16[640,256]{1,0:T(8,128)(2,1)S(1)} %collective-permute-done.12.refs_1_, bf16[2,2,640,1152]{3,2,1,0:T(8,128)(2,1)S(1)} %get-tuple-element.46.refs_2_, ...), custom_call_target="tpu_custom_call" | custom-call | tf_op jit(solution)/shard_map/project_others/pallas_call | solution.py:487
  52.2 1.6 %collective-permute-start.14 = (f32[8,272]{1,0:T(8,128)S(1)}, f32[8,272]{1,0:T(8,128)S(1)}, u32[]{:S(2)}, u32[]{:S(2)}) collective-permute-start(f32[8,272]{1,0:T(8,128)S(1)} %get-tuple-element.51.refs_0_), channel_id=1, source_target_pairs={{0,2},{2,0},{1,3},{3,1},{4,6},{6,4},{5,7},{7,5},{8,10},{10,8},{9,1... | collective-permute-start | bytes 26120 | tf_op jit(solution)/shard_map/ppermute | solution.py:501
  53.8 0.0 copy-done.1
  53.8 1.9 %prepare.1 = (f32[2,256,1152]{2,1,0:T(8,128)S(1)}, f32[3,2,256,1152]{3,2,1,0:T(8,128)S(1)}) custom-call(f32[4,2304]{1,0:T(4,128)S(1)} %copy-done.1, f32[2,272,1152]{2,1,0:T(8,128)} %get-tuple-element.52.value_hbm), custom_call_target="tpu_custom_call" | custom-call | tf_op jit(solution)/shard_map/prepare/pallas_call | solution.py:509
  55.7 0.3 collective-permute-done.14.refs_1_
  56.0 2.8 %finish.1 = bf16[256,2304]{1,0:T(8,128)(2,1)} custom-call(s32[1]{0:T(128)} %bitcast.keep_ref, f32[8,272]{1,0:T(8,128)S(1)} %get-tuple-element.51.refs_0_, f32[8,272]{1,0:T(8,128)S(1)} %collective-permute-done.14.refs_1_, f32[2,256,1152]{2,1,0:T(8,128)S(1)} %get-tuple-element.53.refs_2_, f32[3,2,256,1152]{3,2,1,0:T(8,128)S(1)} %get-tuple-element.54.refs_3_, ...), custom_call_target="tpu_custom_call" | custom-call | tf_op jit(solution)/shard_map/finish/pallas_call | solution.py:524
  (3 shorter events, 0.1 us)
Async XLA Ops:
  0.0 18.5 %collective-permute-start.3 = (bf16[1280,1152]{1,0:T(8,128)(2,1)}, bf16[1280,1152]{1,0:T(8,128)(2,1)}, u32[]{:S(2)}, u32[]{:S(2)}) collective-permute-start(bf16[1280,1152]{1,0:T(8,128)(2,1)} %refs_0_.1), channel_id=1, source_target_pairs={{0,1},{1,0},{2,3},{3,2},{4,5},{5,4},{6,7},{7,6},{8,9},{9,8},{10,11... | collective-permute-start | bytes 8847368 | tf_op jit(solution)/shard_map/ppermute | solution.py:432
  0.5 18.0 %collective-permute-start.4 = (bf16[1280,1152]{1,0:T(8,128)(2,1)}, bf16[1280,1152]{1,0:T(8,128)(2,1)}, u32[]{:S(2)}, u32[]{:S(2)}) collective-permute-start(bf16[1280,1152]{1,0:T(8,128)(2,1)} %refs_1_.1), channel_id=1, source_target_pairs={{0,1},{1,0},{2,3},{3,2},{4,5},{5,4},{6,7},{7,6},{8,9},{9,8},{10,11... | collective-permute-start | bytes 8847368 | tf_op jit(solution)/shard_map/ppermute | solution.py:433
  2.0 6.7 %collective-permute-start = (s32[8,256]{1,0:T(8,128)S(1)}, s32[8,256]{1,0:T(8,128)S(1)}, u32[]{:S(2)}, u32[]{:S(2)}) collective-permute-start(s32[8,256]{1,0:T(8,128)S(1)} %get-tuple-element.39.ids_ref), channel_id=1, source_target_pairs={{0,12},{4,8},{8,4},{12,0},{1,13},{5,9},{9,5},{13,1},{2,14},{6,10},... | collective-permute-start | bytes 24584 | tf_op jit(solution)/shard_map/ppermute | solution.py:337
  7.1 4.0 %collective-permute-start.1 = (s32[8,256]{1,0:T(8,128)S(1)}, s32[8,256]{1,0:T(8,128)S(1)}, u32[]{:S(2)}, u32[]{:S(2)}) collective-permute-start(s32[8,256]{1,0:T(8,128)S(1)} %get-tuple-element.39.ids_ref), channel_id=1, source_target_pairs={{0,8},{1,9},{4,13},{5,12},{8,1},{9,0},{12,4},{13,5},{2,10},{3,11},... | collective-permute-start | bytes 24584 | tf_op jit(solution)/shard_map/ppermute | solution.py:340
  7.2 4.0 %collective-permute-start.2 = (s32[8,256]{1,0:T(8,128)S(1)}, s32[8,256]{1,0:T(8,128)S(1)}, u32[]{:S(2)}, u32[]{:S(2)}) collective-permute-start(s32[8,256]{1,0:T(8,128)S(1)} %get-tuple-element.39.ids_ref), channel_id=1, source_target_pairs={{0,4},{4,0},{8,12},{12,8},{1,5},{5,1},{9,13},{13,9},{2,6},{6,2},{1... | collective-permute-start | bytes 24584 | tf_op jit(solution)/shard_map/ppermute | solution.py:337
  11.1 9.8 %collective-permute-start.9 = (bf16[640,256]{1,0:T(8,128)(2,1)S(1)}, bf16[640,256]{1,0:T(8,128)(2,1)S(1)}, u32[]{:S(2)}, u32[]{:S(2)}) collective-permute-start(bf16[640,256]{1,0:T(8,128)(2,1)S(1)} %pick_rows.4), channel_id=1, source_target_pairs={{0,4},{12,8},{1,5},{13,9},{2,6},{14,10},{3,7},{15,11},{16,20},{28,... | collective-permute-start | bytes 983048 | tf_op jit(solution)/shard_map/ppermute | solution.py:353
  13.2 9.2 %collective-permute-start.7 = (bf16[640,256]{1,0:T(8,128)(2,1)S(1)}, bf16[640,256]{1,0:T(8,128)(2,1)S(1)}, u32[]{:S(2)}, u32[]{:S(2)}) collective-permute-start(bf16[640,256]{1,0:T(8,128)(2,1)S(1)} %pick_rows.4), channel_id=1, source_target_pairs={{4,8},{8,4},{5,9},{9,5},{6,10},{10,6},{7,11},{11,7},{20,24},{24,20... | collective-permute-start | bytes 983048 | tf_op jit(solution)/shard_map/ppermute | solution.py:353
  14.7 7.6 %copy-start = (bf16[256,2304]{1,0:T(8,128)(2,1)S(1)}, bf16[256,2304]{1,0:T(8,128)(2,1)}, u32[]{:S(2)}) copy-start(bf16[256,2304]{1,0:T(8,128)(2,1)} %refs_4_.1) | copy-start | bytes 3538948
  14.7 11.6 %collective-permute-start.5 = (bf16[640,256]{1,0:T(8,128)(2,1)S(1)}, bf16[640,256]{1,0:T(8,128)(2,1)S(1)}, u32[]{:S(2)}, u32[]{:S(2)}) collective-permute-start(bf16[640,256]{1,0:T(8,128)(2,1)S(1)} %pick_rows.5), channel_id=1, source_target_pairs={{0,9},{1,8},{12,5},{13,4},{2,11},{3,10},{14,7},{15,6},{16,25},{17,... | collective-permute-start | bytes 983048 | tf_op jit(solution)/shard_map/ppermute | solution.py:340
  19.3 14.1 %collective-permute-start.6 = (bf16[640,256]{1,0:T(8,128)(2,1)S(1)}, bf16[640,256]{1,0:T(8,128)(2,1)S(1)}, u32[]{:S(2)}, u32[]{:S(2)}) collective-permute-start(bf16[640,256]{1,0:T(8,128)(2,1)S(1)} %pick_rows.6), channel_id=1, source_target_pairs={{0,4},{4,0},{8,12},{12,8},{1,5},{5,1},{9,13},{13,9},{2,6},{6,2},{1... | collective-permute-start | bytes 983048 | tf_op jit(solution)/shard_map/ppermute | solution.py:353
  21.0 16.7 %collective-permute-start.10 = (bf16[640,256]{1,0:T(8,128)(2,1)S(1)}, bf16[640,256]{1,0:T(8,128)(2,1)S(1)}, u32[]{:S(2)}, u32[]{:S(2)}) collective-permute-start(bf16[640,256]{1,0:T(8,128)(2,1)S(1)} %add.20), channel_id=1, source_target_pairs={{4,12},{8,0},{5,13},{9,1},{6,14},{10,2},{7,15},{11,3},{20,28},{24,... | collective-permute-start | bytes 983048 | tf_op jit(solution)/shard_map/ppermute | solution.py:353
  22.4 11.1 %collective-permute-start.8 = (bf16[16,2304]{1,0:T(8,128)(2,1)S(1)}, bf16[16,2304]{1,0:T(8,128)(2,1)S(1)}, u32[]{:S(2)}, u32[]{:S(2)}) collective-permute-start(bf16[16,2304]{1,0:T(8,128)(2,1)S(1)} %slice.6), channel_id=1, source_target_pairs={{0,1},{4,5},{8,9},{12,13},{2,3},{6,7},{10,11},{14,15},{16,17},{20,... | collective-permute-start | bytes 221192 | tf_op jit(solution)/shard_map/ppermute | solution.py:438
  37.9 10.7 %collective-permute-start.12 = (bf16[640,256]{1,0:T(8,128)(2,1)S(1)}, bf16[640,256]{1,0:T(8,128)(2,1)S(1)}, u32[]{:S(2)}, u32[]{:S(2)}) collective-permute-start(bf16[640,256]{1,0:T(8,128)(2,1)S(1)} %merge.1.body_ref), channel_id=1, source_target_pairs={{0,2},{2,0},{1,3},{3,1},{4,6},{6,4},{5,7},{7,5},{8,10},{10,8},{9,1... | collective-permute-start | bytes 983048 | tf_op jit(solution)/shard_map/ppermute | solution.py:449
  39.5 3.5 %collective-permute-start.13 = (bf16[640,128]{1,0:T(8,128)(2,1)S(1)}, bf16[640,128]{1,0:T(8,128)(2,1)S(1)}, u32[]{:S(2)}, u32[]{:S(2)}) collective-permute-start(bf16[640,128]{1,0:T(8,128)(2,1)S(1)} %slice.8), channel_id=1, source_target_pairs={{0,1},{2,3},{4,5},{6,7},{8,9},{10,11},{12,13},{14,15},{16,17},{18,... | collective-permute-start | bytes 491528 | tf_op jit(solution)/shard_map/ppermute | solution.py:462
  41.2 7.4 %collective-permute-start.11 = (bf16[640,128]{1,0:T(8,128)(2,1)S(1)}, bf16[640,128]{1,0:T(8,128)(2,1)S(1)}, u32[]{:S(2)}, u32[]{:S(2)}) collective-permute-start(bf16[640,128]{1,0:T(8,128)(2,1)S(1)} %slice.8), channel_id=1, source_target_pairs={{0,3},{2,1},{4,7},{6,5},{8,11},{10,9},{12,15},{14,13},{16,19},{18,... | collective-permute-start | bytes 491528 | tf_op jit(solution)/shard_map/ppermute | solution.py:462
  48.6 5.2 %copy-start.1 = (f32[4,2304]{1,0:T(4,128)S(1)}, f32[4,2304]{1,0:T(4,128)}, u32[]{:S(2)}) copy-start(f32[4,2304]{1,0:T(4,128)} %refs_5_.3) | copy-start | bytes 110596
  52.2 3.8 %collective-permute-start.14 = (f32[8,272]{1,0:T(8,128)S(1)}, f32[8,272]{1,0:T(8,128)S(1)}, u32[]{:S(2)}, u32[]{:S(2)}) collective-permute-start(f32[8,272]{1,0:T(8,128)S(1)} %get-tuple-element.51.refs_0_), channel_id=1, source_target_pairs={{0,2},{2,0},{1,3},{3,1},{4,6},{6,4},{5,7},{7,5},{8,10},{10,8},{9,1... | collective-permute-start | bytes 26120 | tf_op jit(solution)/shard_map/ppermute | solution.py:501

commit v22 on v21

--- a/solution.py
+++ b/solution.py
@@ -121,16 +121,18 @@
     refs[-1][...] = total.astype(BF16)
 
 
-def fetch(count, tp, depth, source, target, shifts, sems):
+def fetch(count, tp, depth, source, target, parts, sems):
     copies = []
-    for n, s in enumerate(shifts):
-        owner = lax.rem(tp + count - s, count)
-        rows = pl.ds(pl.multiple_of(owner * depth, depth), depth)
+    start = 0
+    for n, (shift, begin, size) in enumerate(parts):
+        owner = lax.rem(tp + count - shift, count)
+        rows = pl.ds(pl.multiple_of(owner * depth + begin, 16), size)
         copy = pltpu.make_async_copy(
-            source.at[rows, :], target.at[pl.ds(n * depth, depth), :], sems.at[n]
+            source.at[rows, :], target.at[pl.ds(start, size), :], sems.at[n]
         )
         copy.start()
         copies.append(copy)
+        start += size
     return copies
 
 
@@ -140,8 +142,8 @@
 
 
 def with_rim(rims, bodies):
-    body = jnp.concatenate([b[...].astype(F32) for b in bodies], axis=0).T.astype(BF16)
-    rim = jnp.concatenate([r[...].astype(F32) for r in rims], axis=0).T.astype(BF16)
+    body = jnp.concatenate([b.astype(F32) for b in bodies], axis=0).T.astype(BF16)
+    rim = jnp.concatenate([r.astype(F32) for r in rims], axis=0).T.astype(BF16)
     return jnp.concatenate([rim[LANES - RIM :], body], axis=0)
 
 
@@ -150,12 +152,14 @@
     key_ref, value_ref, next_ref, states_ref, power_ref, held, sems, next_sems = refs[6:]
     half = value_ref.shape[-1]
     depth = body_ref.shape[0]
+    split = held.shape[2]
+    remainder = [(0, split, depth - split)] + [(n, 0, depth) for n in range(1, count)]
     rep = where_ref[0]
     tp = where_ref[1]
     order = [(far, which) for far in range(2) for which in (1, 0)]
     copies = {
         (far, which): fetch(
-            count, tp, depth, weights[2 * far + which], held.at[far, which], (0,),
+            count, tp, depth, weights[2 * far + which], held.at[far, which], [(0, 0, split)],
             sems.at[2 * far + which],
         )
         for far, which in order
@@ -168,7 +172,7 @@
         here = states_ref[slot].astype(F32)
         power = power + jnp.sum(here * here, axis=1, keepdims=True)
     power_ref[...] = jnp.broadcast_to(power, power_ref.shape)
-    memory = with_rim([rim_ref], [body_ref])
+    memory = with_rim([rim_ref[:split]], [body_ref[:split]])
     later = []
     for far, which in order:
         slot = rep if far == 0 else 1 - rep
@@ -176,7 +180,7 @@
         if not later:
             for f, w in order:
                 later += fetch(
-                    count, tp, depth, weights[2 * f + w], next_ref.at[f, w], range(1, count),
+                    count, tp, depth, weights[2 * f + w], next_ref.at[f, w], remainder,
                     next_sems.at[2 * f + w],
                 )
         target = value_ref if which == 1 else key_ref
@@ -185,11 +189,13 @@
 
 
 def project_others_kernel(count, where_ref, *refs):
-    pieces = count - 1
-    rims, bodies = refs[:pieces], refs[pieces : 2 * pieces]
-    held, begun_keys, begun_values, states_ref, power_ref = refs[2 * pieces :][:5]
-    value_hbm, stats_ref, done, done_sems = refs[2 * pieces + 5 :]
+    rims, bodies = refs[:count], refs[count : 2 * count]
+    held, begun_keys, begun_values, states_ref, power_ref = refs[2 * count :][:5]
+    value_hbm, stats_ref, done, done_sems = refs[2 * count + 5 :]
     rep = where_ref[0]
+    split = count * bodies[0].shape[0] - held.shape[2]
+    rims = [r[split if n == 0 else 0 :] for n, r in enumerate(rims)]
+    bodies = [b[split if n == 0 else 0 :] for n, b in enumerate(bodies)]
     memory = with_rim(rims, bodies)
     sums = [0.0] * 3
     later = []
@@ -463,8 +469,8 @@
 
     rim = memory[:, tokens - LANES :]
     rims = [next_rim(rim, s) for s in range(tps)]
-    others = tps - 1
     field = jax.ShapeDtypeStruct((2, extended, half), F32)
+    split = max(depth // 256 * 256, depth // 2)
     *begun, following, states, power = pl.pallas_call(
         functools.partial(project_own_kernel, tps),
         in_specs=[smem] + [resident] * 2 + [anywhere] * 4 + [resident] * 2,
@@ -472,21 +478,21 @@
         out_shape=(
             field,
             field,
-            pltpu.VMEM((2, 2, others * depth, half), BF16),
+            pltpu.VMEM((2, 2, tps * depth - split, half), BF16),
             jax.ShapeDtypeStruct((2, extended, half), BF16),
             jax.ShapeDtypeStruct((extended, 8), F32),
         ),
         scratch_shapes=[
-            pltpu.VMEM((2, 2, depth, half), BF16),
+            pltpu.VMEM((2, 2, split, half), BF16),
             pltpu.SemaphoreType.DMA((4, 1)),
-            pltpu.SemaphoreType.DMA((4, others)),
+            pltpu.SemaphoreType.DMA((4, tps)),
         ],
         compiler_params=limit(12),
         name="project_own",
     )(where, rims[0], memory, *weights, hidden_halo, hidden)
     values, stats = pl.pallas_call(
         functools.partial(project_others_kernel, tps),
-        in_specs=[smem] + [resident] * (2 * others + 5),
+        in_specs=[smem] + [resident] * (2 * tps + 5),
         out_specs=(pl.BlockSpec(memory_space=pltpu.HBM), resident),
         out_shape=(pltpu.HBM(field.shape, F32), jax.ShapeDtypeStruct((8, extended), F32)),
         scratch_shapes=[
@@ -495,7 +501,7 @@
         ],
         compiler_params=limit(14),
         name="project_others",
-    )(where, *rims[1:], *bodies[1:], following, *begun, states, power)
+    )(where, *rims, *bodies, following, *begun, states, power)
 
     all_stats = [stats] + [
         lax.ppermute(stats, "tp", [(i, (i + s) % tps) for i in range(tps)]) for s in range(1, tps)

time: 59.3 us -> 60.1 us (1.013)
  Pallas kernels: 20 us -> 20.7 us
    pallas_call x1, Pallas kernels: 3.6 us -> 4.32 us  [shards(): pl.pallas_call(functools.partial(project_others_kernel, tps), in_specs=[s...]
where the time goes in v22:
time: 60.1 us; the launch traced here: 59.7 us
  starting transfers between devices  22.9 us (38%)
  Pallas kernels  20.7 us (34%)
  waiting for transfers between devices  15.5 us (26%)
    ppermute x4, waiting for transfers between devices, send(): return lax.ppermute(x, 'mem', pairs)  11.3 us
    pallas_call x1, Pallas kernels, shards(): pl.pallas_call(functools.partial(project_own_kernel, tps), in_specs=[smem...  5.67 us
    ppermute x2, starting transfers between devices, ask(): return lax.ppermute(ids, 'mem', [(i, i ^ x) for i in range(4)])  5.35 us
    ppermute x4, starting transfers between devices, send(): return lax.ppermute(x, 'mem', pairs)  4.76 us
    pallas_call x1, Pallas kernels, shards(): pl.pallas_call(functools.partial(project_others_kernel, tps), in_specs=[s...  4.32 us
    ppermute x2, starting transfers between devices, crossing(): lax.ppermute(x, ('mem', 'rep'), [(2 * a + b, 2 * c + d) for a, b, c, d in...  3.71 us
    pallas_call x4, Pallas kernels, pick(): pl.pallas_call(pick_kernel, in_specs=[pl.BlockSpec(memory_space=pltpu.SME...  3.46 us
    ppermute x2, waiting for transfers between devices, crossing(): lax.ppermute(x, ('mem', 'rep'), [(2 * a + b, 2 * c + d) for a, b, c, d in...  3.36 us
  transfers between devices with their start and end apart: 15, of which 6 were waited for; matrix products, arithmetic and copies ran while one was open for 0% of the time, Pallas kernels for 23%

profile of v22, /device:TPU:0, one launch (start us, length us, event | category | flops | bytes accessed | tf_op | source)
XLA Modules:
  0.0 59.7 jit_solution(17316003864659552833)
XLA Ops:
  0.0 0.5 collective-permute-start.3
  0.5 0.1 collective-permute-start.4
  0.5 1.5 %place_rows.1 = (s32[8,256]{1,0:T(8,128)S(1)}, bf16[8,80,1024]{2,1,0:T(8,128)(2,1)S(1)}, bf16[5,8,1024]{2,1,0:T(8,128)(2,1)S(1)}) custom-call(s32[8,256]{1,0:T(8,128)} %bitcast.11, s32[32,128]{1,0:T(8,128)} %bitcast.10, bf16[8,80,1024]{2,1,0:T(8,128)(2,1)} %bitcast.8, bf16[5,8,1024]{2,1,0:T(8,128)(2,1)} %bitcast.9), custom_call_target="tpu_custom_call" | custom-call | tf_op jit(solution)/shard_map/place_rows/pallas_call | solution.py:412
  2.0 5.1 %collective-permute-start = (s32[8,256]{1,0:T(8,128)S(1)}, s32[8,256]{1,0:T(8,128)S(1)}, u32[]{:S(2)}, u32[]{:S(2)}) collective-permute-start(s32[8,256]{1,0:T(8,128)S(1)} %get-tuple-element.39.ids_ref), channel_id=1, source_target_pairs={{0,12},{4,8},{8,4},{12,0},{1,13},{5,9},{9,5},{13,1},{2,14},{6,10},... | collective-permute-start | bytes 24584 | tf_op jit(solution)/shard_map/ppermute | solution.py:343
  7.1 0.0 collective-permute-start.1
  7.2 0.2 collective-permute-start.2
  7.4 0.9 %decode_tables.1.table_ref = bf16[8,80,1024]{2,1,0:T(8,128)(2,1)S(1)} custom-call(bf16[8,80,1024]{2,1,0:T(8,128)(2,1)S(1)} %get-tuple-element.31.codes_ref, bf16[5,8,1024]{2,1,0:T(8,128)(2,1)S(1)} %get-tuple-element.32.scales_ref), custom_call_target="tpu_custom_call" | custom-call | tf_op jit(solution)/shard_map/decode_tables/pallas_call | solution.py:429
  8.3 0.5 collective-permute-done.ids_ref
  8.8 0.9 %pick_rows.4 = bf16[640,256]{1,0:T(8,128)(2,1)S(1)} custom-call(s32[1]{0:T(128)} %bitcast.3.base_ref, s32[8,256]{1,0:T(8,128)S(1)} %collective-permute-done.ids_ref, bf16[8,80,1024]{2,1,0:T(8,128)(2,1)S(1)} %decode_tables.1.table_ref), custom_call_target="tpu_custom_call" | custom-call | tf_op jit(solution)/shard_map/pick_rows/pallas_call | solution.py:349
  9.6 1.5 %collective-permute-done.1.ids_ref = s32[8,256]{1,0:T(8,128)S(1)} collective-permute-done((s32[8,256]{1,0:T(8,128)S(1)}, s32[8,256]{1,0:T(8,128)S(1)}, u32[]{:S(2)}, u32[]{:S(2)}) %collective-permute-start.1) | collective-permute-done | bytes 8224 | tf_op jit(solution)/shard_map/ppermute | solution.py:346
  11.1 0.0 collective-permute-done.2.ids_ref
  11.1 2.0 %collective-permute-start.9 = (bf16[640,256]{1,0:T(8,128)(2,1)S(1)}, bf16[640,256]{1,0:T(8,128)(2,1)S(1)}, u32[]{:S(2)}, u32[]{:S(2)}) collective-permute-start(bf16[640,256]{1,0:T(8,128)(2,1)S(1)} %pick_rows.4), channel_id=1, source_target_pairs={{0,4},{12,8},{1,5},{13,9},{2,6},{14,10},{3,7},{15,11},{16,20},{28,... | collective-permute-start | bytes 983048 | tf_op jit(solution)/shard_map/ppermute | solution.py:359
  13.2 0.7 %collective-permute-start.7 = (bf16[640,256]{1,0:T(8,128)(2,1)S(1)}, bf16[640,256]{1,0:T(8,128)(2,1)S(1)}, u32[]{:S(2)}, u32[]{:S(2)}) collective-permute-start(bf16[640,256]{1,0:T(8,128)(2,1)S(1)} %pick_rows.4), channel_id=1, source_target_pairs={{4,8},{8,4},{5,9},{9,5},{6,10},{10,6},{7,11},{11,7},{20,24},{24,20... | collective-permute-start | bytes 983048 | tf_op jit(solution)/shard_map/ppermute | solution.py:359
  13.9 0.9 %pick_rows.5 = bf16[640,256]{1,0:T(8,128)(2,1)S(1)} custom-call(s32[1]{0:T(128)} %bitcast.3.base_ref, s32[8,256]{1,0:T(8,128)S(1)} %collective-permute-done.1.ids_ref, bf16[8,80,1024]{2,1,0:T(8,128)(2,1)S(1)} %decode_tables.1.table_ref), custom_call_target="tpu_custom_call" | custom-call | tf_op jit(solution)/shard_map/pick_rows/pallas_call | solution.py:349
  14.7 0.0 copy-start
  14.7 3.7 %collective-permute-start.5 = (bf16[640,256]{1,0:T(8,128)(2,1)S(1)}, bf16[640,256]{1,0:T(8,128)(2,1)S(1)}, u32[]{:S(2)}, u32[]{:S(2)}) collective-permute-start(bf16[640,256]{1,0:T(8,128)(2,1)S(1)} %pick_rows.5), channel_id=1, source_target_pairs={{0,9},{1,8},{12,5},{13,4},{2,11},{3,10},{14,7},{15,6},{16,25},{17,... | collective-permute-start | bytes 983048 | tf_op jit(solution)/shard_map/ppermute | solution.py:346
  18.5 0.0 collective-permute-done.3.refs_2_
  18.5 0.0 collective-permute-done.4.refs_3_
  18.5 0.9 %pick_rows.6 = bf16[640,256]{1,0:T(8,128)(2,1)S(1)} custom-call(s32[1]{0:T(128)} %bitcast.3.base_ref, s32[8,256]{1,0:T(8,128)S(1)} %collective-permute-done.2.ids_ref, bf16[8,80,1024]{2,1,0:T(8,128)(2,1)S(1)} %decode_tables.1.table_ref), custom_call_target="tpu_custom_call" | custom-call | tf_op jit(solution)/shard_map/pick_rows/pallas_call | solution.py:349
  19.3 0.7 %collective-permute-start.6 = (bf16[640,256]{1,0:T(8,128)(2,1)S(1)}, bf16[640,256]{1,0:T(8,128)(2,1)S(1)}, u32[]{:S(2)}, u32[]{:S(2)}) collective-permute-start(bf16[640,256]{1,0:T(8,128)(2,1)S(1)} %pick_rows.6), channel_id=1, source_target_pairs={{0,4},{4,0},{8,12},{12,8},{1,5},{5,1},{9,13},{13,9},{2,6},{6,2},{1... | collective-permute-start | bytes 983048 | tf_op jit(solution)/shard_map/ppermute | solution.py:359
  20.1 0.9 %pick_rows.7 = bf16[640,256]{1,0:T(8,128)(2,1)S(1)} custom-call(s32[1]{0:T(128)} %bitcast.3.base_ref, s32[8,256]{1,0:T(8,128)S(1)} %get-tuple-element.39.ids_ref, bf16[8,80,1024]{2,1,0:T(8,128)(2,1)S(1)} %decode_tables.1.table_ref), custom_call_target="tpu_custom_call" | custom-call | tf_op jit(solution)/shard_map/pick_rows/pallas_call | solution.py:349
  20.9 0.0 collective-permute-done.9
  21.0 0.1 add.20
  21.0 1.3 %collective-permute-start.10 = (bf16[640,256]{1,0:T(8,128)(2,1)S(1)}, bf16[640,256]{1,0:T(8,128)(2,1)S(1)}, u32[]{:S(2)}, u32[]{:S(2)}) collective-permute-start(bf16[640,256]{1,0:T(8,128)(2,1)S(1)} %add.20), channel_id=1, source_target_pairs={{4,12},{8,0},{5,13},{9,1},{6,14},{10,2},{7,15},{11,3},{20,28},{24,... | collective-permute-start | bytes 983048 | tf_op jit(solution)/shard_map/ppermute | solution.py:359
  22.3 0.0 copy-done
  22.4 0.0 collective-permute-done.7.refs_1_
  22.4 2.1 %collective-permute-start.8 = (bf16[16,2304]{1,0:T(8,128)(2,1)S(1)}, bf16[16,2304]{1,0:T(8,128)(2,1)S(1)}, u32[]{:S(2)}, u32[]{:S(2)}) collective-permute-start(bf16[16,2304]{1,0:T(8,128)(2,1)S(1)} %slice.6), channel_id=1, source_target_pairs={{0,1},{4,5},{8,9},{12,13},{2,3},{6,7},{10,11},{14,15},{16,17},{20,... | collective-permute-start | bytes 221192 | tf_op jit(solution)/shard_map/ppermute | solution.py:444
  24.5 1.9 %collective-permute-done.5 = bf16[640,256]{1,0:T(8,128)(2,1)S(1)} collective-permute-done((bf16[640,256]{1,0:T(8,128)(2,1)S(1)}, bf16[640,256]{1,0:T(8,128)(2,1)S(1)}, u32[]{:S(2)}, u32[]{:S(2)}) %collective-permute-start.5) | collective-permute-done | bytes 327712 | tf_op jit(solution)/shard_map/ppermute | solution.py:346
  26.4 7.0 %collective-permute-done.6 = bf16[640,256]{1,0:T(8,128)(2,1)S(1)} collective-permute-done((bf16[640,256]{1,0:T(8,128)(2,1)S(1)}, bf16[640,256]{1,0:T(8,128)(2,1)S(1)}, u32[]{:S(2)}, u32[]{:S(2)}) %collective-permute-start.6) | collective-permute-done | bytes 327712 | tf_op jit(solution)/shard_map/ppermute | solution.py:359
  33.5 0.0 collective-permute-done.8.refs_4_
  33.5 4.3 %collective-permute-done.10.refs_2_ = bf16[640,256]{1,0:T(8,128)(2,1)S(1)} collective-permute-done((bf16[640,256]{1,0:T(8,128)(2,1)S(1)}, bf16[640,256]{1,0:T(8,128)(2,1)S(1)}, u32[]{:S(2)}, u32[]{:S(2)}) %collective-permute-start.10) | collective-permute-done | bytes 327712 | tf_op jit(solution)/shard_map/ppermute | solution.py:359
  37.8 0.1 merge.1.body_ref.refs_2_
  37.9 1.6 %collective-permute-start.13 = (bf16[640,256]{1,0:T(8,128)(2,1)S(1)}, bf16[640,256]{1,0:T(8,128)(2,1)S(1)}, u32[]{:S(2)}, u32[]{:S(2)}) collective-permute-start(bf16[640,256]{1,0:T(8,128)(2,1)S(1)} %merge.1.body_ref.refs_2_), channel_id=1, source_target_pairs={{0,2},{2,0},{1,3},{3,1},{4,6},{6,4},{5,7},{7,5},{8,10},{10,8},{9,1... | collective-permute-start | bytes 983048 | tf_op jit(solution)/shard_map/ppermute | solution.py:455
  39.5 1.7 %collective-permute-start.11 = (bf16[640,128]{1,0:T(8,128)(2,1)S(1)}, bf16[640,128]{1,0:T(8,128)(2,1)S(1)}, u32[]{:S(2)}, u32[]{:S(2)}) collective-permute-start(bf16[640,128]{1,0:T(8,128)(2,1)S(1)} %slice.8), channel_id=1, source_target_pairs={{0,1},{2,3},{4,5},{6,7},{8,9},{10,11},{12,13},{14,15},{16,17},{18,... | collective-permute-start | bytes 491528 | tf_op jit(solution)/shard_map/ppermute | solution.py:468
  41.2 1.6 %collective-permute-start.12 = (bf16[640,128]{1,0:T(8,128)(2,1)S(1)}, bf16[640,128]{1,0:T(8,128)(2,1)S(1)}, u32[]{:S(2)}, u32[]{:S(2)}) collective-permute-start(bf16[640,128]{1,0:T(8,128)(2,1)S(1)} %slice.8), channel_id=1, source_target_pairs={{0,3},{2,1},{4,7},{6,5},{8,11},{10,9},{12,15},{14,13},{16,19},{18,... | collective-permute-start | bytes 491528 | tf_op jit(solution)/shard_map/ppermute | solution.py:468
  42.8 0.1 pad_add_fusion.where_ref
  42.9 0.0 collective-permute-done.11.rim_ref.refs_0_
  42.9 5.7 %project_own.1 = (f32[2,272,1152]{2,1,0:T(8,128)S(1)}, f32[2,272,1152]{2,1,0:T(8,128)S(1)}, bf16[2,2,768,1152]{3,2,1,0:T(8,128)(2,1)S(1)}, bf16[2,272,1152]{2,1,0:T(8,128)(2,1)S(1)}, f32[272,8]{1,0:T(8,128)S(1)}) custom-call(s32[2]{0:T(128)S(1)} %pad_add_fusion.where_ref, bf16[640,128]{1,0:T(8,128)(2,1)S(1)} %collective-permute-done.11.rim_ref.refs_0_, ...), custom_call_target="tpu_custom_call" | custom-call | tf_op jit(solution)/shard_map/project_own/pallas_call | solution.py:474
  48.6 0.0 collective-permute-done.12.refs_1_
  48.6 0.0 collective-permute-done.13.refs_3_
  48.6 0.0 copy-start.1
  48.6 4.3 %project_others.1 = (f32[2,272,1152]{2,1,0:T(8,128)}, f32[8,272]{1,0:T(8,128)S(1)}) custom-call(s32[2]{0:T(128)S(1)} %pad_add_fusion.where_ref, bf16[640,128]{1,0:T(8,128)(2,1)S(1)} %collective-permute-done.11.rim_ref.refs_0_, bf16[640,128]{1,0:T(8,128)(2,1)S(1)} %collective-permute-done.12.refs_1_, bf16[640,256]{1,0:T(8,128)(2,1)S(1)} %merge.1.body_ref.refs_2_, ...), custom_call_target="tpu_custom_call" | custom-call | tf_op jit(solution)/shard_map/project_others/pallas_call | solution.py:493
  53.0 1.6 %collective-permute-start.14 = (f32[8,272]{1,0:T(8,128)S(1)}, f32[8,272]{1,0:T(8,128)S(1)}, u32[]{:S(2)}, u32[]{:S(2)}) collective-permute-start(f32[8,272]{1,0:T(8,128)S(1)} %get-tuple-element.51.refs_0_), channel_id=1, source_target_pairs={{0,2},{2,0},{1,3},{3,1},{4,6},{6,4},{5,7},{7,5},{8,10},{10,8},{9,1... | collective-permute-start | bytes 26120 | tf_op jit(solution)/shard_map/ppermute | solution.py:507
  54.5 0.0 copy-done.1
  54.5 1.9 %prepare.1 = (f32[2,256,1152]{2,1,0:T(8,128)S(1)}, f32[3,2,256,1152]{3,2,1,0:T(8,128)S(1)}) custom-call(f32[4,2304]{1,0:T(4,128)S(1)} %copy-done.1, f32[2,272,1152]{2,1,0:T(8,128)} %get-tuple-element.52.value_hbm), custom_call_target="tpu_custom_call" | custom-call | tf_op jit(solution)/shard_map/prepare/pallas_call | solution.py:515
  56.5 0.3 collective-permute-done.14.refs_1_
  56.7 2.8 %finish.1 = bf16[256,2304]{1,0:T(8,128)(2,1)} custom-call(s32[1]{0:T(128)} %bitcast.keep_ref, f32[8,272]{1,0:T(8,128)S(1)} %get-tuple-element.51.refs_0_, f32[8,272]{1,0:T(8,128)S(1)} %collective-permute-done.14.refs_1_, f32[2,256,1152]{2,1,0:T(8,128)S(1)} %get-tuple-element.53.refs_2_, f32[3,2,256,1152]{3,2,1,0:T(8,128)S(1)} %get-tuple-element.54.refs_3_, ...), custom_call_target="tpu_custom_call" | custom-call | tf_op jit(solution)/shard_map/finish/pallas_call | solution.py:530
  (3 shorter events, 0.1 us)
Async XLA Ops:
  0.0 18.5 %collective-permute-start.3 = (bf16[1280,1152]{1,0:T(8,128)(2,1)}, bf16[1280,1152]{1,0:T(8,128)(2,1)}, u32[]{:S(2)}, u32[]{:S(2)}) collective-permute-start(bf16[1280,1152]{1,0:T(8,128)(2,1)} %refs_0_.1), channel_id=1, source_target_pairs={{0,1},{1,0},{2,3},{3,2},{4,5},{5,4},{6,7},{7,6},{8,9},{9,8},{10,11... | collective-permute-start | bytes 8847368 | tf_op jit(solution)/shard_map/ppermute | solution.py:438
  0.5 18.0 %collective-permute-start.4 = (bf16[1280,1152]{1,0:T(8,128)(2,1)}, bf16[1280,1152]{1,0:T(8,128)(2,1)}, u32[]{:S(2)}, u32[]{:S(2)}) collective-permute-start(bf16[1280,1152]{1,0:T(8,128)(2,1)} %refs_1_.1), channel_id=1, source_target_pairs={{0,1},{1,0},{2,3},{3,2},{4,5},{5,4},{6,7},{7,6},{8,9},{9,8},{10,11... | collective-permute-start | bytes 8847368 | tf_op jit(solution)/shard_map/ppermute | solution.py:439
  2.0 6.7 %collective-permute-start = (s32[8,256]{1,0:T(8,128)S(1)}, s32[8,256]{1,0:T(8,128)S(1)}, u32[]{:S(2)}, u32[]{:S(2)}) collective-permute-start(s32[8,256]{1,0:T(8,128)S(1)} %get-tuple-element.39.ids_ref), channel_id=1, source_target_pairs={{0,12},{4,8},{8,4},{12,0},{1,13},{5,9},{9,5},{13,1},{2,14},{6,10},... | collective-permute-start | bytes 24584 | tf_op jit(solution)/shard_map/ppermute | solution.py:343
  7.1 4.0 %collective-permute-start.1 = (s32[8,256]{1,0:T(8,128)S(1)}, s32[8,256]{1,0:T(8,128)S(1)}, u32[]{:S(2)}, u32[]{:S(2)}) collective-permute-start(s32[8,256]{1,0:T(8,128)S(1)} %get-tuple-element.39.ids_ref), channel_id=1, source_target_pairs={{0,8},{1,9},{4,13},{5,12},{8,1},{9,0},{12,4},{13,5},{2,10},{3,11},... | collective-permute-start | bytes 24584 | tf_op jit(solution)/shard_map/ppermute | solution.py:346
  7.2 4.0 %collective-permute-start.2 = (s32[8,256]{1,0:T(8,128)S(1)}, s32[8,256]{1,0:T(8,128)S(1)}, u32[]{:S(2)}, u32[]{:S(2)}) collective-permute-start(s32[8,256]{1,0:T(8,128)S(1)} %get-tuple-element.39.ids_ref), channel_id=1, source_target_pairs={{0,4},{4,0},{8,12},{12,8},{1,5},{5,1},{9,13},{13,9},{2,6},{6,2},{1... | collective-permute-start | bytes 24584 | tf_op jit(solution)/shard_map/ppermute | solution.py:343
  11.1 9.8 %collective-permute-start.9 = (bf16[640,256]{1,0:T(8,128)(2,1)S(1)}, bf16[640,256]{1,0:T(8,128)(2,1)S(1)}, u32[]{:S(2)}, u32[]{:S(2)}) collective-permute-start(bf16[640,256]{1,0:T(8,128)(2,1)S(1)} %pick_rows.4), channel_id=1, source_target_pairs={{0,4},{12,8},{1,5},{13,9},{2,6},{14,10},{3,7},{15,11},{16,20},{28,... | collective-permute-start | bytes 983048 | tf_op jit(solution)/shard_map/ppermute | solution.py:359
  13.2 9.2 %collective-permute-start.7 = (bf16[640,256]{1,0:T(8,128)(2,1)S(1)}, bf16[640,256]{1,0:T(8,128)(2,1)S(1)}, u32[]{:S(2)}, u32[]{:S(2)}) collective-permute-start(bf16[640,256]{1,0:T(8,128)(2,1)S(1)} %pick_rows.4), channel_id=1, source_target_pairs={{4,8},{8,4},{5,9},{9,5},{6,10},{10,6},{7,11},{11,7},{20,24},{24,20... | collective-permute-start | bytes 983048 | tf_op jit(solution)/shard_map/ppermute | solution.py:359
  14.7 7.6 %copy-start = (bf16[256,2304]{1,0:T(8,128)(2,1)S(1)}, bf16[256,2304]{1,0:T(8,128)(2,1)}, u32[]{:S(2)}) copy-start(bf16[256,2304]{1,0:T(8,128)(2,1)} %refs_4_.1) | copy-start | bytes 3538948
  14.7 11.6 %collective-permute-start.5 = (bf16[640,256]{1,0:T(8,128)(2,1)S(1)}, bf16[640,256]{1,0:T(8,128)(2,1)S(1)}, u32[]{:S(2)}, u32[]{:S(2)}) collective-permute-start(bf16[640,256]{1,0:T(8,128)(2,1)S(1)} %pick_rows.5), channel_id=1, source_target_pairs={{0,9},{1,8},{12,5},{13,4},{2,11},{3,10},{14,7},{15,6},{16,25},{17,... | collective-permute-start | bytes 983048 | tf_op jit(solution)/shard_map/ppermute | solution.py:346
  19.3 14.1 %collective-permute-start.6 = (bf16[640,256]{1,0:T(8,128)(2,1)S(1)}, bf16[640,256]{1,0:T(8,128)(2,1)S(1)}, u32[]{:S(2)}, u32[]{:S(2)}) collective-permute-start(bf16[640,256]{1,0:T(8,128)(2,1)S(1)} %pick_rows.6), channel_id=1, source_target_pairs={{0,4},{4,0},{8,12},{12,8},{1,5},{5,1},{9,13},{13,9},{2,6},{6,2},{1... | collective-permute-start | bytes 983048 | tf_op jit(solution)/shard_map/ppermute | solution.py:359
  21.0 16.7 %collective-permute-start.10 = (bf16[640,256]{1,0:T(8,128)(2,1)S(1)}, bf16[640,256]{1,0:T(8,128)(2,1)S(1)}, u32[]{:S(2)}, u32[]{:S(2)}) collective-permute-start(bf16[640,256]{1,0:T(8,128)(2,1)S(1)} %add.20), channel_id=1, source_target_pairs={{4,12},{8,0},{5,13},{9,1},{6,14},{10,2},{7,15},{11,3},{20,28},{24,... | collective-permute-start | bytes 983048 | tf_op jit(solution)/shard_map/ppermute | solution.py:359
  22.4 11.1 %collective-permute-start.8 = (bf16[16,2304]{1,0:T(8,128)(2,1)S(1)}, bf16[16,2304]{1,0:T(8,128)(2,1)S(1)}, u32[]{:S(2)}, u32[]{:S(2)}) collective-permute-start(bf16[16,2304]{1,0:T(8,128)(2,1)S(1)} %slice.6), channel_id=1, source_target_pairs={{0,1},{4,5},{8,9},{12,13},{2,3},{6,7},{10,11},{14,15},{16,17},{20,... | collective-permute-start | bytes 221192 | tf_op jit(solution)/shard_map/ppermute | solution.py:444
  37.9 10.7 %collective-permute-start.13 = (bf16[640,256]{1,0:T(8,128)(2,1)S(1)}, bf16[640,256]{1,0:T(8,128)(2,1)S(1)}, u32[]{:S(2)}, u32[]{:S(2)}) collective-permute-start(bf16[640,256]{1,0:T(8,128)(2,1)S(1)} %merge.1.body_ref.refs_2_), channel_id=1, source_target_pairs={{0,2},{2,0},{1,3},{3,1},{4,6},{6,4},{5,7},{7,5},{8,10},{10,8},{9,1... | collective-permute-start | bytes 983048 | tf_op jit(solution)/shard_map/ppermute | solution.py:455
  39.5 3.5 %collective-permute-start.11 = (bf16[640,128]{1,0:T(8,128)(2,1)S(1)}, bf16[640,128]{1,0:T(8,128)(2,1)S(1)}, u32[]{:S(2)}, u32[]{:S(2)}) collective-permute-start(bf16[640,128]{1,0:T(8,128)(2,1)S(1)} %slice.8), channel_id=1, source_target_pairs={{0,1},{2,3},{4,5},{6,7},{8,9},{10,11},{12,13},{14,15},{16,17},{18,... | collective-permute-start | bytes 491528 | tf_op jit(solution)/shard_map/ppermute | solution.py:468
  41.2 7.4 %collective-permute-start.12 = (bf16[640,128]{1,0:T(8,128)(2,1)S(1)}, bf16[640,128]{1,0:T(8,128)(2,1)S(1)}, u32[]{:S(2)}, u32[]{:S(2)}) collective-permute-start(bf16[640,128]{1,0:T(8,128)(2,1)S(1)} %slice.8), channel_id=1, source_target_pairs={{0,3},{2,1},{4,7},{6,5},{8,11},{10,9},{12,15},{14,13},{16,19},{18,... | collective-permute-start | bytes 491528 | tf_op jit(solution)/shard_map/ppermute | solution.py:468
  48.6 5.9 %copy-start.1 = (f32[4,2304]{1,0:T(4,128)S(1)}, f32[4,2304]{1,0:T(4,128)}, u32[]{:S(2)}) copy-start(f32[4,2304]{1,0:T(4,128)} %refs_5_.3) | copy-start | bytes 110596
  53.0 3.8 %collective-permute-start.14 = (f32[8,272]{1,0:T(8,128)S(1)}, f32[8,272]{1,0:T(8,128)S(1)}, u32[]{:S(2)}, u32[]{:S(2)}) collective-permute-start(f32[8,272]{1,0:T(8,128)S(1)} %get-tuple-element.51.refs_0_), channel_id=1, source_target_pairs={{0,2},{2,0},{1,3},{3,1},{4,6},{6,4},{5,7},{7,5},{8,10},{10,8},{9,1... | collective-permute-start | bytes 26120 | tf_op jit(solution)/shard_map/ppermute | solution.py:507

commit v23 on v21

--- a/solution.py
+++ b/solution.py
@@ -145,21 +145,36 @@
     return jnp.concatenate([rim[LANES - RIM :], body], axis=0)
 
 
+def load_kernel(count, where_ref, key_hbm, value_hbm, out_ref, sems):
+    copies = []
+    for which, source in enumerate((key_hbm, value_hbm)):
+        depth = out_ref.shape[1]
+        copies += fetch(
+            count, where_ref[1], depth, source, out_ref.at[which], (0,), sems.at[which]
+        )
+    await_all(copies)
+
+
 def project_own_kernel(count, where_ref, rim_ref, body_ref, *refs):
-    weights, hidden_halo, hidden = refs[:4], refs[4], refs[5]
-    key_ref, value_ref, next_ref, states_ref, power_ref, held, sems, next_sems = refs[6:]
+    weights, ready, hidden_halo, hidden = refs[:4], refs[4], refs[5], refs[6]
+    key_ref, value_ref, next_ref, states_ref, power_ref, held, sems, next_sems = refs[7:]
     half = value_ref.shape[-1]
     depth = body_ref.shape[0]
     rep = where_ref[0]
     tp = where_ref[1]
     order = [(far, which) for far in range(2) for which in (1, 0)]
     copies = {
-        (far, which): fetch(
-            count, tp, depth, weights[2 * far + which], held.at[far, which], (0,),
-            sems.at[2 * far + which],
-        )
-        for far, which in order
+        (1, which): fetch(
+            count, tp, depth, weights[2 + which], held.at[which], (0,), sems.at[which]
+        )
+        for which in (1, 0)
     }
+    later = []
+    for f, w in order:
+        later += fetch(
+            count, tp, depth, weights[2 * f + w], next_ref.at[f, w], range(1, count),
+            next_sems.at[2 * f + w],
+        )
     power = 0.0
     for slot in range(2):
         span = slice(slot * half, (slot + 1) * half)
@@ -169,18 +184,11 @@
         power = power + jnp.sum(here * here, axis=1, keepdims=True)
     power_ref[...] = jnp.broadcast_to(power, power_ref.shape)
     memory = with_rim([rim_ref], [body_ref])
-    later = []
     for far, which in order:
         slot = rep if far == 0 else 1 - rep
-        await_all(copies[far, which])
-        if not later:
-            for f, w in order:
-                later += fetch(
-                    count, tp, depth, weights[2 * f + w], next_ref.at[f, w], range(1, count),
-                    next_sems.at[2 * f + w],
-                )
+        await_all(copies.get((far, which), ()))
         target = value_ref if which == 1 else key_ref
-        target[slot] = dot(memory, held[far, which])
+        target[slot] = dot(memory, ready[which] if far == 0 else held[which])
     await_all(later)
 
 
@@ -324,7 +332,7 @@
         name="pick_all",
     )((here * rows).astype(I32).reshape(1), asked, decoded)
     total = lax.psum_scatter(partial, "mem", scatter_dimension=0, tiled=False)
-    return total, meanwhile(partial), settled
+    return total, meanwhile(partial, partial), settled
 
 
 def line_sum(stored, decoded, here, meanwhile, settled):
@@ -369,8 +377,9 @@
     own = pick(after(stored, rows_1))
     beside = send(rows_1, (0, 1), (1, 0), (2, 3), (3, 2))
     onward = after(rows_2, rows_1, own) + inward
+    onward_sum = onward
     onward = send(onward, (1, 3), (2, 0))
-    other = meanwhile(across)
+    other = meanwhile(across, onward_sum)
     own, other = lax.optimization_barrier((own + past + beside, other))
     memory = pl.pallas_call(
         merge_kernel,
@@ -433,17 +442,28 @@
     other_value = lax.ppermute(value_weight, "rep", [(0, 1), (1, 0)])
     needed = [(i, i + 1) for i in range(blocks - 1) if (i + 1) * tokens % seq_length]
 
-    def meanwhile(token):
+    where = jnp.stack([lax.axis_index("rep"), lax.axis_index("tp")]).astype(I32)
+
+    def meanwhile(token, later):
         tail = after(hidden[tokens - RIM :], token)
-        return lax.ppermute(tail, ("mem", "rep"), needed)
+        halo = lax.ppermute(tail, ("mem", "rep"), needed)
+        ready = pl.pallas_call(
+            functools.partial(load_kernel, tps),
+            in_specs=[smem] + [anywhere] * 2,
+            out_specs=resident,
+            out_shape=pltpu.VMEM((2, depth, half), BF16),
+            scratch_shapes=[pltpu.SemaphoreType.DMA((2, 1))],
+            compiler_params=limit(4),
+            name="load_weights",
+        )(where, *[in_hbm(after(w, later)) for w in (key_weight, value_weight)])
+        return halo, ready
 
     summed = line_sum if mems == 4 else scattered_sum
-    memory, hidden_halo, others = summed(
+    memory, (hidden_halo, ready), others = summed(
         stored, decoded, here, meanwhile, (other_key, other_value)
     )
     weights = [in_hbm(w) for w in (key_weight, value_weight, *others)]
 
-    where = jnp.stack([lax.axis_index("rep"), lax.axis_index("tp")]).astype(I32)
     extended = tokens + RIM
     bodies = [memory] + [
         lax.ppermute(memory, "tp", [(i, (i + s) % tps) for i in range(tps)])
@@ -467,7 +487,7 @@
     field = jax.ShapeDtypeStruct((2, extended, half), F32)
     *begun, following, states, power = pl.pallas_call(
         functools.partial(project_own_kernel, tps),
-        in_specs=[smem] + [resident] * 2 + [anywhere] * 4 + [resident] * 2,
+        in_specs=[smem] + [resident] * 2 + [anywhere] * 4 + [resident] * 3,
         out_specs=(resident,) * 5,
         out_shape=(
             field,
@@ -477,13 +497,13 @@
             jax.ShapeDtypeStruct((extended, 8), F32),
         ),
         scratch_shapes=[
-            pltpu.VMEM((2, 2, depth, half), BF16),
-            pltpu.SemaphoreType.DMA((4, 1)),
+            pltpu.VMEM((2, depth, half), BF16),
+            pltpu.SemaphoreType.DMA((2, 1)),
             pltpu.SemaphoreType.DMA((4, others)),
         ],
         compiler_params=limit(12),
         name="project_own",
-    )(where, rims[0], memory, *weights, hidden_halo, hidden)
+    )(where, rims[0], memory, *weights, ready, hidden_halo, hidden)
     values, stats = pl.pallas_call(
         functools.partial(project_others_kernel, tps),
         in_specs=[smem] + [resident] * (2 * others + 5),

time: 59.3 us -> 61.7 us (1.040)
  waiting for transfers between devices: 15.5 us -> 11.6 us
  Pallas kernels: 20 us -> 23.8 us
  other arithmetic: 0.21 us -> 2.25 us
    pallas_call x0 -> x1, Pallas kernels: none -> 2.38 us  [meanwhile(): pl.pallas_call(functools.partial(load_kernel, tps), in_specs=[smem] + [an...]
    ppermute x4, waiting for transfers between devices: 11.3 us -> 9.33 us  [send(): return lax.ppermute(x, 'mem', pairs)]
    ppermute x2, waiting for transfers between devices: 3.36 us -> 1.48 us  [crossing(): lax.ppermute(x, ('mem', 'rep'), [(2 * a + b, 2 * c + d) for a, b, c, d in...]
    add x1, other arithmetic: 0.05 us -> 1.12 us  [line_sum(): own, other = lax.optimization_barrier((own + past + beside, other))]
    add x1, other arithmetic: 0.09 us -> 1.05 us  [line_sum(): onward = after(rows_2, rows_1, own) + inward]
    pallas_call x4, Pallas kernels: 3.46 us -> 4.18 us  [pick(): pl.pallas_call(pick_kernel, in_specs=[pl.BlockSpec(memory_space=pltpu.SME...]
    ppermute x1, starting transfers between devices: 2.12 us -> 2.77 us  [meanwhile(): halo = lax.ppermute(tail, ('mem', 'rep'), needed)]
  transfers between devices with their start and end apart: 15 -> 15, of which waited for: 6 -> 4; matrix products, arithmetic and copies ran while one was open for 0% -> 4% of each run, Pallas kernels for 23% -> 28%
where the time goes in v23:
time: 61.7 us; the launch traced here: 61.3 us
  Pallas kernels  23.8 us (39%)
  starting transfers between devices  23.3 us (38%)
  waiting for transfers between devices  11.6 us (19%)
  other arithmetic  2.25 us (4%)
    ppermute x4, waiting for transfers between devices, send(): return lax.ppermute(x, 'mem', pairs)  9.33 us
    pallas_call x1, Pallas kernels, shards(): pl.pallas_call(functools.partial(project_own_kernel, tps), in_specs=[smem...  6.26 us
    ppermute x2, starting transfers between devices, ask(): return lax.ppermute(ids, 'mem', [(i, i ^ x) for i in range(4)])  5.35 us
    ppermute x4, starting transfers between devices, send(): return lax.ppermute(x, 'mem', pairs)  4.73 us
    pallas_call x4, Pallas kernels, pick(): pl.pallas_call(pick_kernel, in_specs=[pl.BlockSpec(memory_space=pltpu.SME...  4.18 us
    pallas_call x1, Pallas kernels, shards(): pl.pallas_call(functools.partial(project_others_kernel, tps), in_specs=[s...  3.68 us
    ppermute x2, starting transfers between devices, crossing(): lax.ppermute(x, ('mem', 'rep'), [(2 * a + b, 2 * c + d) for a, b, c, d in...  3.6 us
    ppermute x2, starting transfers between devices, next_rim(): return lax.ppermute(rim, ('mem', 'tp', 'rep'), pairs)  3.26 us
  transfers between devices with their start and end apart: 15, of which 4 were waited for; matrix products, arithmetic and copies ran while one was open for 4% of the time, Pallas kernels for 28%

profile of v23, /device:TPU:0, one launch (start us, length us, event | category | flops | bytes accessed | tf_op | source)
XLA Modules:
  0.0 61.3 jit_solution(6932275085119448010)
XLA Ops:
  0.0 0.5 collective-permute-start.3
  0.5 0.1 collective-permute-start.4
  0.5 1.5 %place_rows.1 = (s32[8,256]{1,0:T(8,128)S(1)}, bf16[8,80,1024]{2,1,0:T(8,128)(2,1)S(1)}, bf16[5,8,1024]{2,1,0:T(8,128)(2,1)S(1)}) custom-call(s32[8,256]{1,0:T(8,128)} %bitcast.11, s32[32,128]{1,0:T(8,128)} %bitcast.10, bf16[8,80,1024]{2,1,0:T(8,128)(2,1)} %bitcast.8, bf16[5,8,1024]{2,1,0:T(8,128)(2,1)} %bitcast.9), custom_call_target="tpu_custom_call" | custom-call | tf_op jit(solution)/shard_map/place_rows/pallas_call | solution.py:415
  2.0 5.1 %collective-permute-start = (s32[8,256]{1,0:T(8,128)S(1)}, s32[8,256]{1,0:T(8,128)S(1)}, u32[]{:S(2)}, u32[]{:S(2)}) collective-permute-start(s32[8,256]{1,0:T(8,128)S(1)} %get-tuple-element.42.ids_ref), channel_id=1, source_target_pairs={{0,12},{4,8},{8,4},{12,0},{1,13},{5,9},{9,5},{13,1},{2,14},{6,10},... | collective-permute-start | bytes 24584 | tf_op jit(solution)/shard_map/ppermute | solution.py:345
  7.1 0.0 collective-permute-start.1
  7.2 0.2 collective-permute-start.2
  7.4 0.9 %decode_tables.1.table_ref = bf16[8,80,1024]{2,1,0:T(8,128)(2,1)S(1)} custom-call(bf16[8,80,1024]{2,1,0:T(8,128)(2,1)S(1)} %get-tuple-element.34.codes_ref, bf16[5,8,1024]{2,1,0:T(8,128)(2,1)S(1)} %get-tuple-element.35.scales_ref), custom_call_target="tpu_custom_call" | custom-call | tf_op jit(solution)/shard_map/decode_tables/pallas_call | solution.py:432
  8.3 0.0 copy-start
  8.3 0.5 collective-permute-done.ids_ref
  8.8 0.9 %pick_rows.4 = bf16[640,256]{1,0:T(8,128)(2,1)S(1)} custom-call(s32[1]{0:T(128)} %bitcast.3.base_ref, s32[8,256]{1,0:T(8,128)S(1)} %collective-permute-done.ids_ref, bf16[8,80,1024]{2,1,0:T(8,128)(2,1)S(1)} %decode_tables.1.table_ref), custom_call_target="tpu_custom_call" | custom-call | tf_op jit(solution)/shard_map/pick_rows/pallas_call | solution.py:351
  9.6 1.5 %collective-permute-done.1.ids_ref = s32[8,256]{1,0:T(8,128)S(1)} collective-permute-done((s32[8,256]{1,0:T(8,128)S(1)}, s32[8,256]{1,0:T(8,128)S(1)}, u32[]{:S(2)}, u32[]{:S(2)}) %collective-permute-start.1) | collective-permute-done | bytes 8224 | tf_op jit(solution)/shard_map/ppermute | solution.py:348
  11.1 0.0 collective-permute-done.2.ids_ref
  11.1 2.8 %collective-permute-start.9 = (bf16[640,256]{1,0:T(8,128)(2,1)S(1)}, bf16[640,256]{1,0:T(8,128)(2,1)}, u32[]{:S(2)}, u32[]{:S(2)}) collective-permute-start(bf16[640,256]{1,0:T(8,128)(2,1)S(1)} %pick_rows.4), channel_id=1, source_target_pairs={{0,4},{12,8},{1,5},{13,9},{2,6},{14,10},{3,7},{15,11},{16,20},{28,... | collective-permute-start | bytes 983048 | tf_op jit(solution)/shard_map/ppermute | solution.py:361
  13.9 0.7 %collective-permute-start.7 = (bf16[640,256]{1,0:T(8,128)(2,1)S(1)}, bf16[640,256]{1,0:T(8,128)(2,1)S(1)}, u32[]{:S(2)}, u32[]{:S(2)}) collective-permute-start(bf16[640,256]{1,0:T(8,128)(2,1)S(1)} %pick_rows.4), channel_id=1, source_target_pairs={{4,8},{8,4},{5,9},{9,5},{6,10},{10,6},{7,11},{11,7},{20,24},{24,20... | collective-permute-start | bytes 983048 | tf_op jit(solution)/shard_map/ppermute | solution.py:361
  14.6 0.9 %pick_rows.5 = bf16[640,256]{1,0:T(8,128)(2,1)S(1)} custom-call(s32[1]{0:T(128)} %bitcast.3.base_ref, s32[8,256]{1,0:T(8,128)S(1)} %collective-permute-done.1.ids_ref, bf16[8,80,1024]{2,1,0:T(8,128)(2,1)S(1)} %decode_tables.1.table_ref), custom_call_target="tpu_custom_call" | custom-call | tf_op jit(solution)/shard_map/pick_rows/pallas_call | solution.py:351
  15.4 3.6 %collective-permute-start.5 = (bf16[640,256]{1,0:T(8,128)(2,1)S(1)}, bf16[640,256]{1,0:T(8,128)(2,1)}, u32[]{:S(2)}, u32[]{:S(2)}) collective-permute-start(bf16[640,256]{1,0:T(8,128)(2,1)S(1)} %pick_rows.5), channel_id=1, source_target_pairs={{0,9},{1,8},{12,5},{13,4},{2,11},{3,10},{14,7},{15,6},{16,25},{17,... | collective-permute-start | bytes 983048 | tf_op jit(solution)/shard_map/ppermute | solution.py:348
  19.0 0.0 collective-permute-done.3.refs_2_
  19.0 0.0 collective-permute-done.4.refs_3_
  19.0 1.6 %pick_rows.6 = bf16[640,256]{1,0:T(8,128)(2,1)} custom-call(s32[1]{0:T(128)} %bitcast.3.base_ref, s32[8,256]{1,0:T(8,128)S(1)} %collective-permute-done.2.ids_ref, bf16[8,80,1024]{2,1,0:T(8,128)(2,1)S(1)} %decode_tables.1.table_ref), custom_call_target="tpu_custom_call" | custom-call | tf_op jit(solution)/shard_map/pick_rows/pallas_call | solution.py:351
  20.6 0.0 collective-permute-start.6
  20.6 0.0 copy-done
  20.6 0.9 %pick_rows.7 = bf16[640,256]{1,0:T(8,128)(2,1)S(1)} custom-call(s32[1]{0:T(128)} %bitcast.3.base_ref, s32[8,256]{1,0:T(8,128)S(1)} %get-tuple-element.42.ids_ref, bf16[8,80,1024]{2,1,0:T(8,128)(2,1)S(1)} %decode_tables.1.table_ref), custom_call_target="tpu_custom_call" | custom-call | tf_op jit(solution)/shard_map/pick_rows/pallas_call | solution.py:351
  21.5 0.0 collective-permute-done.9
  21.5 1.1 %add.20 = bf16[640,256]{1,0:T(8,128)(2,1)S(1)} add(bf16[640,256]{1,0:T(8,128)(2,1)S(1)} %pick_rows.5, bf16[640,256]{1,0:T(8,128)(2,1)} %collective-permute-done.9) | non-fusion elementwise | flops 163840 | bytes 983040 | tf_op jit(solution)/shard_map/add | solution.py:379
  22.6 1.3 %collective-permute-start.10 = (bf16[640,256]{1,0:T(8,128)(2,1)S(1)}, bf16[640,256]{1,0:T(8,128)(2,1)S(1)}, u32[]{:S(2)}, u32[]{:S(2)}) collective-permute-start(bf16[640,256]{1,0:T(8,128)(2,1)S(1)} %add.20), channel_id=1, source_target_pairs={{4,12},{8,0},{5,13},{9,1},{6,14},{10,2},{7,15},{11,3},{20,28},{24,... | collective-permute-start | bytes 983048 | tf_op jit(solution)/shard_map/ppermute | solution.py:361
  23.9 0.1 pad_add_fusion.where_ref
  24.0 0.0 collective-permute-done.7.refs_1_
  24.0 2.8 %collective-permute-start.8 = (bf16[16,2304]{1,0:T(8,128)(2,1)S(1)}, bf16[16,2304]{1,0:T(8,128)(2,1)S(1)}, u32[]{:S(2)}, u32[]{:S(2)}) collective-permute-start(bf16[16,2304]{1,0:T(8,128)(2,1)S(1)} %slice.6), channel_id=1, source_target_pairs={{0,1},{4,5},{8,9},{12,13},{2,3},{6,7},{10,11},{14,15},{16,17},{20,... | collective-permute-start | bytes 221192 | tf_op jit(solution)/shard_map/ppermute | solution.py:449
  26.7 2.4 %load_weights.1.refs_4_ = bf16[2,640,1152]{2,1,0:T(8,128)(2,1)S(1)} custom-call(s32[2]{0:T(128)S(1)} %pad_add_fusion.where_ref, bf16[1280,1152]{1,0:T(8,128)(2,1)} %refs_0_.1, bf16[1280,1152]{1,0:T(8,128)(2,1)} %refs_1_.1), custom_call_target="tpu_custom_call" | custom-call | tf_op jit(solution)/shard_map/load_weights/pallas_call | solution.py:450
  29.1 0.0 collective-permute-done.5
  29.1 9.3 %collective-permute-done.6 = bf16[640,256]{1,0:T(8,128)(2,1)} collective-permute-done((bf16[640,256]{1,0:T(8,128)(2,1)}, bf16[640,256]{1,0:T(8,128)(2,1)}, u32[]{:S(2)}, u32[]{:S(2)}) %collective-permute-start.6) | collective-permute-done | bytes 327712 | tf_op jit(solution)/shard_map/ppermute | solution.py:361
  38.5 1.1 %add_add_fusion.refs_0_ = bf16[640,256]{1,0:T(8,128)(2,1)S(1)} fusion(bf16[640,256]{1,0:T(8,128)(2,1)} %collective-permute-done.6, bf16[640,256]{1,0:T(8,128)(2,1)S(1)} %pick_rows.7, bf16[640,256]{1,0:T(8,128)(2,1)} %collective-permute-done.5), kind=kLoop, calls=%fused_computation | loop fusion | flops 327680 | bytes 1310720 | tf_op jit(solution)/shard_map/add | solution.py:383
  39.6 0.0 collective-permute-done.8.refs_5_
  39.6 0.0 collective-permute-done.10.refs_2_
  39.6 0.1 merge.1.body_ref
  39.7 1.6 %collective-permute-start.12 = (bf16[640,256]{1,0:T(8,128)(2,1)S(1)}, bf16[640,256]{1,0:T(8,128)(2,1)S(1)}, u32[]{:S(2)}, u32[]{:S(2)}) collective-permute-start(bf16[640,256]{1,0:T(8,128)(2,1)S(1)} %merge.1.body_ref), channel_id=1, source_target_pairs={{0,2},{2,0},{1,3},{3,1},{4,6},{6,4},{5,7},{7,5},{8,10},{10,8},{9,1... | collective-permute-start | bytes 983048 | tf_op jit(solution)/shard_map/ppermute | solution.py:469
  41.3 1.6 %collective-permute-start.13 = (bf16[640,128]{1,0:T(8,128)(2,1)S(1)}, bf16[640,128]{1,0:T(8,128)(2,1)S(1)}, u32[]{:S(2)}, u32[]{:S(2)}) collective-permute-start(bf16[640,128]{1,0:T(8,128)(2,1)S(1)} %slice.8), channel_id=1, source_target_pairs={{0,1},{2,3},{4,5},{6,7},{8,9},{10,11},{12,13},{14,15},{16,17},{18,... | collective-permute-start | bytes 491528 | tf_op jit(solution)/shard_map/ppermute | solution.py:482
  43.0 1.6 %collective-permute-start.11 = (bf16[640,128]{1,0:T(8,128)(2,1)S(1)}, bf16[640,128]{1,0:T(8,128)(2,1)S(1)}, u32[]{:S(2)}, u32[]{:S(2)}) collective-permute-start(bf16[640,128]{1,0:T(8,128)(2,1)S(1)} %slice.8), channel_id=1, source_target_pairs={{0,3},{2,1},{4,7},{6,5},{8,11},{10,9},{12,15},{14,13},{16,19},{18,... | collective-permute-start | bytes 491528 | tf_op jit(solution)/shard_map/ppermute | solution.py:482
  44.6 0.0 collective-permute-done.13.rim_ref
  44.6 6.3 %project_own.1 = (f32[2,272,1152]{2,1,0:T(8,128)S(1)}, f32[2,272,1152]{2,1,0:T(8,128)S(1)}, bf16[2,2,640,1152]{3,2,1,0:T(8,128)(2,1)S(1)}, bf16[2,272,1152]{2,1,0:T(8,128)(2,1)S(1)}, f32[272,8]{1,0:T(8,128)S(1)}) custom-call(s32[2]{0:T(128)S(1)} %pad_add_fusion.where_ref, bf16[640,128]{1,0:T(8,128)(2,1)S(1)} %collective-permute-done.13.rim_ref, ...), custom_call_target="tpu_custom_call" | custom-call | tf_op jit(solution)/shard_map/project_own/pallas_call | solution.py:488
  50.9 0.0 collective-permute-done.11.refs_0_
  50.9 0.0 collective-permute-done.12.refs_1_
  50.9 0.0 copy-start.1
  50.9 3.7 %project_others.1 = (f32[2,272,1152]{2,1,0:T(8,128)}, f32[8,272]{1,0:T(8,128)S(1)}) custom-call(s32[2]{0:T(128)S(1)} %pad_add_fusion.where_ref, bf16[640,128]{1,0:T(8,128)(2,1)S(1)} %collective-permute-done.11.refs_0_, bf16[640,256]{1,0:T(8,128)(2,1)S(1)} %collective-permute-done.12.refs_1_, bf16[2,2,640,1152]{3,2,1,0:T(8,128)(2,1)S(1)} %get-tuple-element.52.refs_2_, ...), custom_call_target="tpu_custom_call" | custom-call | tf_op jit(solution)/shard_map/project_others/pallas_call | solution.py:507
  54.6 1.6 %collective-permute-start.14 = (f32[8,272]{1,0:T(8,128)S(1)}, f32[8,272]{1,0:T(8,128)S(1)}, u32[]{:S(2)}, u32[]{:S(2)}) collective-permute-start(f32[8,272]{1,0:T(8,128)S(1)} %get-tuple-element.57.refs_0_), channel_id=1, source_target_pairs={{0,2},{2,0},{1,3},{3,1},{4,6},{6,4},{5,7},{7,5},{8,10},{10,8},{9,1... | collective-permute-start | bytes 26120 | tf_op jit(solution)/shard_map/ppermute | solution.py:521
  56.1 1.9 %prepare.1 = (f32[2,256,1152]{2,1,0:T(8,128)S(1)}, f32[3,2,256,1152]{3,2,1,0:T(8,128)S(1)}) custom-call(f32[4,2304]{1,0:T(4,128)S(1)} %copy-done.1, f32[2,272,1152]{2,1,0:T(8,128)} %get-tuple-element.58.value_hbm), custom_call_target="tpu_custom_call" | custom-call | tf_op jit(solution)/shard_map/prepare/pallas_call | solution.py:529
  58.1 0.3 collective-permute-done.14.refs_1_
  58.3 2.8 %finish.1 = bf16[256,2304]{1,0:T(8,128)(2,1)} custom-call(s32[1]{0:T(128)} %bitcast.keep_ref, f32[8,272]{1,0:T(8,128)S(1)} %get-tuple-element.57.refs_0_, f32[8,272]{1,0:T(8,128)S(1)} %collective-permute-done.14.refs_1_, f32[2,256,1152]{2,1,0:T(8,128)S(1)} %get-tuple-element.59.refs_2_, f32[3,2,256,1152]{3,2,1,0:T(8,128)S(1)} %get-tuple-element.60.refs_3_, ...), custom_call_target="tpu_custom_call" | custom-call | tf_op jit(solution)/shard_map/finish/pallas_call | solution.py:544
  (3 shorter events, 0.0 us)
Async XLA Ops:
  0.0 19.0 %collective-permute-start.3 = (bf16[1280,1152]{1,0:T(8,128)(2,1)}, bf16[1280,1152]{1,0:T(8,128)(2,1)}, u32[]{:S(2)}, u32[]{:S(2)}) collective-permute-start(bf16[1280,1152]{1,0:T(8,128)(2,1)} %refs_0_.1), channel_id=1, source_target_pairs={{0,1},{1,0},{2,3},{3,2},{4,5},{5,4},{6,7},{7,6},{8,9},{9,8},{10,11... | collective-permute-start | bytes 8847368 | tf_op jit(solution)/shard_map/ppermute | solution.py:441
  0.5 18.6 %collective-permute-start.4 = (bf16[1280,1152]{1,0:T(8,128)(2,1)}, bf16[1280,1152]{1,0:T(8,128)(2,1)}, u32[]{:S(2)}, u32[]{:S(2)}) collective-permute-start(bf16[1280,1152]{1,0:T(8,128)(2,1)} %refs_1_.1), channel_id=1, source_target_pairs={{0,1},{1,0},{2,3},{3,2},{4,5},{5,4},{6,7},{7,6},{8,9},{9,8},{10,11... | collective-permute-start | bytes 8847368 | tf_op jit(solution)/shard_map/ppermute | solution.py:442
  2.0 6.7 %collective-permute-start = (s32[8,256]{1,0:T(8,128)S(1)}, s32[8,256]{1,0:T(8,128)S(1)}, u32[]{:S(2)}, u32[]{:S(2)}) collective-permute-start(s32[8,256]{1,0:T(8,128)S(1)} %get-tuple-element.42.ids_ref), channel_id=1, source_target_pairs={{0,12},{4,8},{8,4},{12,0},{1,13},{5,9},{9,5},{13,1},{2,14},{6,10},... | collective-permute-start | bytes 24584 | tf_op jit(solution)/shard_map/ppermute | solution.py:345
  7.1 4.0 %collective-permute-start.1 = (s32[8,256]{1,0:T(8,128)S(1)}, s32[8,256]{1,0:T(8,128)S(1)}, u32[]{:S(2)}, u32[]{:S(2)}) collective-permute-start(s32[8,256]{1,0:T(8,128)S(1)} %get-tuple-element.42.ids_ref), channel_id=1, source_target_pairs={{0,8},{1,9},{4,13},{5,12},{8,1},{9,0},{12,4},{13,5},{2,10},{3,11},... | collective-permute-start | bytes 24584 | tf_op jit(solution)/shard_map/ppermute | solution.py:348
  7.2 4.0 %collective-permute-start.2 = (s32[8,256]{1,0:T(8,128)S(1)}, s32[8,256]{1,0:T(8,128)S(1)}, u32[]{:S(2)}, u32[]{:S(2)}) collective-permute-start(s32[8,256]{1,0:T(8,128)S(1)} %get-tuple-element.42.ids_ref), channel_id=1, source_target_pairs={{0,4},{4,0},{8,12},{12,8},{1,5},{5,1},{9,13},{13,9},{2,6},{6,2},{1... | collective-permute-start | bytes 24584 | tf_op jit(solution)/shard_map/ppermute | solution.py:345
  8.3 12.4 %copy-start = (bf16[256,2304]{1,0:T(8,128)(2,1)S(1)}, bf16[256,2304]{1,0:T(8,128)(2,1)}, u32[]{:S(2)}) copy-start(bf16[256,2304]{1,0:T(8,128)(2,1)} %refs_4_.1) | copy-start | bytes 3538948
  11.1 10.4 %collective-permute-start.9 = (bf16[640,256]{1,0:T(8,128)(2,1)S(1)}, bf16[640,256]{1,0:T(8,128)(2,1)}, u32[]{:S(2)}, u32[]{:S(2)}) collective-permute-start(bf16[640,256]{1,0:T(8,128)(2,1)S(1)} %pick_rows.4), channel_id=1, source_target_pairs={{0,4},{12,8},{1,5},{13,9},{2,6},{14,10},{3,7},{15,11},{16,20},{28,... | collective-permute-start | bytes 983048 | tf_op jit(solution)/shard_map/ppermute | solution.py:361
  13.9 10.1 %collective-permute-start.7 = (bf16[640,256]{1,0:T(8,128)(2,1)S(1)}, bf16[640,256]{1,0:T(8,128)(2,1)S(1)}, u32[]{:S(2)}, u32[]{:S(2)}) collective-permute-start(bf16[640,256]{1,0:T(8,128)(2,1)S(1)} %pick_rows.4), channel_id=1, source_target_pairs={{4,8},{8,4},{5,9},{9,5},{6,10},{10,6},{7,11},{11,7},{20,24},{24,20... | collective-permute-start | bytes 983048 | tf_op jit(solution)/shard_map/ppermute | solution.py:361
  15.4 13.7 %collective-permute-start.5 = (bf16[640,256]{1,0:T(8,128)(2,1)S(1)}, bf16[640,256]{1,0:T(8,128)(2,1)}, u32[]{:S(2)}, u32[]{:S(2)}) collective-permute-start(bf16[640,256]{1,0:T(8,128)(2,1)S(1)} %pick_rows.5), channel_id=1, source_target_pairs={{0,9},{1,8},{12,5},{13,4},{2,11},{3,10},{14,7},{15,6},{16,25},{17,... | collective-permute-start | bytes 983048 | tf_op jit(solution)/shard_map/ppermute | solution.py:348
  20.6 17.8 %collective-permute-start.6 = (bf16[640,256]{1,0:T(8,128)(2,1)}, bf16[640,256]{1,0:T(8,128)(2,1)}, u32[]{:S(2)}, u32[]{:S(2)}) collective-permute-start(bf16[640,256]{1,0:T(8,128)(2,1)} %pick_rows.6), channel_id=1, source_target_pairs={{0,4},{4,0},{8,12},{12,8},{1,5},{5,1},{9,13},{13,9},{2,6},{6,2},{1... | collective-permute-start | bytes 983048 | tf_op jit(solution)/shard_map/ppermute | solution.py:361
  22.6 17.0 %collective-permute-start.10 = (bf16[640,256]{1,0:T(8,128)(2,1)S(1)}, bf16[640,256]{1,0:T(8,128)(2,1)S(1)}, u32[]{:S(2)}, u32[]{:S(2)}) collective-permute-start(bf16[640,256]{1,0:T(8,128)(2,1)S(1)} %add.20), channel_id=1, source_target_pairs={{4,12},{8,0},{5,13},{9,1},{6,14},{10,2},{7,15},{11,3},{20,28},{24,... | collective-permute-start | bytes 983048 | tf_op jit(solution)/shard_map/ppermute | solution.py:361
  24.0 15.6 %collective-permute-start.8 = (bf16[16,2304]{1,0:T(8,128)(2,1)S(1)}, bf16[16,2304]{1,0:T(8,128)(2,1)S(1)}, u32[]{:S(2)}, u32[]{:S(2)}) collective-permute-start(bf16[16,2304]{1,0:T(8,128)(2,1)S(1)} %slice.6), channel_id=1, source_target_pairs={{0,1},{4,5},{8,9},{12,13},{2,3},{6,7},{10,11},{14,15},{16,17},{20,... | collective-permute-start | bytes 221192 | tf_op jit(solution)/shard_map/ppermute | solution.py:449
  39.7 11.1 %collective-permute-start.12 = (bf16[640,256]{1,0:T(8,128)(2,1)S(1)}, bf16[640,256]{1,0:T(8,128)(2,1)S(1)}, u32[]{:S(2)}, u32[]{:S(2)}) collective-permute-start(bf16[640,256]{1,0:T(8,128)(2,1)S(1)} %merge.1.body_ref), channel_id=1, source_target_pairs={{0,2},{2,0},{1,3},{3,1},{4,6},{6,4},{5,7},{7,5},{8,10},{10,8},{9,1... | collective-permute-start | bytes 983048 | tf_op jit(solution)/shard_map/ppermute | solution.py:469
  41.3 3.3 %collective-permute-start.13 = (bf16[640,128]{1,0:T(8,128)(2,1)S(1)}, bf16[640,128]{1,0:T(8,128)(2,1)S(1)}, u32[]{:S(2)}, u32[]{:S(2)}) collective-permute-start(bf16[640,128]{1,0:T(8,128)(2,1)S(1)} %slice.8), channel_id=1, source_target_pairs={{0,1},{2,3},{4,5},{6,7},{8,9},{10,11},{12,13},{14,15},{16,17},{18,... | collective-permute-start | bytes 491528 | tf_op jit(solution)/shard_map/ppermute | solution.py:482
  43.0 7.9 %collective-permute-start.11 = (bf16[640,128]{1,0:T(8,128)(2,1)S(1)}, bf16[640,128]{1,0:T(8,128)(2,1)S(1)}, u32[]{:S(2)}, u32[]{:S(2)}) collective-permute-start(bf16[640,128]{1,0:T(8,128)(2,1)S(1)} %slice.8), channel_id=1, source_target_pairs={{0,3},{2,1},{4,7},{6,5},{8,11},{10,9},{12,15},{14,13},{16,19},{18,... | collective-permute-start | bytes 491528 | tf_op jit(solution)/shard_map/ppermute | solution.py:482
  50.9 5.3 %copy-start.1 = (f32[4,2304]{1,0:T(4,128)S(1)}, f32[4,2304]{1,0:T(4,128)}, u32[]{:S(2)}) copy-start(f32[4,2304]{1,0:T(4,128)} %refs_5_.1) | copy-start | bytes 110596
  54.6 3.8 %collective-permute-start.14 = (f32[8,272]{1,0:T(8,128)S(1)}, f32[8,272]{1,0:T(8,128)S(1)}, u32[]{:S(2)}, u32[]{:S(2)}) collective-permute-start(f32[8,272]{1,0:T(8,128)S(1)} %get-tuple-element.57.refs_0_), channel_id=1, source_target_pairs={{0,2},{2,0},{1,3},{3,1},{4,6},{6,4},{5,7},{7,5},{8,10},{10,8},{9,1... | collective-permute-start | bytes 26120 | tf_op jit(solution)/shard_map/ppermute | solution.py:521

commit v24 on v21

--- a/solution.py
+++ b/solution.py
@@ -173,7 +173,7 @@
     for far, which in order:
         slot = rep if far == 0 else 1 - rep
         await_all(copies[far, which])
-        if not later:
+        if (far, which) == (0, 0):
             for f, w in order:
                 later += fetch(
                     count, tp, depth, weights[2 * f + w], next_ref.at[f, w], range(1, count),

time: 59.3 us -> 59.7 us (level)
  no operation moved by 1% of the time
where the time goes in v24:
time: 59.7 us; the launch traced here: 59.3 us
  starting transfers between devices  22.9 us (38%)
  Pallas kernels  20.3 us (34%)
  waiting for transfers between devices  15.5 us (26%)
    ppermute x4, waiting for transfers between devices, send(): return lax.ppermute(x, 'mem', pairs)  11.3 us
    pallas_call x1, Pallas kernels, shards(): pl.pallas_call(functools.partial(project_own_kernel, tps), in_specs=[smem...  6.01 us
    ppermute x2, starting transfers between devices, ask(): return lax.ppermute(ids, 'mem', [(i, i ^ x) for i in range(4)])  5.35 us
    ppermute x4, starting transfers between devices, send(): return lax.ppermute(x, 'mem', pairs)  4.76 us
    ppermute x2, starting transfers between devices, crossing(): lax.ppermute(x, ('mem', 'rep'), [(2 * a + b, 2 * c + d) for a, b, c, d in...  3.71 us
    pallas_call x1, Pallas kernels, shards(): pl.pallas_call(functools.partial(project_others_kernel, tps), in_specs=[s...  3.6 us
    pallas_call x4, Pallas kernels, pick(): pl.pallas_call(pick_kernel, in_specs=[pl.BlockSpec(memory_space=pltpu.SME...  3.46 us
    ppermute x2, waiting for transfers between devices, crossing(): lax.ppermute(x, ('mem', 'rep'), [(2 * a + b, 2 * c + d) for a, b, c, d in...  3.36 us
  transfers between devices with their start and end apart: 15, of which 6 were waited for; matrix products, arithmetic and copies ran while one was open for 0% of the time, Pallas kernels for 23%

profile of v24, /device:TPU:0, one launch (start us, length us, event | category | flops | bytes accessed | tf_op | source)
XLA Modules:
  0.0 59.3 jit_solution(6483131762789482694)
XLA Ops:
  0.0 0.5 collective-permute-start.3
  0.5 0.1 collective-permute-start.4
  0.5 1.5 %place_rows.1 = (s32[8,256]{1,0:T(8,128)S(1)}, bf16[8,80,1024]{2,1,0:T(8,128)(2,1)S(1)}, bf16[5,8,1024]{2,1,0:T(8,128)(2,1)S(1)}) custom-call(s32[8,256]{1,0:T(8,128)} %bitcast.11, s32[32,128]{1,0:T(8,128)} %bitcast.10, bf16[8,80,1024]{2,1,0:T(8,128)(2,1)} %bitcast.8, bf16[5,8,1024]{2,1,0:T(8,128)(2,1)} %bitcast.9), custom_call_target="tpu_custom_call" | custom-call | tf_op jit(solution)/shard_map/place_rows/pallas_call | solution.py:406
  2.0 5.1 %collective-permute-start = (s32[8,256]{1,0:T(8,128)S(1)}, s32[8,256]{1,0:T(8,128)S(1)}, u32[]{:S(2)}, u32[]{:S(2)}) collective-permute-start(s32[8,256]{1,0:T(8,128)S(1)} %get-tuple-element.39.ids_ref), channel_id=1, source_target_pairs={{0,12},{4,8},{8,4},{12,0},{1,13},{5,9},{9,5},{13,1},{2,14},{6,10},... | collective-permute-start | bytes 24584 | tf_op jit(solution)/shard_map/ppermute | solution.py:337
  7.1 0.0 collective-permute-start.1
  7.2 0.2 collective-permute-start.2
  7.4 0.9 %decode_tables.1.table_ref = bf16[8,80,1024]{2,1,0:T(8,128)(2,1)S(1)} custom-call(bf16[8,80,1024]{2,1,0:T(8,128)(2,1)S(1)} %get-tuple-element.31.codes_ref, bf16[5,8,1024]{2,1,0:T(8,128)(2,1)S(1)} %get-tuple-element.32.scales_ref), custom_call_target="tpu_custom_call" | custom-call | tf_op jit(solution)/shard_map/decode_tables/pallas_call | solution.py:423
  8.3 0.5 collective-permute-done.ids_ref
  8.8 0.9 %pick_rows.4 = bf16[640,256]{1,0:T(8,128)(2,1)S(1)} custom-call(s32[1]{0:T(128)} %bitcast.3.base_ref, s32[8,256]{1,0:T(8,128)S(1)} %collective-permute-done.ids_ref, bf16[8,80,1024]{2,1,0:T(8,128)(2,1)S(1)} %decode_tables.1.table_ref), custom_call_target="tpu_custom_call" | custom-call | tf_op jit(solution)/shard_map/pick_rows/pallas_call | solution.py:343
  9.6 1.5 %collective-permute-done.1.ids_ref = s32[8,256]{1,0:T(8,128)S(1)} collective-permute-done((s32[8,256]{1,0:T(8,128)S(1)}, s32[8,256]{1,0:T(8,128)S(1)}, u32[]{:S(2)}, u32[]{:S(2)}) %collective-permute-start.1) | collective-permute-done | bytes 8224 | tf_op jit(solution)/shard_map/ppermute | solution.py:340
  11.1 0.0 collective-permute-done.2.ids_ref
  11.1 2.0 %collective-permute-start.9 = (bf16[640,256]{1,0:T(8,128)(2,1)S(1)}, bf16[640,256]{1,0:T(8,128)(2,1)S(1)}, u32[]{:S(2)}, u32[]{:S(2)}) collective-permute-start(bf16[640,256]{1,0:T(8,128)(2,1)S(1)} %pick_rows.4), channel_id=1, source_target_pairs={{0,4},{12,8},{1,5},{13,9},{2,6},{14,10},{3,7},{15,11},{16,20},{28,... | collective-permute-start | bytes 983048 | tf_op jit(solution)/shard_map/ppermute | solution.py:353
  13.2 0.7 %collective-permute-start.7 = (bf16[640,256]{1,0:T(8,128)(2,1)S(1)}, bf16[640,256]{1,0:T(8,128)(2,1)S(1)}, u32[]{:S(2)}, u32[]{:S(2)}) collective-permute-start(bf16[640,256]{1,0:T(8,128)(2,1)S(1)} %pick_rows.4), channel_id=1, source_target_pairs={{4,8},{8,4},{5,9},{9,5},{6,10},{10,6},{7,11},{11,7},{20,24},{24,20... | collective-permute-start | bytes 983048 | tf_op jit(solution)/shard_map/ppermute | solution.py:353
  13.9 0.9 %pick_rows.5 = bf16[640,256]{1,0:T(8,128)(2,1)S(1)} custom-call(s32[1]{0:T(128)} %bitcast.3.base_ref, s32[8,256]{1,0:T(8,128)S(1)} %collective-permute-done.1.ids_ref, bf16[8,80,1024]{2,1,0:T(8,128)(2,1)S(1)} %decode_tables.1.table_ref), custom_call_target="tpu_custom_call" | custom-call | tf_op jit(solution)/shard_map/pick_rows/pallas_call | solution.py:343
  14.7 0.0 copy-start
  14.7 3.7 %collective-permute-start.5 = (bf16[640,256]{1,0:T(8,128)(2,1)S(1)}, bf16[640,256]{1,0:T(8,128)(2,1)S(1)}, u32[]{:S(2)}, u32[]{:S(2)}) collective-permute-start(bf16[640,256]{1,0:T(8,128)(2,1)S(1)} %pick_rows.5), channel_id=1, source_target_pairs={{0,9},{1,8},{12,5},{13,4},{2,11},{3,10},{14,7},{15,6},{16,25},{17,... | collective-permute-start | bytes 983048 | tf_op jit(solution)/shard_map/ppermute | solution.py:340
  18.5 0.0 collective-permute-done.3.refs_2_
  18.5 0.0 collective-permute-done.4.refs_3_
  18.5 0.9 %pick_rows.6 = bf16[640,256]{1,0:T(8,128)(2,1)S(1)} custom-call(s32[1]{0:T(128)} %bitcast.3.base_ref, s32[8,256]{1,0:T(8,128)S(1)} %collective-permute-done.2.ids_ref, bf16[8,80,1024]{2,1,0:T(8,128)(2,1)S(1)} %decode_tables.1.table_ref), custom_call_target="tpu_custom_call" | custom-call | tf_op jit(solution)/shard_map/pick_rows/pallas_call | solution.py:343
  19.3 0.7 %collective-permute-start.6 = (bf16[640,256]{1,0:T(8,128)(2,1)S(1)}, bf16[640,256]{1,0:T(8,128)(2,1)S(1)}, u32[]{:S(2)}, u32[]{:S(2)}) collective-permute-start(bf16[640,256]{1,0:T(8,128)(2,1)S(1)} %pick_rows.6), channel_id=1, source_target_pairs={{0,4},{4,0},{8,12},{12,8},{1,5},{5,1},{9,13},{13,9},{2,6},{6,2},{1... | collective-permute-start | bytes 983048 | tf_op jit(solution)/shard_map/ppermute | solution.py:353
  20.1 0.9 %pick_rows.7 = bf16[640,256]{1,0:T(8,128)(2,1)S(1)} custom-call(s32[1]{0:T(128)} %bitcast.3.base_ref, s32[8,256]{1,0:T(8,128)S(1)} %get-tuple-element.39.ids_ref, bf16[8,80,1024]{2,1,0:T(8,128)(2,1)S(1)} %decode_tables.1.table_ref), custom_call_target="tpu_custom_call" | custom-call | tf_op jit(solution)/shard_map/pick_rows/pallas_call | solution.py:343
  20.9 0.0 collective-permute-done.9
  21.0 0.1 add.20
  21.0 1.3 %collective-permute-start.10 = (bf16[640,256]{1,0:T(8,128)(2,1)S(1)}, bf16[640,256]{1,0:T(8,128)(2,1)S(1)}, u32[]{:S(2)}, u32[]{:S(2)}) collective-permute-start(bf16[640,256]{1,0:T(8,128)(2,1)S(1)} %add.20), channel_id=1, source_target_pairs={{4,12},{8,0},{5,13},{9,1},{6,14},{10,2},{7,15},{11,3},{20,28},{24,... | collective-permute-start | bytes 983048 | tf_op jit(solution)/shard_map/ppermute | solution.py:353
  22.3 0.0 copy-done
  22.4 0.0 collective-permute-done.7.refs_1_
  22.4 2.1 %collective-permute-start.8 = (bf16[16,2304]{1,0:T(8,128)(2,1)S(1)}, bf16[16,2304]{1,0:T(8,128)(2,1)S(1)}, u32[]{:S(2)}, u32[]{:S(2)}) collective-permute-start(bf16[16,2304]{1,0:T(8,128)(2,1)S(1)} %slice.6), channel_id=1, source_target_pairs={{0,1},{4,5},{8,9},{12,13},{2,3},{6,7},{10,11},{14,15},{16,17},{20,... | collective-permute-start | bytes 221192 | tf_op jit(solution)/shard_map/ppermute | solution.py:438
  24.5 1.9 %collective-permute-done.5 = bf16[640,256]{1,0:T(8,128)(2,1)S(1)} collective-permute-done((bf16[640,256]{1,0:T(8,128)(2,1)S(1)}, bf16[640,256]{1,0:T(8,128)(2,1)S(1)}, u32[]{:S(2)}, u32[]{:S(2)}) %collective-permute-start.5) | collective-permute-done | bytes 327712 | tf_op jit(solution)/shard_map/ppermute | solution.py:340
  26.4 7.0 %collective-permute-done.6 = bf16[640,256]{1,0:T(8,128)(2,1)S(1)} collective-permute-done((bf16[640,256]{1,0:T(8,128)(2,1)S(1)}, bf16[640,256]{1,0:T(8,128)(2,1)S(1)}, u32[]{:S(2)}, u32[]{:S(2)}) %collective-permute-start.6) | collective-permute-done | bytes 327712 | tf_op jit(solution)/shard_map/ppermute | solution.py:353
  33.5 0.0 collective-permute-done.8.refs_4_
  33.5 4.3 %collective-permute-done.10.refs_2_ = bf16[640,256]{1,0:T(8,128)(2,1)S(1)} collective-permute-done((bf16[640,256]{1,0:T(8,128)(2,1)S(1)}, bf16[640,256]{1,0:T(8,128)(2,1)S(1)}, u32[]{:S(2)}, u32[]{:S(2)}) %collective-permute-start.10) | collective-permute-done | bytes 327712 | tf_op jit(solution)/shard_map/ppermute | solution.py:353
  37.8 0.1 merge.1.body_ref
  37.9 1.6 %collective-permute-start.12 = (bf16[640,256]{1,0:T(8,128)(2,1)S(1)}, bf16[640,256]{1,0:T(8,128)(2,1)S(1)}, u32[]{:S(2)}, u32[]{:S(2)}) collective-permute-start(bf16[640,256]{1,0:T(8,128)(2,1)S(1)} %merge.1.body_ref), channel_id=1, source_target_pairs={{0,2},{2,0},{1,3},{3,1},{4,6},{6,4},{5,7},{7,5},{8,10},{10,8},{9,1... | collective-permute-start | bytes 983048 | tf_op jit(solution)/shard_map/ppermute | solution.py:449
  39.5 1.7 %collective-permute-start.13 = (bf16[640,128]{1,0:T(8,128)(2,1)S(1)}, bf16[640,128]{1,0:T(8,128)(2,1)S(1)}, u32[]{:S(2)}, u32[]{:S(2)}) collective-permute-start(bf16[640,128]{1,0:T(8,128)(2,1)S(1)} %slice.8), channel_id=1, source_target_pairs={{0,1},{2,3},{4,5},{6,7},{8,9},{10,11},{12,13},{14,15},{16,17},{18,... | collective-permute-start | bytes 491528 | tf_op jit(solution)/shard_map/ppermute | solution.py:462
  41.2 1.6 %collective-permute-start.11 = (bf16[640,128]{1,0:T(8,128)(2,1)S(1)}, bf16[640,128]{1,0:T(8,128)(2,1)S(1)}, u32[]{:S(2)}, u32[]{:S(2)}) collective-permute-start(bf16[640,128]{1,0:T(8,128)(2,1)S(1)} %slice.8), channel_id=1, source_target_pairs={{0,3},{2,1},{4,7},{6,5},{8,11},{10,9},{12,15},{14,13},{16,19},{18,... | collective-permute-start | bytes 491528 | tf_op jit(solution)/shard_map/ppermute | solution.py:462
  42.8 0.1 pad_add_fusion.where_ref
  42.9 0.0 collective-permute-done.13.rim_ref
  42.9 6.0 %project_own.1 = (f32[2,272,1152]{2,1,0:T(8,128)S(1)}, f32[2,272,1152]{2,1,0:T(8,128)S(1)}, bf16[2,2,640,1152]{3,2,1,0:T(8,128)(2,1)S(1)}, bf16[2,272,1152]{2,1,0:T(8,128)(2,1)S(1)}, f32[272,8]{1,0:T(8,128)S(1)}) custom-call(s32[2]{0:T(128)S(1)} %pad_add_fusion.where_ref, bf16[640,128]{1,0:T(8,128)(2,1)S(1)} %collective-permute-done.13.rim_ref, ...), custom_call_target="tpu_custom_call" | custom-call | tf_op jit(solution)/shard_map/project_own/pallas_call | solution.py:468
  48.9 0.0 collective-permute-done.11.refs_0_
  48.9 0.0 collective-permute-done.12.refs_1_
  49.0 0.0 copy-start.1
  49.0 3.6 %project_others.1 = (f32[2,272,1152]{2,1,0:T(8,128)}, f32[8,272]{1,0:T(8,128)S(1)}) custom-call(s32[2]{0:T(128)S(1)} %pad_add_fusion.where_ref, bf16[640,128]{1,0:T(8,128)(2,1)S(1)} %collective-permute-done.11.refs_0_, bf16[640,256]{1,0:T(8,128)(2,1)S(1)} %collective-permute-done.12.refs_1_, bf16[2,2,640,1152]{3,2,1,0:T(8,128)(2,1)S(1)} %get-tuple-element.46.refs_2_, ...), custom_call_target="tpu_custom_call" | custom-call | tf_op jit(solution)/shard_map/project_others/pallas_call | solution.py:487
  52.6 1.6 %collective-permute-start.14 = (f32[8,272]{1,0:T(8,128)S(1)}, f32[8,272]{1,0:T(8,128)S(1)}, u32[]{:S(2)}, u32[]{:S(2)}) collective-permute-start(f32[8,272]{1,0:T(8,128)S(1)} %get-tuple-element.51.refs_0_), channel_id=1, source_target_pairs={{0,2},{2,0},{1,3},{3,1},{4,6},{6,4},{5,7},{7,5},{8,10},{10,8},{9,1... | collective-permute-start | bytes 26120 | tf_op jit(solution)/shard_map/ppermute | solution.py:501
  54.1 0.0 copy-done.1
  54.1 1.9 %prepare.1 = (f32[2,256,1152]{2,1,0:T(8,128)S(1)}, f32[3,2,256,1152]{3,2,1,0:T(8,128)S(1)}) custom-call(f32[4,2304]{1,0:T(4,128)S(1)} %copy-done.1, f32[2,272,1152]{2,1,0:T(8,128)} %get-tuple-element.52.value_hbm), custom_call_target="tpu_custom_call" | custom-call | tf_op jit(solution)/shard_map/prepare/pallas_call | solution.py:509
  56.1 0.3 collective-permute-done.14.refs_1_
  56.3 2.8 %finish.1 = bf16[256,2304]{1,0:T(8,128)(2,1)} custom-call(s32[1]{0:T(128)} %bitcast.keep_ref, f32[8,272]{1,0:T(8,128)S(1)} %get-tuple-element.51.refs_0_, f32[8,272]{1,0:T(8,128)S(1)} %collective-permute-done.14.refs_1_, f32[2,256,1152]{2,1,0:T(8,128)S(1)} %get-tuple-element.53.refs_2_, f32[3,2,256,1152]{3,2,1,0:T(8,128)S(1)} %get-tuple-element.54.refs_3_, ...), custom_call_target="tpu_custom_call" | custom-call | tf_op jit(solution)/shard_map/finish/pallas_call | solution.py:524
  (3 shorter events, 0.1 us)
Async XLA Ops:
  0.0 18.5 %collective-permute-start.3 = (bf16[1280,1152]{1,0:T(8,128)(2,1)}, bf16[1280,1152]{1,0:T(8,128)(2,1)}, u32[]{:S(2)}, u32[]{:S(2)}) collective-permute-start(bf16[1280,1152]{1,0:T(8,128)(2,1)} %refs_0_.1), channel_id=1, source_target_pairs={{0,1},{1,0},{2,3},{3,2},{4,5},{5,4},{6,7},{7,6},{8,9},{9,8},{10,11... | collective-permute-start | bytes 8847368 | tf_op jit(solution)/shard_map/ppermute | solution.py:432
  0.5 18.0 %collective-permute-start.4 = (bf16[1280,1152]{1,0:T(8,128)(2,1)}, bf16[1280,1152]{1,0:T(8,128)(2,1)}, u32[]{:S(2)}, u32[]{:S(2)}) collective-permute-start(bf16[1280,1152]{1,0:T(8,128)(2,1)} %refs_1_.1), channel_id=1, source_target_pairs={{0,1},{1,0},{2,3},{3,2},{4,5},{5,4},{6,7},{7,6},{8,9},{9,8},{10,11... | collective-permute-start | bytes 8847368 | tf_op jit(solution)/shard_map/ppermute | solution.py:433
  2.0 6.7 %collective-permute-start = (s32[8,256]{1,0:T(8,128)S(1)}, s32[8,256]{1,0:T(8,128)S(1)}, u32[]{:S(2)}, u32[]{:S(2)}) collective-permute-start(s32[8,256]{1,0:T(8,128)S(1)} %get-tuple-element.39.ids_ref), channel_id=1, source_target_pairs={{0,12},{4,8},{8,4},{12,0},{1,13},{5,9},{9,5},{13,1},{2,14},{6,10},... | collective-permute-start | bytes 24584 | tf_op jit(solution)/shard_map/ppermute | solution.py:337
  7.1 4.0 %collective-permute-start.1 = (s32[8,256]{1,0:T(8,128)S(1)}, s32[8,256]{1,0:T(8,128)S(1)}, u32[]{:S(2)}, u32[]{:S(2)}) collective-permute-start(s32[8,256]{1,0:T(8,128)S(1)} %get-tuple-element.39.ids_ref), channel_id=1, source_target_pairs={{0,8},{1,9},{4,13},{5,12},{8,1},{9,0},{12,4},{13,5},{2,10},{3,11},... | collective-permute-start | bytes 24584 | tf_op jit(solution)/shard_map/ppermute | solution.py:340
  7.2 4.0 %collective-permute-start.2 = (s32[8,256]{1,0:T(8,128)S(1)}, s32[8,256]{1,0:T(8,128)S(1)}, u32[]{:S(2)}, u32[]{:S(2)}) collective-permute-start(s32[8,256]{1,0:T(8,128)S(1)} %get-tuple-element.39.ids_ref), channel_id=1, source_target_pairs={{0,4},{4,0},{8,12},{12,8},{1,5},{5,1},{9,13},{13,9},{2,6},{6,2},{1... | collective-permute-start | bytes 24584 | tf_op jit(solution)/shard_map/ppermute | solution.py:337
  11.1 9.8 %collective-permute-start.9 = (bf16[640,256]{1,0:T(8,128)(2,1)S(1)}, bf16[640,256]{1,0:T(8,128)(2,1)S(1)}, u32[]{:S(2)}, u32[]{:S(2)}) collective-permute-start(bf16[640,256]{1,0:T(8,128)(2,1)S(1)} %pick_rows.4), channel_id=1, source_target_pairs={{0,4},{12,8},{1,5},{13,9},{2,6},{14,10},{3,7},{15,11},{16,20},{28,... | collective-permute-start | bytes 983048 | tf_op jit(solution)/shard_map/ppermute | solution.py:353
  13.2 9.2 %collective-permute-start.7 = (bf16[640,256]{1,0:T(8,128)(2,1)S(1)}, bf16[640,256]{1,0:T(8,128)(2,1)S(1)}, u32[]{:S(2)}, u32[]{:S(2)}) collective-permute-start(bf16[640,256]{1,0:T(8,128)(2,1)S(1)} %pick_rows.4), channel_id=1, source_target_pairs={{4,8},{8,4},{5,9},{9,5},{6,10},{10,6},{7,11},{11,7},{20,24},{24,20... | collective-permute-start | bytes 983048 | tf_op jit(solution)/shard_map/ppermute | solution.py:353
  14.7 7.6 %copy-start = (bf16[256,2304]{1,0:T(8,128)(2,1)S(1)}, bf16[256,2304]{1,0:T(8,128)(2,1)}, u32[]{:S(2)}) copy-start(bf16[256,2304]{1,0:T(8,128)(2,1)} %refs_4_.1) | copy-start | bytes 3538948
  14.7 11.6 %collective-permute-start.5 = (bf16[640,256]{1,0:T(8,128)(2,1)S(1)}, bf16[640,256]{1,0:T(8,128)(2,1)S(1)}, u32[]{:S(2)}, u32[]{:S(2)}) collective-permute-start(bf16[640,256]{1,0:T(8,128)(2,1)S(1)} %pick_rows.5), channel_id=1, source_target_pairs={{0,9},{1,8},{12,5},{13,4},{2,11},{3,10},{14,7},{15,6},{16,25},{17,... | collective-permute-start | bytes 983048 | tf_op jit(solution)/shard_map/ppermute | solution.py:340
  19.3 14.1 %collective-permute-start.6 = (bf16[640,256]{1,0:T(8,128)(2,1)S(1)}, bf16[640,256]{1,0:T(8,128)(2,1)S(1)}, u32[]{:S(2)}, u32[]{:S(2)}) collective-permute-start(bf16[640,256]{1,0:T(8,128)(2,1)S(1)} %pick_rows.6), channel_id=1, source_target_pairs={{0,4},{4,0},{8,12},{12,8},{1,5},{5,1},{9,13},{13,9},{2,6},{6,2},{1... | collective-permute-start | bytes 983048 | tf_op jit(solution)/shard_map/ppermute | solution.py:353
  21.0 16.7 %collective-permute-start.10 = (bf16[640,256]{1,0:T(8,128)(2,1)S(1)}, bf16[640,256]{1,0:T(8,128)(2,1)S(1)}, u32[]{:S(2)}, u32[]{:S(2)}) collective-permute-start(bf16[640,256]{1,0:T(8,128)(2,1)S(1)} %add.20), channel_id=1, source_target_pairs={{4,12},{8,0},{5,13},{9,1},{6,14},{10,2},{7,15},{11,3},{20,28},{24,... | collective-permute-start | bytes 983048 | tf_op jit(solution)/shard_map/ppermute | solution.py:353
  22.4 11.1 %collective-permute-start.8 = (bf16[16,2304]{1,0:T(8,128)(2,1)S(1)}, bf16[16,2304]{1,0:T(8,128)(2,1)S(1)}, u32[]{:S(2)}, u32[]{:S(2)}) collective-permute-start(bf16[16,2304]{1,0:T(8,128)(2,1)S(1)} %slice.6), channel_id=1, source_target_pairs={{0,1},{4,5},{8,9},{12,13},{2,3},{6,7},{10,11},{14,15},{16,17},{20,... | collective-permute-start | bytes 221192 | tf_op jit(solution)/shard_map/ppermute | solution.py:438
  37.9 11.1 %collective-permute-start.12 = (bf16[640,256]{1,0:T(8,128)(2,1)S(1)}, bf16[640,256]{1,0:T(8,128)(2,1)S(1)}, u32[]{:S(2)}, u32[]{:S(2)}) collective-permute-start(bf16[640,256]{1,0:T(8,128)(2,1)S(1)} %merge.1.body_ref), channel_id=1, source_target_pairs={{0,2},{2,0},{1,3},{3,1},{4,6},{6,4},{5,7},{7,5},{8,10},{10,8},{9,1... | collective-permute-start | bytes 983048 | tf_op jit(solution)/shard_map/ppermute | solution.py:449
  39.5 3.5 %collective-permute-start.13 = (bf16[640,128]{1,0:T(8,128)(2,1)S(1)}, bf16[640,128]{1,0:T(8,128)(2,1)S(1)}, u32[]{:S(2)}, u32[]{:S(2)}) collective-permute-start(bf16[640,128]{1,0:T(8,128)(2,1)S(1)} %slice.8), channel_id=1, source_target_pairs={{0,1},{2,3},{4,5},{6,7},{8,9},{10,11},{12,13},{14,15},{16,17},{18,... | collective-permute-start | bytes 491528 | tf_op jit(solution)/shard_map/ppermute | solution.py:462
  41.2 7.7 %collective-permute-start.11 = (bf16[640,128]{1,0:T(8,128)(2,1)S(1)}, bf16[640,128]{1,0:T(8,128)(2,1)S(1)}, u32[]{:S(2)}, u32[]{:S(2)}) collective-permute-start(bf16[640,128]{1,0:T(8,128)(2,1)S(1)} %slice.8), channel_id=1, source_target_pairs={{0,3},{2,1},{4,7},{6,5},{8,11},{10,9},{12,15},{14,13},{16,19},{18,... | collective-permute-start | bytes 491528 | tf_op jit(solution)/shard_map/ppermute | solution.py:462
  49.0 5.2 %copy-start.1 = (f32[4,2304]{1,0:T(4,128)S(1)}, f32[4,2304]{1,0:T(4,128)}, u32[]{:S(2)}) copy-start(f32[4,2304]{1,0:T(4,128)} %refs_5_.3) | copy-start | bytes 110596
  52.6 3.8 %collective-permute-start.14 = (f32[8,272]{1,0:T(8,128)S(1)}, f32[8,272]{1,0:T(8,128)S(1)}, u32[]{:S(2)}, u32[]{:S(2)}) collective-permute-start(f32[8,272]{1,0:T(8,128)S(1)} %get-tuple-element.51.refs_0_), channel_id=1, source_target_pairs={{0,2},{2,0},{1,3},{3,1},{4,6},{6,4},{5,7},{7,5},{8,10},{10,8},{9,1... | collective-permute-start | bytes 26120 | tf_op jit(solution)/shard_map/ppermute | solution.py:501

commit v25 on v21

--- a/solution.py
+++ b/solution.py
@@ -42,38 +42,38 @@
     return x.astype(F32).astype(BF16)
 
 
-def place_kernel(
-    ids_hbm, place_hbm, codes_hbm, scales_hbm, out_ref, codes_ref, scales_ref, ids_ref, place_ref, sems
-):
-    copies = [
-        pltpu.make_async_copy(place_hbm, place_ref, sems.at[0]),
-        pltpu.make_async_copy(ids_hbm, ids_ref, sems.at[1]),
-        pltpu.make_async_copy(scales_hbm, scales_ref, sems.at[2]),
-    ]
-    for n in range(codes_ref.shape[0]):
-        copies.append(
-            pltpu.make_async_copy(codes_hbm.at[n], codes_ref.at[n], sems.at[3 + n])
-        )
-    for copy in copies:
-        copy.start()
-    copies[0].wait()
-    place = place_ref[...]
+def place_ids(ids, place, out_ref):
     rows = place.shape[0]
-    heads, tokens = ids_ref.shape
+    heads, tokens = ids.shape
     eye = unit(LANES, BF16)
     table = jnp.concatenate(
         [dot_nt(eye, to_bf16(place >> 8)), dot_nt(eye, to_bf16(place & 255))], axis=0
     ).astype(BF16)
-    copies[1].wait()
     for head in range(heads):
-        row = ids_ref[head : head + 1, :]
+        row = ids[head : head + 1, :]
         hot = to_bf16(iota((rows, tokens), 0) == (row >> 7))
         both = dot(table, hot)
         value = both[:LANES] * 256.0 + both[LANES:]
         chosen = jnp.where(iota(value.shape, 0) == (row & 127), value, 0.0)
         out_ref[head : head + 1, :] = jnp.sum(chosen, axis=0, keepdims=True).astype(I32)
-    for copy in copies[2:]:
-        copy.wait()
+
+
+def place_kernel(ids_ref, place_ref, out_ref):
+    place_ids(ids_ref[...], place_ref[...], out_ref)
+
+
+def fetch_kernel(
+    place_hbm, ids_hbm, codes_hbm, scales_hbm, place_ref, codes_ref, scales_ref, out_ref, ids_ref, sems
+):
+    pairs = [(place_hbm, place_ref), (ids_hbm, ids_ref), (scales_hbm, scales_ref)]
+    pairs += [(codes_hbm.at[n], codes_ref.at[n]) for n in range(codes_ref.shape[0])]
+    copies = []
+    for source, target in pairs:
+        copies.append(pltpu.make_async_copy(source, target, sems.at[len(copies)]))
+        copies[-1].start()
+    await_all(copies[:2])
+    place_ids(ids_ref[...], place_ref[...], out_ref)
+    await_all(copies[2:])
 
 
 def decode_kernel(codes_ref, scales_ref, out_ref):
@@ -305,7 +305,7 @@
     return pltpu.CompilerParams(vmem_limit_bytes=mib << 20)
 
 
-def scattered_sum(stored, decoded, here, meanwhile, settled):
+def scattered_sum(raw, place, stored, decoded, here, meanwhile, settled):
     mems = lax.axis_size("mem")
     heads, width, rows = decoded.shape
     tokens = stored.shape[1]
@@ -327,7 +327,7 @@
     return total, meanwhile(partial), settled
 
 
-def line_sum(stored, decoded, here, meanwhile, settled):
+def line_sum(raw, place, stored, decoded, here, meanwhile, settled):
     heads, width, rows = decoded.shape
     tokens = stored.shape[1]
     base = (here * rows).astype(I32).reshape(1)
@@ -352,20 +352,20 @@
     def send(x, *pairs):
         return lax.ppermute(x, "mem", pairs)
 
-    first = ask(stored, 3)
+    first = ask(raw, 3)
     second = crossing(
-        stored,
+        raw,
         [(m, r, m ^ 2, r ^ int(m in (1, 2))) for m in range(4) for r in range(2)],
     )
-    third = ask(stored, 1)
-    rows_3 = pick(first)
+    third = ask(raw, 1)
+    rows_3 = pick(place(first))
     rows_3, second, third = lax.optimization_barrier((rows_3, second, third))
     inward = send(rows_3, (0, 1), (3, 2))
     across = send(rows_3, (1, 2), (2, 1))
-    rows_2 = pick(after(second, rows_3))
+    rows_2 = pick(place(after(second, rows_3)))
     third, settled = lax.optimization_barrier((after(third, rows_2), settled))
     past = crossing(rows_2, [(m, r, m ^ 2, r ^ 1) for m in (0, 3) for r in range(2)])
-    rows_1 = pick(third)
+    rows_1 = pick(place(third))
     own = pick(after(stored, rows_1))
     beside = send(rows_1, (0, 1), (1, 0), (2, 3), (3, 2))
     onward = after(rows_2, rows_1, own) + inward
@@ -403,23 +403,36 @@
     places = row_place.reshape(-1, LANES)
     codes = table_codes.transpose(0, 2, 1)
     scales = table_scales.transpose(2, 0, 1)
-    stored, codes, scales = pl.pallas_call(
-        place_kernel,
+    raw = row_ids.T
+    placed = jax.ShapeDtypeStruct(raw.shape, I32)
+    places, codes, scales, stored = pl.pallas_call(
+        fetch_kernel,
         in_specs=[anywhere] * 4,
-        out_specs=(resident,) * 3,
+        out_specs=(resident,) * 4,
         out_shape=(
-            jax.ShapeDtypeStruct((heads, tokens), I32),
+            jax.ShapeDtypeStruct(places.shape, I32),
             jax.ShapeDtypeStruct(codes.shape, BF16),
             jax.ShapeDtypeStruct(scales.shape, BF16),
+            placed,
         ),
         scratch_shapes=[
-            pltpu.VMEM((heads, tokens), I32),
-            pltpu.VMEM(places.shape, I32),
+            pltpu.VMEM(raw.shape, I32),
             pltpu.SemaphoreType.DMA((heads + 3,)),
         ],
         compiler_params=limit(4),
-        name="place_rows",
-    )(*[in_hbm(x) for x in (row_ids.T, places, codes, scales)])
+        name="fetch_tables",
+    )(*[in_hbm(x) for x in (places, raw, codes, scales)])
+
+    def place(ids):
+        return pl.pallas_call(
+            place_kernel,
+            in_specs=[resident] * 2,
+            out_specs=resident,
+            out_shape=placed,
+            compiler_params=limit(4),
+            name="place_rows",
+        )(ids, places)
+
     decoded = pl.pallas_call(
         decode_kernel,
         in_specs=[resident] * 2,
@@ -439,7 +452,7 @@
 
     summed = line_sum if mems == 4 else scattered_sum
     memory, hidden_halo, others = summed(
-        stored, decoded, here, meanwhile, (other_key, other_value)
+        raw, place, stored, decoded, here, meanwhile, (other_key, other_value)
     )
     weights = [in_hbm(w) for w in (key_weight, value_weight, *others)]
 

time: 59.3 us -> 59.6 us (level)
  waiting for transfers between devices: 15.5 us -> 12.9 us
  Pallas kernels: 20 us -> 21.7 us
  starting transfers between devices: 22.9 us -> 24 us
    ppermute x2, waiting for transfers between devices: 3.36 us -> 1.34 us  [crossing(): lax.ppermute(x, ('mem', 'rep'), [(2 * a + b, 2 * c + d) for a, b, c, d in...]
    pallas_call x1 -> x4, Pallas kernels: 1.51 us -> 3.24 us  [the longest x3 1.73 us: place(): pl.pallas_call(place_kernel, in_specs=[resident] * 2, out_specs=resident,...]
    ppermute x4, starting transfers between devices: 4.76 us -> 5.68 us  [send(): return lax.ppermute(x, 'mem', pairs)]
    ppermute x1, starting transfers between devices: 2.12 us -> 2.86 us  [meanwhile(): return lax.ppermute(tail, ('mem', 'rep'), needed)]
  transfers between devices with their start and end apart: 15 -> 15, of which waited for: 6 -> 4; matrix products, arithmetic and copies ran while one was open for 0% -> 0% of each run, Pallas kernels for 23% -> 26%
where the time goes in v25:
time: 59.6 us; the launch traced here: 59.2 us
  starting transfers between devices  24 us (40%)
  Pallas kernels  21.7 us (36%)
  waiting for transfers between devices  12.9 us (22%)
    ppermute x4, waiting for transfers between devices, send(): return lax.ppermute(x, 'mem', pairs)  11.2 us
    ppermute x4, starting transfers between devices, send(): return lax.ppermute(x, 'mem', pairs)  5.68 us
    pallas_call x1, Pallas kernels, shards(): pl.pallas_call(functools.partial(project_own_kernel, tps), in_specs=[smem...  5.66 us
    ppermute x2, starting transfers between devices, ask(): return lax.ppermute(ids, 'mem', [(i, i ^ x) for i in range(4)])  5.22 us
    pallas_call x1, Pallas kernels, shards(): pl.pallas_call(functools.partial(project_others_kernel, tps), in_specs=[s...  3.6 us
    pallas_call x4, Pallas kernels, pick(): pl.pallas_call(pick_kernel, in_specs=[pl.BlockSpec(memory_space=pltpu.SME...  3.46 us
    ppermute x2, starting transfers between devices, next_rim(): return lax.ppermute(rim, ('mem', 'tp', 'rep'), pairs)  3.34 us
    ppermute x2, starting transfers between devices, crossing(): lax.ppermute(x, ('mem', 'rep'), [(2 * a + b, 2 * c + d) for a, b, c, d in...  3.28 us
  transfers between devices with their start and end apart: 15, of which 4 were waited for; matrix products, arithmetic and copies ran while one was open for 0% of the time, Pallas kernels for 26%

profile of v25, /device:TPU:0, one launch (start us, length us, event | category | flops | bytes accessed | tf_op | source)
XLA Modules:
  0.0 59.2 jit_solution(14869833887900838834)
XLA Ops:
  0.0 0.5 collective-permute-start.3
  0.5 0.1 collective-permute-start.4
  0.5 5.0 %collective-permute-start = (s32[8,256]{1,0:T(8,128)}, s32[8,256]{1,0:T(8,128)S(1)}, u32[]{:S(2)}, u32[]{:S(2)}) collective-permute-start(s32[8,256]{1,0:T(8,128)} %bitcast.11), channel_id=1, source_target_pairs={{0,12},{4,8},{8,4},{12,0},{1,13},{5,9},{9,5},{13,1},{2,14},{6,10},... | collective-permute-start | bytes 24584 | tf_op jit(solution)/shard_map/ppermute | solution.py:337
  5.6 0.0 collective-permute-start.1
  5.6 0.2 collective-permute-start.2
  5.7 1.5 %fetch_tables.1 = (s32[32,128]{1,0:T(8,128)S(1)}, bf16[8,80,1024]{2,1,0:T(8,128)(2,1)S(1)}, bf16[5,8,1024]{2,1,0:T(8,128)(2,1)S(1)}, s32[8,256]{1,0:T(8,128)S(1)}) custom-call(s32[32,128]{1,0:T(8,128)} %bitcast.10, s32[8,256]{1,0:T(8,128)} %bitcast.14, bf16[8,80,1024]{2,1,0:T(8,128)(2,1)} %bitcast.8, bf16[5,8,1024]{2,1,0:T(8,128)(2,1)} %bitcast.9), custom_call_target="tpu_custom_call" | custom-call | tf_op jit(solution)/shard_map/fetch_tables/pallas_call | solution.py:408
  7.3 0.9 %decode_tables.1.table_ref = bf16[8,80,1024]{2,1,0:T(8,128)(2,1)S(1)} custom-call(bf16[8,80,1024]{2,1,0:T(8,128)(2,1)S(1)} %get-tuple-element.33.codes_ref, bf16[5,8,1024]{2,1,0:T(8,128)(2,1)S(1)} %get-tuple-element.34.scales_ref), custom_call_target="tpu_custom_call" | custom-call | tf_op jit(solution)/shard_map/decode_tables/pallas_call | solution.py:436
  8.1 0.0 collective-permute-done.ids_ref
  8.1 0.6 place_rows.3.ids_ref
  8.7 0.9 %pick_rows.4 = bf16[640,256]{1,0:T(8,128)(2,1)S(1)} custom-call(s32[1]{0:T(128)} %bitcast.3.base_ref, s32[8,256]{1,0:T(8,128)S(1)} %place_rows.3.ids_ref, bf16[8,80,1024]{2,1,0:T(8,128)(2,1)S(1)} %decode_tables.1.table_ref), custom_call_target="tpu_custom_call" | custom-call | tf_op jit(solution)/shard_map/pick_rows/pallas_call | solution.py:343
  9.6 0.2 collective-permute-done.1.ids_ref
  9.7 0.0 collective-permute-done.2.ids_ref
  9.8 3.6 %collective-permute-start.9 = (bf16[640,256]{1,0:T(8,128)(2,1)S(1)}, bf16[640,256]{1,0:T(8,128)(2,1)S(1)}, u32[]{:S(2)}, u32[]{:S(2)}) collective-permute-start(bf16[640,256]{1,0:T(8,128)(2,1)S(1)} %pick_rows.4), channel_id=1, source_target_pairs={{0,4},{12,8},{1,5},{13,9},{2,6},{14,10},{3,7},{15,11},{16,20},{28,... | collective-permute-start | bytes 983048 | tf_op jit(solution)/shard_map/ppermute | solution.py:353
  13.4 0.7 %collective-permute-start.7 = (bf16[640,256]{1,0:T(8,128)(2,1)S(1)}, bf16[640,256]{1,0:T(8,128)(2,1)S(1)}, u32[]{:S(2)}, u32[]{:S(2)}) collective-permute-start(bf16[640,256]{1,0:T(8,128)(2,1)S(1)} %pick_rows.4), channel_id=1, source_target_pairs={{4,8},{8,4},{5,9},{9,5},{6,10},{10,6},{7,11},{11,7},{20,24},{24,20... | collective-permute-start | bytes 983048 | tf_op jit(solution)/shard_map/ppermute | solution.py:353
  14.1 0.6 place_rows.4.ids_ref
  14.7 0.9 %pick_rows.5 = bf16[640,256]{1,0:T(8,128)(2,1)S(1)} custom-call(s32[1]{0:T(128)} %bitcast.3.base_ref, s32[8,256]{1,0:T(8,128)S(1)} %place_rows.4.ids_ref, bf16[8,80,1024]{2,1,0:T(8,128)(2,1)S(1)} %decode_tables.1.table_ref), custom_call_target="tpu_custom_call" | custom-call | tf_op jit(solution)/shard_map/pick_rows/pallas_call | solution.py:343
  15.5 0.0 copy-start
  15.5 3.3 %collective-permute-start.5 = (bf16[640,256]{1,0:T(8,128)(2,1)S(1)}, bf16[640,256]{1,0:T(8,128)(2,1)S(1)}, u32[]{:S(2)}, u32[]{:S(2)}) collective-permute-start(bf16[640,256]{1,0:T(8,128)(2,1)S(1)} %pick_rows.5), channel_id=1, source_target_pairs={{0,9},{1,8},{12,5},{13,4},{2,11},{3,10},{14,7},{15,6},{16,25},{17,... | collective-permute-start | bytes 983048 | tf_op jit(solution)/shard_map/ppermute | solution.py:340
  18.8 0.0 collective-permute-done.3.refs_2_
  18.8 0.0 collective-permute-done.4.refs_3_
  18.9 0.6 place_rows.5.ids_ref
  19.4 0.9 %pick_rows.6 = bf16[640,256]{1,0:T(8,128)(2,1)S(1)} custom-call(s32[1]{0:T(128)} %bitcast.3.base_ref, s32[8,256]{1,0:T(8,128)S(1)} %place_rows.5.ids_ref, bf16[8,80,1024]{2,1,0:T(8,128)(2,1)S(1)} %decode_tables.1.table_ref), custom_call_target="tpu_custom_call" | custom-call | tf_op jit(solution)/shard_map/pick_rows/pallas_call | solution.py:343
  20.3 0.1 collective-permute-start.6
  20.4 0.9 %pick_rows.7 = bf16[640,256]{1,0:T(8,128)(2,1)S(1)} custom-call(s32[1]{0:T(128)} %bitcast.3.base_ref, s32[8,256]{1,0:T(8,128)S(1)} %get-tuple-element.41.ids_ref, bf16[8,80,1024]{2,1,0:T(8,128)(2,1)S(1)} %decode_tables.1.table_ref), custom_call_target="tpu_custom_call" | custom-call | tf_op jit(solution)/shard_map/pick_rows/pallas_call | solution.py:343
  21.2 0.0 collective-permute-done.9
  21.3 0.1 add.20
  21.3 1.3 %collective-permute-start.10 = (bf16[640,256]{1,0:T(8,128)(2,1)S(1)}, bf16[640,256]{1,0:T(8,128)(2,1)S(1)}, u32[]{:S(2)}, u32[]{:S(2)}) collective-permute-start(bf16[640,256]{1,0:T(8,128)(2,1)S(1)} %add.20), channel_id=1, source_target_pairs={{4,12},{8,0},{5,13},{9,1},{6,14},{10,2},{7,15},{11,3},{20,28},{24,... | collective-permute-start | bytes 983048 | tf_op jit(solution)/shard_map/ppermute | solution.py:353
  22.7 0.0 collective-permute-done.7.refs_1_
  22.7 2.9 %collective-permute-start.8 = (bf16[16,2304]{1,0:T(8,128)(2,1)S(1)}, bf16[16,2304]{1,0:T(8,128)(2,1)S(1)}, u32[]{:S(2)}, u32[]{:S(2)}) collective-permute-start(bf16[16,2304]{1,0:T(8,128)(2,1)S(1)} %slice.6), channel_id=1, source_target_pairs={{0,1},{4,5},{8,9},{12,13},{2,3},{6,7},{10,11},{14,15},{16,17},{20,... | collective-permute-start | bytes 221192 | tf_op jit(solution)/shard_map/ppermute | solution.py:451
  25.5 1.2 %collective-permute-done.5 = bf16[640,256]{1,0:T(8,128)(2,1)S(1)} collective-permute-done((bf16[640,256]{1,0:T(8,128)(2,1)S(1)}, bf16[640,256]{1,0:T(8,128)(2,1)S(1)}, u32[]{:S(2)}, u32[]{:S(2)}) %collective-permute-start.5) | collective-permute-done | bytes 327712 | tf_op jit(solution)/shard_map/ppermute | solution.py:340
  26.7 11.2 %collective-permute-done.6 = bf16[640,256]{1,0:T(8,128)(2,1)S(1)} collective-permute-done((bf16[640,256]{1,0:T(8,128)(2,1)S(1)}, bf16[640,256]{1,0:T(8,128)(2,1)S(1)}, u32[]{:S(2)}, u32[]{:S(2)}) %collective-permute-start.6) | collective-permute-done | bytes 327712 | tf_op jit(solution)/shard_map/ppermute | solution.py:353
  38.0 0.0 collective-permute-done.8.refs_4_
  38.0 0.0 collective-permute-done.10.refs_2_
  38.0 0.1 merge.1.body_ref
  38.2 1.6 %collective-permute-start.12 = (bf16[640,256]{1,0:T(8,128)(2,1)S(1)}, bf16[640,256]{1,0:T(8,128)(2,1)S(1)}, u32[]{:S(2)}, u32[]{:S(2)}) collective-permute-start(bf16[640,256]{1,0:T(8,128)(2,1)S(1)} %merge.1.body_ref), channel_id=1, source_target_pairs={{0,2},{2,0},{1,3},{3,1},{4,6},{6,4},{5,7},{7,5},{8,10},{10,8},{9,1... | collective-permute-start | bytes 983048 | tf_op jit(solution)/shard_map/ppermute | solution.py:462
  39.7 1.7 %collective-permute-start.13 = (bf16[640,128]{1,0:T(8,128)(2,1)S(1)}, bf16[640,128]{1,0:T(8,128)(2,1)S(1)}, u32[]{:S(2)}, u32[]{:S(2)}) collective-permute-start(bf16[640,128]{1,0:T(8,128)(2,1)S(1)} %slice.8), channel_id=1, source_target_pairs={{0,1},{2,3},{4,5},{6,7},{8,9},{10,11},{12,13},{14,15},{16,17},{18,... | collective-permute-start | bytes 491528 | tf_op jit(solution)/shard_map/ppermute | solution.py:475
  41.4 1.6 %collective-permute-start.11 = (bf16[640,128]{1,0:T(8,128)(2,1)S(1)}, bf16[640,128]{1,0:T(8,128)(2,1)S(1)}, u32[]{:S(2)}, u32[]{:S(2)}) collective-permute-start(bf16[640,128]{1,0:T(8,128)(2,1)S(1)} %slice.8), channel_id=1, source_target_pairs={{0,3},{2,1},{4,7},{6,5},{8,11},{10,9},{12,15},{14,13},{16,19},{18,... | collective-permute-start | bytes 491528 | tf_op jit(solution)/shard_map/ppermute | solution.py:475
  43.1 0.1 pad_add_fusion.where_ref
  43.2 0.0 collective-permute-done.13.rim_ref
  43.2 5.7 %project_own.1 = (f32[2,272,1152]{2,1,0:T(8,128)S(1)}, f32[2,272,1152]{2,1,0:T(8,128)S(1)}, bf16[2,2,640,1152]{3,2,1,0:T(8,128)(2,1)S(1)}, bf16[2,272,1152]{2,1,0:T(8,128)(2,1)S(1)}, f32[272,8]{1,0:T(8,128)S(1)}) custom-call(s32[2]{0:T(128)S(1)} %pad_add_fusion.where_ref, bf16[640,128]{1,0:T(8,128)(2,1)S(1)} %collective-permute-done.13.rim_ref, ...), custom_call_target="tpu_custom_call" | custom-call | tf_op jit(solution)/shard_map/project_own/pallas_call | solution.py:481
  48.8 0.0 collective-permute-done.11.refs_0_
  48.8 0.0 collective-permute-done.12.refs_1_
  48.8 0.0 copy-start.1
  48.9 3.6 %project_others.1 = (f32[2,272,1152]{2,1,0:T(8,128)}, f32[8,272]{1,0:T(8,128)S(1)}) custom-call(s32[2]{0:T(128)S(1)} %pad_add_fusion.where_ref, bf16[640,128]{1,0:T(8,128)(2,1)S(1)} %collective-permute-done.11.refs_0_, bf16[640,256]{1,0:T(8,128)(2,1)S(1)} %collective-permute-done.12.refs_1_, bf16[2,2,640,1152]{3,2,1,0:T(8,128)(2,1)S(1)} %get-tuple-element.48.refs_2_, ...), custom_call_target="tpu_custom_call" | custom-call | tf_op jit(solution)/shard_map/project_others/pallas_call | solution.py:500
  52.5 1.5 %collective-permute-start.14 = (f32[8,272]{1,0:T(8,128)S(1)}, f32[8,272]{1,0:T(8,128)S(1)}, u32[]{:S(2)}, u32[]{:S(2)}) collective-permute-start(f32[8,272]{1,0:T(8,128)S(1)} %get-tuple-element.53.refs_0_), channel_id=1, source_target_pairs={{0,2},{2,0},{1,3},{3,1},{4,6},{6,4},{5,7},{7,5},{8,10},{10,8},{9,1... | collective-permute-start | bytes 26120 | tf_op jit(solution)/shard_map/ppermute | solution.py:514
  54.0 1.9 %prepare.1 = (f32[2,256,1152]{2,1,0:T(8,128)S(1)}, f32[3,2,256,1152]{3,2,1,0:T(8,128)S(1)}) custom-call(f32[4,2304]{1,0:T(4,128)S(1)} %copy-done.1, f32[2,272,1152]{2,1,0:T(8,128)} %get-tuple-element.54.value_hbm), custom_call_target="tpu_custom_call" | custom-call | tf_op jit(solution)/shard_map/prepare/pallas_call | solution.py:522
  56.0 0.3 collective-permute-done.14.refs_1_
  56.2 2.8 %finish.1 = bf16[256,2304]{1,0:T(8,128)(2,1)} custom-call(s32[1]{0:T(128)} %bitcast.keep_ref, f32[8,272]{1,0:T(8,128)S(1)} %get-tuple-element.53.refs_0_, f32[8,272]{1,0:T(8,128)S(1)} %collective-permute-done.14.refs_1_, f32[2,256,1152]{2,1,0:T(8,128)S(1)} %get-tuple-element.55.refs_2_, f32[3,2,256,1152]{3,2,1,0:T(8,128)S(1)} %get-tuple-element.56.refs_3_, ...), custom_call_target="tpu_custom_call" | custom-call | tf_op jit(solution)/shard_map/finish/pallas_call | solution.py:537
  (5 shorter events, 0.1 us)
Async XLA Ops:
  0.0 18.8 %collective-permute-start.3 = (bf16[1280,1152]{1,0:T(8,128)(2,1)}, bf16[1280,1152]{1,0:T(8,128)(2,1)}, u32[]{:S(2)}, u32[]{:S(2)}) collective-permute-start(bf16[1280,1152]{1,0:T(8,128)(2,1)} %refs_0_.1), channel_id=1, source_target_pairs={{0,1},{1,0},{2,3},{3,2},{4,5},{5,4},{6,7},{7,6},{8,9},{9,8},{10,11... | collective-permute-start | bytes 8847368 | tf_op jit(solution)/shard_map/ppermute | solution.py:445
  0.5 18.4 %collective-permute-start.4 = (bf16[1280,1152]{1,0:T(8,128)(2,1)}, bf16[1280,1152]{1,0:T(8,128)(2,1)}, u32[]{:S(2)}, u32[]{:S(2)}) collective-permute-start(bf16[1280,1152]{1,0:T(8,128)(2,1)} %refs_1_.1), channel_id=1, source_target_pairs={{0,1},{1,0},{2,3},{3,2},{4,5},{5,4},{6,7},{7,6},{8,9},{9,8},{10,11... | collective-permute-start | bytes 8847368 | tf_op jit(solution)/shard_map/ppermute | solution.py:446
  0.5 7.6 %collective-permute-start = (s32[8,256]{1,0:T(8,128)}, s32[8,256]{1,0:T(8,128)S(1)}, u32[]{:S(2)}, u32[]{:S(2)}) collective-permute-start(s32[8,256]{1,0:T(8,128)} %bitcast.11), channel_id=1, source_target_pairs={{0,12},{4,8},{8,4},{12,0},{1,13},{5,9},{9,5},{13,1},{2,14},{6,10},... | collective-permute-start | bytes 24584 | tf_op jit(solution)/shard_map/ppermute | solution.py:337
  5.6 4.2 %collective-permute-start.1 = (s32[8,256]{1,0:T(8,128)}, s32[8,256]{1,0:T(8,128)S(1)}, u32[]{:S(2)}, u32[]{:S(2)}) collective-permute-start(s32[8,256]{1,0:T(8,128)} %bitcast.12), channel_id=1, source_target_pairs={{0,8},{1,9},{4,13},{5,12},{8,1},{9,0},{12,4},{13,5},{2,10},{3,11},... | collective-permute-start | bytes 24584 | tf_op jit(solution)/shard_map/ppermute | solution.py:340
  5.6 4.2 %collective-permute-start.2 = (s32[8,256]{1,0:T(8,128)}, s32[8,256]{1,0:T(8,128)S(1)}, u32[]{:S(2)}, u32[]{:S(2)}) collective-permute-start(s32[8,256]{1,0:T(8,128)} %bitcast.13), channel_id=1, source_target_pairs={{0,4},{4,0},{8,12},{12,8},{1,5},{5,1},{9,13},{13,9},{2,6},{6,2},{1... | collective-permute-start | bytes 24584 | tf_op jit(solution)/shard_map/ppermute | solution.py:337
  9.8 11.5 %collective-permute-start.9 = (bf16[640,256]{1,0:T(8,128)(2,1)S(1)}, bf16[640,256]{1,0:T(8,128)(2,1)S(1)}, u32[]{:S(2)}, u32[]{:S(2)}) collective-permute-start(bf16[640,256]{1,0:T(8,128)(2,1)S(1)} %pick_rows.4), channel_id=1, source_target_pairs={{0,4},{12,8},{1,5},{13,9},{2,6},{14,10},{3,7},{15,11},{16,20},{28,... | collective-permute-start | bytes 983048 | tf_op jit(solution)/shard_map/ppermute | solution.py:353
  13.4 9.3 %collective-permute-start.7 = (bf16[640,256]{1,0:T(8,128)(2,1)S(1)}, bf16[640,256]{1,0:T(8,128)(2,1)S(1)}, u32[]{:S(2)}, u32[]{:S(2)}) collective-permute-start(bf16[640,256]{1,0:T(8,128)(2,1)S(1)} %pick_rows.4), channel_id=1, source_target_pairs={{4,8},{8,4},{5,9},{9,5},{6,10},{10,6},{7,11},{11,7},{20,24},{24,20... | collective-permute-start | bytes 983048 | tf_op jit(solution)/shard_map/ppermute | solution.py:353
  15.5 7.1 %copy-start = (bf16[256,2304]{1,0:T(8,128)(2,1)S(1)}, bf16[256,2304]{1,0:T(8,128)(2,1)}, u32[]{:S(2)}) copy-start(bf16[256,2304]{1,0:T(8,128)(2,1)} %refs_4_.1) | copy-start | bytes 3538948
  15.5 11.2 %collective-permute-start.5 = (bf16[640,256]{1,0:T(8,128)(2,1)S(1)}, bf16[640,256]{1,0:T(8,128)(2,1)S(1)}, u32[]{:S(2)}, u32[]{:S(2)}) collective-permute-start(bf16[640,256]{1,0:T(8,128)(2,1)S(1)} %pick_rows.5), channel_id=1, source_target_pairs={{0,9},{1,8},{12,5},{13,4},{2,11},{3,10},{14,7},{15,6},{16,25},{17,... | collective-permute-start | bytes 983048 | tf_op jit(solution)/shard_map/ppermute | solution.py:340
  20.3 17.7 %collective-permute-start.6 = (bf16[640,256]{1,0:T(8,128)(2,1)S(1)}, bf16[640,256]{1,0:T(8,128)(2,1)S(1)}, u32[]{:S(2)}, u32[]{:S(2)}) collective-permute-start(bf16[640,256]{1,0:T(8,128)(2,1)S(1)} %pick_rows.6), channel_id=1, source_target_pairs={{0,4},{4,0},{8,12},{12,8},{1,5},{5,1},{9,13},{13,9},{2,6},{6,2},{1... | collective-permute-start | bytes 983048 | tf_op jit(solution)/shard_map/ppermute | solution.py:353
  21.3 16.7 %collective-permute-start.10 = (bf16[640,256]{1,0:T(8,128)(2,1)S(1)}, bf16[640,256]{1,0:T(8,128)(2,1)S(1)}, u32[]{:S(2)}, u32[]{:S(2)}) collective-permute-start(bf16[640,256]{1,0:T(8,128)(2,1)S(1)} %add.20), channel_id=1, source_target_pairs={{4,12},{8,0},{5,13},{9,1},{6,14},{10,2},{7,15},{11,3},{20,28},{24,... | collective-permute-start | bytes 983048 | tf_op jit(solution)/shard_map/ppermute | solution.py:353
  22.7 15.3 %collective-permute-start.8 = (bf16[16,2304]{1,0:T(8,128)(2,1)S(1)}, bf16[16,2304]{1,0:T(8,128)(2,1)S(1)}, u32[]{:S(2)}, u32[]{:S(2)}) collective-permute-start(bf16[16,2304]{1,0:T(8,128)(2,1)S(1)} %slice.6), channel_id=1, source_target_pairs={{0,1},{4,5},{8,9},{12,13},{2,3},{6,7},{10,11},{14,15},{16,17},{20,... | collective-permute-start | bytes 221192 | tf_op jit(solution)/shard_map/ppermute | solution.py:451
  38.2 10.7 %collective-permute-start.12 = (bf16[640,256]{1,0:T(8,128)(2,1)S(1)}, bf16[640,256]{1,0:T(8,128)(2,1)S(1)}, u32[]{:S(2)}, u32[]{:S(2)}) collective-permute-start(bf16[640,256]{1,0:T(8,128)(2,1)S(1)} %merge.1.body_ref), channel_id=1, source_target_pairs={{0,2},{2,0},{1,3},{3,1},{4,6},{6,4},{5,7},{7,5},{8,10},{10,8},{9,1... | collective-permute-start | bytes 983048 | tf_op jit(solution)/shard_map/ppermute | solution.py:462
  39.7 3.4 %collective-permute-start.13 = (bf16[640,128]{1,0:T(8,128)(2,1)S(1)}, bf16[640,128]{1,0:T(8,128)(2,1)S(1)}, u32[]{:S(2)}, u32[]{:S(2)}) collective-permute-start(bf16[640,128]{1,0:T(8,128)(2,1)S(1)} %slice.8), channel_id=1, source_target_pairs={{0,1},{2,3},{4,5},{6,7},{8,9},{10,11},{12,13},{14,15},{16,17},{18,... | collective-permute-start | bytes 491528 | tf_op jit(solution)/shard_map/ppermute | solution.py:475
  41.4 7.4 %collective-permute-start.11 = (bf16[640,128]{1,0:T(8,128)(2,1)S(1)}, bf16[640,128]{1,0:T(8,128)(2,1)S(1)}, u32[]{:S(2)}, u32[]{:S(2)}) collective-permute-start(bf16[640,128]{1,0:T(8,128)(2,1)S(1)} %slice.8), channel_id=1, source_target_pairs={{0,3},{2,1},{4,7},{6,5},{8,11},{10,9},{12,15},{14,13},{16,19},{18,... | collective-permute-start | bytes 491528 | tf_op jit(solution)/shard_map/ppermute | solution.py:475
  48.8 5.2 %copy-start.1 = (f32[4,2304]{1,0:T(4,128)S(1)}, f32[4,2304]{1,0:T(4,128)}, u32[]{:S(2)}) copy-start(f32[4,2304]{1,0:T(4,128)} %refs_5_.3) | copy-start | bytes 110596
  52.5 3.8 %collective-permute-start.14 = (f32[8,272]{1,0:T(8,128)S(1)}, f32[8,272]{1,0:T(8,128)S(1)}, u32[]{:S(2)}, u32[]{:S(2)}) collective-permute-start(f32[8,272]{1,0:T(8,128)S(1)} %get-tuple-element.53.refs_0_), channel_id=1, source_target_pairs={{0,2},{2,0},{1,3},{3,1},{4,6},{6,4},{5,7},{7,5},{8,10},{10,8},{9,1... | collective-permute-start | bytes 26120 | tf_op jit(solution)/shard_map/ppermute | solution.py:514

commit v26 on v25

--- a/solution.py
+++ b/solution.py
@@ -362,12 +362,12 @@
     rows_3, second, third = lax.optimization_barrier((rows_3, second, third))
     inward = send(rows_3, (0, 1), (3, 2))
     across = send(rows_3, (1, 2), (2, 1))
-    rows_2 = pick(place(after(second, rows_3)))
-    third, settled = lax.optimization_barrier((after(third, rows_2), settled))
+    rows_1 = pick(place(after(third, rows_3)))
+    beside = send(rows_1, (0, 1), (1, 0), (2, 3), (3, 2))
+    second, settled = lax.optimization_barrier((after(second, rows_1), settled))
+    rows_2 = pick(place(second))
     past = crossing(rows_2, [(m, r, m ^ 2, r ^ 1) for m in (0, 3) for r in range(2)])
-    rows_1 = pick(place(third))
-    own = pick(after(stored, rows_1))
-    beside = send(rows_1, (0, 1), (1, 0), (2, 3), (3, 2))
+    own = pick(after(stored, rows_2))
     onward = after(rows_2, rows_1, own) + inward
     onward = send(onward, (1, 3), (2, 0))
     other = meanwhile(across)

time: 59.6 us -> 63.1 us (1.059)
  waiting for transfers between devices: 12.9 us -> 16.6 us
    ppermute x2, waiting for transfers between devices: 1.34 us -> 5.63 us  [crossing(): lax.ppermute(x, ('mem', 'rep'), [(2 * a + b, 2 * c + d) for a, b, c, d in...]
    ppermute x4, starting transfers between devices: 5.68 us -> 7.28 us  [send(): return lax.ppermute(x, 'mem', pairs)]
    ppermute x2, starting transfers between devices: 3.28 us -> 2.41 us  [crossing(): lax.ppermute(x, ('mem', 'rep'), [(2 * a + b, 2 * c + d) for a, b, c, d in...]
  transfers between devices with their start and end apart: 15 -> 15, of which waited for: 4 -> 5; matrix products, arithmetic and copies ran while one was open for 0% -> 0% of each run, Pallas kernels for 26% -> 24%
where the time goes in v26:
time: 63.1 us; the launch traced here: 62.8 us
  starting transfers between devices  23.9 us (38%)
  Pallas kernels  21.7 us (34%)
  waiting for transfers between devices  16.6 us (26%)
    ppermute x4, waiting for transfers between devices, send(): return lax.ppermute(x, 'mem', pairs)  10.6 us
    ppermute x4, starting transfers between devices, send(): return lax.ppermute(x, 'mem', pairs)  7.28 us
    pallas_call x1, Pallas kernels, shards(): pl.pallas_call(functools.partial(project_own_kernel, tps), in_specs=[smem...  5.66 us
    ppermute x2, waiting for transfers between devices, crossing(): lax.ppermute(x, ('mem', 'rep'), [(2 * a + b, 2 * c + d) for a, b, c, d in...  5.63 us
    ppermute x2, starting transfers between devices, ask(): return lax.ppermute(ids, 'mem', [(i, i ^ x) for i in range(4)])  5.22 us
    pallas_call x1, Pallas kernels, shards(): pl.pallas_call(functools.partial(project_others_kernel, tps), in_specs=[s...  3.6 us
    pallas_call x4, Pallas kernels, pick(): pl.pallas_call(pick_kernel, in_specs=[pl.BlockSpec(memory_space=pltpu.SME...  3.46 us
    ppermute x2, starting transfers between devices, next_rim(): return lax.ppermute(rim, ('mem', 'tp', 'rep'), pairs)  2.97 us
  transfers between devices with their start and end apart: 15, of which 5 were waited for; matrix products, arithmetic and copies ran while one was open for 0% of the time, Pallas kernels for 24%

profile of v26, /device:TPU:0, one launch (start us, length us, event | category | flops | bytes accessed | tf_op | source)
XLA Modules:
  0.0 62.8 jit_solution(7600987776365464962)
XLA Ops:
  0.0 0.5 collective-permute-start.3
  0.5 0.1 collective-permute-start.4
  0.5 5.0 %collective-permute-start = (s32[8,256]{1,0:T(8,128)}, s32[8,256]{1,0:T(8,128)S(1)}, u32[]{:S(2)}, u32[]{:S(2)}) collective-permute-start(s32[8,256]{1,0:T(8,128)} %bitcast.11), channel_id=1, source_target_pairs={{0,12},{4,8},{8,4},{12,0},{1,13},{5,9},{9,5},{13,1},{2,14},{6,10},... | collective-permute-start | bytes 24584 | tf_op jit(solution)/shard_map/ppermute | solution.py:337
  5.6 0.0 collective-permute-start.1
  5.6 0.2 collective-permute-start.2
  5.7 1.5 %fetch_tables.1 = (s32[32,128]{1,0:T(8,128)S(1)}, bf16[8,80,1024]{2,1,0:T(8,128)(2,1)S(1)}, bf16[5,8,1024]{2,1,0:T(8,128)(2,1)S(1)}, s32[8,256]{1,0:T(8,128)S(1)}) custom-call(s32[32,128]{1,0:T(8,128)} %bitcast.10, s32[8,256]{1,0:T(8,128)} %bitcast.14, bf16[8,80,1024]{2,1,0:T(8,128)(2,1)} %bitcast.8, bf16[5,8,1024]{2,1,0:T(8,128)(2,1)} %bitcast.9), custom_call_target="tpu_custom_call" | custom-call | tf_op jit(solution)/shard_map/fetch_tables/pallas_call | solution.py:408
  7.3 0.9 %decode_tables.1.table_ref = bf16[8,80,1024]{2,1,0:T(8,128)(2,1)S(1)} custom-call(bf16[8,80,1024]{2,1,0:T(8,128)(2,1)S(1)} %get-tuple-element.33.codes_ref, bf16[5,8,1024]{2,1,0:T(8,128)(2,1)S(1)} %get-tuple-element.34.scales_ref), custom_call_target="tpu_custom_call" | custom-call | tf_op jit(solution)/shard_map/decode_tables/pallas_call | solution.py:436
  8.1 0.0 collective-permute-done.ids_ref
  8.1 0.6 place_rows.3.ids_ref
  8.7 0.9 %pick_rows.4 = bf16[640,256]{1,0:T(8,128)(2,1)S(1)} custom-call(s32[1]{0:T(128)} %bitcast.3.base_ref, s32[8,256]{1,0:T(8,128)S(1)} %place_rows.3.ids_ref, bf16[8,80,1024]{2,1,0:T(8,128)(2,1)S(1)} %decode_tables.1.table_ref), custom_call_target="tpu_custom_call" | custom-call | tf_op jit(solution)/shard_map/pick_rows/pallas_call | solution.py:343
  9.6 0.2 collective-permute-done.1.ids_ref
  9.7 0.0 collective-permute-done.2.ids_ref
  9.8 3.6 %collective-permute-start.9 = (bf16[640,256]{1,0:T(8,128)(2,1)S(1)}, bf16[640,256]{1,0:T(8,128)(2,1)S(1)}, u32[]{:S(2)}, u32[]{:S(2)}) collective-permute-start(bf16[640,256]{1,0:T(8,128)(2,1)S(1)} %pick_rows.4), channel_id=1, source_target_pairs={{0,4},{12,8},{1,5},{13,9},{2,6},{14,10},{3,7},{15,11},{16,20},{28,... | collective-permute-start | bytes 983048 | tf_op jit(solution)/shard_map/ppermute | solution.py:353
  13.4 0.7 %collective-permute-start.7 = (bf16[640,256]{1,0:T(8,128)(2,1)S(1)}, bf16[640,256]{1,0:T(8,128)(2,1)S(1)}, u32[]{:S(2)}, u32[]{:S(2)}) collective-permute-start(bf16[640,256]{1,0:T(8,128)(2,1)S(1)} %pick_rows.4), channel_id=1, source_target_pairs={{4,8},{8,4},{5,9},{9,5},{6,10},{10,6},{7,11},{11,7},{20,24},{24,20... | collective-permute-start | bytes 983048 | tf_op jit(solution)/shard_map/ppermute | solution.py:353
  14.1 0.6 place_rows.4.ids_ref
  14.7 0.9 %pick_rows.5 = bf16[640,256]{1,0:T(8,128)(2,1)S(1)} custom-call(s32[1]{0:T(128)} %bitcast.3.base_ref, s32[8,256]{1,0:T(8,128)S(1)} %place_rows.4.ids_ref, bf16[8,80,1024]{2,1,0:T(8,128)(2,1)S(1)} %decode_tables.1.table_ref), custom_call_target="tpu_custom_call" | custom-call | tf_op jit(solution)/shard_map/pick_rows/pallas_call | solution.py:343
  15.5 0.0 copy-start
  15.5 1.7 %collective-permute-start.6 = (bf16[640,256]{1,0:T(8,128)(2,1)S(1)}, bf16[640,256]{1,0:T(8,128)(2,1)S(1)}, u32[]{:S(2)}, u32[]{:S(2)}) collective-permute-start(bf16[640,256]{1,0:T(8,128)(2,1)S(1)} %pick_rows.5), channel_id=1, source_target_pairs={{0,4},{4,0},{8,12},{12,8},{1,5},{5,1},{9,13},{13,9},{2,6},{6,2},{1... | collective-permute-start | bytes 983048 | tf_op jit(solution)/shard_map/ppermute | solution.py:353
  17.2 0.0 collective-permute-done.3.refs_2_
  17.2 0.0 collective-permute-done.4.refs_3_
  17.2 0.6 place_rows.5.ids_ref
  17.8 0.9 %pick_rows.6 = bf16[640,256]{1,0:T(8,128)(2,1)S(1)} custom-call(s32[1]{0:T(128)} %bitcast.3.base_ref, s32[8,256]{1,0:T(8,128)S(1)} %place_rows.5.ids_ref, bf16[8,80,1024]{2,1,0:T(8,128)(2,1)S(1)} %decode_tables.1.table_ref), custom_call_target="tpu_custom_call" | custom-call | tf_op jit(solution)/shard_map/pick_rows/pallas_call | solution.py:343
  18.7 2.4 %collective-permute-start.5 = (bf16[640,256]{1,0:T(8,128)(2,1)S(1)}, bf16[640,256]{1,0:T(8,128)(2,1)S(1)}, u32[]{:S(2)}, u32[]{:S(2)}) collective-permute-start(bf16[640,256]{1,0:T(8,128)(2,1)S(1)} %pick_rows.6), channel_id=1, source_target_pairs={{0,9},{1,8},{12,5},{13,4},{2,11},{3,10},{14,7},{15,6},{16,25},{17,... | collective-permute-start | bytes 983048 | tf_op jit(solution)/shard_map/ppermute | solution.py:340
  21.1 0.9 %pick_rows.7 = bf16[640,256]{1,0:T(8,128)(2,1)S(1)} custom-call(s32[1]{0:T(128)} %bitcast.3.base_ref, s32[8,256]{1,0:T(8,128)S(1)} %get-tuple-element.41.ids_ref, bf16[8,80,1024]{2,1,0:T(8,128)(2,1)S(1)} %decode_tables.1.table_ref), custom_call_target="tpu_custom_call" | custom-call | tf_op jit(solution)/shard_map/pick_rows/pallas_call | solution.py:343
  21.9 0.0 collective-permute-done.9
  22.0 0.1 add.20
  22.0 1.3 %collective-permute-start.10 = (bf16[640,256]{1,0:T(8,128)(2,1)S(1)}, bf16[640,256]{1,0:T(8,128)(2,1)S(1)}, u32[]{:S(2)}, u32[]{:S(2)}) collective-permute-start(bf16[640,256]{1,0:T(8,128)(2,1)S(1)} %add.20), channel_id=1, source_target_pairs={{4,12},{8,0},{5,13},{9,1},{6,14},{10,2},{7,15},{11,3},{20,28},{24,... | collective-permute-start | bytes 983048 | tf_op jit(solution)/shard_map/ppermute | solution.py:353
  23.4 0.0 collective-permute-done.7.refs_1_
  23.4 2.4 %collective-permute-start.8 = (bf16[16,2304]{1,0:T(8,128)(2,1)S(1)}, bf16[16,2304]{1,0:T(8,128)(2,1)S(1)}, u32[]{:S(2)}, u32[]{:S(2)}) collective-permute-start(bf16[16,2304]{1,0:T(8,128)(2,1)S(1)} %slice.6), channel_id=1, source_target_pairs={{0,1},{4,5},{8,9},{12,13},{2,3},{6,7},{10,11},{14,15},{16,17},{20,... | collective-permute-start | bytes 221192 | tf_op jit(solution)/shard_map/ppermute | solution.py:451
  25.8 2.7 %collective-permute-done.6 = bf16[640,256]{1,0:T(8,128)(2,1)S(1)} collective-permute-done((bf16[640,256]{1,0:T(8,128)(2,1)S(1)}, bf16[640,256]{1,0:T(8,128)(2,1)S(1)}, u32[]{:S(2)}, u32[]{:S(2)}) %collective-permute-start.6) | collective-permute-done | bytes 327712 | tf_op jit(solution)/shard_map/ppermute | solution.py:353
  28.5 5.5 %collective-permute-done.5 = bf16[640,256]{1,0:T(8,128)(2,1)S(1)} collective-permute-done((bf16[640,256]{1,0:T(8,128)(2,1)S(1)}, bf16[640,256]{1,0:T(8,128)(2,1)S(1)}, u32[]{:S(2)}, u32[]{:S(2)}) %collective-permute-start.5) | collective-permute-done | bytes 327712 | tf_op jit(solution)/shard_map/ppermute | solution.py:340
  34.1 0.0 collective-permute-done.8.refs_4_
  34.1 7.9 %collective-permute-done.10.refs_2_ = bf16[640,256]{1,0:T(8,128)(2,1)S(1)} collective-permute-done((bf16[640,256]{1,0:T(8,128)(2,1)S(1)}, bf16[640,256]{1,0:T(8,128)(2,1)S(1)}, u32[]{:S(2)}, u32[]{:S(2)}) %collective-permute-start.10) | collective-permute-done | bytes 327712 | tf_op jit(solution)/shard_map/ppermute | solution.py:353
  42.0 0.1 merge.1.body_ref
  42.1 1.6 %collective-permute-start.12 = (bf16[640,256]{1,0:T(8,128)(2,1)S(1)}, bf16[640,256]{1,0:T(8,128)(2,1)S(1)}, u32[]{:S(2)}, u32[]{:S(2)}) collective-permute-start(bf16[640,256]{1,0:T(8,128)(2,1)S(1)} %merge.1.body_ref), channel_id=1, source_target_pairs={{0,2},{2,0},{1,3},{3,1},{4,6},{6,4},{5,7},{7,5},{8,10},{10,8},{9,1... | collective-permute-start | bytes 983048 | tf_op jit(solution)/shard_map/ppermute | solution.py:462
  43.7 1.3 %collective-permute-start.13 = (bf16[640,128]{1,0:T(8,128)(2,1)S(1)}, bf16[640,128]{1,0:T(8,128)(2,1)S(1)}, u32[]{:S(2)}, u32[]{:S(2)}) collective-permute-start(bf16[640,128]{1,0:T(8,128)(2,1)S(1)} %slice.8), channel_id=1, source_target_pairs={{0,1},{2,3},{4,5},{6,7},{8,9},{10,11},{12,13},{14,15},{16,17},{18,... | collective-permute-start | bytes 491528 | tf_op jit(solution)/shard_map/ppermute | solution.py:475
  45.0 1.6 %collective-permute-start.11 = (bf16[640,128]{1,0:T(8,128)(2,1)S(1)}, bf16[640,128]{1,0:T(8,128)(2,1)S(1)}, u32[]{:S(2)}, u32[]{:S(2)}) collective-permute-start(bf16[640,128]{1,0:T(8,128)(2,1)S(1)} %slice.8), channel_id=1, source_target_pairs={{0,3},{2,1},{4,7},{6,5},{8,11},{10,9},{12,15},{14,13},{16,19},{18,... | collective-permute-start | bytes 491528 | tf_op jit(solution)/shard_map/ppermute | solution.py:475
  46.7 0.1 pad_add_fusion.where_ref
  46.7 0.0 collective-permute-done.13.rim_ref
  46.8 5.7 %project_own.1 = (f32[2,272,1152]{2,1,0:T(8,128)S(1)}, f32[2,272,1152]{2,1,0:T(8,128)S(1)}, bf16[2,2,640,1152]{3,2,1,0:T(8,128)(2,1)S(1)}, bf16[2,272,1152]{2,1,0:T(8,128)(2,1)S(1)}, f32[272,8]{1,0:T(8,128)S(1)}) custom-call(s32[2]{0:T(128)S(1)} %pad_add_fusion.where_ref, bf16[640,128]{1,0:T(8,128)(2,1)S(1)} %collective-permute-done.13.rim_ref, ...), custom_call_target="tpu_custom_call" | custom-call | tf_op jit(solution)/shard_map/project_own/pallas_call | solution.py:481
  52.4 0.0 collective-permute-done.11.refs_0_
  52.4 0.0 collective-permute-done.12.refs_1_
  52.4 0.0 copy-start.1
  52.5 3.6 %project_others.1 = (f32[2,272,1152]{2,1,0:T(8,128)}, f32[8,272]{1,0:T(8,128)S(1)}) custom-call(s32[2]{0:T(128)S(1)} %pad_add_fusion.where_ref, bf16[640,128]{1,0:T(8,128)(2,1)S(1)} %collective-permute-done.11.refs_0_, bf16[640,256]{1,0:T(8,128)(2,1)S(1)} %collective-permute-done.12.refs_1_, bf16[2,2,640,1152]{3,2,1,0:T(8,128)(2,1)S(1)} %get-tuple-element.48.refs_2_, ...), custom_call_target="tpu_custom_call" | custom-call | tf_op jit(solution)/shard_map/project_others/pallas_call | solution.py:500
  56.1 1.5 %collective-permute-start.14 = (f32[8,272]{1,0:T(8,128)S(1)}, f32[8,272]{1,0:T(8,128)S(1)}, u32[]{:S(2)}, u32[]{:S(2)}) collective-permute-start(f32[8,272]{1,0:T(8,128)S(1)} %get-tuple-element.53.refs_0_), channel_id=1, source_target_pairs={{0,2},{2,0},{1,3},{3,1},{4,6},{6,4},{5,7},{7,5},{8,10},{10,8},{9,1... | collective-permute-start | bytes 26120 | tf_op jit(solution)/shard_map/ppermute | solution.py:514
  57.6 1.9 %prepare.1 = (f32[2,256,1152]{2,1,0:T(8,128)S(1)}, f32[3,2,256,1152]{3,2,1,0:T(8,128)S(1)}) custom-call(f32[4,2304]{1,0:T(4,128)S(1)} %copy-done.1, f32[2,272,1152]{2,1,0:T(8,128)} %get-tuple-element.54.value_hbm), custom_call_target="tpu_custom_call" | custom-call | tf_op jit(solution)/shard_map/prepare/pallas_call | solution.py:522
  59.5 0.3 collective-permute-done.14.refs_1_
  59.8 2.8 %finish.1 = bf16[256,2304]{1,0:T(8,128)(2,1)} custom-call(s32[1]{0:T(128)} %bitcast.keep_ref, f32[8,272]{1,0:T(8,128)S(1)} %get-tuple-element.53.refs_0_, f32[8,272]{1,0:T(8,128)S(1)} %collective-permute-done.14.refs_1_, f32[2,256,1152]{2,1,0:T(8,128)S(1)} %get-tuple-element.55.refs_2_, f32[3,2,256,1152]{3,2,1,0:T(8,128)S(1)} %get-tuple-element.56.refs_3_, ...), custom_call_target="tpu_custom_call" | custom-call | tf_op jit(solution)/shard_map/finish/pallas_call | solution.py:537
  (5 shorter events, 0.1 us)
Async XLA Ops:
  0.0 17.2 %collective-permute-start.3 = (bf16[1280,1152]{1,0:T(8,128)(2,1)}, bf16[1280,1152]{1,0:T(8,128)(2,1)}, u32[]{:S(2)}, u32[]{:S(2)}) collective-permute-start(bf16[1280,1152]{1,0:T(8,128)(2,1)} %refs_0_.1), channel_id=1, source_target_pairs={{0,1},{1,0},{2,3},{3,2},{4,5},{5,4},{6,7},{7,6},{8,9},{9,8},{10,11... | collective-permute-start | bytes 8847368 | tf_op jit(solution)/shard_map/ppermute | solution.py:445
  0.5 16.8 %collective-permute-start.4 = (bf16[1280,1152]{1,0:T(8,128)(2,1)}, bf16[1280,1152]{1,0:T(8,128)(2,1)}, u32[]{:S(2)}, u32[]{:S(2)}) collective-permute-start(bf16[1280,1152]{1,0:T(8,128)(2,1)} %refs_1_.1), channel_id=1, source_target_pairs={{0,1},{1,0},{2,3},{3,2},{4,5},{5,4},{6,7},{7,6},{8,9},{9,8},{10,11... | collective-permute-start | bytes 8847368 | tf_op jit(solution)/shard_map/ppermute | solution.py:446
  0.5 7.6 %collective-permute-start = (s32[8,256]{1,0:T(8,128)}, s32[8,256]{1,0:T(8,128)S(1)}, u32[]{:S(2)}, u32[]{:S(2)}) collective-permute-start(s32[8,256]{1,0:T(8,128)} %bitcast.11), channel_id=1, source_target_pairs={{0,12},{4,8},{8,4},{12,0},{1,13},{5,9},{9,5},{13,1},{2,14},{6,10},... | collective-permute-start | bytes 24584 | tf_op jit(solution)/shard_map/ppermute | solution.py:337
  5.6 4.2 %collective-permute-start.1 = (s32[8,256]{1,0:T(8,128)}, s32[8,256]{1,0:T(8,128)S(1)}, u32[]{:S(2)}, u32[]{:S(2)}) collective-permute-start(s32[8,256]{1,0:T(8,128)} %bitcast.12), channel_id=1, source_target_pairs={{0,8},{1,9},{4,13},{5,12},{8,1},{9,0},{12,4},{13,5},{2,10},{3,11},... | collective-permute-start | bytes 24584 | tf_op jit(solution)/shard_map/ppermute | solution.py:340
  5.6 4.2 %collective-permute-start.2 = (s32[8,256]{1,0:T(8,128)}, s32[8,256]{1,0:T(8,128)S(1)}, u32[]{:S(2)}, u32[]{:S(2)}) collective-permute-start(s32[8,256]{1,0:T(8,128)} %bitcast.13), channel_id=1, source_target_pairs={{0,4},{4,0},{8,12},{12,8},{1,5},{5,1},{9,13},{13,9},{2,6},{6,2},{1... | collective-permute-start | bytes 24584 | tf_op jit(solution)/shard_map/ppermute | solution.py:337
  9.8 12.2 %collective-permute-start.9 = (bf16[640,256]{1,0:T(8,128)(2,1)S(1)}, bf16[640,256]{1,0:T(8,128)(2,1)S(1)}, u32[]{:S(2)}, u32[]{:S(2)}) collective-permute-start(bf16[640,256]{1,0:T(8,128)(2,1)S(1)} %pick_rows.4), channel_id=1, source_target_pairs={{0,4},{12,8},{1,5},{13,9},{2,6},{14,10},{3,7},{15,11},{16,20},{28,... | collective-permute-start | bytes 983048 | tf_op jit(solution)/shard_map/ppermute | solution.py:353
  13.4 10.0 %collective-permute-start.7 = (bf16[640,256]{1,0:T(8,128)(2,1)S(1)}, bf16[640,256]{1,0:T(8,128)(2,1)S(1)}, u32[]{:S(2)}, u32[]{:S(2)}) collective-permute-start(bf16[640,256]{1,0:T(8,128)(2,1)S(1)} %pick_rows.4), channel_id=1, source_target_pairs={{4,8},{8,4},{5,9},{9,5},{6,10},{10,6},{7,11},{11,7},{20,24},{24,20... | collective-permute-start | bytes 983048 | tf_op jit(solution)/shard_map/ppermute | solution.py:353
  15.5 7.8 %copy-start = (bf16[256,2304]{1,0:T(8,128)(2,1)S(1)}, bf16[256,2304]{1,0:T(8,128)(2,1)}, u32[]{:S(2)}) copy-start(bf16[256,2304]{1,0:T(8,128)(2,1)} %refs_4_.1) | copy-start | bytes 3538948
  15.5 13.0 %collective-permute-start.6 = (bf16[640,256]{1,0:T(8,128)(2,1)S(1)}, bf16[640,256]{1,0:T(8,128)(2,1)S(1)}, u32[]{:S(2)}, u32[]{:S(2)}) collective-permute-start(bf16[640,256]{1,0:T(8,128)(2,1)S(1)} %pick_rows.5), channel_id=1, source_target_pairs={{0,4},{4,0},{8,12},{12,8},{1,5},{5,1},{9,13},{13,9},{2,6},{6,2},{1... | collective-permute-start | bytes 983048 | tf_op jit(solution)/shard_map/ppermute | solution.py:353
  18.7 15.4 %collective-permute-start.5 = (bf16[640,256]{1,0:T(8,128)(2,1)S(1)}, bf16[640,256]{1,0:T(8,128)(2,1)S(1)}, u32[]{:S(2)}, u32[]{:S(2)}) collective-permute-start(bf16[640,256]{1,0:T(8,128)(2,1)S(1)} %pick_rows.6), channel_id=1, source_target_pairs={{0,9},{1,8},{12,5},{13,4},{2,11},{3,10},{14,7},{15,6},{16,25},{17,... | collective-permute-start | bytes 983048 | tf_op jit(solution)/shard_map/ppermute | solution.py:340
  22.0 19.9 %collective-permute-start.10 = (bf16[640,256]{1,0:T(8,128)(2,1)S(1)}, bf16[640,256]{1,0:T(8,128)(2,1)S(1)}, u32[]{:S(2)}, u32[]{:S(2)}) collective-permute-start(bf16[640,256]{1,0:T(8,128)(2,1)S(1)} %add.20), channel_id=1, source_target_pairs={{4,12},{8,0},{5,13},{9,1},{6,14},{10,2},{7,15},{11,3},{20,28},{24,... | collective-permute-start | bytes 983048 | tf_op jit(solution)/shard_map/ppermute | solution.py:353
  23.4 10.7 %collective-permute-start.8 = (bf16[16,2304]{1,0:T(8,128)(2,1)S(1)}, bf16[16,2304]{1,0:T(8,128)(2,1)S(1)}, u32[]{:S(2)}, u32[]{:S(2)}) collective-permute-start(bf16[16,2304]{1,0:T(8,128)(2,1)S(1)} %slice.6), channel_id=1, source_target_pairs={{0,1},{4,5},{8,9},{12,13},{2,3},{6,7},{10,11},{14,15},{16,17},{20,... | collective-permute-start | bytes 221192 | tf_op jit(solution)/shard_map/ppermute | solution.py:451
  42.1 10.3 %collective-permute-start.12 = (bf16[640,256]{1,0:T(8,128)(2,1)S(1)}, bf16[640,256]{1,0:T(8,128)(2,1)S(1)}, u32[]{:S(2)}, u32[]{:S(2)}) collective-permute-start(bf16[640,256]{1,0:T(8,128)(2,1)S(1)} %merge.1.body_ref), channel_id=1, source_target_pairs={{0,2},{2,0},{1,3},{3,1},{4,6},{6,4},{5,7},{7,5},{8,10},{10,8},{9,1... | collective-permute-start | bytes 983048 | tf_op jit(solution)/shard_map/ppermute | solution.py:462
  43.7 3.1 %collective-permute-start.13 = (bf16[640,128]{1,0:T(8,128)(2,1)S(1)}, bf16[640,128]{1,0:T(8,128)(2,1)S(1)}, u32[]{:S(2)}, u32[]{:S(2)}) collective-permute-start(bf16[640,128]{1,0:T(8,128)(2,1)S(1)} %slice.8), channel_id=1, source_target_pairs={{0,1},{2,3},{4,5},{6,7},{8,9},{10,11},{12,13},{14,15},{16,17},{18,... | collective-permute-start | bytes 491528 | tf_op jit(solution)/shard_map/ppermute | solution.py:475
  45.0 7.4 %collective-permute-start.11 = (bf16[640,128]{1,0:T(8,128)(2,1)S(1)}, bf16[640,128]{1,0:T(8,128)(2,1)S(1)}, u32[]{:S(2)}, u32[]{:S(2)}) collective-permute-start(bf16[640,128]{1,0:T(8,128)(2,1)S(1)} %slice.8), channel_id=1, source_target_pairs={{0,3},{2,1},{4,7},{6,5},{8,11},{10,9},{12,15},{14,13},{16,19},{18,... | collective-permute-start | bytes 491528 | tf_op jit(solution)/shard_map/ppermute | solution.py:475
  52.4 5.2 %copy-start.1 = (f32[4,2304]{1,0:T(4,128)S(1)}, f32[4,2304]{1,0:T(4,128)}, u32[]{:S(2)}) copy-start(f32[4,2304]{1,0:T(4,128)} %refs_5_.3) | copy-start | bytes 110596
  56.1 3.8 %collective-permute-start.14 = (f32[8,272]{1,0:T(8,128)S(1)}, f32[8,272]{1,0:T(8,128)S(1)}, u32[]{:S(2)}, u32[]{:S(2)}) collective-permute-start(f32[8,272]{1,0:T(8,128)S(1)} %get-tuple-element.53.refs_0_), channel_id=1, source_target_pairs={{0,2},{2,0},{1,3},{3,1},{4,6},{6,4},{5,7},{7,5},{8,10},{10,8},{9,1... | collective-permute-start | bytes 26120 | tf_op jit(solution)/shard_map/ppermute | solution.py:514

commit v27 on v21

--- a/solution.py
+++ b/solution.py
@@ -160,14 +160,6 @@
         )
         for far, which in order
     }
-    power = 0.0
-    for slot in range(2):
-        span = slice(slot * half, (slot + 1) * half)
-        states_ref[slot, :RIM] = hidden_halo[:, span]
-        states_ref[slot, RIM:] = hidden[:, span]
-        here = states_ref[slot].astype(F32)
-        power = power + jnp.sum(here * here, axis=1, keepdims=True)
-    power_ref[...] = jnp.broadcast_to(power, power_ref.shape)
     memory = with_rim([rim_ref], [body_ref])
     later = []
     for far, which in order:
@@ -181,6 +173,15 @@
                 )
         target = value_ref if which == 1 else key_ref
         target[slot] = dot(memory, held[far, which])
+        if (far, which) == (0, 1):
+            power = 0.0
+            for side in range(2):
+                span = slice(side * half, (side + 1) * half)
+                states_ref[side, :RIM] = hidden_halo[:, span]
+                states_ref[side, RIM:] = hidden[:, span]
+                here = states_ref[side].astype(F32)
+                power = power + jnp.sum(here * here, axis=1, keepdims=True)
+            power_ref[...] = jnp.broadcast_to(power, power_ref.shape)
     await_all(later)
 
 

time: 59.3 us -> 59.2 us (level)
  no operation moved by 1% of the time
where the time goes in v27:
time: 59.2 us; the launch traced here: 58.9 us
  starting transfers between devices  22.9 us (39%)
  Pallas kernels  19.9 us (34%)
  waiting for transfers between devices  15.5 us (26%)
    ppermute x4, waiting for transfers between devices, send(): return lax.ppermute(x, 'mem', pairs)  11.3 us
    pallas_call x1, Pallas kernels, shards(): pl.pallas_call(functools.partial(project_own_kernel, tps), in_specs=[smem...  5.55 us
    ppermute x2, starting transfers between devices, ask(): return lax.ppermute(ids, 'mem', [(i, i ^ x) for i in range(4)])  5.35 us
    ppermute x4, starting transfers between devices, send(): return lax.ppermute(x, 'mem', pairs)  4.76 us
    ppermute x2, starting transfers between devices, crossing(): lax.ppermute(x, ('mem', 'rep'), [(2 * a + b, 2 * c + d) for a, b, c, d in...  3.71 us
    pallas_call x1, Pallas kernels, shards(): pl.pallas_call(functools.partial(project_others_kernel, tps), in_specs=[s...  3.6 us
    pallas_call x4, Pallas kernels, pick(): pl.pallas_call(pick_kernel, in_specs=[pl.BlockSpec(memory_space=pltpu.SME...  3.46 us
    ppermute x2, waiting for transfers between devices, crossing(): lax.ppermute(x, ('mem', 'rep'), [(2 * a + b, 2 * c + d) for a, b, c, d in...  3.36 us
  transfers between devices with their start and end apart: 15, of which 6 were waited for; matrix products, arithmetic and copies ran while one was open for 0% of the time, Pallas kernels for 23%

profile of v27, /device:TPU:0, one launch (start us, length us, event | category | flops | bytes accessed | tf_op | source)
XLA Modules:
  0.0 58.9 jit_solution(11740403484296480460)
XLA Ops:
  0.0 0.5 collective-permute-start.3
  0.5 0.1 collective-permute-start.4
  0.5 1.5 %place_rows.1 = (s32[8,256]{1,0:T(8,128)S(1)}, bf16[8,80,1024]{2,1,0:T(8,128)(2,1)S(1)}, bf16[5,8,1024]{2,1,0:T(8,128)(2,1)S(1)}) custom-call(s32[8,256]{1,0:T(8,128)} %bitcast.11, s32[32,128]{1,0:T(8,128)} %bitcast.10, bf16[8,80,1024]{2,1,0:T(8,128)(2,1)} %bitcast.8, bf16[5,8,1024]{2,1,0:T(8,128)(2,1)} %bitcast.9), custom_call_target="tpu_custom_call" | custom-call | tf_op jit(solution)/shard_map/place_rows/pallas_call | solution.py:407
  2.0 5.1 %collective-permute-start = (s32[8,256]{1,0:T(8,128)S(1)}, s32[8,256]{1,0:T(8,128)S(1)}, u32[]{:S(2)}, u32[]{:S(2)}) collective-permute-start(s32[8,256]{1,0:T(8,128)S(1)} %get-tuple-element.39.ids_ref), channel_id=1, source_target_pairs={{0,12},{4,8},{8,4},{12,0},{1,13},{5,9},{9,5},{13,1},{2,14},{6,10},... | collective-permute-start | bytes 24584 | tf_op jit(solution)/shard_map/ppermute | solution.py:338
  7.1 0.0 collective-permute-start.1
  7.2 0.2 collective-permute-start.2
  7.4 0.9 %decode_tables.1.table_ref = bf16[8,80,1024]{2,1,0:T(8,128)(2,1)S(1)} custom-call(bf16[8,80,1024]{2,1,0:T(8,128)(2,1)S(1)} %get-tuple-element.31.codes_ref, bf16[5,8,1024]{2,1,0:T(8,128)(2,1)S(1)} %get-tuple-element.32.scales_ref), custom_call_target="tpu_custom_call" | custom-call | tf_op jit(solution)/shard_map/decode_tables/pallas_call | solution.py:424
  8.3 0.5 collective-permute-done.ids_ref
  8.8 0.9 %pick_rows.4 = bf16[640,256]{1,0:T(8,128)(2,1)S(1)} custom-call(s32[1]{0:T(128)} %bitcast.3.base_ref, s32[8,256]{1,0:T(8,128)S(1)} %collective-permute-done.ids_ref, bf16[8,80,1024]{2,1,0:T(8,128)(2,1)S(1)} %decode_tables.1.table_ref), custom_call_target="tpu_custom_call" | custom-call | tf_op jit(solution)/shard_map/pick_rows/pallas_call | solution.py:344
  9.6 1.5 %collective-permute-done.1.ids_ref = s32[8,256]{1,0:T(8,128)S(1)} collective-permute-done((s32[8,256]{1,0:T(8,128)S(1)}, s32[8,256]{1,0:T(8,128)S(1)}, u32[]{:S(2)}, u32[]{:S(2)}) %collective-permute-start.1) | collective-permute-done | bytes 8224 | tf_op jit(solution)/shard_map/ppermute | solution.py:341
  11.1 0.0 collective-permute-done.2.ids_ref
  11.1 2.0 %collective-permute-start.9 = (bf16[640,256]{1,0:T(8,128)(2,1)S(1)}, bf16[640,256]{1,0:T(8,128)(2,1)S(1)}, u32[]{:S(2)}, u32[]{:S(2)}) collective-permute-start(bf16[640,256]{1,0:T(8,128)(2,1)S(1)} %pick_rows.4), channel_id=1, source_target_pairs={{0,4},{12,8},{1,5},{13,9},{2,6},{14,10},{3,7},{15,11},{16,20},{28,... | collective-permute-start | bytes 983048 | tf_op jit(solution)/shard_map/ppermute | solution.py:354
  13.2 0.7 %collective-permute-start.7 = (bf16[640,256]{1,0:T(8,128)(2,1)S(1)}, bf16[640,256]{1,0:T(8,128)(2,1)S(1)}, u32[]{:S(2)}, u32[]{:S(2)}) collective-permute-start(bf16[640,256]{1,0:T(8,128)(2,1)S(1)} %pick_rows.4), channel_id=1, source_target_pairs={{4,8},{8,4},{5,9},{9,5},{6,10},{10,6},{7,11},{11,7},{20,24},{24,20... | collective-permute-start | bytes 983048 | tf_op jit(solution)/shard_map/ppermute | solution.py:354
  13.9 0.9 %pick_rows.5 = bf16[640,256]{1,0:T(8,128)(2,1)S(1)} custom-call(s32[1]{0:T(128)} %bitcast.3.base_ref, s32[8,256]{1,0:T(8,128)S(1)} %collective-permute-done.1.ids_ref, bf16[8,80,1024]{2,1,0:T(8,128)(2,1)S(1)} %decode_tables.1.table_ref), custom_call_target="tpu_custom_call" | custom-call | tf_op jit(solution)/shard_map/pick_rows/pallas_call | solution.py:344
  14.7 0.0 copy-start
  14.7 3.7 %collective-permute-start.5 = (bf16[640,256]{1,0:T(8,128)(2,1)S(1)}, bf16[640,256]{1,0:T(8,128)(2,1)S(1)}, u32[]{:S(2)}, u32[]{:S(2)}) collective-permute-start(bf16[640,256]{1,0:T(8,128)(2,1)S(1)} %pick_rows.5), channel_id=1, source_target_pairs={{0,9},{1,8},{12,5},{13,4},{2,11},{3,10},{14,7},{15,6},{16,25},{17,... | collective-permute-start | bytes 983048 | tf_op jit(solution)/shard_map/ppermute | solution.py:341
  18.5 0.0 collective-permute-done.3.refs_2_
  18.5 0.0 collective-permute-done.4.refs_3_
  18.5 0.9 %pick_rows.6 = bf16[640,256]{1,0:T(8,128)(2,1)S(1)} custom-call(s32[1]{0:T(128)} %bitcast.3.base_ref, s32[8,256]{1,0:T(8,128)S(1)} %collective-permute-done.2.ids_ref, bf16[8,80,1024]{2,1,0:T(8,128)(2,1)S(1)} %decode_tables.1.table_ref), custom_call_target="tpu_custom_call" | custom-call | tf_op jit(solution)/shard_map/pick_rows/pallas_call | solution.py:344
  19.3 0.7 %collective-permute-start.6 = (bf16[640,256]{1,0:T(8,128)(2,1)S(1)}, bf16[640,256]{1,0:T(8,128)(2,1)S(1)}, u32[]{:S(2)}, u32[]{:S(2)}) collective-permute-start(bf16[640,256]{1,0:T(8,128)(2,1)S(1)} %pick_rows.6), channel_id=1, source_target_pairs={{0,4},{4,0},{8,12},{12,8},{1,5},{5,1},{9,13},{13,9},{2,6},{6,2},{1... | collective-permute-start | bytes 983048 | tf_op jit(solution)/shard_map/ppermute | solution.py:354
  20.1 0.9 %pick_rows.7 = bf16[640,256]{1,0:T(8,128)(2,1)S(1)} custom-call(s32[1]{0:T(128)} %bitcast.3.base_ref, s32[8,256]{1,0:T(8,128)S(1)} %get-tuple-element.39.ids_ref, bf16[8,80,1024]{2,1,0:T(8,128)(2,1)S(1)} %decode_tables.1.table_ref), custom_call_target="tpu_custom_call" | custom-call | tf_op jit(solution)/shard_map/pick_rows/pallas_call | solution.py:344
  20.9 0.0 collective-permute-done.9
  21.0 0.1 add.20
  21.0 1.3 %collective-permute-start.10 = (bf16[640,256]{1,0:T(8,128)(2,1)S(1)}, bf16[640,256]{1,0:T(8,128)(2,1)S(1)}, u32[]{:S(2)}, u32[]{:S(2)}) collective-permute-start(bf16[640,256]{1,0:T(8,128)(2,1)S(1)} %add.20), channel_id=1, source_target_pairs={{4,12},{8,0},{5,13},{9,1},{6,14},{10,2},{7,15},{11,3},{20,28},{24,... | collective-permute-start | bytes 983048 | tf_op jit(solution)/shard_map/ppermute | solution.py:354
  22.3 0.0 copy-done
  22.4 0.0 collective-permute-done.7.refs_1_
  22.4 2.1 %collective-permute-start.8 = (bf16[16,2304]{1,0:T(8,128)(2,1)S(1)}, bf16[16,2304]{1,0:T(8,128)(2,1)S(1)}, u32[]{:S(2)}, u32[]{:S(2)}) collective-permute-start(bf16[16,2304]{1,0:T(8,128)(2,1)S(1)} %slice.6), channel_id=1, source_target_pairs={{0,1},{4,5},{8,9},{12,13},{2,3},{6,7},{10,11},{14,15},{16,17},{20,... | collective-permute-start | bytes 221192 | tf_op jit(solution)/shard_map/ppermute | solution.py:439
  24.5 1.9 %collective-permute-done.5 = bf16[640,256]{1,0:T(8,128)(2,1)S(1)} collective-permute-done((bf16[640,256]{1,0:T(8,128)(2,1)S(1)}, bf16[640,256]{1,0:T(8,128)(2,1)S(1)}, u32[]{:S(2)}, u32[]{:S(2)}) %collective-permute-start.5) | collective-permute-done | bytes 327712 | tf_op jit(solution)/shard_map/ppermute | solution.py:341
  26.4 7.0 %collective-permute-done.6 = bf16[640,256]{1,0:T(8,128)(2,1)S(1)} collective-permute-done((bf16[640,256]{1,0:T(8,128)(2,1)S(1)}, bf16[640,256]{1,0:T(8,128)(2,1)S(1)}, u32[]{:S(2)}, u32[]{:S(2)}) %collective-permute-start.6) | collective-permute-done | bytes 327712 | tf_op jit(solution)/shard_map/ppermute | solution.py:354
  33.5 0.0 collective-permute-done.8.refs_4_
  33.5 4.3 %collective-permute-done.10.refs_2_ = bf16[640,256]{1,0:T(8,128)(2,1)S(1)} collective-permute-done((bf16[640,256]{1,0:T(8,128)(2,1)S(1)}, bf16[640,256]{1,0:T(8,128)(2,1)S(1)}, u32[]{:S(2)}, u32[]{:S(2)}) %collective-permute-start.10) | collective-permute-done | bytes 327712 | tf_op jit(solution)/shard_map/ppermute | solution.py:354
  37.8 0.1 merge.1.body_ref
  37.9 1.6 %collective-permute-start.12 = (bf16[640,256]{1,0:T(8,128)(2,1)S(1)}, bf16[640,256]{1,0:T(8,128)(2,1)S(1)}, u32[]{:S(2)}, u32[]{:S(2)}) collective-permute-start(bf16[640,256]{1,0:T(8,128)(2,1)S(1)} %merge.1.body_ref), channel_id=1, source_target_pairs={{0,2},{2,0},{1,3},{3,1},{4,6},{6,4},{5,7},{7,5},{8,10},{10,8},{9,1... | collective-permute-start | bytes 983048 | tf_op jit(solution)/shard_map/ppermute | solution.py:450
  39.5 1.7 %collective-permute-start.13 = (bf16[640,128]{1,0:T(8,128)(2,1)S(1)}, bf16[640,128]{1,0:T(8,128)(2,1)S(1)}, u32[]{:S(2)}, u32[]{:S(2)}) collective-permute-start(bf16[640,128]{1,0:T(8,128)(2,1)S(1)} %slice.8), channel_id=1, source_target_pairs={{0,1},{2,3},{4,5},{6,7},{8,9},{10,11},{12,13},{14,15},{16,17},{18,... | collective-permute-start | bytes 491528 | tf_op jit(solution)/shard_map/ppermute | solution.py:463
  41.2 1.6 %collective-permute-start.11 = (bf16[640,128]{1,0:T(8,128)(2,1)S(1)}, bf16[640,128]{1,0:T(8,128)(2,1)S(1)}, u32[]{:S(2)}, u32[]{:S(2)}) collective-permute-start(bf16[640,128]{1,0:T(8,128)(2,1)S(1)} %slice.8), channel_id=1, source_target_pairs={{0,3},{2,1},{4,7},{6,5},{8,11},{10,9},{12,15},{14,13},{16,19},{18,... | collective-permute-start | bytes 491528 | tf_op jit(solution)/shard_map/ppermute | solution.py:463
  42.8 0.1 pad_add_fusion.where_ref
  42.9 0.0 collective-permute-done.13.rim_ref
  42.9 5.6 %project_own.1 = (f32[2,272,1152]{2,1,0:T(8,128)S(1)}, f32[2,272,1152]{2,1,0:T(8,128)S(1)}, bf16[2,2,640,1152]{3,2,1,0:T(8,128)(2,1)S(1)}, bf16[2,272,1152]{2,1,0:T(8,128)(2,1)S(1)}, f32[272,8]{1,0:T(8,128)S(1)}) custom-call(s32[2]{0:T(128)S(1)} %pad_add_fusion.where_ref, bf16[640,128]{1,0:T(8,128)(2,1)S(1)} %collective-permute-done.13.rim_ref, ...), custom_call_target="tpu_custom_call" | custom-call | tf_op jit(solution)/shard_map/project_own/pallas_call | solution.py:469
  48.5 0.0 collective-permute-done.11.refs_0_
  48.5 0.0 collective-permute-done.12.refs_1_
  48.5 0.0 copy-start.1
  48.5 3.6 %project_others.1 = (f32[2,272,1152]{2,1,0:T(8,128)}, f32[8,272]{1,0:T(8,128)S(1)}) custom-call(s32[2]{0:T(128)S(1)} %pad_add_fusion.where_ref, bf16[640,128]{1,0:T(8,128)(2,1)S(1)} %collective-permute-done.11.refs_0_, bf16[640,256]{1,0:T(8,128)(2,1)S(1)} %collective-permute-done.12.refs_1_, bf16[2,2,640,1152]{3,2,1,0:T(8,128)(2,1)S(1)} %get-tuple-element.46.refs_2_, ...), custom_call_target="tpu_custom_call" | custom-call | tf_op jit(solution)/shard_map/project_others/pallas_call | solution.py:488
  52.1 1.6 %collective-permute-start.14 = (f32[8,272]{1,0:T(8,128)S(1)}, f32[8,272]{1,0:T(8,128)S(1)}, u32[]{:S(2)}, u32[]{:S(2)}) collective-permute-start(f32[8,272]{1,0:T(8,128)S(1)} %get-tuple-element.51.refs_0_), channel_id=1, source_target_pairs={{0,2},{2,0},{1,3},{3,1},{4,6},{6,4},{5,7},{7,5},{8,10},{10,8},{9,1... | collective-permute-start | bytes 26120 | tf_op jit(solution)/shard_map/ppermute | solution.py:502
  53.7 0.0 copy-done.1
  53.7 1.9 %prepare.1 = (f32[2,256,1152]{2,1,0:T(8,128)S(1)}, f32[3,2,256,1152]{3,2,1,0:T(8,128)S(1)}) custom-call(f32[4,2304]{1,0:T(4,128)S(1)} %copy-done.1, f32[2,272,1152]{2,1,0:T(8,128)} %get-tuple-element.52.value_hbm), custom_call_target="tpu_custom_call" | custom-call | tf_op jit(solution)/shard_map/prepare/pallas_call | solution.py:510
  55.6 0.3 collective-permute-done.14.refs_1_
  55.9 2.8 %finish.1 = bf16[256,2304]{1,0:T(8,128)(2,1)} custom-call(s32[1]{0:T(128)} %bitcast.keep_ref, f32[8,272]{1,0:T(8,128)S(1)} %get-tuple-element.51.refs_0_, f32[8,272]{1,0:T(8,128)S(1)} %collective-permute-done.14.refs_1_, f32[2,256,1152]{2,1,0:T(8,128)S(1)} %get-tuple-element.53.refs_2_, f32[3,2,256,1152]{3,2,1,0:T(8,128)S(1)} %get-tuple-element.54.refs_3_, ...), custom_call_target="tpu_custom_call" | custom-call | tf_op jit(solution)/shard_map/finish/pallas_call | solution.py:525
  (3 shorter events, 0.1 us)
Async XLA Ops:
  0.0 18.5 %collective-permute-start.3 = (bf16[1280,1152]{1,0:T(8,128)(2,1)}, bf16[1280,1152]{1,0:T(8,128)(2,1)}, u32[]{:S(2)}, u32[]{:S(2)}) collective-permute-start(bf16[1280,1152]{1,0:T(8,128)(2,1)} %refs_0_.1), channel_id=1, source_target_pairs={{0,1},{1,0},{2,3},{3,2},{4,5},{5,4},{6,7},{7,6},{8,9},{9,8},{10,11... | collective-permute-start | bytes 8847368 | tf_op jit(solution)/shard_map/ppermute | solution.py:433
  0.5 18.0 %collective-permute-start.4 = (bf16[1280,1152]{1,0:T(8,128)(2,1)}, bf16[1280,1152]{1,0:T(8,128)(2,1)}, u32[]{:S(2)}, u32[]{:S(2)}) collective-permute-start(bf16[1280,1152]{1,0:T(8,128)(2,1)} %refs_1_.1), channel_id=1, source_target_pairs={{0,1},{1,0},{2,3},{3,2},{4,5},{5,4},{6,7},{7,6},{8,9},{9,8},{10,11... | collective-permute-start | bytes 8847368 | tf_op jit(solution)/shard_map/ppermute | solution.py:434
  2.0 6.7 %collective-permute-start = (s32[8,256]{1,0:T(8,128)S(1)}, s32[8,256]{1,0:T(8,128)S(1)}, u32[]{:S(2)}, u32[]{:S(2)}) collective-permute-start(s32[8,256]{1,0:T(8,128)S(1)} %get-tuple-element.39.ids_ref), channel_id=1, source_target_pairs={{0,12},{4,8},{8,4},{12,0},{1,13},{5,9},{9,5},{13,1},{2,14},{6,10},... | collective-permute-start | bytes 24584 | tf_op jit(solution)/shard_map/ppermute | solution.py:338
  7.1 4.0 %collective-permute-start.1 = (s32[8,256]{1,0:T(8,128)S(1)}, s32[8,256]{1,0:T(8,128)S(1)}, u32[]{:S(2)}, u32[]{:S(2)}) collective-permute-start(s32[8,256]{1,0:T(8,128)S(1)} %get-tuple-element.39.ids_ref), channel_id=1, source_target_pairs={{0,8},{1,9},{4,13},{5,12},{8,1},{9,0},{12,4},{13,5},{2,10},{3,11},... | collective-permute-start | bytes 24584 | tf_op jit(solution)/shard_map/ppermute | solution.py:341
  7.2 4.0 %collective-permute-start.2 = (s32[8,256]{1,0:T(8,128)S(1)}, s32[8,256]{1,0:T(8,128)S(1)}, u32[]{:S(2)}, u32[]{:S(2)}) collective-permute-start(s32[8,256]{1,0:T(8,128)S(1)} %get-tuple-element.39.ids_ref), channel_id=1, source_target_pairs={{0,4},{4,0},{8,12},{12,8},{1,5},{5,1},{9,13},{13,9},{2,6},{6,2},{1... | collective-permute-start | bytes 24584 | tf_op jit(solution)/shard_map/ppermute | solution.py:338
  11.1 9.8 %collective-permute-start.9 = (bf16[640,256]{1,0:T(8,128)(2,1)S(1)}, bf16[640,256]{1,0:T(8,128)(2,1)S(1)}, u32[]{:S(2)}, u32[]{:S(2)}) collective-permute-start(bf16[640,256]{1,0:T(8,128)(2,1)S(1)} %pick_rows.4), channel_id=1, source_target_pairs={{0,4},{12,8},{1,5},{13,9},{2,6},{14,10},{3,7},{15,11},{16,20},{28,... | collective-permute-start | bytes 983048 | tf_op jit(solution)/shard_map/ppermute | solution.py:354
  13.2 9.2 %collective-permute-start.7 = (bf16[640,256]{1,0:T(8,128)(2,1)S(1)}, bf16[640,256]{1,0:T(8,128)(2,1)S(1)}, u32[]{:S(2)}, u32[]{:S(2)}) collective-permute-start(bf16[640,256]{1,0:T(8,128)(2,1)S(1)} %pick_rows.4), channel_id=1, source_target_pairs={{4,8},{8,4},{5,9},{9,5},{6,10},{10,6},{7,11},{11,7},{20,24},{24,20... | collective-permute-start | bytes 983048 | tf_op jit(solution)/shard_map/ppermute | solution.py:354
  14.7 7.6 %copy-start = (bf16[256,2304]{1,0:T(8,128)(2,1)S(1)}, bf16[256,2304]{1,0:T(8,128)(2,1)}, u32[]{:S(2)}) copy-start(bf16[256,2304]{1,0:T(8,128)(2,1)} %refs_4_.1) | copy-start | bytes 3538948
  14.7 11.6 %collective-permute-start.5 = (bf16[640,256]{1,0:T(8,128)(2,1)S(1)}, bf16[640,256]{1,0:T(8,128)(2,1)S(1)}, u32[]{:S(2)}, u32[]{:S(2)}) collective-permute-start(bf16[640,256]{1,0:T(8,128)(2,1)S(1)} %pick_rows.5), channel_id=1, source_target_pairs={{0,9},{1,8},{12,5},{13,4},{2,11},{3,10},{14,7},{15,6},{16,25},{17,... | collective-permute-start | bytes 983048 | tf_op jit(solution)/shard_map/ppermute | solution.py:341
  19.3 14.1 %collective-permute-start.6 = (bf16[640,256]{1,0:T(8,128)(2,1)S(1)}, bf16[640,256]{1,0:T(8,128)(2,1)S(1)}, u32[]{:S(2)}, u32[]{:S(2)}) collective-permute-start(bf16[640,256]{1,0:T(8,128)(2,1)S(1)} %pick_rows.6), channel_id=1, source_target_pairs={{0,4},{4,0},{8,12},{12,8},{1,5},{5,1},{9,13},{13,9},{2,6},{6,2},{1... | collective-permute-start | bytes 983048 | tf_op jit(solution)/shard_map/ppermute | solution.py:354
  21.0 16.7 %collective-permute-start.10 = (bf16[640,256]{1,0:T(8,128)(2,1)S(1)}, bf16[640,256]{1,0:T(8,128)(2,1)S(1)}, u32[]{:S(2)}, u32[]{:S(2)}) collective-permute-start(bf16[640,256]{1,0:T(8,128)(2,1)S(1)} %add.20), channel_id=1, source_target_pairs={{4,12},{8,0},{5,13},{9,1},{6,14},{10,2},{7,15},{11,3},{20,28},{24,... | collective-permute-start | bytes 983048 | tf_op jit(solution)/shard_map/ppermute | solution.py:354
  22.4 11.1 %collective-permute-start.8 = (bf16[16,2304]{1,0:T(8,128)(2,1)S(1)}, bf16[16,2304]{1,0:T(8,128)(2,1)S(1)}, u32[]{:S(2)}, u32[]{:S(2)}) collective-permute-start(bf16[16,2304]{1,0:T(8,128)(2,1)S(1)} %slice.6), channel_id=1, source_target_pairs={{0,1},{4,5},{8,9},{12,13},{2,3},{6,7},{10,11},{14,15},{16,17},{20,... | collective-permute-start | bytes 221192 | tf_op jit(solution)/shard_map/ppermute | solution.py:439
  37.9 10.6 %collective-permute-start.12 = (bf16[640,256]{1,0:T(8,128)(2,1)S(1)}, bf16[640,256]{1,0:T(8,128)(2,1)S(1)}, u32[]{:S(2)}, u32[]{:S(2)}) collective-permute-start(bf16[640,256]{1,0:T(8,128)(2,1)S(1)} %merge.1.body_ref), channel_id=1, source_target_pairs={{0,2},{2,0},{1,3},{3,1},{4,6},{6,4},{5,7},{7,5},{8,10},{10,8},{9,1... | collective-permute-start | bytes 983048 | tf_op jit(solution)/shard_map/ppermute | solution.py:450
  39.5 3.5 %collective-permute-start.13 = (bf16[640,128]{1,0:T(8,128)(2,1)S(1)}, bf16[640,128]{1,0:T(8,128)(2,1)S(1)}, u32[]{:S(2)}, u32[]{:S(2)}) collective-permute-start(bf16[640,128]{1,0:T(8,128)(2,1)S(1)} %slice.8), channel_id=1, source_target_pairs={{0,1},{2,3},{4,5},{6,7},{8,9},{10,11},{12,13},{14,15},{16,17},{18,... | collective-permute-start | bytes 491528 | tf_op jit(solution)/shard_map/ppermute | solution.py:463
  41.2 7.3 %collective-permute-start.11 = (bf16[640,128]{1,0:T(8,128)(2,1)S(1)}, bf16[640,128]{1,0:T(8,128)(2,1)S(1)}, u32[]{:S(2)}, u32[]{:S(2)}) collective-permute-start(bf16[640,128]{1,0:T(8,128)(2,1)S(1)} %slice.8), channel_id=1, source_target_pairs={{0,3},{2,1},{4,7},{6,5},{8,11},{10,9},{12,15},{14,13},{16,19},{18,... | collective-permute-start | bytes 491528 | tf_op jit(solution)/shard_map/ppermute | solution.py:463
  48.5 5.2 %copy-start.1 = (f32[4,2304]{1,0:T(4,128)S(1)}, f32[4,2304]{1,0:T(4,128)}, u32[]{:S(2)}) copy-start(f32[4,2304]{1,0:T(4,128)} %refs_5_.3) | copy-start | bytes 110596
  52.1 3.8 %collective-permute-start.14 = (f32[8,272]{1,0:T(8,128)S(1)}, f32[8,272]{1,0:T(8,128)S(1)}, u32[]{:S(2)}, u32[]{:S(2)}) collective-permute-start(f32[8,272]{1,0:T(8,128)S(1)} %get-tuple-element.51.refs_0_), channel_id=1, source_target_pairs={{0,2},{2,0},{1,3},{3,1},{4,6},{6,4},{5,7},{7,5},{8,10},{10,8},{9,1... | collective-permute-start | bytes 26120 | tf_op jit(solution)/shard_map/ppermute | solution.py:502

commit v28 on v27

--- a/solution.py
+++ b/solution.py
@@ -43,16 +43,15 @@
 
 
 def place_kernel(
-    ids_hbm, place_hbm, codes_hbm, scales_hbm, out_ref, codes_ref, scales_ref, ids_ref, place_ref, sems
+    ids_hbm, place_hbm, codes_hbm, out_ref, codes_ref, ids_ref, place_ref, sems
 ):
     copies = [
         pltpu.make_async_copy(place_hbm, place_ref, sems.at[0]),
         pltpu.make_async_copy(ids_hbm, ids_ref, sems.at[1]),
-        pltpu.make_async_copy(scales_hbm, scales_ref, sems.at[2]),
     ]
     for n in range(codes_ref.shape[0]):
         copies.append(
-            pltpu.make_async_copy(codes_hbm.at[n], codes_ref.at[n], sems.at[3 + n])
+            pltpu.make_async_copy(codes_hbm.at[n], codes_ref.at[n], sems.at[2 + n])
         )
     for copy in copies:
         copy.start()
@@ -87,10 +86,11 @@
     parity = (parity ^ (parity >> 1)) & 1
     same = (entry >> 4) == (column >> 4)
     rotation = jnp.where(same, 0.25 - 0.5 * parity.astype(F32), 0.0).astype(BF16)
+    scales = scales_ref[...].astype(F32)
     for head in range(heads):
         factors = jnp.concatenate(
             [
-                jnp.broadcast_to(scales_ref[b, head : head + 1, :].astype(F32), (16, rows))
+                jnp.broadcast_to(scales[b, head : head + 1, :], (16, rows))
                 for b in range(blocks)
             ],
             axis=0,
@@ -404,23 +404,22 @@
     places = row_place.reshape(-1, LANES)
     codes = table_codes.transpose(0, 2, 1)
     scales = table_scales.transpose(2, 0, 1)
-    stored, codes, scales = pl.pallas_call(
+    stored, codes = pl.pallas_call(
         place_kernel,
-        in_specs=[anywhere] * 4,
-        out_specs=(resident,) * 3,
+        in_specs=[anywhere] * 3,
+        out_specs=(resident,) * 2,
         out_shape=(
             jax.ShapeDtypeStruct((heads, tokens), I32),
             jax.ShapeDtypeStruct(codes.shape, BF16),
-            jax.ShapeDtypeStruct(scales.shape, BF16),
         ),
         scratch_shapes=[
             pltpu.VMEM((heads, tokens), I32),
             pltpu.VMEM(places.shape, I32),
-            pltpu.SemaphoreType.DMA((heads + 3,)),
+            pltpu.SemaphoreType.DMA((heads + 2,)),
         ],
         compiler_params=limit(4),
         name="place_rows",
-    )(*[in_hbm(x) for x in (row_ids.T, places, codes, scales)])
+    )(*[in_hbm(x) for x in (row_ids.T, places, codes)])
     decoded = pl.pallas_call(
         decode_kernel,
         in_specs=[resident] * 2,

time: 59.2 us -> 59.3 us (level)
  waiting for transfers between devices: 15.5 us -> 14.6 us
  local copies, waits for them, and re-layouts: 0.03 us -> 0.92 us
    ppermute x4, waiting for transfers between devices: 11.3 us -> 10.2 us  [send(): return lax.ppermute(x, 'mem', pairs)]
    unnamed x4 -> x6, local copies, waits for them, and re-layouts: 0.01 us -> 0.9 us
    ppermute x2, waiting for transfers between devices: 3.36 us -> 4.1 us  [crossing(): lax.ppermute(x, ('mem', 'rep'), [(2 * a + b, 2 * c + d) for a, b, c, d in...]
  transfers between devices with their start and end apart: 15 -> 15, of which waited for: 6 -> 5; matrix products, arithmetic and copies ran while one was open for 0% -> 0% of each run, Pallas kernels for 23% -> 22%
where the time goes in v28:
time: 59.3 us; the launch traced here: 59 us
  starting transfers between devices  23.1 us (39%)
  Pallas kernels  19.8 us (33%)
  waiting for transfers between devices  14.6 us (25%)
  local copies, waits for them, and re-layouts  0.92 us (2%)
    ppermute x4, waiting for transfers between devices, send(): return lax.ppermute(x, 'mem', pairs)  10.2 us
    pallas_call x1, Pallas kernels, shards(): pl.pallas_call(functools.partial(project_own_kernel, tps), in_specs=[smem...  5.55 us
    ppermute x2, starting transfers between devices, ask(): return lax.ppermute(ids, 'mem', [(i, i ^ x) for i in range(4)])  5.35 us
    ppermute x4, starting transfers between devices, send(): return lax.ppermute(x, 'mem', pairs)  5.18 us
    ppermute x2, waiting for transfers between devices, crossing(): lax.ppermute(x, ('mem', 'rep'), [(2 * a + b, 2 * c + d) for a, b, c, d in...  4.1 us
    pallas_call x1, Pallas kernels, shards(): pl.pallas_call(functools.partial(project_others_kernel, tps), in_specs=[s...  3.6 us
    pallas_call x4, Pallas kernels, pick(): pl.pallas_call(pick_kernel, in_specs=[pl.BlockSpec(memory_space=pltpu.SME...  3.46 us
    ppermute x2, starting transfers between devices, next_rim(): return lax.ppermute(rim, ('mem', 'tp', 'rep'), pairs)  3.36 us
  transfers between devices with their start and end apart: 15, of which 5 were waited for; matrix products, arithmetic and copies ran while one was open for 0% of the time, Pallas kernels for 22%

profile of v28, /device:TPU:0, one launch (start us, length us, event | category | flops | bytes accessed | tf_op | source)
XLA Modules:
  0.0 59.0 jit_solution(8908307697398807559)
XLA Ops:
  0.0 0.5 collective-permute-start.3
  0.5 0.1 collective-permute-start.4
  0.5 1.5 %place_rows.1 = (s32[8,256]{1,0:T(8,128)S(1)}, bf16[8,80,1024]{2,1,0:T(8,128)(2,1)S(1)}) custom-call(s32[8,256]{1,0:T(8,128)} %bitcast.11, s32[32,128]{1,0:T(8,128)} %bitcast.10, bf16[8,80,1024]{2,1,0:T(8,128)(2,1)} %bitcast.9), custom_call_target="tpu_custom_call" | custom-call | tf_op jit(solution)/shard_map/place_rows/pallas_call | solution.py:407
  2.0 5.1 %collective-permute-start = (s32[8,256]{1,0:T(8,128)S(1)}, s32[8,256]{1,0:T(8,128)S(1)}, u32[]{:S(2)}, u32[]{:S(2)}) collective-permute-start(s32[8,256]{1,0:T(8,128)S(1)} %get-tuple-element.37.ids_ref), channel_id=1, source_target_pairs={{0,12},{4,8},{8,4},{12,0},{1,13},{5,9},{9,5},{13,1},{2,14},{6,10},... | collective-permute-start | bytes 24584 | tf_op jit(solution)/shard_map/ppermute | solution.py:338
  7.1 0.0 collective-permute-start.1
  7.1 0.2 collective-permute-start.2
  7.4 0.9 %copy-done.2 = bf16[8,1024,5]{1,0,2:T(8,128)(2,1)S(1)} copy-done((bf16[8,1024,5]{1,0,2:T(8,128)(2,1)S(1)}, bf16[8,1024,5]{1,0,2:T(8,128)(2,1)}, u32[]{:S(2)}) %copy-start.2) | copy-done | bytes 81944
  8.3 0.8 %decode_tables.1.table_ref = bf16[8,80,1024]{2,1,0:T(8,128)(2,1)S(1)} custom-call(bf16[8,80,1024]{2,1,0:T(8,128)(2,1)S(1)} %get-tuple-element.30.codes_ref, bf16[5,8,1024]{2,1,0:T(8,128)(2,1)S(1)} %bitcast.8), custom_call_target="tpu_custom_call" | custom-call | tf_op jit(solution)/shard_map/decode_tables/pallas_call | solution.py:423
  9.1 0.0 collective-permute-done.ids_ref
  9.1 0.9 %pick_rows.4 = bf16[640,256]{1,0:T(8,128)(2,1)S(1)} custom-call(s32[1]{0:T(128)} %bitcast.3.base_ref, s32[8,256]{1,0:T(8,128)S(1)} %collective-permute-done.ids_ref, bf16[8,80,1024]{2,1,0:T(8,128)(2,1)S(1)} %decode_tables.1.table_ref), custom_call_target="tpu_custom_call" | custom-call | tf_op jit(solution)/shard_map/pick_rows/pallas_call | solution.py:344
  9.9 1.2 %collective-permute-done.1.ids_ref = s32[8,256]{1,0:T(8,128)S(1)} collective-permute-done((s32[8,256]{1,0:T(8,128)S(1)}, s32[8,256]{1,0:T(8,128)S(1)}, u32[]{:S(2)}, u32[]{:S(2)}) %collective-permute-start.1) | collective-permute-done | bytes 8224 | tf_op jit(solution)/shard_map/ppermute | solution.py:341
  11.1 0.0 collective-permute-done.2.ids_ref
  11.1 2.6 %collective-permute-start.9 = (bf16[640,256]{1,0:T(8,128)(2,1)S(1)}, bf16[640,256]{1,0:T(8,128)(2,1)S(1)}, u32[]{:S(2)}, u32[]{:S(2)}) collective-permute-start(bf16[640,256]{1,0:T(8,128)(2,1)S(1)} %pick_rows.4), channel_id=1, source_target_pairs={{0,4},{12,8},{1,5},{13,9},{2,6},{14,10},{3,7},{15,11},{16,20},{28,... | collective-permute-start | bytes 983048 | tf_op jit(solution)/shard_map/ppermute | solution.py:354
  13.7 0.7 %collective-permute-start.7 = (bf16[640,256]{1,0:T(8,128)(2,1)S(1)}, bf16[640,256]{1,0:T(8,128)(2,1)S(1)}, u32[]{:S(2)}, u32[]{:S(2)}) collective-permute-start(bf16[640,256]{1,0:T(8,128)(2,1)S(1)} %pick_rows.4), channel_id=1, source_target_pairs={{4,8},{8,4},{5,9},{9,5},{6,10},{10,6},{7,11},{11,7},{20,24},{24,20... | collective-permute-start | bytes 983048 | tf_op jit(solution)/shard_map/ppermute | solution.py:354
  14.4 0.9 %pick_rows.5 = bf16[640,256]{1,0:T(8,128)(2,1)S(1)} custom-call(s32[1]{0:T(128)} %bitcast.3.base_ref, s32[8,256]{1,0:T(8,128)S(1)} %collective-permute-done.1.ids_ref, bf16[8,80,1024]{2,1,0:T(8,128)(2,1)S(1)} %decode_tables.1.table_ref), custom_call_target="tpu_custom_call" | custom-call | tf_op jit(solution)/shard_map/pick_rows/pallas_call | solution.py:344
  15.2 0.0 copy-start
  15.3 3.3 %collective-permute-start.5 = (bf16[640,256]{1,0:T(8,128)(2,1)S(1)}, bf16[640,256]{1,0:T(8,128)(2,1)S(1)}, u32[]{:S(2)}, u32[]{:S(2)}) collective-permute-start(bf16[640,256]{1,0:T(8,128)(2,1)S(1)} %pick_rows.5), channel_id=1, source_target_pairs={{0,9},{1,8},{12,5},{13,4},{2,11},{3,10},{14,7},{15,6},{16,25},{17,... | collective-permute-start | bytes 983048 | tf_op jit(solution)/shard_map/ppermute | solution.py:341
  18.5 0.0 collective-permute-done.3.refs_2_
  18.6 0.0 collective-permute-done.4.refs_3_
  18.6 0.9 %pick_rows.6 = bf16[640,256]{1,0:T(8,128)(2,1)S(1)} custom-call(s32[1]{0:T(128)} %bitcast.3.base_ref, s32[8,256]{1,0:T(8,128)S(1)} %collective-permute-done.2.ids_ref, bf16[8,80,1024]{2,1,0:T(8,128)(2,1)S(1)} %decode_tables.1.table_ref), custom_call_target="tpu_custom_call" | custom-call | tf_op jit(solution)/shard_map/pick_rows/pallas_call | solution.py:344
  19.4 0.6 %collective-permute-start.6 = (bf16[640,256]{1,0:T(8,128)(2,1)S(1)}, bf16[640,256]{1,0:T(8,128)(2,1)S(1)}, u32[]{:S(2)}, u32[]{:S(2)}) collective-permute-start(bf16[640,256]{1,0:T(8,128)(2,1)S(1)} %pick_rows.6), channel_id=1, source_target_pairs={{0,4},{4,0},{8,12},{12,8},{1,5},{5,1},{9,13},{13,9},{2,6},{6,2},{1... | collective-permute-start | bytes 983048 | tf_op jit(solution)/shard_map/ppermute | solution.py:354
  20.1 0.9 %pick_rows.7 = bf16[640,256]{1,0:T(8,128)(2,1)S(1)} custom-call(s32[1]{0:T(128)} %bitcast.3.base_ref, s32[8,256]{1,0:T(8,128)S(1)} %get-tuple-element.37.ids_ref, bf16[8,80,1024]{2,1,0:T(8,128)(2,1)S(1)} %decode_tables.1.table_ref), custom_call_target="tpu_custom_call" | custom-call | tf_op jit(solution)/shard_map/pick_rows/pallas_call | solution.py:344
  20.9 0.0 collective-permute-done.9
  20.9 0.1 add.20
  21.0 1.3 %collective-permute-start.10 = (bf16[640,256]{1,0:T(8,128)(2,1)S(1)}, bf16[640,256]{1,0:T(8,128)(2,1)S(1)}, u32[]{:S(2)}, u32[]{:S(2)}) collective-permute-start(bf16[640,256]{1,0:T(8,128)(2,1)S(1)} %add.20), channel_id=1, source_target_pairs={{4,12},{8,0},{5,13},{9,1},{6,14},{10,2},{7,15},{11,3},{20,28},{24,... | collective-permute-start | bytes 983048 | tf_op jit(solution)/shard_map/ppermute | solution.py:354
  22.3 0.0 copy-done
  22.3 0.0 collective-permute-done.7.refs_1_
  22.4 2.3 %collective-permute-start.8 = (bf16[16,2304]{1,0:T(8,128)(2,1)S(1)}, bf16[16,2304]{1,0:T(8,128)(2,1)S(1)}, u32[]{:S(2)}, u32[]{:S(2)}) collective-permute-start(bf16[16,2304]{1,0:T(8,128)(2,1)S(1)} %slice.6), channel_id=1, source_target_pairs={{0,1},{4,5},{8,9},{12,13},{2,3},{6,7},{10,11},{14,15},{16,17},{20,... | collective-permute-start | bytes 221192 | tf_op jit(solution)/shard_map/ppermute | solution.py:438
  24.7 2.9 %collective-permute-done.5 = bf16[640,256]{1,0:T(8,128)(2,1)S(1)} collective-permute-done((bf16[640,256]{1,0:T(8,128)(2,1)S(1)}, bf16[640,256]{1,0:T(8,128)(2,1)S(1)}, u32[]{:S(2)}, u32[]{:S(2)}) %collective-permute-start.5) | collective-permute-done | bytes 327712 | tf_op jit(solution)/shard_map/ppermute | solution.py:341
  27.6 6.7 %collective-permute-done.6 = bf16[640,256]{1,0:T(8,128)(2,1)S(1)} collective-permute-done((bf16[640,256]{1,0:T(8,128)(2,1)S(1)}, bf16[640,256]{1,0:T(8,128)(2,1)S(1)}, u32[]{:S(2)}, u32[]{:S(2)}) %collective-permute-start.6) | collective-permute-done | bytes 327712 | tf_op jit(solution)/shard_map/ppermute | solution.py:354
  34.4 0.0 collective-permute-done.8.refs_4_
  34.4 3.5 %collective-permute-done.10.refs_2_ = bf16[640,256]{1,0:T(8,128)(2,1)S(1)} collective-permute-done((bf16[640,256]{1,0:T(8,128)(2,1)S(1)}, bf16[640,256]{1,0:T(8,128)(2,1)S(1)}, u32[]{:S(2)}, u32[]{:S(2)}) %collective-permute-start.10) | collective-permute-done | bytes 327712 | tf_op jit(solution)/shard_map/ppermute | solution.py:354
  37.8 0.1 merge.1.body_ref
  38.0 1.6 %collective-permute-start.12 = (bf16[640,256]{1,0:T(8,128)(2,1)S(1)}, bf16[640,256]{1,0:T(8,128)(2,1)S(1)}, u32[]{:S(2)}, u32[]{:S(2)}) collective-permute-start(bf16[640,256]{1,0:T(8,128)(2,1)S(1)} %merge.1.body_ref), channel_id=1, source_target_pairs={{0,2},{2,0},{1,3},{3,1},{4,6},{6,4},{5,7},{7,5},{8,10},{10,8},{9,1... | collective-permute-start | bytes 983048 | tf_op jit(solution)/shard_map/ppermute | solution.py:449
  39.5 1.7 %collective-permute-start.13 = (bf16[640,128]{1,0:T(8,128)(2,1)S(1)}, bf16[640,128]{1,0:T(8,128)(2,1)S(1)}, u32[]{:S(2)}, u32[]{:S(2)}) collective-permute-start(bf16[640,128]{1,0:T(8,128)(2,1)S(1)} %slice.8), channel_id=1, source_target_pairs={{0,1},{2,3},{4,5},{6,7},{8,9},{10,11},{12,13},{14,15},{16,17},{18,... | collective-permute-start | bytes 491528 | tf_op jit(solution)/shard_map/ppermute | solution.py:462
  41.3 1.6 %collective-permute-start.11 = (bf16[640,128]{1,0:T(8,128)(2,1)S(1)}, bf16[640,128]{1,0:T(8,128)(2,1)S(1)}, u32[]{:S(2)}, u32[]{:S(2)}) collective-permute-start(bf16[640,128]{1,0:T(8,128)(2,1)S(1)} %slice.8), channel_id=1, source_target_pairs={{0,3},{2,1},{4,7},{6,5},{8,11},{10,9},{12,15},{14,13},{16,19},{18,... | collective-permute-start | bytes 491528 | tf_op jit(solution)/shard_map/ppermute | solution.py:462
  42.9 0.1 pad_add_fusion.where_ref
  43.0 0.0 collective-permute-done.13.rim_ref
  43.0 5.6 %project_own.1 = (f32[2,272,1152]{2,1,0:T(8,128)S(1)}, f32[2,272,1152]{2,1,0:T(8,128)S(1)}, bf16[2,2,640,1152]{3,2,1,0:T(8,128)(2,1)S(1)}, bf16[2,272,1152]{2,1,0:T(8,128)(2,1)S(1)}, f32[272,8]{1,0:T(8,128)S(1)}) custom-call(s32[2]{0:T(128)S(1)} %pad_add_fusion.where_ref, bf16[640,128]{1,0:T(8,128)(2,1)S(1)} %collective-permute-done.13.rim_ref, ...), custom_call_target="tpu_custom_call" | custom-call | tf_op jit(solution)/shard_map/project_own/pallas_call | solution.py:468
  48.6 0.0 collective-permute-done.11.refs_0_
  48.6 0.0 collective-permute-done.12.refs_1_
  48.6 0.0 copy-start.1
  48.6 3.6 %project_others.1 = (f32[2,272,1152]{2,1,0:T(8,128)}, f32[8,272]{1,0:T(8,128)S(1)}) custom-call(s32[2]{0:T(128)S(1)} %pad_add_fusion.where_ref, bf16[640,128]{1,0:T(8,128)(2,1)S(1)} %collective-permute-done.11.refs_0_, bf16[640,256]{1,0:T(8,128)(2,1)S(1)} %collective-permute-done.12.refs_1_, bf16[2,2,640,1152]{3,2,1,0:T(8,128)(2,1)S(1)} %get-tuple-element.44.refs_2_, ...), custom_call_target="tpu_custom_call" | custom-call | tf_op jit(solution)/shard_map/project_others/pallas_call | solution.py:487
  52.2 1.6 %collective-permute-start.14 = (f32[8,272]{1,0:T(8,128)S(1)}, f32[8,272]{1,0:T(8,128)S(1)}, u32[]{:S(2)}, u32[]{:S(2)}) collective-permute-start(f32[8,272]{1,0:T(8,128)S(1)} %get-tuple-element.49.refs_0_), channel_id=1, source_target_pairs={{0,2},{2,0},{1,3},{3,1},{4,6},{6,4},{5,7},{7,5},{8,10},{10,8},{9,1... | collective-permute-start | bytes 26120 | tf_op jit(solution)/shard_map/ppermute | solution.py:501
  53.8 0.0 copy-done.1
  53.8 1.9 %prepare.1 = (f32[2,256,1152]{2,1,0:T(8,128)S(1)}, f32[3,2,256,1152]{3,2,1,0:T(8,128)S(1)}) custom-call(f32[4,2304]{1,0:T(4,128)S(1)} %copy-done.1, f32[2,272,1152]{2,1,0:T(8,128)} %get-tuple-element.50.value_hbm), custom_call_target="tpu_custom_call" | custom-call | tf_op jit(solution)/shard_map/prepare/pallas_call | solution.py:509
  55.7 0.3 collective-permute-done.14.refs_1_
  56.0 2.8 %finish.1 = bf16[256,2304]{1,0:T(8,128)(2,1)} custom-call(s32[1]{0:T(128)} %bitcast.keep_ref, f32[8,272]{1,0:T(8,128)S(1)} %get-tuple-element.49.refs_0_, f32[8,272]{1,0:T(8,128)S(1)} %collective-permute-done.14.refs_1_, f32[2,256,1152]{2,1,0:T(8,128)S(1)} %get-tuple-element.51.refs_2_, f32[3,2,256,1152]{3,2,1,0:T(8,128)S(1)} %get-tuple-element.52.refs_3_, ...), custom_call_target="tpu_custom_call" | custom-call | tf_op jit(solution)/shard_map/finish/pallas_call | solution.py:524
  (4 shorter events, 0.1 us)
Async XLA Ops:
  0.0 18.5 %collective-permute-start.3 = (bf16[1280,1152]{1,0:T(8,128)(2,1)}, bf16[1280,1152]{1,0:T(8,128)(2,1)}, u32[]{:S(2)}, u32[]{:S(2)}) collective-permute-start(bf16[1280,1152]{1,0:T(8,128)(2,1)} %refs_0_.1), channel_id=1, source_target_pairs={{0,1},{1,0},{2,3},{3,2},{4,5},{5,4},{6,7},{7,6},{8,9},{9,8},{10,11... | collective-permute-start | bytes 8847368 | tf_op jit(solution)/shard_map/ppermute | solution.py:432
  0.5 18.1 %collective-permute-start.4 = (bf16[1280,1152]{1,0:T(8,128)(2,1)}, bf16[1280,1152]{1,0:T(8,128)(2,1)}, u32[]{:S(2)}, u32[]{:S(2)}) collective-permute-start(bf16[1280,1152]{1,0:T(8,128)(2,1)} %refs_1_.1), channel_id=1, source_target_pairs={{0,1},{1,0},{2,3},{3,2},{4,5},{5,4},{6,7},{7,6},{8,9},{9,8},{10,11... | collective-permute-start | bytes 8847368 | tf_op jit(solution)/shard_map/ppermute | solution.py:433
  2.0 7.1 %collective-permute-start = (s32[8,256]{1,0:T(8,128)S(1)}, s32[8,256]{1,0:T(8,128)S(1)}, u32[]{:S(2)}, u32[]{:S(2)}) collective-permute-start(s32[8,256]{1,0:T(8,128)S(1)} %get-tuple-element.37.ids_ref), channel_id=1, source_target_pairs={{0,12},{4,8},{8,4},{12,0},{1,13},{5,9},{9,5},{13,1},{2,14},{6,10},... | collective-permute-start | bytes 24584 | tf_op jit(solution)/shard_map/ppermute | solution.py:338
  7.1 4.0 %collective-permute-start.1 = (s32[8,256]{1,0:T(8,128)S(1)}, s32[8,256]{1,0:T(8,128)S(1)}, u32[]{:S(2)}, u32[]{:S(2)}) collective-permute-start(s32[8,256]{1,0:T(8,128)S(1)} %get-tuple-element.37.ids_ref), channel_id=1, source_target_pairs={{0,8},{1,9},{4,13},{5,12},{8,1},{9,0},{12,4},{13,5},{2,10},{3,11},... | collective-permute-start | bytes 24584 | tf_op jit(solution)/shard_map/ppermute | solution.py:341
  7.1 4.0 %collective-permute-start.2 = (s32[8,256]{1,0:T(8,128)S(1)}, s32[8,256]{1,0:T(8,128)S(1)}, u32[]{:S(2)}, u32[]{:S(2)}) collective-permute-start(s32[8,256]{1,0:T(8,128)S(1)} %get-tuple-element.37.ids_ref), channel_id=1, source_target_pairs={{0,4},{4,0},{8,12},{12,8},{1,5},{5,1},{9,13},{13,9},{2,6},{6,2},{1... | collective-permute-start | bytes 24584 | tf_op jit(solution)/shard_map/ppermute | solution.py:338
  7.4 0.9 %copy-start.2 = (bf16[8,1024,5]{1,0,2:T(8,128)(2,1)S(1)}, bf16[8,1024,5]{1,0,2:T(8,128)(2,1)}, u32[]{:S(2)}) copy-start(bf16[8,1024,5]{1,0,2:T(8,128)(2,1)} %param.12) | copy-start | bytes 245764
  11.1 9.8 %collective-permute-start.9 = (bf16[640,256]{1,0:T(8,128)(2,1)S(1)}, bf16[640,256]{1,0:T(8,128)(2,1)S(1)}, u32[]{:S(2)}, u32[]{:S(2)}) collective-permute-start(bf16[640,256]{1,0:T(8,128)(2,1)S(1)} %pick_rows.4), channel_id=1, source_target_pairs={{0,4},{12,8},{1,5},{13,9},{2,6},{14,10},{3,7},{15,11},{16,20},{28,... | collective-permute-start | bytes 983048 | tf_op jit(solution)/shard_map/ppermute | solution.py:354
  13.7 8.7 %collective-permute-start.7 = (bf16[640,256]{1,0:T(8,128)(2,1)S(1)}, bf16[640,256]{1,0:T(8,128)(2,1)S(1)}, u32[]{:S(2)}, u32[]{:S(2)}) collective-permute-start(bf16[640,256]{1,0:T(8,128)(2,1)S(1)} %pick_rows.4), channel_id=1, source_target_pairs={{4,8},{8,4},{5,9},{9,5},{6,10},{10,6},{7,11},{11,7},{20,24},{24,20... | collective-permute-start | bytes 983048 | tf_op jit(solution)/shard_map/ppermute | solution.py:354
  15.2 7.1 %copy-start = (bf16[256,2304]{1,0:T(8,128)(2,1)S(1)}, bf16[256,2304]{1,0:T(8,128)(2,1)}, u32[]{:S(2)}) copy-start(bf16[256,2304]{1,0:T(8,128)(2,1)} %refs_4_.1) | copy-start | bytes 3538948
  15.3 12.3 %collective-permute-start.5 = (bf16[640,256]{1,0:T(8,128)(2,1)S(1)}, bf16[640,256]{1,0:T(8,128)(2,1)S(1)}, u32[]{:S(2)}, u32[]{:S(2)}) collective-permute-start(bf16[640,256]{1,0:T(8,128)(2,1)S(1)} %pick_rows.5), channel_id=1, source_target_pairs={{0,9},{1,8},{12,5},{13,4},{2,11},{3,10},{14,7},{15,6},{16,25},{17,... | collective-permute-start | bytes 983048 | tf_op jit(solution)/shard_map/ppermute | solution.py:341
  19.4 14.9 %collective-permute-start.6 = (bf16[640,256]{1,0:T(8,128)(2,1)S(1)}, bf16[640,256]{1,0:T(8,128)(2,1)S(1)}, u32[]{:S(2)}, u32[]{:S(2)}) collective-permute-start(bf16[640,256]{1,0:T(8,128)(2,1)S(1)} %pick_rows.6), channel_id=1, source_target_pairs={{0,4},{4,0},{8,12},{12,8},{1,5},{5,1},{9,13},{13,9},{2,6},{6,2},{1... | collective-permute-start | bytes 983048 | tf_op jit(solution)/shard_map/ppermute | solution.py:354
  21.0 16.8 %collective-permute-start.10 = (bf16[640,256]{1,0:T(8,128)(2,1)S(1)}, bf16[640,256]{1,0:T(8,128)(2,1)S(1)}, u32[]{:S(2)}, u32[]{:S(2)}) collective-permute-start(bf16[640,256]{1,0:T(8,128)(2,1)S(1)} %add.20), channel_id=1, source_target_pairs={{4,12},{8,0},{5,13},{9,1},{6,14},{10,2},{7,15},{11,3},{20,28},{24,... | collective-permute-start | bytes 983048 | tf_op jit(solution)/shard_map/ppermute | solution.py:354
  22.4 12.0 %collective-permute-start.8 = (bf16[16,2304]{1,0:T(8,128)(2,1)S(1)}, bf16[16,2304]{1,0:T(8,128)(2,1)S(1)}, u32[]{:S(2)}, u32[]{:S(2)}) collective-permute-start(bf16[16,2304]{1,0:T(8,128)(2,1)S(1)} %slice.6), channel_id=1, source_target_pairs={{0,1},{4,5},{8,9},{12,13},{2,3},{6,7},{10,11},{14,15},{16,17},{20,... | collective-permute-start | bytes 221192 | tf_op jit(solution)/shard_map/ppermute | solution.py:438
  38.0 10.6 %collective-permute-start.12 = (bf16[640,256]{1,0:T(8,128)(2,1)S(1)}, bf16[640,256]{1,0:T(8,128)(2,1)S(1)}, u32[]{:S(2)}, u32[]{:S(2)}) collective-permute-start(bf16[640,256]{1,0:T(8,128)(2,1)S(1)} %merge.1.body_ref), channel_id=1, source_target_pairs={{0,2},{2,0},{1,3},{3,1},{4,6},{6,4},{5,7},{7,5},{8,10},{10,8},{9,1... | collective-permute-start | bytes 983048 | tf_op jit(solution)/shard_map/ppermute | solution.py:449
  39.5 3.5 %collective-permute-start.13 = (bf16[640,128]{1,0:T(8,128)(2,1)S(1)}, bf16[640,128]{1,0:T(8,128)(2,1)S(1)}, u32[]{:S(2)}, u32[]{:S(2)}) collective-permute-start(bf16[640,128]{1,0:T(8,128)(2,1)S(1)} %slice.8), channel_id=1, source_target_pairs={{0,1},{2,3},{4,5},{6,7},{8,9},{10,11},{12,13},{14,15},{16,17},{18,... | collective-permute-start | bytes 491528 | tf_op jit(solution)/shard_map/ppermute | solution.py:462
  41.3 7.3 %collective-permute-start.11 = (bf16[640,128]{1,0:T(8,128)(2,1)S(1)}, bf16[640,128]{1,0:T(8,128)(2,1)S(1)}, u32[]{:S(2)}, u32[]{:S(2)}) collective-permute-start(bf16[640,128]{1,0:T(8,128)(2,1)S(1)} %slice.8), channel_id=1, source_target_pairs={{0,3},{2,1},{4,7},{6,5},{8,11},{10,9},{12,15},{14,13},{16,19},{18,... | collective-permute-start | bytes 491528 | tf_op jit(solution)/shard_map/ppermute | solution.py:462
  48.6 5.2 %copy-start.1 = (f32[4,2304]{1,0:T(4,128)S(1)}, f32[4,2304]{1,0:T(4,128)}, u32[]{:S(2)}) copy-start(f32[4,2304]{1,0:T(4,128)} %refs_5_.3) | copy-start | bytes 110596
  52.2 3.8 %collective-permute-start.14 = (f32[8,272]{1,0:T(8,128)S(1)}, f32[8,272]{1,0:T(8,128)S(1)}, u32[]{:S(2)}, u32[]{:S(2)}) collective-permute-start(f32[8,272]{1,0:T(8,128)S(1)} %get-tuple-element.49.refs_0_), channel_id=1, source_target_pairs={{0,2},{2,0},{1,3},{3,1},{4,6},{6,4},{5,7},{7,5},{8,10},{10,8},{9,1... | collective-permute-start | bytes 26120 | tf_op jit(solution)/shard_map/ppermute | solution.py:501

commit v29 on v28

--- a/solution.py
+++ b/solution.py
@@ -429,8 +429,8 @@
         name="decode_tables",
     )(codes, scales)
     here = lax.axis_index("mem")
-    other_key = lax.ppermute(key_weight, "rep", [(0, 1), (1, 0)])
-    other_value = lax.ppermute(value_weight, "rep", [(0, 1), (1, 0)])
+    other_key = lax.ppermute(after(key_weight, decoded), "rep", [(0, 1), (1, 0)])
+    other_value = lax.ppermute(after(value_weight, decoded), "rep", [(0, 1), (1, 0)])
     needed = [(i, i + 1) for i in range(blocks - 1) if (i + 1) * tokens % seq_length]
 
     def meanwhile(token):

time: 59.3 us -> 60.9 us (1.027)
  waiting for transfers between devices: 14.6 us -> 16.3 us
    ppermute x2, waiting for transfers between devices: 0.01 us -> 1.38 us  [ask(): return lax.ppermute(ids, 'mem', [(i, i ^ x) for i in range(4)])]
  transfers between devices with their start and end apart: 15 -> 15, of which waited for: 5 -> 6; matrix products, arithmetic and copies ran while one was open for 0% -> 0% of each run, Pallas kernels for 22% -> 18%
where the time goes in v29:
time: 60.9 us; the launch traced here: 60.6 us
  starting transfers between devices  22.9 us (38%)
  Pallas kernels  19.8 us (33%)
  waiting for transfers between devices  16.3 us (27%)
  local copies, waits for them, and re-layouts  0.91 us (1%)
    ppermute x4, waiting for transfers between devices, send(): return lax.ppermute(x, 'mem', pairs)  10.5 us
    pallas_call x1, Pallas kernels, shards(): pl.pallas_call(functools.partial(project_own_kernel, tps), in_specs=[smem...  5.55 us
    ppermute x2, starting transfers between devices, ask(): return lax.ppermute(ids, 'mem', [(i, i ^ x) for i in range(4)])  5.28 us
    ppermute x4, starting transfers between devices, send(): return lax.ppermute(x, 'mem', pairs)  4.76 us
    ppermute x2, waiting for transfers between devices, crossing(): lax.ppermute(x, ('mem', 'rep'), [(2 * a + b, 2 * c + d) for a, b, c, d in...  4.16 us
    ppermute x2, starting transfers between devices, crossing(): lax.ppermute(x, ('mem', 'rep'), [(2 * a + b, 2 * c + d) for a, b, c, d in...  3.71 us
    pallas_call x1, Pallas kernels, shards(): pl.pallas_call(functools.partial(project_others_kernel, tps), in_specs=[s...  3.6 us
    pallas_call x4, Pallas kernels, pick(): pl.pallas_call(pick_kernel, in_specs=[pl.BlockSpec(memory_space=pltpu.SME...  3.46 us
  transfers between devices with their start and end apart: 15, of which 6 were waited for; matrix products, arithmetic and copies ran while one was open for 0% of the time, Pallas kernels for 18%

profile of v29, /device:TPU:0, one launch (start us, length us, event | category | flops | bytes accessed | tf_op | source)
XLA Modules:
  0.0 60.6 jit_solution(8977647746522547326)
XLA Ops:
  0.0 1.5 %place_rows.1 = (s32[8,256]{1,0:T(8,128)S(1)}, bf16[8,80,1024]{2,1,0:T(8,128)(2,1)S(1)}) custom-call(s32[8,256]{1,0:T(8,128)} %bitcast.11, s32[32,128]{1,0:T(8,128)} %bitcast.10, bf16[8,80,1024]{2,1,0:T(8,128)(2,1)} %bitcast.9), custom_call_target="tpu_custom_call" | custom-call | tf_op jit(solution)/shard_map/place_rows/pallas_call | solution.py:407
  1.5 0.0 copy-start.2
  1.5 0.9 %copy-done.2 = bf16[8,1024,5]{1,0,2:T(8,128)(2,1)S(1)} copy-done((bf16[8,1024,5]{1,0,2:T(8,128)(2,1)S(1)}, bf16[8,1024,5]{1,0,2:T(8,128)(2,1)}, u32[]{:S(2)}) %copy-start.2) | copy-done | bytes 81944
  2.4 0.8 %decode_tables.1.table_ref = bf16[8,80,1024]{2,1,0:T(8,128)(2,1)S(1)} custom-call(bf16[8,80,1024]{2,1,0:T(8,128)(2,1)S(1)} %get-tuple-element.32.codes_ref, bf16[5,8,1024]{2,1,0:T(8,128)(2,1)S(1)} %bitcast.8), custom_call_target="tpu_custom_call" | custom-call | tf_op jit(solution)/shard_map/decode_tables/pallas_call | solution.py:423
  3.2 0.5 collective-permute-start.3
  3.7 0.1 collective-permute-start.4
  3.8 5.0 %collective-permute-start = (s32[8,256]{1,0:T(8,128)S(1)}, s32[8,256]{1,0:T(8,128)S(1)}, u32[]{:S(2)}, u32[]{:S(2)}) collective-permute-start(s32[8,256]{1,0:T(8,128)S(1)} %get-tuple-element.41.ids_ref), channel_id=1, source_target_pairs={{0,12},{4,8},{8,4},{12,0},{1,13},{5,9},{9,5},{13,1},{2,14},{6,10},... | collective-permute-start | bytes 24584 | tf_op jit(solution)/shard_map/ppermute | solution.py:338
  8.8 0.0 collective-permute-start.1
  8.8 0.2 collective-permute-start.2
  9.1 1.4 %collective-permute-done.ids_ref = s32[8,256]{1,0:T(8,128)S(1)} collective-permute-done((s32[8,256]{1,0:T(8,128)S(1)}, s32[8,256]{1,0:T(8,128)S(1)}, u32[]{:S(2)}, u32[]{:S(2)}) %collective-permute-start) | collective-permute-done | bytes 8224 | tf_op jit(solution)/shard_map/ppermute | solution.py:338
  10.5 0.9 %pick_rows.4 = bf16[640,256]{1,0:T(8,128)(2,1)S(1)} custom-call(s32[1]{0:T(128)} %bitcast.3.base_ref, s32[8,256]{1,0:T(8,128)S(1)} %collective-permute-done.ids_ref, bf16[8,80,1024]{2,1,0:T(8,128)(2,1)S(1)} %decode_tables.1.table_ref), custom_call_target="tpu_custom_call" | custom-call | tf_op jit(solution)/shard_map/pick_rows/pallas_call | solution.py:344
  11.3 1.6 %collective-permute-done.1.ids_ref = s32[8,256]{1,0:T(8,128)S(1)} collective-permute-done((s32[8,256]{1,0:T(8,128)S(1)}, s32[8,256]{1,0:T(8,128)S(1)}, u32[]{:S(2)}, u32[]{:S(2)}) %collective-permute-start.1) | collective-permute-done | bytes 8224 | tf_op jit(solution)/shard_map/ppermute | solution.py:341
  12.9 0.0 collective-permute-done.2.ids_ref
  12.9 2.0 %collective-permute-start.9 = (bf16[640,256]{1,0:T(8,128)(2,1)S(1)}, bf16[640,256]{1,0:T(8,128)(2,1)S(1)}, u32[]{:S(2)}, u32[]{:S(2)}) collective-permute-start(bf16[640,256]{1,0:T(8,128)(2,1)S(1)} %pick_rows.4), channel_id=1, source_target_pairs={{0,4},{12,8},{1,5},{13,9},{2,6},{14,10},{3,7},{15,11},{16,20},{28,... | collective-permute-start | bytes 983048 | tf_op jit(solution)/shard_map/ppermute | solution.py:354
  14.9 0.7 %collective-permute-start.7 = (bf16[640,256]{1,0:T(8,128)(2,1)S(1)}, bf16[640,256]{1,0:T(8,128)(2,1)S(1)}, u32[]{:S(2)}, u32[]{:S(2)}) collective-permute-start(bf16[640,256]{1,0:T(8,128)(2,1)S(1)} %pick_rows.4), channel_id=1, source_target_pairs={{4,8},{8,4},{5,9},{9,5},{6,10},{10,6},{7,11},{11,7},{20,24},{24,20... | collective-permute-start | bytes 983048 | tf_op jit(solution)/shard_map/ppermute | solution.py:354
  15.5 0.9 %pick_rows.5 = bf16[640,256]{1,0:T(8,128)(2,1)S(1)} custom-call(s32[1]{0:T(128)} %bitcast.3.base_ref, s32[8,256]{1,0:T(8,128)S(1)} %collective-permute-done.1.ids_ref, bf16[8,80,1024]{2,1,0:T(8,128)(2,1)S(1)} %decode_tables.1.table_ref), custom_call_target="tpu_custom_call" | custom-call | tf_op jit(solution)/shard_map/pick_rows/pallas_call | solution.py:344
  16.4 0.0 copy-start
  16.4 3.7 %collective-permute-start.5 = (bf16[640,256]{1,0:T(8,128)(2,1)S(1)}, bf16[640,256]{1,0:T(8,128)(2,1)S(1)}, u32[]{:S(2)}, u32[]{:S(2)}) collective-permute-start(bf16[640,256]{1,0:T(8,128)(2,1)S(1)} %pick_rows.5), channel_id=1, source_target_pairs={{0,9},{1,8},{12,5},{13,4},{2,11},{3,10},{14,7},{15,6},{16,25},{17,... | collective-permute-start | bytes 983048 | tf_op jit(solution)/shard_map/ppermute | solution.py:341
  20.1 0.0 collective-permute-done.3.refs_2_
  20.1 0.0 collective-permute-done.4.refs_3_
  20.2 0.9 %pick_rows.6 = bf16[640,256]{1,0:T(8,128)(2,1)S(1)} custom-call(s32[1]{0:T(128)} %bitcast.3.base_ref, s32[8,256]{1,0:T(8,128)S(1)} %collective-permute-done.2.ids_ref, bf16[8,80,1024]{2,1,0:T(8,128)(2,1)S(1)} %decode_tables.1.table_ref), custom_call_target="tpu_custom_call" | custom-call | tf_op jit(solution)/shard_map/pick_rows/pallas_call | solution.py:344
  21.0 0.8 %collective-permute-start.6 = (bf16[640,256]{1,0:T(8,128)(2,1)S(1)}, bf16[640,256]{1,0:T(8,128)(2,1)S(1)}, u32[]{:S(2)}, u32[]{:S(2)}) collective-permute-start(bf16[640,256]{1,0:T(8,128)(2,1)S(1)} %pick_rows.6), channel_id=1, source_target_pairs={{0,4},{4,0},{8,12},{12,8},{1,5},{5,1},{9,13},{13,9},{2,6},{6,2},{1... | collective-permute-start | bytes 983048 | tf_op jit(solution)/shard_map/ppermute | solution.py:354
  21.8 0.9 %pick_rows.7 = bf16[640,256]{1,0:T(8,128)(2,1)S(1)} custom-call(s32[1]{0:T(128)} %bitcast.3.base_ref, s32[8,256]{1,0:T(8,128)S(1)} %get-tuple-element.41.ids_ref, bf16[8,80,1024]{2,1,0:T(8,128)(2,1)S(1)} %decode_tables.1.table_ref), custom_call_target="tpu_custom_call" | custom-call | tf_op jit(solution)/shard_map/pick_rows/pallas_call | solution.py:344
  22.7 0.0 collective-permute-done.9
  22.7 0.1 add.20
  22.8 1.3 %collective-permute-start.10 = (bf16[640,256]{1,0:T(8,128)(2,1)S(1)}, bf16[640,256]{1,0:T(8,128)(2,1)S(1)}, u32[]{:S(2)}, u32[]{:S(2)}) collective-permute-start(bf16[640,256]{1,0:T(8,128)(2,1)S(1)} %add.20), channel_id=1, source_target_pairs={{4,12},{8,0},{5,13},{9,1},{6,14},{10,2},{7,15},{11,3},{20,28},{24,... | collective-permute-start | bytes 983048 | tf_op jit(solution)/shard_map/ppermute | solution.py:354
  24.1 0.0 copy-done
  24.1 0.0 collective-permute-done.7.refs_1_
  24.1 2.1 %collective-permute-start.8 = (bf16[16,2304]{1,0:T(8,128)(2,1)S(1)}, bf16[16,2304]{1,0:T(8,128)(2,1)S(1)}, u32[]{:S(2)}, u32[]{:S(2)}) collective-permute-start(bf16[16,2304]{1,0:T(8,128)(2,1)S(1)} %slice.6), channel_id=1, source_target_pairs={{0,1},{4,5},{8,9},{12,13},{2,3},{6,7},{10,11},{14,15},{16,17},{20,... | collective-permute-start | bytes 221192 | tf_op jit(solution)/shard_map/ppermute | solution.py:438
  26.3 2.6 %collective-permute-done.5 = bf16[640,256]{1,0:T(8,128)(2,1)S(1)} collective-permute-done((bf16[640,256]{1,0:T(8,128)(2,1)S(1)}, bf16[640,256]{1,0:T(8,128)(2,1)S(1)}, u32[]{:S(2)}, u32[]{:S(2)}) %collective-permute-start.5) | collective-permute-done | bytes 327712 | tf_op jit(solution)/shard_map/ppermute | solution.py:341
  28.9 6.9 %collective-permute-done.6 = bf16[640,256]{1,0:T(8,128)(2,1)S(1)} collective-permute-done((bf16[640,256]{1,0:T(8,128)(2,1)S(1)}, bf16[640,256]{1,0:T(8,128)(2,1)S(1)}, u32[]{:S(2)}, u32[]{:S(2)}) %collective-permute-start.6) | collective-permute-done | bytes 327712 | tf_op jit(solution)/shard_map/ppermute | solution.py:354
  35.8 0.0 collective-permute-done.8.refs_4_
  35.8 3.6 %collective-permute-done.10.refs_2_ = bf16[640,256]{1,0:T(8,128)(2,1)S(1)} collective-permute-done((bf16[640,256]{1,0:T(8,128)(2,1)S(1)}, bf16[640,256]{1,0:T(8,128)(2,1)S(1)}, u32[]{:S(2)}, u32[]{:S(2)}) %collective-permute-start.10) | collective-permute-done | bytes 327712 | tf_op jit(solution)/shard_map/ppermute | solution.py:354
  39.4 0.1 merge.1.body_ref
  39.6 1.6 %collective-permute-start.12 = (bf16[640,256]{1,0:T(8,128)(2,1)S(1)}, bf16[640,256]{1,0:T(8,128)(2,1)S(1)}, u32[]{:S(2)}, u32[]{:S(2)}) collective-permute-start(bf16[640,256]{1,0:T(8,128)(2,1)S(1)} %merge.1.body_ref), channel_id=1, source_target_pairs={{0,2},{2,0},{1,3},{3,1},{4,6},{6,4},{5,7},{7,5},{8,10},{10,8},{9,1... | collective-permute-start | bytes 983048 | tf_op jit(solution)/shard_map/ppermute | solution.py:449
  41.1 1.7 %collective-permute-start.13 = (bf16[640,128]{1,0:T(8,128)(2,1)S(1)}, bf16[640,128]{1,0:T(8,128)(2,1)S(1)}, u32[]{:S(2)}, u32[]{:S(2)}) collective-permute-start(bf16[640,128]{1,0:T(8,128)(2,1)S(1)} %slice.8), channel_id=1, source_target_pairs={{0,1},{2,3},{4,5},{6,7},{8,9},{10,11},{12,13},{14,15},{16,17},{18,... | collective-permute-start | bytes 491528 | tf_op jit(solution)/shard_map/ppermute | solution.py:462
  42.9 1.6 %collective-permute-start.11 = (bf16[640,128]{1,0:T(8,128)(2,1)S(1)}, bf16[640,128]{1,0:T(8,128)(2,1)S(1)}, u32[]{:S(2)}, u32[]{:S(2)}) collective-permute-start(bf16[640,128]{1,0:T(8,128)(2,1)S(1)} %slice.8), channel_id=1, source_target_pairs={{0,3},{2,1},{4,7},{6,5},{8,11},{10,9},{12,15},{14,13},{16,19},{18,... | collective-permute-start | bytes 491528 | tf_op jit(solution)/shard_map/ppermute | solution.py:462
  44.5 0.1 pad_add_fusion.where_ref
  44.6 0.0 collective-permute-done.13.rim_ref
  44.6 5.6 %project_own.1 = (f32[2,272,1152]{2,1,0:T(8,128)S(1)}, f32[2,272,1152]{2,1,0:T(8,128)S(1)}, bf16[2,2,640,1152]{3,2,1,0:T(8,128)(2,1)S(1)}, bf16[2,272,1152]{2,1,0:T(8,128)(2,1)S(1)}, f32[272,8]{1,0:T(8,128)S(1)}) custom-call(s32[2]{0:T(128)S(1)} %pad_add_fusion.where_ref, bf16[640,128]{1,0:T(8,128)(2,1)S(1)} %collective-permute-done.13.rim_ref, ...), custom_call_target="tpu_custom_call" | custom-call | tf_op jit(solution)/shard_map/project_own/pallas_call | solution.py:468
  50.2 0.0 collective-permute-done.11.refs_0_
  50.2 0.0 collective-permute-done.12.refs_1_
  50.2 0.0 copy-start.1
  50.2 3.6 %project_others.1 = (f32[2,272,1152]{2,1,0:T(8,128)}, f32[8,272]{1,0:T(8,128)S(1)}) custom-call(s32[2]{0:T(128)S(1)} %pad_add_fusion.where_ref, bf16[640,128]{1,0:T(8,128)(2,1)S(1)} %collective-permute-done.11.refs_0_, bf16[640,256]{1,0:T(8,128)(2,1)S(1)} %collective-permute-done.12.refs_1_, bf16[2,2,640,1152]{3,2,1,0:T(8,128)(2,1)S(1)} %get-tuple-element.48.refs_2_, ...), custom_call_target="tpu_custom_call" | custom-call | tf_op jit(solution)/shard_map/project_others/pallas_call | solution.py:487
  53.8 1.6 %collective-permute-start.14 = (f32[8,272]{1,0:T(8,128)S(1)}, f32[8,272]{1,0:T(8,128)S(1)}, u32[]{:S(2)}, u32[]{:S(2)}) collective-permute-start(f32[8,272]{1,0:T(8,128)S(1)} %get-tuple-element.53.refs_0_), channel_id=1, source_target_pairs={{0,2},{2,0},{1,3},{3,1},{4,6},{6,4},{5,7},{7,5},{8,10},{10,8},{9,1... | collective-permute-start | bytes 26120 | tf_op jit(solution)/shard_map/ppermute | solution.py:501
  55.4 1.9 %prepare.1 = (f32[2,256,1152]{2,1,0:T(8,128)S(1)}, f32[3,2,256,1152]{3,2,1,0:T(8,128)S(1)}) custom-call(f32[4,2304]{1,0:T(4,128)S(1)} %copy-done.1, f32[2,272,1152]{2,1,0:T(8,128)} %get-tuple-element.54.value_hbm), custom_call_target="tpu_custom_call" | custom-call | tf_op jit(solution)/shard_map/prepare/pallas_call | solution.py:509
  57.3 0.3 collective-permute-done.14.refs_1_
  57.6 2.8 %finish.1 = bf16[256,2304]{1,0:T(8,128)(2,1)} custom-call(s32[1]{0:T(128)} %bitcast.keep_ref, f32[8,272]{1,0:T(8,128)S(1)} %get-tuple-element.53.refs_0_, f32[8,272]{1,0:T(8,128)S(1)} %collective-permute-done.14.refs_1_, f32[2,256,1152]{2,1,0:T(8,128)S(1)} %get-tuple-element.55.refs_2_, f32[3,2,256,1152]{3,2,1,0:T(8,128)S(1)} %get-tuple-element.56.refs_3_, ...), custom_call_target="tpu_custom_call" | custom-call | tf_op jit(solution)/shard_map/finish/pallas_call | solution.py:524
  (4 shorter events, 0.1 us)
Async XLA Ops:
  1.5 0.9 %copy-start.2 = (bf16[8,1024,5]{1,0,2:T(8,128)(2,1)S(1)}, bf16[8,1024,5]{1,0,2:T(8,128)(2,1)}, u32[]{:S(2)}) copy-start(bf16[8,1024,5]{1,0,2:T(8,128)(2,1)} %param.12) | copy-start | bytes 245764
  3.2 16.9 %collective-permute-start.3 = (bf16[1280,1152]{1,0:T(8,128)(2,1)}, bf16[1280,1152]{1,0:T(8,128)(2,1)}, u32[]{:S(2)}, u32[]{:S(2)}) collective-permute-start(bf16[1280,1152]{1,0:T(8,128)(2,1)} %refs_0_.1), channel_id=1, source_target_pairs={{0,1},{1,0},{2,3},{3,2},{4,5},{5,4},{6,7},{7,6},{8,9},{9,8},{10,11... | collective-permute-start | bytes 8847368 | tf_op jit(solution)/shard_map/ppermute | solution.py:432
  3.7 16.4 %collective-permute-start.4 = (bf16[1280,1152]{1,0:T(8,128)(2,1)}, bf16[1280,1152]{1,0:T(8,128)(2,1)}, u32[]{:S(2)}, u32[]{:S(2)}) collective-permute-start(bf16[1280,1152]{1,0:T(8,128)(2,1)} %refs_1_.1), channel_id=1, source_target_pairs={{0,1},{1,0},{2,3},{3,2},{4,5},{5,4},{6,7},{7,6},{8,9},{9,8},{10,11... | collective-permute-start | bytes 8847368 | tf_op jit(solution)/shard_map/ppermute | solution.py:433
  3.8 6.7 %collective-permute-start = (s32[8,256]{1,0:T(8,128)S(1)}, s32[8,256]{1,0:T(8,128)S(1)}, u32[]{:S(2)}, u32[]{:S(2)}) collective-permute-start(s32[8,256]{1,0:T(8,128)S(1)} %get-tuple-element.41.ids_ref), channel_id=1, source_target_pairs={{0,12},{4,8},{8,4},{12,0},{1,13},{5,9},{9,5},{13,1},{2,14},{6,10},... | collective-permute-start | bytes 24584 | tf_op jit(solution)/shard_map/ppermute | solution.py:338
  8.8 4.0 %collective-permute-start.1 = (s32[8,256]{1,0:T(8,128)S(1)}, s32[8,256]{1,0:T(8,128)S(1)}, u32[]{:S(2)}, u32[]{:S(2)}) collective-permute-start(s32[8,256]{1,0:T(8,128)S(1)} %get-tuple-element.41.ids_ref), channel_id=1, source_target_pairs={{0,8},{1,9},{4,13},{5,12},{8,1},{9,0},{12,4},{13,5},{2,10},{3,11},... | collective-permute-start | bytes 24584 | tf_op jit(solution)/shard_map/ppermute | solution.py:341
  8.8 4.0 %collective-permute-start.2 = (s32[8,256]{1,0:T(8,128)S(1)}, s32[8,256]{1,0:T(8,128)S(1)}, u32[]{:S(2)}, u32[]{:S(2)}) collective-permute-start(s32[8,256]{1,0:T(8,128)S(1)} %get-tuple-element.41.ids_ref), channel_id=1, source_target_pairs={{0,4},{4,0},{8,12},{12,8},{1,5},{5,1},{9,13},{13,9},{2,6},{6,2},{1... | collective-permute-start | bytes 24584 | tf_op jit(solution)/shard_map/ppermute | solution.py:338
  12.9 9.8 %collective-permute-start.9 = (bf16[640,256]{1,0:T(8,128)(2,1)S(1)}, bf16[640,256]{1,0:T(8,128)(2,1)S(1)}, u32[]{:S(2)}, u32[]{:S(2)}) collective-permute-start(bf16[640,256]{1,0:T(8,128)(2,1)S(1)} %pick_rows.4), channel_id=1, source_target_pairs={{0,4},{12,8},{1,5},{13,9},{2,6},{14,10},{3,7},{15,11},{16,20},{28,... | collective-permute-start | bytes 983048 | tf_op jit(solution)/shard_map/ppermute | solution.py:354
  14.9 9.3 %collective-permute-start.7 = (bf16[640,256]{1,0:T(8,128)(2,1)S(1)}, bf16[640,256]{1,0:T(8,128)(2,1)S(1)}, u32[]{:S(2)}, u32[]{:S(2)}) collective-permute-start(bf16[640,256]{1,0:T(8,128)(2,1)S(1)} %pick_rows.4), channel_id=1, source_target_pairs={{4,8},{8,4},{5,9},{9,5},{6,10},{10,6},{7,11},{11,7},{20,24},{24,20... | collective-permute-start | bytes 983048 | tf_op jit(solution)/shard_map/ppermute | solution.py:354
  16.4 7.7 %copy-start = (bf16[256,2304]{1,0:T(8,128)(2,1)S(1)}, bf16[256,2304]{1,0:T(8,128)(2,1)}, u32[]{:S(2)}) copy-start(bf16[256,2304]{1,0:T(8,128)(2,1)} %refs_4_.1) | copy-start | bytes 3538948
  16.4 12.4 %collective-permute-start.5 = (bf16[640,256]{1,0:T(8,128)(2,1)S(1)}, bf16[640,256]{1,0:T(8,128)(2,1)S(1)}, u32[]{:S(2)}, u32[]{:S(2)}) collective-permute-start(bf16[640,256]{1,0:T(8,128)(2,1)S(1)} %pick_rows.5), channel_id=1, source_target_pairs={{0,9},{1,8},{12,5},{13,4},{2,11},{3,10},{14,7},{15,6},{16,25},{17,... | collective-permute-start | bytes 983048 | tf_op jit(solution)/shard_map/ppermute | solution.py:341
  21.0 14.7 %collective-permute-start.6 = (bf16[640,256]{1,0:T(8,128)(2,1)S(1)}, bf16[640,256]{1,0:T(8,128)(2,1)S(1)}, u32[]{:S(2)}, u32[]{:S(2)}) collective-permute-start(bf16[640,256]{1,0:T(8,128)(2,1)S(1)} %pick_rows.6), channel_id=1, source_target_pairs={{0,4},{4,0},{8,12},{12,8},{1,5},{5,1},{9,13},{13,9},{2,6},{6,2},{1... | collective-permute-start | bytes 983048 | tf_op jit(solution)/shard_map/ppermute | solution.py:354
  22.8 16.6 %collective-permute-start.10 = (bf16[640,256]{1,0:T(8,128)(2,1)S(1)}, bf16[640,256]{1,0:T(8,128)(2,1)S(1)}, u32[]{:S(2)}, u32[]{:S(2)}) collective-permute-start(bf16[640,256]{1,0:T(8,128)(2,1)S(1)} %add.20), channel_id=1, source_target_pairs={{4,12},{8,0},{5,13},{9,1},{6,14},{10,2},{7,15},{11,3},{20,28},{24,... | collective-permute-start | bytes 983048 | tf_op jit(solution)/shard_map/ppermute | solution.py:354
  24.1 11.7 %collective-permute-start.8 = (bf16[16,2304]{1,0:T(8,128)(2,1)S(1)}, bf16[16,2304]{1,0:T(8,128)(2,1)S(1)}, u32[]{:S(2)}, u32[]{:S(2)}) collective-permute-start(bf16[16,2304]{1,0:T(8,128)(2,1)S(1)} %slice.6), channel_id=1, source_target_pairs={{0,1},{4,5},{8,9},{12,13},{2,3},{6,7},{10,11},{14,15},{16,17},{20,... | collective-permute-start | bytes 221192 | tf_op jit(solution)/shard_map/ppermute | solution.py:438
  39.6 10.6 %collective-permute-start.12 = (bf16[640,256]{1,0:T(8,128)(2,1)S(1)}, bf16[640,256]{1,0:T(8,128)(2,1)S(1)}, u32[]{:S(2)}, u32[]{:S(2)}) collective-permute-start(bf16[640,256]{1,0:T(8,128)(2,1)S(1)} %merge.1.body_ref), channel_id=1, source_target_pairs={{0,2},{2,0},{1,3},{3,1},{4,6},{6,4},{5,7},{7,5},{8,10},{10,8},{9,1... | collective-permute-start | bytes 983048 | tf_op jit(solution)/shard_map/ppermute | solution.py:449
  41.1 3.5 %collective-permute-start.13 = (bf16[640,128]{1,0:T(8,128)(2,1)S(1)}, bf16[640,128]{1,0:T(8,128)(2,1)S(1)}, u32[]{:S(2)}, u32[]{:S(2)}) collective-permute-start(bf16[640,128]{1,0:T(8,128)(2,1)S(1)} %slice.8), channel_id=1, source_target_pairs={{0,1},{2,3},{4,5},{6,7},{8,9},{10,11},{12,13},{14,15},{16,17},{18,... | collective-permute-start | bytes 491528 | tf_op jit(solution)/shard_map/ppermute | solution.py:462
  42.9 7.3 %collective-permute-start.11 = (bf16[640,128]{1,0:T(8,128)(2,1)S(1)}, bf16[640,128]{1,0:T(8,128)(2,1)S(1)}, u32[]{:S(2)}, u32[]{:S(2)}) collective-permute-start(bf16[640,128]{1,0:T(8,128)(2,1)S(1)} %slice.8), channel_id=1, source_target_pairs={{0,3},{2,1},{4,7},{6,5},{8,11},{10,9},{12,15},{14,13},{16,19},{18,... | collective-permute-start | bytes 491528 | tf_op jit(solution)/shard_map/ppermute | solution.py:462
  50.2 5.2 %copy-start.1 = (f32[4,2304]{1,0:T(4,128)S(1)}, f32[4,2304]{1,0:T(4,128)}, u32[]{:S(2)}) copy-start(f32[4,2304]{1,0:T(4,128)} %refs_5_.3) | copy-start | bytes 110596
  53.8 3.8 %collective-permute-start.14 = (f32[8,272]{1,0:T(8,128)S(1)}, f32[8,272]{1,0:T(8,128)S(1)}, u32[]{:S(2)}, u32[]{:S(2)}) collective-permute-start(f32[8,272]{1,0:T(8,128)S(1)} %get-tuple-element.53.refs_0_), channel_id=1, source_target_pairs={{0,2},{2,0},{1,3},{3,1},{4,6},{6,4},{5,7},{7,5},{8,10},{10,8},{9,1... | collective-permute-start | bytes 26120 | tf_op jit(solution)/shard_map/ppermute | solution.py:501
